TPU v7x, 32 devices: a whole 2x2x4 slice. The times are simulated.
32 devices in a mesh: req: 4 (over y, core), exp: 8 (over z, x).
Axes of the slice: x: 2, y: 2, z: 4, core: 2. Of those that a mesh axis runs over, the one named last changes fastest.
Arguments:
- resid: bfloat16 [2048, 2048], P(('req', 'exp')), may hold values from -27 to 27
- queries: bfloat16 [2048, 2048], P(('req', 'exp')), may hold values from -6 to 6
- cache_key: bfloat16 [64, 128, 2048], P(('req', 'exp')), may hold values from -6 to 6
- cache_value: bfloat16 [64, 128, 2048], P(('req', 'exp')), may hold values from -6 to 6
- page_table: int32 [16, 4], P('req'), may hold values from 0 to 15, as said below
- row_request: int32 [2048], P('req'), may hold values from 0 to 3, as said below
- row_position: int32 [2048], P('req'), may hold values from 0 to 511, as said below
- out_proj: bfloat16 [2048, 2048], P('exp'), may hold values from -0.375 to 0.375
- norm_gain: float32 [2048], replicated, may hold values from 0.5 to 1.5
- expert_gate: bfloat16 [32, 2048, 1408], P(('req', 'exp')), as said below
- expert_up: bfloat16 [32, 2048, 1408], P(('req', 'exp')), as said below
- expert_down: bfloat16 [32, 1408, 2048], P(('req', 'exp')), as said below
- shared_gate: bfloat16 [2048, 5632], P(None, 'exp'), may hold values from -0.125 to 0.125
- shared_up: bfloat16 [2048, 5632], P(None, 'exp'), may hold values from -0.125 to 0.125
- shared_down: bfloat16 [5632, 2048], P('exp'), may hold values from -0.078125 to 0.078125
- shared_scalar: bfloat16 [2048], replicated, may hold values from -0.375 to 0.375
- slot_expert: int32 [32], replicated, may hold values from 0 to 14, as said below
- route_expert: int32 [2048, 4], replicated, may hold values from 0 to 14, as said below
- route_gate: float32 [2048, 4], P(('req', 'exp')), may hold values from 0.05 to 0.5
Outputs:
- output: bfloat16 [2048, 2048], P(('req', 'exp'))
Inputs may be any that keep to these rules, and one draw needn't show every extreme that they name: `page_table`: within each request group the table names each of the group's 16 pages once; page p of group g lies on the device of req index g and exp index p // 2. `row_request`: each group's rows are in order of request; every request has one row or more; half of the requests of a group have exactly one row. `row_position`: the rows of one request hold consecutive positions ending at the request's length minus one. `slot_expert`: every expert is held by one slot or more. `route_expert`: each row names 4 different experts. In each aligned block of 64 rows (the rows of one device) no expert is named more than 24 times, and one expert is named exactly 24 times in every block. `expert_gate`: slots that hold the same expert hold equal weights. `expert_up`: slots that hold the same expert hold equal weights. `expert_down`: slots that hold the same expert hold equal weights.
All inputs are finite; a program needn't handle non-finite values.
Results may differ from a plain program's by a relative error of at most 0.006.
Values may be sent and summed in bfloat16 or wider, within the bound.
No kernel may reach another device: no remote copies, remote signals or barrier semaphores. Data moves between devices by JAX's collectives and lax.ppermute only.
A program may use at most 128 MiB of HBM per device.

v0:
```python
import math

import jax
import jax.numpy as jnp
from jax import lax
from jax.sharding import PartitionSpec as P

HEADS = 16
HEAD_DIM = 128
TOPK = 4


def expert_block(rows, gate_w, up_w, down_w):
    gate = jnp.dot(rows, gate_w, preferred_element_type=jnp.float32)
    upper = jnp.dot(rows, up_w, preferred_element_type=jnp.float32)
    hidden = (jax.nn.silu(gate) * upper).astype(jnp.bfloat16)
    return jnp.dot(hidden, down_w, preferred_element_type=jnp.float32).astype(jnp.bfloat16)


def rms_normed(stream, norm_gain):
    scale_row = lax.rsqrt(jnp.mean(stream * stream, axis=1, keepdims=True) + 1e-06)
    return (stream * scale_row * norm_gain[None, :]).astype(jnp.bfloat16)


def shards(
    resid,
    queries,
    cache_key,
    cache_value,
    page_table,
    row_request,
    row_position,
    out_proj,
    norm_gain,
    expert_gate,
    expert_up,
    expert_down,
    shared_gate,
    shared_up,
    shared_down,
    shared_scalar,
    slot_expert,
    route_expert,
    route_gate,
):
    exp_count = lax.axis_size("exp")
    req_count = lax.axis_size("req")
    slot_count = exp_count * req_count
    exp_index = lax.axis_index("exp")
    own_slot = lax.axis_index("req") * exp_count + exp_index
    tok_rows = resid.shape[0]
    model_width = resid.shape[1]
    group_rows = row_request.shape[0]
    pages_here = cache_key.shape[0]
    page_len = cache_key.shape[1]
    req_slots = page_table.shape[0]
    max_pages = page_table.shape[1]
    capacity = 3 * tok_rows * TOPK // slot_count
    whole_queries = lax.all_gather(queries, "exp", axis=0, tiled=True)
    page_ids = exp_index * pages_here + jnp.arange(pages_here, dtype=jnp.int32)
    hits = (page_table[None, :, :] == page_ids[:, None, None]).astype(jnp.int32)
    page_request = jnp.sum(
        hits * jnp.arange(req_slots, dtype=jnp.int32)[None, :, None], axis=(1, 2)
    )
    page_slot = jnp.sum(hits * jnp.arange(max_pages, dtype=jnp.int32)[None, None, :], axis=(1, 2))
    key_position = (
        page_slot[:, None] * page_len + jnp.arange(page_len, dtype=jnp.int32)[None, :]
    ).reshape(-1)
    key_request = jnp.repeat(page_request, page_len)
    visible = (row_request[:, None] == key_request[None, :]) & (
        key_position[None, :] <= row_position[:, None]
    )
    key_count = pages_here * page_len
    query_heads = whole_queries.reshape(group_rows, HEADS, HEAD_DIM)
    key_heads = cache_key.reshape(key_count, HEADS, HEAD_DIM)
    value_heads = cache_value.reshape(key_count, HEADS, HEAD_DIM)
    scores = jnp.einsum(
        "rhd,khd->hrk", query_heads, key_heads, preferred_element_type=jnp.float32
    ) * HEAD_DIM ** (-0.5)
    scores = jnp.where(visible[None], scores, -1e30)
    top = lax.pmax(jnp.max(scores, axis=2), "exp")
    weights = jnp.where(visible[None], jnp.exp(scores - top[:, :, None]), 0.0)
    denominators = jnp.transpose(jnp.sum(weights, axis=2))
    numerators = jnp.einsum(
        "hrk,khd->rhd",
        weights.astype(jnp.bfloat16),
        value_heads,
        preferred_element_type=jnp.float32,
    ).reshape(group_rows, model_width)
    num_cols, den_cols = (
        lax.psum_scatter(numerators, "exp", scatter_dimension=1, tiled=True),
        lax.psum_scatter(denominators, "exp", scatter_dimension=1, tiled=True),
    )
    local_heads = den_cols.shape[1]
    attention = (
        (num_cols.reshape(group_rows, local_heads, HEAD_DIM) / den_cols[:, :, None])
        .reshape(group_rows, local_heads * HEAD_DIM)
        .astype(jnp.bfloat16)
    )
    mixed = lax.psum_scatter(
        jnp.dot(attention, out_proj, preferred_element_type=jnp.float32),
        "exp",
        scatter_dimension=0,
        tiled=True,
    )
    stream = resid.astype(jnp.float32) + mixed
    normed = rms_normed(stream, norm_gain)
    piece = lax.all_gather(normed, "exp", axis=0, tiled=True)
    gate = jnp.dot(piece, shared_gate, preferred_element_type=jnp.float32)
    upper = jnp.dot(piece, shared_up, preferred_element_type=jnp.float32)
    shared_hidden = (jax.nn.silu(gate) * upper).astype(jnp.bfloat16)
    shared_out = lax.psum_scatter(
        jnp.dot(shared_hidden, shared_down, preferred_element_type=jnp.float32).astype(
            jnp.bfloat16
        ),
        "exp",
        scatter_dimension=0,
        tiled=True,
    ).astype(jnp.float32)
    shared_scale = jax.nn.sigmoid(
        jnp.dot(normed, shared_scalar, preferred_element_type=jnp.float32)
    )
    slot_ids = jnp.arange(slot_count, dtype=jnp.int32)
    same_expert = slot_expert[:, None] == slot_expert[None, :]
    copy_rank = jnp.sum(
        (same_expert & (slot_ids[None, :] < slot_ids[:, None])).astype(jnp.int32), axis=1
    )
    own_routes = lax.dynamic_slice_in_dim(route_expert, own_slot * tok_rows, tok_rows, 0).reshape(
        -1
    )
    holds = own_routes[:, None] == slot_expert[None, :]
    copy_total = jnp.sum(holds.astype(jnp.int32), axis=1)
    own_mark = slot_ids == own_slot
    own_expert = jnp.sum(jnp.where(own_mark, slot_expert, 0))
    own_rank = jnp.sum(jnp.where(own_mark, copy_rank, 0))
    wanted = jnp.zeros_like(copy_total)
    taken = jnp.broadcast_to(own_rank == 0, (slot_count,))
    chosen = holds & (copy_rank[None, :] == wanted[:, None])
    target = jnp.sum(jnp.where(chosen, slot_ids[None, :], 0), axis=1)
    onehot = chosen.astype(jnp.int32)
    position = jnp.sum(jnp.cumsum(onehot, axis=0) * onehot, axis=1) - 1
    buffer_index = target * capacity + position
    entry_rows = jnp.repeat(normed, TOPK, axis=0)
    outgoing = (
        jnp.zeros((slot_count * capacity, model_width), jnp.bfloat16)
        .at[buffer_index]
        .set(entry_rows)
    )
    outgoing = outgoing.reshape(slot_count, capacity, model_width)
    named = (
        jnp.sum((route_expert == own_expert).astype(jnp.int32), axis=1)
        .reshape(slot_count, tok_rows)
        .sum(axis=1)
    )
    arrived = jnp.where(taken, named, 0)
    incoming = lax.all_to_all(outgoing, ("req", "exp"), split_axis=0, concat_axis=0, tiled=True)
    filled = (jnp.arange(capacity, dtype=jnp.int32)[None, :] < arrived[:, None]).reshape(-1)
    packed_order = jnp.argsort(1 - filled.astype(jnp.int32), stable=True)
    packed = incoming.reshape(-1, model_width)[packed_order]
    live = jnp.sum(filled.astype(jnp.int32))
    tile = math.gcd(128, slot_count * capacity)

    def tile_step(step, results):
        rows = lax.dynamic_slice_in_dim(packed, step * tile, tile, 0)
        answer = expert_block(rows, expert_gate[0], expert_up[0], expert_down[0])
        return lax.dynamic_update_slice_in_dim(results, answer, step * tile, 0)

    results = lax.fori_loop(0, (live + tile - 1) // tile, tile_step, jnp.zeros_like(packed))
    answered = (
        jnp.zeros_like(results)
        .at[packed_order]
        .set(results)
        .reshape(slot_count, capacity, model_width)
    )
    returned = lax.all_to_all(
        answered, ("req", "exp"), split_axis=0, concat_axis=0, tiled=True
    ).reshape(-1, model_width)
    expert_out = returned[buffer_index].reshape(tok_rows, TOPK, model_width)
    routed = jnp.sum(expert_out.astype(jnp.float32) * route_gate[:, :, None], axis=1)
    return (stream + shared_scale[:, None] * shared_out + routed).astype(jnp.bfloat16)


def solution(mesh):
    placed = (
        P(("req", "exp"), None),
        P(("req", "exp"), None),
        P(("req", "exp"), None, None),
        P(("req", "exp"), None, None),
        P("req", None),
        P("req"),
        P("req"),
        P("exp", None),
        P(),
        P(("req", "exp"), None, None),
        P(("req", "exp"), None, None),
        P(("req", "exp"), None, None),
        P(None, "exp"),
        P(None, "exp"),
        P("exp", None),
        P(),
        P(),
        P(),
        P(("req", "exp"), None),
    )
    return jax.shard_map(
        shards, mesh=mesh, in_specs=placed, out_specs=P(("req", "exp"), None), check_vma=False
    )
```

profile of v0, /device:TPU:0, one launch (start us, length us, event | category | flops | bytes accessed | tf_op | source)
XLA Modules:
  0.0 619.2 jit_solution(8242843037521300704)
XLA Ops:
  12.9 48.6 %all-gather.3.cloned.1.call-done = bf16[512,2048]{1,0:T(8,128)(2,1)} async-done(((bf16[64,2048]{1,0:T(8,128)(2,1)}), bf16[512,2048]{1,0:T(8,128)(2,1)}) %all-gather.3.cloned.1.call-update) | async-done | bytes 2097168 | tf_op jit(solution)/shard_map/all_gather | solution.py:59
  65.4 6.9 %fusion.28 = (f32[16,512]{1,0:T(8,128)S(1)}, f32[16,512,256]{1,2,0:T(8,128)}) fusion(pred[512,256]{0,1:T(8,128)(4,1)S(1)} %compare_and_fusion, bf16[512,16,128]{0,2,1:T(8,128)(2,1)} %bitcast.88, bf16[256,16,128]{2,1,0:T(8,128)(2,1)} %bitcast.89), kind=kOutput, calls=%fused_computation.22 | convolution fusion | flops 543154176 | bytes 11698176 | tf_op jit(solution)/shard_map/rhd,khd->hrk/dot_general | solution.py:77
  72.3 34.6 %pmax.7 = f32[16,512]{1,0:T(8,128)S(1)} all-reduce(f32[16,512]{1,0:T(8,128)S(1)} %get-tuple-element.66), channel_id=1, replica_groups=mesh['req'=4,'exp'=8] {'exp'}, use_global_device_ids=true, to_apply=%region_3.4 | all-reduce | flops 8192 | bytes 65536 | tf_op jit(solution)/shard_map/pmax | solution.py:81
  107.0 8.2 %fusion.31 = f32[16,512,128]{1,2,0:T(8,128)} fusion(f32[16,512,256]{1,2,0:T(8,128)} %get-tuple-element.67, f32[16,512]{1,0:T(8,128)S(1)} %pmax.7, pred[512,256]{0,1:T(8,128)(4,1)S(1)} %compare_and_fusion, bf16[256,16,128]{2,1,0:T(8,128)(2,1)} %bitcast.93), kind=kOutput, calls=%fused_computation.25 | convolution fusion | flops 547356672 | bytes 13795328 | tf_op jit(solution)/shard_map/hrk,khd->rhd/dot_general | solution.py:84
  117.0 4.9 fusion.29
  121.9 34.9 %all-reduce = f32[512,16]{0,1:T(8,128)S(1)} all-reduce(f32[512,16]{0,1:T(8,128)S(1)} %bitcast.94), channel_id=3, replica_groups=mesh['req'=4,'exp'=8] {'exp'}, use_global_device_ids=true, to_apply=%region_6.7.clone | all-reduce | flops 8192 | bytes 65536
  156.8 44.2 %reduce-scatter.4.cloned.1.call-done = f32[512,256]{0,1:T(8,128)} async-done(((f32[512,2048]{0,1:T(8,128)}), f32[512,256]{0,1:T(8,128)}) %reduce-scatter.4.cloned.1.call-update) | async-done | bytes 524304 | tf_op jit(solution)/shard_map/reduce_scatter | solution.py:91
  208.4 85.5 %reduce-scatter.6.cloned.1.call-done = f32[64,2048]{1,0:T(8,128)} async-done(((f32[512,2048]{1,0:T(8,128)}), f32[64,2048]{1,0:T(8,128)}) %reduce-scatter.6.cloned.1.call-update) | async-done | bytes 524304 | tf_op jit(solution)/shard_map/reduce_scatter | solution.py:100
  300.0 5.0 scatter_custom_fusion
  305.0 4.5 all-to-all-start
  313.0 4.4 sort.17
  317.4 89.9 %all-to-all-done = bf16[32,24,2048]{2,1,0:T(8,128)(2,1)} async-done(((bf16[32,24,2048]{2,1,0:T(8,128)(2,1)}), bf16[32,24,2048]{2,1,0:T(8,128)(2,1)}, u32[]{:S(2)}, u32[]{:S(2)}) %all-to-all-start) | async-done | bytes 3145760 | tf_op jit(solution)/shard_map/all_to_all | solution.py:156
  407.3 9.4 %gather_fusion = bf16[768,2048]{1,0:T(8,128)(2,1)} fusion(bf16[768,2048]{1,0:T(8,128)(2,1)} %bitcast.15, s32[1024]{0:T(1024)S(1)} %pad_clamp_fusion.1), kind=kCustom, calls=%fused_computation | custom fusion | bytes 6294528 | tf_op jit(solution)/shard_map/gather | solution.py:159
  418.8 60.6 %while.10 = (s32[]{:T(128)}, bf16[768,2048]{1,0:T(8,128)(2,1)}, s32[]{:T(128)}, bf16[768,2048]{1,0:T(8,128)(2,1)}, bf16[1,2048,1408]{2,1,0:T(8,128)(2,1)}, /*ind...) while((s32[]{:T(128)}, bf16[768,2048]{1,0:T(8,128)(2,1)}, ...), condition=%wide.region_23.24_spmd, body=%wide.region_22.23_spmd.sunk | while | flops 2215936000 | bytes 20317344 | solution.py:168
  418.8 4.7 fusion.86
  423.5 7.4 %fusion.87 = bf16[768,2048]{1,0:T(8,128)(2,1)} fusion(bf16[768,2048]{1,0:T(8,128)(2,1)} %get-tuple-element.128, s32[]{:T(128)S(6)} %select_n.89, bf16[1,1408,2048]{2,1,0:T(8,128)(2,1)} %get-tuple-element.144, bf16[1,2048,1408]{2,1,0:T(8,128)(2,1)} %get-tuple-element.143, f32[128,1408]{1,0:T(8,128)} %fusion.86, bf16[768,2048]{1,0:T(8,128)(2,1)} %get-tuple-element.141), kind=kOutput, calls=%fused_computation.13.clone.1 | convolution fusion | flops 1477738496 | bytes 13304832 | tf_op jit(solution)/shard_map/while/body/dot_general | solution.py:17
  430.9 4.7 fusion.86
  435.6 7.4 %fusion.87 = bf16[768,2048]{1,0:T(8,128)(2,1)} fusion(bf16[768,2048]{1,0:T(8,128)(2,1)} %get-tuple-element.128, s32[]{:T(128)S(6)} %select_n.89, bf16[1,1408,2048]{2,1,0:T(8,128)(2,1)} %get-tuple-element.144, bf16[1,2048,1408]{2,1,0:T(8,128)(2,1)} %get-tuple-element.143, f32[128,1408]{1,0:T(8,128)} %fusion.86, bf16[768,2048]{1,0:T(8,128)(2,1)} %get-tuple-element.141), kind=kOutput, calls=%fused_computation.13.clone.1 | convolution fusion | flops 1477738496 | bytes 13304832 | tf_op jit(solution)/shard_map/while/body/dot_general | solution.py:17
  443.1 4.7 fusion.86
  447.7 7.4 %fusion.87 = bf16[768,2048]{1,0:T(8,128)(2,1)} fusion(bf16[768,2048]{1,0:T(8,128)(2,1)} %get-tuple-element.128, s32[]{:T(128)S(6)} %select_n.89, bf16[1,1408,2048]{2,1,0:T(8,128)(2,1)} %get-tuple-element.144, bf16[1,2048,1408]{2,1,0:T(8,128)(2,1)} %get-tuple-element.143, f32[128,1408]{1,0:T(8,128)} %fusion.86, bf16[768,2048]{1,0:T(8,128)(2,1)} %get-tuple-element.141), kind=kOutput, calls=%fused_computation.13.clone.1 | convolution fusion | flops 1477738496 | bytes 13304832 | tf_op jit(solution)/shard_map/while/body/dot_general | solution.py:17
  455.1 4.7 fusion.86
  459.8 7.4 %fusion.87 = bf16[768,2048]{1,0:T(8,128)(2,1)} fusion(bf16[768,2048]{1,0:T(8,128)(2,1)} %get-tuple-element.128, s32[]{:T(128)S(6)} %select_n.89, bf16[1,1408,2048]{2,1,0:T(8,128)(2,1)} %get-tuple-element.144, bf16[1,2048,1408]{2,1,0:T(8,128)(2,1)} %get-tuple-element.143, f32[128,1408]{1,0:T(8,128)} %fusion.86, bf16[768,2048]{1,0:T(8,128)(2,1)} %get-tuple-element.141), kind=kOutput, calls=%fused_computation.13.clone.1 | convolution fusion | flops 1477738496 | bytes 13304832 | tf_op jit(solution)/shard_map/while/body/dot_general | solution.py:17
  467.3 4.7 fusion.86
  471.9 7.5 %fusion.87 = bf16[768,2048]{1,0:T(8,128)(2,1)} fusion(bf16[768,2048]{1,0:T(8,128)(2,1)} %get-tuple-element.128, s32[]{:T(128)S(6)} %select_n.89, bf16[1,1408,2048]{2,1,0:T(8,128)(2,1)} %get-tuple-element.144, bf16[1,2048,1408]{2,1,0:T(8,128)(2,1)} %get-tuple-element.143, f32[128,1408]{1,0:T(8,128)} %fusion.86, bf16[768,2048]{1,0:T(8,128)(2,1)} %get-tuple-element.141), kind=kOutput, calls=%fused_computation.13.clone.1 | convolution fusion | flops 1477738496 | bytes 13304832 | tf_op jit(solution)/shard_map/while/body/dot_general | solution.py:17
  479.4 9.9 %scatter_custom_fusion.1 = bf16[768,2048]{1,0:T(8,128)(2,1)} fusion(s32[768]{0:T(1024)S(1)} %compare_select_fusion, bf16[768,2048]{1,0:T(8,128)(2,1)} %get-tuple-element.45, bf16[]{:T(256)} %constant.74.clone.1), kind=kCustom, calls=%fused_computation.33 | custom fusion | bytes 3146240 | tf_op jit(solution)/shard_map/scatter | solution.py:172
  489.3 10.7 %all-to-all-start.1 = ((bf16[32,24,2048]{2,1,0:T(8,128)(2,1)}), bf16[32,24,2048]{2,1,0:T(8,128)(2,1)}, u32[]{:S(2)}, u32[]{:S(2)}) async-start(bf16[32,24,2048]{2,1,0:T(8,128)(2,1)} %bitcast.87), calls=%async_computation.4 | async-start | bytes 6291456 | tf_op jit(solution)/shard_map/all_to_all | solution.py:175
  500.1 5.3 fusion.63
  505.4 7.7 %convolution_convert_fusion = bf16[512,2048]{1,0:T(8,128)(2,1)} fusion(bf16[704,2048]{1,0:T(8,128)(2,1)S(1)} %copy-done, bf16[512,2048]{1,0:T(8,128)(2,1)} %all-gather.5.cloned.1.call-done, bf16[2048,704]{0,1:T(8,128)(2,1)} %param.34, f32[512,704]{0,1:T(8,128)} %fusion.63), kind=kOutput, calls=%fused_computation.31 | convolution fusion | flops 2956001280 | bytes 11403264 | tf_op jit(solution)/shard_map/dot_general | solution.py:113
  513.5 75.9 %all-to-all-done.1 = bf16[32,24,2048]{2,1,0:T(8,128)(2,1)} async-done(((bf16[32,24,2048]{2,1,0:T(8,128)(2,1)}), bf16[32,24,2048]{2,1,0:T(8,128)(2,1)}, u32[]{:S(2)}, u32[]{:S(2)}) %all-to-all-start.1) | async-done | bytes 3145760 | tf_op jit(solution)/shard_map/all_to_all | solution.py:175
  589.4 5.6 gather_fusion.1
  597.8 4.0 multiply_reduce_fusion
  601.8 8.8 %reduce-scatter.8.cloned.1.call-done = bf16[64,2048]{1,0:T(8,128)(2,1)} async-done(((bf16[512,2048]{1,0:T(8,128)(2,1)}), bf16[64,2048]{1,0:T(8,128)(2,1)}) %reduce-scatter.8.cloned.1.call-update) | async-done | bytes 262160 | tf_op jit(solution)/shard_map/reduce_scatter | solution.py:112
  (87 shorter events, 34.5 us)
Async XLA Ops:
  6.5 498.9 %copy-start = (bf16[704,2048]{1,0:T(8,128)(2,1)S(1)}, bf16[704,2048]{1,0:T(8,128)(2,1)}, u32[]{:S(2)}) copy-start(bf16[704,2048]{1,0:T(8,128)(2,1)} %param.35) | copy-start | bytes 8650756
  6.5 5.9 copy-start.12
  6.5 6.2 copy-start.10
  6.5 6.2 copy-start.9
  6.5 55.0 %all-gather.3.cloned.1.call-start = ((), (), s32[]{:S(2)}) async-start(), calls=%async_computation.5 | async-start | bytes 2359296 | tf_op jit(solution)/shard_map/all_gather | solution.py:59
  7.3 193.7 %reduce-scatter.4.cloned.1.call-start = ((), (), s32[]{:S(2)}) async-start(), calls=%async_computation.6 | async-start | bytes 4718592 | tf_op jit(solution)/shard_map/reduce_scatter | solution.py:91
  115.1 0.7 copy-start.13
  115.2 178.8 %reduce-scatter.6.cloned.1.call-start = ((), (), s32[]{:S(2)}) async-start(), calls=%async_computation.7 | async-start | bytes 4718592 | tf_op jit(solution)/shard_map/reduce_scatter | solution.py:100
  206.0 0.8 copy-start.5
  206.0 1.1 copy-start.7
  206.0 87.9 %copy-start.4 = (bf16[64,2048]{1,0:T(8,128)(2,1)S(1)}, bf16[64,2048]{1,0:T(8,128)(2,1)}, u32[]{:S(2)}) copy-start(bf16[64,2048]{1,0:T(8,128)(2,1)} %param.21) | copy-start | bytes 786436
  206.0 89.1 %copy-start.6 = (f32[2048]{0:T(1024)S(1)}, f32[2048]{0:T(1024)}, u32[]{:S(2)}) copy-start(f32[2048]{0:T(1024)} %param.29) | copy-start | bytes 24580
  296.3 8.6 %copy-start.2 = (bf16[64,2048]{1,0:T(8,128)(2,1)}, bf16[64,2048]{1,0:T(8,128)(2,1)S(1)}, u32[]{:S(2)}) copy-start(bf16[64,2048]{1,0:T(8,128)(2,1)S(1)} %multiply_convert_fusion) | copy-start | bytes 786436
  305.0 102.4 %all-to-all-start = ((bf16[32,24,2048]{2,1,0:T(8,128)(2,1)}), bf16[32,24,2048]{2,1,0:T(8,128)(2,1)}, u32[]{:S(2)}, u32[]{:S(2)}) async-start(bf16[32,24,2048]{2,1,0:T(8,128)(2,1)} %bitcast.86), calls=%async_computation.3 | async-start | bytes 6291456 | tf_op jit(solution)/shard_map/all_to_all | solution.py:156
  309.4 190.7 %all-gather.5.cloned.1.call-start = ((), (), s32[]{:S(2)}) async-start(), calls=%async_computation.8 | async-start | bytes 2359296 | tf_op jit(solution)/shard_map/all_gather | solution.py:108
  489.3 100.0 %all-to-all-start.1 = ((bf16[32,24,2048]{2,1,0:T(8,128)(2,1)}), bf16[32,24,2048]{2,1,0:T(8,128)(2,1)}, u32[]{:S(2)}, u32[]{:S(2)}) async-start(bf16[32,24,2048]{2,1,0:T(8,128)(2,1)} %bitcast.87), calls=%async_computation.4 | async-start | bytes 6291456 | tf_op jit(solution)/shard_map/all_to_all | solution.py:175
  500.1 110.5 %reduce-scatter.8.cloned.1.call-start = ((), (), s32[]{:S(2)}) async-start(), calls=%async_computation.9 | async-start | bytes 2359296 | tf_op jit(solution)/shard_map/reduce_scatter | solution.py:112
  505.4 7.7 %copy-start.11 = (f32[64,4]{0,1:T(4,128)S(1)}, f32[64,4]{0,1:T(4,128)}, u32[]{:S(2)}) copy-start(f32[64,4]{0,1:T(4,128)} %param.39) | copy-start | bytes 3076
  505.4 7.8 %copy-start.8 = (bf16[2048]{0:T(1024)(128)(2,1)S(1)}, bf16[2048]{0:T(1024)(128)(2,1)}, u32[]{:S(2)}) copy-start(bf16[2048]{0:T(1024)(128)(2,1)} %param.36) | copy-start | bytes 12292
  505.4 7.9 %copy-start.3 = (bf16[64,2048]{1,0:T(8,128)(2,1)S(1)}, bf16[64,2048]{1,0:T(8,128)(2,1)}, u32[]{:S(2)}) copy-start(bf16[64,2048]{1,0:T(8,128)(2,1)} %copy-done.2) | copy-start | bytes 786436
  595.0 15.6 %copy-start.1 = (f32[64,2048]{1,0:T(8,128)S(1)}, f32[64,2048]{1,0:T(8,128)}, u32[]{:S(2)}) copy-start(f32[64,2048]{1,0:T(8,128)} %reduce-scatter.6.cloned.1.call-done) | copy-start | bytes 1572868
Sparse Core Ops, SparseCore 0:
  9.5 51.9 all-gather.2
  115.3 85.6 reduce-scatter.3
  206.1 87.7 reduce-scatter.5
  317.5 82.9 all-gather.4
  513.3 97.2 reduce-scatter.7
where the time goes:
time: 620 us; the launch traced here: 619 us
  waiting for transfers between devices  354 us (57%)
  matrix products  92.6 us (15%)
  blocking collectives  69.5 us (11%)
  local copies, waits for them, and re-layouts  50.2 us (8%)
  other arithmetic  22.3 us (4%)
  starting transfers between devices  15.4 us (2%)
  between operations  15.2 us (2%)
    all_to_all x1, waiting for transfers between devices, shards(): lax.all_to_all(outgoing, ('req', 'exp'), split_axis=0, concat_axis=0, til...  89.9 us
    reduce_scatter x1, waiting for transfers between devices, shards(): lax.psum_scatter(jnp.dot(attention, out_proj, preferred_element_type=jnp....  85.5 us
    all_to_all x1, waiting for transfers between devices, shards(): lax.all_to_all(answered, ('req', 'exp'), split_axis=0, concat_axis=0, til...  75.9 us
    all_gather x1, waiting for transfers between devices, shards(): whole_queries = lax.all_gather(queries, 'exp', axis=0, tiled=True)  48.6 us
    reduce_scatter x1, waiting for transfers between devices, shards(): lax.psum_scatter(numerators, 'exp', scatter_dimension=1, tiled=True)  44.2 us
    dot_general x5, matrix products, expert_block(): jnp.dot(hidden, down_w, preferred_element_type=jnp.float32)  37.1 us
    unnamed x1, blocking collectives  34.9 us
    pmax x1, blocking collectives, shards(): top = lax.pmax(jnp.max(scores, axis=2), 'exp')  34.6 us
  transfers between devices with their start and end apart: 7, of which 6 were waited for; matrix products, arithmetic and copies ran while one was open for 20% of the time, Pallas kernels for 0%

commit v1 on v0

v1 whole, which is shorter than its diff:
```python
import functools
import math

import jax
import jax.numpy as jnp
from jax import lax
from jax.experimental import pallas as pl
from jax.experimental.pallas import tpu as pltpu
from jax.sharding import PartitionSpec as P

HEAD_DIM = 128
TOPK = 4
CORES = 2
Z_CHIPS = 4


def attend_kernel(
    tokens, tok_rows, scale, order, moved, row_req, row_pos, key_req, key_pos, proj, out
):
    step = pl.program_id(0)
    sources = [order[step * 2], order[step * 2 + 1]]
    holders = moved.shape[0]
    columns = moved.shape[2]
    request = jnp.concatenate([row_req[s] for s in sources], axis=0)
    position = jnp.concatenate([row_pos[s] for s in sources], axis=0)
    visible = (request == key_req[...]) & (key_pos[...] <= position)
    parts = []
    for head in range(columns // HEAD_DIM):
        cols = slice(head * HEAD_DIM, (head + 1) * HEAD_DIM)
        query = jnp.concatenate([moved[s, 2 * tokens :, cols] for s in sources], axis=0)
        keys = moved[:, :tokens, cols].reshape(holders * tokens, HEAD_DIM)
        values = moved[:, tokens : 2 * tokens, cols].reshape(holders * tokens, HEAD_DIM)
        scores = (
            lax.dot_general(
                query, keys, (((1,), (1,)), ((), ())), preferred_element_type=jnp.float32
            )
            * scale
        )
        scores = jnp.where(visible, scores, -1e30)
        top = jnp.max(scores, axis=1, keepdims=True)
        weights = jnp.where(visible, jnp.exp(scores - top), 0.0)
        total = jnp.sum(weights, axis=1, keepdims=True)
        summed = jnp.dot(
            weights.astype(jnp.bfloat16), values, preferred_element_type=jnp.float32
        )
        parts.append((summed / total).astype(jnp.bfloat16))
    attention = jnp.concatenate(parts, axis=1) if len(parts) > 1 else parts[0]
    out[...] = jnp.dot(attention, proj[...], preferred_element_type=jnp.float32).astype(
        jnp.bfloat16
    )


def attend(moved, order, row_request, row_position, key_request, key_position, proj, tokens):
    holders, _, columns = moved.shape
    tok_rows = moved.shape[1] - 2 * tokens
    width = proj.shape[1]
    keys = holders * tokens
    whole = lambda *shape: pl.BlockSpec(shape, lambda i, order: (0,) * len(shape))
    return pl.pallas_call(
        functools.partial(attend_kernel, tokens, tok_rows, HEAD_DIM ** (-0.5)),
        out_shape=jax.ShapeDtypeStruct((holders * tok_rows, width), jnp.bfloat16),
        grid_spec=pltpu.PrefetchScalarGridSpec(
            num_scalar_prefetch=1,
            grid=(holders // 2,),
            in_specs=[
                whole(*moved.shape),
                whole(holders, tok_rows, 1),
                whole(holders, tok_rows, 1),
                whole(1, keys),
                whole(1, keys),
                whole(*proj.shape),
            ],
            out_specs=pl.BlockSpec((2 * tok_rows, width), lambda i, order: (i, 0)),
        ),
        compiler_params=pltpu.CompilerParams(vmem_limit_bytes=48 * 1024 * 1024),
        cost_estimate=pl.CostEstimate(
            flops=4 * holders * tok_rows * (keys * columns + columns * width),
            bytes_accessed=2 * (moved.size + proj.size + holders * tok_rows * width),
            transcendentals=holders * tok_rows * keys * columns // HEAD_DIM,
        ),
    )(
        order,
        moved,
        row_request.reshape(holders, tok_rows, 1),
        row_position.reshape(holders, tok_rows, 1),
        key_request.reshape(1, keys),
        key_position.reshape(1, keys),
        proj,
    )


def rms_normed(stream, norm_gain):
    scale_row = lax.rsqrt(jnp.mean(stream * stream, axis=1, keepdims=True) + 1e-06)
    return (stream * scale_row * norm_gain[None, :]).astype(jnp.bfloat16)


def shards(
    resid,
    queries,
    cache_key,
    cache_value,
    page_table,
    row_request,
    row_position,
    out_proj,
    norm_gain,
    expert_gate,
    expert_up,
    expert_down,
    shared_gate,
    shared_up,
    shared_down,
    shared_scalar,
    slot_expert,
    route_expert,
    route_gate,
):
    f32, bf16, i32 = jnp.float32, jnp.bfloat16, jnp.int32
    exp_count = lax.axis_size("exp")
    req_count = lax.axis_size("req")
    slot_count = exp_count * req_count
    nz, nc = math.gcd(Z_CHIPS, exp_count), CORES
    nx, ny = exp_count // nz, req_count // nc
    exp_index = lax.axis_index("exp")
    req_index = lax.axis_index("req")
    own_slot = req_index * exp_count + exp_index
    iz, ix = exp_index // nx, exp_index % nx
    iy, ic = req_index // nc, req_index % nc
    tok_rows, width = resid.shape
    pages_here, page_len, _ = cache_key.shape
    req_slots, max_pages = page_table.shape
    tokens = pages_here * page_len
    capacity = 3 * tok_rows * TOPK // slot_count

    def shift(value, along, by):
        if along in "zx":
            pairs = [
                (
                    z * nx + x,
                    ((z + by) % nz) * nx + x if along == "z" else z * nx + (x + by) % nx,
                )
                for z in range(nz)
                for x in range(nx)
            ]
            return lax.ppermute(value, "exp", pairs)
        pairs = [
            (
                y * nc + c,
                ((y + by) % ny) * nc + c if along == "y" else y * nc + (c + by) % nc,
            )
            for y in range(ny)
            for c in range(nc)
        ]
        return lax.ppermute(value, "req", pairs)

    rel_exp = jnp.stack(
        [((iz - dz) % nz) * nx + (ix - dx) % nx for dz in range(nz) for dx in range(nx)]
    ).astype(i32)
    rel_req = jnp.stack(
        [((iy - dy) % ny) * nc + (ic - dc) % nc for dy in range(ny) for dc in range(nc)]
    ).astype(i32)

    columns = width // exp_count
    by_heads = lambda a: jnp.transpose(a.reshape(-1, exp_count, columns), (1, 0, 2))
    moved = lax.all_to_all(
        jnp.concatenate([by_heads(cache_key), by_heads(cache_value), by_heads(queries)], axis=1),
        "exp",
        split_axis=0,
        concat_axis=0,
        tiled=True,
    )
    page_ids = jnp.arange(pages_here * exp_count, dtype=i32)
    hits = (page_table[None, :, :] == page_ids[:, None, None]).astype(i32)
    page_request = jnp.sum(hits * jnp.arange(req_slots, dtype=i32)[None, :, None], axis=(1, 2))
    page_slot = jnp.sum(hits * jnp.arange(max_pages, dtype=i32)[None, None, :], axis=(1, 2))
    key_position = page_slot[:, None] * page_len + jnp.arange(page_len, dtype=i32)[None, :]
    key_request = jnp.broadcast_to(page_request[:, None], key_position.shape)
    mixed = attend(
        moved, rel_exp, row_request, row_position, key_request, key_position, out_proj, tokens
    ).reshape(nz, nx, tok_rows, width)

    total = resid.astype(f32)
    for dz in reversed(range(nz)):
        line = mixed[dz, 0].astype(f32)
        for dx in range(1, nx):
            line = line + shift(mixed[dz, dx], "x", -dx).astype(f32)
        total = total + (shift(line.astype(bf16), "z", -dz).astype(f32) if dz else line)
    stream = total
    normed = rms_normed(stream, norm_gain)

    slot_ids = jnp.arange(slot_count, dtype=i32)
    own_mark = slot_ids == own_slot
    own_expert = jnp.sum(jnp.where(own_mark, slot_expert, 0))
    twins = slot_expert == own_expert
    copies = jnp.sum(twins.astype(i32))
    own_rank = jnp.sum((twins & (slot_ids < own_slot)).astype(i32))
    named = route_expert == own_expert
    all_gates = lax.all_gather(route_gate, ("req", "exp"), axis=0, tiled=True)
    row_gate = jnp.sum(jnp.where(named, all_gates, 0.0), axis=1).reshape(slot_count, tok_rows)
    mine = (
        jnp.any(named, axis=1).reshape(slot_count, tok_rows)
        & (slot_ids % copies == own_rank)[:, None]
    )
    rel_slots = (rel_req[:, None] * exp_count + rel_exp[None, :]).reshape(-1)
    chunk_rows = exp_count * tok_rows
    entries = exp_count * capacity
    row_gate = row_gate[rel_slots].reshape(req_count, chunk_rows)
    mine = mine[rel_slots].reshape(req_count, chunk_rows)
    place = jnp.cumsum(mine.astype(i32), axis=1) - 1
    pick = (
        (place[:, None, :] == jnp.arange(entries, dtype=i32)[None, :, None]) & mine[:, None, :]
    ).astype(bf16)

    piece = {}
    for dz in range(nz):
        piece[dz, 0, 0] = shift(normed, "z", dz) if dz else normed
    x_first = {dz: dz < (nz + 1) // 2 for dz in range(nz)}
    for dz in range(nz):
        if x_first[dz]:
            for dx in range(1, nx):
                piece[dz, dx, 0] = shift(piece[dz, 0, 0], "x", dx)
            for dx in range(nx):
                for dy in range(1, ny):
                    piece[dz, dx, dy] = shift(piece[dz, dx, 0], "y", dy)
        else:
            for dx in range(1, nx):
                piece[dz, dx, 0] = shift(piece[dz, 0, 0], "x", dx)
            for dy in range(1, ny):
                piece[dz, 0, dy] = shift(piece[dz, 0, 0], "y", dy)
                for dx in range(1, nx):
                    piece[dz, dx, dy] = shift(piece[dz, 0, dy], "x", dx)
    chunks = {}
    for dy in range(ny):
        chunks[dy, 0] = jnp.concatenate(
            [piece[dz, dx, dy] for dz in range(nz) for dx in range(nx)], axis=0
        )
        for dc in range(1, nc):
            chunks[dy, dc] = shift(chunks[dy, 0], "core", dc)

    def routed(dy, dc):
        index = dy * nc + dc
        rows = jnp.dot(pick[index], chunks[dy, dc], preferred_element_type=f32).astype(bf16)
        gate = jnp.dot(rows, expert_gate[0], preferred_element_type=f32)
        upper = jnp.dot(rows, expert_up[0], preferred_element_type=f32)
        hidden = (jax.nn.silu(gate) * upper).astype(bf16)
        answer = jnp.dot(hidden, expert_down[0], preferred_element_type=f32).astype(bf16)
        placed = lax.dot_general(
            pick[index], answer, (((0,), (0,)), ((), ())), preferred_element_type=f32
        )
        return placed * row_gate[index][:, None]

    own = chunks[0, 0]
    gate = jnp.dot(own, shared_gate, preferred_element_type=f32)
    upper = jnp.dot(own, shared_up, preferred_element_type=f32)
    shared_hidden = (jax.nn.silu(gate) * upper).astype(bf16)
    shared_scale = jax.nn.sigmoid(jnp.dot(own, shared_scalar, preferred_element_type=f32))
    shared = shared_scale[:, None] * jnp.dot(
        shared_hidden, shared_down, preferred_element_type=f32
    )

    sums = {}
    for dy in range(ny):
        here = routed(dy, 0)
        if dy == 0:
            here = here + shared
        for dc in range(1, nc):
            here = here + shift(routed(dy, dc).astype(bf16), "core", -dc).astype(f32)
        here = here.astype(bf16).reshape(nz, nx, tok_rows, width)
        for dz in range(nz):
            for dx in range(nx):
                sums[dz, dx, dy] = here[dz, dx]
    total = stream
    for dz in reversed(range(nz)):
        line = {}
        if x_first[dz]:
            for dx in range(nx):
                line[dx] = sums[dz, dx, 0].astype(f32)
                for dy in range(1, ny):
                    line[dx] = line[dx] + shift(sums[dz, dx, dy], "y", -dy).astype(f32)
            out = line[0]
            for dx in range(1, nx):
                out = out + shift(line[dx].astype(bf16), "x", -dx).astype(f32)
        else:
            for dy in range(ny):
                line[dy] = sums[dz, 0, dy].astype(f32)
                for dx in range(1, nx):
                    line[dy] = line[dy] + shift(sums[dz, dx, dy], "x", -dx).astype(f32)
            out = line[0]
            for dy in range(1, ny):
                out = out + shift(line[dy].astype(bf16), "y", -dy).astype(f32)
        total = total + (shift(out.astype(bf16), "z", -dz).astype(f32) if dz else out)
    return total.astype(bf16)


def solution(mesh):
    placed = (
        P(("req", "exp"), None),
        P(("req", "exp"), None),
        P(("req", "exp"), None, None),
        P(("req", "exp"), None, None),
        P("req", None),
        P("req"),
        P("req"),
        P("exp", None),
        P(),
        P(("req", "exp"), None, None),
        P(("req", "exp"), None, None),
        P(("req", "exp"), None, None),
        P(None, "exp"),
        P(None, "exp"),
        P("exp", None),
        P(),
        P(),
        P(),
        P(("req", "exp"), None),
    )
    return jax.shard_map(
        shards, mesh=mesh, in_specs=placed, out_specs=P(("req", "exp"), None), check_vma=False
    )
```

time: 620 us -> 387 us (0.62)
  waiting for transfers between devices: 354 us -> 129 us
  starting transfers between devices: 15.4 us -> 47 us
  local copies, waits for them, and re-layouts: 50.2 us -> 31.1 us
  matrix products: 92.6 us -> 77.5 us
  between operations: 15.2 us -> 1.82 us
  Pallas kernels: 0 us -> 9.13 us
  other arithmetic: 22.3 us -> 14.9 us
    reduce_scatter x3 -> x0, waiting for transfers between devices: 139 us -> none  [the longest x1 85.5 us: shards(): lax.psum_scatter(jnp.dot(attention, out_proj, preferred_element_type=jnp....]
    all_to_all x2 -> x1, waiting for transfers between devices: 166 us -> 48.2 us  [shards(): lax.all_to_all(jnp.concatenate([by_heads(cache_key), by_heads(cache_value...]
    ppermute x0 -> x41, waiting for transfers between devices: none -> 80.4 us  [the longest x25 72.5 us: shift(): return lax.ppermute(value, 'exp', pairs)]
    all_gather x0 -> x1, blocking collectives: none -> 73.1 us  [shards(): all_gates = lax.all_gather(route_gate, ('req', 'exp'), axis=0, tiled=True)]
    all_gather x2 -> x0, waiting for transfers between devices: 48.6 us -> none  [the longest x1 48.6 us: shards(): whole_queries = lax.all_gather(queries, 'exp', axis=0, tiled=True)]
    ppermute x0 -> x41, starting transfers between devices: none -> 39.6 us  [the longest x25 20.8 us: shift(): return lax.ppermute(value, 'exp', pairs)]
    unnamed x1 -> x0, blocking collectives: 34.9 us -> none
    pmax x1 -> x0, blocking collectives: 34.6 us -> none  [shards(): top = lax.pmax(jnp.max(scores, axis=2), 'exp')]
  transfers between devices with their start and end apart: 7 -> 42, of which waited for: 6 -> 18; matrix products, arithmetic and copies ran while one was open for 20% -> 27% of each run, Pallas kernels for 0% -> 0%
where the time goes in v1:
time: 387 us; the launch traced here: 383 us
  waiting for transfers between devices  129 us (33%)
  matrix products  77.5 us (20%)
  blocking collectives  73.1 us (19%)
  starting transfers between devices  47 us (12%)
  local copies, waits for them, and re-layouts  31.1 us (8%)
  other arithmetic  14.9 us (4%)
  Pallas kernels  9.13 us (2%)
    all_gather x1, blocking collectives, shards(): all_gates = lax.all_gather(route_gate, ('req', 'exp'), axis=0, tiled=True)  73.1 us
    ppermute x25, waiting for transfers between devices, shift(): return lax.ppermute(value, 'exp', pairs)  72.5 us
    all_to_all x1, waiting for transfers between devices, shards(): lax.all_to_all(jnp.concatenate([by_heads(cache_key), by_heads(cache_value...  48.2 us
    dot_general x4, matrix products, routed(): lax.dot_general(pick[index], answer, (((0,), (0,)), ((), ())), preferred_...  25.9 us
    unnamed x78, local copies, waits for them, and re-layouts  22.7 us
    ppermute x25, starting transfers between devices, shift(): return lax.ppermute(value, 'exp', pairs)  20.8 us
    ppermute x16, starting transfers between devices, shift(): return lax.ppermute(value, 'req', pairs)  18.8 us
    dot_general x4, matrix products, routed(): gate = jnp.dot(rows, expert_gate[0], preferred_element_type=f32)  14.1 us
  transfers between devices with their start and end apart: 42, of which 18 were waited for; matrix products, arithmetic and copies ran while one was open for 27% of the time, Pallas kernels for 0%

profile of v1, /device:TPU:0, one launch (start us, length us, event | category | flops | bytes accessed | tf_op | source)
XLA Modules:
  0.0 383.1 jit_solution(125713938618925110)
XLA Ops:
  5.2 7.4 %all-to-all-start = ((bf16[8,576,256]{2,1,0:T(8,128)(2,1)}), bf16[8,576,256]{2,1,0:T(8,128)(2,1)}, u32[]{:S(2)}, u32[]{:S(2)}) async-start(bf16[8,576,256]{2,1,0:T(8,128)(2,1)} %pad_maximum_fusion), calls=%async_computation | async-start | bytes 4718592 | tf_op jit(solution)/shard_map/all_to_all | solution.py:165
  18.4 48.2 %all-to-all-done.moved = bf16[8,576,256]{2,1,0:T(8,128)(2,1)} async-done(((bf16[8,576,256]{2,1,0:T(8,128)(2,1)}), bf16[8,576,256]{2,1,0:T(8,128)(2,1)}, u32[]{:S(2)}, u32[]{:S(2)}) %all-to-all-start) | async-done | bytes 2359328 | tf_op jit(solution)/shard_map/all_to_all | solution.py:165
  67.9 9.1 %shard_map.181 = bf16[512,2048]{1,0:T(8,128)(2,1)S(1)} custom-call(s32[8]{0:T(128)S(1)} %stack.50.order, bf16[8,576,256]{2,1,0:T(8,128)(2,1)} %all-to-all-done.moved, s32[8,64,1]{2,1,0:T(8,128)S(1)} %reshape.255.row_req, s32[8,64,1]{2,1,0:T(8,128)S(1)} %reshape.256.row_pos, s32[1,2048]{1,0:T(1,128)S(1)} %bitcast.233, s32[1,2048]{1,0:T(1,128)S(1)} %bitcast.232, ...), custom_call_target="tpu_custom_call" | custom-call | flops 2147483648 | bytes 5505024 | tf_op jit(solution)/shard_map/pallas_call | solution.py:59
  84.8 73.1 %all-gather = f32[32,64,4]{1,2,0:T(4,128)S(1)} all-gather(f32[1,64,4]{1,2,0:T(4,128)S(1)} %bitcast.249), channel_id=1, replica_groups=mesh['req'=4,'exp'=8] {'req','exp'}, dimensions={0}, use_global_device_ids=true | all-gather | bytes 33792 | tf_op jit(solution)/shard_map/all_gather | solution.py:198
  160.4 3.8 collective-permute-start.5
  165.3 6.4 %collective-permute-done.1 = bf16[64,2048]{1,0:T(8,128)(2,1)S(1)} collective-permute-done((bf16[64,2048]{1,0:T(8,128)(2,1)}, bf16[64,2048]{1,0:T(8,128)(2,1)S(1)}, u32[]{:S(2)}, u32[]{:S(2)}) %collective-permute-start.1) | collective-permute-done | bytes 262176 | tf_op jit(solution)/shard_map/ppermute | solution.py:145
  172.5 10.6 %collective-permute-done.3 = bf16[64,2048]{1,0:T(8,128)(2,1)} collective-permute-done((bf16[64,2048]{1,0:T(8,128)(2,1)}, bf16[64,2048]{1,0:T(8,128)(2,1)}, u32[]{:S(2)}, u32[]{:S(2)}) %collective-permute-start.3) | collective-permute-done | bytes 262176 | tf_op jit(solution)/shard_map/ppermute | solution.py:145
  190.7 4.8 %collective-permute-done.12 = bf16[64,2048]{1,0:T(8,128)(2,1)} collective-permute-done((bf16[64,2048]{1,0:T(8,128)(2,1)}, bf16[64,2048]{1,0:T(8,128)(2,1)}, u32[]{:S(2)}, u32[]{:S(2)}) %collective-permute-start.12) | collective-permute-done | bytes 262176 | tf_op jit(solution)/shard_map/ppermute | solution.py:145
  197.1 11.8 %collective-permute-done.10 = bf16[64,2048]{1,0:T(8,128)(2,1)} collective-permute-done((bf16[64,2048]{1,0:T(8,128)(2,1)}, bf16[64,2048]{1,0:T(8,128)(2,1)}, u32[]{:S(2)}, u32[]{:S(2)}) %collective-permute-start.10) | collective-permute-done | bytes 262176 | tf_op jit(solution)/shard_map/ppermute | solution.py:145
  217.1 6.9 %collective-permute-done.9 = bf16[64,2048]{1,0:T(8,128)(2,1)S(1)} collective-permute-done((bf16[64,2048]{1,0:T(8,128)(2,1)}, bf16[64,2048]{1,0:T(8,128)(2,1)S(1)}, u32[]{:S(2)}, u32[]{:S(2)}) %collective-permute-start.9) | collective-permute-done | bytes 262176 | tf_op jit(solution)/shard_map/ppermute | solution.py:145
  235.3 2.8 fusion.100
  241.9 6.8 %fusion.62 = f32[512,2048]{1,0:T(8,128)} fusion(bf16[192,1408]{1,0:T(8,128)(2,1)} %fusion.45, bf16[1,1408,2048]{2,1,0:T(8,128)(2,1)} %param.30, pred[4,192,512]{2,1,0:T(32,128)(4,1)} %copy-done.5), kind=kOutput, calls=%fused_computation.49 | convolution fusion | flops 1510342656 | bytes 10600448 | tf_op jit(solution)/shard_map/dot_general | solution.py:247
  256.9 2.8 collective-permute-done.20
  262.1 3.6 collective-permute-done.22
  268.9 3.1 convolution_convert_fusion.1
  274.4 4.2 %fusion.20 = f32[192,1408]{1,0:T(8,128)S(1)} fusion(bf16[192,2048]{1,0:T(8,128)(2,1)S(1)} %convolution_convert_fusion.2, bf16[1,2048,1408]{2,1,0:T(8,128)(2,1)} %param.28), kind=kOutput, calls=%fused_computation.22 | convolution fusion | flops 1107296256 | bytes 7634944 | tf_op jit(solution)/shard_map/dot_general | solution.py:243
  278.6 2.5 fusion.42
  281.1 6.2 %multiply_convert_fusion.1 = bf16[512,2048]{1,0:T(8,128)(2,1)} fusion(f32[512]{0:T(512)S(1)} %mul.187, bf16[192,1408]{1,0:T(8,128)(2,1)} %fusion.42, bf16[1,1408,2048]{2,1,0:T(8,128)(2,1)} %param.30, pred[4,192,512]{2,1,0:T(32,128)(4,1)} %copy-done.5), kind=kOutput, calls=%fused_computation.29 | convolution fusion | flops 1512439808 | bytes 8505344 | tf_op jit(solution)/shard_map/dot_general | solution.py:247
  290.3 4.2 %fusion.16 = f32[192,1408]{1,0:T(8,128)S(1)} fusion(bf16[192,2048]{1,0:T(8,128)(2,1)S(1)} %convolution_convert_fusion, bf16[1,2048,1408]{2,1,0:T(8,128)(2,1)} %param.28), kind=kOutput, calls=%fused_computation.18 | convolution fusion | flops 1107296256 | bytes 7634944 | tf_op jit(solution)/shard_map/dot_general | solution.py:243
  296.8 6.1 %multiply_convert_fusion = bf16[512,2048]{1,0:T(8,128)(2,1)} fusion(f32[512]{0:T(512)S(1)} %mul.197, bf16[192,1408]{1,0:T(8,128)(2,1)} %fusion.36, bf16[1,1408,2048]{2,1,0:T(8,128)(2,1)} %param.30, pred[4,192,512]{2,1,0:T(32,128)(4,1)} %copy-done.5), kind=kOutput, calls=%fused_computation.27 | convolution fusion | flops 1512439808 | bytes 8505344 | tf_op jit(solution)/shard_map/dot_general | solution.py:247
  302.9 4.3 %fusion.18 = f32[192,1408]{1,0:T(8,128)S(1)} fusion(bf16[192,2048]{1,0:T(8,128)(2,1)} %convolution_convert_fusion.1, bf16[1,2048,1408]{2,1,0:T(8,128)(2,1)} %param.28), kind=kOutput, calls=%fused_computation.20 | convolution fusion | flops 1107296256 | bytes 7634944 | tf_op jit(solution)/shard_map/dot_general | solution.py:243
  307.3 4.9 %fusion.39 = bf16[192,1408]{1,0:T(8,128)(2,1)} fusion(bf16[192,2048]{1,0:T(8,128)(2,1)S(1)} %copy-done.8, bf16[1,2048,1408]{2,1,0:T(8,128)(2,1)} %param.29, f32[192,1408]{1,0:T(8,128)S(1)} %fusion.18), kind=kOutput, calls=%fused_computation.35 | convolution fusion | flops 1108918272 | bytes 8175616 | tf_op jit(solution)/shard_map/dot_general | solution.py:244
  312.2 10.3 %add_convert_fusion.1 = bf16[512,2048]{1,0:T(8,128)(2,1)} fusion(bf16[512,2048]{1,0:T(8,128)(2,1)} %collective-permute-done.15, f32[512,2048]{1,0:T(8,128)} %fusion.62, bf16[704,2048]{1,0:T(8,128)(2,1)S(1)} %copy-done, f32[512]{0:T(512)S(1)} %add_divide_fusion, f32[512]{0:T(512)S(1)} %mul.178, f32[512,704]{0,1:T(8,128)} %fusion.100, ...), kind=kOutput, calls=%fused_computation.28 | convolution fusion | flops 2961244160 | bytes 17698816 | tf_op jit(solution)/shard_map/dot_general | solution.py:257
  322.5 6.8 %add_convert_fusion = bf16[512,2048]{1,0:T(8,128)(2,1)} fusion(bf16[512,2048]{1,0:T(8,128)(2,1)} %collective-permute-done.26, f32[512]{0:T(512)S(1)} %mul.192, bf16[192,1408]{1,0:T(8,128)(2,1)} %fusion.39, bf16[1,1408,2048]{2,1,0:T(8,128)(2,1)} %param.30, pred[4,192,512]{2,1,0:T(32,128)(4,1)} %copy-done.5), kind=kOutput, calls=%fused_computation.26 | convolution fusion | flops 1514536960 | bytes 10602496 | tf_op jit(solution)/shard_map/dot_general | solution.py:247
  336.7 3.3 collective-permute-done.27
  341.7 4.0 %collective-permute-done.31 = bf16[64,2048]{1,0:T(8,128)(2,1)S(1)} collective-permute-done((bf16[64,2048]{1,0:T(8,128)(2,1)S(1)}, bf16[64,2048]{1,0:T(8,128)(2,1)S(1)}, u32[]{:S(2)}, u32[]{:S(2)}) %collective-permute-start.31) | collective-permute-done | bytes 262176 | tf_op jit(solution)/shard_map/ppermute | solution.py:145
  348.5 2.8 collective-permute-done.16
  352.9 3.6 collective-permute-done.30
  358.0 3.0 collective-permute-done.32
  366.7 3.7 collective-permute-done.36
  371.1 3.6 collective-permute-done.29
  374.7 7.4 %collective-permute-done.33 = bf16[64,2048]{1,0:T(8,128)(2,1)S(1)} collective-permute-done((bf16[64,2048]{1,0:T(8,128)(2,1)S(1)}, bf16[64,2048]{1,0:T(8,128)(2,1)S(1)}, u32[]{:S(2)}, u32[]{:S(2)}) %collective-permute-start.33) | collective-permute-done | bytes 262176 | tf_op jit(solution)/shard_map/ppermute | solution.py:145
  (208 shorter events, 99.1 us)
Async XLA Ops:
  5.2 61.4 %all-to-all-start = ((bf16[8,576,256]{2,1,0:T(8,128)(2,1)}), bf16[8,576,256]{2,1,0:T(8,128)(2,1)}, u32[]{:S(2)}, u32[]{:S(2)}) async-start(bf16[8,576,256]{2,1,0:T(8,128)(2,1)} %pad_maximum_fusion), calls=%async_computation | async-start | bytes 4718592 | tf_op jit(solution)/shard_map/all_to_all | solution.py:165
  79.4 78.7 %collective-permute-start = (bf16[64,2048]{1,0:T(8,128)(2,1)}, bf16[64,2048]{1,0:T(8,128)(2,1)}, u32[]{:S(2)}, u32[]{:S(2)}) collective-permute-start(bf16[64,2048]{1,0:T(8,128)(2,1)} %get-tuple-element.32), channel_id=1, source_target_pairs={{0,1},{1,0},{2,3},{3,2},{4,5},{5,4},{6,7},{7,6},{8,9},{9,8},{10,11... | collective-permute-start | bytes 786440 | tf_op jit(solution)/shard_map/ppermute | solution.py:145
  80.8 77.2 %collective-permute-start.4 = (bf16[64,2048]{1,0:T(8,128)(2,1)}, bf16[64,2048]{1,0:T(8,128)(2,1)}, u32[]{:S(2)}, u32[]{:S(2)}) collective-permute-start(bf16[64,2048]{1,0:T(8,128)(2,1)} %get-tuple-element.34), channel_id=1, source_target_pairs={{0,1},{1,0},{2,3},{3,2},{4,5},{5,4},{6,7},{7,6},{8,9},{9,8},{10,11... | collective-permute-start | bytes 786440 | tf_op jit(solution)/shard_map/ppermute | solution.py:145
  81.4 76.7 %collective-permute-start.2 = (bf16[64,2048]{1,0:T(8,128)(2,1)}, bf16[64,2048]{1,0:T(8,128)(2,1)}, u32[]{:S(2)}, u32[]{:S(2)}) collective-permute-start(bf16[64,2048]{1,0:T(8,128)(2,1)} %get-tuple-element.35), channel_id=1, source_target_pairs={{0,1},{1,0},{2,3},{3,2},{4,5},{5,4},{6,7},{7,6},{8,9},{9,8},{10,11... | collective-permute-start | bytes 786440 | tf_op jit(solution)/shard_map/ppermute | solution.py:145
  160.4 11.3 %collective-permute-start.1 = (bf16[64,2048]{1,0:T(8,128)(2,1)}, bf16[64,2048]{1,0:T(8,128)(2,1)S(1)}, u32[]{:S(2)}, u32[]{:S(2)}) collective-permute-start(bf16[64,2048]{1,0:T(8,128)(2,1)} %get-tuple-element.29), channel_id=1, source_target_pairs={{0,2},{1,3},{2,4},{3,5},{4,6},{5,7},{6,0},{7,1},{8,10},{9,11},{10,... | collective-permute-start | bytes 786440 | tf_op jit(solution)/shard_map/ppermute | solution.py:145
  160.4 11.4 %collective-permute-start.5 = (bf16[64,2048]{1,0:T(8,128)(2,1)}, bf16[64,2048]{1,0:T(8,128)(2,1)}, u32[]{:S(2)}, u32[]{:S(2)}) collective-permute-start(bf16[64,2048]{1,0:T(8,128)(2,1)} %get-tuple-element.30), channel_id=1, source_target_pairs={{0,6},{1,7},{2,0},{3,1},{4,2},{5,3},{6,4},{7,5},{8,14},{9,15},{10,... | collective-permute-start | bytes 786440 | tf_op jit(solution)/shard_map/ppermute | solution.py:145
  164.3 18.8 %collective-permute-start.3 = (bf16[64,2048]{1,0:T(8,128)(2,1)}, bf16[64,2048]{1,0:T(8,128)(2,1)}, u32[]{:S(2)}, u32[]{:S(2)}) collective-permute-start(bf16[64,2048]{1,0:T(8,128)(2,1)} %get-tuple-element.31), channel_id=1, source_target_pairs={{0,4},{1,5},{2,6},{3,7},{4,0},{5,1},{6,2},{7,3},{8,12},{9,13},{10,... | collective-permute-start | bytes 786440 | tf_op jit(solution)/shard_map/ppermute | solution.py:145
  185.7 23.2 %collective-permute-start.10 = (bf16[64,2048]{1,0:T(8,128)(2,1)}, bf16[64,2048]{1,0:T(8,128)(2,1)}, u32[]{:S(2)}, u32[]{:S(2)}) collective-permute-start(bf16[64,2048]{1,0:T(8,128)(2,1)} %get-tuple-element.10), channel_id=1, source_target_pairs={{0,4},{1,5},{2,6},{3,7},{4,0},{5,1},{6,2},{7,3},{8,12},{9,13},{10,... | collective-permute-start | bytes 786440 | tf_op jit(solution)/shard_map/ppermute | solution.py:145
  185.7 23.4 %collective-permute-start.8 = (bf16[64,2048]{1,0:T(8,128)(2,1)}, bf16[64,2048]{1,0:T(8,128)(2,1)}, u32[]{:S(2)}, u32[]{:S(2)}) collective-permute-start(bf16[64,2048]{1,0:T(8,128)(2,1)} %get-tuple-element.10), channel_id=1, source_target_pairs={{0,2},{1,3},{2,4},{3,5},{4,6},{5,7},{6,0},{7,1},{8,10},{9,11},{10,... | collective-permute-start | bytes 786440 | tf_op jit(solution)/shard_map/ppermute | solution.py:145
  187.7 23.3 %collective-permute-start.7 = (bf16[64,2048]{1,0:T(8,128)(2,1)}, bf16[64,2048]{1,0:T(8,128)(2,1)}, u32[]{:S(2)}, u32[]{:S(2)}) collective-permute-start(bf16[64,2048]{1,0:T(8,128)(2,1)} %get-tuple-element.10), channel_id=1, source_target_pairs={{0,1},{1,0},{2,3},{3,2},{4,5},{5,4},{6,7},{7,6},{8,9},{9,8},{10,11... | collective-permute-start | bytes 786440 | tf_op jit(solution)/shard_map/ppermute | solution.py:145
  189.1 26.8 %collective-permute-start.17 = (bf16[64,2048]{1,0:T(8,128)(2,1)}, bf16[64,2048]{1,0:T(8,128)(2,1)S(1)}, u32[]{:S(2)}, u32[]{:S(2)}) collective-permute-start(bf16[64,2048]{1,0:T(8,128)(2,1)} %get-tuple-element.10), channel_id=1, source_target_pairs={{0,16},{8,24},{16,0},{24,8},{1,17},{9,25},{17,1},{25,9},{2,18},{10... | collective-permute-start | bytes 786440 | tf_op jit(solution)/shard_map/ppermute | solution.py:154
  195.5 55.4 %collective-permute-start.23 = (bf16[64,2048]{1,0:T(8,128)(2,1)}, bf16[64,2048]{1,0:T(8,128)(2,1)}, u32[]{:S(2)}, u32[]{:S(2)}) collective-permute-start(bf16[64,2048]{1,0:T(8,128)(2,1)} %collective-permute-done.12), channel_id=1, source_target_pairs={{0,16},{8,24},{16,0},{24,8},{1,17},{9,25},{17,1},{25,9},{2,18},{10... | collective-permute-start | bytes 786440 | tf_op jit(solution)/shard_map/ppermute | solution.py:154
  208.9 23.2 %collective-permute-start.13 = (bf16[64,2048]{1,0:T(8,128)(2,1)}, bf16[64,2048]{1,0:T(8,128)(2,1)S(1)}, u32[]{:S(2)}, u32[]{:S(2)}) collective-permute-start(bf16[64,2048]{1,0:T(8,128)(2,1)} %collective-permute-done.12), channel_id=1, source_target_pairs={{0,1},{1,0},{2,3},{3,2},{4,5},{5,4},{6,7},{7,6},{8,9},{9,8},{10,11... | collective-permute-start | bytes 786440 | tf_op jit(solution)/shard_map/ppermute | solution.py:145
  209.1 42.4 %collective-permute-start.21 = (bf16[64,2048]{1,0:T(8,128)(2,1)}, bf16[64,2048]{1,0:T(8,128)(2,1)}, u32[]{:S(2)}, u32[]{:S(2)}) collective-permute-start(bf16[64,2048]{1,0:T(8,128)(2,1)} %collective-permute-done.10), channel_id=1, source_target_pairs={{0,16},{8,24},{16,0},{24,8},{1,17},{9,25},{17,1},{25,9},{2,18},{10... | collective-permute-start | bytes 786440 | tf_op jit(solution)/shard_map/ppermute | solution.py:154
  211.0 13.0 %collective-permute-start.9 = (bf16[64,2048]{1,0:T(8,128)(2,1)}, bf16[64,2048]{1,0:T(8,128)(2,1)S(1)}, u32[]{:S(2)}, u32[]{:S(2)}) collective-permute-start(bf16[64,2048]{1,0:T(8,128)(2,1)} %collective-permute-done.8), channel_id=1, source_target_pairs={{0,1},{1,0},{2,3},{3,2},{4,5},{5,4},{6,7},{7,6},{8,9},{9,8},{10,11... | collective-permute-start | bytes 786440 | tf_op jit(solution)/shard_map/ppermute | solution.py:145
  215.9 12.2 %collective-permute-start.11 = (bf16[64,2048]{1,0:T(8,128)(2,1)}, bf16[64,2048]{1,0:T(8,128)(2,1)S(1)}, u32[]{:S(2)}, u32[]{:S(2)}) collective-permute-start(bf16[64,2048]{1,0:T(8,128)(2,1)} %collective-permute-done.10), channel_id=1, source_target_pairs={{0,1},{1,0},{2,3},{3,2},{4,5},{5,4},{6,7},{7,6},{8,9},{9,8},{10,11... | collective-permute-start | bytes 786440 | tf_op jit(solution)/shard_map/ppermute | solution.py:145
  224.0 31.2 %collective-permute-start.19 = (bf16[64,2048]{1,0:T(8,128)(2,1)}, bf16[64,2048]{1,0:T(8,128)(2,1)}, u32[]{:S(2)}, u32[]{:S(2)}) collective-permute-start(bf16[64,2048]{1,0:T(8,128)(2,1)} %collective-permute-done.8), channel_id=1, source_target_pairs={{0,16},{8,24},{16,0},{24,8},{1,17},{9,25},{17,1},{25,9},{2,18},{10... | collective-permute-start | bytes 786440 | tf_op jit(solution)/shard_map/ppermute | solution.py:154
  228.1 23.9 %collective-permute-start.18 = (bf16[64,2048]{1,0:T(8,128)(2,1)}, bf16[64,2048]{1,0:T(8,128)(2,1)}, u32[]{:S(2)}, u32[]{:S(2)}) collective-permute-start(bf16[64,2048]{1,0:T(8,128)(2,1)} %collective-permute-done.7), channel_id=1, source_target_pairs={{0,16},{8,24},{16,0},{24,8},{1,17},{9,25},{17,1},{25,9},{2,18},{10... | collective-permute-start | bytes 786440 | tf_op jit(solution)/shard_map/ppermute | solution.py:154
  232.9 39.1 %collective-permute-start.14 = (bf16[512,2048]{1,0:T(8,128)(2,1)}, bf16[512,2048]{1,0:T(8,128)(2,1)}, u32[]{:S(2)}, u32[]{:S(2)}) collective-permute-start(bf16[512,2048]{1,0:T(8,128)(2,1)} %constant_dynamic-update-slice_fusion), channel_id=1, source_target_pairs={{0,8},{8,0},{16,24},{24,16},{1,9},{9,1},{17,25},{25,17},{2,10},{10... | collective-permute-start | bytes 6291464 | tf_op jit(solution)/shard_map/ppermute | solution.py:154
  251.5 16.7 %collective-permute-start.24 = (bf16[64,2048]{1,0:T(8,128)(2,1)}, bf16[64,2048]{1,0:T(8,128)(2,1)S(1)}, u32[]{:S(2)}, u32[]{:S(2)}) collective-permute-start(bf16[64,2048]{1,0:T(8,128)(2,1)} %collective-permute-done.23), channel_id=1, source_target_pairs={{0,1},{1,0},{2,3},{3,2},{4,5},{5,4},{6,7},{7,6},{8,9},{9,8},{10,11... | collective-permute-start | bytes 786440 | tf_op jit(solution)/shard_map/ppermute | solution.py:145
  252.0 13.7 %collective-permute-start.22 = (bf16[64,2048]{1,0:T(8,128)(2,1)}, bf16[64,2048]{1,0:T(8,128)(2,1)S(1)}, u32[]{:S(2)}, u32[]{:S(2)}) collective-permute-start(bf16[64,2048]{1,0:T(8,128)(2,1)} %collective-permute-done.21), channel_id=1, source_target_pairs={{0,1},{1,0},{2,3},{3,2},{4,5},{5,4},{6,7},{7,6},{8,9},{9,8},{10,11... | collective-permute-start | bytes 786440 | tf_op jit(solution)/shard_map/ppermute | solution.py:145
  268.9 18.9 %collective-permute-start.25 = (bf16[512,2048]{1,0:T(8,128)(2,1)}, bf16[512,2048]{1,0:T(8,128)(2,1)}, u32[]{:S(2)}, u32[]{:S(2)}) collective-permute-start(bf16[512,2048]{1,0:T(8,128)(2,1)} %constant_dynamic-update-slice_fusion.8), channel_id=1, source_target_pairs={{0,8},{8,0},{16,24},{24,16},{1,9},{9,1},{17,25},{25,17},{2,10},{10... | collective-permute-start | bytes 6291464 | tf_op jit(solution)/shard_map/ppermute | solution.py:154
  287.4 24.8 %collective-permute-start.15 = (bf16[512,2048]{1,0:T(8,128)(2,1)}, bf16[512,2048]{1,0:T(8,128)(2,1)}, u32[]{:S(2)}, u32[]{:S(2)}) collective-permute-start(bf16[512,2048]{1,0:T(8,128)(2,1)} %multiply_convert_fusion.1), channel_id=1, source_target_pairs={{0,8},{8,0},{16,24},{24,16},{1,9},{9,1},{17,25},{25,17},{2,10},{10... | collective-permute-start | bytes 6291464 | tf_op jit(solution)/shard_map/ppermute | solution.py:154
  302.9 19.6 %collective-permute-start.26 = (bf16[512,2048]{1,0:T(8,128)(2,1)}, bf16[512,2048]{1,0:T(8,128)(2,1)}, u32[]{:S(2)}, u32[]{:S(2)}) collective-permute-start(bf16[512,2048]{1,0:T(8,128)(2,1)} %multiply_convert_fusion), channel_id=1, source_target_pairs={{0,8},{8,0},{16,24},{24,16},{1,9},{9,1},{17,25},{25,17},{2,10},{10... | collective-permute-start | bytes 6291464 | tf_op jit(solution)/shard_map/ppermute | solution.py:154
  331.4 14.2 %collective-permute-start.31 = (bf16[64,2048]{1,0:T(8,128)(2,1)S(1)}, bf16[64,2048]{1,0:T(8,128)(2,1)S(1)}, u32[]{:S(2)}, u32[]{:S(2)}) collective-permute-start(bf16[64,2048]{1,0:T(8,128)(2,1)S(1)} %get-tuple-element.28), channel_id=1, source_target_pairs={{0,1},{1,0},{2,3},{3,2},{4,5},{5,4},{6,7},{7,6},{8,9},{9,8},{10,11... | collective-permute-start | bytes 786440 | tf_op jit(solution)/shard_map/ppermute | solution.py:145
  333.0 18.3 %collective-permute-start.16 = (bf16[64,2048]{1,0:T(8,128)(2,1)S(1)}, bf16[64,2048]{1,0:T(8,128)(2,1)S(1)}, u32[]{:S(2)}, u32[]{:S(2)}) collective-permute-start(bf16[64,2048]{1,0:T(8,128)(2,1)S(1)} %get-tuple-element.19), channel_id=1, source_target_pairs={{0,1},{1,0},{2,3},{3,2},{4,5},{5,4},{6,7},{7,6},{8,9},{9,8},{10,11... | collective-permute-start | bytes 786440 | tf_op jit(solution)/shard_map/ppermute | solution.py:145
  333.6 22.9 %collective-permute-start.30 = (bf16[64,2048]{1,0:T(8,128)(2,1)S(1)}, bf16[64,2048]{1,0:T(8,128)(2,1)S(1)}, u32[]{:S(2)}, u32[]{:S(2)}) collective-permute-start(bf16[64,2048]{1,0:T(8,128)(2,1)S(1)} %get-tuple-element.20), channel_id=1, source_target_pairs={{0,1},{1,0},{2,3},{3,2},{4,5},{5,4},{6,7},{7,6},{8,9},{9,8},{10,11... | collective-permute-start | bytes 786440 | tf_op jit(solution)/shard_map/ppermute | solution.py:145
  335.1 22.9 %collective-permute-start.39 = (bf16[64,2048]{1,0:T(8,128)(2,1)S(1)}, bf16[64,2048]{1,0:T(8,128)(2,1)S(1)}, u32[]{:S(2)}, u32[]{:S(2)}) collective-permute-start(bf16[64,2048]{1,0:T(8,128)(2,1)S(1)} %get-tuple-element.24), channel_id=1, source_target_pairs={{0,16},{8,24},{16,0},{24,8},{1,17},{9,25},{17,1},{25,9},{2,18},{10... | collective-permute-start | bytes 786440 | tf_op jit(solution)/shard_map/ppermute | solution.py:154
  340.1 18.0 %collective-permute-start.35 = (bf16[64,2048]{1,0:T(8,128)(2,1)S(1)}, bf16[64,2048]{1,0:T(8,128)(2,1)S(1)}, u32[]{:S(2)}, u32[]{:S(2)}) collective-permute-start(bf16[64,2048]{1,0:T(8,128)(2,1)S(1)} %get-tuple-element.26), channel_id=1, source_target_pairs={{0,16},{8,24},{16,0},{24,8},{1,17},{9,25},{17,1},{25,9},{2,18},{10... | collective-permute-start | bytes 786440 | tf_op jit(solution)/shard_map/ppermute | solution.py:154
  346.8 11.2 %collective-permute-start.28 = (bf16[64,2048]{1,0:T(8,128)(2,1)S(1)}, bf16[64,2048]{1,0:T(8,128)(2,1)S(1)}, u32[]{:S(2)}, u32[]{:S(2)}) collective-permute-start(bf16[64,2048]{1,0:T(8,128)(2,1)S(1)} %get-tuple-element.21), channel_id=1, source_target_pairs={{0,16},{8,24},{16,0},{24,8},{1,17},{9,25},{17,1},{25,9},{2,18},{10... | collective-permute-start | bytes 786440 | tf_op jit(solution)/shard_map/ppermute | solution.py:154
  366.7 15.4 %collective-permute-start.33 = (bf16[64,2048]{1,0:T(8,128)(2,1)S(1)}, bf16[64,2048]{1,0:T(8,128)(2,1)S(1)}, u32[]{:S(2)}, u32[]{:S(2)}) collective-permute-start(bf16[64,2048]{1,0:T(8,128)(2,1)S(1)} %get-tuple-element.18), channel_id=1, source_target_pairs={{0,4},{1,5},{2,6},{3,7},{4,0},{5,1},{6,2},{7,3},{8,12},{9,13},{10,... | collective-permute-start | bytes 786440 | tf_op jit(solution)/shard_map/ppermute | solution.py:145
  370.5 11.6 %collective-permute-start.37 = (bf16[64,2048]{1,0:T(8,128)(2,1)S(1)}, bf16[64,2048]{1,0:T(8,128)(2,1)S(1)}, u32[]{:S(2)}, u32[]{:S(2)}) collective-permute-start(bf16[64,2048]{1,0:T(8,128)(2,1)S(1)} %fusion.77), channel_id=1, source_target_pairs={{0,6},{1,7},{2,0},{3,1},{4,2},{5,3},{6,4},{7,5},{8,14},{9,15},{10,... | collective-permute-start | bytes 786440 | tf_op jit(solution)/shard_map/ppermute | solution.py:145
  (40 other events, 665.5 us)

commit v2 on v1

--- a/solution.py
+++ b/solution.py
@@ -52,16 +52,17 @@
 
 def attend(moved, order, row_request, row_position, key_request, key_position, proj, tokens):
     holders, _, columns = moved.shape
+    blocks = order.shape[0]
     tok_rows = moved.shape[1] - 2 * tokens
     width = proj.shape[1]
     keys = holders * tokens
     whole = lambda *shape: pl.BlockSpec(shape, lambda i, order: (0,) * len(shape))
     return pl.pallas_call(
         functools.partial(attend_kernel, tokens, tok_rows, HEAD_DIM ** (-0.5)),
-        out_shape=jax.ShapeDtypeStruct((holders * tok_rows, width), jnp.bfloat16),
+        out_shape=jax.ShapeDtypeStruct((blocks * tok_rows, width), jnp.bfloat16),
         grid_spec=pltpu.PrefetchScalarGridSpec(
             num_scalar_prefetch=1,
-            grid=(holders // 2,),
+            grid=(blocks // 2,),
             in_specs=[
                 whole(*moved.shape),
                 whole(holders, tok_rows, 1),
@@ -74,9 +75,9 @@
         ),
         compiler_params=pltpu.CompilerParams(vmem_limit_bytes=48 * 1024 * 1024),
         cost_estimate=pl.CostEstimate(
-            flops=4 * holders * tok_rows * (keys * columns + columns * width),
-            bytes_accessed=2 * (moved.size + proj.size + holders * tok_rows * width),
-            transcendentals=holders * tok_rows * keys * columns // HEAD_DIM,
+            flops=2 * blocks * tok_rows * columns * (2 * keys + width),
+            bytes_accessed=2 * (moved.size + proj.size + blocks * tok_rows * width),
+            transcendentals=blocks * tok_rows * keys * columns // HEAD_DIM,
         ),
     )(
         order,
@@ -86,6 +87,163 @@
         key_request.reshape(1, keys),
         key_position.reshape(1, keys),
         proj,
+    )
+
+
+def join_kernel(count, *refs):
+    parts, out, sems = refs[:count], refs[count], refs[count + 1]
+    rows = parts[0].shape[0]
+    copies = [
+        pltpu.make_async_copy(part, out.at[pl.ds(i * rows, rows)], sems.at[i])
+        for i, part in enumerate(parts)
+    ]
+    for copy in copies:
+        copy.start()
+    for copy in copies:
+        copy.wait()
+
+
+def join(parts):
+    rows, width = parts[0].shape
+    any_spec = pl.BlockSpec(memory_space=pl.ANY)
+    return pl.pallas_call(
+        functools.partial(join_kernel, len(parts)),
+        out_shape=jax.ShapeDtypeStruct((len(parts) * rows, width), parts[0].dtype),
+        in_specs=[any_spec] * len(parts),
+        out_specs=any_spec,
+        scratch_shapes=[pltpu.SemaphoreType.DMA((len(parts),))],
+        cost_estimate=pl.CostEstimate(
+            flops=0, bytes_accessed=4 * len(parts) * rows * width, transcendentals=0
+        ),
+    )(*parts)
+
+
+def silu(value):
+    return value / (1.0 + jnp.exp(-value))
+
+
+def shared_kernel(rows, scalar, gate_w, up_w, down_w, out, gate_v, up_v, down_v, sems):
+    copies = [
+        pltpu.make_async_copy(src, dst, sems.at[i])
+        for i, (src, dst) in enumerate(((gate_w, gate_v), (up_w, up_v), (down_w, down_v)))
+    ]
+    for copy in copies:
+        copy.start()
+    block = rows[...]
+    logit = jnp.sum(
+        block.astype(jnp.float32) * scalar[...].astype(jnp.float32), axis=1, keepdims=True
+    )
+    scale = 1.0 / (1.0 + jnp.exp(-logit))
+    copies[0].wait()
+    gate = jnp.dot(block, gate_v[...], preferred_element_type=jnp.float32)
+    copies[1].wait()
+    upper = jnp.dot(block, up_v[...], preferred_element_type=jnp.float32)
+    hidden = (silu(gate) * upper).astype(jnp.bfloat16)
+    copies[2].wait()
+    result = jnp.dot(hidden, down_v[...], preferred_element_type=jnp.float32)
+    out[...] = (scale * result).astype(jnp.bfloat16)
+
+
+def shared_expert(rows, scalar, gate_w, up_w, down_w):
+    any_spec = pl.BlockSpec(memory_space=pl.ANY)
+    vmem = pl.BlockSpec(memory_space=pltpu.VMEM)
+    return pl.pallas_call(
+        shared_kernel,
+        out_shape=jax.ShapeDtypeStruct(rows.shape, jnp.bfloat16),
+        in_specs=[vmem, vmem, any_spec, any_spec, any_spec],
+        out_specs=vmem,
+        scratch_shapes=[
+            pltpu.VMEM(gate_w.shape, jnp.bfloat16),
+            pltpu.VMEM(up_w.shape, jnp.bfloat16),
+            pltpu.VMEM(down_w.shape, jnp.bfloat16),
+            pltpu.SemaphoreType.DMA((3,)),
+        ],
+        compiler_params=pltpu.CompilerParams(vmem_limit_bytes=48 * 1024 * 1024),
+        cost_estimate=pl.CostEstimate(
+            flops=6 * rows.shape[0] * gate_w.size,
+            bytes_accessed=6 * gate_w.size + 4 * rows.size,
+            transcendentals=rows.shape[0] * gate_w.shape[1],
+        ),
+    )(rows, scalar.reshape(1, -1), gate_w, up_w, down_w)
+
+
+def routed_kernel(
+    count, entries, *refs
+):
+    chunks, refs = refs[:count], refs[count:]
+    place_row, place_col, row_gate, extra, gate_w, up_w, down_w = refs[:7]
+    outs, refs = refs[7 : 7 + count], refs[7 + count :]
+    packed, gate_v, up_v, down_v, sems = refs
+    copies = [
+        pltpu.make_async_copy(src.at[0], dst, sems.at[i])
+        for i, (src, dst) in enumerate(((gate_w, gate_v), (up_w, up_v), (down_w, down_v)))
+    ]
+    for copy in copies:
+        copy.start()
+    size = chunks[0].shape[0]
+    for c in range(count):
+        wanted = lax.broadcasted_iota(jnp.int32, (entries, size), 0)
+        pick = jnp.where(place_row[c] == wanted, 1.0, 0.0).astype(jnp.bfloat16)
+        packed[c * entries : (c + 1) * entries, :] = jnp.dot(
+            pick, chunks[c][...], preferred_element_type=jnp.float32
+        ).astype(jnp.bfloat16)
+    copies[0].wait()
+    gate = jnp.dot(packed[...], gate_v[...], preferred_element_type=jnp.float32)
+    copies[1].wait()
+    upper = jnp.dot(packed[...], up_v[...], preferred_element_type=jnp.float32)
+    hidden = (silu(gate) * upper).astype(jnp.bfloat16)
+    copies[2].wait()
+    answer = jnp.dot(hidden, down_v[...], preferred_element_type=jnp.float32).astype(
+        jnp.bfloat16
+    )
+    for c in range(count):
+        wanted = lax.broadcasted_iota(jnp.int32, (size, entries), 1)
+        put = jnp.where(place_col[c] == wanted, 1.0, 0.0).astype(jnp.bfloat16)
+        placed = row_gate[c] * jnp.dot(
+            put,
+            answer[c * entries : (c + 1) * entries, :],
+            preferred_element_type=jnp.float32,
+        )
+        if c == 0 and extra.shape[0] == size:
+            placed = placed + extra[...].astype(jnp.float32)
+        outs[c][...] = placed.astype(jnp.bfloat16)
+
+
+def routed_expert(chunks, place, row_gate, extra, gate_w, up_w, down_w, entries):
+    count = len(chunks)
+    size, width = chunks[0].shape
+    hidden = gate_w.shape[2]
+    any_spec = pl.BlockSpec(memory_space=pl.ANY)
+    vmem = pl.BlockSpec(memory_space=pltpu.VMEM)
+    if extra is None:
+        extra = jnp.zeros((8, 128), jnp.bfloat16)
+    return pl.pallas_call(
+        functools.partial(routed_kernel, count, entries),
+        out_shape=[jax.ShapeDtypeStruct((size, width), jnp.bfloat16)] * count,
+        in_specs=[vmem] * (count + 4) + [any_spec] * 3,
+        out_specs=[vmem] * count,
+        scratch_shapes=[
+            pltpu.VMEM((count * entries, width), jnp.bfloat16),
+            pltpu.VMEM((width, hidden), jnp.bfloat16),
+            pltpu.VMEM((width, hidden), jnp.bfloat16),
+            pltpu.VMEM((hidden, width), jnp.bfloat16),
+            pltpu.SemaphoreType.DMA((3,)),
+        ],
+        compiler_params=pltpu.CompilerParams(vmem_limit_bytes=56 * 1024 * 1024),
+        cost_estimate=pl.CostEstimate(
+            flops=2 * count * entries * (3 * gate_w.size + 2 * size * width),
+            bytes_accessed=6 * gate_w.size + 4 * count * size * width,
+            transcendentals=count * entries * hidden,
+        ),
+    )(
+        *chunks,
+        place.reshape(count, 1, size),
+        place.reshape(count, size, 1),
+        row_gate.reshape(count, size, 1),
+        extra,
+        gate_w,
+        up_w,
+        down_w,
     )
 
 
@@ -175,41 +333,44 @@
     page_slot = jnp.sum(hits * jnp.arange(max_pages, dtype=i32)[None, None, :], axis=(1, 2))
     key_position = page_slot[:, None] * page_len + jnp.arange(page_len, dtype=i32)[None, :]
     key_request = jnp.broadcast_to(page_request[:, None], key_position.shape)
-    mixed = attend(
-        moved, rel_exp, row_request, row_position, key_request, key_position, out_proj, tokens
-    ).reshape(nz, nx, tok_rows, width)
-
-    total = resid.astype(f32)
-    for dz in reversed(range(nz)):
-        line = mixed[dz, 0].astype(f32)
-        for dx in range(1, nx):
-            line = line + shift(mixed[dz, dx], "x", -dx).astype(f32)
-        total = total + (shift(line.astype(bf16), "z", -dz).astype(f32) if dz else line)
-    stream = total
-    normed = rms_normed(stream, norm_gain)
-
     slot_ids = jnp.arange(slot_count, dtype=i32)
     own_mark = slot_ids == own_slot
     own_expert = jnp.sum(jnp.where(own_mark, slot_expert, 0))
     twins = slot_expert == own_expert
     copies = jnp.sum(twins.astype(i32))
     own_rank = jnp.sum((twins & (slot_ids < own_slot)).astype(i32))
-    named = route_expert == own_expert
-    all_gates = lax.all_gather(route_gate, ("req", "exp"), axis=0, tiled=True)
-    row_gate = jnp.sum(jnp.where(named, all_gates, 0.0), axis=1).reshape(slot_count, tok_rows)
-    mine = (
-        jnp.any(named, axis=1).reshape(slot_count, tok_rows)
-        & (slot_ids % copies == own_rank)[:, None]
-    )
+    gates = jnp.transpose(route_gate)
+    gates = jnp.stack([shift(gates, "z", dz) if dz else gates for dz in range(nz)])
+    gates = jnp.stack([shift(gates, "x", dx) if dx else gates for dx in range(nx)], axis=1)
+    gates = jnp.stack([shift(gates, "y", dy) if dy else gates for dy in range(ny)])
+    gates = jnp.stack([shift(gates, "core", dc) if dc else gates for dc in range(nc)], axis=1)
+    gates = gates.reshape(slot_count, TOPK, tok_rows)
     rel_slots = (rel_req[:, None] * exp_count + rel_exp[None, :]).reshape(-1)
+    named = (route_expert == own_expert).reshape(slot_count, tok_rows, TOPK)[rel_slots]
+    named = jnp.transpose(named, (0, 2, 1))
     chunk_rows = exp_count * tok_rows
-    entries = exp_count * capacity
-    row_gate = row_gate[rel_slots].reshape(req_count, chunk_rows)
-    mine = mine[rel_slots].reshape(req_count, chunk_rows)
-    place = jnp.cumsum(mine.astype(i32), axis=1) - 1
-    pick = (
-        (place[:, None, :] == jnp.arange(entries, dtype=i32)[None, :, None]) & mine[:, None, :]
-    ).astype(bf16)
+    entries = -(-exp_count * capacity // 16) * 16
+    row_gate = jnp.sum(jnp.where(named, gates, 0.0), axis=1).reshape(ny, nc, chunk_rows)
+    mine = jnp.any(named, axis=1) & (rel_slots % copies == own_rank)[:, None]
+    mine = mine.reshape(ny, nc, chunk_rows)
+    place = jnp.where(mine, jnp.cumsum(mine.astype(i32), axis=2) - 1, -1)
+    moved, place, row_gate = lax.optimization_barrier((moved, place, row_gate))
+
+    half = exp_count // 2
+    mixed = [
+        attend(moved, o, row_request, row_position, key_request, key_position, out_proj, tokens)
+        .reshape(nz // 2, nx, tok_rows, width)
+        for o in (rel_exp[:half], rel_exp[half:])
+    ]
+
+    total = resid.astype(f32)
+    for dz in reversed(range(nz)):
+        line = mixed[dz // (nz // 2)][dz % (nz // 2), 0].astype(f32)
+        for dx in range(1, nx):
+            line = line + shift(mixed[dz // (nz // 2)][dz % (nz // 2), dx], "x", -dx).astype(f32)
+        total = total + (shift(line.astype(bf16), "z", -dz).astype(f32) if dz else line)
+    stream = total
+    normed = rms_normed(stream, norm_gain)
 
     piece = {}
     for dz in range(nz):
@@ -231,40 +392,30 @@
                     piece[dz, dx, dy] = shift(piece[dz, 0, dy], "x", dx)
     chunks = {}
     for dy in range(ny):
-        chunks[dy, 0] = jnp.concatenate(
-            [piece[dz, dx, dy] for dz in range(nz) for dx in range(nx)], axis=0
-        )
+        chunks[dy, 0] = join([piece[dz, dx, dy] for dz in range(nz) for dx in range(nx)])
         for dc in range(1, nc):
             chunks[dy, dc] = shift(chunks[dy, 0], "core", dc)
 
-    def routed(dy, dc):
-        index = dy * nc + dc
-        rows = jnp.dot(pick[index], chunks[dy, dc], preferred_element_type=f32).astype(bf16)
-        gate = jnp.dot(rows, expert_gate[0], preferred_element_type=f32)
-        upper = jnp.dot(rows, expert_up[0], preferred_element_type=f32)
-        hidden = (jax.nn.silu(gate) * upper).astype(bf16)
-        answer = jnp.dot(hidden, expert_down[0], preferred_element_type=f32).astype(bf16)
-        placed = lax.dot_general(
-            pick[index], answer, (((0,), (0,)), ((), ())), preferred_element_type=f32
-        )
-        return placed * row_gate[index][:, None]
-
-    own = chunks[0, 0]
-    gate = jnp.dot(own, shared_gate, preferred_element_type=f32)
-    upper = jnp.dot(own, shared_up, preferred_element_type=f32)
-    shared_hidden = (jax.nn.silu(gate) * upper).astype(bf16)
-    shared_scale = jax.nn.sigmoid(jnp.dot(own, shared_scalar, preferred_element_type=f32))
-    shared = shared_scale[:, None] * jnp.dot(
-        shared_hidden, shared_down, preferred_element_type=f32
-    )
-
     sums = {}
     for dy in range(ny):
-        here = routed(dy, 0)
+        extra = None
         if dy == 0:
-            here = here + shared
+            extra = shared_expert(
+                chunks[0, 0], shared_scalar, shared_gate, shared_up, shared_down
+            )
+        answers = routed_expert(
+            [chunks[dy, dc] for dc in range(nc)],
+            place[dy],
+            row_gate[dy],
+            extra,
+            expert_gate,
+            expert_up,
+            expert_down,
+            entries,
+        )
+        here = answers[0].astype(f32)
         for dc in range(1, nc):
-            here = here + shift(routed(dy, dc).astype(bf16), "core", -dc).astype(f32)
+            here = here + shift(answers[dc], "core", -dc).astype(f32)
         here = here.astype(bf16).reshape(nz, nx, tok_rows, width)
         for dz in range(nz):
             for dx in range(nx):

time: 387 us -> 445 us (1.15)
  Pallas kernels: 9.13 us -> 178 us
  matrix products: 77.5 us -> 0 us
  blocking collectives: 73.1 us -> 0 us
  starting transfers between devices: 47 us -> 73 us
  waiting for transfers between devices: 129 us -> 150 us
    pallas_call x0 -> x5, Pallas kernels: none -> 170 us  [the longest x2 129 us: join(): pl.pallas_call(functools.partial(join_kernel, len(parts)), out_shape=jax....]
    dot_general x19 -> x0, matrix products: 77.5 us -> none  [the longest x4 25.9 us: routed(): lax.dot_general(pick[index], answer, (((0,), (0,)), ((), ())), preferred_...]
    all_gather x1 -> x0, blocking collectives: 73.1 us -> none  [shards(): all_gates = lax.all_gather(route_gate, ('req', 'exp'), axis=0, tiled=True)]
    all_to_all x1, waiting for transfers between devices: 48.2 us -> 0.01 us  [shards(): lax.all_to_all(jnp.concatenate([by_heads(cache_key), by_heads(cache_value...]
    ppermute x25 -> x29, waiting for transfers between devices: 72.5 us -> 113 us  [shift(): return lax.ppermute(value, 'exp', pairs)]
    ppermute x16 -> x18, waiting for transfers between devices: 7.89 us -> 36.8 us  [shift(): return lax.ppermute(value, 'req', pairs)]
    ppermute x25 -> x29, starting transfers between devices: 20.8 us -> 46.9 us  [shift(): return lax.ppermute(value, 'exp', pairs)]
    unnamed x78 -> x70, local copies, waits for them, and re-layouts: 22.7 us -> 16.5 us
  transfers between devices with their start and end apart: 42 -> 48, of which waited for: 18 -> 28; matrix products, arithmetic and copies ran while one was open for 27% -> 6% of each run, Pallas kernels for 0% -> 25%
where the time goes in v2:
time: 445 us; the launch traced here: 441 us
  Pallas kernels  178 us (40%)
  waiting for transfers between devices  150 us (34%)
  starting transfers between devices  73 us (16%)
  local copies, waits for them, and re-layouts  26.8 us (6%)
  other arithmetic  11.7 us (3%)
    pallas_call x2, Pallas kernels, join(): pl.pallas_call(functools.partial(join_kernel, len(parts)), out_shape=jax....  129 us
    ppermute x29, waiting for transfers between devices, shift(): return lax.ppermute(value, 'exp', pairs)  113 us
    ppermute x29, starting transfers between devices, shift(): return lax.ppermute(value, 'exp', pairs)  46.9 us
    ppermute x18, waiting for transfers between devices, shift(): return lax.ppermute(value, 'req', pairs)  36.8 us
    pallas_call x2, Pallas kernels, routed_expert(): pl.pallas_call(functools.partial(routed_kernel, count, entries), out_shap...  32.1 us
    ppermute x18, starting transfers between devices, shift(): return lax.ppermute(value, 'req', pairs)  18.7 us
    unnamed x70, local copies, waits for them, and re-layouts  16.5 us
  transfers between devices with their start and end apart: 48, of which 28 were waited for; matrix products, arithmetic and copies ran while one was open for 6% of the time, Pallas kernels for 25%

profile of v2, /device:TPU:0, one launch (start us, length us, event | category | flops | bytes accessed | tf_op | source)
XLA Modules:
  0.0 441.2 jit_solution(13744815767354972028)
XLA Ops:
  4.0 7.4 %all-to-all-start = ((bf16[8,576,256]{2,1,0:T(8,128)(2,1)}), bf16[8,576,256]{2,1,0:T(8,128)(2,1)S(1)}, u32[]{:S(2)}, u32[]{:S(2)}) async-start(bf16[8,576,256]{2,1,0:T(8,128)(2,1)} %pad_maximum_fusion), calls=%async_computation | async-start | bytes 4718592 | tf_op jit(solution)/shard_map/all_to_all | solution.py:323
  25.9 27.9 %collective-permute-done = f32[4,64]{1,0:T(4,128)S(1)} collective-permute-done((f32[4,64]{1,0:T(4,128)S(1)}, f32[4,64]{1,0:T(4,128)S(1)}, u32[]{:S(2)}, u32[]{:S(2)}) %collective-permute-start) | collective-permute-done | bytes 1056 | tf_op jit(solution)/shard_map/ppermute | solution.py:303
  53.8 11.7 %collective-permute-done.1 = f32[4,64]{1,0:T(4,128)S(1)} collective-permute-done((f32[4,64]{1,0:T(4,128)S(1)}, f32[4,64]{1,0:T(4,128)S(1)}, u32[]{:S(2)}, u32[]{:S(2)}) %collective-permute-start.1) | collective-permute-done | bytes 1056 | tf_op jit(solution)/shard_map/ppermute | solution.py:303
  77.9 4.0 shard_map.181
  84.1 4.0 shard_map.182
  91.1 5.6 %collective-permute-done.8 = bf16[64,2048]{1,0:T(8,128)(2,1)S(1)} collective-permute-done((bf16[64,2048]{1,0:T(8,128)(2,1)S(1)}, bf16[64,2048]{1,0:T(8,128)(2,1)S(1)}, u32[]{:S(2)}, u32[]{:S(2)}) %collective-permute-start.8) | collective-permute-done | bytes 262176 | tf_op jit(solution)/shard_map/ppermute | solution.py:303
  108.0 9.6 %collective-permute-done.9 = bf16[64,2048]{1,0:T(8,128)(2,1)S(1)} collective-permute-done((bf16[64,2048]{1,0:T(8,128)(2,1)S(1)}, bf16[64,2048]{1,0:T(8,128)(2,1)S(1)}, u32[]{:S(2)}, u32[]{:S(2)}) %collective-permute-start.9) | collective-permute-done | bytes 262176 | tf_op jit(solution)/shard_map/ppermute | solution.py:303
  118.2 5.4 %collective-permute-start.14 = (bf16[64,2048]{1,0:T(8,128)(2,1)S(1)}, bf16[64,2048]{1,0:T(8,128)(2,1)S(1)}, u32[]{:S(2)}, u32[]{:S(2)}) collective-permute-start(bf16[64,2048]{1,0:T(8,128)(2,1)S(1)} %multiply_convert_fusion.refs_0_), channel_id=1, source_target_pairs={{0,2},{1,3},{2,4},{3,5},{4,6},{5,7},{6,0},{7,1},{8,10},{9,11},{10,... | collective-permute-start | bytes 786440 | tf_op jit(solution)/shard_map/ppermute | solution.py:303
  127.5 4.0 collective-permute-done.14.refs_2_
  132.1 8.3 %collective-permute-done.16.refs_4_ = bf16[64,2048]{1,0:T(8,128)(2,1)S(1)} collective-permute-done((bf16[64,2048]{1,0:T(8,128)(2,1)S(1)}, bf16[64,2048]{1,0:T(8,128)(2,1)S(1)}, u32[]{:S(2)}, u32[]{:S(2)}) %collective-permute-start.16) | collective-permute-done | bytes 262176 | tf_op jit(solution)/shard_map/ppermute | solution.py:303
  142.4 7.1 %collective-permute-done.17.refs_5_ = bf16[64,2048]{1,0:T(8,128)(2,1)S(1)} collective-permute-done((bf16[64,2048]{1,0:T(8,128)(2,1)S(1)}, bf16[64,2048]{1,0:T(8,128)(2,1)S(1)}, u32[]{:S(2)}, u32[]{:S(2)}) %collective-permute-start.17) | collective-permute-done | bytes 262176 | tf_op jit(solution)/shard_map/ppermute | solution.py:303
  149.6 4.6 %collective-permute-done.19.refs_7_ = bf16[64,2048]{1,0:T(8,128)(2,1)S(1)} collective-permute-done((bf16[64,2048]{1,0:T(8,128)(2,1)S(1)}, bf16[64,2048]{1,0:T(8,128)(2,1)S(1)}, u32[]{:S(2)}, u32[]{:S(2)}) %collective-permute-start.19) | collective-permute-done | bytes 262176 | tf_op jit(solution)/shard_map/ppermute | solution.py:303
  154.9 64.7 %shard_map.183.rows.refs_0_ = bf16[512,2048]{1,0:T(8,128)(2,1)} custom-call(bf16[64,2048]{1,0:T(8,128)(2,1)} %copy-done.9, bf16[64,2048]{1,0:T(8,128)(2,1)} %copy-done.13, bf16[64,2048]{1,0:T(8,128)(2,1)} %copy-done.11, bf16[64,2048]{1,0:T(8,128)(2,1)} %copy-done.12, bf16[64,2048]{1,0:T(8,128)(2,1)} %copy-done.15, bf16[64,2048]{1,0:T(8,128)(2,1)} %copy-done.22, ...), custom_call_target="tpu_custom_call" | custom-call | bytes 4194304 | tf_op jit(solution)/shard_map/pallas_call | solution.py:109
  223.8 5.4 %collective-permute-done.23.refs_0_ = bf16[64,2048]{1,0:T(8,128)(2,1)} collective-permute-done((bf16[64,2048]{1,0:T(8,128)(2,1)}, bf16[64,2048]{1,0:T(8,128)(2,1)}, u32[]{:S(2)}, u32[]{:S(2)}) %collective-permute-start.23) | collective-permute-done | bytes 262176 | tf_op jit(solution)/shard_map/ppermute | solution.py:312
  230.7 4.0 collective-permute-done.27.refs_4_
  236.2 4.1 collective-permute-done.29.refs_6_
  241.0 5.0 %collective-permute-done.24.refs_1_ = bf16[64,2048]{1,0:T(8,128)(2,1)S(1)} collective-permute-done((bf16[64,2048]{1,0:T(8,128)(2,1)}, bf16[64,2048]{1,0:T(8,128)(2,1)S(1)}, u32[]{:S(2)}, u32[]{:S(2)}) %collective-permute-start.24) | collective-permute-done | bytes 262176 | tf_op jit(solution)/shard_map/ppermute | solution.py:312
  246.6 5.0 %collective-permute-done.25.refs_2_ = bf16[64,2048]{1,0:T(8,128)(2,1)S(1)} collective-permute-done((bf16[64,2048]{1,0:T(8,128)(2,1)}, bf16[64,2048]{1,0:T(8,128)(2,1)S(1)}, u32[]{:S(2)}, u32[]{:S(2)}) %collective-permute-start.25) | collective-permute-done | bytes 262176 | tf_op jit(solution)/shard_map/ppermute | solution.py:312
  251.5 5.2 %collective-permute-done.26.refs_3_ = bf16[64,2048]{1,0:T(8,128)(2,1)S(1)} collective-permute-done((bf16[64,2048]{1,0:T(8,128)(2,1)}, bf16[64,2048]{1,0:T(8,128)(2,1)S(1)}, u32[]{:S(2)}, u32[]{:S(2)}) %collective-permute-start.26) | collective-permute-done | bytes 262176 | tf_op jit(solution)/shard_map/ppermute | solution.py:312
  258.2 64.7 %shard_map.186.refs_0_ = bf16[512,2048]{1,0:T(8,128)(2,1)} custom-call(bf16[64,2048]{1,0:T(8,128)(2,1)} %collective-permute-done.23.refs_0_, bf16[64,2048]{1,0:T(8,128)(2,1)} %copy-done.18, bf16[64,2048]{1,0:T(8,128)(2,1)} %copy-done.19, bf16[64,2048]{1,0:T(8,128)(2,1)} %copy-done.20, bf16[64,2048]{1,0:T(8,128)(2,1)} %copy-done.16, ...), custom_call_target="tpu_custom_call" | custom-call | bytes 4194304 | tf_op jit(solution)/shard_map/pallas_call | solution.py:109
  325.8 4.6 %copy.78.up_w = bf16[2048,704]{1,0:T(8,128)(2,1)} copy(bf16[2048,704]{0,1:T(8,128)(2,1)} %param.32) | data formatting | bytes 5767168 | tf_op args[13]
  336.7 8.8 %shard_map.184.refs_5_ = bf16[512,2048]{1,0:T(8,128)(2,1)S(1)} custom-call(bf16[512,2048]{1,0:T(8,128)(2,1)S(1)} %copy-done.3, bf16[1,2048]{1,0:T(2,128)(2,1)S(1)} %reshape.225.scalar, bf16[2048,704]{1,0:T(8,128)(2,1)} %copy.77.gate_w, bf16[2048,704]{1,0:T(8,128)(2,1)} %copy.78.up_w, bf16[704,2048]{1,0:T(8,128)(2,1)} %down_w.1), custom_call_target="tpu_custom_call" | custom-call | flops 4429185024 | bytes 12845056 | tf_op jit(solution)/shard_map/pallas_call | solution.py:150
  346.9 16.4 %shard_map.185 = (bf16[512,2048]{1,0:T(8,128)(2,1)}, bf16[512,2048]{1,0:T(8,128)(2,1)}) custom-call(bf16[512,2048]{1,0:T(8,128)(2,1)} %shard_map.183.rows.refs_0_, bf16[512,2048]{1,0:T(8,128)(2,1)} %collective-permute-done.20.refs_1_, s32[2,1,512]{2,1,0:T(1,128)} %get-tuple-element.54.refs_2_, s32[2,512,1]{2,1,0:T(8,128)} %copy.79.refs_3_, ...), custom_call_target="tpu_custom_call" | custom-call | flops 8254390272 | bytes 25690112 | tf_op jit(solution)/shard_map/pallas_call | solution.py:220
  364.4 15.7 %shard_map.187 = (bf16[512,2048]{1,0:T(8,128)(2,1)}, bf16[512,2048]{1,0:T(8,128)(2,1)}) custom-call(bf16[512,2048]{1,0:T(8,128)(2,1)} %shard_map.186.refs_0_, bf16[512,2048]{1,0:T(8,128)(2,1)} %collective-permute-done.31.refs_1_, s32[2,1,512]{2,1,0:T(1,128)} %get-tuple-element.53.refs_2_, s32[2,512,1]{2,1,0:T(8,128)} %reshape_squeeze.24.refs_3_, ...), custom_call_target="tpu_custom_call" | custom-call | flops 8254390272 | bytes 25690112 | tf_op jit(solution)/shard_map/pallas_call | solution.py:220
  381.1 3.4 collective-permute-done.32
  391.3 3.5 collective-permute-done.33
  396.3 4.1 collective-permute-done.37
  402.1 3.9 collective-permute-done.22
  407.5 3.3 collective-permute-done.36
  417.6 4.9 %collective-permute-start.35 = (bf16[64,2048]{1,0:T(8,128)(2,1)S(1)}, bf16[64,2048]{1,0:T(8,128)(2,1)S(1)}, u32[]{:S(2)}, u32[]{:S(2)}) collective-permute-start(bf16[64,2048]{1,0:T(8,128)(2,1)S(1)} %get-tuple-element.25), channel_id=1, source_target_pairs={{0,2},{1,3},{2,4},{3,5},{4,6},{5,7},{6,0},{7,1},{8,10},{9,11},{10,... | collective-permute-start | bytes 786440 | tf_op jit(solution)/shard_map/ppermute | solution.py:303
  422.5 3.4 collective-permute-start.39
  432.7 7.6 %collective-permute-done.39 = bf16[64,2048]{1,0:T(8,128)(2,1)S(1)} collective-permute-done((bf16[64,2048]{1,0:T(8,128)(2,1)S(1)}, bf16[64,2048]{1,0:T(8,128)(2,1)S(1)}, u32[]{:S(2)}, u32[]{:S(2)}) %collective-permute-start.39) | collective-permute-done | bytes 262176 | tf_op jit(solution)/shard_map/ppermute | solution.py:303
  (210 shorter events, 102.4 us)
Async XLA Ops:
  4.0 71.2 %all-to-all-start = ((bf16[8,576,256]{2,1,0:T(8,128)(2,1)}), bf16[8,576,256]{2,1,0:T(8,128)(2,1)S(1)}, u32[]{:S(2)}, u32[]{:S(2)}) async-start(bf16[8,576,256]{2,1,0:T(8,128)(2,1)} %pad_maximum_fusion), calls=%async_computation | async-start | bytes 4718592 | tf_op jit(solution)/shard_map/all_to_all | solution.py:323
  11.4 42.3 %collective-permute-start = (f32[4,64]{1,0:T(4,128)S(1)}, f32[4,64]{1,0:T(4,128)S(1)}, u32[]{:S(2)}, u32[]{:S(2)}) collective-permute-start(f32[4,64]{1,0:T(4,128)S(1)} %bitcast.188), channel_id=1, source_target_pairs={{0,2},{1,3},{2,4},{3,5},{4,6},{5,7},{6,0},{7,1},{8,10},{9,11},{10,... | collective-permute-start | bytes 3080 | tf_op jit(solution)/shard_map/ppermute | solution.py:303
  13.5 52.0 %collective-permute-start.1 = (f32[4,64]{1,0:T(4,128)S(1)}, f32[4,64]{1,0:T(4,128)S(1)}, u32[]{:S(2)}, u32[]{:S(2)}) collective-permute-start(f32[4,64]{1,0:T(4,128)S(1)} %bitcast.189), channel_id=1, source_target_pairs={{0,4},{1,5},{2,6},{3,7},{4,0},{5,1},{6,2},{7,3},{8,12},{9,13},{10,... | collective-permute-start | bytes 3080 | tf_op jit(solution)/shard_map/ppermute | solution.py:303
  15.8 49.6 %collective-permute-start.2 = (f32[4,64]{1,0:T(4,128)S(1)}, f32[4,64]{1,0:T(4,128)S(1)}, u32[]{:S(2)}, u32[]{:S(2)}) collective-permute-start(f32[4,64]{1,0:T(4,128)S(1)} %bitcast.190), channel_id=1, source_target_pairs={{0,6},{1,7},{2,0},{3,1},{4,2},{5,3},{6,4},{7,5},{8,14},{9,15},{10,... | collective-permute-start | bytes 3080 | tf_op jit(solution)/shard_map/ppermute | solution.py:303
  88.2 14.2 %collective-permute-start.10 = (bf16[64,2048]{1,0:T(8,128)(2,1)S(1)}, bf16[64,2048]{1,0:T(8,128)(2,1)S(1)}, u32[]{:S(2)}, u32[]{:S(2)}) collective-permute-start(bf16[64,2048]{1,0:T(8,128)(2,1)S(1)} %get-tuple-element.43), channel_id=1, source_target_pairs={{0,1},{1,0},{2,3},{3,2},{4,5},{5,4},{6,7},{7,6},{8,9},{9,8},{10,11... | collective-permute-start | bytes 786440 | tf_op jit(solution)/shard_map/ppermute | solution.py:303
  89.7 17.9 %collective-permute-start.12 = (bf16[64,2048]{1,0:T(8,128)(2,1)S(1)}, bf16[64,2048]{1,0:T(8,128)(2,1)S(1)}, u32[]{:S(2)}, u32[]{:S(2)}) collective-permute-start(bf16[64,2048]{1,0:T(8,128)(2,1)S(1)} %get-tuple-element.44), channel_id=1, source_target_pairs={{0,1},{1,0},{2,3},{3,2},{4,5},{5,4},{6,7},{7,6},{8,9},{9,8},{10,11... | collective-permute-start | bytes 786440 | tf_op jit(solution)/shard_map/ppermute | solution.py:303
  97.5 20.2 %collective-permute-start.9 = (bf16[64,2048]{1,0:T(8,128)(2,1)S(1)}, bf16[64,2048]{1,0:T(8,128)(2,1)S(1)}, u32[]{:S(2)}, u32[]{:S(2)}) collective-permute-start(bf16[64,2048]{1,0:T(8,128)(2,1)S(1)} %get-tuple-element.40), channel_id=1, source_target_pairs={{0,4},{1,5},{2,6},{3,7},{4,0},{5,1},{6,2},{7,3},{8,12},{9,13},{10,... | collective-permute-start | bytes 786440 | tf_op jit(solution)/shard_map/ppermute | solution.py:303
  102.4 15.2 %collective-permute-start.11 = (bf16[64,2048]{1,0:T(8,128)(2,1)S(1)}, bf16[64,2048]{1,0:T(8,128)(2,1)S(1)}, u32[]{:S(2)}, u32[]{:S(2)}) collective-permute-start(bf16[64,2048]{1,0:T(8,128)(2,1)S(1)} %fusion.14), channel_id=1, source_target_pairs={{0,6},{1,7},{2,0},{3,1},{4,2},{5,3},{6,4},{7,5},{8,14},{9,15},{10,... | collective-permute-start | bytes 786440 | tf_op jit(solution)/shard_map/ppermute | solution.py:303
  118.2 13.3 %collective-permute-start.14 = (bf16[64,2048]{1,0:T(8,128)(2,1)S(1)}, bf16[64,2048]{1,0:T(8,128)(2,1)S(1)}, u32[]{:S(2)}, u32[]{:S(2)}) collective-permute-start(bf16[64,2048]{1,0:T(8,128)(2,1)S(1)} %multiply_convert_fusion.refs_0_), channel_id=1, source_target_pairs={{0,2},{1,3},{2,4},{3,5},{4,6},{5,7},{6,0},{7,1},{8,10},{9,11},{10,... | collective-permute-start | bytes 786440 | tf_op jit(solution)/shard_map/ppermute | solution.py:303
  123.6 16.8 %collective-permute-start.16 = (bf16[64,2048]{1,0:T(8,128)(2,1)S(1)}, bf16[64,2048]{1,0:T(8,128)(2,1)S(1)}, u32[]{:S(2)}, u32[]{:S(2)}) collective-permute-start(bf16[64,2048]{1,0:T(8,128)(2,1)S(1)} %multiply_convert_fusion.refs_0_), channel_id=1, source_target_pairs={{0,4},{1,5},{2,6},{3,7},{4,0},{5,1},{6,2},{7,3},{8,12},{9,13},{10,... | collective-permute-start | bytes 786440 | tf_op jit(solution)/shard_map/ppermute | solution.py:303
  124.7 16.3 %collective-permute-start.18 = (bf16[64,2048]{1,0:T(8,128)(2,1)S(1)}, bf16[64,2048]{1,0:T(8,128)(2,1)S(1)}, u32[]{:S(2)}, u32[]{:S(2)}) collective-permute-start(bf16[64,2048]{1,0:T(8,128)(2,1)S(1)} %multiply_convert_fusion.refs_0_), channel_id=1, source_target_pairs={{0,6},{1,7},{2,0},{3,1},{4,2},{5,3},{6,4},{7,5},{8,14},{9,15},{10,... | collective-permute-start | bytes 786440 | tf_op jit(solution)/shard_map/ppermute | solution.py:303
  126.0 16.4 %collective-permute-start.13 = (bf16[64,2048]{1,0:T(8,128)(2,1)S(1)}, bf16[64,2048]{1,0:T(8,128)(2,1)S(1)}, u32[]{:S(2)}, u32[]{:S(2)}) collective-permute-start(bf16[64,2048]{1,0:T(8,128)(2,1)S(1)} %multiply_convert_fusion.refs_0_), channel_id=1, source_target_pairs={{0,1},{1,0},{2,3},{3,2},{4,5},{5,4},{6,7},{7,6},{8,9},{9,8},{10,11... | collective-permute-start | bytes 786440 | tf_op jit(solution)/shard_map/ppermute | solution.py:303
  219.6 127.2 %collective-permute-start.20 = (bf16[512,2048]{1,0:T(8,128)(2,1)}, bf16[512,2048]{1,0:T(8,128)(2,1)}, u32[]{:S(2)}, u32[]{:S(2)}) collective-permute-start(bf16[512,2048]{1,0:T(8,128)(2,1)} %shard_map.183.rows.refs_0_), channel_id=1, source_target_pairs={{0,8},{8,0},{16,24},{24,16},{1,9},{9,1},{17,25},{25,17},{2,10},{10... | collective-permute-start | bytes 6291464 | tf_op jit(solution)/shard_map/ppermute | solution.py:312
  221.3 13.4 %collective-permute-start.27 = (bf16[64,2048]{1,0:T(8,128)(2,1)}, bf16[64,2048]{1,0:T(8,128)(2,1)S(1)}, u32[]{:S(2)}, u32[]{:S(2)}) collective-permute-start(bf16[64,2048]{1,0:T(8,128)(2,1)} %copy-done.15), channel_id=1, source_target_pairs={{0,16},{8,24},{16,0},{24,8},{1,17},{9,25},{17,1},{25,9},{2,18},{10... | collective-permute-start | bytes 786440 | tf_op jit(solution)/shard_map/ppermute | solution.py:312
  221.8 18.5 %collective-permute-start.29 = (bf16[64,2048]{1,0:T(8,128)(2,1)}, bf16[64,2048]{1,0:T(8,128)(2,1)S(1)}, u32[]{:S(2)}, u32[]{:S(2)}) collective-permute-start(bf16[64,2048]{1,0:T(8,128)(2,1)} %copy-done.14), channel_id=1, source_target_pairs={{0,16},{8,24},{16,0},{24,8},{1,17},{9,25},{17,1},{25,9},{2,18},{10... | collective-permute-start | bytes 786440 | tf_op jit(solution)/shard_map/ppermute | solution.py:312
  223.3 22.6 %collective-permute-start.24 = (bf16[64,2048]{1,0:T(8,128)(2,1)}, bf16[64,2048]{1,0:T(8,128)(2,1)S(1)}, u32[]{:S(2)}, u32[]{:S(2)}) collective-permute-start(bf16[64,2048]{1,0:T(8,128)(2,1)} %copy-done.13), channel_id=1, source_target_pairs={{0,16},{8,24},{16,0},{24,8},{1,17},{9,25},{17,1},{25,9},{2,18},{10... | collective-permute-start | bytes 786440 | tf_op jit(solution)/shard_map/ppermute | solution.py:312
  229.2 22.4 %collective-permute-start.25 = (bf16[64,2048]{1,0:T(8,128)(2,1)}, bf16[64,2048]{1,0:T(8,128)(2,1)S(1)}, u32[]{:S(2)}, u32[]{:S(2)}) collective-permute-start(bf16[64,2048]{1,0:T(8,128)(2,1)} %copy-done.11), channel_id=1, source_target_pairs={{0,16},{8,24},{16,0},{24,8},{1,17},{9,25},{17,1},{25,9},{2,18},{10... | collective-permute-start | bytes 786440 | tf_op jit(solution)/shard_map/ppermute | solution.py:312
  234.7 22.0 %collective-permute-start.26 = (bf16[64,2048]{1,0:T(8,128)(2,1)}, bf16[64,2048]{1,0:T(8,128)(2,1)S(1)}, u32[]{:S(2)}, u32[]{:S(2)}) collective-permute-start(bf16[64,2048]{1,0:T(8,128)(2,1)} %copy-done.12), channel_id=1, source_target_pairs={{0,16},{8,24},{16,0},{24,8},{1,17},{9,25},{17,1},{25,9},{2,18},{10... | collective-permute-start | bytes 786440 | tf_op jit(solution)/shard_map/ppermute | solution.py:312
  240.3 16.4 %collective-permute-start.28 = (bf16[64,2048]{1,0:T(8,128)(2,1)S(1)}, bf16[64,2048]{1,0:T(8,128)(2,1)S(1)}, u32[]{:S(2)}, u32[]{:S(2)}) collective-permute-start(bf16[64,2048]{1,0:T(8,128)(2,1)S(1)} %collective-permute-done.27.refs_4_), channel_id=1, source_target_pairs={{0,1},{1,0},{2,3},{3,2},{4,5},{5,4},{6,7},{7,6},{8,9},{9,8},{10,11... | collective-permute-start | bytes 786440 | tf_op jit(solution)/shard_map/ppermute | solution.py:303
  322.9 41.0 %collective-permute-start.31 = (bf16[512,2048]{1,0:T(8,128)(2,1)}, bf16[512,2048]{1,0:T(8,128)(2,1)}, u32[]{:S(2)}, u32[]{:S(2)}) collective-permute-start(bf16[512,2048]{1,0:T(8,128)(2,1)} %shard_map.186.refs_0_), channel_id=1, source_target_pairs={{0,8},{8,0},{16,24},{24,16},{1,9},{9,1},{17,25},{25,17},{2,10},{10... | collective-permute-start | bytes 6291464 | tf_op jit(solution)/shard_map/ppermute | solution.py:312
  363.3 16.9 %collective-permute-start.21 = (bf16[512,2048]{1,0:T(8,128)(2,1)}, bf16[512,2048]{1,0:T(8,128)(2,1)S(1)}, u32[]{:S(2)}, u32[]{:S(2)}) collective-permute-start(bf16[512,2048]{1,0:T(8,128)(2,1)} %get-tuple-element.16), channel_id=1, source_target_pairs={{0,8},{8,0},{16,24},{24,16},{1,9},{9,1},{17,25},{25,17},{2,10},{10... | collective-permute-start | bytes 6291464 | tf_op jit(solution)/shard_map/ppermute | solution.py:312
  386.3 14.1 %collective-permute-start.37 = (bf16[64,2048]{1,0:T(8,128)(2,1)S(1)}, bf16[64,2048]{1,0:T(8,128)(2,1)S(1)}, u32[]{:S(2)}, u32[]{:S(2)}) collective-permute-start(bf16[64,2048]{1,0:T(8,128)(2,1)S(1)} %get-tuple-element.38), channel_id=1, source_target_pairs={{0,1},{1,0},{2,3},{3,2},{4,5},{5,4},{6,7},{7,6},{8,9},{9,8},{10,11... | collective-permute-start | bytes 786440 | tf_op jit(solution)/shard_map/ppermute | solution.py:303
  387.7 18.3 %collective-permute-start.22 = (bf16[64,2048]{1,0:T(8,128)(2,1)S(1)}, bf16[64,2048]{1,0:T(8,128)(2,1)S(1)}, u32[]{:S(2)}, u32[]{:S(2)}) collective-permute-start(bf16[64,2048]{1,0:T(8,128)(2,1)S(1)} %get-tuple-element.29), channel_id=1, source_target_pairs={{0,1},{1,0},{2,3},{3,2},{4,5},{5,4},{6,7},{7,6},{8,9},{9,8},{10,11... | collective-permute-start | bytes 786440 | tf_op jit(solution)/shard_map/ppermute | solution.py:303
  388.4 22.4 %collective-permute-start.36 = (bf16[64,2048]{1,0:T(8,128)(2,1)S(1)}, bf16[64,2048]{1,0:T(8,128)(2,1)S(1)}, u32[]{:S(2)}, u32[]{:S(2)}) collective-permute-start(bf16[64,2048]{1,0:T(8,128)(2,1)S(1)} %get-tuple-element.30), channel_id=1, source_target_pairs={{0,1},{1,0},{2,3},{3,2},{4,5},{5,4},{6,7},{7,6},{8,9},{9,8},{10,11... | collective-permute-start | bytes 786440 | tf_op jit(solution)/shard_map/ppermute | solution.py:303
  389.8 22.6 %collective-permute-start.41 = (bf16[64,2048]{1,0:T(8,128)(2,1)S(1)}, bf16[64,2048]{1,0:T(8,128)(2,1)S(1)}, u32[]{:S(2)}, u32[]{:S(2)}) collective-permute-start(bf16[64,2048]{1,0:T(8,128)(2,1)S(1)} %get-tuple-element.36), channel_id=1, source_target_pairs={{0,16},{8,24},{16,0},{24,8},{1,17},{9,25},{17,1},{25,9},{2,18},{10... | collective-permute-start | bytes 786440 | tf_op jit(solution)/shard_map/ppermute | solution.py:312
  394.8 17.6 %collective-permute-start.45 = (bf16[64,2048]{1,0:T(8,128)(2,1)S(1)}, bf16[64,2048]{1,0:T(8,128)(2,1)S(1)}, u32[]{:S(2)}, u32[]{:S(2)}) collective-permute-start(bf16[64,2048]{1,0:T(8,128)(2,1)S(1)} %get-tuple-element.34), channel_id=1, source_target_pairs={{0,16},{8,24},{16,0},{24,8},{1,17},{9,25},{17,1},{25,9},{2,18},{10... | collective-permute-start | bytes 786440 | tf_op jit(solution)/shard_map/ppermute | solution.py:312
  410.8 15.1 %collective-permute-start.40 = (bf16[64,2048]{1,0:T(8,128)(2,1)S(1)}, bf16[64,2048]{1,0:T(8,128)(2,1)S(1)}, u32[]{:S(2)}, u32[]{:S(2)}) collective-permute-start(bf16[64,2048]{1,0:T(8,128)(2,1)S(1)} %get-tuple-element.37), channel_id=1, source_target_pairs={{0,16},{8,24},{16,0},{24,8},{1,17},{9,25},{17,1},{25,9},{2,18},{10... | collective-permute-start | bytes 786440 | tf_op jit(solution)/shard_map/ppermute | solution.py:312
  416.1 13.6 %collective-permute-start.44 = (bf16[64,2048]{1,0:T(8,128)(2,1)S(1)}, bf16[64,2048]{1,0:T(8,128)(2,1)S(1)}, u32[]{:S(2)}, u32[]{:S(2)}) collective-permute-start(bf16[64,2048]{1,0:T(8,128)(2,1)S(1)} %get-tuple-element.35), channel_id=1, source_target_pairs={{0,16},{8,24},{16,0},{24,8},{1,17},{9,25},{17,1},{25,9},{2,18},{10... | collective-permute-start | bytes 786440 | tf_op jit(solution)/shard_map/ppermute | solution.py:312
  417.6 15.1 %collective-permute-start.35 = (bf16[64,2048]{1,0:T(8,128)(2,1)S(1)}, bf16[64,2048]{1,0:T(8,128)(2,1)S(1)}, u32[]{:S(2)}, u32[]{:S(2)}) collective-permute-start(bf16[64,2048]{1,0:T(8,128)(2,1)S(1)} %get-tuple-element.25), channel_id=1, source_target_pairs={{0,2},{1,3},{2,4},{3,5},{4,6},{5,7},{6,0},{7,1},{8,10},{9,11},{10,... | collective-permute-start | bytes 786440 | tf_op jit(solution)/shard_map/ppermute | solution.py:303
  422.5 17.7 %collective-permute-start.39 = (bf16[64,2048]{1,0:T(8,128)(2,1)S(1)}, bf16[64,2048]{1,0:T(8,128)(2,1)S(1)}, u32[]{:S(2)}, u32[]{:S(2)}) collective-permute-start(bf16[64,2048]{1,0:T(8,128)(2,1)S(1)} %get-tuple-element.28), channel_id=1, source_target_pairs={{0,4},{1,5},{2,6},{3,7},{4,0},{5,1},{6,2},{7,3},{8,12},{9,13},{10,... | collective-permute-start | bytes 786440 | tf_op jit(solution)/shard_map/ppermute | solution.py:303
  426.0 14.3 %collective-permute-start.46 = (bf16[64,2048]{1,0:T(8,128)(2,1)S(1)}, bf16[64,2048]{1,0:T(8,128)(2,1)S(1)}, u32[]{:S(2)}, u32[]{:S(2)}) collective-permute-start(bf16[64,2048]{1,0:T(8,128)(2,1)S(1)} %get-tuple-element.26), channel_id=1, source_target_pairs={{0,1},{1,0},{2,3},{3,2},{4,5},{5,4},{6,7},{7,6},{8,9},{9,8},{10,11... | collective-permute-start | bytes 786440 | tf_op jit(solution)/shard_map/ppermute | solution.py:303
  426.6 13.7 %collective-permute-start.43 = (bf16[64,2048]{1,0:T(8,128)(2,1)S(1)}, bf16[64,2048]{1,0:T(8,128)(2,1)S(1)}, u32[]{:S(2)}, u32[]{:S(2)}) collective-permute-start(bf16[64,2048]{1,0:T(8,128)(2,1)S(1)} %fusion.6), channel_id=1, source_target_pairs={{0,6},{1,7},{2,0},{3,1},{4,2},{5,3},{6,4},{7,5},{8,14},{9,15},{10,... | collective-permute-start | bytes 786440 | tf_op jit(solution)/shard_map/ppermute | solution.py:303
  (49 other events, 761.1 us)

commit v3 on v2

v3 whole, which is shorter than its diff:
```python
import functools

import jax
import jax.numpy as jnp
from jax import lax
from jax.experimental import pallas as pl
from jax.experimental.pallas import tpu as pltpu
from jax.sharding import PartitionSpec as P

HEAD_DIM = 128
TOPK = 4
CORES = 2
Z_CHIPS = 4


def pack_kernel(order, *refs):
    parts, out = refs[:-1], refs[-1]
    at = 0
    for part in parts:
        rows = part.shape[0]
        out[at : at + rows, :] = part[...]
        at += rows


def pack(parts, order, columns):
    count = order.shape[0]
    rows = sum(p.shape[0] for p in parts)
    return pl.pallas_call(
        pack_kernel,
        out_shape=jax.ShapeDtypeStruct((rows, count * columns), parts[0].dtype),
        grid_spec=pltpu.PrefetchScalarGridSpec(
            num_scalar_prefetch=1,
            grid=(count,),
            in_specs=[
                pl.BlockSpec((p.shape[0], columns), lambda j, order: (0, order[j]))
                for p in parts
            ],
            out_specs=pl.BlockSpec((rows, columns), lambda j, order: (0, j)),
        ),
        cost_estimate=pl.CostEstimate(
            flops=0, bytes_accessed=4 * rows * count * columns, transcendentals=0
        ),
    )(order, *parts)


def attend_kernel(members, tokens, page_len, scale, page_req, page_slot, *refs):
    blocks, far, refs = refs[:members], refs[members : 2 * members], refs[2 * members :]
    row_req, row_pos, out, level = refs
    keys = jnp.concatenate([block[:tokens, :] for block in blocks], axis=0)
    values = jnp.concatenate([block[tokens : 2 * tokens, :] for block in blocks], axis=0)
    near = [block[2 * tokens :, :] for block in blocks]
    size = sum(q.shape[0] for q in near)
    for side, query in enumerate((near, [q[...] for q in far])):
        lanes = slice(side * size, (side + 1) * size)
        query = jnp.concatenate(query, axis=0)
        request, position = row_req[:, lanes], row_pos[:, lanes]
        scores = (
            lax.dot_general(
                keys, query, (((1,), (1,)), ((), ())), preferred_element_type=jnp.float32
            )
            * scale
        )
        token = lax.broadcasted_iota(jnp.int32, (page_len, size), 0)
        visible = jnp.concatenate(
            [
                (request == page_req[page]) & (token + page_slot[page] * page_len <= position)
                for page in range(members * tokens // page_len)
            ],
            axis=0,
        )
        scores = jnp.where(visible, scores, -1e30)
        top = jnp.max(scores, axis=0, keepdims=True)
        weights = jnp.where(visible, jnp.exp(scores - top), 0.0)
        total = jnp.sum(weights, axis=0, keepdims=True)
        summed = lax.dot_general(
            values,
            weights.astype(jnp.bfloat16),
            (((0,), (0,)), ((), ())),
            preferred_element_type=jnp.float32,
        )
        seen = total > 0.0
        total = jnp.where(seen, total, 1.0)
        out[:, lanes] = (summed / total).astype(jnp.bfloat16)
        level[0, :, lanes] = jnp.where(seen, top + jnp.log(total), -1e30)


def attend(blocks, far, row_req, row_pos, page_req, page_slot, page_len):
    members, rows = len(blocks), row_req.shape[1]
    block_rows, columns = blocks[0].shape
    tok_rows = far[0].shape[0]
    tokens = (block_rows - tok_rows) // 2
    heads = columns // HEAD_DIM
    by_head = lambda n: pl.BlockSpec((n, HEAD_DIM), lambda h, *_: (0, h))
    whole = pl.BlockSpec((1, rows), lambda h, *_: (0, 0))
    return pl.pallas_call(
        functools.partial(attend_kernel, members, tokens, page_len, HEAD_DIM ** (-0.5)),
        out_shape=[
            jax.ShapeDtypeStruct((columns, rows), jnp.bfloat16),
            jax.ShapeDtypeStruct((heads, 1, rows), jnp.float32),
        ],
        grid_spec=pltpu.PrefetchScalarGridSpec(
            num_scalar_prefetch=2,
            grid=(heads,),
            in_specs=[by_head(block_rows)] * members + [by_head(tok_rows)] * members + [whole] * 2,
            out_specs=[
                pl.BlockSpec((HEAD_DIM, rows), lambda h, *_: (h, 0)),
                pl.BlockSpec((1, 1, rows), lambda h, *_: (h, 0, 0)),
            ],
        ),
        compiler_params=pltpu.CompilerParams(vmem_limit_bytes=48 * 1024 * 1024),
        cost_estimate=pl.CostEstimate(
            flops=4 * rows * members * tokens * columns,
            bytes_accessed=2 * members * (block_rows + tok_rows) * columns,
            transcendentals=rows * members * tokens * heads,
        ),
    )(page_req, page_slot, *blocks, *far, row_req, row_pos)


def project_kernel(mine, mine_level, theirs, their_level, proj, out):
    parts = []
    for head in range(mine.shape[0] // HEAD_DIM):
        dims = slice(head * HEAD_DIM, (head + 1) * HEAD_DIM)
        share = 1.0 / (1.0 + jnp.exp(their_level[head] - mine_level[head]))
        other = 1.0 / (1.0 + jnp.exp(mine_level[head] - their_level[head]))
        both = share * mine[dims, :].astype(jnp.float32) + other * theirs[dims, :].astype(
            jnp.float32
        )
        parts.append(both.astype(jnp.bfloat16))
    attention = jnp.concatenate(parts, axis=0) if len(parts) > 1 else parts[0]
    out[...] = lax.dot_general(
        attention, proj[...], (((0,), (0,)), ((), ())), preferred_element_type=jnp.float32
    ).astype(jnp.bfloat16)


def project(mine, mine_level, theirs, their_level, proj):
    columns, width = proj.shape
    rows = mine.shape[1]
    heads = columns // HEAD_DIM
    size = rows // 4
    return pl.pallas_call(
        project_kernel,
        out_shape=jax.ShapeDtypeStruct((rows, width), jnp.bfloat16),
        grid=(4,),
        in_specs=[
            pl.BlockSpec((columns, size), lambda i: (0, i)),
            pl.BlockSpec((heads, 1, size), lambda i: (0, 0, i)),
            pl.BlockSpec((columns, size), lambda i: (0, (i + 2) % 4)),
            pl.BlockSpec((heads, 1, size), lambda i: (0, 0, (i + 2) % 4)),
            pl.BlockSpec((columns, width), lambda i: (0, 0)),
        ],
        out_specs=pl.BlockSpec((size, width), lambda i: (i, 0)),
        cost_estimate=pl.CostEstimate(
            flops=2 * rows * columns * width,
            bytes_accessed=2 * (2 * columns * rows + columns * width + rows * width),
            transcendentals=2 * rows * heads,
        ),
    )(mine, mine_level, theirs, their_level, proj)


def join_kernel(*refs):
    parts, out = refs[:-1], refs[-1]
    rows = parts[0].shape[0]
    for i, part in enumerate(parts):
        out[i * rows : (i + 1) * rows, :] = part[...]


def join(parts):
    rows, width = parts[0].shape
    vmem = pl.BlockSpec(memory_space=pltpu.VMEM)
    return pl.pallas_call(
        join_kernel,
        out_shape=jax.ShapeDtypeStruct((len(parts) * rows, width), parts[0].dtype),
        in_specs=[vmem] * len(parts),
        out_specs=vmem,
        cost_estimate=pl.CostEstimate(
            flops=0, bytes_accessed=4 * len(parts) * rows * width, transcendentals=0
        ),
    )(*parts)


def silu(value):
    return value / (1.0 + jnp.exp(-value))


def shared_kernel(rows, scalar, gate_w, up_w, down_w, out, gate_v, up_v, down_v, sems):
    copies = [
        pltpu.make_async_copy(src, dst, sems.at[i])
        for i, (src, dst) in enumerate(((gate_w, gate_v), (up_w, up_v), (down_w, down_v)))
    ]
    for copy in copies:
        copy.start()
    block = rows[...]
    logit = jnp.sum(
        block.astype(jnp.float32) * scalar[...].astype(jnp.float32), axis=1, keepdims=True
    )
    scale = 1.0 / (1.0 + jnp.exp(-logit))
    copies[0].wait()
    across = (((1,), (1,)), ((), ()))
    gate = lax.dot_general(block, gate_v[...], across, preferred_element_type=jnp.float32)
    copies[1].wait()
    upper = lax.dot_general(block, up_v[...], across, preferred_element_type=jnp.float32)
    hidden = (silu(gate) * upper).astype(jnp.bfloat16)
    copies[2].wait()
    result = jnp.dot(hidden, down_v[...], preferred_element_type=jnp.float32)
    out[...] = (scale * result).astype(jnp.bfloat16)


def shared_expert(rows, scalar, gate_w, up_w, down_w):
    any_spec = pl.BlockSpec(memory_space=pl.ANY)
    vmem = pl.BlockSpec(memory_space=pltpu.VMEM)
    return pl.pallas_call(
        shared_kernel,
        out_shape=jax.ShapeDtypeStruct(rows.shape, jnp.bfloat16),
        in_specs=[vmem, vmem, any_spec, any_spec, any_spec],
        out_specs=vmem,
        scratch_shapes=[
            pltpu.VMEM(gate_w.shape, jnp.bfloat16),
            pltpu.VMEM(up_w.shape, jnp.bfloat16),
            pltpu.VMEM(down_w.shape, jnp.bfloat16),
            pltpu.SemaphoreType.DMA((3,)),
        ],
        compiler_params=pltpu.CompilerParams(vmem_limit_bytes=48 * 1024 * 1024),
        cost_estimate=pl.CostEstimate(
            flops=6 * rows.shape[0] * gate_w.size,
            bytes_accessed=6 * gate_w.size + 4 * rows.size,
            transcendentals=rows.shape[0] * gate_w.shape[0],
        ),
    )(rows, scalar.reshape(1, -1), gate_w, up_w, down_w)


def routed_kernel(count, entries, *refs):
    chunks, refs = refs[:count], refs[count:]
    place_row, place_col, row_gate, extra, gate_w, up_w, down_w = refs[:7]
    outs, refs = refs[7 : 7 + count], refs[7 + count :]
    packed, gate_v, up_v, down_v, sems = refs
    copies = [
        pltpu.make_async_copy(src.at[0], dst, sems.at[i])
        for i, (src, dst) in enumerate(((gate_w, gate_v), (up_w, up_v), (down_w, down_v)))
    ]
    for copy in copies:
        copy.start()
    size = chunks[0].shape[0]
    for c in range(count):
        wanted = lax.broadcasted_iota(jnp.int32, (entries, size), 0)
        pick = jnp.where(place_row[c] == wanted, 1.0, 0.0).astype(jnp.bfloat16)
        packed[c * entries : (c + 1) * entries, :] = jnp.dot(
            pick, chunks[c][...], preferred_element_type=jnp.float32
        ).astype(jnp.bfloat16)
    copies[0].wait()
    gate = jnp.dot(packed[...], gate_v[...], preferred_element_type=jnp.float32)
    copies[1].wait()
    upper = jnp.dot(packed[...], up_v[...], preferred_element_type=jnp.float32)
    hidden = (silu(gate) * upper).astype(jnp.bfloat16)
    copies[2].wait()
    answer = jnp.dot(hidden, down_v[...], preferred_element_type=jnp.float32).astype(
        jnp.bfloat16
    )
    for c in range(count):
        wanted = lax.broadcasted_iota(jnp.int32, (size, entries), 1)
        put = jnp.where(place_col[c] == wanted, 1.0, 0.0).astype(jnp.bfloat16)
        placed = row_gate[c] * jnp.dot(
            put,
            answer[c * entries : (c + 1) * entries, :],
            preferred_element_type=jnp.float32,
        )
        if c == 0 and extra.shape[0] == size:
            placed = placed + extra[...].astype(jnp.float32)
        outs[c][...] = placed.astype(jnp.bfloat16)


def routed_expert(chunks, place, row_gate, extra, gate_w, up_w, down_w, entries):
    count = len(chunks)
    size, width = chunks[0].shape
    hidden = gate_w.shape[2]
    any_spec = pl.BlockSpec(memory_space=pl.ANY)
    vmem = pl.BlockSpec(memory_space=pltpu.VMEM)
    if extra is None:
        extra = jnp.zeros((8, 128), jnp.bfloat16)
    return pl.pallas_call(
        functools.partial(routed_kernel, count, entries),
        out_shape=[jax.ShapeDtypeStruct((size, width), jnp.bfloat16)] * count,
        in_specs=[vmem] * (count + 4) + [any_spec] * 3,
        out_specs=[vmem] * count,
        scratch_shapes=[
            pltpu.VMEM((count * entries, width), jnp.bfloat16),
            pltpu.VMEM((width, hidden), jnp.bfloat16),
            pltpu.VMEM((width, hidden), jnp.bfloat16),
            pltpu.VMEM((hidden, width), jnp.bfloat16),
            pltpu.SemaphoreType.DMA((3,)),
        ],
        compiler_params=pltpu.CompilerParams(vmem_limit_bytes=56 * 1024 * 1024),
        cost_estimate=pl.CostEstimate(
            flops=2 * count * entries * (3 * gate_w.size + 2 * size * width),
            bytes_accessed=6 * gate_w.size + 4 * count * size * width,
            transcendentals=count * entries * hidden,
        ),
    )(
        *chunks,
        place.reshape(count, 1, size),
        place.reshape(count, size, 1),
        row_gate.reshape(count, size, 1),
        extra,
        gate_w,
        up_w,
        down_w,
    )


def rms_normed(stream, norm_gain):
    scale_row = lax.rsqrt(jnp.mean(stream * stream, axis=1, keepdims=True) + 1e-06)
    return (stream * scale_row * norm_gain[None, :]).astype(jnp.bfloat16)


def shards(
    resid,
    queries,
    cache_key,
    cache_value,
    page_table,
    row_request,
    row_position,
    out_proj,
    norm_gain,
    expert_gate,
    expert_up,
    expert_down,
    shared_gate,
    shared_up,
    shared_down,
    shared_scalar,
    slot_expert,
    route_expert,
    route_gate,
):
    f32, bf16, i32 = jnp.float32, jnp.bfloat16, jnp.int32
    exp_count = lax.axis_size("exp")
    req_count = lax.axis_size("req")
    slot_count = exp_count * req_count
    nc, nx, ny = CORES, exp_count // Z_CHIPS, req_count // CORES
    exp_index = lax.axis_index("exp")
    req_index = lax.axis_index("req")
    own_slot = req_index * exp_count + exp_index
    iz, ix = exp_index // nx, exp_index % nx
    ih, il = iz // 2, iz % 2
    iy, ic = req_index // nc, req_index % nc
    tok_rows, width = resid.shape
    pages_here, page_len, _ = cache_key.shape
    req_slots, max_pages = page_table.shape
    tokens = pages_here * page_len
    capacity = 3 * tok_rows * TOPK // slot_count

    zs = [(dh, dl) for dh in range(2) for dl in range(2)]

    def send(value, dh, dl, dx):
        if not (dh or dl or dx % nx):
            return value
        pairs = [
            (
                (h * 2 + l) * nx + x,
                ((h + dh) % 2 * 2 + (l + dl) % 2) * nx + (x + dx) % nx,
            )
            for h in range(2)
            for l in range(2)
            for x in range(nx)
        ]
        return lax.ppermute(value, "exp", pairs)

    def send_req(value, dy, dc):
        if not (dy % ny or dc % nc):
            return value
        pairs = [
            (y * nc + c, (y + dy) % ny * nc + (c + dc) % nc)
            for y in range(ny)
            for c in range(nc)
        ]
        return lax.ppermute(value, "req", pairs)

    rel_exp = jnp.stack(
        [
            ((ih + dh) % 2 * 2 + (il + dl) % 2) * nx + (ix - dx) % nx
            for dh, dl in zs
            for dx in range(nx)
        ]
    ).astype(i32)
    rel_req = jnp.stack(
        [((iy - dy) % ny) * nc + (ic - dc) % nc for dy in range(ny) for dc in range(nc)]
    ).astype(i32)

    columns = width // exp_count
    keys = cache_key.reshape(tokens, width)
    values = cache_value.reshape(tokens, width)
    far_queries = send(queries, 1, 0, 0)
    members = [(dl, dx) for dl in range(2) for dx in range(nx)]
    orders = [
        jnp.stack(
            [((ih + j) % 2 * 2 + (il + dl) % 2) * nx + (ix + dx) % nx for j in range(2)]
        ).astype(i32)
        for dl, dx in members
    ]
    blocks = {}
    for m in reversed(range(len(members))):
        blocks[m] = send(pack([keys, values, queries], orders[m], columns), 0, *members[m])
    far = [
        send(pack([far_queries], orders[m], columns), 0, *members[m])
        for m in range(len(members))
    ]
    blocks = [blocks[m] for m in range(len(members))]
    page_ids = (
        rel_exp[: len(members), None] * pages_here + jnp.arange(pages_here, dtype=i32)[None, :]
    ).reshape(-1)
    hits = (page_table[None, :, :] == page_ids[:, None, None]).astype(i32)
    page_request = jnp.sum(hits * jnp.arange(req_slots, dtype=i32)[None, :, None], axis=(1, 2))
    page_slot = jnp.sum(hits * jnp.arange(max_pages, dtype=i32)[None, None, :], axis=(1, 2))
    rel_rows = lambda a: a.reshape(exp_count, tok_rows)[rel_exp].reshape(1, -1)
    partial, level = attend(
        blocks,
        far,
        rel_rows(row_request),
        rel_rows(row_position),
        page_request,
        page_slot,
        page_len,
    )
    other = send(partial[columns:], 1, 0, 0)
    other_level = send(level[columns // HEAD_DIM :], 1, 0, 0)

    slot_ids = jnp.arange(slot_count, dtype=i32)
    own_mark = slot_ids == own_slot
    own_expert = jnp.sum(jnp.where(own_mark, slot_expert, 0))
    twins = slot_expert == own_expert
    copies = jnp.sum(twins.astype(i32))
    own_rank = jnp.sum((twins & (slot_ids < own_slot)).astype(i32))
    gates = jnp.transpose(route_gate)
    gates = jnp.stack([send_req(gates, 0, dc) for dc in range(nc)])
    gates = jnp.stack([send_req(gates, dy, 0) for dy in range(ny)])
    gates = jnp.stack([send(gates, 0, 0, dx) for dx in range(nx)], axis=2)
    gates = jnp.stack([send(gates, 0, dl, 0) for dl in range(2)], axis=2)
    gates = jnp.stack([send(gates, dh, 0, 0) for dh in range(2)], axis=2)
    gates = gates.reshape(slot_count, TOPK, tok_rows)
    rel_slots = (rel_req[:, None] * exp_count + rel_exp[None, :]).reshape(-1)
    named = (route_expert == own_expert).reshape(slot_count, tok_rows, TOPK)[rel_slots]
    named = jnp.transpose(named, (0, 2, 1))
    chunk_rows = exp_count * tok_rows
    entries = -(-exp_count * capacity // 16) * 16
    row_gate = jnp.sum(jnp.where(named, gates, 0.0), axis=1).reshape(ny, nc, chunk_rows)
    mine = jnp.any(named, axis=1) & (rel_slots % copies == own_rank)[:, None]
    mine = mine.reshape(ny, nc, chunk_rows)
    place = jnp.where(mine, jnp.cumsum(mine.astype(i32), axis=2) - 1, -1)
    other, place, row_gate = lax.optimization_barrier((other, place, row_gate))

    mixed = project(partial, level, other, other_level, out_proj)
    mixed = mixed.reshape(len(zs), nx, tok_rows, width)
    total = resid.astype(f32)
    for i in reversed(range(len(zs))):
        line = mixed[i, 0].astype(f32)
        for dx in range(1, nx):
            line = line + send(mixed[i, dx], 0, 0, -dx).astype(f32)
        total = total + (send(line.astype(bf16), *zs[i], 0).astype(f32) if i else line)
    stream = total
    normed = rms_normed(stream, norm_gain)

    piece = {}
    for i in reversed(range(len(zs))):
        piece[i, 0, 0] = send(normed, *zs[i], 0)
    x_first = [dh == 0 for dh, dl in zs]
    for i in range(len(zs)):
        for dx in range(1, nx):
            piece[i, dx, 0] = send(piece[i, 0, 0], 0, 0, dx)
        if x_first[i]:
            for dx in range(nx):
                for dy in range(1, ny):
                    piece[i, dx, dy] = send_req(piece[i, dx, 0], dy, 0)
        else:
            for dy in range(1, ny):
                piece[i, 0, dy] = send_req(piece[i, 0, 0], dy, 0)
                for dx in range(1, nx):
                    piece[i, dx, dy] = send(piece[i, 0, dy], 0, 0, dx)
    chunks = {}
    for dy in range(ny):
        chunks[dy, 0] = join([piece[i, dx, dy] for i in range(len(zs)) for dx in range(nx)])
        for dc in range(1, nc):
            chunks[dy, dc] = send_req(chunks[dy, 0], 0, dc)

    sums = {}
    for dy in range(ny):
        extra = None
        if dy == 0:
            extra = shared_expert(
                chunks[0, 0], shared_scalar, shared_gate.T, shared_up.T, shared_down
            )
        answers = routed_expert(
            [chunks[dy, dc] for dc in range(nc)],
            place[dy],
            row_gate[dy],
            extra,
            expert_gate,
            expert_up,
            expert_down,
            entries,
        )
        here = answers[0].astype(f32)
        for dc in range(1, nc):
            here = here + send_req(answers[dc], 0, -dc).astype(f32)
        here = here.astype(bf16).reshape(len(zs), nx, tok_rows, width)
        for i in range(len(zs)):
            for dx in range(nx):
                sums[i, dx, dy] = here[i, dx]
    total = stream
    for i in reversed(range(len(zs))):
        line = {}
        if x_first[i]:
            for dx in range(nx):
                line[dx] = sums[i, dx, 0].astype(f32)
                for dy in range(1, ny):
                    line[dx] = line[dx] + send_req(sums[i, dx, dy], -dy, 0).astype(f32)
            out = line[0]
            for dx in range(1, nx):
                out = out + send(line[dx].astype(bf16), 0, 0, -dx).astype(f32)
        else:
            for dy in range(ny):
                line[dy] = sums[i, 0, dy].astype(f32)
                for dx in range(1, nx):
                    line[dy] = line[dy] + send(sums[i, dx, dy], 0, 0, -dx).astype(f32)
            out = line[0]
            for dy in range(1, ny):
                out = out + send_req(line[dy].astype(bf16), -dy, 0).astype(f32)
        total = total + (send(out.astype(bf16), *zs[i], 0).astype(f32) if i else out)
    return total.astype(bf16)


def solution(mesh):
    placed = (
        P(("req", "exp"), None),
        P(("req", "exp"), None),
        P(("req", "exp"), None, None),
        P(("req", "exp"), None, None),
        P("req", None),
        P("req"),
        P("req"),
        P("exp", None),
        P(),
        P(("req", "exp"), None, None),
        P(("req", "exp"), None, None),
        P(("req", "exp"), None, None),
        P(None, "exp"),
        P(None, "exp"),
        P("exp", None),
        P(),
        P(),
        P(),
        P(("req", "exp"), None),
    )
    return jax.shard_map(
        shards, mesh=mesh, in_specs=placed, out_specs=P(("req", "exp"), None), check_vma=False
    )
```

time: 445 us -> 308 us (0.69)
  Pallas kernels: 178 us -> 77.9 us
  waiting for transfers between devices: 150 us -> 122 us
  local copies, waits for them, and re-layouts: 26.8 us -> 17.8 us
    pallas_call x4 -> x12, Pallas kernels: 137 us -> 36.9 us  [the longest x8 18.6 us: pack(): pl.pallas_call(pack_kernel, out_shape=jax.ShapeDtypeStruct((rows, count *...]
    ppermute x47 -> x55, waiting for transfers between devices: 150 us -> 122 us  [the longest x37 84.6 us: send(): return lax.ppermute(value, 'exp', pairs)]
    unnamed x70 -> x74, local copies, waits for them, and re-layouts: 16.5 us -> 7.44 us
    ppermute x47 -> x55, starting transfers between devices: 65.6 us -> 73.6 us  [the longest x37 55 us: send(): return lax.ppermute(value, 'exp', pairs)]
    all_to_all x1 -> x0, starting transfers between devices: 7.4 us -> none  [shards(): lax.all_to_all(jnp.concatenate([by_heads(cache_key), by_heads(cache_value...]
  transfers between devices with their start and end apart: 48 -> 55, of which waited for: 28 -> 27; matrix products, arithmetic and copies ran while one was open for 6% -> 6% of each run, Pallas kernels for 25% -> 23%
where the time goes in v3:
time: 308 us; the launch traced here: 306 us
  waiting for transfers between devices  122 us (40%)
  Pallas kernels  77.9 us (25%)
  starting transfers between devices  73.6 us (24%)
  local copies, waits for them, and re-layouts  17.8 us (6%)
  other arithmetic  12.5 us (4%)
    ppermute x37, waiting for transfers between devices, send(): return lax.ppermute(value, 'exp', pairs)  84.6 us
    ppermute x37, starting transfers between devices, send(): return lax.ppermute(value, 'exp', pairs)  55 us
    ppermute x18, waiting for transfers between devices, send_req(): return lax.ppermute(value, 'req', pairs)  37.3 us
    pallas_call x2, Pallas kernels, routed_expert(): pl.pallas_call(functools.partial(routed_kernel, count, entries), out_shap...  32.2 us
    ppermute x18, starting transfers between devices, send_req(): return lax.ppermute(value, 'req', pairs)  18.7 us
    pallas_call x8, Pallas kernels, pack(): pl.pallas_call(pack_kernel, out_shape=jax.ShapeDtypeStruct((rows, count *...  18.6 us
    pallas_call x1, Pallas kernels, shared_expert(): pl.pallas_call(shared_kernel, out_shape=jax.ShapeDtypeStruct(rows.shape,...  8.74 us
    pallas_call x1, Pallas kernels, attend(): pl.pallas_call(functools.partial(attend_kernel, members, tokens, page_len...  7.81 us
  transfers between devices with their start and end apart: 55, of which 27 were waited for; matrix products, arithmetic and copies ran while one was open for 6% of the time, Pallas kernels for 23%

profile of v3, /device:TPU:0, one launch (start us, length us, event | category | flops | bytes accessed | tf_op | source)
XLA Modules:
  0.0 305.6 jit_solution(7466778730654557270)
XLA Ops:
  0.0 4.0 %collective-permute-start.3 = (bf16[64,2048]{1,0:T(8,128)(2,1)}, bf16[64,2048]{1,0:T(8,128)(2,1)S(1)}, u32[]{:S(2)}, u32[]{:S(2)}) collective-permute-start(bf16[64,2048]{1,0:T(8,128)(2,1)} %refs_2_.7), channel_id=1, source_target_pairs={{0,4},{1,5},{2,6},{3,7},{4,0},{5,1},{6,2},{7,3},{8,12},{9,13},{10,... | collective-permute-start | bytes 786440 | tf_op jit(solution)/shard_map/ppermute | solution.py:366
  31.1 11.5 %collective-permute-done.10 = f32[2,2,4,64]{3,2,1,0:T(4,128)S(1)} collective-permute-done((f32[2,2,4,64]{3,2,1,0:T(4,128)S(1)}, f32[2,2,4,64]{3,2,1,0:T(4,128)S(1)}, u32[]{:S(2)}, u32[]{:S(2)}) %collective-permute-start.10) | collective-permute-done | bytes 4128 | tf_op jit(solution)/shard_map/ppermute | solution.py:366
  60.2 3.8 %collective-permute-start.12 = (f32[2,2,2,2,4,64]{5,4,1,0,3,2:T(4,128)S(1)}, f32[2,2,2,2,4,64]{5,4,1,0,3,2:T(4,128)S(1)}, u32[]{:S(2)}, u32[]{:S(2)}) collective-permute-start(f32[2,2,2,2,4,64]{5,4,1,0,3,2:T(4,128)S(1)} %get-tuple-element.51), channel_id=1, source_target_pairs={{0,4},{1,5},{2,6},{3,7},{4,0},{5,1},{6,2},{7,3},{8,12},{9,13},{10,... | collective-permute-start | bytes 49160 | tf_op jit(solution)/shard_map/ppermute | solution.py:366
  66.0 7.8 %shard_map.189 = (bf16[512,512]{1,0:T(8,128)(2,1)S(1)}, f32[4,1,512]{2,1,0:T(1,128)S(1)}) custom-call(s32[8]{0:T(128)S(1)} %get-tuple-element.24.page_req, s32[8]{0:T(128)S(1)} %get-tuple-element.23.page_slot, bf16[576,512]{1,0:T(8,128)(2,1)S(1)} %copy-done.2, bf16[576,512]{1,0:T(8,128)(2,1)S(1)} %collective-permute-done.refs_1_, ...), custom_call_target="tpu_custom_call" | custom-call | flops 1073741824 | bytes 2621440 | tf_op jit(solution)/shard_map/pallas_call | solution.py:95
  77.2 6.4 %collective-permute-done.7.theirs = bf16[256,512]{1,0:T(8,128)(2,1)S(1)} collective-permute-done((bf16[256,512]{1,0:T(8,128)(2,1)S(1)}, bf16[256,512]{1,0:T(8,128)(2,1)S(1)}, u32[]{:S(2)}, u32[]{:S(2)}) %collective-permute-start.7) | collective-permute-done | bytes 262176 | tf_op jit(solution)/shard_map/ppermute | solution.py:366
  84.8 4.6 %shard_map.190 = bf16[512,2048]{1,0:T(8,128)(2,1)} custom-call(bf16[512,512]{1,0:T(8,128)(2,1)} %copy-done.1, f32[4,1,512]{2,1,0:T(1,128)} %copy-done.4, bf16[256,512]{1,0:T(8,128)(2,1)} %copy-done.22, f32[2,1,512]{2,1,0:T(1,128)} %copy-done.30, bf16[256,2048]{1,0:T(8,128)(2,1)} %proj.1), custom_call_target="tpu_custom_call" | custom-call | flops 536870912 | bytes 3670016 | tf_op jit(solution)/shard_map/pallas_call | solution.py:140
  97.2 2.8 collective-permute-done.18
  100.1 2.8 collective-permute-done.16
  103.2 3.0 collective-permute-start.17
  107.6 9.4 %collective-permute-done.19 = bf16[64,2048]{1,0:T(8,128)(2,1)S(1)} collective-permute-done((bf16[64,2048]{1,0:T(8,128)(2,1)S(1)}, bf16[64,2048]{1,0:T(8,128)(2,1)S(1)}, u32[]{:S(2)}, u32[]{:S(2)}) %collective-permute-start.19) | collective-permute-done | bytes 262176 | tf_op jit(solution)/shard_map/ppermute | solution.py:366
  117.0 6.4 %collective-permute-done.15 = bf16[64,2048]{1,0:T(8,128)(2,1)S(1)} collective-permute-done((bf16[64,2048]{1,0:T(8,128)(2,1)S(1)}, bf16[64,2048]{1,0:T(8,128)(2,1)S(1)}, u32[]{:S(2)}, u32[]{:S(2)}) %collective-permute-start.15) | collective-permute-done | bytes 262176 | tf_op jit(solution)/shard_map/ppermute | solution.py:366
  123.9 6.2 %collective-permute-start.22 = (bf16[64,2048]{1,0:T(8,128)(2,1)S(1)}, bf16[64,2048]{1,0:T(8,128)(2,1)S(1)}, u32[]{:S(2)}, u32[]{:S(2)}) collective-permute-start(bf16[64,2048]{1,0:T(8,128)(2,1)S(1)} %multiply_convert_fusion.refs_0_), channel_id=1, source_target_pairs={{0,2},{1,3},{2,0},{3,1},{4,6},{5,7},{6,4},{7,5},{8,10},{9,11},{10,... | collective-permute-start | bytes 786440 | tf_op jit(solution)/shard_map/ppermute | solution.py:366
  138.1 5.4 %collective-permute-done.26.refs_6_ = bf16[64,2048]{1,0:T(8,128)(2,1)S(1)} collective-permute-done((bf16[64,2048]{1,0:T(8,128)(2,1)S(1)}, bf16[64,2048]{1,0:T(8,128)(2,1)S(1)}, u32[]{:S(2)}, u32[]{:S(2)}) %collective-permute-start.26) | collective-permute-done | bytes 262176 | tf_op jit(solution)/shard_map/ppermute | solution.py:366
  145.5 4.4 %collective-permute-done.27.refs_7_ = bf16[64,2048]{1,0:T(8,128)(2,1)S(1)} collective-permute-done((bf16[64,2048]{1,0:T(8,128)(2,1)S(1)}, bf16[64,2048]{1,0:T(8,128)(2,1)S(1)}, u32[]{:S(2)}, u32[]{:S(2)}) %collective-permute-start.27) | collective-permute-done | bytes 262176 | tf_op jit(solution)/shard_map/ppermute | solution.py:366
  150.7 3.0 shard_map.191.rows.refs_0_
  157.7 5.3 %collective-permute-done.31.refs_0_ = bf16[64,2048]{1,0:T(8,128)(2,1)S(1)} collective-permute-done((bf16[64,2048]{1,0:T(8,128)(2,1)}, bf16[64,2048]{1,0:T(8,128)(2,1)S(1)}, u32[]{:S(2)}, u32[]{:S(2)}) %collective-permute-start.31) | collective-permute-done | bytes 262176 | tf_op jit(solution)/shard_map/ppermute | solution.py:376
  164.5 4.1 %collective-permute-done.32.refs_1_ = bf16[64,2048]{1,0:T(8,128)(2,1)S(1)} collective-permute-done((bf16[64,2048]{1,0:T(8,128)(2,1)}, bf16[64,2048]{1,0:T(8,128)(2,1)S(1)}, u32[]{:S(2)}, u32[]{:S(2)}) %collective-permute-start.32) | collective-permute-done | bytes 262176 | tf_op jit(solution)/shard_map/ppermute | solution.py:376
  170.2 4.1 %collective-permute-done.35.refs_4_ = bf16[64,2048]{1,0:T(8,128)(2,1)S(1)} collective-permute-done((bf16[64,2048]{1,0:T(8,128)(2,1)}, bf16[64,2048]{1,0:T(8,128)(2,1)S(1)}, u32[]{:S(2)}, u32[]{:S(2)}) %collective-permute-start.35) | collective-permute-done | bytes 262176 | tf_op jit(solution)/shard_map/ppermute | solution.py:376
  174.5 5.3 %collective-permute-done.37.refs_6_ = bf16[64,2048]{1,0:T(8,128)(2,1)S(1)} collective-permute-done((bf16[64,2048]{1,0:T(8,128)(2,1)}, bf16[64,2048]{1,0:T(8,128)(2,1)S(1)}, u32[]{:S(2)}, u32[]{:S(2)}) %collective-permute-start.37) | collective-permute-done | bytes 262176 | tf_op jit(solution)/shard_map/ppermute | solution.py:376
  180.2 5.3 %collective-permute-done.33.refs_2_ = bf16[64,2048]{1,0:T(8,128)(2,1)S(1)} collective-permute-done((bf16[64,2048]{1,0:T(8,128)(2,1)}, bf16[64,2048]{1,0:T(8,128)(2,1)S(1)}, u32[]{:S(2)}, u32[]{:S(2)}) %collective-permute-start.33) | collective-permute-done | bytes 262176 | tf_op jit(solution)/shard_map/ppermute | solution.py:376
  185.5 5.2 %collective-permute-done.34.refs_3_ = bf16[64,2048]{1,0:T(8,128)(2,1)S(1)} collective-permute-done((bf16[64,2048]{1,0:T(8,128)(2,1)}, bf16[64,2048]{1,0:T(8,128)(2,1)S(1)}, u32[]{:S(2)}, u32[]{:S(2)}) %collective-permute-start.34) | collective-permute-done | bytes 262176 | tf_op jit(solution)/shard_map/ppermute | solution.py:376
  192.2 3.0 shard_map.194.refs_0_
  199.9 8.7 %shard_map.192.refs_5_ = bf16[512,2048]{1,0:T(8,128)(2,1)S(1)} custom-call(bf16[512,2048]{1,0:T(8,128)(2,1)S(1)} %copy-done, bf16[1,2048]{1,0:T(2,128)(2,1)S(1)} %reshape.518.scalar, bf16[704,2048]{1,0:T(8,128)(2,1)} %bitcast.187, bf16[704,2048]{1,0:T(8,128)(2,1)} %bitcast.188, bf16[704,2048]{1,0:T(8,128)(2,1)} %down_w.1), custom_call_target="tpu_custom_call" | custom-call | flops 4429185024 | bytes 12845056 | tf_op jit(solution)/shard_map/pallas_call | solution.py:211
  210.0 16.6 %shard_map.193 = (bf16[512,2048]{1,0:T(8,128)(2,1)}, bf16[512,2048]{1,0:T(8,128)(2,1)}) custom-call(bf16[512,2048]{1,0:T(8,128)(2,1)} %shard_map.191.rows.refs_0_, bf16[512,2048]{1,0:T(8,128)(2,1)} %collective-permute-done.28.refs_1_, s32[2,1,512]{2,1,0:T(1,128)} %get-tuple-element.59.refs_2_, s32[2,512,1]{2,1,0:T(8,128)} %copy.50.refs_3_, ...), custom_call_target="tpu_custom_call" | custom-call | flops 8254390272 | bytes 25690112 | tf_op jit(solution)/shard_map/pallas_call | solution.py:279
  227.7 15.6 %shard_map.195 = (bf16[512,2048]{1,0:T(8,128)(2,1)}, bf16[512,2048]{1,0:T(8,128)(2,1)}) custom-call(bf16[512,2048]{1,0:T(8,128)(2,1)} %shard_map.194.refs_0_, bf16[512,2048]{1,0:T(8,128)(2,1)} %collective-permute-done.39.refs_1_, s32[2,1,512]{2,1,0:T(1,128)} %get-tuple-element.58.refs_2_, s32[2,512,1]{2,1,0:T(8,128)} %reshape_squeeze.24.refs_3_, ...), custom_call_target="tpu_custom_call" | custom-call | flops 8254390272 | bytes 25690112 | tf_op jit(solution)/shard_map/pallas_call | solution.py:279
  244.3 3.5 %collective-permute-done.40 = bf16[512,2048]{1,0:T(8,128)(2,1)S(1)} collective-permute-done((bf16[512,2048]{1,0:T(8,128)(2,1)}, bf16[512,2048]{1,0:T(8,128)(2,1)S(1)}, u32[]{:S(2)}, u32[]{:S(2)}) %collective-permute-start.40) | collective-permute-done | bytes 2097184 | tf_op jit(solution)/shard_map/ppermute | solution.py:376
  254.7 3.5 %collective-permute-done.41 = bf16[64,2048]{1,0:T(8,128)(2,1)S(1)} collective-permute-done((bf16[64,2048]{1,0:T(8,128)(2,1)S(1)}, bf16[64,2048]{1,0:T(8,128)(2,1)S(1)}, u32[]{:S(2)}, u32[]{:S(2)}) %collective-permute-start.41) | collective-permute-done | bytes 262176 | tf_op jit(solution)/shard_map/ppermute | solution.py:366
  259.7 4.1 %collective-permute-done.45 = bf16[64,2048]{1,0:T(8,128)(2,1)S(1)} collective-permute-done((bf16[64,2048]{1,0:T(8,128)(2,1)S(1)}, bf16[64,2048]{1,0:T(8,128)(2,1)S(1)}, u32[]{:S(2)}, u32[]{:S(2)}) %collective-permute-start.45) | collective-permute-done | bytes 262176 | tf_op jit(solution)/shard_map/ppermute | solution.py:366
  265.5 3.9 %collective-permute-done.30 = bf16[64,2048]{1,0:T(8,128)(2,1)S(1)} collective-permute-done((bf16[64,2048]{1,0:T(8,128)(2,1)S(1)}, bf16[64,2048]{1,0:T(8,128)(2,1)S(1)}, u32[]{:S(2)}, u32[]{:S(2)}) %collective-permute-start.30) | collective-permute-done | bytes 262176 | tf_op jit(solution)/shard_map/ppermute | solution.py:366
  270.9 3.3 %collective-permute-done.44 = bf16[64,2048]{1,0:T(8,128)(2,1)S(1)} collective-permute-done((bf16[64,2048]{1,0:T(8,128)(2,1)S(1)}, bf16[64,2048]{1,0:T(8,128)(2,1)S(1)}, u32[]{:S(2)}, u32[]{:S(2)}) %collective-permute-start.44) | collective-permute-done | bytes 262176 | tf_op jit(solution)/shard_map/ppermute | solution.py:366
  282.4 4.7 %collective-permute-start.47 = (bf16[64,2048]{1,0:T(8,128)(2,1)S(1)}, bf16[64,2048]{1,0:T(8,128)(2,1)S(1)}, u32[]{:S(2)}, u32[]{:S(2)}) collective-permute-start(bf16[64,2048]{1,0:T(8,128)(2,1)S(1)} %get-tuple-element.32), channel_id=1, source_target_pairs={{0,4},{1,5},{2,6},{3,7},{4,0},{5,1},{6,2},{7,3},{8,12},{9,13},{10,... | collective-permute-start | bytes 786440 | tf_op jit(solution)/shard_map/ppermute | solution.py:366
  290.5 12.2 %collective-permute-done.47 = bf16[64,2048]{1,0:T(8,128)(2,1)S(1)} collective-permute-done((bf16[64,2048]{1,0:T(8,128)(2,1)S(1)}, bf16[64,2048]{1,0:T(8,128)(2,1)S(1)}, u32[]{:S(2)}, u32[]{:S(2)}) %collective-permute-start.47) | collective-permute-done | bytes 262176 | tf_op jit(solution)/shard_map/ppermute | solution.py:366
  (243 shorter events, 113.7 us)
Async XLA Ops:
  0.0 42.8 %collective-permute-start.3 = (bf16[64,2048]{1,0:T(8,128)(2,1)}, bf16[64,2048]{1,0:T(8,128)(2,1)S(1)}, u32[]{:S(2)}, u32[]{:S(2)}) collective-permute-start(bf16[64,2048]{1,0:T(8,128)(2,1)} %refs_2_.7), channel_id=1, source_target_pairs={{0,4},{1,5},{2,6},{3,7},{4,0},{5,1},{6,2},{7,3},{8,12},{9,13},{10,... | collective-permute-start | bytes 786440 | tf_op jit(solution)/shard_map/ppermute | solution.py:366
  7.3 56.8 %collective-permute-start = (bf16[576,512]{1,0:T(8,128)(2,1)}, bf16[576,512]{1,0:T(8,128)(2,1)S(1)}, u32[]{:S(2)}, u32[]{:S(2)}) collective-permute-start(bf16[576,512]{1,0:T(8,128)(2,1)} %shard_map.182), channel_id=1, source_target_pairs={{0,1},{1,0},{2,3},{3,2},{4,5},{5,4},{6,7},{7,6},{8,9},{9,8},{10,11... | collective-permute-start | bytes 1769480 | tf_op jit(solution)/shard_map/ppermute | solution.py:366
  12.0 52.1 %collective-permute-start.1 = (bf16[576,512]{1,0:T(8,128)(2,1)}, bf16[576,512]{1,0:T(8,128)(2,1)S(1)}, u32[]{:S(2)}, u32[]{:S(2)}) collective-permute-start(bf16[576,512]{1,0:T(8,128)(2,1)} %shard_map.183), channel_id=1, source_target_pairs={{0,2},{1,3},{2,0},{3,1},{4,6},{5,7},{6,4},{7,5},{8,10},{9,11},{10,... | collective-permute-start | bytes 1769480 | tf_op jit(solution)/shard_map/ppermute | solution.py:366
  16.8 47.3 %collective-permute-start.2 = (bf16[576,512]{1,0:T(8,128)(2,1)}, bf16[576,512]{1,0:T(8,128)(2,1)S(1)}, u32[]{:S(2)}, u32[]{:S(2)}) collective-permute-start(bf16[576,512]{1,0:T(8,128)(2,1)} %shard_map.184), channel_id=1, source_target_pairs={{0,3},{1,2},{2,1},{3,0},{4,7},{5,6},{6,5},{7,4},{8,11},{9,10},{10,... | collective-permute-start | bytes 1769480 | tf_op jit(solution)/shard_map/ppermute | solution.py:366
  29.6 13.0 %collective-permute-start.10 = (f32[2,2,4,64]{3,2,1,0:T(4,128)S(1)}, f32[2,2,4,64]{3,2,1,0:T(4,128)S(1)}, u32[]{:S(2)}, u32[]{:S(2)}) collective-permute-start(f32[2,2,4,64]{3,2,1,0:T(4,128)S(1)} %get-tuple-element.61), channel_id=1, source_target_pairs={{0,1},{1,0},{2,3},{3,2},{4,5},{5,4},{6,7},{7,6},{8,9},{9,8},{10,11... | collective-permute-start | bytes 12296 | tf_op jit(solution)/shard_map/ppermute | solution.py:366
  42.7 12.4 %collective-permute-start.11 = (f32[2,2,2,4,64]{4,3,1,0,2:T(4,128)S(1)}, f32[2,2,2,4,64]{4,3,1,0,2:T(4,128)S(1)}, u32[]{:S(2)}, u32[]{:S(2)}) collective-permute-start(f32[2,2,2,4,64]{4,3,1,0,2:T(4,128)S(1)} %get-tuple-element.53), channel_id=1, source_target_pairs={{0,2},{1,3},{2,0},{3,1},{4,6},{5,7},{6,4},{7,5},{8,10},{9,11},{10,... | collective-permute-start | bytes 24584 | tf_op jit(solution)/shard_map/ppermute | solution.py:366
  45.6 11.5 %collective-permute-start.4 = (bf16[64,512]{1,0:T(8,128)(2,1)}, bf16[64,512]{1,0:T(8,128)(2,1)S(1)}, u32[]{:S(2)}, u32[]{:S(2)}) collective-permute-start(bf16[64,512]{1,0:T(8,128)(2,1)} %shard_map.186), channel_id=1, source_target_pairs={{0,1},{1,0},{2,3},{3,2},{4,5},{5,4},{6,7},{7,6},{8,9},{9,8},{10,11... | collective-permute-start | bytes 196616 | tf_op jit(solution)/shard_map/ppermute | solution.py:366
  60.2 14.8 %collective-permute-start.12 = (f32[2,2,2,2,4,64]{5,4,1,0,3,2:T(4,128)S(1)}, f32[2,2,2,2,4,64]{5,4,1,0,3,2:T(4,128)S(1)}, u32[]{:S(2)}, u32[]{:S(2)}) collective-permute-start(f32[2,2,2,2,4,64]{5,4,1,0,3,2:T(4,128)S(1)} %get-tuple-element.51), channel_id=1, source_target_pairs={{0,4},{1,5},{2,6},{3,7},{4,0},{5,1},{6,2},{7,3},{8,12},{9,13},{10,... | collective-permute-start | bytes 49160 | tf_op jit(solution)/shard_map/ppermute | solution.py:366
  93.8 13.8 %collective-permute-start.20 = (bf16[64,2048]{1,0:T(8,128)(2,1)S(1)}, bf16[64,2048]{1,0:T(8,128)(2,1)S(1)}, u32[]{:S(2)}, u32[]{:S(2)}) collective-permute-start(bf16[64,2048]{1,0:T(8,128)(2,1)S(1)} %get-tuple-element.47), channel_id=1, source_target_pairs={{0,1},{1,0},{2,3},{3,2},{4,5},{5,4},{6,7},{7,6},{8,9},{9,8},{10,11... | collective-permute-start | bytes 786440 | tf_op jit(solution)/shard_map/ppermute | solution.py:366
  103.1 13.9 %collective-permute-start.19 = (bf16[64,2048]{1,0:T(8,128)(2,1)S(1)}, bf16[64,2048]{1,0:T(8,128)(2,1)S(1)}, u32[]{:S(2)}, u32[]{:S(2)}) collective-permute-start(bf16[64,2048]{1,0:T(8,128)(2,1)S(1)} %get-tuple-element.44), channel_id=1, source_target_pairs={{0,2},{1,3},{2,0},{3,1},{4,6},{5,7},{6,4},{7,5},{8,10},{9,11},{10,... | collective-permute-start | bytes 786440 | tf_op jit(solution)/shard_map/ppermute | solution.py:366
  103.2 13.8 %collective-permute-start.17 = (bf16[64,2048]{1,0:T(8,128)(2,1)S(1)}, bf16[64,2048]{1,0:T(8,128)(2,1)S(1)}, u32[]{:S(2)}, u32[]{:S(2)}) collective-permute-start(bf16[64,2048]{1,0:T(8,128)(2,1)S(1)} %get-tuple-element.45), channel_id=1, source_target_pairs={{0,4},{1,5},{2,6},{3,7},{4,0},{5,1},{6,2},{7,3},{8,12},{9,13},{10,... | collective-permute-start | bytes 786440 | tf_op jit(solution)/shard_map/ppermute | solution.py:366
  106.2 17.2 %collective-permute-start.15 = (bf16[64,2048]{1,0:T(8,128)(2,1)S(1)}, bf16[64,2048]{1,0:T(8,128)(2,1)S(1)}, u32[]{:S(2)}, u32[]{:S(2)}) collective-permute-start(bf16[64,2048]{1,0:T(8,128)(2,1)S(1)} %get-tuple-element.43), channel_id=1, source_target_pairs={{0,6},{1,7},{2,4},{3,5},{4,2},{5,3},{6,0},{7,1},{8,14},{9,15},{10,... | collective-permute-start | bytes 786440 | tf_op jit(solution)/shard_map/ppermute | solution.py:366
  132.1 11.5 %collective-permute-start.26 = (bf16[64,2048]{1,0:T(8,128)(2,1)S(1)}, bf16[64,2048]{1,0:T(8,128)(2,1)S(1)}, u32[]{:S(2)}, u32[]{:S(2)}) collective-permute-start(bf16[64,2048]{1,0:T(8,128)(2,1)S(1)} %multiply_convert_fusion.refs_0_), channel_id=1, source_target_pairs={{0,6},{1,7},{2,4},{3,5},{4,2},{5,3},{6,0},{7,1},{8,14},{9,15},{10,... | collective-permute-start | bytes 786440 | tf_op jit(solution)/shard_map/ppermute | solution.py:366
  153.6 56.4 %collective-permute-start.28 = (bf16[512,2048]{1,0:T(8,128)(2,1)}, bf16[512,2048]{1,0:T(8,128)(2,1)}, u32[]{:S(2)}, u32[]{:S(2)}) collective-permute-start(bf16[512,2048]{1,0:T(8,128)(2,1)} %shard_map.191.rows.refs_0_), channel_id=1, source_target_pairs={{0,8},{8,0},{16,24},{24,16},{1,9},{9,1},{17,25},{25,17},{2,10},{10... | collective-permute-start | bytes 6291464 | tf_op jit(solution)/shard_map/ppermute | solution.py:376
  155.2 13.4 %collective-permute-start.32 = (bf16[64,2048]{1,0:T(8,128)(2,1)}, bf16[64,2048]{1,0:T(8,128)(2,1)S(1)}, u32[]{:S(2)}, u32[]{:S(2)}) collective-permute-start(bf16[64,2048]{1,0:T(8,128)(2,1)} %copy-done.16), channel_id=1, source_target_pairs={{0,16},{8,24},{16,0},{24,8},{1,17},{9,25},{17,1},{25,9},{2,18},{10... | collective-permute-start | bytes 786440 | tf_op jit(solution)/shard_map/ppermute | solution.py:376
  155.7 18.5 %collective-permute-start.35 = (bf16[64,2048]{1,0:T(8,128)(2,1)}, bf16[64,2048]{1,0:T(8,128)(2,1)S(1)}, u32[]{:S(2)}, u32[]{:S(2)}) collective-permute-start(bf16[64,2048]{1,0:T(8,128)(2,1)} %copy-done.15), channel_id=1, source_target_pairs={{0,16},{8,24},{16,0},{24,8},{1,17},{9,25},{17,1},{25,9},{2,18},{10... | collective-permute-start | bytes 786440 | tf_op jit(solution)/shard_map/ppermute | solution.py:376
  157.3 22.6 %collective-permute-start.37 = (bf16[64,2048]{1,0:T(8,128)(2,1)}, bf16[64,2048]{1,0:T(8,128)(2,1)S(1)}, u32[]{:S(2)}, u32[]{:S(2)}) collective-permute-start(bf16[64,2048]{1,0:T(8,128)(2,1)} %copy-done.14), channel_id=1, source_target_pairs={{0,16},{8,24},{16,0},{24,8},{1,17},{9,25},{17,1},{25,9},{2,18},{10... | collective-permute-start | bytes 786440 | tf_op jit(solution)/shard_map/ppermute | solution.py:376
  163.0 22.5 %collective-permute-start.33 = (bf16[64,2048]{1,0:T(8,128)(2,1)}, bf16[64,2048]{1,0:T(8,128)(2,1)S(1)}, u32[]{:S(2)}, u32[]{:S(2)}) collective-permute-start(bf16[64,2048]{1,0:T(8,128)(2,1)} %copy-done.12), channel_id=1, source_target_pairs={{0,16},{8,24},{16,0},{24,8},{1,17},{9,25},{17,1},{25,9},{2,18},{10... | collective-permute-start | bytes 786440 | tf_op jit(solution)/shard_map/ppermute | solution.py:376
  168.6 22.0 %collective-permute-start.34 = (bf16[64,2048]{1,0:T(8,128)(2,1)}, bf16[64,2048]{1,0:T(8,128)(2,1)S(1)}, u32[]{:S(2)}, u32[]{:S(2)}) collective-permute-start(bf16[64,2048]{1,0:T(8,128)(2,1)} %copy-done.13), channel_id=1, source_target_pairs={{0,16},{8,24},{16,0},{24,8},{1,17},{9,25},{17,1},{25,9},{2,18},{10... | collective-permute-start | bytes 786440 | tf_op jit(solution)/shard_map/ppermute | solution.py:376
  174.2 16.4 %collective-permute-start.36 = (bf16[64,2048]{1,0:T(8,128)(2,1)S(1)}, bf16[64,2048]{1,0:T(8,128)(2,1)S(1)}, u32[]{:S(2)}, u32[]{:S(2)}) collective-permute-start(bf16[64,2048]{1,0:T(8,128)(2,1)S(1)} %collective-permute-done.35.refs_4_), channel_id=1, source_target_pairs={{0,1},{1,0},{2,3},{3,2},{4,5},{5,4},{6,7},{7,6},{8,9},{9,8},{10,11... | collective-permute-start | bytes 786440 | tf_op jit(solution)/shard_map/ppermute | solution.py:366
  195.2 31.9 %collective-permute-start.39 = (bf16[512,2048]{1,0:T(8,128)(2,1)}, bf16[512,2048]{1,0:T(8,128)(2,1)}, u32[]{:S(2)}, u32[]{:S(2)}) collective-permute-start(bf16[512,2048]{1,0:T(8,128)(2,1)} %shard_map.194.refs_0_), channel_id=1, source_target_pairs={{0,8},{8,0},{16,24},{24,16},{1,9},{9,1},{17,25},{25,17},{2,10},{10... | collective-permute-start | bytes 6291464 | tf_op jit(solution)/shard_map/ppermute | solution.py:376
  226.6 16.9 %collective-permute-start.29 = (bf16[512,2048]{1,0:T(8,128)(2,1)}, bf16[512,2048]{1,0:T(8,128)(2,1)S(1)}, u32[]{:S(2)}, u32[]{:S(2)}) collective-permute-start(bf16[512,2048]{1,0:T(8,128)(2,1)} %get-tuple-element.20), channel_id=1, source_target_pairs={{0,8},{8,0},{16,24},{24,16},{1,9},{9,1},{17,25},{25,17},{2,10},{10... | collective-permute-start | bytes 6291464 | tf_op jit(solution)/shard_map/ppermute | solution.py:376
  249.3 14.5 %collective-permute-start.45 = (bf16[64,2048]{1,0:T(8,128)(2,1)S(1)}, bf16[64,2048]{1,0:T(8,128)(2,1)S(1)}, u32[]{:S(2)}, u32[]{:S(2)}) collective-permute-start(bf16[64,2048]{1,0:T(8,128)(2,1)S(1)} %get-tuple-element.42), channel_id=1, source_target_pairs={{0,1},{1,0},{2,3},{3,2},{4,5},{5,4},{6,7},{7,6},{8,9},{9,8},{10,11... | collective-permute-start | bytes 786440 | tf_op jit(solution)/shard_map/ppermute | solution.py:366
  251.1 18.3 %collective-permute-start.30 = (bf16[64,2048]{1,0:T(8,128)(2,1)S(1)}, bf16[64,2048]{1,0:T(8,128)(2,1)S(1)}, u32[]{:S(2)}, u32[]{:S(2)}) collective-permute-start(bf16[64,2048]{1,0:T(8,128)(2,1)S(1)} %get-tuple-element.33), channel_id=1, source_target_pairs={{0,1},{1,0},{2,3},{3,2},{4,5},{5,4},{6,7},{7,6},{8,9},{9,8},{10,11... | collective-permute-start | bytes 786440 | tf_op jit(solution)/shard_map/ppermute | solution.py:366
  251.4 22.8 %collective-permute-start.44 = (bf16[64,2048]{1,0:T(8,128)(2,1)S(1)}, bf16[64,2048]{1,0:T(8,128)(2,1)S(1)}, u32[]{:S(2)}, u32[]{:S(2)}) collective-permute-start(bf16[64,2048]{1,0:T(8,128)(2,1)S(1)} %get-tuple-element.34), channel_id=1, source_target_pairs={{0,1},{1,0},{2,3},{3,2},{4,5},{5,4},{6,7},{7,6},{8,9},{9,8},{10,11... | collective-permute-start | bytes 786440 | tf_op jit(solution)/shard_map/ppermute | solution.py:366
  253.2 22.6 %collective-permute-start.53 = (bf16[64,2048]{1,0:T(8,128)(2,1)S(1)}, bf16[64,2048]{1,0:T(8,128)(2,1)S(1)}, u32[]{:S(2)}, u32[]{:S(2)}) collective-permute-start(bf16[64,2048]{1,0:T(8,128)(2,1)S(1)} %get-tuple-element.38), channel_id=1, source_target_pairs={{0,16},{8,24},{16,0},{24,8},{1,17},{9,25},{17,1},{25,9},{2,18},{10... | collective-permute-start | bytes 786440 | tf_op jit(solution)/shard_map/ppermute | solution.py:376
  258.2 17.6 %collective-permute-start.49 = (bf16[64,2048]{1,0:T(8,128)(2,1)S(1)}, bf16[64,2048]{1,0:T(8,128)(2,1)S(1)}, u32[]{:S(2)}, u32[]{:S(2)}) collective-permute-start(bf16[64,2048]{1,0:T(8,128)(2,1)S(1)} %get-tuple-element.40), channel_id=1, source_target_pairs={{0,16},{8,24},{16,0},{24,8},{1,17},{9,25},{17,1},{25,9},{2,18},{10... | collective-permute-start | bytes 786440 | tf_op jit(solution)/shard_map/ppermute | solution.py:376
  263.9 11.8 %collective-permute-start.42 = (bf16[64,2048]{1,0:T(8,128)(2,1)S(1)}, bf16[64,2048]{1,0:T(8,128)(2,1)S(1)}, u32[]{:S(2)}, u32[]{:S(2)}) collective-permute-start(bf16[64,2048]{1,0:T(8,128)(2,1)S(1)} %get-tuple-element.35), channel_id=1, source_target_pairs={{0,16},{8,24},{16,0},{24,8},{1,17},{9,25},{17,1},{25,9},{2,18},{10... | collective-permute-start | bytes 786440 | tf_op jit(solution)/shard_map/ppermute | solution.py:376
  274.2 12.9 %collective-permute-start.48 = (bf16[64,2048]{1,0:T(8,128)(2,1)S(1)}, bf16[64,2048]{1,0:T(8,128)(2,1)S(1)}, u32[]{:S(2)}, u32[]{:S(2)}) collective-permute-start(bf16[64,2048]{1,0:T(8,128)(2,1)S(1)} %get-tuple-element.41), channel_id=1, source_target_pairs={{0,16},{8,24},{16,0},{24,8},{1,17},{9,25},{17,1},{25,9},{2,18},{10... | collective-permute-start | bytes 786440 | tf_op jit(solution)/shard_map/ppermute | solution.py:376
  282.4 20.4 %collective-permute-start.47 = (bf16[64,2048]{1,0:T(8,128)(2,1)S(1)}, bf16[64,2048]{1,0:T(8,128)(2,1)S(1)}, u32[]{:S(2)}, u32[]{:S(2)}) collective-permute-start(bf16[64,2048]{1,0:T(8,128)(2,1)S(1)} %get-tuple-element.32), channel_id=1, source_target_pairs={{0,4},{1,5},{2,6},{3,7},{4,0},{5,1},{6,2},{7,3},{8,12},{9,13},{10,... | collective-permute-start | bytes 786440 | tf_op jit(solution)/shard_map/ppermute | solution.py:366
  287.1 15.6 %collective-permute-start.43 = (bf16[64,2048]{1,0:T(8,128)(2,1)S(1)}, bf16[64,2048]{1,0:T(8,128)(2,1)S(1)}, u32[]{:S(2)}, u32[]{:S(2)}) collective-permute-start(bf16[64,2048]{1,0:T(8,128)(2,1)S(1)} %get-tuple-element.29), channel_id=1, source_target_pairs={{0,6},{1,7},{2,4},{3,5},{4,2},{5,3},{6,0},{7,1},{8,14},{9,15},{10,... | collective-permute-start | bytes 786440 | tf_op jit(solution)/shard_map/ppermute | solution.py:366
  289.7 15.0 %collective-permute-start.51 = (bf16[64,2048]{1,0:T(8,128)(2,1)S(1)}, bf16[64,2048]{1,0:T(8,128)(2,1)S(1)}, u32[]{:S(2)}, u32[]{:S(2)}) collective-permute-start(bf16[64,2048]{1,0:T(8,128)(2,1)S(1)} %fusion.6), channel_id=1, source_target_pairs={{0,2},{1,3},{2,0},{3,1},{4,6},{5,7},{6,4},{7,5},{8,10},{9,11},{10,... | collective-permute-start | bytes 786440 | tf_op jit(solution)/shard_map/ppermute | solution.py:366
  (60 other events, 617.6 us)

commit v4 on v3

--- a/solution.py
+++ b/solution.py
@@ -13,34 +13,61 @@
 Z_CHIPS = 4
 
 
-def pack_kernel(order, *refs):
-    parts, out = refs[:-1], refs[-1]
-    at = 0
-    for part in parts:
-        rows = part.shape[0]
-        out[at : at + rows, :] = part[...]
-        at += rows
-
-
-def pack(parts, order, columns):
-    count = order.shape[0]
-    rows = sum(p.shape[0] for p in parts)
-    return pl.pallas_call(
-        pack_kernel,
-        out_shape=jax.ShapeDtypeStruct((rows, count * columns), parts[0].dtype),
+def pack_kernel(members, order, keys, values, queries, gates, blocks, far):
+    weights = gates[...]
+    high = weights.astype(jnp.bfloat16).astype(jnp.float32)
+    middle = (weights - high).astype(jnp.bfloat16).astype(jnp.float32)
+    low = weights - high - middle
+    weights = jnp.concatenate([high, middle, low, jnp.zeros_like(low)], axis=0)
+    weights = weights.astype(jnp.bfloat16)
+    for m in range(members):
+        tokens, rows = keys[m].shape[0], queries[m].shape[0]
+        blocks[m][:tokens, :] = keys[m][...]
+        blocks[m][tokens : 2 * tokens, :] = values[m][...]
+        blocks[m][2 * tokens : 2 * tokens + rows, :] = queries[m][...]
+        blocks[m][2 * tokens + rows :, :] = weights
+        far[m][...] = queries[m][...]
+
+
+def pack(keys, values, queries, gates, order, columns):
+    members = order.shape[0] // 2
+    tokens, rows = keys.shape[0], queries.shape[0]
+    block_rows = 2 * tokens + rows + 4 * gates.shape[0]
+
+    def kernel(order, *refs):
+        group = lambda i: refs[i * members : (i + 1) * members]
+        pack_kernel(
+            members,
+            order,
+            group(0),
+            group(1),
+            group(2),
+            refs[3 * members],
+            refs[3 * members + 1 : 4 * members + 1],
+            refs[4 * members + 1 :],
+        )
+
+    def column(n, m):
+        return pl.BlockSpec((n, columns), lambda j, order: (0, order[2 * m + j]))
+
+    result = pl.pallas_call(
+        kernel,
+        out_shape=[jax.ShapeDtypeStruct((block_rows, 2 * columns), keys.dtype)] * members
+        + [jax.ShapeDtypeStruct((rows, 2 * columns), keys.dtype)] * members,
         grid_spec=pltpu.PrefetchScalarGridSpec(
             num_scalar_prefetch=1,
-            grid=(count,),
-            in_specs=[
-                pl.BlockSpec((p.shape[0], columns), lambda j, order: (0, order[j]))
-                for p in parts
-            ],
-            out_specs=pl.BlockSpec((rows, columns), lambda j, order: (0, j)),
-        ),
+            grid=(2,),
+            in_specs=[column(n, m) for n in (tokens, tokens, rows) for m in range(members)]
+            + [pl.BlockSpec((gates.shape[0], columns), lambda j, order: (0, j))],
+            out_specs=[pl.BlockSpec((block_rows, columns), lambda j, order: (0, j))] * members
+            + [pl.BlockSpec((rows, columns), lambda j, order: (0, 1 - j))] * members,
+        ),
+        compiler_params=pltpu.CompilerParams(vmem_limit_bytes=32 * 1024 * 1024),
         cost_estimate=pl.CostEstimate(
-            flops=0, bytes_accessed=4 * rows * count * columns, transcendentals=0
-        ),
-    )(order, *parts)
+            flops=0, bytes_accessed=8 * members * block_rows * columns, transcendentals=0
+        ),
+    )(order, *[keys] * members, *[values] * members, *[queries] * members, gates)
+    return result[:members], result[members:]
 
 
 def attend_kernel(members, tokens, page_len, scale, page_req, page_slot, *refs):
@@ -48,7 +75,8 @@
     row_req, row_pos, out, level = refs
     keys = jnp.concatenate([block[:tokens, :] for block in blocks], axis=0)
     values = jnp.concatenate([block[tokens : 2 * tokens, :] for block in blocks], axis=0)
-    near = [block[2 * tokens :, :] for block in blocks]
+    tok_rows = far[0].shape[0]
+    near = [block[2 * tokens : 2 * tokens + tok_rows, :] for block in blocks]
     size = sum(q.shape[0] for q in near)
     for side, query in enumerate((near, [q[...] for q in far])):
         lanes = slice(side * size, (side + 1) * size)
@@ -84,11 +112,10 @@
         level[0, :, lanes] = jnp.where(seen, top + jnp.log(total), -1e30)
 
 
-def attend(blocks, far, row_req, row_pos, page_req, page_slot, page_len):
+def attend(blocks, far, row_req, row_pos, page_req, page_slot, page_len, tokens):
     members, rows = len(blocks), row_req.shape[1]
     block_rows, columns = blocks[0].shape
     tok_rows = far[0].shape[0]
-    tokens = (block_rows - tok_rows) // 2
     heads = columns // HEAD_DIM
     by_head = lambda n: pl.BlockSpec((n, HEAD_DIM), lambda h, *_: (0, h))
     whole = pl.BlockSpec((1, rows), lambda h, *_: (0, 0))
@@ -116,7 +143,7 @@
     )(page_req, page_slot, *blocks, *far, row_req, row_pos)
 
 
-def project_kernel(mine, mine_level, theirs, their_level, proj, out):
+def project_kernel(mine, mine_level, theirs, their_level, proj, stay, go):
     parts = []
     for head in range(mine.shape[0] // HEAD_DIM):
         dims = slice(head * HEAD_DIM, (head + 1) * HEAD_DIM)
@@ -127,34 +154,65 @@
         )
         parts.append(both.astype(jnp.bfloat16))
     attention = jnp.concatenate(parts, axis=0) if len(parts) > 1 else parts[0]
-    out[...] = lax.dot_general(
+    mixed = lax.dot_general(
         attention, proj[...], (((0,), (0,)), ((), ())), preferred_element_type=jnp.float32
-    ).astype(jnp.bfloat16)
-
-
-def project(mine, mine_level, theirs, their_level, proj):
+    )
+    rows = stay.shape[0]
+    stay[...] = mixed[:rows, :]
+    go[...] = mixed[rows:, :].astype(jnp.bfloat16)
+
+
+def project(place, mine, mine_level, theirs, their_level, proj, tok_rows):
     columns, width = proj.shape
-    rows = mine.shape[1]
     heads = columns // HEAD_DIM
-    size = rows // 4
+    size = mine.shape[1] // 4
     return pl.pallas_call(
         project_kernel,
-        out_shape=jax.ShapeDtypeStruct((rows, width), jnp.bfloat16),
-        grid=(4,),
+        out_shape=[
+            jax.ShapeDtypeStruct((tok_rows, width), jnp.float32),
+            jax.ShapeDtypeStruct((size - tok_rows, width), jnp.bfloat16),
+        ],
+        grid=(1,),
         in_specs=[
-            pl.BlockSpec((columns, size), lambda i: (0, i)),
-            pl.BlockSpec((heads, 1, size), lambda i: (0, 0, i)),
-            pl.BlockSpec((columns, size), lambda i: (0, (i + 2) % 4)),
-            pl.BlockSpec((heads, 1, size), lambda i: (0, 0, (i + 2) % 4)),
+            pl.BlockSpec((columns, size), lambda i: (0, place)),
+            pl.BlockSpec((heads, 1, size), lambda i: (0, 0, place)),
+            pl.BlockSpec((columns, size), lambda i: (0, (place + 2) % 4)),
+            pl.BlockSpec((heads, 1, size), lambda i: (0, 0, (place + 2) % 4)),
             pl.BlockSpec((columns, width), lambda i: (0, 0)),
         ],
-        out_specs=pl.BlockSpec((size, width), lambda i: (i, 0)),
+        out_specs=[
+            pl.BlockSpec((tok_rows, width), lambda i: (0, 0)),
+            pl.BlockSpec((size - tok_rows, width), lambda i: (0, 0)),
+        ],
         cost_estimate=pl.CostEstimate(
-            flops=2 * rows * columns * width,
-            bytes_accessed=2 * (2 * columns * rows + columns * width + rows * width),
-            transcendentals=2 * rows * heads,
+            flops=2 * size * columns * width,
+            bytes_accessed=2 * (2 * columns * size + columns * width + size * width),
+            transcendentals=2 * size * heads,
         ),
     )(mine, mine_level, theirs, their_level, proj)
+
+
+def add_kernel(*refs):
+    parts, out = refs[:-1], refs[-1]
+    total = parts[0][...].astype(jnp.float32)
+    for part in parts[1:]:
+        total = total + part[...].astype(jnp.float32)
+    out[...] = total.astype(out.dtype)
+
+
+def add_up(parts, dtype):
+    vmem = pl.BlockSpec(memory_space=pltpu.VMEM)
+    return pl.pallas_call(
+        add_kernel,
+        out_shape=jax.ShapeDtypeStruct(parts[0].shape, dtype),
+        in_specs=[vmem] * len(parts),
+        out_specs=vmem,
+        cost_estimate=pl.CostEstimate(
+            flops=len(parts) * parts[0].size,
+            bytes_accessed=4 * len(parts) * parts[0].size,
+            transcendentals=0,
+        ),
+    )(*parts)
 
 
 def join_kernel(*refs):
@@ -228,43 +286,52 @@
     )(rows, scalar.reshape(1, -1), gate_w, up_w, down_w)
 
 
-def routed_kernel(count, entries, *refs):
+def routed_kernel(count, entries, has_extra, *refs):
     chunks, refs = refs[:count], refs[count:]
-    place_row, place_col, row_gate, extra, gate_w, up_w, down_w = refs[:7]
-    outs, refs = refs[7 : 7 + count], refs[7 + count :]
-    packed, gate_v, up_v, down_v, sems = refs
+    place, row_gate, extra, gate_w, up_w, down_w = refs[:6]
+    outs, refs = refs[6 : 6 + count], refs[6 + count :]
+    rows, packed, gate_v, up_v, down_v, extra_v, sems = refs
+    moves = [(chunks[c], rows.at[c]) for c in range(count)]
+    moves += [(gate_w.at[0], gate_v), (up_w.at[0], up_v), (down_w.at[0], down_v)]
+    if has_extra:
+        moves.append((extra, extra_v))
     copies = [
-        pltpu.make_async_copy(src.at[0], dst, sems.at[i])
-        for i, (src, dst) in enumerate(((gate_w, gate_v), (up_w, up_v), (down_w, down_v)))
+        pltpu.make_async_copy(src, dst, sems.at[i]) for i, (src, dst) in enumerate(moves)
     ]
     for copy in copies:
         copy.start()
     size = chunks[0].shape[0]
+    wanted = lax.broadcasted_iota(jnp.int32, (entries, size), 0)
+    picks, weights = [], []
     for c in range(count):
-        wanted = lax.broadcasted_iota(jnp.int32, (entries, size), 0)
-        pick = jnp.where(place_row[c] == wanted, 1.0, 0.0).astype(jnp.bfloat16)
+        pick = jnp.where(place[c] == wanted, 1.0, 0.0)
+        picks.append(pick.astype(jnp.bfloat16))
+        weights.append(jnp.sum(pick * row_gate[c], axis=1, keepdims=True))
+        copies[c].wait()
         packed[c * entries : (c + 1) * entries, :] = jnp.dot(
-            pick, chunks[c][...], preferred_element_type=jnp.float32
+            picks[c], rows[c], preferred_element_type=jnp.float32
         ).astype(jnp.bfloat16)
-    copies[0].wait()
+    copies[count].wait()
     gate = jnp.dot(packed[...], gate_v[...], preferred_element_type=jnp.float32)
-    copies[1].wait()
+    copies[count + 1].wait()
     upper = jnp.dot(packed[...], up_v[...], preferred_element_type=jnp.float32)
     hidden = (silu(gate) * upper).astype(jnp.bfloat16)
-    copies[2].wait()
+    copies[count + 2].wait()
     answer = jnp.dot(hidden, down_v[...], preferred_element_type=jnp.float32).astype(
         jnp.bfloat16
     )
+    if has_extra:
+        copies[count + 3].wait()
     for c in range(count):
-        wanted = lax.broadcasted_iota(jnp.int32, (size, entries), 1)
-        put = jnp.where(place_col[c] == wanted, 1.0, 0.0).astype(jnp.bfloat16)
-        placed = row_gate[c] * jnp.dot(
-            put,
-            answer[c * entries : (c + 1) * entries, :],
+        scaled = answer[c * entries : (c + 1) * entries, :].astype(jnp.float32) * weights[c]
+        placed = lax.dot_general(
+            picks[c],
+            scaled.astype(jnp.bfloat16),
+            (((0,), (0,)), ((), ())),
             preferred_element_type=jnp.float32,
         )
-        if c == 0 and extra.shape[0] == size:
-            placed = placed + extra[...].astype(jnp.float32)
+        if c == 0 and has_extra:
+            placed = placed + extra_v[...].astype(jnp.float32)
         outs[c][...] = placed.astype(jnp.bfloat16)
 
 
@@ -274,19 +341,22 @@
     hidden = gate_w.shape[2]
     any_spec = pl.BlockSpec(memory_space=pl.ANY)
     vmem = pl.BlockSpec(memory_space=pltpu.VMEM)
-    if extra is None:
-        extra = jnp.zeros((8, 128), jnp.bfloat16)
+    has_extra = extra is not None
+    if not has_extra:
+        extra = jnp.zeros((16, 128), jnp.bfloat16)
     return pl.pallas_call(
-        functools.partial(routed_kernel, count, entries),
+        functools.partial(routed_kernel, count, entries, has_extra),
         out_shape=[jax.ShapeDtypeStruct((size, width), jnp.bfloat16)] * count,
-        in_specs=[vmem] * (count + 4) + [any_spec] * 3,
+        in_specs=[any_spec] * count + [vmem] * 2 + [any_spec] * 4,
         out_specs=[vmem] * count,
         scratch_shapes=[
+            pltpu.VMEM((count, size, width), jnp.bfloat16),
             pltpu.VMEM((count * entries, width), jnp.bfloat16),
             pltpu.VMEM((width, hidden), jnp.bfloat16),
             pltpu.VMEM((width, hidden), jnp.bfloat16),
             pltpu.VMEM((hidden, width), jnp.bfloat16),
-            pltpu.SemaphoreType.DMA((3,)),
+            pltpu.VMEM(extra.shape, jnp.bfloat16),
+            pltpu.SemaphoreType.DMA((count + 4,)),
         ],
         compiler_params=pltpu.CompilerParams(vmem_limit_bytes=56 * 1024 * 1024),
         cost_estimate=pl.CostEstimate(
@@ -294,16 +364,7 @@
             bytes_accessed=6 * gate_w.size + 4 * count * size * width,
             transcendentals=count * entries * hidden,
         ),
-    )(
-        *chunks,
-        place.reshape(count, 1, size),
-        place.reshape(count, size, 1),
-        row_gate.reshape(count, size, 1),
-        extra,
-        gate_w,
-        up_w,
-        down_w,
-    )
+    )(*chunks, place, row_gate, extra, gate_w, up_w, down_w)
 
 
 def rms_normed(stream, norm_gain):
@@ -389,22 +450,18 @@
     columns = width // exp_count
     keys = cache_key.reshape(tokens, width)
     values = cache_value.reshape(tokens, width)
-    far_queries = send(queries, 1, 0, 0)
     members = [(dl, dx) for dl in range(2) for dx in range(nx)]
-    orders = [
-        jnp.stack(
-            [((ih + j) % 2 * 2 + (il + dl) % 2) * nx + (ix + dx) % nx for j in range(2)]
-        ).astype(i32)
-        for dl, dx in members
-    ]
-    blocks = {}
-    for m in reversed(range(len(members))):
-        blocks[m] = send(pack([keys, values, queries], orders[m], columns), 0, *members[m])
-    far = [
-        send(pack([far_queries], orders[m], columns), 0, *members[m])
-        for m in range(len(members))
-    ]
-    blocks = [blocks[m] for m in range(len(members))]
+    order = jnp.stack(
+        [
+            ((ih + j) % 2 * 2 + (il + dl) % 2) * nx + (ix + dx) % nx
+            for dl, dx in members
+            for j in range(2)
+        ]
+    ).astype(i32)
+    gates = jnp.pad(jnp.transpose(route_gate), ((0, 0), (0, 2 * columns - tok_rows)))
+    blocks, far = pack(keys, values, queries, gates, order, columns)
+    blocks = [send(blocks[m], 0, *members[m]) for m in range(len(members))]
+    far = [send(far[m], 1, *members[m]) for m in range(len(members))]
     page_ids = (
         rel_exp[: len(members), None] * pages_here + jnp.arange(pages_here, dtype=i32)[None, :]
     ).reshape(-1)
@@ -420,6 +477,7 @@
         page_request,
         page_slot,
         page_len,
+        tokens,
     )
     other = send(partial[columns:], 1, 0, 0)
     other_level = send(level[columns // HEAD_DIM :], 1, 0, 0)
@@ -430,13 +488,14 @@
     twins = slot_expert == own_expert
     copies = jnp.sum(twins.astype(i32))
     own_rank = jnp.sum((twins & (slot_ids < own_slot)).astype(i32))
-    gates = jnp.transpose(route_gate)
-    gates = jnp.stack([send_req(gates, 0, dc) for dc in range(nc)])
+    gates = [block[2 * tokens + tok_rows :, :tok_rows].astype(f32) for block in blocks]
+    gates = jnp.stack([g[:TOPK] + g[TOPK : 2 * TOPK] + g[2 * TOPK : 3 * TOPK] for g in gates])
+    gates = gates.reshape(2, nx, TOPK, tok_rows)
+    gates = jnp.stack([send(gates, dh, 0, 0) for dh in range(2)])
     gates = jnp.stack([send_req(gates, dy, 0) for dy in range(ny)])
-    gates = jnp.stack([send(gates, 0, 0, dx) for dx in range(nx)], axis=2)
-    gates = jnp.stack([send(gates, 0, dl, 0) for dl in range(2)], axis=2)
-    gates = jnp.stack([send(gates, dh, 0, 0) for dh in range(2)], axis=2)
-    gates = gates.reshape(slot_count, TOPK, tok_rows)
+    gates = jnp.stack([send_req(gates, 0, dc) for dc in range(nc)], axis=1)
+    gates = jnp.transpose(gates, (0, 1, 4, 2, 3, 5, 6)).reshape(slot_count, TOPK, tok_rows)
+    rel_exp = jnp.transpose(rel_exp.reshape(len(zs), nx)).reshape(-1)
     rel_slots = (rel_req[:, None] * exp_count + rel_exp[None, :]).reshape(-1)
     named = (route_expert == own_expert).reshape(slot_count, tok_rows, TOPK)[rel_slots]
     named = jnp.transpose(named, (0, 2, 1))
@@ -446,50 +505,57 @@
     mine = jnp.any(named, axis=1) & (rel_slots % copies == own_rank)[:, None]
     mine = mine.reshape(ny, nc, chunk_rows)
     place = jnp.where(mine, jnp.cumsum(mine.astype(i32), axis=2) - 1, -1)
-    other, place, row_gate = lax.optimization_barrier((other, place, row_gate))
-
-    mixed = project(partial, level, other, other_level, out_proj)
-    mixed = mixed.reshape(len(zs), nx, tok_rows, width)
+    place = place.reshape(ny, nc, 1, chunk_rows)
+    row_gate = row_gate.reshape(ny, nc, 1, chunk_rows)
+
     total = resid.astype(f32)
+    stays, goes = {}, {}
     for i in reversed(range(len(zs))):
-        line = mixed[i, 0].astype(f32)
-        for dx in range(1, nx):
-            line = line + send(mixed[i, dx], 0, 0, -dx).astype(f32)
-        total = total + (send(line.astype(bf16), *zs[i], 0).astype(f32) if i else line)
+        stays[i], go = project(i, partial, level, other, other_level, out_proj, tok_rows)
+        goes[i] = [
+            send(go[(dx - 1) * tok_rows : dx * tok_rows], 0, 0, -dx) for dx in range(1, nx)
+        ]
+    for i in reversed(range(len(zs))):
+        if i:
+            line = add_up([stays[i]] + goes[i], bf16)
+            total = total + send(line, *zs[i], 0).astype(f32)
+        else:
+            total = total + stays[i]
+            for come in goes[i]:
+                total = total + come.astype(f32)
     stream = total
     normed = rms_normed(stream, norm_gain)
-
+    normed, place, row_gate = lax.optimization_barrier((normed, place, row_gate))
+
+    line = [send(normed, *zs[i], 0) for i in range(len(zs))]
     piece = {}
-    for i in reversed(range(len(zs))):
-        piece[i, 0, 0] = send(normed, *zs[i], 0)
-    x_first = [dh == 0 for dh, dl in zs]
     for i in range(len(zs)):
+        piece[i, 0, 0] = line[i]
+        new = {}
+        for dy in range(1, ny):
+            new[i, 0, dy] = send_req(line[i], dy, 0)
         for dx in range(1, nx):
-            piece[i, dx, 0] = send(piece[i, 0, 0], 0, 0, dx)
-        if x_first[i]:
-            for dx in range(nx):
+            new[i, dx, 0] = send(line[i], 0, 0, dx)
+            if i:
                 for dy in range(1, ny):
-                    piece[i, dx, dy] = send_req(piece[i, dx, 0], dy, 0)
-        else:
-            for dy in range(1, ny):
-                piece[i, 0, dy] = send_req(piece[i, 0, 0], dy, 0)
-                for dx in range(1, nx):
-                    piece[i, dx, dy] = send(piece[i, 0, dy], 0, 0, dx)
-    chunks = {}
-    for dy in range(ny):
-        chunks[dy, 0] = join([piece[i, dx, dy] for i in range(len(zs)) for dx in range(nx)])
-        for dc in range(1, nc):
-            chunks[dy, dc] = send_req(chunks[dy, 0], 0, dc)
-
-    sums = {}
-    for dy in range(ny):
-        extra = None
-        if dy == 0:
-            extra = shared_expert(
-                chunks[0, 0], shared_scalar, shared_gate.T, shared_up.T, shared_down
-            )
+                    new[i - 1, dx, dy] = send(piece[i - 1, 0, dy], 0, 0, dx)
+        names = list(new)
+        tied = lax.optimization_barrier([new[name] for name in names] + line[i + 1 : i + 2])
+        if i + 1 < len(zs):
+            line[i + 1] = tied[-1]
+        for name, value in zip(names, tied):
+            piece[name] = value
+    last = len(zs) - 1
+    for dy in range(1, ny):
+        for dx in range(1, nx):
+            piece[last, dx, dy] = send(piece[last, 0, dy], 0, 0, dx)
+
+    def chunk_of(dy):
+        return join([piece[i, dx, dy] for dx in range(nx) for i in range(len(zs))])
+
+    def answers_of(dy, chunk, partners, extra):
         answers = routed_expert(
-            [chunks[dy, dc] for dc in range(nc)],
+            [chunk] + partners,
             place[dy],
             row_gate[dy],
             extra,
@@ -501,30 +567,44 @@
         here = answers[0].astype(f32)
         for dc in range(1, nc):
             here = here + send_req(answers[dc], 0, -dc).astype(f32)
-        here = here.astype(bf16).reshape(len(zs), nx, tok_rows, width)
-        for i in range(len(zs)):
-            for dx in range(nx):
-                sums[i, dx, dy] = here[i, dx]
+        return here.astype(bf16).reshape(nx, len(zs), tok_rows, width)
+
+    partners_of = lambda chunk: [send_req(chunk, 0, dc) for dc in range(1, nc)]
+    chunk = chunk_of(0)
+    partners = partners_of(chunk)
+    extra = shared_expert(chunk, shared_scalar, shared_gate.T, shared_up.T, shared_down)
+    sums, later = {}, {}
+    for dy in range(ny):
+        if dy + 1 < ny:
+            names = [(i, dx, dy + 1) for dx in range(nx) for i in range(len(zs))]
+            tied = lax.optimization_barrier(
+                [extra] + partners + [piece[name] for name in names]
+            ) if extra is not None else None
+            if tied is not None:
+                extra, partners = tied[0], list(tied[1 : 1 + len(partners)])
+                for name, value in zip(names, tied[1 + len(partners) :]):
+                    piece[name] = value
+            following = chunk_of(dy + 1)
+            following_partners = partners_of(following)
+        here = answers_of(dy, chunk, partners, extra)
+        half = len(zs) // 2
+        for low in (half, 0):
+            group = here[0, low : low + half].astype(f32)
+            for dx in range(1, nx):
+                group = group + send(here[dx, low : low + half], 0, 0, -dx).astype(f32)
+            for i in range(half):
+                sums[low + i, dy] = group[i]
+        if dy + 1 < ny:
+            chunk, partners, extra = following, following_partners, None
+
     total = stream
     for i in reversed(range(len(zs))):
-        line = {}
-        if x_first[i]:
-            for dx in range(nx):
-                line[dx] = sums[i, dx, 0].astype(f32)
-                for dy in range(1, ny):
-                    line[dx] = line[dx] + send_req(sums[i, dx, dy], -dy, 0).astype(f32)
-            out = line[0]
-            for dx in range(1, nx):
-                out = out + send(line[dx].astype(bf16), 0, 0, -dx).astype(f32)
+        parts = [sums[i, 0]] + [send_req(sums[i, dy].astype(bf16), -dy, 0) for dy in range(1, ny)]
+        if i:
+            total = total + send(add_up(parts, bf16), *zs[i], 0).astype(f32)
         else:
-            for dy in range(ny):
-                line[dy] = sums[i, 0, dy].astype(f32)
-                for dx in range(1, nx):
-                    line[dy] = line[dy] + send(sums[i, dx, dy], 0, 0, -dx).astype(f32)
-            out = line[0]
-            for dy in range(1, ny):
-                out = out + send_req(line[dy].astype(bf16), -dy, 0).astype(f32)
-        total = total + (send(out.astype(bf16), *zs[i], 0).astype(f32) if i else out)
+            for part in parts:
+                total = total + part.astype(f32)
     return total.astype(bf16)
 
 

time: 308 us -> 309 us (level)
  starting transfers between devices: 73.6 us -> 58 us
  waiting for transfers between devices: 122 us -> 137 us
  local copies, waits for them, and re-layouts: 17.8 us -> 23 us
    ppermute x37 -> x35, waiting for transfers between devices: 84.6 us -> 119 us  [send(): return lax.ppermute(value, 'exp', pairs)]
    ppermute x18 -> x14, waiting for transfers between devices: 37.3 us -> 17.8 us  [send_req(): return lax.ppermute(value, 'req', pairs)]
    ppermute x18 -> x14, starting transfers between devices: 18.7 us -> 8.9 us  [send_req(): return lax.ppermute(value, 'req', pairs)]
    unnamed x74 -> x82, local copies, waits for them, and re-layouts: 7.44 us -> 14.6 us
    ppermute x37 -> x35, starting transfers between devices: 55 us -> 49.1 us  [send(): return lax.ppermute(value, 'exp', pairs)]
    another operation x7 -> x3, local copies, waits for them, and re-layouts: 4.76 us -> 0.17 us  [the longest x1 0.08 us: shards(): jnp.stack([((ih + j) % 2 * 2 + (il + dl) % 2) * nx + (ix + dx) % nx for d...]
    pallas_call x11 -> x13, Pallas kernels: 55.4 us -> 54.7 us  [the longest x2 30.7 us: routed_expert(): pl.pallas_call(functools.partial(routed_kernel, count, entries, has_extra...]
  transfers between devices with their start and end apart: 55 -> 49, of which waited for: 27 -> 29; matrix products, arithmetic and copies ran while one was open for 6% -> 5% of each run, Pallas kernels for 23% -> 20%
where the time goes in v4:
time: 309 us; the launch traced here: 307 us
  waiting for transfers between devices  137 us (44%)
  Pallas kernels  77.2 us (25%)
  starting transfers between devices  58 us (19%)
  local copies, waits for them, and re-layouts  23 us (7%)
  other arithmetic  9.86 us (3%)
    ppermute x35, waiting for transfers between devices, send(): return lax.ppermute(value, 'exp', pairs)  119 us
    ppermute x35, starting transfers between devices, send(): return lax.ppermute(value, 'exp', pairs)  49.1 us
    pallas_call x2, Pallas kernels, routed_expert(): pl.pallas_call(functools.partial(routed_kernel, count, entries, has_extra...  30.7 us
    ppermute x14, waiting for transfers between devices, send_req(): return lax.ppermute(value, 'req', pairs)  17.8 us
    unnamed x82, local copies, waits for them, and re-layouts  14.6 us
    pallas_call x6, Pallas kernels, add_up(): pl.pallas_call(add_kernel, out_shape=jax.ShapeDtypeStruct(parts[0].shape,...  11.1 us
    pallas_call x4, Pallas kernels, project(): pl.pallas_call(project_kernel, out_shape=[jax.ShapeDtypeStruct((tok_rows,...  10.3 us
    ppermute x14, starting transfers between devices, send_req(): return lax.ppermute(value, 'req', pairs)  8.9 us
  transfers between devices with their start and end apart: 49, of which 29 were waited for; matrix products, arithmetic and copies ran while one was open for 5% of the time, Pallas kernels for 20%

profile of v4, /device:TPU:0, one launch (start us, length us, event | category | flops | bytes accessed | tf_op | source)
XLA Modules:
  0.0 306.6 jit_solution(18183166779906794002)
XLA Ops:
  4.2 2.6 shard_map.181
  6.8 2.9 collective-permute-start
  11.3 3.0 collective-permute-start.3
  24.9 14.3 %collective-permute-done.3.refs_4_ = bf16[64,512]{1,0:T(8,128)(2,1)S(1)} collective-permute-done((bf16[64,512]{1,0:T(8,128)(2,1)S(1)}, bf16[64,512]{1,0:T(8,128)(2,1)S(1)}, u32[]{:S(2)}, u32[]{:S(2)}) %collective-permute-start.3) | collective-permute-done | bytes 65568 | tf_op jit(solution)/shard_map/ppermute | solution.py:427
  39.3 3.0 collective-permute-start.5
  45.4 3.9 %collective-permute-done.6.refs_7_ = bf16[64,512]{1,0:T(8,128)(2,1)S(1)} collective-permute-done((bf16[64,512]{1,0:T(8,128)(2,1)S(1)}, bf16[64,512]{1,0:T(8,128)(2,1)S(1)}, u32[]{:S(2)}, u32[]{:S(2)}) %collective-permute-start.6) | collective-permute-done | bytes 65568 | tf_op jit(solution)/shard_map/ppermute | solution.py:427
  49.3 7.8 %shard_map.182 = (bf16[512,512]{1,0:T(8,128)(2,1)S(1)}, f32[4,1,512]{2,1,0:T(1,128)S(1)}) custom-call(s32[8]{0:T(128)S(1)} %get-tuple-element.104.page_req, s32[8]{0:T(128)S(1)} %get-tuple-element.103.page_slot, bf16[592,512]{1,0:T(8,128)(2,1)S(1)} %get-tuple-element.54.refs_0_, bf16[592,512]{1,0:T(8,128)(2,1)S(1)} %collective-permute-done.refs_1_, ...), custom_call_target="tpu_custom_call" | custom-call | flops 1073741824 | bytes 2686976 | tf_op jit(solution)/shard_map/pallas_call | solution.py:122
  61.6 7.4 %collective-permute-done.16 = f32[2,2,4,64]{3,0,1,2:T(2,128)S(1)} collective-permute-done((f32[2,2,4,64]{3,0,1,2:T(2,128)S(1)}, f32[2,2,4,64]{3,0,1,2:T(2,128)S(1)}, u32[]{:S(2)}, u32[]{:S(2)}) %collective-permute-start.16) | collective-permute-done | bytes 4128 | tf_op jit(solution)/shard_map/ppermute | solution.py:427
  72.0 2.6 shard_map.187
  74.6 2.6 shard_map.185
  82.0 2.6 shard_map.189
  99.7 14.1 %collective-permute-done.12 = bf16[64,2048]{1,0:T(8,128)(2,1)S(1)} collective-permute-done((bf16[64,2048]{1,0:T(8,128)(2,1)}, bf16[64,2048]{1,0:T(8,128)(2,1)S(1)}, u32[]{:S(2)}, u32[]{:S(2)}) %collective-permute-start.12) | collective-permute-done | bytes 262176 | tf_op jit(solution)/shard_map/ppermute | solution.py:427
  114.8 5.3 %collective-permute-start.21 = (bf16[64,2048]{1,0:T(8,128)(2,1)S(1)}, bf16[64,2048]{1,0:T(8,128)(2,1)S(1)}, u32[]{:S(2)}, u32[]{:S(2)}) collective-permute-start(bf16[64,2048]{1,0:T(8,128)(2,1)S(1)} %multiply_convert_fusion.refs_0_), channel_id=1, source_target_pairs={{0,2},{1,3},{2,0},{3,1},{4,6},{5,7},{6,4},{7,5},{8,10},{9,11},{10,... | collective-permute-start | bytes 786440 | tf_op jit(solution)/shard_map/ppermute | solution.py:427
  121.2 8.7 %collective-permute-done.21.refs_1_ = bf16[64,2048]{1,0:T(8,128)(2,1)S(1)} collective-permute-done((bf16[64,2048]{1,0:T(8,128)(2,1)S(1)}, bf16[64,2048]{1,0:T(8,128)(2,1)S(1)}, u32[]{:S(2)}, u32[]{:S(2)}) %collective-permute-start.21) | collective-permute-done | bytes 262176 | tf_op jit(solution)/shard_map/ppermute | solution.py:427
  133.5 2.6 collective-permute-start.29
  139.6 3.7 %collective-permute-done.24.refs_4_ = bf16[64,2048]{1,0:T(8,128)(2,1)S(1)} collective-permute-done((bf16[64,2048]{1,0:T(8,128)(2,1)S(1)}, bf16[64,2048]{1,0:T(8,128)(2,1)S(1)}, u32[]{:S(2)}, u32[]{:S(2)}) %collective-permute-start.24) | collective-permute-done | bytes 262176 | tf_op jit(solution)/shard_map/ppermute | solution.py:427
  145.3 4.3 %collective-permute-done.26.refs_2_ = bf16[64,2048]{1,0:T(8,128)(2,1)S(1)} collective-permute-done((bf16[64,2048]{1,0:T(8,128)(2,1)S(1)}, bf16[64,2048]{1,0:T(8,128)(2,1)S(1)}, u32[]{:S(2)}, u32[]{:S(2)}) %collective-permute-start.26) | collective-permute-done | bytes 262176 | tf_op jit(solution)/shard_map/ppermute | solution.py:437
  151.5 3.9 %collective-permute-done.28.refs_5_ = bf16[64,2048]{1,0:T(8,128)(2,1)S(1)} collective-permute-done((bf16[64,2048]{1,0:T(8,128)(2,1)S(1)}, bf16[64,2048]{1,0:T(8,128)(2,1)S(1)}, u32[]{:S(2)}, u32[]{:S(2)}) %collective-permute-start.28) | collective-permute-done | bytes 262176 | tf_op jit(solution)/shard_map/ppermute | solution.py:427
  157.6 4.2 %collective-permute-done.30.refs_3_ = bf16[64,2048]{1,0:T(8,128)(2,1)S(1)} collective-permute-done((bf16[64,2048]{1,0:T(8,128)(2,1)S(1)}, bf16[64,2048]{1,0:T(8,128)(2,1)S(1)}, u32[]{:S(2)}, u32[]{:S(2)}) %collective-permute-start.30) | collective-permute-done | bytes 262176 | tf_op jit(solution)/shard_map/ppermute | solution.py:437
  165.0 3.0 shard_map.190.rows.refs_0_
  171.6 8.7 %shard_map.191.refs_4_ = bf16[512,2048]{1,0:T(8,128)(2,1)S(1)} custom-call(bf16[512,2048]{1,0:T(8,128)(2,1)S(1)} %copy-done.4, bf16[1,2048]{1,0:T(2,128)(2,1)S(1)} %reshape.550.scalar, bf16[704,2048]{1,0:T(8,128)(2,1)} %bitcast.151, bf16[704,2048]{1,0:T(8,128)(2,1)} %bitcast.152, bf16[704,2048]{1,0:T(8,128)(2,1)} %down_w.1), custom_call_target="tpu_custom_call" | custom-call | flops 4429185024 | bytes 12845056 | tf_op jit(solution)/shard_map/pallas_call | solution.py:269
  182.4 3.0 shard_map.193.refs_0_
  186.9 15.5 %shard_map.192 = (bf16[512,2048]{1,0:T(8,128)(2,1)}, bf16[512,2048]{1,0:T(8,128)(2,1)}) custom-call(bf16[512,2048]{1,0:T(8,128)(2,1)} %shard_map.190.rows.refs_0_, bf16[512,2048]{1,0:T(8,128)(2,1)} %collective-permute-done.33.refs_1_, s32[2,1,512]{2,1,0:T(1,128)} %get-tuple-element.130.refs_2_, f32[2,1,512]{2,1,0:T(1,128)} %get-tuple-element.128.refs_3_, ...), custom_call_target="tpu_custom_call" | custom-call | flops 8254390272 | bytes 25690112 | tf_op jit(solution)/shard_map/pallas_call | solution.py:347
  204.2 15.2 %shard_map.194 = (bf16[512,2048]{1,0:T(8,128)(2,1)}, bf16[512,2048]{1,0:T(8,128)(2,1)}) custom-call(bf16[512,2048]{1,0:T(8,128)(2,1)} %shard_map.193.refs_0_, bf16[512,2048]{1,0:T(8,128)(2,1)} %copy-done.40, s32[2,1,512]{2,1,0:T(1,128)} %get-tuple-element.129.refs_2_, f32[2,1,512]{2,1,0:T(1,128)} %get-tuple-element.127.refs_3_, ...), custom_call_target="tpu_custom_call" | custom-call | flops 8254390272 | bytes 25690112 | tf_op jit(solution)/shard_map/pallas_call | solution.py:347
  226.9 8.7 %collective-permute-done.36 = bf16[2,64,2048]{2,1,0:T(8,128)(2,1)S(1)} collective-permute-done((bf16[2,64,2048]{2,1,0:T(8,128)(2,1)S(1)}, bf16[2,64,2048]{2,1,0:T(8,128)(2,1)S(1)}, u32[]{:S(2)}, u32[]{:S(2)}) %collective-permute-start.36) | collective-permute-done | bytes 524320 | tf_op jit(solution)/shard_map/ppermute | solution.py:427
  235.6 11.2 %collective-permute-done.44 = bf16[2,64,2048]{2,1,0:T(8,128)(2,1)S(1)} collective-permute-done((bf16[2,64,2048]{2,1,0:T(8,128)(2,1)S(1)}, bf16[2,64,2048]{2,1,0:T(8,128)(2,1)S(1)}, u32[]{:S(2)}, u32[]{:S(2)}) %collective-permute-start.44) | collective-permute-done | bytes 524320 | tf_op jit(solution)/shard_map/ppermute | solution.py:427
  248.3 9.8 %collective-permute-done.39 = bf16[2,64,2048]{2,1,0:T(8,128)(2,1)S(1)} collective-permute-done((bf16[2,64,2048]{2,1,0:T(8,128)(2,1)S(1)}, bf16[2,64,2048]{2,1,0:T(8,128)(2,1)S(1)}, u32[]{:S(2)}, u32[]{:S(2)}) %collective-permute-start.39) | collective-permute-done | bytes 524320 | tf_op jit(solution)/shard_map/ppermute | solution.py:427
  258.1 10.6 %collective-permute-done.45 = bf16[2,64,2048]{2,1,0:T(8,128)(2,1)S(1)} collective-permute-done((bf16[2,64,2048]{2,1,0:T(8,128)(2,1)S(1)}, bf16[2,64,2048]{2,1,0:T(8,128)(2,1)S(1)}, u32[]{:S(2)}, u32[]{:S(2)}) %collective-permute-start.45) | collective-permute-done | bytes 524320 | tf_op jit(solution)/shard_map/ppermute | solution.py:427
  274.2 4.3 %collective-permute-done.46.refs_1_ = bf16[64,2048]{1,0:T(8,128)(2,1)} collective-permute-done((bf16[64,2048]{1,0:T(8,128)(2,1)S(1)}, bf16[64,2048]{1,0:T(8,128)(2,1)}, u32[]{:S(2)}, u32[]{:S(2)}) %collective-permute-start.46) | collective-permute-done | bytes 262176 | tf_op jit(solution)/shard_map/ppermute | solution.py:437
  281.0 3.1 %collective-permute-done.42.refs_1_ = bf16[64,2048]{1,0:T(8,128)(2,1)S(1)} collective-permute-done((bf16[64,2048]{1,0:T(8,128)(2,1)S(1)}, bf16[64,2048]{1,0:T(8,128)(2,1)S(1)}, u32[]{:S(2)}, u32[]{:S(2)}) %collective-permute-start.42) | collective-permute-done | bytes 262176 | tf_op jit(solution)/shard_map/ppermute | solution.py:437
  292.3 2.9 collective-permute-start.41
  295.2 10.5 %collective-permute-done.43 = bf16[64,2048]{1,0:T(8,128)(2,1)S(1)} collective-permute-done((bf16[64,2048]{1,0:T(8,128)(2,1)}, bf16[64,2048]{1,0:T(8,128)(2,1)S(1)}, u32[]{:S(2)}, u32[]{:S(2)}) %collective-permute-start.43) | collective-permute-done | bytes 262176 | tf_op jit(solution)/shard_map/ppermute | solution.py:427
  (245 shorter events, 98.6 us)
Async XLA Ops:
  6.8 42.6 %collective-permute-start = (bf16[592,512]{1,0:T(8,128)(2,1)}, bf16[592,512]{1,0:T(8,128)(2,1)S(1)}, u32[]{:S(2)}, u32[]{:S(2)}) collective-permute-start(bf16[592,512]{1,0:T(8,128)(2,1)} %get-tuple-element.55), channel_id=1, source_target_pairs={{0,1},{1,0},{2,3},{3,2},{4,5},{5,4},{6,7},{7,6},{8,9},{9,8},{10,11... | collective-permute-start | bytes 1818632 | tf_op jit(solution)/shard_map/ppermute | solution.py:427
  9.7 39.6 %collective-permute-start.1 = (bf16[592,512]{1,0:T(8,128)(2,1)}, bf16[592,512]{1,0:T(8,128)(2,1)S(1)}, u32[]{:S(2)}, u32[]{:S(2)}) collective-permute-start(bf16[592,512]{1,0:T(8,128)(2,1)} %get-tuple-element.56), channel_id=1, source_target_pairs={{0,2},{1,3},{2,0},{3,1},{4,6},{5,7},{6,4},{7,5},{8,10},{9,11},{10,... | collective-permute-start | bytes 1818632 | tf_op jit(solution)/shard_map/ppermute | solution.py:427
  11.3 38.0 %collective-permute-start.2 = (bf16[592,512]{1,0:T(8,128)(2,1)}, bf16[592,512]{1,0:T(8,128)(2,1)S(1)}, u32[]{:S(2)}, u32[]{:S(2)}) collective-permute-start(bf16[592,512]{1,0:T(8,128)(2,1)} %get-tuple-element.57), channel_id=1, source_target_pairs={{0,3},{1,2},{2,1},{3,0},{4,7},{5,6},{6,5},{7,4},{8,11},{9,10},{10,... | collective-permute-start | bytes 1818632 | tf_op jit(solution)/shard_map/ppermute | solution.py:427
  11.3 28.0 %collective-permute-start.3 = (bf16[64,512]{1,0:T(8,128)(2,1)S(1)}, bf16[64,512]{1,0:T(8,128)(2,1)S(1)}, u32[]{:S(2)}, u32[]{:S(2)}) collective-permute-start(bf16[64,512]{1,0:T(8,128)(2,1)S(1)} %get-tuple-element.58), channel_id=1, source_target_pairs={{0,4},{1,5},{2,6},{3,7},{4,0},{5,1},{6,2},{7,3},{8,12},{9,13},{10,... | collective-permute-start | bytes 196616 | tf_op jit(solution)/shard_map/ppermute | solution.py:427
  14.3 28.0 %collective-permute-start.4 = (bf16[64,512]{1,0:T(8,128)(2,1)S(1)}, bf16[64,512]{1,0:T(8,128)(2,1)S(1)}, u32[]{:S(2)}, u32[]{:S(2)}) collective-permute-start(bf16[64,512]{1,0:T(8,128)(2,1)S(1)} %get-tuple-element.59), channel_id=1, source_target_pairs={{0,5},{1,4},{2,7},{3,6},{4,1},{5,0},{6,3},{7,2},{8,13},{9,12},{10,... | collective-permute-start | bytes 196616 | tf_op jit(solution)/shard_map/ppermute | solution.py:427
  57.2 13.5 %collective-permute-start.7 = (bf16[256,512]{1,0:T(8,128)(2,1)S(1)}, bf16[256,512]{1,0:T(8,128)(2,1)S(1)}, u32[]{:S(2)}, u32[]{:S(2)}) collective-permute-start(bf16[256,512]{1,0:T(8,128)(2,1)S(1)} %slice.126), channel_id=1, source_target_pairs={{0,4},{1,5},{2,6},{3,7},{4,0},{5,1},{6,2},{7,3},{8,12},{9,13},{10,... | collective-permute-start | bytes 786440 | tf_op jit(solution)/shard_map/ppermute | solution.py:427
  57.9 11.1 %collective-permute-start.16 = (f32[2,2,4,64]{3,0,1,2:T(2,128)S(1)}, f32[2,2,4,64]{3,0,1,2:T(2,128)S(1)}, u32[]{:S(2)}, u32[]{:S(2)}) collective-permute-start(f32[2,2,4,64]{3,0,1,2:T(2,128)S(1)} %copy.36), channel_id=1, source_target_pairs={{0,4},{1,5},{2,6},{3,7},{4,0},{5,1},{6,2},{7,3},{8,12},{9,13},{10,... | collective-permute-start | bytes 12296 | tf_op jit(solution)/shard_map/ppermute | solution.py:427
  69.1 12.8 %collective-permute-start.17 = (f32[2,2,2,4,64]{4,1,0,2,3:T(2,128)S(1)}, f32[2,2,2,4,64]{4,1,0,2,3:T(2,128)S(1)}, u32[]{:S(2)}, u32[]{:S(2)}) collective-permute-start(f32[2,2,2,4,64]{4,1,0,2,3:T(2,128)S(1)} %get-tuple-element.126), channel_id=1, source_target_pairs={{0,16},{8,24},{16,0},{24,8},{1,17},{9,25},{17,1},{25,9},{2,18},{10... | collective-permute-start | bytes 24584 | tf_op jit(solution)/shard_map/ppermute | solution.py:437
  74.6 12.1 %collective-permute-start.13 = (bf16[64,2048]{1,0:T(8,128)(2,1)}, bf16[64,2048]{1,0:T(8,128)(2,1)S(1)}, u32[]{:S(2)}, u32[]{:S(2)}) collective-permute-start(bf16[64,2048]{1,0:T(8,128)(2,1)} %get-tuple-element.69), channel_id=1, source_target_pairs={{0,1},{1,0},{2,3},{3,2},{4,5},{5,4},{6,7},{7,6},{8,9},{9,8},{10,11... | collective-permute-start | bytes 786440 | tf_op jit(solution)/shard_map/ppermute | solution.py:427
  77.1 12.5 %collective-permute-start.11 = (bf16[64,2048]{1,0:T(8,128)(2,1)}, bf16[64,2048]{1,0:T(8,128)(2,1)S(1)}, u32[]{:S(2)}, u32[]{:S(2)}) collective-permute-start(bf16[64,2048]{1,0:T(8,128)(2,1)} %get-tuple-element.67), channel_id=1, source_target_pairs={{0,1},{1,0},{2,3},{3,2},{4,5},{5,4},{6,7},{7,6},{8,9},{9,8},{10,11... | collective-permute-start | bytes 786440 | tf_op jit(solution)/shard_map/ppermute | solution.py:427
  81.7 13.6 %collective-permute-start.9 = (bf16[64,2048]{1,0:T(8,128)(2,1)}, bf16[64,2048]{1,0:T(8,128)(2,1)S(1)}, u32[]{:S(2)}, u32[]{:S(2)}) collective-permute-start(bf16[64,2048]{1,0:T(8,128)(2,1)} %get-tuple-element.65), channel_id=1, source_target_pairs={{0,1},{1,0},{2,3},{3,2},{4,5},{5,4},{6,7},{7,6},{8,9},{9,8},{10,11... | collective-permute-start | bytes 786440 | tf_op jit(solution)/shard_map/ppermute | solution.py:427
  82.0 16.8 %collective-permute-start.18 = (f32[2,2,2,2,4,64]{5,2,1,3,0,4:T(2,128)S(1)}, f32[2,2,2,2,4,64]{5,2,1,3,0,4:T(2,128)S(1)}, u32[]{:S(2)}, u32[]{:S(2)}) collective-permute-start(f32[2,2,2,2,4,64]{5,2,1,3,0,4:T(2,128)S(1)} %get-tuple-element.124), channel_id=1, source_target_pairs={{0,8},{8,0},{16,24},{24,16},{1,9},{9,1},{17,25},{25,17},{2,10},{10... | collective-permute-start | bytes 49160 | tf_op jit(solution)/shard_map/ppermute | solution.py:437
  84.6 14.4 %collective-permute-start.15 = (bf16[64,2048]{1,0:T(8,128)(2,1)}, bf16[64,2048]{1,0:T(8,128)(2,1)S(1)}, u32[]{:S(2)}, u32[]{:S(2)}) collective-permute-start(bf16[64,2048]{1,0:T(8,128)(2,1)} %get-tuple-element.71), channel_id=1, source_target_pairs={{0,1},{1,0},{2,3},{3,2},{4,5},{5,4},{6,7},{7,6},{8,9},{9,8},{10,11... | collective-permute-start | bytes 786440 | tf_op jit(solution)/shard_map/ppermute | solution.py:427
  92.2 21.5 %collective-permute-start.12 = (bf16[64,2048]{1,0:T(8,128)(2,1)}, bf16[64,2048]{1,0:T(8,128)(2,1)S(1)}, u32[]{:S(2)}, u32[]{:S(2)}) collective-permute-start(bf16[64,2048]{1,0:T(8,128)(2,1)} %shard_map.186), channel_id=1, source_target_pairs={{0,4},{1,5},{2,6},{3,7},{4,0},{5,1},{6,2},{7,3},{8,12},{9,13},{10,... | collective-permute-start | bytes 786440 | tf_op jit(solution)/shard_map/ppermute | solution.py:427
  97.8 15.9 %collective-permute-start.10 = (bf16[64,2048]{1,0:T(8,128)(2,1)}, bf16[64,2048]{1,0:T(8,128)(2,1)S(1)}, u32[]{:S(2)}, u32[]{:S(2)}) collective-permute-start(bf16[64,2048]{1,0:T(8,128)(2,1)} %shard_map.184), channel_id=1, source_target_pairs={{0,6},{1,7},{2,4},{3,5},{4,2},{5,3},{6,0},{7,1},{8,14},{9,15},{10,... | collective-permute-start | bytes 786440 | tf_op jit(solution)/shard_map/ppermute | solution.py:427
  114.8 15.1 %collective-permute-start.21 = (bf16[64,2048]{1,0:T(8,128)(2,1)S(1)}, bf16[64,2048]{1,0:T(8,128)(2,1)S(1)}, u32[]{:S(2)}, u32[]{:S(2)}) collective-permute-start(bf16[64,2048]{1,0:T(8,128)(2,1)S(1)} %multiply_convert_fusion.refs_0_), channel_id=1, source_target_pairs={{0,2},{1,3},{2,0},{3,1},{4,6},{5,7},{6,4},{7,5},{8,10},{9,11},{10,... | collective-permute-start | bytes 786440 | tf_op jit(solution)/shard_map/ppermute | solution.py:427
  120.1 17.8 %collective-permute-start.25 = (bf16[64,2048]{1,0:T(8,128)(2,1)S(1)}, bf16[64,2048]{1,0:T(8,128)(2,1)S(1)}, u32[]{:S(2)}, u32[]{:S(2)}) collective-permute-start(bf16[64,2048]{1,0:T(8,128)(2,1)S(1)} %multiply_convert_fusion.refs_0_), channel_id=1, source_target_pairs={{0,4},{1,5},{2,6},{3,7},{4,0},{5,1},{6,2},{7,3},{8,12},{9,13},{10,... | collective-permute-start | bytes 786440 | tf_op jit(solution)/shard_map/ppermute | solution.py:427
  133.5 11.9 %collective-permute-start.29 = (bf16[64,2048]{1,0:T(8,128)(2,1)S(1)}, bf16[64,2048]{1,0:T(8,128)(2,1)S(1)}, u32[]{:S(2)}, u32[]{:S(2)}) collective-permute-start(bf16[64,2048]{1,0:T(8,128)(2,1)S(1)} %multiply_convert_fusion.refs_0_), channel_id=1, source_target_pairs={{0,6},{1,7},{2,4},{3,5},{4,2},{5,3},{6,0},{7,1},{8,14},{9,15},{10,... | collective-permute-start | bytes 786440 | tf_op jit(solution)/shard_map/ppermute | solution.py:427
  168.0 13.8 %collective-permute-start.33 = (bf16[512,2048]{1,0:T(8,128)(2,1)}, bf16[512,2048]{1,0:T(8,128)(2,1)}, u32[]{:S(2)}, u32[]{:S(2)}) collective-permute-start(bf16[512,2048]{1,0:T(8,128)(2,1)} %shard_map.190.rows.refs_0_), channel_id=1, source_target_pairs={{0,8},{8,0},{16,24},{24,16},{1,9},{9,1},{17,25},{25,17},{2,10},{10... | collective-permute-start | bytes 6291464 | tf_op jit(solution)/shard_map/ppermute | solution.py:437
  168.1 13.7 %collective-permute-start.34 = (bf16[64,2048]{1,0:T(8,128)(2,1)}, bf16[64,2048]{1,0:T(8,128)(2,1)S(1)}, u32[]{:S(2)}, u32[]{:S(2)}) collective-permute-start(bf16[64,2048]{1,0:T(8,128)(2,1)} %copy-done.23), channel_id=1, source_target_pairs={{0,1},{1,0},{2,3},{3,2},{4,5},{5,4},{6,7},{7,6},{8,9},{9,8},{10,11... | collective-permute-start | bytes 786440 | tf_op jit(solution)/shard_map/ppermute | solution.py:427
  185.4 17.3 %collective-permute-start.37 = (bf16[512,2048]{1,0:T(8,128)(2,1)}, bf16[512,2048]{1,0:T(8,128)(2,1)S(1)}, u32[]{:S(2)}, u32[]{:S(2)}) collective-permute-start(bf16[512,2048]{1,0:T(8,128)(2,1)} %shard_map.193.refs_0_), channel_id=1, source_target_pairs={{0,8},{8,0},{16,24},{24,16},{1,9},{9,1},{17,25},{25,17},{2,10},{10... | collective-permute-start | bytes 6291464 | tf_op jit(solution)/shard_map/ppermute | solution.py:437
  202.4 17.2 %collective-permute-start.35 = (bf16[512,2048]{1,0:T(8,128)(2,1)}, bf16[512,2048]{1,0:T(8,128)(2,1)S(1)}, u32[]{:S(2)}, u32[]{:S(2)}) collective-permute-start(bf16[512,2048]{1,0:T(8,128)(2,1)} %get-tuple-element.92), channel_id=1, source_target_pairs={{0,8},{8,0},{16,24},{24,16},{1,9},{9,1},{17,25},{25,17},{2,10},{10... | collective-permute-start | bytes 6291464 | tf_op jit(solution)/shard_map/ppermute | solution.py:437
  220.8 14.8 %collective-permute-start.36 = (bf16[2,64,2048]{2,1,0:T(8,128)(2,1)S(1)}, bf16[2,64,2048]{2,1,0:T(8,128)(2,1)S(1)}, u32[]{:S(2)}, u32[]{:S(2)}) collective-permute-start(bf16[2,64,2048]{2,1,0:T(8,128)(2,1)S(1)} %get-tuple-element.115), channel_id=1, source_target_pairs={{0,1},{1,0},{2,3},{3,2},{4,5},{5,4},{6,7},{7,6},{8,9},{9,8},{10,11... | collective-permute-start | bytes 1572872 | tf_op jit(solution)/shard_map/ppermute | solution.py:427
  221.1 25.7 %collective-permute-start.44 = (bf16[2,64,2048]{2,1,0:T(8,128)(2,1)S(1)}, bf16[2,64,2048]{2,1,0:T(8,128)(2,1)S(1)}, u32[]{:S(2)}, u32[]{:S(2)}) collective-permute-start(bf16[2,64,2048]{2,1,0:T(8,128)(2,1)S(1)} %get-tuple-element.116), channel_id=1, source_target_pairs={{0,1},{1,0},{2,3},{3,2},{4,5},{5,4},{6,7},{7,6},{8,9},{9,8},{10,11... | collective-permute-start | bytes 1572872 | tf_op jit(solution)/shard_map/ppermute | solution.py:427
  224.8 33.3 %collective-permute-start.39 = (bf16[2,64,2048]{2,1,0:T(8,128)(2,1)S(1)}, bf16[2,64,2048]{2,1,0:T(8,128)(2,1)S(1)}, u32[]{:S(2)}, u32[]{:S(2)}) collective-permute-start(bf16[2,64,2048]{2,1,0:T(8,128)(2,1)S(1)} %get-tuple-element.111), channel_id=1, source_target_pairs={{0,1},{1,0},{2,3},{3,2},{4,5},{5,4},{6,7},{7,6},{8,9},{9,8},{10,11... | collective-permute-start | bytes 1572872 | tf_op jit(solution)/shard_map/ppermute | solution.py:427
  225.1 43.6 %collective-permute-start.45 = (bf16[2,64,2048]{2,1,0:T(8,128)(2,1)S(1)}, bf16[2,64,2048]{2,1,0:T(8,128)(2,1)S(1)}, u32[]{:S(2)}, u32[]{:S(2)}) collective-permute-start(bf16[2,64,2048]{2,1,0:T(8,128)(2,1)S(1)} %get-tuple-element.112), channel_id=1, source_target_pairs={{0,1},{1,0},{2,3},{3,2},{4,5},{5,4},{6,7},{7,6},{8,9},{9,8},{10,11... | collective-permute-start | bytes 1572872 | tf_op jit(solution)/shard_map/ppermute | solution.py:427
  270.3 13.7 %collective-permute-start.42 = (bf16[64,2048]{1,0:T(8,128)(2,1)S(1)}, bf16[64,2048]{1,0:T(8,128)(2,1)S(1)}, u32[]{:S(2)}, u32[]{:S(2)}) collective-permute-start(bf16[64,2048]{1,0:T(8,128)(2,1)S(1)} %get-tuple-element.120), channel_id=1, source_target_pairs={{0,16},{8,24},{16,0},{24,8},{1,17},{9,25},{17,1},{25,9},{2,18},{10... | collective-permute-start | bytes 786440 | tf_op jit(solution)/shard_map/ppermute | solution.py:437
  271.3 18.3 %collective-permute-start.40 = (bf16[64,2048]{1,0:T(8,128)(2,1)S(1)}, bf16[64,2048]{1,0:T(8,128)(2,1)S(1)}, u32[]{:S(2)}, u32[]{:S(2)}) collective-permute-start(bf16[64,2048]{1,0:T(8,128)(2,1)S(1)} %get-tuple-element.119), channel_id=1, source_target_pairs={{0,16},{8,24},{16,0},{24,8},{1,17},{9,25},{17,1},{25,9},{2,18},{10... | collective-permute-start | bytes 786440 | tf_op jit(solution)/shard_map/ppermute | solution.py:437
  273.3 21.9 %collective-permute-start.48 = (bf16[64,2048]{1,0:T(8,128)(2,1)S(1)}, bf16[64,2048]{1,0:T(8,128)(2,1)S(1)}, u32[]{:S(2)}, u32[]{:S(2)}) collective-permute-start(bf16[64,2048]{1,0:T(8,128)(2,1)S(1)} %get-tuple-element.122), channel_id=1, source_target_pairs={{0,16},{8,24},{16,0},{24,8},{1,17},{9,25},{17,1},{25,9},{2,18},{10... | collective-permute-start | bytes 786440 | tf_op jit(solution)/shard_map/ppermute | solution.py:437
  280.4 14.8 %collective-permute-start.47 = (bf16[64,2048]{1,0:T(8,128)(2,1)}, bf16[64,2048]{1,0:T(8,128)(2,1)S(1)}, u32[]{:S(2)}, u32[]{:S(2)}) collective-permute-start(bf16[64,2048]{1,0:T(8,128)(2,1)} %shard_map.197), channel_id=1, source_target_pairs={{0,2},{1,3},{2,0},{3,1},{4,6},{5,7},{6,4},{7,5},{8,10},{9,11},{10,... | collective-permute-start | bytes 786440 | tf_op jit(solution)/shard_map/ppermute | solution.py:427
  286.6 19.1 %collective-permute-start.43 = (bf16[64,2048]{1,0:T(8,128)(2,1)}, bf16[64,2048]{1,0:T(8,128)(2,1)S(1)}, u32[]{:S(2)}, u32[]{:S(2)}) collective-permute-start(bf16[64,2048]{1,0:T(8,128)(2,1)} %shard_map.196), channel_id=1, source_target_pairs={{0,4},{1,5},{2,6},{3,7},{4,0},{5,1},{6,2},{7,3},{8,12},{9,13},{10,... | collective-permute-start | bytes 786440 | tf_op jit(solution)/shard_map/ppermute | solution.py:427
  292.3 13.4 %collective-permute-start.41 = (bf16[64,2048]{1,0:T(8,128)(2,1)}, bf16[64,2048]{1,0:T(8,128)(2,1)S(1)}, u32[]{:S(2)}, u32[]{:S(2)}) collective-permute-start(bf16[64,2048]{1,0:T(8,128)(2,1)} %shard_map.195), channel_id=1, source_target_pairs={{0,6},{1,7},{2,4},{3,5},{4,2},{5,3},{6,0},{7,1},{8,14},{9,15},{10,... | collective-permute-start | bytes 786440 | tf_op jit(solution)/shard_map/ppermute | solution.py:427
  (58 other events, 755.6 us)

commit v5 on v4

--- a/solution.py
+++ b/solution.py
@@ -13,7 +13,9 @@
 Z_CHIPS = 4
 
 
-def pack_kernel(members, order, keys, values, queries, gates, blocks, far):
+def pack_kernel(members, *refs):
+    keys, values, queries = (refs[i * members : (i + 1) * members] for i in range(3))
+    gates, blocks = refs[3 * members], refs[3 * members + 1 :]
     weights = gates[...]
     high = weights.astype(jnp.bfloat16).astype(jnp.float32)
     middle = (weights - high).astype(jnp.bfloat16).astype(jnp.float32)
@@ -26,48 +28,40 @@
         blocks[m][tokens : 2 * tokens, :] = values[m][...]
         blocks[m][2 * tokens : 2 * tokens + rows, :] = queries[m][...]
         blocks[m][2 * tokens + rows :, :] = weights
-        far[m][...] = queries[m][...]
-
-
-def pack(keys, values, queries, gates, order, columns):
+
+
+def pack_far_kernel(members, *refs):
+    for m in range(members):
+        refs[members + m][...] = refs[m][...]
+
+
+def pack(parts, gates, order, columns):
     members = order.shape[0] // 2
-    tokens, rows = keys.shape[0], queries.shape[0]
-    block_rows = 2 * tokens + rows + 4 * gates.shape[0]
-
-    def kernel(order, *refs):
-        group = lambda i: refs[i * members : (i + 1) * members]
-        pack_kernel(
-            members,
-            order,
-            group(0),
-            group(1),
-            group(2),
-            refs[3 * members],
-            refs[3 * members + 1 : 4 * members + 1],
-            refs[4 * members + 1 :],
-        )
+    rows = sum(p.shape[0] for p in parts) + (0 if gates is None else 4 * gates.shape[0])
+    kernel = functools.partial(pack_far_kernel if gates is None else pack_kernel, members)
 
     def column(n, m):
         return pl.BlockSpec((n, columns), lambda j, order: (0, order[2 * m + j]))
 
-    result = pl.pallas_call(
-        kernel,
-        out_shape=[jax.ShapeDtypeStruct((block_rows, 2 * columns), keys.dtype)] * members
-        + [jax.ShapeDtypeStruct((rows, 2 * columns), keys.dtype)] * members,
+    in_specs = [column(p.shape[0], m) for p in parts for m in range(members)]
+    operands = [p for p in parts for m in range(members)]
+    if gates is not None:
+        in_specs.append(pl.BlockSpec((gates.shape[0], columns), lambda j, order: (0, j)))
+        operands.append(gates)
+    return pl.pallas_call(
+        lambda order, *refs: kernel(*refs),
+        out_shape=[jax.ShapeDtypeStruct((rows, 2 * columns), parts[0].dtype)] * members,
         grid_spec=pltpu.PrefetchScalarGridSpec(
             num_scalar_prefetch=1,
             grid=(2,),
-            in_specs=[column(n, m) for n in (tokens, tokens, rows) for m in range(members)]
-            + [pl.BlockSpec((gates.shape[0], columns), lambda j, order: (0, j))],
-            out_specs=[pl.BlockSpec((block_rows, columns), lambda j, order: (0, j))] * members
-            + [pl.BlockSpec((rows, columns), lambda j, order: (0, 1 - j))] * members,
+            in_specs=in_specs,
+            out_specs=[pl.BlockSpec((rows, columns), lambda j, order: (0, j))] * members,
         ),
         compiler_params=pltpu.CompilerParams(vmem_limit_bytes=32 * 1024 * 1024),
         cost_estimate=pl.CostEstimate(
-            flops=0, bytes_accessed=8 * members * block_rows * columns, transcendentals=0
-        ),
-    )(order, *[keys] * members, *[values] * members, *[queries] * members, gates)
-    return result[:members], result[members:]
+            flops=0, bytes_accessed=8 * members * rows * columns, transcendentals=0
+        ),
+    )(order, *operands)
 
 
 def attend_kernel(members, tokens, page_len, scale, page_req, page_slot, *refs):
@@ -143,7 +137,8 @@
     )(page_req, page_slot, *blocks, *far, row_req, row_pos)
 
 
-def project_kernel(mine, mine_level, theirs, their_level, proj, stay, go):
+def project_kernel(mine, mine_level, theirs, their_level, proj, stay, *gos):
+    place = 3 - pl.program_id(0)
     parts = []
     for head in range(mine.shape[0] // HEAD_DIM):
         dims = slice(head * HEAD_DIM, (head + 1) * HEAD_DIM)
@@ -159,60 +154,36 @@
     )
     rows = stay.shape[0]
     stay[...] = mixed[:rows, :]
-    go[...] = mixed[rows:, :].astype(jnp.bfloat16)
-
-
-def project(place, mine, mine_level, theirs, their_level, proj, tok_rows):
+    for i, go in enumerate(gos):
+        @pl.when(place == i)
+        def _(go=go):
+            go[...] = mixed[rows:, :].astype(jnp.bfloat16)
+
+
+def project(mine, mine_level, theirs, their_level, proj, tok_rows):
     columns, width = proj.shape
     heads = columns // HEAD_DIM
     size = mine.shape[1] // 4
     return pl.pallas_call(
         project_kernel,
-        out_shape=[
-            jax.ShapeDtypeStruct((tok_rows, width), jnp.float32),
-            jax.ShapeDtypeStruct((size - tok_rows, width), jnp.bfloat16),
-        ],
-        grid=(1,),
+        out_shape=[jax.ShapeDtypeStruct((4 * tok_rows, width), jnp.float32)]
+        + [jax.ShapeDtypeStruct((size - tok_rows, width), jnp.bfloat16)] * 4,
+        grid=(4,),
         in_specs=[
-            pl.BlockSpec((columns, size), lambda i: (0, place)),
-            pl.BlockSpec((heads, 1, size), lambda i: (0, 0, place)),
-            pl.BlockSpec((columns, size), lambda i: (0, (place + 2) % 4)),
-            pl.BlockSpec((heads, 1, size), lambda i: (0, 0, (place + 2) % 4)),
+            pl.BlockSpec((columns, size), lambda i: (0, 3 - i)),
+            pl.BlockSpec((heads, 1, size), lambda i: (0, 0, 3 - i)),
+            pl.BlockSpec((columns, size), lambda i: (0, (5 - i) % 4)),
+            pl.BlockSpec((heads, 1, size), lambda i: (0, 0, (5 - i) % 4)),
             pl.BlockSpec((columns, width), lambda i: (0, 0)),
         ],
-        out_specs=[
-            pl.BlockSpec((tok_rows, width), lambda i: (0, 0)),
-            pl.BlockSpec((size - tok_rows, width), lambda i: (0, 0)),
-        ],
+        out_specs=[pl.BlockSpec((tok_rows, width), lambda i: (3 - i, 0))]
+        + [pl.BlockSpec((size - tok_rows, width), lambda i: (0, 0))] * 4,
         cost_estimate=pl.CostEstimate(
-            flops=2 * size * columns * width,
-            bytes_accessed=2 * (2 * columns * size + columns * width + size * width),
-            transcendentals=2 * size * heads,
+            flops=8 * size * columns * width,
+            bytes_accessed=2 * (8 * columns * size + columns * width + 4 * size * width),
+            transcendentals=8 * size * heads,
         ),
     )(mine, mine_level, theirs, their_level, proj)
-
-
-def add_kernel(*refs):
-    parts, out = refs[:-1], refs[-1]
-    total = parts[0][...].astype(jnp.float32)
-    for part in parts[1:]:
-        total = total + part[...].astype(jnp.float32)
-    out[...] = total.astype(out.dtype)
-
-
-def add_up(parts, dtype):
-    vmem = pl.BlockSpec(memory_space=pltpu.VMEM)
-    return pl.pallas_call(
-        add_kernel,
-        out_shape=jax.ShapeDtypeStruct(parts[0].shape, dtype),
-        in_specs=[vmem] * len(parts),
-        out_specs=vmem,
-        cost_estimate=pl.CostEstimate(
-            flops=len(parts) * parts[0].size,
-            bytes_accessed=4 * len(parts) * parts[0].size,
-            transcendentals=0,
-        ),
-    )(*parts)
 
 
 def join_kernel(*refs):
@@ -450,6 +421,7 @@
     columns = width // exp_count
     keys = cache_key.reshape(tokens, width)
     values = cache_value.reshape(tokens, width)
+    far_queries = send(queries, 1, 0, 0)
     members = [(dl, dx) for dl in range(2) for dx in range(nx)]
     order = jnp.stack(
         [
@@ -459,9 +431,10 @@
         ]
     ).astype(i32)
     gates = jnp.pad(jnp.transpose(route_gate), ((0, 0), (0, 2 * columns - tok_rows)))
-    blocks, far = pack(keys, values, queries, gates, order, columns)
+    blocks = pack([keys, values, queries], gates, order, columns)
     blocks = [send(blocks[m], 0, *members[m]) for m in range(len(members))]
-    far = [send(far[m], 1, *members[m]) for m in range(len(members))]
+    far = pack([far_queries], None, order, columns)
+    far = [send(far[m], 0, *members[m]) for m in range(len(members))]
     page_ids = (
         rel_exp[: len(members), None] * pages_here + jnp.arange(pages_here, dtype=i32)[None, :]
     ).reshape(-1)
@@ -508,52 +481,58 @@
     place = place.reshape(ny, nc, 1, chunk_rows)
     row_gate = row_gate.reshape(ny, nc, 1, chunk_rows)
 
-    total = resid.astype(f32)
-    stays, goes = {}, {}
+    tie = lax.optimization_barrier
+    last = len(zs) - 1
+
+    stay, *goes = project(partial, level, other, other_level, out_proj, tok_rows)
+    stay = stay.reshape(len(zs), tok_rows, width)
+    comes = [
+        [send(go[(dx - 1) * tok_rows : dx * tok_rows], 0, 0, -dx) for dx in range(1, nx)]
+        for go in goes
+    ]
+    lines = {}
     for i in reversed(range(len(zs))):
-        stays[i], go = project(i, partial, level, other, other_level, out_proj, tok_rows)
-        goes[i] = [
-            send(go[(dx - 1) * tok_rows : dx * tok_rows], 0, 0, -dx) for dx in range(1, nx)
-        ]
-    for i in reversed(range(len(zs))):
+        line = stay[i]
+        for come in comes[i]:
+            line = line + come.astype(f32)
         if i:
-            line = add_up([stays[i]] + goes[i], bf16)
-            total = total + send(line, *zs[i], 0).astype(f32)
-        else:
-            total = total + stays[i]
-            for come in goes[i]:
-                total = total + come.astype(f32)
-    stream = total
+            line = line.astype(bf16)
+            comes[i - 1], line = tie((comes[i - 1], line))
+            line = send(line, *zs[i], 0)
+        lines[i] = line
+    stream = resid.astype(f32) + lines[0]
+    for i in range(1, len(zs)):
+        stream = stream + lines[i].astype(f32)
     normed = rms_normed(stream, norm_gain)
-    normed, place, row_gate = lax.optimization_barrier((normed, place, row_gate))
+    normed, place, row_gate = tie((normed, place, row_gate))
 
     line = [send(normed, *zs[i], 0) for i in range(len(zs))]
     piece = {}
     for i in range(len(zs)):
         piece[i, 0, 0] = line[i]
-        new = {}
+        for dx in range(1, nx):
+            piece[i, dx, 0] = send(line[i], 0, 0, dx)
         for dy in range(1, ny):
-            new[i, 0, dy] = send_req(line[i], dy, 0)
-        for dx in range(1, nx):
-            new[i, dx, 0] = send(line[i], 0, 0, dx)
-            if i:
-                for dy in range(1, ny):
-                    new[i - 1, dx, dy] = send(piece[i - 1, 0, dy], 0, 0, dx)
-        names = list(new)
-        tied = lax.optimization_barrier([new[name] for name in names] + line[i + 1 : i + 2])
-        if i + 1 < len(zs):
-            line[i + 1] = tied[-1]
-        for name, value in zip(names, tied):
-            piece[name] = value
-    last = len(zs) - 1
+            piece[i, 0, dy] = send_req(line[i], dy, 0)
+    piece = tie(piece)
     for dy in range(1, ny):
         for dx in range(1, nx):
-            piece[last, dx, dy] = send(piece[last, 0, dy], 0, 0, dx)
-
-    def chunk_of(dy):
-        return join([piece[i, dx, dy] for dx in range(nx) for i in range(len(zs))])
-
-    def answers_of(dy, chunk, partners, extra):
+            for i in range(len(zs)):
+                piece[i, dx, dy] = send(piece[i, 0, dy], 0, 0, dx)
+
+    chunk_of = lambda dy: join([piece[i, dx, dy] for dx in range(nx) for i in range(len(zs))])
+    partners_of = lambda chunk: [send_req(chunk, 0, dc) for dc in range(1, nc)]
+    chunk = chunk_of(0)
+    partners = partners_of(chunk)
+    extra = shared_expert(chunk, shared_scalar, shared_gate.T, shared_up.T, shared_down)
+    if ny > 1:
+        half = [(i, dx, 1) for dx in range(1, nx) for i in range(len(zs) // 2)]
+        extra, partners, *arrived = tie((extra, partners, *[piece[n] for n in half]))
+        for name, value in zip(half, arrived):
+            piece[name] = value
+
+    sums = {}
+    for dy in range(ny):
         answers = routed_expert(
             [chunk] + partners,
             place[dy],
@@ -564,47 +543,60 @@
             expert_down,
             entries,
         )
+        extra = None
+        answers, *rest = tie((answers, *[piece[i, dx, d] for i, dx, d in piece if d == dy + 1]))
+        for name, value in zip([n for n in piece if n[2] == dy + 1], rest):
+            piece[name] = value
+        others = [send_req(answers[dc], 0, -dc) for dc in range(1, nc)]
+        if dy + 1 < ny:
+            chunk = chunk_of(dy + 1)
+            chunk, others = tie((chunk, others))
+            partners = partners_of(chunk)
         here = answers[0].astype(f32)
-        for dc in range(1, nc):
-            here = here + send_req(answers[dc], 0, -dc).astype(f32)
-        return here.astype(bf16).reshape(nx, len(zs), tok_rows, width)
-
-    partners_of = lambda chunk: [send_req(chunk, 0, dc) for dc in range(1, nc)]
-    chunk = chunk_of(0)
-    partners = partners_of(chunk)
-    extra = shared_expert(chunk, shared_scalar, shared_gate.T, shared_up.T, shared_down)
-    sums, later = {}, {}
-    for dy in range(ny):
+        for come in others:
+            here = here + come.astype(f32)
+        here = here.reshape(nx, len(zs), tok_rows, width)
+        gone = here[1:].astype(bf16)
         if dy + 1 < ny:
-            names = [(i, dx, dy + 1) for dx in range(nx) for i in range(len(zs))]
-            tied = lax.optimization_barrier(
-                [extra] + partners + [piece[name] for name in names]
-            ) if extra is not None else None
-            if tied is not None:
-                extra, partners = tied[0], list(tied[1 : 1 + len(partners)])
-                for name, value in zip(names, tied[1 + len(partners) :]):
-                    piece[name] = value
-            following = chunk_of(dy + 1)
-            following_partners = partners_of(following)
-        here = answers_of(dy, chunk, partners, extra)
-        half = len(zs) // 2
-        for low in (half, 0):
-            group = here[0, low : low + half].astype(f32)
-            for dx in range(1, nx):
-                group = group + send(here[dx, low : low + half], 0, 0, -dx).astype(f32)
-            for i in range(half):
-                sums[low + i, dy] = group[i]
-        if dy + 1 < ny:
-            chunk, partners, extra = following, following_partners, None
-
-    total = stream
+            partners, gone = tie((partners, gone))
+            comes = [send(gone[dx - 1], 0, 0, -dx) for dx in range(1, nx)]
+            comes = [[come[i] for come in comes] for i in range(len(zs))]
+        else:
+            comes = [
+                [send(gone[dx - 1, i], 0, 0, -dx) for dx in range(1, nx)] for i in range(len(zs))
+            ]
+        sums[dy] = (here[0], comes)
+
+    lines = {}
     for i in reversed(range(len(zs))):
-        parts = [sums[i, 0]] + [send_req(sums[i, dy].astype(bf16), -dy, 0) for dy in range(1, ny)]
+        total = {}
+        for dy in range(ny):
+            here, comes = sums[dy]
+            total[dy] = here[i]
+            for come in comes[i]:
+                total[dy] = total[dy] + come.astype(f32)
+        goes = [total[dy].astype(bf16) for dy in range(1, ny)]
         if i:
-            total = total + send(add_up(parts, bf16), *zs[i], 0).astype(f32)
+            comes = sums[ny - 1][1]
+            comes[i - 1], goes = tie((comes[i - 1], goes))
+        lines[i] = (total[0], [send_req(go, -dy, 0) for dy, go in enumerate(goes, 1)])
+    home = stream
+    arrived = {}
+    for i in reversed(range(len(zs))):
+        total, comes = lines[i]
+        for come in comes:
+            total = total + come.astype(f32)
+        if i:
+            total = total.astype(bf16)
+            here, comes = lines[i - 1]
+            comes, total = tie((comes, total))
+            lines[i - 1] = (here, comes)
+            arrived[i] = send(total, *zs[i], 0)
         else:
-            for part in parts:
-                total = total + part.astype(f32)
+            home = home + total
+    for i in range(1, len(zs)):
+        home = home + arrived[i].astype(f32)
+    total = home
     return total.astype(bf16)
 
 

time: 309 us -> 331 us (1.071)
  waiting for transfers between devices: 137 us -> 172 us
  Pallas kernels: 77.2 us -> 61.5 us
  other arithmetic: 9.86 us -> 16.6 us
  local copies, waits for them, and re-layouts: 23 us -> 17.1 us
    ppermute x14, waiting for transfers between devices: 17.8 us -> 37.3 us  [send_req(): return lax.ppermute(value, 'req', pairs)]
    ppermute x35 -> x36, waiting for transfers between devices: 119 us -> 135 us  [send(): return lax.ppermute(value, 'exp', pairs)]
    pallas_call x11 -> x3, Pallas kernels: 24 us -> 8.32 us  [the longest x1 4.95 us: project(): pl.pallas_call(project_kernel, out_shape=[jax.ShapeDtypeStruct((4 * tok_r...]
    add x1 -> x2, other arithmetic: 0.33 us -> 4.68 us  [shards(): here = here + come.astype(f32)]
    unnamed x82 -> x68, local copies, waits for them, and re-layouts: 14.6 us -> 10.6 us
    ppermute x35 -> x36, starting transfers between devices: 49.1 us -> 52 us  [send(): return lax.ppermute(value, 'exp', pairs)]
  transfers between devices with their start and end apart: 49 -> 50, of which waited for: 29 -> 22; matrix products, arithmetic and copies ran while one was open for 5% -> 5% of each run, Pallas kernels for 20% -> 11%
where the time goes in v5:
time: 331 us; the launch traced here: 330 us
  waiting for transfers between devices  172 us (52%)
  Pallas kernels  61.5 us (19%)
  starting transfers between devices  60.1 us (18%)
  local copies, waits for them, and re-layouts  17.1 us (5%)
  other arithmetic  16.6 us (5%)
    ppermute x36, waiting for transfers between devices, send(): return lax.ppermute(value, 'exp', pairs)  135 us
    ppermute x36, starting transfers between devices, send(): return lax.ppermute(value, 'exp', pairs)  52 us
    ppermute x14, waiting for transfers between devices, send_req(): return lax.ppermute(value, 'req', pairs)  37.3 us
    pallas_call x2, Pallas kernels, routed_expert(): pl.pallas_call(functools.partial(routed_kernel, count, entries, has_extra...  30.5 us
    unnamed x68, local copies, waits for them, and re-layouts  10.6 us
    pallas_call x1, Pallas kernels, shared_expert(): pl.pallas_call(shared_kernel, out_shape=jax.ShapeDtypeStruct(rows.shape,...  8.74 us
    ppermute x14, starting transfers between devices, send_req(): return lax.ppermute(value, 'req', pairs)  8.14 us
    pallas_call x1, Pallas kernels, attend(): pl.pallas_call(functools.partial(attend_kernel, members, tokens, page_len...  7.82 us
  transfers between devices with their start and end apart: 50, of which 22 were waited for; matrix products, arithmetic and copies ran while one was open for 5% of the time, Pallas kernels for 11%

profile of v5, /device:TPU:0, one launch (start us, length us, event | category | flops | bytes accessed | tf_op | source)
XLA Modules:
  0.0 329.7 jit_solution(9762057197438396524)
XLA Ops:
  0.0 4.0 %collective-permute-start.3 = (bf16[64,2048]{1,0:T(8,128)(2,1)}, bf16[64,2048]{1,0:T(8,128)(2,1)S(1)}, u32[]{:S(2)}, u32[]{:S(2)}) collective-permute-start(bf16[64,2048]{1,0:T(8,128)(2,1)} %refs_11_.1), channel_id=1, source_target_pairs={{0,4},{1,5},{2,6},{3,7},{4,0},{5,1},{6,2},{7,3},{8,12},{9,13},{10,... | collective-permute-start | bytes 786440 | tf_op jit(solution)/shard_map/ppermute | solution.py:398
  8.2 2.6 shard_map.181
  29.7 13.5 %collective-permute-done.2.refs_3_ = bf16[592,512]{1,0:T(8,128)(2,1)S(1)} collective-permute-done((bf16[592,512]{1,0:T(8,128)(2,1)}, bf16[592,512]{1,0:T(8,128)(2,1)S(1)}, u32[]{:S(2)}, u32[]{:S(2)}) %collective-permute-start.2) | collective-permute-done | bytes 606240 | tf_op jit(solution)/shard_map/ppermute | solution.py:398
  45.9 7.8 %shard_map.183 = (bf16[512,512]{1,0:T(8,128)(2,1)S(1)}, f32[4,1,512]{2,1,0:T(1,128)S(1)}) custom-call(s32[8]{0:T(128)S(1)} %get-tuple-element.146.page_req, s32[8]{0:T(128)S(1)} %get-tuple-element.145.page_slot, bf16[592,512]{1,0:T(8,128)(2,1)S(1)} %get-tuple-element.75.refs_0_, bf16[592,512]{1,0:T(8,128)(2,1)S(1)} %collective-permute-done.refs_1_, ...), custom_call_target="tpu_custom_call" | custom-call | flops 1073741824 | bytes 2686976 | tf_op jit(solution)/shard_map/pallas_call | solution.py:116
  54.5 2.3 collective-permute-start.16
  58.2 10.9 %collective-permute-done.16 = f32[2,2,4,64]{3,0,1,2:T(2,128)S(1)} collective-permute-done((f32[2,2,4,64]{3,0,1,2:T(2,128)S(1)}, f32[2,2,4,64]{3,0,1,2:T(2,128)S(1)}, u32[]{:S(2)}, u32[]{:S(2)}) %collective-permute-start.16) | collective-permute-done | bytes 4128 | tf_op jit(solution)/shard_map/ppermute | solution.py:398
  72.0 5.0 %shard_map.184 = (f32[256,2048]{1,0:T(8,128)}, bf16[64,2048]{1,0:T(8,128)(2,1)}, bf16[64,2048]{1,0:T(8,128)(2,1)}, bf16[64,2048]{1,0:T(8,128)(2,1)}, bf16[64,2048]{1,0:T(8,128)(2,1)}) custom-call(bf16[512,512]{1,0:T(8,128)(2,1)} %copy-done.4, f32[4,1,512]{2,1,0:T(1,128)} %copy-done.5, bf16[256,512]{1,0:T(8,128)(2,1)} %copy-done.32, f32[2,1,512]{2,1,0:T(1,128)} %copy-done.33, ...), custom_call_target="tpu_custom_call" | custom-call | flops 536870912 | bytes 3670016 | tf_op jit(solution)/shard_map/pallas_call | solution.py:167
  81.5 5.0 %collective-permute-done.12 = bf16[64,2048]{1,0:T(8,128)(2,1)S(1)} collective-permute-done((bf16[64,2048]{1,0:T(8,128)(2,1)}, bf16[64,2048]{1,0:T(8,128)(2,1)S(1)}, u32[]{:S(2)}, u32[]{:S(2)}) %collective-permute-start.12) | collective-permute-done | bytes 262176 | tf_op jit(solution)/shard_map/ppermute | solution.py:398
  87.6 13.6 %collective-permute-done.11 = bf16[64,2048]{1,0:T(8,128)(2,1)S(1)} collective-permute-done((bf16[64,2048]{1,0:T(8,128)(2,1)}, bf16[64,2048]{1,0:T(8,128)(2,1)S(1)}, u32[]{:S(2)}, u32[]{:S(2)}) %collective-permute-start.11) | collective-permute-done | bytes 262176 | tf_op jit(solution)/shard_map/ppermute | solution.py:398
  103.5 2.9 collective-permute-start.14
  108.1 5.9 %collective-permute-done.13 = bf16[64,2048]{1,0:T(8,128)(2,1)S(1)} collective-permute-done((bf16[64,2048]{1,0:T(8,128)(2,1)S(1)}, bf16[64,2048]{1,0:T(8,128)(2,1)S(1)}, u32[]{:S(2)}, u32[]{:S(2)}) %collective-permute-start.13) | collective-permute-done | bytes 262176 | tf_op jit(solution)/shard_map/ppermute | solution.py:398
  114.0 10.9 %collective-permute-done.14 = bf16[64,2048]{1,0:T(8,128)(2,1)S(1)} collective-permute-done((bf16[64,2048]{1,0:T(8,128)(2,1)S(1)}, bf16[64,2048]{1,0:T(8,128)(2,1)S(1)}, u32[]{:S(2)}, u32[]{:S(2)}) %collective-permute-start.14) | collective-permute-done | bytes 262176 | tf_op jit(solution)/shard_map/ppermute | solution.py:398
  128.4 6.7 %collective-permute-start.24 = (bf16[64,2048]{1,0:T(8,128)(2,1)S(1)}, bf16[64,2048]{1,0:T(8,128)(2,1)S(1)}, u32[]{:S(2)}, u32[]{:S(2)}) collective-permute-start(bf16[64,2048]{1,0:T(8,128)(2,1)S(1)} %multiply_convert_fusion.refs_0_), channel_id=1, source_target_pairs={{0,4},{1,5},{2,6},{3,7},{4,0},{5,1},{6,2},{7,3},{8,12},{9,13},{10,... | collective-permute-start | bytes 786440 | tf_op jit(solution)/shard_map/ppermute | solution.py:398
  137.9 12.9 %collective-permute-done.24.refs_2_ = bf16[64,2048]{1,0:T(8,128)(2,1)S(1)} collective-permute-done((bf16[64,2048]{1,0:T(8,128)(2,1)S(1)}, bf16[64,2048]{1,0:T(8,128)(2,1)S(1)}, u32[]{:S(2)}, u32[]{:S(2)}) %collective-permute-start.24) | collective-permute-done | bytes 262176 | tf_op jit(solution)/shard_map/ppermute | solution.py:398
  155.3 4.7 %collective-permute-done.28.refs_3_ = bf16[64,2048]{1,0:T(8,128)(2,1)S(1)} collective-permute-done((bf16[64,2048]{1,0:T(8,128)(2,1)S(1)}, bf16[64,2048]{1,0:T(8,128)(2,1)S(1)}, u32[]{:S(2)}, u32[]{:S(2)}) %collective-permute-start.28) | collective-permute-done | bytes 262176 | tf_op jit(solution)/shard_map/ppermute | solution.py:408
  160.5 5.2 %collective-permute-done.25.refs_2_ = bf16[64,2048]{1,0:T(8,128)(2,1)} collective-permute-done((bf16[64,2048]{1,0:T(8,128)(2,1)S(1)}, bf16[64,2048]{1,0:T(8,128)(2,1)}, u32[]{:S(2)}, u32[]{:S(2)}) %collective-permute-start.25) | collective-permute-done | bytes 262176 | tf_op jit(solution)/shard_map/ppermute | solution.py:408
  165.7 3.7 %collective-permute-done.22.refs_1_ = bf16[64,2048]{1,0:T(8,128)(2,1)S(1)} collective-permute-done((bf16[64,2048]{1,0:T(8,128)(2,1)S(1)}, bf16[64,2048]{1,0:T(8,128)(2,1)S(1)}, u32[]{:S(2)}, u32[]{:S(2)}) %collective-permute-start.22) | collective-permute-done | bytes 262176 | tf_op jit(solution)/shard_map/ppermute | solution.py:408
  169.5 3.1 shard_map.185.rows.refs_0_
  179.5 8.7 %shard_map.186.refs_4_ = bf16[512,2048]{1,0:T(8,128)(2,1)S(1)} custom-call(bf16[512,2048]{1,0:T(8,128)(2,1)S(1)} %copy-done.3, bf16[1,2048]{1,0:T(2,128)(2,1)S(1)} %reshape.599.scalar, bf16[704,2048]{1,0:T(8,128)(2,1)} %bitcast.128, bf16[704,2048]{1,0:T(8,128)(2,1)} %bitcast.129, bf16[704,2048]{1,0:T(8,128)(2,1)} %down_w.1), custom_call_target="tpu_custom_call" | custom-call | flops 4429185024 | bytes 12845056 | tf_op jit(solution)/shard_map/pallas_call | solution.py:240
  191.1 15.4 %shard_map.187 = (bf16[512,2048]{1,0:T(8,128)(2,1)}, bf16[512,2048]{1,0:T(8,128)(2,1)}) custom-call(bf16[512,2048]{1,0:T(8,128)(2,1)} %shard_map.185.rows.refs_0_, bf16[512,2048]{1,0:T(8,128)(2,1)} %copy-done.31, s32[2,1,512]{2,1,0:T(1,128)} %get-tuple-element.162.refs_2_, f32[2,1,512]{2,1,0:T(1,128)} %get-tuple-element.160.refs_3_, ...), custom_call_target="tpu_custom_call" | custom-call | flops 8254390272 | bytes 25690112 | tf_op jit(solution)/shard_map/pallas_call | solution.py:318
  208.0 3.0 shard_map.188.refs_0_
  212.6 2.3 convert_add_fusion.1
  217.6 15.1 %shard_map.189 = (bf16[512,2048]{1,0:T(8,128)(2,1)}, bf16[512,2048]{1,0:T(8,128)(2,1)}) custom-call(bf16[512,2048]{1,0:T(8,128)(2,1)} %shard_map.188.refs_0_, bf16[512,2048]{1,0:T(8,128)(2,1)} %collective-permute-done.36.refs_1_, s32[2,1,512]{2,1,0:T(1,128)} %get-tuple-element.161.refs_2_, f32[2,1,512]{2,1,0:T(1,128)} %get-tuple-element.159.refs_3_, ...), custom_call_target="tpu_custom_call" | custom-call | flops 8254390272 | bytes 25690112 | tf_op jit(solution)/shard_map/pallas_call | solution.py:318
  232.9 4.2 %collective-permute-done.38 = bf16[512,2048]{1,0:T(8,128)(2,1)S(1)} collective-permute-done((bf16[512,2048]{1,0:T(8,128)(2,1)}, bf16[512,2048]{1,0:T(8,128)(2,1)S(1)}, u32[]{:S(2)}, u32[]{:S(2)}) %collective-permute-start.38) | collective-permute-done | bytes 2097184 | tf_op jit(solution)/shard_map/ppermute | solution.py:408
  237.1 2.3 convert_add_fusion
  245.4 3.6 %collective-permute-done.42 = bf16[64,2048]{1,0:T(8,128)(2,1)S(1)} collective-permute-done((bf16[64,2048]{1,0:T(8,128)(2,1)S(1)}, bf16[64,2048]{1,0:T(8,128)(2,1)S(1)}, u32[]{:S(2)}, u32[]{:S(2)}) %collective-permute-start.42) | collective-permute-done | bytes 262176 | tf_op jit(solution)/shard_map/ppermute | solution.py:398
  249.0 33.7 %collective-permute-done.41 = bf16[64,2048]{1,0:T(8,128)(2,1)S(1)} collective-permute-done((bf16[64,2048]{1,0:T(8,128)(2,1)S(1)}, bf16[64,2048]{1,0:T(8,128)(2,1)S(1)}, u32[]{:S(2)}, u32[]{:S(2)}) %collective-permute-start.41) | collective-permute-done | bytes 262176 | tf_op jit(solution)/shard_map/ppermute | solution.py:398
  283.3 4.2 %collective-permute-done.40 = bf16[64,2048]{1,0:T(8,128)(2,1)S(1)} collective-permute-done((bf16[64,2048]{1,0:T(8,128)(2,1)S(1)}, bf16[64,2048]{1,0:T(8,128)(2,1)S(1)}, u32[]{:S(2)}, u32[]{:S(2)}) %collective-permute-start.40) | collective-permute-done | bytes 262176 | tf_op jit(solution)/shard_map/ppermute | solution.py:398
  290.3 16.2 %collective-permute-done.45 = bf16[64,2048]{1,0:T(8,128)(2,1)S(1)} collective-permute-done((bf16[64,2048]{1,0:T(8,128)(2,1)S(1)}, bf16[64,2048]{1,0:T(8,128)(2,1)S(1)}, u32[]{:S(2)}, u32[]{:S(2)}) %collective-permute-start.45) | collective-permute-done | bytes 262176 | tf_op jit(solution)/shard_map/ppermute | solution.py:408
  306.9 3.4 %collective-permute-start.48 = (bf16[64,2048]{1,0:T(8,128)(2,1)S(1)}, bf16[64,2048]{1,0:T(8,128)(2,1)S(1)}, u32[]{:S(2)}, u32[]{:S(2)}) collective-permute-start(bf16[64,2048]{1,0:T(8,128)(2,1)S(1)} %fusion.3), channel_id=1, source_target_pairs={{0,4},{1,5},{2,6},{3,7},{4,0},{5,1},{6,2},{7,3},{8,12},{9,13},{10,... | collective-permute-start | bytes 786440 | tf_op jit(solution)/shard_map/ppermute | solution.py:398
  311.1 6.4 %collective-permute-done.47 = bf16[64,2048]{1,0:T(8,128)(2,1)S(1)} collective-permute-done((bf16[64,2048]{1,0:T(8,128)(2,1)S(1)}, bf16[64,2048]{1,0:T(8,128)(2,1)S(1)}, u32[]{:S(2)}, u32[]{:S(2)}) %collective-permute-start.47) | collective-permute-done | bytes 262176 | tf_op jit(solution)/shard_map/ppermute | solution.py:398
  317.5 11.3 %collective-permute-done.48 = bf16[64,2048]{1,0:T(8,128)(2,1)S(1)} collective-permute-done((bf16[64,2048]{1,0:T(8,128)(2,1)S(1)}, bf16[64,2048]{1,0:T(8,128)(2,1)S(1)}, u32[]{:S(2)}, u32[]{:S(2)}) %collective-permute-start.48) | collective-permute-done | bytes 262176 | tf_op jit(solution)/shard_map/ppermute | solution.py:398
  (230 shorter events, 77.2 us)
Async XLA Ops:
  0.0 23.9 %collective-permute-start.3 = (bf16[64,2048]{1,0:T(8,128)(2,1)}, bf16[64,2048]{1,0:T(8,128)(2,1)S(1)}, u32[]{:S(2)}, u32[]{:S(2)}) collective-permute-start(bf16[64,2048]{1,0:T(8,128)(2,1)} %refs_11_.1), channel_id=1, source_target_pairs={{0,4},{1,5},{2,6},{3,7},{4,0},{5,1},{6,2},{7,3},{8,12},{9,13},{10,... | collective-permute-start | bytes 786440 | tf_op jit(solution)/shard_map/ppermute | solution.py:398
  10.8 17.1 %collective-permute-start = (bf16[592,512]{1,0:T(8,128)(2,1)}, bf16[592,512]{1,0:T(8,128)(2,1)S(1)}, u32[]{:S(2)}, u32[]{:S(2)}) collective-permute-start(bf16[592,512]{1,0:T(8,128)(2,1)} %get-tuple-element.76), channel_id=1, source_target_pairs={{0,1},{1,0},{2,3},{3,2},{4,5},{5,4},{6,7},{7,6},{8,9},{9,8},{10,11... | collective-permute-start | bytes 1818632 | tf_op jit(solution)/shard_map/ppermute | solution.py:398
  12.3 17.4 %collective-permute-start.1 = (bf16[592,512]{1,0:T(8,128)(2,1)}, bf16[592,512]{1,0:T(8,128)(2,1)S(1)}, u32[]{:S(2)}, u32[]{:S(2)}) collective-permute-start(bf16[592,512]{1,0:T(8,128)(2,1)} %get-tuple-element.77), channel_id=1, source_target_pairs={{0,2},{1,3},{2,0},{3,1},{4,6},{5,7},{6,4},{7,5},{8,10},{9,11},{10,... | collective-permute-start | bytes 1818632 | tf_op jit(solution)/shard_map/ppermute | solution.py:398
  13.9 29.4 %collective-permute-start.2 = (bf16[592,512]{1,0:T(8,128)(2,1)}, bf16[592,512]{1,0:T(8,128)(2,1)S(1)}, u32[]{:S(2)}, u32[]{:S(2)}) collective-permute-start(bf16[592,512]{1,0:T(8,128)(2,1)} %get-tuple-element.78), channel_id=1, source_target_pairs={{0,3},{1,2},{2,1},{3,0},{4,7},{5,6},{6,5},{7,4},{8,11},{9,10},{10,... | collective-permute-start | bytes 1818632 | tf_op jit(solution)/shard_map/ppermute | solution.py:398
  24.7 18.5 %collective-permute-start.4 = (bf16[64,512]{1,0:T(8,128)(2,1)S(1)}, bf16[64,512]{1,0:T(8,128)(2,1)S(1)}, u32[]{:S(2)}, u32[]{:S(2)}) collective-permute-start(bf16[64,512]{1,0:T(8,128)(2,1)S(1)} %get-tuple-element.80), channel_id=1, source_target_pairs={{0,1},{1,0},{2,3},{3,2},{4,5},{5,4},{6,7},{7,6},{8,9},{9,8},{10,11... | collective-permute-start | bytes 196616 | tf_op jit(solution)/shard_map/ppermute | solution.py:398
  26.3 17.3 %collective-permute-start.5 = (bf16[64,512]{1,0:T(8,128)(2,1)S(1)}, bf16[64,512]{1,0:T(8,128)(2,1)S(1)}, u32[]{:S(2)}, u32[]{:S(2)}) collective-permute-start(bf16[64,512]{1,0:T(8,128)(2,1)S(1)} %get-tuple-element.81), channel_id=1, source_target_pairs={{0,2},{1,3},{2,0},{3,1},{4,6},{5,7},{6,4},{7,5},{8,10},{9,11},{10,... | collective-permute-start | bytes 196616 | tf_op jit(solution)/shard_map/ppermute | solution.py:398
  27.9 18.1 %collective-permute-start.6 = (bf16[64,512]{1,0:T(8,128)(2,1)S(1)}, bf16[64,512]{1,0:T(8,128)(2,1)S(1)}, u32[]{:S(2)}, u32[]{:S(2)}) collective-permute-start(bf16[64,512]{1,0:T(8,128)(2,1)S(1)} %get-tuple-element.82), channel_id=1, source_target_pairs={{0,3},{1,2},{2,1},{3,0},{4,7},{5,6},{6,5},{7,4},{8,11},{9,10},{10,... | collective-permute-start | bytes 196616 | tf_op jit(solution)/shard_map/ppermute | solution.py:398
  53.8 16.9 %collective-permute-start.7 = (bf16[256,512]{1,0:T(8,128)(2,1)S(1)}, bf16[256,512]{1,0:T(8,128)(2,1)S(1)}, u32[]{:S(2)}, u32[]{:S(2)}) collective-permute-start(bf16[256,512]{1,0:T(8,128)(2,1)S(1)} %slice.168), channel_id=1, source_target_pairs={{0,4},{1,5},{2,6},{3,7},{4,0},{5,1},{6,2},{7,3},{8,12},{9,13},{10,... | collective-permute-start | bytes 786440 | tf_op jit(solution)/shard_map/ppermute | solution.py:398
  77.9 30.0 %collective-permute-start.18 = (f32[2,2,2,2,4,64]{5,2,1,3,0,4:T(2,128)S(1)}, f32[2,2,2,2,4,64]{5,2,1,3,0,4:T(2,128)S(1)}, u32[]{:S(2)}, u32[]{:S(2)}) collective-permute-start(f32[2,2,2,2,4,64]{5,2,1,3,0,4:T(2,128)S(1)} %get-tuple-element.156), channel_id=1, source_target_pairs={{0,8},{8,0},{16,24},{24,16},{1,9},{9,1},{17,25},{25,17},{2,10},{10... | collective-permute-start | bytes 49160 | tf_op jit(solution)/shard_map/ppermute | solution.py:408
  77.9 25.4 %collective-permute-start.9 = (bf16[64,2048]{1,0:T(8,128)(2,1)}, bf16[64,2048]{1,0:T(8,128)(2,1)S(1)}, u32[]{:S(2)}, u32[]{:S(2)}) collective-permute-start(bf16[64,2048]{1,0:T(8,128)(2,1)} %get-tuple-element.86), channel_id=1, source_target_pairs={{0,1},{1,0},{2,3},{3,2},{4,5},{5,4},{6,7},{7,6},{8,9},{9,8},{10,11... | collective-permute-start | bytes 786440 | tf_op jit(solution)/shard_map/ppermute | solution.py:398
  79.5 22.8 %collective-permute-start.10 = (bf16[64,2048]{1,0:T(8,128)(2,1)}, bf16[64,2048]{1,0:T(8,128)(2,1)S(1)}, u32[]{:S(2)}, u32[]{:S(2)}) collective-permute-start(bf16[64,2048]{1,0:T(8,128)(2,1)} %get-tuple-element.87), channel_id=1, source_target_pairs={{0,1},{1,0},{2,3},{3,2},{4,5},{5,4},{6,7},{7,6},{8,9},{9,8},{10,11... | collective-permute-start | bytes 786440 | tf_op jit(solution)/shard_map/ppermute | solution.py:398
  80.0 21.1 %collective-permute-start.11 = (bf16[64,2048]{1,0:T(8,128)(2,1)}, bf16[64,2048]{1,0:T(8,128)(2,1)S(1)}, u32[]{:S(2)}, u32[]{:S(2)}) collective-permute-start(bf16[64,2048]{1,0:T(8,128)(2,1)} %get-tuple-element.88), channel_id=1, source_target_pairs={{0,1},{1,0},{2,3},{3,2},{4,5},{5,4},{6,7},{7,6},{8,9},{9,8},{10,11... | collective-permute-start | bytes 786440 | tf_op jit(solution)/shard_map/ppermute | solution.py:398
  103.5 21.4 %collective-permute-start.14 = (bf16[64,2048]{1,0:T(8,128)(2,1)S(1)}, bf16[64,2048]{1,0:T(8,128)(2,1)S(1)}, u32[]{:S(2)}, u32[]{:S(2)}) collective-permute-start(bf16[64,2048]{1,0:T(8,128)(2,1)S(1)} %add_convert_fusion.1), channel_id=1, source_target_pairs={{0,4},{1,5},{2,6},{3,7},{4,0},{5,1},{6,2},{7,3},{8,12},{9,13},{10,... | collective-permute-start | bytes 786440 | tf_op jit(solution)/shard_map/ppermute | solution.py:398
  106.4 18.5 %collective-permute-start.15 = (bf16[64,2048]{1,0:T(8,128)(2,1)S(1)}, bf16[64,2048]{1,0:T(8,128)(2,1)S(1)}, u32[]{:S(2)}, u32[]{:S(2)}) collective-permute-start(bf16[64,2048]{1,0:T(8,128)(2,1)S(1)} %add_convert_fusion.2), channel_id=1, source_target_pairs={{0,6},{1,7},{2,4},{3,5},{4,2},{5,3},{6,0},{7,1},{8,14},{9,15},{10,... | collective-permute-start | bytes 786440 | tf_op jit(solution)/shard_map/ppermute | solution.py:398
  128.4 22.4 %collective-permute-start.24 = (bf16[64,2048]{1,0:T(8,128)(2,1)S(1)}, bf16[64,2048]{1,0:T(8,128)(2,1)S(1)}, u32[]{:S(2)}, u32[]{:S(2)}) collective-permute-start(bf16[64,2048]{1,0:T(8,128)(2,1)S(1)} %multiply_convert_fusion.refs_0_), channel_id=1, source_target_pairs={{0,4},{1,5},{2,6},{3,7},{4,0},{5,1},{6,2},{7,3},{8,12},{9,13},{10,... | collective-permute-start | bytes 786440 | tf_op jit(solution)/shard_map/ppermute | solution.py:398
  135.0 16.2 %collective-permute-start.21 = (bf16[64,2048]{1,0:T(8,128)(2,1)S(1)}, bf16[64,2048]{1,0:T(8,128)(2,1)S(1)}, u32[]{:S(2)}, u32[]{:S(2)}) collective-permute-start(bf16[64,2048]{1,0:T(8,128)(2,1)S(1)} %multiply_convert_fusion.refs_0_), channel_id=1, source_target_pairs={{0,2},{1,3},{2,0},{3,1},{4,6},{5,7},{6,4},{7,5},{8,10},{9,11},{10,... | collective-permute-start | bytes 786440 | tf_op jit(solution)/shard_map/ppermute | solution.py:398
  135.0 17.8 %collective-permute-start.20 = (bf16[64,2048]{1,0:T(8,128)(2,1)S(1)}, bf16[64,2048]{1,0:T(8,128)(2,1)S(1)}, u32[]{:S(2)}, u32[]{:S(2)}) collective-permute-start(bf16[64,2048]{1,0:T(8,128)(2,1)S(1)} %multiply_convert_fusion.refs_0_), channel_id=1, source_target_pairs={{0,1},{1,0},{2,3},{3,2},{4,5},{5,4},{6,7},{7,6},{8,9},{9,8},{10,11... | collective-permute-start | bytes 786440 | tf_op jit(solution)/shard_map/ppermute | solution.py:398
  136.6 17.7 %collective-permute-start.19 = (bf16[64,2048]{1,0:T(8,128)(2,1)S(1)}, bf16[64,2048]{1,0:T(8,128)(2,1)S(1)}, u32[]{:S(2)}, u32[]{:S(2)}) collective-permute-start(bf16[64,2048]{1,0:T(8,128)(2,1)S(1)} %multiply_convert_fusion.refs_0_), channel_id=1, source_target_pairs={{0,16},{8,24},{16,0},{24,8},{1,17},{9,25},{17,1},{25,9},{2,18},{10... | collective-permute-start | bytes 786440 | tf_op jit(solution)/shard_map/ppermute | solution.py:408
  137.1 17.7 %collective-permute-start.29 = (bf16[64,2048]{1,0:T(8,128)(2,1)S(1)}, bf16[64,2048]{1,0:T(8,128)(2,1)S(1)}, u32[]{:S(2)}, u32[]{:S(2)}) collective-permute-start(bf16[64,2048]{1,0:T(8,128)(2,1)S(1)} %collective-permute-done.27.refs_3_), channel_id=1, source_target_pairs={{0,1},{1,0},{2,3},{3,2},{4,5},{5,4},{6,7},{7,6},{8,9},{9,8},{10,11... | collective-permute-start | bytes 786440 | tf_op jit(solution)/shard_map/ppermute | solution.py:398
  172.6 17.1 %collective-permute-start.30 = (bf16[512,2048]{1,0:T(8,128)(2,1)}, bf16[512,2048]{1,0:T(8,128)(2,1)S(1)}, u32[]{:S(2)}, u32[]{:S(2)}) collective-permute-start(bf16[512,2048]{1,0:T(8,128)(2,1)} %shard_map.185.rows.refs_0_), channel_id=1, source_target_pairs={{0,8},{8,0},{16,24},{24,16},{1,9},{9,1},{17,25},{25,17},{2,10},{10... | collective-permute-start | bytes 6291464 | tf_op jit(solution)/shard_map/ppermute | solution.py:408
  173.8 15.8 %collective-permute-start.31 = (bf16[64,2048]{1,0:T(8,128)(2,1)S(1)}, bf16[64,2048]{1,0:T(8,128)(2,1)S(1)}, u32[]{:S(2)}, u32[]{:S(2)}) collective-permute-start(bf16[64,2048]{1,0:T(8,128)(2,1)S(1)} %collective-permute-done.19.refs_0_), channel_id=1, source_target_pairs={{0,1},{1,0},{2,3},{3,2},{4,5},{5,4},{6,7},{7,6},{8,9},{9,8},{10,11... | collective-permute-start | bytes 786440 | tf_op jit(solution)/shard_map/ppermute | solution.py:398
  175.8 30.7 %collective-permute-start.33 = (bf16[64,2048]{1,0:T(8,128)(2,1)}, bf16[64,2048]{1,0:T(8,128)(2,1)S(1)}, u32[]{:S(2)}, u32[]{:S(2)}) collective-permute-start(bf16[64,2048]{1,0:T(8,128)(2,1)} %collective-permute-done.25.refs_2_), channel_id=1, source_target_pairs={{0,1},{1,0},{2,3},{3,2},{4,5},{5,4},{6,7},{7,6},{8,9},{9,8},{10,11... | collective-permute-start | bytes 786440 | tf_op jit(solution)/shard_map/ppermute | solution.py:398
  177.4 29.2 %collective-permute-start.34 = (bf16[64,2048]{1,0:T(8,128)(2,1)S(1)}, bf16[64,2048]{1,0:T(8,128)(2,1)S(1)}, u32[]{:S(2)}, u32[]{:S(2)}) collective-permute-start(bf16[64,2048]{1,0:T(8,128)(2,1)S(1)} %collective-permute-done.28.refs_3_), channel_id=1, source_target_pairs={{0,1},{1,0},{2,3},{3,2},{4,5},{5,4},{6,7},{7,6},{8,9},{9,8},{10,11... | collective-permute-start | bytes 786440 | tf_op jit(solution)/shard_map/ppermute | solution.py:398
  241.3 48.9 %collective-permute-start.37 = (bf16[4,64,2048]{2,1,0:T(8,128)(2,1)S(1)}, bf16[4,64,2048]{2,1,0:T(8,128)(2,1)S(1)}, u32[]{:S(2)}, u32[]{:S(2)}) collective-permute-start(bf16[4,64,2048]{2,1,0:T(8,128)(2,1)S(1)} %bitcast.117), channel_id=1, source_target_pairs={{0,1},{1,0},{2,3},{3,2},{4,5},{5,4},{6,7},{7,6},{8,9},{9,8},{10,11... | collective-permute-start | bytes 3145736 | tf_op jit(solution)/shard_map/ppermute | solution.py:398
  241.8 45.7 %collective-permute-start.39 = (bf16[64,2048]{1,0:T(8,128)(2,1)S(1)}, bf16[64,2048]{1,0:T(8,128)(2,1)S(1)}, u32[]{:S(2)}, u32[]{:S(2)}) collective-permute-start(bf16[64,2048]{1,0:T(8,128)(2,1)S(1)} %get-tuple-element.151), channel_id=1, source_target_pairs={{0,1},{1,0},{2,3},{3,2},{4,5},{5,4},{6,7},{7,6},{8,9},{9,8},{10,11... | collective-permute-start | bytes 786440 | tf_op jit(solution)/shard_map/ppermute | solution.py:398
  243.3 39.3 %collective-permute-start.41 = (bf16[64,2048]{1,0:T(8,128)(2,1)S(1)}, bf16[64,2048]{1,0:T(8,128)(2,1)S(1)}, u32[]{:S(2)}, u32[]{:S(2)}) collective-permute-start(bf16[64,2048]{1,0:T(8,128)(2,1)S(1)} %get-tuple-element.153), channel_id=1, source_target_pairs={{0,1},{1,0},{2,3},{3,2},{4,5},{5,4},{6,7},{7,6},{8,9},{9,8},{10,11... | collective-permute-start | bytes 786440 | tf_op jit(solution)/shard_map/ppermute | solution.py:398
  243.8 43.6 %collective-permute-start.40 = (bf16[64,2048]{1,0:T(8,128)(2,1)S(1)}, bf16[64,2048]{1,0:T(8,128)(2,1)S(1)}, u32[]{:S(2)}, u32[]{:S(2)}) collective-permute-start(bf16[64,2048]{1,0:T(8,128)(2,1)S(1)} %get-tuple-element.154), channel_id=1, source_target_pairs={{0,1},{1,0},{2,3},{3,2},{4,5},{5,4},{6,7},{7,6},{8,9},{9,8},{10,11... | collective-permute-start | bytes 786440 | tf_op jit(solution)/shard_map/ppermute | solution.py:398
  287.6 19.0 %collective-permute-start.43 = (bf16[64,2048]{1,0:T(8,128)(2,1)S(1)}, bf16[64,2048]{1,0:T(8,128)(2,1)S(1)}, u32[]{:S(2)}, u32[]{:S(2)}) collective-permute-start(bf16[64,2048]{1,0:T(8,128)(2,1)S(1)} %fusion.9), channel_id=1, source_target_pairs={{0,16},{8,24},{16,0},{24,8},{1,17},{9,25},{17,1},{25,9},{2,18},{10... | collective-permute-start | bytes 786440 | tf_op jit(solution)/shard_map/ppermute | solution.py:408
  288.1 18.4 %collective-permute-start.44 = (bf16[64,2048]{1,0:T(8,128)(2,1)S(1)}, bf16[64,2048]{1,0:T(8,128)(2,1)S(1)}, u32[]{:S(2)}, u32[]{:S(2)}) collective-permute-start(bf16[64,2048]{1,0:T(8,128)(2,1)S(1)} %fusion.8), channel_id=1, source_target_pairs={{0,16},{8,24},{16,0},{24,8},{1,17},{9,25},{17,1},{25,9},{2,18},{10... | collective-permute-start | bytes 786440 | tf_op jit(solution)/shard_map/ppermute | solution.py:408
  289.7 16.7 %collective-permute-start.45 = (bf16[64,2048]{1,0:T(8,128)(2,1)S(1)}, bf16[64,2048]{1,0:T(8,128)(2,1)S(1)}, u32[]{:S(2)}, u32[]{:S(2)}) collective-permute-start(bf16[64,2048]{1,0:T(8,128)(2,1)S(1)} %fusion.7), channel_id=1, source_target_pairs={{0,16},{8,24},{16,0},{24,8},{1,17},{9,25},{17,1},{25,9},{2,18},{10... | collective-permute-start | bytes 786440 | tf_op jit(solution)/shard_map/ppermute | solution.py:408
  306.9 21.8 %collective-permute-start.48 = (bf16[64,2048]{1,0:T(8,128)(2,1)S(1)}, bf16[64,2048]{1,0:T(8,128)(2,1)S(1)}, u32[]{:S(2)}, u32[]{:S(2)}) collective-permute-start(bf16[64,2048]{1,0:T(8,128)(2,1)S(1)} %fusion.3), channel_id=1, source_target_pairs={{0,4},{1,5},{2,6},{3,7},{4,0},{5,1},{6,2},{7,3},{8,12},{9,13},{10,... | collective-permute-start | bytes 786440 | tf_op jit(solution)/shard_map/ppermute | solution.py:398
  310.3 18.5 %collective-permute-start.49 = (bf16[64,2048]{1,0:T(8,128)(2,1)S(1)}, bf16[64,2048]{1,0:T(8,128)(2,1)S(1)}, u32[]{:S(2)}, u32[]{:S(2)}) collective-permute-start(bf16[64,2048]{1,0:T(8,128)(2,1)S(1)} %fusion.1), channel_id=1, source_target_pairs={{0,6},{1,7},{2,4},{3,5},{4,2},{5,3},{6,0},{7,1},{8,14},{9,15},{10,... | collective-permute-start | bytes 786440 | tf_op jit(solution)/shard_map/ppermute | solution.py:398
  (52 other events, 685.7 us)

commit v6 on v5

--- a/solution.py
+++ b/solution.py
@@ -137,8 +137,7 @@
     )(page_req, page_slot, *blocks, *far, row_req, row_pos)
 
 
-def project_kernel(mine, mine_level, theirs, their_level, proj, stay, *gos):
-    place = 3 - pl.program_id(0)
+def project_kernel(mine, mine_level, theirs, their_level, proj, stay, go):
     parts = []
     for head in range(mine.shape[0] // HEAD_DIM):
         dims = slice(head * HEAD_DIM, (head + 1) * HEAD_DIM)
@@ -152,36 +151,38 @@
     mixed = lax.dot_general(
         attention, proj[...], (((0,), (0,)), ((), ())), preferred_element_type=jnp.float32
     )
-    rows = stay.shape[0]
-    stay[...] = mixed[:rows, :]
-    for i, go in enumerate(gos):
-        @pl.when(place == i)
-        def _(go=go):
-            go[...] = mixed[rows:, :].astype(jnp.bfloat16)
-
-
-def project(mine, mine_level, theirs, their_level, proj, tok_rows):
+    rows = stay.shape[1]
+    stay[0] = mixed[:rows, :]
+    go[0] = mixed[rows:, :].astype(jnp.bfloat16)
+
+
+def project(pair, mine, mine_level, theirs, their_level, proj, tok_rows):
     columns, width = proj.shape
     heads = columns // HEAD_DIM
     size = mine.shape[1] // 4
+    here, there = 2 * pair, 2 * (1 - pair)
     return pl.pallas_call(
         project_kernel,
-        out_shape=[jax.ShapeDtypeStruct((4 * tok_rows, width), jnp.float32)]
-        + [jax.ShapeDtypeStruct((size - tok_rows, width), jnp.bfloat16)] * 4,
-        grid=(4,),
+        out_shape=[
+            jax.ShapeDtypeStruct((2, tok_rows, width), jnp.float32),
+            jax.ShapeDtypeStruct((2, size - tok_rows, width), jnp.bfloat16),
+        ],
+        grid=(2,),
         in_specs=[
-            pl.BlockSpec((columns, size), lambda i: (0, 3 - i)),
-            pl.BlockSpec((heads, 1, size), lambda i: (0, 0, 3 - i)),
-            pl.BlockSpec((columns, size), lambda i: (0, (5 - i) % 4)),
-            pl.BlockSpec((heads, 1, size), lambda i: (0, 0, (5 - i) % 4)),
+            pl.BlockSpec((columns, size), lambda i: (0, here + i)),
+            pl.BlockSpec((heads, 1, size), lambda i: (0, 0, here + i)),
+            pl.BlockSpec((columns, size), lambda i: (0, there + i)),
+            pl.BlockSpec((heads, 1, size), lambda i: (0, 0, there + i)),
             pl.BlockSpec((columns, width), lambda i: (0, 0)),
         ],
-        out_specs=[pl.BlockSpec((tok_rows, width), lambda i: (3 - i, 0))]
-        + [pl.BlockSpec((size - tok_rows, width), lambda i: (0, 0))] * 4,
+        out_specs=[
+            pl.BlockSpec((1, tok_rows, width), lambda i: (i, 0, 0)),
+            pl.BlockSpec((1, size - tok_rows, width), lambda i: (i, 0, 0)),
+        ],
         cost_estimate=pl.CostEstimate(
-            flops=8 * size * columns * width,
-            bytes_accessed=2 * (8 * columns * size + columns * width + 4 * size * width),
-            transcendentals=8 * size * heads,
+            flops=4 * size * columns * width,
+            bytes_accessed=2 * (4 * columns * size + columns * width + 2 * size * width),
+            transcendentals=4 * size * heads,
         ),
     )(mine, mine_level, theirs, their_level, proj)
 
@@ -257,12 +258,19 @@
     )(rows, scalar.reshape(1, -1), gate_w, up_w, down_w)
 
 
-def routed_kernel(count, entries, has_extra, *refs):
-    chunks, refs = refs[:count], refs[count:]
+def routed_kernel(parts, entries, has_extra, *refs):
+    count, total = len(parts), sum(parts)
+    pieces, refs = refs[:total], refs[total:]
     place, row_gate, extra, gate_w, up_w, down_w = refs[:6]
     outs, refs = refs[6 : 6 + count], refs[6 + count :]
     rows, packed, gate_v, up_v, down_v, extra_v, sems = refs
-    moves = [(chunks[c], rows.at[c]) for c in range(count)]
+    moves, chunk_copies = [], []
+    for c, n in enumerate(parts):
+        at = 0
+        chunk_copies.append(range(len(moves), len(moves) + n))
+        for piece in pieces[sum(parts[:c]) : sum(parts[: c + 1])]:
+            moves.append((piece, rows.at[c, pl.ds(at, piece.shape[0])]))
+            at += piece.shape[0]
     moves += [(gate_w.at[0], gate_v), (up_w.at[0], up_v), (down_w.at[0], down_v)]
     if has_extra:
         moves.append((extra, extra_v))
@@ -271,28 +279,29 @@
     ]
     for copy in copies:
         copy.start()
-    size = chunks[0].shape[0]
+    size = rows.shape[1]
     wanted = lax.broadcasted_iota(jnp.int32, (entries, size), 0)
     picks, weights = [], []
     for c in range(count):
         pick = jnp.where(place[c] == wanted, 1.0, 0.0)
         picks.append(pick.astype(jnp.bfloat16))
         weights.append(jnp.sum(pick * row_gate[c], axis=1, keepdims=True))
-        copies[c].wait()
+        for i in chunk_copies[c]:
+            copies[i].wait()
         packed[c * entries : (c + 1) * entries, :] = jnp.dot(
             picks[c], rows[c], preferred_element_type=jnp.float32
         ).astype(jnp.bfloat16)
-    copies[count].wait()
+    copies[total].wait()
     gate = jnp.dot(packed[...], gate_v[...], preferred_element_type=jnp.float32)
-    copies[count + 1].wait()
+    copies[total + 1].wait()
     upper = jnp.dot(packed[...], up_v[...], preferred_element_type=jnp.float32)
     hidden = (silu(gate) * upper).astype(jnp.bfloat16)
-    copies[count + 2].wait()
+    copies[total + 2].wait()
     answer = jnp.dot(hidden, down_v[...], preferred_element_type=jnp.float32).astype(
         jnp.bfloat16
     )
     if has_extra:
-        copies[count + 3].wait()
+        copies[total + 3].wait()
     for c in range(count):
         scaled = answer[c * entries : (c + 1) * entries, :].astype(jnp.float32) * weights[c]
         placed = lax.dot_general(
@@ -308,7 +317,10 @@
 
 def routed_expert(chunks, place, row_gate, extra, gate_w, up_w, down_w, entries):
     count = len(chunks)
-    size, width = chunks[0].shape
+    parts = [len(chunk) for chunk in chunks]
+    total = sum(parts)
+    size = sum(piece.shape[0] for piece in chunks[0])
+    width = chunks[0][0].shape[1]
     hidden = gate_w.shape[2]
     any_spec = pl.BlockSpec(memory_space=pl.ANY)
     vmem = pl.BlockSpec(memory_space=pltpu.VMEM)
@@ -316,9 +328,9 @@
     if not has_extra:
         extra = jnp.zeros((16, 128), jnp.bfloat16)
     return pl.pallas_call(
-        functools.partial(routed_kernel, count, entries, has_extra),
+        functools.partial(routed_kernel, parts, entries, has_extra),
         out_shape=[jax.ShapeDtypeStruct((size, width), jnp.bfloat16)] * count,
-        in_specs=[any_spec] * count + [vmem] * 2 + [any_spec] * 4,
+        in_specs=[any_spec] * total + [vmem] * 2 + [any_spec] * 4,
         out_specs=[vmem] * count,
         scratch_shapes=[
             pltpu.VMEM((count, size, width), jnp.bfloat16),
@@ -327,7 +339,7 @@
             pltpu.VMEM((width, hidden), jnp.bfloat16),
             pltpu.VMEM((hidden, width), jnp.bfloat16),
             pltpu.VMEM(extra.shape, jnp.bfloat16),
-            pltpu.SemaphoreType.DMA((count + 4,)),
+            pltpu.SemaphoreType.DMA((total + 4,)),
         ],
         compiler_params=pltpu.CompilerParams(vmem_limit_bytes=56 * 1024 * 1024),
         cost_estimate=pl.CostEstimate(
@@ -335,7 +347,7 @@
             bytes_accessed=6 * gate_w.size + 4 * count * size * width,
             transcendentals=count * entries * hidden,
         ),
-    )(*chunks, place, row_gate, extra, gate_w, up_w, down_w)
+    )(*[piece for chunk in chunks for piece in chunk], place, row_gate, extra, gate_w, up_w, down_w)
 
 
 def rms_normed(stream, norm_gain):
@@ -442,6 +454,10 @@
     page_request = jnp.sum(hits * jnp.arange(req_slots, dtype=i32)[None, :, None], axis=(1, 2))
     page_slot = jnp.sum(hits * jnp.arange(max_pages, dtype=i32)[None, None, :], axis=(1, 2))
     rel_rows = lambda a: a.reshape(exp_count, tok_rows)[rel_exp].reshape(1, -1)
+    gates = [block[2 * tokens + tok_rows :, :tok_rows].astype(f32) for block in blocks]
+    gates = jnp.stack([g[:TOPK] + g[TOPK : 2 * TOPK] + g[2 * TOPK : 3 * TOPK] for g in gates])
+    gates = gates.reshape(2, nx, TOPK, tok_rows)
+    gates = jnp.stack([send(gates, dh, 0, 0) for dh in range(2)])
     partial, level = attend(
         blocks,
         far,
@@ -452,8 +468,11 @@
         page_len,
         tokens,
     )
+    partial, level, gates = lax.optimization_barrier((partial, level, gates))
+    gates = jnp.stack([send_req(gates, dy, 0) for dy in range(ny)])
     other = send(partial[columns:], 1, 0, 0)
     other_level = send(level[columns // HEAD_DIM :], 1, 0, 0)
+    other, other_level, gates = lax.optimization_barrier((other, other_level, gates))
 
     slot_ids = jnp.arange(slot_count, dtype=i32)
     own_mark = slot_ids == own_slot
@@ -461,11 +480,6 @@
     twins = slot_expert == own_expert
     copies = jnp.sum(twins.astype(i32))
     own_rank = jnp.sum((twins & (slot_ids < own_slot)).astype(i32))
-    gates = [block[2 * tokens + tok_rows :, :tok_rows].astype(f32) for block in blocks]
-    gates = jnp.stack([g[:TOPK] + g[TOPK : 2 * TOPK] + g[2 * TOPK : 3 * TOPK] for g in gates])
-    gates = gates.reshape(2, nx, TOPK, tok_rows)
-    gates = jnp.stack([send(gates, dh, 0, 0) for dh in range(2)])
-    gates = jnp.stack([send_req(gates, dy, 0) for dy in range(ny)])
     gates = jnp.stack([send_req(gates, 0, dc) for dc in range(nc)], axis=1)
     gates = jnp.transpose(gates, (0, 1, 4, 2, 3, 5, 6)).reshape(slot_count, TOPK, tok_rows)
     rel_exp = jnp.transpose(rel_exp.reshape(len(zs), nx)).reshape(-1)
@@ -484,25 +498,30 @@
     tie = lax.optimization_barrier
     last = len(zs) - 1
 
-    stay, *goes = project(partial, level, other, other_level, out_proj, tok_rows)
-    stay = stay.reshape(len(zs), tok_rows, width)
-    comes = [
-        [send(go[(dx - 1) * tok_rows : dx * tok_rows], 0, 0, -dx) for dx in range(1, nx)]
-        for go in goes
-    ]
-    lines = {}
-    for i in reversed(range(len(zs))):
-        line = stay[i]
-        for come in comes[i]:
+    tie = lax.optimization_barrier
+
+    stays, comes = {}, {}
+    mine = partial
+    for pair in (1, 0):
+        stays[pair], go = project(pair, mine, level, other, other_level, out_proj, tok_rows)
+        mine, _ = tie((partial, go))
+        go = go.reshape(2, nx - 1, tok_rows, width)
+        comes[pair] = [send(go[:, dx - 1], 0, 0, -dx) for dx in range(1, nx)]
+    stream = resid.astype(f32)
+    arrived = []
+    for pair in (1, 0):
+        line = stays[pair]
+        for come in comes[pair]:
             line = line + come.astype(f32)
-        if i:
-            line = line.astype(bf16)
-            comes[i - 1], line = tie((comes[i - 1], line))
-            line = send(line, *zs[i], 0)
-        lines[i] = line
-    stream = resid.astype(f32) + lines[0]
-    for i in range(1, len(zs)):
-        stream = stream + lines[i].astype(f32)
+        for i in (1, 0):
+            if pair or i:
+                go = line[i].astype(bf16)
+                comes[0], _ = tie((comes[0], go))
+                arrived.append(send(go, *zs[2 * pair + i], 0))
+            else:
+                stream = stream + line[0]
+    for come in arrived:
+        stream = stream + come.astype(f32)
     normed = rms_normed(stream, norm_gain)
     normed, place, row_gate = tie((normed, place, row_gate))
 
@@ -515,26 +534,23 @@
         for dy in range(1, ny):
             piece[i, 0, dy] = send_req(line[i], dy, 0)
     piece = tie(piece)
+    chunk = join([piece[i, dx, 0] for dx in range(nx) for i in range(len(zs))])
+    chunks = {(0, 0): [chunk]}
+    for dc in range(1, nc):
+        chunks[0, dc] = [send_req(chunk, 0, dc)]
     for dy in range(1, ny):
-        for dx in range(1, nx):
-            for i in range(len(zs)):
-                piece[i, dx, dy] = send(piece[i, 0, dy], 0, 0, dx)
-
-    chunk_of = lambda dy: join([piece[i, dx, dy] for dx in range(nx) for i in range(len(zs))])
-    partners_of = lambda chunk: [send_req(chunk, 0, dc) for dc in range(1, nc)]
-    chunk = chunk_of(0)
-    partners = partners_of(chunk)
+        half = join([piece[i, 0, dy] for i in range(len(zs))])
+        chunks[dy, 0] = [send(half, 0, 0, dx) for dx in range(nx)]
     extra = shared_expert(chunk, shared_scalar, shared_gate.T, shared_up.T, shared_down)
-    if ny > 1:
-        half = [(i, dx, 1) for dx in range(1, nx) for i in range(len(zs) // 2)]
-        extra, partners, *arrived = tie((extra, partners, *[piece[n] for n in half]))
-        for name, value in zip(half, arrived):
-            piece[name] = value
-
-    sums = {}
+    partners = [chunks[0, dc] for dc in range(1, nc)]
+    extra, partners = tie((extra, partners))
+    for dc in range(1, nc):
+        chunks[0, dc] = partners[dc - 1]
+
+    kept, comes = {}, {}
     for dy in range(ny):
         answers = routed_expert(
-            [chunk] + partners,
+            [chunks[dy, dc] for dc in range(nc)],
             place[dy],
             row_gate[dy],
             extra,
@@ -544,58 +560,54 @@
             entries,
         )
         extra = None
-        answers, *rest = tie((answers, *[piece[i, dx, d] for i, dx, d in piece if d == dy + 1]))
-        for name, value in zip([n for n in piece if n[2] == dy + 1], rest):
-            piece[name] = value
+        if dy:
+            answers, comes[dy - 1][1] = tie((answers, comes[dy - 1][1]))
+        if dy + 1 < ny:
+            answers, chunks[dy + 1, 0] = tie((answers, chunks[dy + 1, 0]))
+            for dc in range(1, nc):
+                chunks[dy + 1, dc] = [send_req(part, 0, dc) for part in chunks[dy + 1, 0]]
         others = [send_req(answers[dc], 0, -dc) for dc in range(1, nc)]
+        parts = [answers[0]] + others
+        comes[dy] = {}
+        for pair in (1, 0):
+            gone = [
+                part.reshape(nx, 2, 2, tok_rows, width)[1:, pair].astype(f32) for part in parts
+            ]
+            gone = sum(gone[1:], gone[0]).astype(bf16)
+            comes[dy][pair] = [send(gone[dx - 1], 0, 0, -dx) for dx in range(1, nx)]
+            if pair:
+                parts, _ = tie((parts, gone))
         if dy + 1 < ny:
-            chunk = chunk_of(dy + 1)
-            chunk, others = tie((chunk, others))
-            partners = partners_of(chunk)
-        here = answers[0].astype(f32)
-        for come in others:
-            here = here + come.astype(f32)
-        here = here.reshape(nx, len(zs), tok_rows, width)
-        gone = here[1:].astype(bf16)
-        if dy + 1 < ny:
-            partners, gone = tie((partners, gone))
-            comes = [send(gone[dx - 1], 0, 0, -dx) for dx in range(1, nx)]
-            comes = [[come[i] for come in comes] for i in range(len(zs))]
-        else:
-            comes = [
-                [send(gone[dx - 1, i], 0, 0, -dx) for dx in range(1, nx)] for i in range(len(zs))
-            ]
-        sums[dy] = (here[0], comes)
-
-    lines = {}
-    for i in reversed(range(len(zs))):
-        total = {}
-        for dy in range(ny):
-            here, comes = sums[dy]
-            total[dy] = here[i]
-            for come in comes[i]:
-                total[dy] = total[dy] + come.astype(f32)
-        goes = [total[dy].astype(bf16) for dy in range(1, ny)]
-        if i:
-            comes = sums[ny - 1][1]
-            comes[i - 1], goes = tie((comes[i - 1], goes))
-        lines[i] = (total[0], [send_req(go, -dy, 0) for dy, go in enumerate(goes, 1)])
+            following = [chunks[dy + 1, dc] for dc in range(nc)]
+            following, _ = tie((following, gone))
+            for dc in range(nc):
+                chunks[dy + 1, dc] = following[dc]
+        elif dy:
+            parts, comes[dy - 1][0] = tie((parts, comes[dy - 1][0]))
+        kept[dy] = parts
+
+    def line_of(dy, pair):
+        line = [p.reshape(nx, 2, 2, tok_rows, width)[0, pair].astype(f32) for p in kept[dy]]
+        return sum([come.astype(f32) for come in comes[dy][pair]], sum(line[1:], line[0]))
+
     home = stream
-    arrived = {}
-    for i in reversed(range(len(zs))):
-        total, comes = lines[i]
-        for come in comes:
-            total = total + come.astype(f32)
-        if i:
-            total = total.astype(bf16)
-            here, comes = lines[i - 1]
-            comes, total = tie((comes, total))
-            lines[i - 1] = (here, comes)
-            arrived[i] = send(total, *zs[i], 0)
-        else:
-            home = home + total
-    for i in range(1, len(zs)):
-        home = home + arrived[i].astype(f32)
+    over_y, arrived = {}, []
+    for pair in (1, 0):
+        goes = [line_of(dy, pair).astype(bf16) for dy in range(1, ny)]
+        over_y[pair] = [send_req(go, -dy, 0) for dy, go in enumerate(goes, 1)]
+        if pair:
+            comes[ny - 1][0], _ = tie((comes[ny - 1][0], goes))
+    for pair in (1, 0):
+        total = sum([come.astype(f32) for come in over_y[pair]], line_of(0, pair))
+        for i in (1, 0):
+            if pair or i:
+                go = total[i].astype(bf16)
+                over_y[0], _ = tie((over_y[0], go))
+                arrived.append(send(go, *zs[2 * pair + i], 0))
+            else:
+                home = home + total[0]
+    for come in arrived:
+        home = home + come.astype(f32)
     total = home
     return total.astype(bf16)
 

time: 331 us -> 283 us (0.85)
  waiting for transfers between devices: 172 us -> 133 us
  other arithmetic: 16.6 us -> 11.1 us
    ppermute x36 -> x30, waiting for transfers between devices: 135 us -> 108 us  [send(): return lax.ppermute(value, 'exp', pairs)]
    ppermute x14 -> x13, waiting for transfers between devices: 37.3 us -> 24.8 us  [send_req(): return lax.ppermute(value, 'req', pairs)]
    add x2, other arithmetic: 4.68 us -> 0.42 us  [the longest x1 0.31 us: shards(): total = sum([come.astype(f32) for come in over_y[pair]], line_of(0, pair))]
    unnamed x68 -> x74, local copies, waits for them, and re-layouts: 10.6 us -> 7.5 us
    ppermute x36 -> x30, starting transfers between devices: 52 us -> 49.2 us  [send(): return lax.ppermute(value, 'exp', pairs)]
    ppermute x14 -> x13, starting transfers between devices: 8.14 us -> 10.1 us  [send_req(): return lax.ppermute(value, 'req', pairs)]
    pallas_call x3 -> x4, Pallas kernels: 35.5 us -> 36.9 us  [the longest x2 30.8 us: routed_expert(): pl.pallas_call(functools.partial(routed_kernel, parts, entries, has_extra...]
  transfers between devices with their start and end apart: 50 -> 43, of which waited for: 22 -> 22; matrix products, arithmetic and copies ran while one was open for 5% -> 5% of each run, Pallas kernels for 11% -> 20%
where the time goes in v6:
time: 283 us; the launch traced here: 281 us
  waiting for transfers between devices  133 us (47%)
  Pallas kernels  62.1 us (22%)
  starting transfers between devices  59.3 us (21%)
  local copies, waits for them, and re-layouts  13.8 us (5%)
  other arithmetic  11.1 us (4%)
    ppermute x30, waiting for transfers between devices, send(): return lax.ppermute(value, 'exp', pairs)  108 us
    ppermute x30, starting transfers between devices, send(): return lax.ppermute(value, 'exp', pairs)  49.2 us
    pallas_call x2, Pallas kernels, routed_expert(): pl.pallas_call(functools.partial(routed_kernel, parts, entries, has_extra...  30.8 us
    ppermute x13, waiting for transfers between devices, send_req(): return lax.ppermute(value, 'req', pairs)  24.8 us
    ppermute x13, starting transfers between devices, send_req(): return lax.ppermute(value, 'req', pairs)  10.1 us
    pallas_call x1, Pallas kernels, shared_expert(): pl.pallas_call(shared_kernel, out_shape=jax.ShapeDtypeStruct(rows.shape,...  8.74 us
    pallas_call x1, Pallas kernels, attend(): pl.pallas_call(functools.partial(attend_kernel, members, tokens, page_len...  7.82 us
    unnamed x74, local copies, waits for them, and re-layouts  7.5 us
  transfers between devices with their start and end apart: 43, of which 22 were waited for; matrix products, arithmetic and copies ran while one was open for 5% of the time, Pallas kernels for 20%

profile of v6, /device:TPU:0, one launch (start us, length us, event | category | flops | bytes accessed | tf_op | source)
XLA Modules:
  0.0 281.4 jit_solution(14235600435106400543)
XLA Ops:
  0.0 4.0 %collective-permute-start.3 = (bf16[64,2048]{1,0:T(8,128)(2,1)}, bf16[64,2048]{1,0:T(8,128)(2,1)S(1)}, u32[]{:S(2)}, u32[]{:S(2)}) collective-permute-start(bf16[64,2048]{1,0:T(8,128)(2,1)} %refs_11_.1), channel_id=1, source_target_pairs={{0,4},{1,5},{2,6},{3,7},{4,0},{5,1},{6,2},{7,3},{8,12},{9,13},{10,... | collective-permute-start | bytes 786440 | tf_op jit(solution)/shard_map/ppermute | solution.py:410
  8.2 2.6 shard_map.181
  25.4 17.8 %collective-permute-done.2.refs_3_ = bf16[592,512]{1,0:T(8,128)(2,1)S(1)} collective-permute-done((bf16[592,512]{1,0:T(8,128)(2,1)}, bf16[592,512]{1,0:T(8,128)(2,1)S(1)}, u32[]{:S(2)}, u32[]{:S(2)}) %collective-permute-start.2) | collective-permute-done | bytes 606240 | tf_op jit(solution)/shard_map/ppermute | solution.py:410
  43.7 3.7 %collective-permute-start.7 = (f32[2,2,4,64]{3,0,1,2:T(2,128)S(1)}, f32[2,2,4,64]{3,0,1,2:T(2,128)S(1)}, u32[]{:S(2)}, u32[]{:S(2)}) collective-permute-start(f32[2,2,4,64]{3,0,1,2:T(2,128)S(1)} %copy.34), channel_id=1, source_target_pairs={{0,4},{1,5},{2,6},{3,7},{4,0},{5,1},{6,2},{7,3},{8,12},{9,13},{10,... | collective-permute-start | bytes 12296 | tf_op jit(solution)/shard_map/ppermute | solution.py:410
  48.4 7.8 %shard_map.183 = (bf16[512,512]{1,0:T(8,128)(2,1)S(1)}, f32[4,1,512]{2,1,0:T(1,128)S(1)}) custom-call(s32[8]{0:T(128)S(1)} %get-tuple-element.136.page_req, s32[8]{0:T(128)S(1)} %get-tuple-element.135.page_slot, bf16[592,512]{1,0:T(8,128)(2,1)S(1)} %get-tuple-element.70.refs_0_, bf16[592,512]{1,0:T(8,128)(2,1)S(1)} %collective-permute-done.refs_1_, ...), custom_call_target="tpu_custom_call" | custom-call | flops 1073741824 | bytes 2686976 | tf_op jit(solution)/shard_map/pallas_call | solution.py:116
  62.2 7.8 %collective-permute-done.9.their_level = f32[2,1,512]{2,1,0:T(1,128)S(1)} collective-permute-done((f32[2,1,512]{2,1,0:T(1,128)S(1)}, f32[2,1,512]{2,1,0:T(1,128)S(1)}, u32[]{:S(2)}, u32[]{:S(2)}) %collective-permute-start.9) | collective-permute-done | bytes 4128 | tf_op jit(solution)/shard_map/ppermute | solution.py:410
  71.3 3.0 %shard_map.184 = (f32[2,64,2048]{2,1,0:T(8,128)}, bf16[2,64,2048]{2,1,0:T(8,128)(2,1)}) custom-call(bf16[512,512]{1,0:T(8,128)(2,1)} %copy-done.3, f32[4,1,512]{2,1,0:T(1,128)} %copy-done.5, bf16[256,512]{1,0:T(8,128)(2,1)} %copy-done.9, f32[2,1,512]{2,1,0:T(1,128)} %copy-done.27, bf16[256,2048]{1,0:T(8,128)(2,1)} %proj.3), custom_call_target="tpu_custom_call" | custom-call | flops 268435456 | bytes 2359296 | tf_op jit(solution)/shard_map/pallas_call | solution.py:164
  77.4 3.0 %shard_map.185 = (f32[2,64,2048]{2,1,0:T(8,128)}, bf16[2,64,2048]{2,1,0:T(8,128)(2,1)}) custom-call(bf16[512,512]{1,0:T(8,128)(2,1)} %copy-done.3, f32[4,1,512]{2,1,0:T(1,128)} %copy-done.5, bf16[256,512]{1,0:T(8,128)(2,1)} %copy-done.9, f32[2,1,512]{2,1,0:T(1,128)} %copy-done.27, bf16[256,2048]{1,0:T(8,128)(2,1)} %proj.3), custom_call_target="tpu_custom_call" | custom-call | flops 268435456 | bytes 2359296 | tf_op jit(solution)/shard_map/pallas_call | solution.py:164
  81.4 8.1 %collective-permute-done.12 = bf16[2,64,2048]{2,1,0:T(8,128)(2,1)S(1)} collective-permute-done((bf16[2,64,2048]{2,1,0:T(8,128)(2,1)}, bf16[2,64,2048]{2,1,0:T(8,128)(2,1)S(1)}, u32[]{:S(2)}, u32[]{:S(2)}) %collective-permute-start.12) | collective-permute-done | bytes 524320 | tf_op jit(solution)/shard_map/ppermute | solution.py:410
  89.7 2.3 collective-permute-start.13
  91.9 6.8 %collective-permute-done.11 = bf16[2,64,2048]{2,1,0:T(8,128)(2,1)S(1)} collective-permute-done((bf16[2,64,2048]{2,1,0:T(8,128)(2,1)}, bf16[2,64,2048]{2,1,0:T(8,128)(2,1)S(1)}, u32[]{:S(2)}, u32[]{:S(2)}) %collective-permute-start.11) | collective-permute-done | bytes 524320 | tf_op jit(solution)/shard_map/ppermute | solution.py:410
  98.9 3.9 %collective-permute-start.15 = (bf16[64,2048]{1,0:T(8,128)(2,1)S(1)}, bf16[64,2048]{1,0:T(8,128)(2,1)S(1)}, u32[]{:S(2)}, u32[]{:S(2)}) collective-permute-start(bf16[64,2048]{1,0:T(8,128)(2,1)S(1)} %fusion.18), channel_id=1, source_target_pairs={{0,2},{1,3},{2,0},{3,1},{4,6},{5,7},{6,4},{7,5},{8,10},{9,11},{10,... | collective-permute-start | bytes 786440 | tf_op jit(solution)/shard_map/ppermute | solution.py:410
  103.0 9.2 %collective-permute-done.15 = bf16[64,2048]{1,0:T(8,128)(2,1)S(1)} collective-permute-done((bf16[64,2048]{1,0:T(8,128)(2,1)S(1)}, bf16[64,2048]{1,0:T(8,128)(2,1)S(1)}, u32[]{:S(2)}, u32[]{:S(2)}) %collective-permute-start.15) | collective-permute-done | bytes 262176 | tf_op jit(solution)/shard_map/ppermute | solution.py:410
  114.3 3.5 %collective-permute-start.22 = (bf16[64,2048]{1,0:T(8,128)(2,1)S(1)}, bf16[64,2048]{1,0:T(8,128)(2,1)S(1)}, u32[]{:S(2)}, u32[]{:S(2)}) collective-permute-start(bf16[64,2048]{1,0:T(8,128)(2,1)S(1)} %multiply_convert_fusion.refs_0_), channel_id=1, source_target_pairs={{0,4},{1,5},{2,6},{3,7},{4,0},{5,1},{6,2},{7,3},{8,12},{9,13},{10,... | collective-permute-start | bytes 786440 | tf_op jit(solution)/shard_map/ppermute | solution.py:410
  124.6 3.3 %collective-permute-start.21 = (bf16[64,2048]{1,0:T(8,128)(2,1)S(1)}, bf16[64,2048]{1,0:T(8,128)(2,1)S(1)}, u32[]{:S(2)}, u32[]{:S(2)}) collective-permute-start(bf16[64,2048]{1,0:T(8,128)(2,1)S(1)} %collective-permute-done.19.refs_1_), channel_id=1, source_target_pairs={{0,1},{1,0},{2,3},{3,2},{4,5},{5,4},{6,7},{7,6},{8,9},{9,8},{10,11... | collective-permute-start | bytes 786440 | tf_op jit(solution)/shard_map/ppermute | solution.py:410
  127.9 7.7 %collective-permute-done.22.refs_2_ = bf16[64,2048]{1,0:T(8,128)(2,1)S(1)} collective-permute-done((bf16[64,2048]{1,0:T(8,128)(2,1)S(1)}, bf16[64,2048]{1,0:T(8,128)(2,1)S(1)}, u32[]{:S(2)}, u32[]{:S(2)}) %collective-permute-start.22) | collective-permute-done | bytes 262176 | tf_op jit(solution)/shard_map/ppermute | solution.py:410
  139.7 2.3 collective-permute-done.23.refs_2_
  146.8 3.0 %shard_map.186.rows.refs_0_ = bf16[512,2048]{1,0:T(8,128)(2,1)} custom-call(bf16[64,2048]{1,0:T(8,128)(2,1)} %copy-done.13, bf16[64,2048]{1,0:T(8,128)(2,1)} %copy-done.15, bf16[64,2048]{1,0:T(8,128)(2,1)} %copy-done.16, bf16[64,2048]{1,0:T(8,128)(2,1)} %copy-done.18, bf16[64,2048]{1,0:T(8,128)(2,1)} %copy-done.17, bf16[64,2048]{1,0:T(8,128)(2,1)} %copy-done.19, ...), custom_call_target="tpu_custom_call" | custom-call | bytes 4194304 | tf_op jit(solution)/shard_map/pallas_call | solution.py:200
  151.0 2.2 shard_map.189.refs_0_
  153.2 2.3 collective-permute-start.29
  155.6 8.7 %shard_map.187.refs_4_ = bf16[512,2048]{1,0:T(8,128)(2,1)S(1)} custom-call(bf16[512,2048]{1,0:T(8,128)(2,1)S(1)} %copy-done.4, bf16[1,2048]{1,0:T(2,128)(2,1)S(1)} %reshape.642.scalar, bf16[704,2048]{1,0:T(8,128)(2,1)} %bitcast.182, bf16[704,2048]{1,0:T(8,128)(2,1)} %bitcast.183, bf16[704,2048]{1,0:T(8,128)(2,1)} %down_w.1), custom_call_target="tpu_custom_call" | custom-call | flops 4429185024 | bytes 12845056 | tf_op jit(solution)/shard_map/pallas_call | solution.py:241
  165.6 15.6 %shard_map.188 = (bf16[512,2048]{1,0:T(8,128)(2,1)}, bf16[512,2048]{1,0:T(8,128)(2,1)}) custom-call(bf16[512,2048]{1,0:T(8,128)(2,1)} %shard_map.186.rows.refs_0_, bf16[512,2048]{1,0:T(8,128)(2,1)} %collective-permute-done.28.refs_1_, s32[2,1,512]{2,1,0:T(1,128)} %get-tuple-element.148.refs_2_, f32[2,1,512]{2,1,0:T(1,128)} %get-tuple-element.146.refs_3_, ...), custom_call_target="tpu_custom_call" | custom-call | flops 8254390272 | bytes 25690112 | tf_op jit(solution)/shard_map/pallas_call | solution.py:330
  182.1 4.9 %collective-permute-done.31.refs_2_ = bf16[256,2048]{1,0:T(8,128)(2,1)S(1)} collective-permute-done((bf16[256,2048]{1,0:T(8,128)(2,1)S(1)}, bf16[256,2048]{1,0:T(8,128)(2,1)S(1)}, u32[]{:S(2)}, u32[]{:S(2)}) %collective-permute-start.31) | collective-permute-done | bytes 1048608 | tf_op jit(solution)/shard_map/ppermute | solution.py:420
  190.9 15.2 %shard_map.190 = (bf16[512,2048]{1,0:T(8,128)(2,1)}, bf16[512,2048]{1,0:T(8,128)(2,1)}) custom-call(bf16[256,2048]{1,0:T(8,128)(2,1)} %shard_map.189.refs_0_, bf16[256,2048]{1,0:T(8,128)(2,1)} %copy-done.34, bf16[256,2048]{1,0:T(8,128)(2,1)} %copy-done.35, bf16[256,2048]{1,0:T(8,128)(2,1)} %copy-done.36, s32[2,1,512]{2,1,0:T(1,128)} %get-tuple-element.147.refs_4_, ...), custom_call_target="tpu_custom_call" | custom-call | flops 8254390272 | bytes 25690112 | tf_op jit(solution)/shard_map/pallas_call | solution.py:330
  208.3 2.3 collective-permute-done.34
  214.0 7.2 %collective-permute-done.35 = bf16[2,64,2048]{2,1,0:T(8,128)(2,1)S(1)} collective-permute-done((bf16[2,64,2048]{2,1,0:T(8,128)(2,1)S(1)}, bf16[2,64,2048]{2,1,0:T(8,128)(2,1)S(1)}, u32[]{:S(2)}, u32[]{:S(2)}) %collective-permute-start.35) | collective-permute-done | bytes 524320 | tf_op jit(solution)/shard_map/ppermute | solution.py:410
  221.2 11.2 %collective-permute-done.37 = bf16[2,64,2048]{2,1,0:T(8,128)(2,1)S(1)} collective-permute-done((bf16[2,64,2048]{2,1,0:T(8,128)(2,1)S(1)}, bf16[2,64,2048]{2,1,0:T(8,128)(2,1)S(1)}, u32[]{:S(2)}, u32[]{:S(2)}) %collective-permute-start.37) | collective-permute-done | bytes 524320 | tf_op jit(solution)/shard_map/ppermute | solution.py:410
  233.9 9.5 %collective-permute-done.36 = bf16[2,64,2048]{2,1,0:T(8,128)(2,1)S(1)} collective-permute-done((bf16[2,64,2048]{2,1,0:T(8,128)(2,1)S(1)}, bf16[2,64,2048]{2,1,0:T(8,128)(2,1)S(1)}, u32[]{:S(2)}, u32[]{:S(2)}) %collective-permute-start.36) | collective-permute-done | bytes 524320 | tf_op jit(solution)/shard_map/ppermute | solution.py:410
  246.4 10.9 %collective-permute-done.38 = bf16[2,64,2048]{2,1,0:T(8,128)(2,1)S(1)} collective-permute-done((bf16[2,64,2048]{2,1,0:T(8,128)(2,1)S(1)}, bf16[2,64,2048]{2,1,0:T(8,128)(2,1)S(1)}, u32[]{:S(2)}, u32[]{:S(2)}) %collective-permute-start.38) | collective-permute-done | bytes 524320 | tf_op jit(solution)/shard_map/ppermute | solution.py:420
  260.0 2.0 collective-permute-start.40
  262.0 6.6 %collective-permute-done.42 = bf16[64,2048]{1,0:T(8,128)(2,1)S(1)} collective-permute-done((bf16[64,2048]{1,0:T(8,128)(2,1)S(1)}, bf16[64,2048]{1,0:T(8,128)(2,1)S(1)}, u32[]{:S(2)}, u32[]{:S(2)}) %collective-permute-start.42) | collective-permute-done | bytes 262176 | tf_op jit(solution)/shard_map/ppermute | solution.py:410
  268.6 11.9 %collective-permute-done.41 = bf16[64,2048]{1,0:T(8,128)(2,1)S(1)} collective-permute-done((bf16[64,2048]{1,0:T(8,128)(2,1)S(1)}, bf16[64,2048]{1,0:T(8,128)(2,1)S(1)}, u32[]{:S(2)}, u32[]{:S(2)}) %collective-permute-start.41) | collective-permute-done | bytes 262176 | tf_op jit(solution)/shard_map/ppermute | solution.py:410
  (222 shorter events, 69.0 us)
Async XLA Ops:
  0.0 21.4 %collective-permute-start.3 = (bf16[64,2048]{1,0:T(8,128)(2,1)}, bf16[64,2048]{1,0:T(8,128)(2,1)S(1)}, u32[]{:S(2)}, u32[]{:S(2)}) collective-permute-start(bf16[64,2048]{1,0:T(8,128)(2,1)} %refs_11_.1), channel_id=1, source_target_pairs={{0,4},{1,5},{2,6},{3,7},{4,0},{5,1},{6,2},{7,3},{8,12},{9,13},{10,... | collective-permute-start | bytes 786440 | tf_op jit(solution)/shard_map/ppermute | solution.py:410
  10.8 32.8 %collective-permute-start = (bf16[592,512]{1,0:T(8,128)(2,1)}, bf16[592,512]{1,0:T(8,128)(2,1)S(1)}, u32[]{:S(2)}, u32[]{:S(2)}) collective-permute-start(bf16[592,512]{1,0:T(8,128)(2,1)} %get-tuple-element.71), channel_id=1, source_target_pairs={{0,1},{1,0},{2,3},{3,2},{4,5},{5,4},{6,7},{7,6},{8,9},{9,8},{10,11... | collective-permute-start | bytes 1818632 | tf_op jit(solution)/shard_map/ppermute | solution.py:410
  12.3 31.3 %collective-permute-start.1 = (bf16[592,512]{1,0:T(8,128)(2,1)}, bf16[592,512]{1,0:T(8,128)(2,1)S(1)}, u32[]{:S(2)}, u32[]{:S(2)}) collective-permute-start(bf16[592,512]{1,0:T(8,128)(2,1)} %get-tuple-element.72), channel_id=1, source_target_pairs={{0,2},{1,3},{2,0},{3,1},{4,6},{5,7},{6,4},{7,5},{8,10},{9,11},{10,... | collective-permute-start | bytes 1818632 | tf_op jit(solution)/shard_map/ppermute | solution.py:410
  13.9 29.3 %collective-permute-start.2 = (bf16[592,512]{1,0:T(8,128)(2,1)}, bf16[592,512]{1,0:T(8,128)(2,1)S(1)}, u32[]{:S(2)}, u32[]{:S(2)}) collective-permute-start(bf16[592,512]{1,0:T(8,128)(2,1)} %get-tuple-element.73), channel_id=1, source_target_pairs={{0,3},{1,2},{2,1},{3,0},{4,7},{5,6},{6,5},{7,4},{8,11},{9,10},{10,... | collective-permute-start | bytes 1818632 | tf_op jit(solution)/shard_map/ppermute | solution.py:410
  22.2 25.2 %collective-permute-start.4 = (bf16[64,512]{1,0:T(8,128)(2,1)S(1)}, bf16[64,512]{1,0:T(8,128)(2,1)S(1)}, u32[]{:S(2)}, u32[]{:S(2)}) collective-permute-start(bf16[64,512]{1,0:T(8,128)(2,1)S(1)} %get-tuple-element.75), channel_id=1, source_target_pairs={{0,1},{1,0},{2,3},{3,2},{4,5},{5,4},{6,7},{7,6},{8,9},{9,8},{10,11... | collective-permute-start | bytes 196616 | tf_op jit(solution)/shard_map/ppermute | solution.py:410
  23.8 23.6 %collective-permute-start.5 = (bf16[64,512]{1,0:T(8,128)(2,1)S(1)}, bf16[64,512]{1,0:T(8,128)(2,1)S(1)}, u32[]{:S(2)}, u32[]{:S(2)}) collective-permute-start(bf16[64,512]{1,0:T(8,128)(2,1)S(1)} %get-tuple-element.76), channel_id=1, source_target_pairs={{0,2},{1,3},{2,0},{3,1},{4,6},{5,7},{6,4},{7,5},{8,10},{9,11},{10,... | collective-permute-start | bytes 196616 | tf_op jit(solution)/shard_map/ppermute | solution.py:410
  43.7 12.6 %collective-permute-start.7 = (f32[2,2,4,64]{3,0,1,2:T(2,128)S(1)}, f32[2,2,4,64]{3,0,1,2:T(2,128)S(1)}, u32[]{:S(2)}, u32[]{:S(2)}) collective-permute-start(f32[2,2,4,64]{3,0,1,2:T(2,128)S(1)} %copy.34), channel_id=1, source_target_pairs={{0,4},{1,5},{2,6},{3,7},{4,0},{5,1},{6,2},{7,3},{8,12},{9,13},{10,... | collective-permute-start | bytes 12296 | tf_op jit(solution)/shard_map/ppermute | solution.py:410
  56.3 13.7 %collective-permute-start.8 = (bf16[256,512]{1,0:T(8,128)(2,1)S(1)}, bf16[256,512]{1,0:T(8,128)(2,1)S(1)}, u32[]{:S(2)}, u32[]{:S(2)}) collective-permute-start(bf16[256,512]{1,0:T(8,128)(2,1)S(1)} %slice.168), channel_id=1, source_target_pairs={{0,4},{1,5},{2,6},{3,7},{4,0},{5,1},{6,2},{7,3},{8,12},{9,13},{10,... | collective-permute-start | bytes 786440 | tf_op jit(solution)/shard_map/ppermute | solution.py:410
  74.4 15.1 %collective-permute-start.12 = (bf16[2,64,2048]{2,1,0:T(8,128)(2,1)}, bf16[2,64,2048]{2,1,0:T(8,128)(2,1)S(1)}, u32[]{:S(2)}, u32[]{:S(2)}) collective-permute-start(bf16[2,64,2048]{2,1,0:T(8,128)(2,1)} %get-tuple-element.85), channel_id=1, source_target_pairs={{0,1},{1,0},{2,3},{3,2},{4,5},{5,4},{6,7},{7,6},{8,9},{9,8},{10,11... | collective-permute-start | bytes 1572872 | tf_op jit(solution)/shard_map/ppermute | solution.py:410
  80.4 18.3 %collective-permute-start.11 = (bf16[2,64,2048]{2,1,0:T(8,128)(2,1)}, bf16[2,64,2048]{2,1,0:T(8,128)(2,1)S(1)}, u32[]{:S(2)}, u32[]{:S(2)}) collective-permute-start(bf16[2,64,2048]{2,1,0:T(8,128)(2,1)} %get-tuple-element.88), channel_id=1, source_target_pairs={{0,1},{1,0},{2,3},{3,2},{4,5},{5,4},{6,7},{7,6},{8,9},{9,8},{10,11... | collective-permute-start | bytes 1572872 | tf_op jit(solution)/shard_map/ppermute | solution.py:410
  81.4 21.4 %collective-permute-start.16 = (f32[2,2,2,2,4,64]{5,2,1,3,0,4:T(2,128)S(1)}, f32[2,2,2,2,4,64]{5,2,1,3,0,4:T(2,128)S(1)}, u32[]{:S(2)}, u32[]{:S(2)}) collective-permute-start(f32[2,2,2,2,4,64]{5,2,1,3,0,4:T(2,128)S(1)} %pad_maximum_fusion.1), channel_id=1, source_target_pairs={{0,8},{8,0},{16,24},{24,16},{1,9},{9,1},{17,25},{25,17},{2,10},{10... | collective-permute-start | bytes 49160 | tf_op jit(solution)/shard_map/ppermute | solution.py:420
  89.7 22.6 %collective-permute-start.13 = (bf16[64,2048]{1,0:T(8,128)(2,1)S(1)}, bf16[64,2048]{1,0:T(8,128)(2,1)S(1)}, u32[]{:S(2)}, u32[]{:S(2)}) collective-permute-start(bf16[64,2048]{1,0:T(8,128)(2,1)S(1)} %get-tuple-element.144), channel_id=1, source_target_pairs={{0,6},{1,7},{2,4},{3,5},{4,2},{5,3},{6,0},{7,1},{8,14},{9,15},{10,... | collective-permute-start | bytes 786440 | tf_op jit(solution)/shard_map/ppermute | solution.py:410
  98.7 13.5 %collective-permute-start.14 = (bf16[64,2048]{1,0:T(8,128)(2,1)S(1)}, bf16[64,2048]{1,0:T(8,128)(2,1)S(1)}, u32[]{:S(2)}, u32[]{:S(2)}) collective-permute-start(bf16[64,2048]{1,0:T(8,128)(2,1)S(1)} %get-tuple-element.143), channel_id=1, source_target_pairs={{0,4},{1,5},{2,6},{3,7},{4,0},{5,1},{6,2},{7,3},{8,12},{9,13},{10,... | collective-permute-start | bytes 786440 | tf_op jit(solution)/shard_map/ppermute | solution.py:410
  98.9 13.3 %collective-permute-start.15 = (bf16[64,2048]{1,0:T(8,128)(2,1)S(1)}, bf16[64,2048]{1,0:T(8,128)(2,1)S(1)}, u32[]{:S(2)}, u32[]{:S(2)}) collective-permute-start(bf16[64,2048]{1,0:T(8,128)(2,1)S(1)} %fusion.18), channel_id=1, source_target_pairs={{0,2},{1,3},{2,0},{3,1},{4,6},{5,7},{6,4},{7,5},{8,10},{9,11},{10,... | collective-permute-start | bytes 786440 | tf_op jit(solution)/shard_map/ppermute | solution.py:410
  112.7 10.0 %collective-permute-start.19 = (bf16[64,2048]{1,0:T(8,128)(2,1)S(1)}, bf16[64,2048]{1,0:T(8,128)(2,1)S(1)}, u32[]{:S(2)}, u32[]{:S(2)}) collective-permute-start(bf16[64,2048]{1,0:T(8,128)(2,1)S(1)} %multiply_convert_fusion.refs_0_), channel_id=1, source_target_pairs={{0,2},{1,3},{2,0},{3,1},{4,6},{5,7},{6,4},{7,5},{8,10},{9,11},{10,... | collective-permute-start | bytes 786440 | tf_op jit(solution)/shard_map/ppermute | solution.py:410
  112.8 11.9 %collective-permute-start.17 = (bf16[64,2048]{1,0:T(8,128)(2,1)S(1)}, bf16[64,2048]{1,0:T(8,128)(2,1)S(1)}, u32[]{:S(2)}, u32[]{:S(2)}) collective-permute-start(bf16[64,2048]{1,0:T(8,128)(2,1)S(1)} %multiply_convert_fusion.refs_0_), channel_id=1, source_target_pairs={{0,16},{8,24},{16,0},{24,8},{1,17},{9,25},{17,1},{25,9},{2,18},{10... | collective-permute-start | bytes 786440 | tf_op jit(solution)/shard_map/ppermute | solution.py:420
  114.3 21.3 %collective-permute-start.22 = (bf16[64,2048]{1,0:T(8,128)(2,1)S(1)}, bf16[64,2048]{1,0:T(8,128)(2,1)S(1)}, u32[]{:S(2)}, u32[]{:S(2)}) collective-permute-start(bf16[64,2048]{1,0:T(8,128)(2,1)S(1)} %multiply_convert_fusion.refs_0_), channel_id=1, source_target_pairs={{0,4},{1,5},{2,6},{3,7},{4,0},{5,1},{6,2},{7,3},{8,12},{9,13},{10,... | collective-permute-start | bytes 786440 | tf_op jit(solution)/shard_map/ppermute | solution.py:410
  117.8 18.6 %collective-permute-start.18 = (bf16[64,2048]{1,0:T(8,128)(2,1)S(1)}, bf16[64,2048]{1,0:T(8,128)(2,1)S(1)}, u32[]{:S(2)}, u32[]{:S(2)}) collective-permute-start(bf16[64,2048]{1,0:T(8,128)(2,1)S(1)} %multiply_convert_fusion.refs_0_), channel_id=1, source_target_pairs={{0,1},{1,0},{2,3},{3,2},{4,5},{5,4},{6,7},{7,6},{8,9},{9,8},{10,11... | collective-permute-start | bytes 786440 | tf_op jit(solution)/shard_map/ppermute | solution.py:410
  119.3 19.0 %collective-permute-start.25 = (bf16[64,2048]{1,0:T(8,128)(2,1)S(1)}, bf16[64,2048]{1,0:T(8,128)(2,1)S(1)}, u32[]{:S(2)}, u32[]{:S(2)}) collective-permute-start(bf16[64,2048]{1,0:T(8,128)(2,1)S(1)} %multiply_convert_fusion.refs_0_), channel_id=1, source_target_pairs={{0,6},{1,7},{2,4},{3,5},{4,2},{5,3},{6,0},{7,1},{8,14},{9,15},{10,... | collective-permute-start | bytes 786440 | tf_op jit(solution)/shard_map/ppermute | solution.py:410
  122.7 16.6 %collective-permute-start.20 = (bf16[64,2048]{1,0:T(8,128)(2,1)S(1)}, bf16[64,2048]{1,0:T(8,128)(2,1)S(1)}, u32[]{:S(2)}, u32[]{:S(2)}) collective-permute-start(bf16[64,2048]{1,0:T(8,128)(2,1)S(1)} %collective-permute-done.19.refs_1_), channel_id=1, source_target_pairs={{0,16},{8,24},{16,0},{24,8},{1,17},{9,25},{17,1},{25,9},{2,18},{10... | collective-permute-start | bytes 786440 | tf_op jit(solution)/shard_map/ppermute | solution.py:420
  124.6 15.1 %collective-permute-start.21 = (bf16[64,2048]{1,0:T(8,128)(2,1)S(1)}, bf16[64,2048]{1,0:T(8,128)(2,1)S(1)}, u32[]{:S(2)}, u32[]{:S(2)}) collective-permute-start(bf16[64,2048]{1,0:T(8,128)(2,1)S(1)} %collective-permute-done.19.refs_1_), channel_id=1, source_target_pairs={{0,1},{1,0},{2,3},{3,2},{4,5},{5,4},{6,7},{7,6},{8,9},{9,8},{10,11... | collective-permute-start | bytes 786440 | tf_op jit(solution)/shard_map/ppermute | solution.py:410
  149.8 15.8 %collective-permute-start.28 = (bf16[512,2048]{1,0:T(8,128)(2,1)}, bf16[512,2048]{1,0:T(8,128)(2,1)}, u32[]{:S(2)}, u32[]{:S(2)}) collective-permute-start(bf16[512,2048]{1,0:T(8,128)(2,1)} %shard_map.186.rows.refs_0_), channel_id=1, source_target_pairs={{0,8},{8,0},{16,24},{24,16},{1,9},{9,1},{17,25},{25,17},{2,10},{10... | collective-permute-start | bytes 6291464 | tf_op jit(solution)/shard_map/ppermute | solution.py:420
  153.2 28.0 %collective-permute-start.29 = (bf16[256,2048]{1,0:T(8,128)(2,1)}, bf16[256,2048]{1,0:T(8,128)(2,1)S(1)}, u32[]{:S(2)}, u32[]{:S(2)}) collective-permute-start(bf16[256,2048]{1,0:T(8,128)(2,1)} %shard_map.189.refs_0_), channel_id=1, source_target_pairs={{0,1},{1,0},{2,3},{3,2},{4,5},{5,4},{6,7},{7,6},{8,9},{9,8},{10,11... | collective-permute-start | bytes 3145736 | tf_op jit(solution)/shard_map/ppermute | solution.py:410
  190.0 16.0 %collective-permute-start.33 = (bf16[2,64,2048]{2,1,0:T(8,128)(2,1)S(1)}, bf16[2,64,2048]{2,1,0:T(8,128)(2,1)S(1)}, u32[]{:S(2)}, u32[]{:S(2)}) collective-permute-start(bf16[2,64,2048]{2,1,0:T(8,128)(2,1)S(1)} %fusion.5), channel_id=1, source_target_pairs={{0,1},{1,0},{2,3},{3,2},{4,5},{5,4},{6,7},{7,6},{8,9},{9,8},{10,11... | collective-permute-start | bytes 1572872 | tf_op jit(solution)/shard_map/ppermute | solution.py:410
  206.4 14.8 %collective-permute-start.35 = (bf16[2,64,2048]{2,1,0:T(8,128)(2,1)S(1)}, bf16[2,64,2048]{2,1,0:T(8,128)(2,1)S(1)}, u32[]{:S(2)}, u32[]{:S(2)}) collective-permute-start(bf16[2,64,2048]{2,1,0:T(8,128)(2,1)S(1)} %fusion.6), channel_id=1, source_target_pairs={{0,1},{1,0},{2,3},{3,2},{4,5},{5,4},{6,7},{7,6},{8,9},{9,8},{10,11... | collective-permute-start | bytes 1572872 | tf_op jit(solution)/shard_map/ppermute | solution.py:410
  211.7 20.7 %collective-permute-start.37 = (bf16[2,64,2048]{2,1,0:T(8,128)(2,1)S(1)}, bf16[2,64,2048]{2,1,0:T(8,128)(2,1)S(1)}, u32[]{:S(2)}, u32[]{:S(2)}) collective-permute-start(bf16[2,64,2048]{2,1,0:T(8,128)(2,1)S(1)} %fusion.8), channel_id=1, source_target_pairs={{0,1},{1,0},{2,3},{3,2},{4,5},{5,4},{6,7},{7,6},{8,9},{9,8},{10,11... | collective-permute-start | bytes 1572872 | tf_op jit(solution)/shard_map/ppermute | solution.py:410
  213.8 29.5 %collective-permute-start.36 = (bf16[2,64,2048]{2,1,0:T(8,128)(2,1)S(1)}, bf16[2,64,2048]{2,1,0:T(8,128)(2,1)S(1)}, u32[]{:S(2)}, u32[]{:S(2)}) collective-permute-start(bf16[2,64,2048]{2,1,0:T(8,128)(2,1)S(1)} %fusion.7), channel_id=1, source_target_pairs={{0,1},{1,0},{2,3},{3,2},{4,5},{5,4},{6,7},{7,6},{8,9},{9,8},{10,11... | collective-permute-start | bytes 1572872 | tf_op jit(solution)/shard_map/ppermute | solution.py:410
  232.7 13.3 %collective-permute-start.39 = (bf16[2,64,2048]{2,1,0:T(8,128)(2,1)S(1)}, bf16[2,64,2048]{2,1,0:T(8,128)(2,1)S(1)}, u32[]{:S(2)}, u32[]{:S(2)}) collective-permute-start(bf16[2,64,2048]{2,1,0:T(8,128)(2,1)S(1)} %fusion.2), channel_id=1, source_target_pairs={{0,16},{8,24},{16,0},{24,8},{1,17},{9,25},{17,1},{25,9},{2,18},{10... | collective-permute-start | bytes 1572872 | tf_op jit(solution)/shard_map/ppermute | solution.py:420
  243.6 13.7 %collective-permute-start.38 = (bf16[2,64,2048]{2,1,0:T(8,128)(2,1)S(1)}, bf16[2,64,2048]{2,1,0:T(8,128)(2,1)S(1)}, u32[]{:S(2)}, u32[]{:S(2)}) collective-permute-start(bf16[2,64,2048]{2,1,0:T(8,128)(2,1)S(1)} %fusion.3), channel_id=1, source_target_pairs={{0,16},{8,24},{16,0},{24,8},{1,17},{9,25},{17,1},{25,9},{2,18},{10... | collective-permute-start | bytes 1572872 | tf_op jit(solution)/shard_map/ppermute | solution.py:420
  257.6 11.0 %collective-permute-start.42 = (bf16[64,2048]{1,0:T(8,128)(2,1)S(1)}, bf16[64,2048]{1,0:T(8,128)(2,1)S(1)}, u32[]{:S(2)}, u32[]{:S(2)}) collective-permute-start(bf16[64,2048]{1,0:T(8,128)(2,1)S(1)} %fusion.19), channel_id=1, source_target_pairs={{0,2},{1,3},{2,0},{3,1},{4,6},{5,7},{6,4},{7,5},{8,10},{9,11},{10,... | collective-permute-start | bytes 786440 | tf_op jit(solution)/shard_map/ppermute | solution.py:410
  259.2 21.3 %collective-permute-start.41 = (bf16[64,2048]{1,0:T(8,128)(2,1)S(1)}, bf16[64,2048]{1,0:T(8,128)(2,1)S(1)}, u32[]{:S(2)}, u32[]{:S(2)}) collective-permute-start(bf16[64,2048]{1,0:T(8,128)(2,1)S(1)} %get-tuple-element.141), channel_id=1, source_target_pairs={{0,4},{1,5},{2,6},{3,7},{4,0},{5,1},{6,2},{7,3},{8,12},{9,13},{10,... | collective-permute-start | bytes 786440 | tf_op jit(solution)/shard_map/ppermute | solution.py:410
  260.0 20.5 %collective-permute-start.40 = (bf16[64,2048]{1,0:T(8,128)(2,1)S(1)}, bf16[64,2048]{1,0:T(8,128)(2,1)S(1)}, u32[]{:S(2)}, u32[]{:S(2)}) collective-permute-start(bf16[64,2048]{1,0:T(8,128)(2,1)S(1)} %get-tuple-element.142), channel_id=1, source_target_pairs={{0,6},{1,7},{2,4},{3,5},{4,2},{5,3},{6,0},{7,1},{8,14},{9,15},{10,... | collective-permute-start | bytes 786440 | tf_op jit(solution)/shard_map/ppermute | solution.py:410
  (48 other events, 457.2 us)

commit v7 on v6

--- a/solution.py
+++ b/solution.py
@@ -64,57 +64,55 @@
     )(order, *operands)
 
 
-def attend_kernel(members, tokens, page_len, scale, page_req, page_slot, *refs):
-    blocks, far, refs = refs[:members], refs[members : 2 * members], refs[2 * members :]
-    row_req, row_pos, out, level = refs
+def attend_kernel(members, tokens, tok_rows, page_len, scale, page_req, page_slot, *refs):
+    blocks, refs = refs[:members], refs[members:]
+    if len(refs) > 4:
+        query, refs = [q[...] for q in refs[:members]], refs[members:]
+    else:
+        query = [block[2 * tokens : 2 * tokens + tok_rows, :] for block in blocks]
+    request, position, out, level = refs
+    request, position = request[...], position[...]
     keys = jnp.concatenate([block[:tokens, :] for block in blocks], axis=0)
     values = jnp.concatenate([block[tokens : 2 * tokens, :] for block in blocks], axis=0)
-    tok_rows = far[0].shape[0]
-    near = [block[2 * tokens : 2 * tokens + tok_rows, :] for block in blocks]
-    size = sum(q.shape[0] for q in near)
-    for side, query in enumerate((near, [q[...] for q in far])):
-        lanes = slice(side * size, (side + 1) * size)
-        query = jnp.concatenate(query, axis=0)
-        request, position = row_req[:, lanes], row_pos[:, lanes]
-        scores = (
-            lax.dot_general(
-                keys, query, (((1,), (1,)), ((), ())), preferred_element_type=jnp.float32
-            )
-            * scale
-        )
-        token = lax.broadcasted_iota(jnp.int32, (page_len, size), 0)
-        visible = jnp.concatenate(
-            [
-                (request == page_req[page]) & (token + page_slot[page] * page_len <= position)
-                for page in range(members * tokens // page_len)
-            ],
-            axis=0,
-        )
-        scores = jnp.where(visible, scores, -1e30)
-        top = jnp.max(scores, axis=0, keepdims=True)
-        weights = jnp.where(visible, jnp.exp(scores - top), 0.0)
-        total = jnp.sum(weights, axis=0, keepdims=True)
-        summed = lax.dot_general(
-            values,
-            weights.astype(jnp.bfloat16),
-            (((0,), (0,)), ((), ())),
-            preferred_element_type=jnp.float32,
-        )
-        seen = total > 0.0
-        total = jnp.where(seen, total, 1.0)
-        out[:, lanes] = (summed / total).astype(jnp.bfloat16)
-        level[0, :, lanes] = jnp.where(seen, top + jnp.log(total), -1e30)
-
-
-def attend(blocks, far, row_req, row_pos, page_req, page_slot, page_len, tokens):
+    query = jnp.concatenate(query, axis=0)
+    scores = (
+        lax.dot_general(keys, query, (((1,), (1,)), ((), ())), preferred_element_type=jnp.float32)
+        * scale
+    )
+    token = lax.broadcasted_iota(jnp.int32, (page_len, query.shape[0]), 0)
+    visible = jnp.concatenate(
+        [
+            (request == page_req[page]) & (token + page_slot[page] * page_len <= position)
+            for page in range(members * tokens // page_len)
+        ],
+        axis=0,
+    )
+    scores = jnp.where(visible, scores, -1e30)
+    top = jnp.max(scores, axis=0, keepdims=True)
+    weights = jnp.where(visible, jnp.exp(scores - top), 0.0)
+    total = jnp.sum(weights, axis=0, keepdims=True)
+    summed = lax.dot_general(
+        values,
+        weights.astype(jnp.bfloat16),
+        (((0,), (0,)), ((), ())),
+        preferred_element_type=jnp.float32,
+    )
+    seen = total > 0.0
+    total = jnp.where(seen, total, 1.0)
+    out[...] = (summed / total).astype(jnp.bfloat16)
+    level[0] = jnp.where(seen, top + jnp.log(total), -1e30)
+
+
+def attend(blocks, far, row_req, row_pos, page_req, page_slot, page_len, tokens, tok_rows):
     members, rows = len(blocks), row_req.shape[1]
     block_rows, columns = blocks[0].shape
-    tok_rows = far[0].shape[0]
     heads = columns // HEAD_DIM
     by_head = lambda n: pl.BlockSpec((n, HEAD_DIM), lambda h, *_: (0, h))
     whole = pl.BlockSpec((1, rows), lambda h, *_: (0, 0))
     return pl.pallas_call(
-        functools.partial(attend_kernel, members, tokens, page_len, HEAD_DIM ** (-0.5)),
+        functools.partial(
+            attend_kernel, members, tokens, tok_rows, page_len, HEAD_DIM ** (-0.5)
+        ),
         out_shape=[
             jax.ShapeDtypeStruct((columns, rows), jnp.bfloat16),
             jax.ShapeDtypeStruct((heads, 1, rows), jnp.float32),
@@ -122,7 +120,7 @@
         grid_spec=pltpu.PrefetchScalarGridSpec(
             num_scalar_prefetch=2,
             grid=(heads,),
-            in_specs=[by_head(block_rows)] * members + [by_head(tok_rows)] * members + [whole] * 2,
+            in_specs=[by_head(block_rows)] * members + [by_head(tok_rows)] * len(far) + [whole] * 2,
             out_specs=[
                 pl.BlockSpec((HEAD_DIM, rows), lambda h, *_: (h, 0)),
                 pl.BlockSpec((1, 1, rows), lambda h, *_: (h, 0, 0)),
@@ -137,54 +135,64 @@
     )(page_req, page_slot, *blocks, *far, row_req, row_pos)
 
 
-def project_kernel(mine, mine_level, theirs, their_level, proj, stay, go):
+def project_kernel(order, mine, mine_level, theirs, their_level, own, *refs):
+    quarters, (stay, go, proj) = refs[:-3], refs[-3:]
+    rows, size = own.shape[0], quarters[0].shape[0]
+    proj[:rows, :] = own[...]
+    for k, quarter in enumerate(quarters):
+        at = pl.multiple_of(rows + order[k] * size, size)
+        proj[pl.ds(at, size), :] = quarter[...]
     parts = []
-    for head in range(mine.shape[0] // HEAD_DIM):
+    heads = mine.shape[0] // HEAD_DIM
+    for head in range(heads):
+        twin = (head + heads // 2) % heads
         dims = slice(head * HEAD_DIM, (head + 1) * HEAD_DIM)
-        share = 1.0 / (1.0 + jnp.exp(their_level[head] - mine_level[head]))
-        other = 1.0 / (1.0 + jnp.exp(mine_level[head] - their_level[head]))
-        both = share * mine[dims, :].astype(jnp.float32) + other * theirs[dims, :].astype(
-            jnp.float32
-        )
+        twin_dims = slice(twin * HEAD_DIM, (twin + 1) * HEAD_DIM)
+        share = 1.0 / (1.0 + jnp.exp(their_level[twin] - mine_level[head]))
+        other = 1.0 / (1.0 + jnp.exp(mine_level[head] - their_level[twin]))
+        both = share * mine[dims, :].astype(jnp.float32) + other * theirs[
+            twin_dims, :
+        ].astype(jnp.float32)
         parts.append(both.astype(jnp.bfloat16))
-    attention = jnp.concatenate(parts, axis=0) if len(parts) > 1 else parts[0]
+    attention = jnp.concatenate(parts, axis=0)
     mixed = lax.dot_general(
         attention, proj[...], (((0,), (0,)), ((), ())), preferred_element_type=jnp.float32
     )
-    rows = stay.shape[1]
-    stay[0] = mixed[:rows, :]
-    go[0] = mixed[rows:, :].astype(jnp.bfloat16)
-
-
-def project(pair, mine, mine_level, theirs, their_level, proj, tok_rows):
-    columns, width = proj.shape
-    heads = columns // HEAD_DIM
-    size = mine.shape[1] // 4
-    here, there = 2 * pair, 2 * (1 - pair)
+    kept = stay.shape[0]
+    stay[...] = mixed[:kept, :]
+    go[...] = mixed[kept:, :].astype(jnp.bfloat16)
+
+
+def project(place, order, mine, mine_level, theirs, their_level, own, quarters, tok_rows):
+    dims, width = mine.shape[0], own.shape[1]
+    heads = dims // HEAD_DIM
+    size = mine.shape[1] // 2
+    whole = lambda a: pl.BlockSpec(a.shape, lambda i, order: (0, 0))
+    values = pl.BlockSpec((dims, size), lambda i, order: (0, place))
+    levels = pl.BlockSpec((heads, 1, size), lambda i, order: (0, 0, place))
     return pl.pallas_call(
         project_kernel,
         out_shape=[
-            jax.ShapeDtypeStruct((2, tok_rows, width), jnp.float32),
-            jax.ShapeDtypeStruct((2, size - tok_rows, width), jnp.bfloat16),
+            jax.ShapeDtypeStruct((tok_rows, width), jnp.float32),
+            jax.ShapeDtypeStruct((size - tok_rows, width), jnp.bfloat16),
         ],
-        grid=(2,),
-        in_specs=[
-            pl.BlockSpec((columns, size), lambda i: (0, here + i)),
-            pl.BlockSpec((heads, 1, size), lambda i: (0, 0, here + i)),
-            pl.BlockSpec((columns, size), lambda i: (0, there + i)),
-            pl.BlockSpec((heads, 1, size), lambda i: (0, 0, there + i)),
-            pl.BlockSpec((columns, width), lambda i: (0, 0)),
-        ],
-        out_specs=[
-            pl.BlockSpec((1, tok_rows, width), lambda i: (i, 0, 0)),
-            pl.BlockSpec((1, size - tok_rows, width), lambda i: (i, 0, 0)),
-        ],
+        grid_spec=pltpu.PrefetchScalarGridSpec(
+            num_scalar_prefetch=1,
+            grid=(1,),
+            in_specs=[values, levels, values, levels, whole(own)] + [whole(q) for q in quarters],
+            out_specs=[
+                pl.BlockSpec((tok_rows, width), lambda i, order: (0, 0)),
+                pl.BlockSpec((size - tok_rows, width), lambda i, order: (0, 0)),
+            ],
+            scratch_shapes=[pltpu.VMEM((dims, width), jnp.bfloat16)],
+        ),
+        compiler_params=pltpu.CompilerParams(vmem_limit_bytes=32 * 1024 * 1024),
         cost_estimate=pl.CostEstimate(
-            flops=4 * size * columns * width,
-            bytes_accessed=2 * (4 * columns * size + columns * width + 2 * size * width),
-            transcendentals=4 * size * heads,
-        ),
-    )(mine, mine_level, theirs, their_level, proj)
+            flops=2 * size * dims * width,
+            bytes_accessed=2 * (2 * dims * size + dims * width + 3 * size * width),
+            transcendentals=2 * size * heads,
+        ),
+    )(order, mine, mine_level, theirs, their_level, own, *quarters)
 
 
 def join_kernel(*refs):
@@ -419,6 +427,12 @@
         ]
         return lax.ppermute(value, "req", pairs)
 
+    def swap_y(value):
+        pairs = [(y * nc + c, (y ^ 1) * nc + c) for y in range(ny) for c in range(nc)]
+        return lax.ppermute(value, "req", pairs)
+
+    tie = lax.optimization_barrier
+
     rel_exp = jnp.stack(
         [
             ((ih + dh) % 2 * 2 + (il + dl) % 2) * nx + (ix - dx) % nx
@@ -433,6 +447,14 @@
     columns = width // exp_count
     keys = cache_key.reshape(tokens, width)
     values = cache_value.reshape(tokens, width)
+    quarter_rows = out_proj.shape[0] // (2 * nc)
+    quarter = lax.dynamic_slice_in_dim(
+        out_proj, (iy % 2 * nc + ic) * quarter_rows, quarter_rows, 0
+    )
+    quarters = [send(quarter, 1, 0, 0)]
+    quarter_order = jnp.stack(
+        [(iy + dy) % 2 * nc + (ic + dc) % nc for dc in range(nc) for dy in range(2)]
+    ).astype(i32)
     far_queries = send(queries, 1, 0, 0)
     members = [(dl, dx) for dl in range(2) for dx in range(nx)]
     order = jnp.stack(
@@ -445,34 +467,45 @@
     gates = jnp.pad(jnp.transpose(route_gate), ((0, 0), (0, 2 * columns - tok_rows)))
     blocks = pack([keys, values, queries], gates, order, columns)
     blocks = [send(blocks[m], 0, *members[m]) for m in range(len(members))]
-    far = pack([far_queries], None, order, columns)
-    far = [send(far[m], 0, *members[m]) for m in range(len(members))]
+    far = list(pack([far_queries], None, order, columns))
+    for m in range(1, len(members)):
+        if m > 2:
+            far[m], far[m - 2] = tie((far[m], far[m - 2]))
+        far[m] = send(far[m], 0, *members[m])
     page_ids = (
         rel_exp[: len(members), None] * pages_here + jnp.arange(pages_here, dtype=i32)[None, :]
     ).reshape(-1)
     hits = (page_table[None, :, :] == page_ids[:, None, None]).astype(i32)
     page_request = jnp.sum(hits * jnp.arange(req_slots, dtype=i32)[None, :, None], axis=(1, 2))
     page_slot = jnp.sum(hits * jnp.arange(max_pages, dtype=i32)[None, None, :], axis=(1, 2))
-    rel_rows = lambda a: a.reshape(exp_count, tok_rows)[rel_exp].reshape(1, -1)
+    rel_rows = lambda a: a.reshape(exp_count, tok_rows)[rel_exp].reshape(2, 1, -1)
+    row_req, row_pos = rel_rows(row_request), rel_rows(row_position)
     gates = [block[2 * tokens + tok_rows :, :tok_rows].astype(f32) for block in blocks]
     gates = jnp.stack([g[:TOPK] + g[TOPK : 2 * TOPK] + g[2 * TOPK : 3 * TOPK] for g in gates])
     gates = gates.reshape(2, nx, TOPK, tok_rows)
+
+    def attend_half(side, queries):
+        return attend(
+            blocks,
+            queries,
+            row_req[side],
+            row_pos[side],
+            page_request,
+            page_slot,
+            page_len,
+            tokens,
+            tok_rows,
+        )
+
     gates = jnp.stack([send(gates, dh, 0, 0) for dh in range(2)])
-    partial, level = attend(
-        blocks,
-        far,
-        rel_rows(row_request),
-        rel_rows(row_position),
-        page_request,
-        page_slot,
-        page_len,
-        tokens,
-    )
-    partial, level, gates = lax.optimization_barrier((partial, level, gates))
+    quarters.append(swap_y(quarters[0]))
+    theirs, their_level = attend_half(1, far)
+    theirs, their_level, gates, quarters = tie((theirs, their_level, gates, quarters))
+    theirs, their_level = send(theirs, 1, 0, 0), send(their_level, 1, 0, 0)
     gates = jnp.stack([send_req(gates, dy, 0) for dy in range(ny)])
-    other = send(partial[columns:], 1, 0, 0)
-    other_level = send(level[columns // HEAD_DIM :], 1, 0, 0)
-    other, other_level, gates = lax.optimization_barrier((other, other_level, gates))
+    quarters += [send_req(q, 0, dc) for dc in range(1, nc) for q in quarters[:2]]
+    mine, level = attend_half(0, [])
+    mine, level, gates, quarters = tie((mine, level, gates, quarters))
 
     slot_ids = jnp.arange(slot_count, dtype=i32)
     own_mark = slot_ids == own_slot
@@ -489,43 +522,32 @@
     chunk_rows = exp_count * tok_rows
     entries = -(-exp_count * capacity // 16) * 16
     row_gate = jnp.sum(jnp.where(named, gates, 0.0), axis=1).reshape(ny, nc, chunk_rows)
-    mine = jnp.any(named, axis=1) & (rel_slots % copies == own_rank)[:, None]
-    mine = mine.reshape(ny, nc, chunk_rows)
-    place = jnp.where(mine, jnp.cumsum(mine.astype(i32), axis=2) - 1, -1)
+    served = jnp.any(named, axis=1) & (rel_slots % copies == own_rank)[:, None]
+    served = served.reshape(ny, nc, chunk_rows)
+    place = jnp.where(served, jnp.cumsum(served.astype(i32), axis=2) - 1, -1)
     place = place.reshape(ny, nc, 1, chunk_rows)
     row_gate = row_gate.reshape(ny, nc, 1, chunk_rows)
 
-    tie = lax.optimization_barrier
-    last = len(zs) - 1
-
-    tie = lax.optimization_barrier
-
     stays, comes = {}, {}
-    mine = partial
-    for pair in (1, 0):
-        stays[pair], go = project(pair, mine, level, other, other_level, out_proj, tok_rows)
-        mine, _ = tie((partial, go))
-        go = go.reshape(2, nx - 1, tok_rows, width)
-        comes[pair] = [send(go[:, dx - 1], 0, 0, -dx) for dx in range(1, nx)]
-    stream = resid.astype(f32)
-    arrived = []
-    for pair in (1, 0):
-        line = stays[pair]
-        for come in comes[pair]:
-            line = line + come.astype(f32)
-        for i in (1, 0):
-            if pair or i:
-                go = line[i].astype(bf16)
-                comes[0], _ = tie((comes[0], go))
-                arrived.append(send(go, *zs[2 * pair + i], 0))
-            else:
-                stream = stream + line[0]
-    for come in arrived:
-        stream = stream + come.astype(f32)
+    proj = out_proj
+    for dl in (1, 0):
+        stays[dl], go = project(
+            dl, quarter_order, mine, level, theirs, their_level, proj, quarters, tok_rows
+        )
+        comes[dl] = [
+            send(go[(dx - 1) * tok_rows : dx * tok_rows], 0, 0, -dx) for dx in range(1, nx)
+        ]
+        proj, _ = tie((proj, go))
+    line = sum([come.astype(f32) for come in comes[1]], stays[1]).astype(bf16)
+    comes[0], _ = tie((comes[0], line))
+    line = send(line, 0, 1, 0)
+    stream = sum([come.astype(f32) for come in comes[0]], resid.astype(f32) + stays[0])
+    stream = stream + line.astype(f32)
     normed = rms_normed(stream, norm_gain)
     normed, place, row_gate = tie((normed, place, row_gate))
 
-    line = [send(normed, *zs[i], 0) for i in range(len(zs))]
+    far_line = send(normed, 1, 0, 0)
+    line = [normed, send(normed, 0, 1, 0), far_line, send(far_line, 0, 1, 0)]
     piece = {}
     for i in range(len(zs)):
         piece[i, 0, 0] = line[i]
@@ -547,6 +569,7 @@
     for dc in range(1, nc):
         chunks[0, dc] = partners[dc - 1]
 
+    places = lambda part: part.astype(f32).reshape(nx, 2, 2, tok_rows, width)
     kept, comes = {}, {}
     for dy in range(ny):
         answers = routed_expert(
@@ -561,54 +584,48 @@
         )
         extra = None
         if dy:
-            answers, comes[dy - 1][1] = tie((answers, comes[dy - 1][1]))
+            answers, comes[dy - 1] = tie((answers, comes[dy - 1]))
         if dy + 1 < ny:
             answers, chunks[dy + 1, 0] = tie((answers, chunks[dy + 1, 0]))
             for dc in range(1, nc):
                 chunks[dy + 1, dc] = [send_req(part, 0, dc) for part in chunks[dy + 1, 0]]
-        others = [send_req(answers[dc], 0, -dc) for dc in range(1, nc)]
-        parts = [answers[0]] + others
-        comes[dy] = {}
-        for pair in (1, 0):
-            gone = [
-                part.reshape(nx, 2, 2, tok_rows, width)[1:, pair].astype(f32) for part in parts
-            ]
-            gone = sum(gone[1:], gone[0]).astype(bf16)
-            comes[dy][pair] = [send(gone[dx - 1], 0, 0, -dx) for dx in range(1, nx)]
-            if pair:
-                parts, _ = tie((parts, gone))
+        parts = [answers[0]] + [send_req(answers[dc], 0, -dc) for dc in range(1, nc)]
         if dy + 1 < ny:
+            gone = sum([places(p)[1:] for p in parts[1:]], places(parts[0])[1:]).astype(bf16)
+            comes[dy] = [send(gone[dx - 1], 0, 0, -dx) for dx in range(1, nx)]
             following = [chunks[dy + 1, dc] for dc in range(nc)]
             following, _ = tie((following, gone))
             for dc in range(nc):
                 chunks[dy + 1, dc] = following[dc]
-        elif dy:
-            parts, comes[dy - 1][0] = tie((parts, comes[dy - 1][0]))
         kept[dy] = parts
 
-    def line_of(dy, pair):
-        line = [p.reshape(nx, 2, 2, tok_rows, width)[0, pair].astype(f32) for p in kept[dy]]
-        return sum([come.astype(f32) for come in comes[dy][pair]], sum(line[1:], line[0]))
-
-    home = stream
-    over_y, arrived = {}, []
-    for pair in (1, 0):
-        goes = [line_of(dy, pair).astype(bf16) for dy in range(1, ny)]
-        over_y[pair] = [send_req(go, -dy, 0) for dy, go in enumerate(goes, 1)]
-        if pair:
-            comes[ny - 1][0], _ = tie((comes[ny - 1][0], goes))
-    for pair in (1, 0):
-        total = sum([come.astype(f32) for come in over_y[pair]], line_of(0, pair))
-        for i in (1, 0):
-            if pair or i:
-                go = total[i].astype(bf16)
-                over_y[0], _ = tie((over_y[0], go))
-                arrived.append(send(go, *zs[2 * pair + i], 0))
-            else:
-                home = home + total[0]
-    for come in arrived:
-        home = home + come.astype(f32)
-    total = home
+    def line_of(dy, dl):
+        line = [places(p)[0, :, dl] for p in kept[dy]]
+        if dy + 1 < ny:
+            line += [come.astype(f32)[:, dl] for come in comes[dy]]
+        else:
+            line += [come.astype(f32) for come in last[dl]]
+        return sum(line[1:], line[0])
+
+    last = {}
+    parts = kept[ny - 1]
+    for dl in (1, 0):
+        gone = sum([places(p)[1:, :, dl] for p in parts[1:]], places(parts[0])[1:, :, dl])
+        gone = gone.astype(bf16)
+        last[dl] = [send(gone[dx - 1], 0, 0, -dx) for dx in range(1, nx)]
+        parts, _ = tie((parts, gone))
+    over_y = {}
+    for dl in (1, 0):
+        goes = [line_of(dy, dl).astype(bf16) for dy in range(1, ny)]
+        if dl:
+            last[0], _ = tie((last[0], goes))
+        else:
+            goes, over_y[1] = tie((goes, over_y[1]))
+        over_y[dl] = [send_req(go, -dy, 0) for dy, go in enumerate(goes, 1)]
+    near = sum([come.astype(f32) for come in over_y[1]], line_of(0, 1)).astype(bf16)
+    near = send(near, 0, 1, 0)
+    total = sum([come.astype(f32) for come in over_y[0]], line_of(0, 0)) + near.astype(f32)
+    total = stream + total[0] + send(total[1].astype(bf16), 1, 0, 0).astype(f32)
     return total.astype(bf16)
 
 

time: 283 us -> 258 us (0.912)
  waiting for transfers between devices: 133 us -> 93.9 us
  local copies, waits for them, and re-layouts: 13.8 us -> 24.6 us
  other arithmetic: 11.1 us -> 15.1 us
    ppermute x30 -> x27, waiting for transfers between devices: 108 us -> 82.7 us  [send(): return lax.ppermute(value, 'exp', pairs)]
    ppermute x13 -> x15, waiting for transfers between devices: 24.8 us -> 11.2 us  [send_req(): return lax.ppermute(value, 'req', pairs)]
    unnamed x74 -> x82, local copies, waits for them, and re-layouts: 7.5 us -> 15.2 us
    ppermute x13 -> x15, starting transfers between devices: 10.1 us -> 7.56 us  [send_req(): return lax.ppermute(value, 'req', pairs)]
    ppermute x30 -> x27, starting transfers between devices: 49.2 us -> 51.7 us  [send(): return lax.ppermute(value, 'exp', pairs)]
    pallas_call x3 -> x4, Pallas kernels: 13.9 us -> 13.3 us  [the longest x2 8.98 us: attend(): pl.pallas_call(functools.partial(attend_kernel, members, tokens, tok_rows...]
  transfers between devices with their start and end apart: 43 -> 43, of which waited for: 22 -> 23; matrix products, arithmetic and copies ran while one was open for 5% -> 8% of each run, Pallas kernels for 20% -> 22%
where the time goes in v7:
time: 258 us
  waiting for transfers between devices  93.9 us (36%)
  Pallas kernels  61.3 us (24%)
  starting transfers between devices  60.8 us (24%)
  local copies, waits for them, and re-layouts  24.6 us (10%)
  other arithmetic  15.1 us (6%)
    ppermute x27, waiting for transfers between devices, send(): return lax.ppermute(value, 'exp', pairs)  82.7 us
    ppermute x27, starting transfers between devices, send(): return lax.ppermute(value, 'exp', pairs)  51.7 us
    pallas_call x2, Pallas kernels, routed_expert(): pl.pallas_call(functools.partial(routed_kernel, parts, entries, has_extra...  30.7 us
    unnamed x82, local copies, waits for them, and re-layouts  15.2 us
    ppermute x15, waiting for transfers between devices, send_req(): return lax.ppermute(value, 'req', pairs)  11.2 us
    pallas_call x2, Pallas kernels, attend(): pl.pallas_call(functools.partial(attend_kernel, members, tokens, tok_rows...  8.98 us
    pallas_call x1, Pallas kernels, shared_expert(): pl.pallas_call(shared_kernel, out_shape=jax.ShapeDtypeStruct(rows.shape,...  8.74 us
    ppermute x15, starting transfers between devices, send_req(): return lax.ppermute(value, 'req', pairs)  7.56 us
  transfers between devices with their start and end apart: 43, of which 23 were waited for; matrix products, arithmetic and copies ran while one was open for 8% of the time, Pallas kernels for 22%

profile of v7, /device:TPU:0, one launch (start us, length us, event | category | flops | bytes accessed | tf_op | source)
XLA Modules:
  0.0 257.5 jit_solution(7515620790015865616)
XLA Ops:
  1.7 4.0 %collective-permute-start.8 = (bf16[64,2048]{1,0:T(8,128)(2,1)}, bf16[64,2048]{1,0:T(8,128)(2,1)}, u32[]{:S(2)}, u32[]{:S(2)}) collective-permute-start(bf16[64,2048]{1,0:T(8,128)(2,1)} %constant_dynamic-slice_fusion), channel_id=1, source_target_pairs={{0,4},{1,5},{2,6},{3,7},{4,0},{5,1},{6,2},{7,3},{8,12},{9,13},{10,... | collective-permute-start | bytes 786440 | tf_op jit(solution)/shard_map/ppermute | solution.py:418
  9.9 2.6 shard_map.181
  25.4 3.8 %collective-permute-done.3.refs_0_.refs_1_.refs_2_.refs_3_ = bf16[64,2048]{1,0:T(8,128)(2,1)S(1)} collective-permute-done((bf16[64,2048]{1,0:T(8,128)(2,1)}, bf16[64,2048]{1,0:T(8,128)(2,1)S(1)}, u32[]{:S(2)}, u32[]{:S(2)}) %collective-permute-start.3) | collective-permute-done | bytes 262176 | tf_op jit(solution)/shard_map/ppermute | solution.py:418
  35.9 13.4 %collective-permute-start.6 = (bf16[64,512]{1,0:T(8,128)(2,1)S(1)}, bf16[64,512]{1,0:T(8,128)(2,1)S(1)}, u32[]{:S(2)}, u32[]{:S(2)}) collective-permute-start(bf16[64,512]{1,0:T(8,128)(2,1)S(1)} %get-tuple-element.85), channel_id=1, source_target_pairs={{0,3},{1,2},{2,1},{3,0},{4,7},{5,6},{6,5},{7,4},{8,11},{9,10},{10,... | collective-permute-start | bytes 196616 | tf_op jit(solution)/shard_map/ppermute | solution.py:418
  49.3 4.2 %collective-permute-done.2.refs_3_ = bf16[592,512]{1,0:T(8,128)(2,1)S(1)} collective-permute-done((bf16[592,512]{1,0:T(8,128)(2,1)}, bf16[592,512]{1,0:T(8,128)(2,1)S(1)}, u32[]{:S(2)}, u32[]{:S(2)}) %collective-permute-start.2) | collective-permute-done | bytes 606240 | tf_op jit(solution)/shard_map/ppermute | solution.py:418
  53.6 2.9 %collective-permute-start.7 = (f32[2,2,4,64]{3,0,1,2:T(2,128)S(1)}, f32[2,2,4,64]{3,0,1,2:T(2,128)S(1)}, u32[]{:S(2)}, u32[]{:S(2)}) collective-permute-start(f32[2,2,4,64]{3,0,1,2:T(2,128)S(1)} %copy.68), channel_id=1, source_target_pairs={{0,4},{1,5},{2,6},{3,7},{4,0},{5,1},{6,2},{7,3},{8,12},{9,13},{10,... | collective-permute-start | bytes 12296 | tf_op jit(solution)/shard_map/ppermute | solution.py:418
  56.5 4.5 %shard_map.184 = (bf16[512,256]{1,0:T(8,128)(2,1)S(1)}, f32[4,1,256]{2,1,0:T(1,128)S(1)}) custom-call(s32[8]{0:T(128)S(1)} %get-tuple-element.144.page_req, s32[8]{0:T(128)S(1)} %get-tuple-element.143.page_slot, bf16[592,512]{1,0:T(8,128)(2,1)S(1)} %get-tuple-element.74.refs_0_, bf16[592,512]{1,0:T(8,128)(2,1)S(1)} %collective-permute-done.refs_1_, ...), custom_call_target="tpu_custom_call" | custom-call | flops 536870912 | bytes 2686976 | tf_op jit(solution)/shard_map/pallas_call | solution.py:112
  64.5 4.5 %shard_map.182 = (bf16[512,256]{1,0:T(8,128)(2,1)S(1)}, f32[4,1,256]{2,1,0:T(1,128)S(1)}) custom-call(s32[8]{0:T(128)S(1)} %get-tuple-element.144.page_req, s32[8]{0:T(128)S(1)} %get-tuple-element.143.page_slot, bf16[592,512]{1,0:T(8,128)(2,1)S(1)} %get-tuple-element.74.refs_0_, bf16[592,512]{1,0:T(8,128)(2,1)S(1)} %collective-permute-done.refs_1_, ...), custom_call_target="tpu_custom_call" | custom-call | flops 536870912 | bytes 2686976 | tf_op jit(solution)/shard_map/pallas_call | solution.py:112
  70.8 2.8 %collective-permute-done.14.their_level = f32[4,1,256]{2,1,0:T(1,128)S(1)} collective-permute-done((f32[4,1,256]{2,1,0:T(1,128)S(1)}, f32[4,1,256]{2,1,0:T(1,128)S(1)}, u32[]{:S(2)}, u32[]{:S(2)}) %collective-permute-start.14) | collective-permute-done | bytes 4128 | tf_op jit(solution)/shard_map/ppermute | solution.py:418
  73.6 2.2 shard_map.185
  81.9 2.1 shard_map.186
  85.8 2.4 collective-permute-start.17
  88.5 4.4 %collective-permute-done.15 = bf16[64,2048]{1,0:T(8,128)(2,1)S(1)} collective-permute-done((bf16[64,2048]{1,0:T(8,128)(2,1)S(1)}, bf16[64,2048]{1,0:T(8,128)(2,1)S(1)}, u32[]{:S(2)}, u32[]{:S(2)}) %collective-permute-start.15) | collective-permute-done | bytes 262176 | tf_op jit(solution)/shard_map/ppermute | solution.py:418
  92.9 2.1 collective-permute-done.17
  100.8 9.1 %collective-permute-done.24.refs_2_ = bf16[64,2048]{1,0:T(8,128)(2,1)S(1)} collective-permute-done((bf16[64,2048]{1,0:T(8,128)(2,1)S(1)}, bf16[64,2048]{1,0:T(8,128)(2,1)S(1)}, u32[]{:S(2)}, u32[]{:S(2)}) %collective-permute-start.24) | collective-permute-done | bytes 262176 | tf_op jit(solution)/shard_map/ppermute | solution.py:418
  113.9 3.2 %collective-permute-done.27.refs_3_ = bf16[64,2048]{1,0:T(8,128)(2,1)S(1)} collective-permute-done((bf16[64,2048]{1,0:T(8,128)(2,1)S(1)}, bf16[64,2048]{1,0:T(8,128)(2,1)S(1)}, u32[]{:S(2)}, u32[]{:S(2)}) %collective-permute-start.27) | collective-permute-done | bytes 262176 | tf_op jit(solution)/shard_map/ppermute | solution.py:418
  120.7 4.0 %collective-permute-done.23.refs_5_ = bf16[64,2048]{1,0:T(8,128)(2,1)S(1)} collective-permute-done((bf16[64,2048]{1,0:T(8,128)(2,1)S(1)}, bf16[64,2048]{1,0:T(8,128)(2,1)S(1)}, u32[]{:S(2)}, u32[]{:S(2)}) %collective-permute-start.23) | collective-permute-done | bytes 262176 | tf_op jit(solution)/shard_map/ppermute | solution.py:418
  126.3 2.4 collective-permute-done.29.refs_7_
  130.1 3.0 %shard_map.187.rows.refs_0_ = bf16[512,2048]{1,0:T(8,128)(2,1)} custom-call(bf16[64,2048]{1,0:T(8,128)(2,1)} %copy-done.19, bf16[64,2048]{1,0:T(8,128)(2,1)} %copy-done.21, bf16[64,2048]{1,0:T(8,128)(2,1)} %copy-done.20, bf16[64,2048]{1,0:T(8,128)(2,1)} %copy-done.23, bf16[64,2048]{1,0:T(8,128)(2,1)} %copy-done.22, bf16[64,2048]{1,0:T(8,128)(2,1)} %copy-done.25, ...), custom_call_target="tpu_custom_call" | custom-call | bytes 4194304 | tf_op jit(solution)/shard_map/pallas_call | solution.py:208
  134.3 2.2 shard_map.190.refs_0_
  138.9 8.7 %shard_map.188.refs_4_ = bf16[512,2048]{1,0:T(8,128)(2,1)S(1)} custom-call(bf16[512,2048]{1,0:T(8,128)(2,1)S(1)} %copy-done.4, bf16[1,2048]{1,0:T(2,128)(2,1)S(1)} %reshape.605.scalar, bf16[704,2048]{1,0:T(8,128)(2,1)} %bitcast.240, bf16[704,2048]{1,0:T(8,128)(2,1)} %bitcast.241, bf16[704,2048]{1,0:T(8,128)(2,1)} %down_w.1), custom_call_target="tpu_custom_call" | custom-call | flops 4429185024 | bytes 12845056 | tf_op jit(solution)/shard_map/pallas_call | solution.py:249
  150.4 15.6 %shard_map.189 = (bf16[512,2048]{1,0:T(8,128)(2,1)}, bf16[512,2048]{1,0:T(8,128)(2,1)}) custom-call(bf16[512,2048]{1,0:T(8,128)(2,1)} %shard_map.187.rows.refs_0_, bf16[512,2048]{1,0:T(8,128)(2,1)} %copy-done.38, s32[2,1,512]{2,1,0:T(1,128)} %get-tuple-element.152.refs_2_, f32[2,1,512]{2,1,0:T(1,128)} %get-tuple-element.150.refs_3_, ...), custom_call_target="tpu_custom_call" | custom-call | flops 8254390272 | bytes 25690112 | tf_op jit(solution)/shard_map/pallas_call | solution.py:338
  166.9 2.1 convert_element_type.139
  177.7 15.1 %shard_map.191 = (bf16[512,2048]{1,0:T(8,128)(2,1)}, bf16[512,2048]{1,0:T(8,128)(2,1)}) custom-call(bf16[256,2048]{1,0:T(8,128)(2,1)} %shard_map.190.refs_0_, bf16[256,2048]{1,0:T(8,128)(2,1)} %collective-permute-done.31.refs_1_, bf16[256,2048]{1,0:T(8,128)(2,1)} %copy-done.39, bf16[256,2048]{1,0:T(8,128)(2,1)} %copy-done.40, ...), custom_call_target="tpu_custom_call" | custom-call | flops 8254390272 | bytes 25690112 | tf_op jit(solution)/shard_map/pallas_call | solution.py:338
  192.8 6.5 %collective-permute-done.35 = bf16[2,2,64,2048]{3,2,0,1:T(8,128)(2,1)S(1)} collective-permute-done((bf16[2,2,64,2048]{3,2,0,1:T(8,128)(2,1)}, bf16[2,2,64,2048]{3,2,0,1:T(8,128)(2,1)S(1)}, u32[]{:S(2)}, u32[]{:S(2)}) %collective-permute-start.35) | collective-permute-done | bytes 1048608 | tf_op jit(solution)/shard_map/ppermute | solution.py:418
  199.3 2.1 convert.10
  201.4 2.3 collective-permute-done.36
  207.9 11.2 %collective-permute-done.38 = bf16[2,64,2048]{2,1,0:T(8,128)(2,1)S(1)} collective-permute-done((bf16[2,64,2048]{2,1,0:T(8,128)(2,1)S(1)}, bf16[2,64,2048]{2,1,0:T(8,128)(2,1)S(1)}, u32[]{:S(2)}, u32[]{:S(2)}) %collective-permute-start.38) | collective-permute-done | bytes 524320 | tf_op jit(solution)/shard_map/ppermute | solution.py:418
  220.7 8.8 %collective-permute-done.37 = bf16[2,64,2048]{2,1,0:T(8,128)(2,1)S(1)} collective-permute-done((bf16[2,64,2048]{2,1,0:T(8,128)(2,1)S(1)}, bf16[2,64,2048]{2,1,0:T(8,128)(2,1)S(1)}, u32[]{:S(2)}, u32[]{:S(2)}) %collective-permute-start.37) | collective-permute-done | bytes 524320 | tf_op jit(solution)/shard_map/ppermute | solution.py:418
  234.3 9.4 %collective-permute-done.41 = bf16[2,64,2048]{2,1,0:T(8,128)(2,1)S(1)} collective-permute-done((bf16[2,64,2048]{2,1,0:T(8,128)(2,1)S(1)}, bf16[2,64,2048]{2,1,0:T(8,128)(2,1)S(1)}, u32[]{:S(2)}, u32[]{:S(2)}) %collective-permute-start.41) | collective-permute-done | bytes 524320 | tf_op jit(solution)/shard_map/ppermute | solution.py:418
  245.5 2.6 %collective-permute-start.42 = (bf16[64,2048]{1,0:T(8,128)(2,1)S(1)}, bf16[64,2048]{1,0:T(8,128)(2,1)S(1)}, u32[]{:S(2)}, u32[]{:S(2)}) collective-permute-start(bf16[64,2048]{1,0:T(8,128)(2,1)S(1)} %fusion.26), channel_id=1, source_target_pairs={{0,4},{1,5},{2,6},{3,7},{4,0},{5,1},{6,2},{7,3},{8,12},{9,13},{10,... | collective-permute-start | bytes 786440 | tf_op jit(solution)/shard_map/ppermute | solution.py:418
  248.2 8.5 %collective-permute-done.42 = bf16[64,2048]{1,0:T(8,128)(2,1)S(1)} collective-permute-done((bf16[64,2048]{1,0:T(8,128)(2,1)S(1)}, bf16[64,2048]{1,0:T(8,128)(2,1)S(1)}, u32[]{:S(2)}, u32[]{:S(2)}) %collective-permute-start.42) | collective-permute-done | bytes 262176 | tf_op jit(solution)/shard_map/ppermute | solution.py:418
  (236 shorter events, 82.9 us)
Async XLA Ops:
  1.7 30.0 %collective-permute-start.8 = (bf16[64,2048]{1,0:T(8,128)(2,1)}, bf16[64,2048]{1,0:T(8,128)(2,1)}, u32[]{:S(2)}, u32[]{:S(2)}) collective-permute-start(bf16[64,2048]{1,0:T(8,128)(2,1)} %constant_dynamic-slice_fusion), channel_id=1, source_target_pairs={{0,4},{1,5},{2,6},{3,7},{4,0},{5,1},{6,2},{7,3},{8,12},{9,13},{10,... | collective-permute-start | bytes 786440 | tf_op jit(solution)/shard_map/ppermute | solution.py:418
  5.7 23.5 %collective-permute-start.3 = (bf16[64,2048]{1,0:T(8,128)(2,1)}, bf16[64,2048]{1,0:T(8,128)(2,1)S(1)}, u32[]{:S(2)}, u32[]{:S(2)}) collective-permute-start(bf16[64,2048]{1,0:T(8,128)(2,1)} %refs_11_.1), channel_id=1, source_target_pairs={{0,4},{1,5},{2,6},{3,7},{4,0},{5,1},{6,2},{7,3},{8,12},{9,13},{10,... | collective-permute-start | bytes 786440 | tf_op jit(solution)/shard_map/ppermute | solution.py:418
  12.5 23.4 %collective-permute-start = (bf16[592,512]{1,0:T(8,128)(2,1)}, bf16[592,512]{1,0:T(8,128)(2,1)S(1)}, u32[]{:S(2)}, u32[]{:S(2)}) collective-permute-start(bf16[592,512]{1,0:T(8,128)(2,1)} %get-tuple-element.75), channel_id=1, source_target_pairs={{0,1},{1,0},{2,3},{3,2},{4,5},{5,4},{6,7},{7,6},{8,9},{9,8},{10,11... | collective-permute-start | bytes 1818632 | tf_op jit(solution)/shard_map/ppermute | solution.py:418
  14.3 35.0 %collective-permute-start.1 = (bf16[592,512]{1,0:T(8,128)(2,1)}, bf16[592,512]{1,0:T(8,128)(2,1)S(1)}, u32[]{:S(2)}, u32[]{:S(2)}) collective-permute-start(bf16[592,512]{1,0:T(8,128)(2,1)} %get-tuple-element.76), channel_id=1, source_target_pairs={{0,2},{1,3},{2,0},{3,1},{4,6},{5,7},{6,4},{7,5},{8,10},{9,11},{10,... | collective-permute-start | bytes 1818632 | tf_op jit(solution)/shard_map/ppermute | solution.py:418
  15.9 37.7 %collective-permute-start.2 = (bf16[592,512]{1,0:T(8,128)(2,1)}, bf16[592,512]{1,0:T(8,128)(2,1)S(1)}, u32[]{:S(2)}, u32[]{:S(2)}) collective-permute-start(bf16[592,512]{1,0:T(8,128)(2,1)} %get-tuple-element.77), channel_id=1, source_target_pairs={{0,3},{1,2},{2,1},{3,0},{4,7},{5,6},{6,5},{7,4},{8,11},{9,10},{10,... | collective-permute-start | bytes 1818632 | tf_op jit(solution)/shard_map/ppermute | solution.py:418
  31.7 24.8 %collective-permute-start.5 = (bf16[64,512]{1,0:T(8,128)(2,1)S(1)}, bf16[64,512]{1,0:T(8,128)(2,1)S(1)}, u32[]{:S(2)}, u32[]{:S(2)}) collective-permute-start(bf16[64,512]{1,0:T(8,128)(2,1)S(1)} %get-tuple-element.84), channel_id=1, source_target_pairs={{0,2},{1,3},{2,0},{3,1},{4,6},{5,7},{6,4},{7,5},{8,10},{9,11},{10,... | collective-permute-start | bytes 196616 | tf_op jit(solution)/shard_map/ppermute | solution.py:418
  34.3 26.7 %collective-permute-start.9 = (bf16[64,2048]{1,0:T(8,128)(2,1)}, bf16[64,2048]{1,0:T(8,128)(2,1)S(1)}, u32[]{:S(2)}, u32[]{:S(2)}) collective-permute-start(bf16[64,2048]{1,0:T(8,128)(2,1)} %collective-permute-done.8.refs_0_), channel_id=1, source_target_pairs={{0,16},{8,24},{16,0},{24,8},{1,17},{9,25},{17,1},{25,9},{2,18},{10... | collective-permute-start | bytes 786440 | tf_op jit(solution)/shard_map/ppermute | solution.py:432
  35.9 20.6 %collective-permute-start.6 = (bf16[64,512]{1,0:T(8,128)(2,1)S(1)}, bf16[64,512]{1,0:T(8,128)(2,1)S(1)}, u32[]{:S(2)}, u32[]{:S(2)}) collective-permute-start(bf16[64,512]{1,0:T(8,128)(2,1)S(1)} %get-tuple-element.85), channel_id=1, source_target_pairs={{0,3},{1,2},{2,1},{3,0},{4,7},{5,6},{6,5},{7,4},{8,11},{9,10},{10,... | collective-permute-start | bytes 196616 | tf_op jit(solution)/shard_map/ppermute | solution.py:418
  61.1 12.5 %collective-permute-start.13 = (bf16[512,256]{1,0:T(8,128)(2,1)S(1)}, bf16[512,256]{1,0:T(8,128)(2,1)S(1)}, u32[]{:S(2)}, u32[]{:S(2)}) collective-permute-start(bf16[512,256]{1,0:T(8,128)(2,1)S(1)} %get-tuple-element.93), channel_id=1, source_target_pairs={{0,4},{1,5},{2,6},{3,7},{4,0},{5,1},{6,2},{7,3},{8,12},{9,13},{10,... | collective-permute-start | bytes 786440 | tf_op jit(solution)/shard_map/ppermute | solution.py:418
  75.8 10.0 %collective-permute-start.16 = (bf16[64,2048]{1,0:T(8,128)(2,1)S(1)}, bf16[64,2048]{1,0:T(8,128)(2,1)S(1)}, u32[]{:S(2)}, u32[]{:S(2)}) collective-permute-start(bf16[64,2048]{1,0:T(8,128)(2,1)S(1)} %get-tuple-element.99), channel_id=1, source_target_pairs={{0,1},{1,0},{2,3},{3,2},{4,5},{5,4},{6,7},{7,6},{8,9},{9,8},{10,11... | collective-permute-start | bytes 786440 | tf_op jit(solution)/shard_map/ppermute | solution.py:418
  77.2 11.1 %collective-permute-start.18 = (f32[2,2,2,2,4,64]{5,2,1,3,0,4:T(2,128)S(1)}, f32[2,2,2,2,4,64]{5,2,1,3,0,4:T(2,128)S(1)}, u32[]{:S(2)}, u32[]{:S(2)}) collective-permute-start(f32[2,2,2,2,4,64]{5,2,1,3,0,4:T(2,128)S(1)} %pad_maximum_fusion.1), channel_id=1, source_target_pairs={{0,8},{8,0},{16,24},{24,16},{1,9},{9,1},{17,25},{25,17},{2,10},{10... | collective-permute-start | bytes 49160 | tf_op jit(solution)/shard_map/ppermute | solution.py:428
  85.8 9.1 %collective-permute-start.17 = (bf16[64,2048]{1,0:T(8,128)(2,1)S(1)}, bf16[64,2048]{1,0:T(8,128)(2,1)S(1)}, u32[]{:S(2)}, u32[]{:S(2)}) collective-permute-start(bf16[64,2048]{1,0:T(8,128)(2,1)S(1)} %add_convert_fusion.1), channel_id=1, source_target_pairs={{0,2},{1,3},{2,0},{3,1},{4,6},{5,7},{6,4},{7,5},{8,10},{9,11},{10,... | collective-permute-start | bytes 786440 | tf_op jit(solution)/shard_map/ppermute | solution.py:418
  95.3 14.5 %collective-permute-start.24 = (bf16[64,2048]{1,0:T(8,128)(2,1)S(1)}, bf16[64,2048]{1,0:T(8,128)(2,1)S(1)}, u32[]{:S(2)}, u32[]{:S(2)}) collective-permute-start(bf16[64,2048]{1,0:T(8,128)(2,1)S(1)} %multiply_convert_fusion.refs_0_), channel_id=1, source_target_pairs={{0,4},{1,5},{2,6},{3,7},{4,0},{5,1},{6,2},{7,3},{8,12},{9,13},{10,... | collective-permute-start | bytes 786440 | tf_op jit(solution)/shard_map/ppermute | solution.py:418
  97.0 14.4 %collective-permute-start.21 = (bf16[64,2048]{1,0:T(8,128)(2,1)S(1)}, bf16[64,2048]{1,0:T(8,128)(2,1)S(1)}, u32[]{:S(2)}, u32[]{:S(2)}) collective-permute-start(bf16[64,2048]{1,0:T(8,128)(2,1)S(1)} %multiply_convert_fusion.refs_0_), channel_id=1, source_target_pairs={{0,2},{1,3},{2,0},{3,1},{4,6},{5,7},{6,4},{7,5},{8,10},{9,11},{10,... | collective-permute-start | bytes 786440 | tf_op jit(solution)/shard_map/ppermute | solution.py:418
  98.8 13.2 %collective-permute-start.20 = (bf16[64,2048]{1,0:T(8,128)(2,1)S(1)}, bf16[64,2048]{1,0:T(8,128)(2,1)S(1)}, u32[]{:S(2)}, u32[]{:S(2)}) collective-permute-start(bf16[64,2048]{1,0:T(8,128)(2,1)S(1)} %multiply_convert_fusion.refs_0_), channel_id=1, source_target_pairs={{0,1},{1,0},{2,3},{3,2},{4,5},{5,4},{6,7},{7,6},{8,9},{9,8},{10,11... | collective-permute-start | bytes 786440 | tf_op jit(solution)/shard_map/ppermute | solution.py:418
  100.3 12.7 %collective-permute-start.19 = (bf16[64,2048]{1,0:T(8,128)(2,1)S(1)}, bf16[64,2048]{1,0:T(8,128)(2,1)S(1)}, u32[]{:S(2)}, u32[]{:S(2)}) collective-permute-start(bf16[64,2048]{1,0:T(8,128)(2,1)S(1)} %multiply_convert_fusion.refs_0_), channel_id=1, source_target_pairs={{0,16},{8,24},{16,0},{24,8},{1,17},{9,25},{17,1},{25,9},{2,18},{10... | collective-permute-start | bytes 786440 | tf_op jit(solution)/shard_map/ppermute | solution.py:428
  109.9 9.2 %collective-permute-start.26 = (bf16[64,2048]{1,0:T(8,128)(2,1)S(1)}, bf16[64,2048]{1,0:T(8,128)(2,1)S(1)}, u32[]{:S(2)}, u32[]{:S(2)}) collective-permute-start(bf16[64,2048]{1,0:T(8,128)(2,1)S(1)} %collective-permute-done.24.refs_2_), channel_id=1, source_target_pairs={{0,1},{1,0},{2,3},{3,2},{4,5},{5,4},{6,7},{7,6},{8,9},{9,8},{10,11... | collective-permute-start | bytes 786440 | tf_op jit(solution)/shard_map/ppermute | solution.py:418
  111.4 9.3 %collective-permute-start.25 = (bf16[64,2048]{1,0:T(8,128)(2,1)S(1)}, bf16[64,2048]{1,0:T(8,128)(2,1)S(1)}, u32[]{:S(2)}, u32[]{:S(2)}) collective-permute-start(bf16[64,2048]{1,0:T(8,128)(2,1)S(1)} %collective-permute-done.24.refs_2_), channel_id=1, source_target_pairs={{0,16},{8,24},{16,0},{24,8},{1,17},{9,25},{17,1},{25,9},{2,18},{10... | collective-permute-start | bytes 786440 | tf_op jit(solution)/shard_map/ppermute | solution.py:428
  112.0 12.7 %collective-permute-start.23 = (bf16[64,2048]{1,0:T(8,128)(2,1)S(1)}, bf16[64,2048]{1,0:T(8,128)(2,1)S(1)}, u32[]{:S(2)}, u32[]{:S(2)}) collective-permute-start(bf16[64,2048]{1,0:T(8,128)(2,1)S(1)} %collective-permute-done.21.refs_1_), channel_id=1, source_target_pairs={{0,1},{1,0},{2,3},{3,2},{4,5},{5,4},{6,7},{7,6},{8,9},{9,8},{10,11... | collective-permute-start | bytes 786440 | tf_op jit(solution)/shard_map/ppermute | solution.py:418
  113.0 13.4 %collective-permute-start.22 = (bf16[64,2048]{1,0:T(8,128)(2,1)S(1)}, bf16[64,2048]{1,0:T(8,128)(2,1)S(1)}, u32[]{:S(2)}, u32[]{:S(2)}) collective-permute-start(bf16[64,2048]{1,0:T(8,128)(2,1)S(1)} %collective-permute-done.21.refs_1_), channel_id=1, source_target_pairs={{0,16},{8,24},{16,0},{24,8},{1,17},{9,25},{17,1},{25,9},{2,18},{10... | collective-permute-start | bytes 786440 | tf_op jit(solution)/shard_map/ppermute | solution.py:428
  117.2 11.5 %collective-permute-start.29 = (bf16[64,2048]{1,0:T(8,128)(2,1)S(1)}, bf16[64,2048]{1,0:T(8,128)(2,1)S(1)}, u32[]{:S(2)}, u32[]{:S(2)}) collective-permute-start(bf16[64,2048]{1,0:T(8,128)(2,1)S(1)} %collective-permute-done.27.refs_3_), channel_id=1, source_target_pairs={{0,1},{1,0},{2,3},{3,2},{4,5},{5,4},{6,7},{7,6},{8,9},{9,8},{10,11... | collective-permute-start | bytes 786440 | tf_op jit(solution)/shard_map/ppermute | solution.py:418
  119.1 10.9 %collective-permute-start.28 = (bf16[64,2048]{1,0:T(8,128)(2,1)S(1)}, bf16[64,2048]{1,0:T(8,128)(2,1)}, u32[]{:S(2)}, u32[]{:S(2)}) collective-permute-start(bf16[64,2048]{1,0:T(8,128)(2,1)S(1)} %collective-permute-done.27.refs_3_), channel_id=1, source_target_pairs={{0,16},{8,24},{16,0},{24,8},{1,17},{9,25},{17,1},{25,9},{2,18},{10... | collective-permute-start | bytes 786440 | tf_op jit(solution)/shard_map/ppermute | solution.py:428
  133.0 16.0 %collective-permute-start.30 = (bf16[512,2048]{1,0:T(8,128)(2,1)}, bf16[512,2048]{1,0:T(8,128)(2,1)S(1)}, u32[]{:S(2)}, u32[]{:S(2)}) collective-permute-start(bf16[512,2048]{1,0:T(8,128)(2,1)} %shard_map.187.rows.refs_0_), channel_id=1, source_target_pairs={{0,8},{8,0},{16,24},{24,16},{1,9},{9,1},{17,25},{25,17},{2,10},{10... | collective-permute-start | bytes 6291464 | tf_op jit(solution)/shard_map/ppermute | solution.py:428
  136.5 29.5 %collective-permute-start.31 = (bf16[256,2048]{1,0:T(8,128)(2,1)}, bf16[256,2048]{1,0:T(8,128)(2,1)}, u32[]{:S(2)}, u32[]{:S(2)}) collective-permute-start(bf16[256,2048]{1,0:T(8,128)(2,1)} %shard_map.190.refs_0_), channel_id=1, source_target_pairs={{0,1},{1,0},{2,3},{3,2},{4,5},{5,4},{6,7},{7,6},{8,9},{9,8},{10,11... | collective-permute-start | bytes 3145736 | tf_op jit(solution)/shard_map/ppermute | solution.py:418
  166.6 9.5 %collective-permute-start.34 = (bf16[256,2048]{1,0:T(8,128)(2,1)}, bf16[256,2048]{1,0:T(8,128)(2,1)S(1)}, u32[]{:S(2)}, u32[]{:S(2)}) collective-permute-start(bf16[256,2048]{1,0:T(8,128)(2,1)} %collective-permute-done.31.refs_1_), channel_id=1, source_target_pairs={{0,8},{8,0},{16,24},{24,16},{1,9},{9,1},{17,25},{25,17},{2,10},{10... | collective-permute-start | bytes 3145736 | tf_op jit(solution)/shard_map/ppermute | solution.py:428
  173.9 25.4 %collective-permute-start.35 = (bf16[2,2,64,2048]{3,2,0,1:T(8,128)(2,1)}, bf16[2,2,64,2048]{3,2,0,1:T(8,128)(2,1)S(1)}, u32[]{:S(2)}, u32[]{:S(2)}) collective-permute-start(bf16[2,2,64,2048]{3,2,0,1:T(8,128)(2,1)} %copy.77), channel_id=1, source_target_pairs={{0,1},{1,0},{2,3},{3,2},{4,5},{5,4},{6,7},{7,6},{8,9},{9,8},{10,11... | collective-permute-start | bytes 3145736 | tf_op jit(solution)/shard_map/ppermute | solution.py:418
  204.3 14.8 %collective-permute-start.38 = (bf16[2,64,2048]{2,1,0:T(8,128)(2,1)S(1)}, bf16[2,64,2048]{2,1,0:T(8,128)(2,1)S(1)}, u32[]{:S(2)}, u32[]{:S(2)}) collective-permute-start(bf16[2,64,2048]{2,1,0:T(8,128)(2,1)S(1)} %fusion.22), channel_id=1, source_target_pairs={{0,1},{1,0},{2,3},{3,2},{4,5},{5,4},{6,7},{7,6},{8,9},{9,8},{10,11... | collective-permute-start | bytes 1572872 | tf_op jit(solution)/shard_map/ppermute | solution.py:418
  207.0 22.6 %collective-permute-start.37 = (bf16[2,64,2048]{2,1,0:T(8,128)(2,1)S(1)}, bf16[2,64,2048]{2,1,0:T(8,128)(2,1)S(1)}, u32[]{:S(2)}, u32[]{:S(2)}) collective-permute-start(bf16[2,64,2048]{2,1,0:T(8,128)(2,1)S(1)} %fusion.21), channel_id=1, source_target_pairs={{0,1},{1,0},{2,3},{3,2},{4,5},{5,4},{6,7},{7,6},{8,9},{9,8},{10,11... | collective-permute-start | bytes 1572872 | tf_op jit(solution)/shard_map/ppermute | solution.py:418
  219.4 12.4 %collective-permute-start.39 = (bf16[2,64,2048]{2,1,0:T(8,128)(2,1)S(1)}, bf16[2,64,2048]{2,1,0:T(8,128)(2,1)S(1)}, u32[]{:S(2)}, u32[]{:S(2)}) collective-permute-start(bf16[2,64,2048]{2,1,0:T(8,128)(2,1)S(1)} %fusion.11), channel_id=1, source_target_pairs={{0,16},{8,24},{16,0},{24,8},{1,17},{9,25},{17,1},{25,9},{2,18},{10... | collective-permute-start | bytes 1572872 | tf_op jit(solution)/shard_map/ppermute | solution.py:428
  232.1 11.6 %collective-permute-start.41 = (bf16[2,64,2048]{2,1,0:T(8,128)(2,1)S(1)}, bf16[2,64,2048]{2,1,0:T(8,128)(2,1)S(1)}, u32[]{:S(2)}, u32[]{:S(2)}) collective-permute-start(bf16[2,64,2048]{2,1,0:T(8,128)(2,1)S(1)} %fusion.3), channel_id=1, source_target_pairs={{0,2},{1,3},{2,0},{3,1},{4,6},{5,7},{6,4},{7,5},{8,10},{9,11},{10,... | collective-permute-start | bytes 1572872 | tf_op jit(solution)/shard_map/ppermute | solution.py:418
  234.0 11.1 %collective-permute-start.40 = (bf16[2,64,2048]{2,1,0:T(8,128)(2,1)S(1)}, bf16[2,64,2048]{2,1,0:T(8,128)(2,1)S(1)}, u32[]{:S(2)}, u32[]{:S(2)}) collective-permute-start(bf16[2,64,2048]{2,1,0:T(8,128)(2,1)S(1)} %fusion.15), channel_id=1, source_target_pairs={{0,16},{8,24},{16,0},{24,8},{1,17},{9,25},{17,1},{25,9},{2,18},{10... | collective-permute-start | bytes 1572872 | tf_op jit(solution)/shard_map/ppermute | solution.py:428
  245.5 11.2 %collective-permute-start.42 = (bf16[64,2048]{1,0:T(8,128)(2,1)S(1)}, bf16[64,2048]{1,0:T(8,128)(2,1)S(1)}, u32[]{:S(2)}, u32[]{:S(2)}) collective-permute-start(bf16[64,2048]{1,0:T(8,128)(2,1)S(1)} %fusion.26), channel_id=1, source_target_pairs={{0,4},{1,5},{2,6},{3,7},{4,0},{5,1},{6,2},{7,3},{8,12},{9,13},{10,... | collective-permute-start | bytes 786440 | tf_op jit(solution)/shard_map/ppermute | solution.py:418
  (52 other events, 511.0 us)

commit v8 on v7

--- a/solution.py
+++ b/solution.py
@@ -220,20 +220,24 @@
     return value / (1.0 + jnp.exp(-value))
 
 
-def shared_kernel(rows, scalar, gate_w, up_w, down_w, out, gate_v, up_v, down_v, sems):
+def shared_kernel(count, *refs):
+    pieces, (scalar, gate_w, up_w, down_w, out, gate_v, up_v, down_v, sems) = (
+        refs[:count],
+        refs[count:],
+    )
     copies = [
         pltpu.make_async_copy(src, dst, sems.at[i])
         for i, (src, dst) in enumerate(((gate_w, gate_v), (up_w, up_v), (down_w, down_v)))
     ]
     for copy in copies:
         copy.start()
-    block = rows[...]
+    block = jnp.concatenate([piece[...] for piece in pieces], axis=0)
     logit = jnp.sum(
         block.astype(jnp.float32) * scalar[...].astype(jnp.float32), axis=1, keepdims=True
     )
     scale = 1.0 / (1.0 + jnp.exp(-logit))
+    across = (((1,), (1,)), ((), ()))
     copies[0].wait()
-    across = (((1,), (1,)), ((), ()))
     gate = lax.dot_general(block, gate_v[...], across, preferred_element_type=jnp.float32)
     copies[1].wait()
     upper = lax.dot_general(block, up_v[...], across, preferred_element_type=jnp.float32)
@@ -243,13 +247,15 @@
     out[...] = (scale * result).astype(jnp.bfloat16)
 
 
-def shared_expert(rows, scalar, gate_w, up_w, down_w):
+def shared_expert(pieces, scalar, gate_w, up_w, down_w):
     any_spec = pl.BlockSpec(memory_space=pl.ANY)
     vmem = pl.BlockSpec(memory_space=pltpu.VMEM)
+    rows = sum(piece.shape[0] for piece in pieces)
+    width = pieces[0].shape[1]
     return pl.pallas_call(
-        shared_kernel,
-        out_shape=jax.ShapeDtypeStruct(rows.shape, jnp.bfloat16),
-        in_specs=[vmem, vmem, any_spec, any_spec, any_spec],
+        functools.partial(shared_kernel, len(pieces)),
+        out_shape=jax.ShapeDtypeStruct((rows, width), jnp.bfloat16),
+        in_specs=[vmem] * (len(pieces) + 1) + [any_spec] * 3,
         out_specs=vmem,
         scratch_shapes=[
             pltpu.VMEM(gate_w.shape, jnp.bfloat16),
@@ -257,21 +263,23 @@
             pltpu.VMEM(down_w.shape, jnp.bfloat16),
             pltpu.SemaphoreType.DMA((3,)),
         ],
-        compiler_params=pltpu.CompilerParams(vmem_limit_bytes=48 * 1024 * 1024),
+        compiler_params=pltpu.CompilerParams(vmem_limit_bytes=40 * 1024 * 1024),
         cost_estimate=pl.CostEstimate(
-            flops=6 * rows.shape[0] * gate_w.size,
-            bytes_accessed=6 * gate_w.size + 4 * rows.size,
-            transcendentals=rows.shape[0] * gate_w.shape[0],
-        ),
-    )(rows, scalar.reshape(1, -1), gate_w, up_w, down_w)
-
-
-def routed_kernel(parts, entries, has_extra, *refs):
+            flops=6 * rows * gate_w.size,
+            bytes_accessed=6 * gate_w.size + 4 * rows * width,
+            transcendentals=rows * gate_w.shape[0],
+        ),
+    )(*pieces, scalar.reshape(1, -1), gate_w, up_w, down_w)
+
+
+def routed_kernel(parts, extras, entries, cuts, *refs):
     count, total = len(parts), sum(parts)
     pieces, refs = refs[:total], refs[total:]
-    place, row_gate, extra, gate_w, up_w, down_w = refs[:6]
-    outs, refs = refs[6 : 6 + count], refs[6 + count :]
-    rows, packed, gate_v, up_v, down_v, extra_v, sems = refs
+    place, row_gate = refs[:2]
+    more, refs = refs[2 : 2 + extras], refs[2 + extras :]
+    (gate_w, up_w, down_w), refs = refs[:3], refs[3:]
+    outs, refs = refs[: count * cuts], refs[count * cuts :]
+    rows, packed, gate_v, up_v, down_v, more_v, sems = refs
     moves, chunk_copies = [], []
     for c, n in enumerate(parts):
         at = 0
@@ -280,8 +288,10 @@
             moves.append((piece, rows.at[c, pl.ds(at, piece.shape[0])]))
             at += piece.shape[0]
     moves += [(gate_w.at[0], gate_v), (up_w.at[0], up_v), (down_w.at[0], down_v)]
-    if has_extra:
-        moves.append((extra, extra_v))
+    at = 0
+    for extra in more:
+        moves.append((extra, more_v.at[pl.ds(at, extra.shape[0])]))
+        at += extra.shape[0]
     copies = [
         pltpu.make_async_copy(src, dst, sems.at[i]) for i, (src, dst) in enumerate(moves)
     ]
@@ -308,8 +318,9 @@
     answer = jnp.dot(hidden, down_v[...], preferred_element_type=jnp.float32).astype(
         jnp.bfloat16
     )
-    if has_extra:
-        copies[total + 3].wait()
+    for i in range(extras):
+        copies[total + 3 + i].wait()
+    cut = size // cuts
     for c in range(count):
         scaled = answer[c * entries : (c + 1) * entries, :].astype(jnp.float32) * weights[c]
         placed = lax.dot_general(
@@ -318,12 +329,14 @@
             (((0,), (0,)), ((), ())),
             preferred_element_type=jnp.float32,
         )
-        if c == 0 and has_extra:
-            placed = placed + extra_v[...].astype(jnp.float32)
-        outs[c][...] = placed.astype(jnp.bfloat16)
-
-
-def routed_expert(chunks, place, row_gate, extra, gate_w, up_w, down_w, entries):
+        if c == 0 and extras:
+            placed = placed + more_v[...].astype(jnp.float32)
+        placed = placed.astype(jnp.bfloat16)
+        for k in range(cuts):
+            outs[c * cuts + k][...] = placed[k * cut : (k + 1) * cut, :]
+
+
+def routed_expert(chunks, place, row_gate, more, gate_w, up_w, down_w, entries, cuts):
     count = len(chunks)
     parts = [len(chunk) for chunk in chunks]
     total = sum(parts)
@@ -332,22 +345,21 @@
     hidden = gate_w.shape[2]
     any_spec = pl.BlockSpec(memory_space=pl.ANY)
     vmem = pl.BlockSpec(memory_space=pltpu.VMEM)
-    has_extra = extra is not None
-    if not has_extra:
-        extra = jnp.zeros((16, 128), jnp.bfloat16)
-    return pl.pallas_call(
-        functools.partial(routed_kernel, parts, entries, has_extra),
-        out_shape=[jax.ShapeDtypeStruct((size, width), jnp.bfloat16)] * count,
-        in_specs=[any_spec] * total + [vmem] * 2 + [any_spec] * 4,
-        out_specs=[vmem] * count,
+    out_shape = jax.ShapeDtypeStruct((size // cuts, width), jnp.bfloat16)
+    more_rows = sum(extra.shape[0] for extra in more) if more else 16
+    outs = pl.pallas_call(
+        functools.partial(routed_kernel, parts, len(more), entries, cuts),
+        out_shape=[out_shape] * (count * cuts),
+        in_specs=[any_spec] * total + [vmem] * 2 + [any_spec] * (len(more) + 3),
+        out_specs=[vmem] * (count * cuts),
         scratch_shapes=[
             pltpu.VMEM((count, size, width), jnp.bfloat16),
             pltpu.VMEM((count * entries, width), jnp.bfloat16),
             pltpu.VMEM((width, hidden), jnp.bfloat16),
             pltpu.VMEM((width, hidden), jnp.bfloat16),
             pltpu.VMEM((hidden, width), jnp.bfloat16),
-            pltpu.VMEM(extra.shape, jnp.bfloat16),
-            pltpu.SemaphoreType.DMA((total + 4,)),
+            pltpu.VMEM((more_rows, width), jnp.bfloat16),
+            pltpu.SemaphoreType.DMA((total + 3 + len(more),)),
         ],
         compiler_params=pltpu.CompilerParams(vmem_limit_bytes=56 * 1024 * 1024),
         cost_estimate=pl.CostEstimate(
@@ -355,7 +367,8 @@
             bytes_accessed=6 * gate_w.size + 4 * count * size * width,
             transcendentals=count * entries * hidden,
         ),
-    )(*[piece for chunk in chunks for piece in chunk], place, row_gate, extra, gate_w, up_w, down_w)
+    )(*[piece for chunk in chunks for piece in chunk], place, row_gate, *more, gate_w, up_w, down_w)
+    return [outs[c * cuts : (c + 1) * cuts] for c in range(count)]
 
 
 def rms_normed(stream, norm_gain):
@@ -478,11 +491,30 @@
     hits = (page_table[None, :, :] == page_ids[:, None, None]).astype(i32)
     page_request = jnp.sum(hits * jnp.arange(req_slots, dtype=i32)[None, :, None], axis=(1, 2))
     page_slot = jnp.sum(hits * jnp.arange(max_pages, dtype=i32)[None, None, :], axis=(1, 2))
-    rel_rows = lambda a: a.reshape(exp_count, tok_rows)[rel_exp].reshape(2, 1, -1)
-    row_req, row_pos = rel_rows(row_request), rel_rows(row_position)
+    by_place = lambda a: a.reshape(exp_count, tok_rows)[rel_exp].reshape(2, 1, -1)
+    row_req, row_pos = by_place(row_request), by_place(row_position)
     gates = [block[2 * tokens + tok_rows :, :tok_rows].astype(f32) for block in blocks]
     gates = jnp.stack([g[:TOPK] + g[TOPK : 2 * TOPK] + g[2 * TOPK : 3 * TOPK] for g in gates])
     gates = gates.reshape(2, nx, TOPK, tok_rows)
+
+    slot_ids = jnp.arange(slot_count, dtype=i32)
+    own_mark = slot_ids == own_slot
+    own_expert = jnp.sum(jnp.where(own_mark, slot_expert, 0))
+    twins = slot_expert == own_expert
+    copies = jnp.sum(twins.astype(i32))
+    own_rank = jnp.sum((twins & (slot_ids < own_slot)).astype(i32))
+    rel_rows = jnp.transpose(rel_exp.reshape(2, 2, nx)[:, ::-1], (2, 1, 0)).reshape(-1)
+    rel_slots = (rel_req[:, None] * exp_count + rel_rows[None, :]).reshape(-1)
+    named = (route_expert == own_expert).reshape(slot_count, tok_rows, TOPK)[rel_slots]
+    named = jnp.transpose(named, (0, 2, 1))
+    chunk_rows = exp_count * tok_rows
+    entries = -(-exp_count * capacity // 16) * 16
+    served = jnp.any(named, axis=1) & (rel_slots % copies == own_rank)[:, None]
+    served = served.reshape(ny, nc, chunk_rows)
+    place = jnp.where(served, jnp.cumsum(served.astype(i32), axis=2) - 1, -1)
+    place = place.reshape(ny, nc, 1, chunk_rows)
+
+    place, named, blocks = tie((place, named, blocks))
 
     def attend_half(side, queries):
         return attend(
@@ -506,27 +538,6 @@
     quarters += [send_req(q, 0, dc) for dc in range(1, nc) for q in quarters[:2]]
     mine, level = attend_half(0, [])
     mine, level, gates, quarters = tie((mine, level, gates, quarters))
-
-    slot_ids = jnp.arange(slot_count, dtype=i32)
-    own_mark = slot_ids == own_slot
-    own_expert = jnp.sum(jnp.where(own_mark, slot_expert, 0))
-    twins = slot_expert == own_expert
-    copies = jnp.sum(twins.astype(i32))
-    own_rank = jnp.sum((twins & (slot_ids < own_slot)).astype(i32))
-    gates = jnp.stack([send_req(gates, 0, dc) for dc in range(nc)], axis=1)
-    gates = jnp.transpose(gates, (0, 1, 4, 2, 3, 5, 6)).reshape(slot_count, TOPK, tok_rows)
-    rel_exp = jnp.transpose(rel_exp.reshape(len(zs), nx)).reshape(-1)
-    rel_slots = (rel_req[:, None] * exp_count + rel_exp[None, :]).reshape(-1)
-    named = (route_expert == own_expert).reshape(slot_count, tok_rows, TOPK)[rel_slots]
-    named = jnp.transpose(named, (0, 2, 1))
-    chunk_rows = exp_count * tok_rows
-    entries = -(-exp_count * capacity // 16) * 16
-    row_gate = jnp.sum(jnp.where(named, gates, 0.0), axis=1).reshape(ny, nc, chunk_rows)
-    served = jnp.any(named, axis=1) & (rel_slots % copies == own_rank)[:, None]
-    served = served.reshape(ny, nc, chunk_rows)
-    place = jnp.where(served, jnp.cumsum(served.astype(i32), axis=2) - 1, -1)
-    place = place.reshape(ny, nc, 1, chunk_rows)
-    row_gate = row_gate.reshape(ny, nc, 1, chunk_rows)
 
     stays, comes = {}, {}
     proj = out_proj
@@ -544,88 +555,124 @@
     stream = sum([come.astype(f32) for come in comes[0]], resid.astype(f32) + stays[0])
     stream = stream + line.astype(f32)
     normed = rms_normed(stream, norm_gain)
-    normed, place, row_gate = tie((normed, place, row_gate))
+    gates = jnp.stack([send_req(gates, 0, dc) for dc in range(nc)], axis=1)
+    gates = jnp.transpose(gates[:, :, :, ::-1], (0, 1, 4, 3, 2, 5, 6))
+    gates = gates.reshape(slot_count, TOPK, tok_rows)
+    row_gate = jnp.sum(jnp.where(named, gates, 0.0), axis=1).reshape(ny, nc, 1, chunk_rows)
 
     far_line = send(normed, 1, 0, 0)
     line = [normed, send(normed, 0, 1, 0), far_line, send(far_line, 0, 1, 0)]
-    piece = {}
-    for i in range(len(zs)):
-        piece[i, 0, 0] = line[i]
-        for dx in range(1, nx):
-            piece[i, dx, 0] = send(line[i], 0, 0, dx)
-        for dy in range(1, ny):
-            piece[i, 0, dy] = send_req(line[i], dy, 0)
-    piece = tie(piece)
-    chunk = join([piece[i, dx, 0] for dx in range(nx) for i in range(len(zs))])
-    chunks = {(0, 0): [chunk]}
+    order = [1, 3, 0, 2]
+    over_x = {(i, dx): send(line[i], 0, 0, dx) for i in order for dx in range(1, nx)}
+    over_y = {(i, dy): send_req(line[i], dy, 0) for i in order for dy in range(1, ny)}
+
+    halves = [[line[i] for i in order]]
+    shared_weights = (shared_scalar, shared_gate.T, shared_up.T, shared_down)
+    shared = [shared_expert(halves[0], *shared_weights)]
+    chunks = {(0, 0): [join(halves[0])]}
     for dc in range(1, nc):
-        chunks[0, dc] = [send_req(chunk, 0, dc)]
+        chunks[0, dc] = [send_req(chunks[0, 0][0], 0, dc)]
+    over_x, over_y, shared, row_gate = tie((over_x, over_y, shared, row_gate))
+    for dx in range(1, nx):
+        half = [over_x[i, dx] for i in order]
+        chunks[0, 0].append(join(half))
+        for dc in range(1, nc):
+            chunks[0, dc].append(send_req(chunks[0, 0][dx], 0, dc))
+        halves.append(half)
     for dy in range(1, ny):
-        half = join([piece[i, 0, dy] for i in range(len(zs))])
-        chunks[dy, 0] = [send(half, 0, 0, dx) for dx in range(nx)]
-    extra = shared_expert(chunk, shared_scalar, shared_gate.T, shared_up.T, shared_down)
-    partners = [chunks[0, dc] for dc in range(1, nc)]
-    extra, partners = tie((extra, partners))
-    for dc in range(1, nc):
-        chunks[0, dc] = partners[dc - 1]
-
-    places = lambda part: part.astype(f32).reshape(nx, 2, 2, tok_rows, width)
-    kept, comes = {}, {}
-    for dy in range(ny):
-        answers = routed_expert(
-            [chunks[dy, dc] for dc in range(nc)],
-            place[dy],
-            row_gate[dy],
-            extra,
+        half = join([over_y[i, dy] for i in order])
+        chunks[dy, 0] = [half] + [send(half, 0, 0, dx) for dx in range(1, nx)]
+        for dc in range(1, nc):
+            chunks[dy, dc] = [send_req(half, 0, dc)]
+    for dx in range(1, nx):
+        shared.append(shared_expert(halves[dx], *shared_weights))
+    early = [chunks[0, dc] for dc in range(1, nc)] + [
+        chunks[dy, dc] for dy in range(1, ny) for dc in range(1, nc)
+    ]
+    shared, early = tie((shared, early))
+    names = [(0, dc) for dc in range(1, nc)] + [
+        (dy, dc) for dy in range(1, ny) for dc in range(1, nc)
+    ]
+    for name, chunk in zip(names, early):
+        chunks[name] = chunk
+
+    def answers_of(dy, dcs, more, cuts):
+        return routed_expert(
+            [chunks[dy, dc] for dc in dcs],
+            jnp.concatenate([place[dy, dc : dc + 1] for dc in dcs]),
+            jnp.concatenate([row_gate[dy, dc : dc + 1] for dc in dcs]),
+            more,
             expert_gate,
             expert_up,
             expert_down,
             entries,
+            cuts,
         )
-        extra = None
+
+    def add_up(parts):
+        return sum([part.astype(f32) for part in parts[1:]], parts[0].astype(f32))
+
+    cores = list(range(nc))
+    kept, comes = {}, {}
+    for dy in range(ny - 1):
+        answers = answers_of(dy, cores, shared, nx)
+        shared = []
         if dy:
             answers, comes[dy - 1] = tie((answers, comes[dy - 1]))
-        if dy + 1 < ny:
-            answers, chunks[dy + 1, 0] = tie((answers, chunks[dy + 1, 0]))
-            for dc in range(1, nc):
-                chunks[dy + 1, dc] = [send_req(part, 0, dc) for part in chunks[dy + 1, 0]]
-        parts = [answers[0]] + [send_req(answers[dc], 0, -dc) for dc in range(1, nc)]
-        if dy + 1 < ny:
-            gone = sum([places(p)[1:] for p in parts[1:]], places(parts[0])[1:]).astype(bf16)
-            comes[dy] = [send(gone[dx - 1], 0, 0, -dx) for dx in range(1, nx)]
-            following = [chunks[dy + 1, dc] for dc in range(nc)]
-            following, _ = tie((following, gone))
-            for dc in range(nc):
-                chunks[dy + 1, dc] = following[dc]
-        kept[dy] = parts
-
-    def line_of(dy, dl):
-        line = [places(p)[0, :, dl] for p in kept[dy]]
-        if dy + 1 < ny:
-            line += [come.astype(f32)[:, dl] for come in comes[dy]]
+        answers, chunks[dy + 1, 0] = tie((answers, chunks[dy + 1, 0]))
+        for dc in range(1, nc):
+            chunks[dy + 1, dc] += [send_req(part, 0, dc) for part in chunks[dy + 1, 0][1:]]
+        others = [[send_req(part, 0, -dc) for part in answers[dc][::-1]][::-1] for dc in cores[1:]]
+        kept[dy] = [answers[0][0]] + [other[0] for other in others]
+        gone = [
+            add_up([answers[0][dx]] + [other[dx] for other in others]).astype(bf16)
+            for dx in range(1, nx)
+        ]
+        comes[dy] = [send(go, 0, 0, -dx) for dx, go in enumerate(gone, 1)]
+        following = [chunks[dy + 1, dc] for dc in cores]
+        following, _ = tie((following, gone))
+        for dc in cores:
+            chunks[dy + 1, dc] = following[dc]
+    end = ny - 1
+    others = []
+    for dc in cores[1:]:
+        (answer,) = answers_of(end, [dc], [], 1)
+        chunks[end, 0], _ = tie((chunks[end, 0], answer))
+        others.append(send_req(answer[0], 0, -dc))
+    (answer,) = answers_of(end, [0], shared, 2 * nx)
+    answer, others, comes = tie((answer, others, comes))
+    cut = chunk_rows // (2 * nx)
+
+    last = {}
+    for k in range(2):
+        gone = [
+            add_up(
+                [answer[2 * dx + k]]
+                + [other[(2 * dx + k) * cut : (2 * dx + k + 1) * cut] for other in others]
+            ).astype(bf16)
+            for dx in range(1, nx)
+        ]
+        last[k] = [send(go, 0, 0, -dx) for dx, go in enumerate(gone, 1)]
+        others, _ = tie((others, gone))
+
+    def line_of(dy, k):
+        rows = slice(k * cut, (k + 1) * cut)
+        if dy < end:
+            return add_up([part[rows] for part in kept[dy] + comes[dy]])
+        return add_up([answer[k]] + [other[rows] for other in others] + last[k])
+
+    home = {}
+    for k in range(2):
+        goes = [line_of(dy, k).astype(bf16) for dy in range(1, ny)]
+        if k:
+            goes, home[0] = tie((goes, home[0]))
         else:
-            line += [come.astype(f32) for come in last[dl]]
-        return sum(line[1:], line[0])
-
-    last = {}
-    parts = kept[ny - 1]
-    for dl in (1, 0):
-        gone = sum([places(p)[1:, :, dl] for p in parts[1:]], places(parts[0])[1:, :, dl])
-        gone = gone.astype(bf16)
-        last[dl] = [send(gone[dx - 1], 0, 0, -dx) for dx in range(1, nx)]
-        parts, _ = tie((parts, gone))
-    over_y = {}
-    for dl in (1, 0):
-        goes = [line_of(dy, dl).astype(bf16) for dy in range(1, ny)]
-        if dl:
-            last[0], _ = tie((last[0], goes))
-        else:
-            goes, over_y[1] = tie((goes, over_y[1]))
-        over_y[dl] = [send_req(go, -dy, 0) for dy, go in enumerate(goes, 1)]
-    near = sum([come.astype(f32) for come in over_y[1]], line_of(0, 1)).astype(bf16)
-    near = send(near, 0, 1, 0)
-    total = sum([come.astype(f32) for come in over_y[0]], line_of(0, 0)) + near.astype(f32)
-    total = stream + total[0] + send(total[1].astype(bf16), 1, 0, 0).astype(f32)
+            last[1], _ = tie((last[1], goes))
+        home[k] = [send_req(go, -dy, 0) for dy, go in enumerate(goes, 1)]
+    near = send(add_up([line_of(0, 0)] + home[0]).astype(bf16), 0, 1, 0)
+    total = add_up([line_of(0, 1)] + home[1] + [near])
+    far = send(total[tok_rows:].astype(bf16), 1, 0, 0)
+    total = add_up([stream, total[:tok_rows], far])
     return total.astype(bf16)
 
 

time: 258 us -> 259 us (level)
  starting transfers between devices: 60.8 us -> 44.6 us
  waiting for transfers between devices: 93.9 us -> 104 us
  Pallas kernels: 61.3 us -> 70.6 us
    ppermute x27, starting transfers between devices: 51.7 us -> 36.8 us  [send(): return lax.ppermute(value, 'exp', pairs)]
    ppermute x27, waiting for transfers between devices: 82.7 us -> 94.8 us  [send(): return lax.ppermute(value, 'exp', pairs)]
    pallas_call x3 -> x5, Pallas kernels: 39.5 us -> 47.8 us  [the longest x3 36.4 us: routed_expert(): pl.pallas_call(functools.partial(routed_kernel, parts, len(more), entries...]
    reshape x2 -> x0, other arithmetic: 2.62 us -> none  [shards(): places = lambda part: part.astype(f32).reshape(nx, 2, 2, tok_rows, width)]
    ppermute x15 -> x17, waiting for transfers between devices: 11.2 us -> 8.91 us  [send_req(): return lax.ppermute(value, 'req', pairs)]
    pallas_call x2 -> x3, Pallas kernels: 5.21 us -> 6.82 us  [join(): pl.pallas_call(join_kernel, out_shape=jax.ShapeDtypeStruct((len(parts) *...]
    ppermute x15 -> x17, starting transfers between devices: 7.56 us -> 6.26 us  [send_req(): return lax.ppermute(value, 'req', pairs)]
    unnamed x82 -> x64, local copies, waits for them, and re-layouts: 15.2 us -> 15.7 us
  transfers between devices with their start and end apart: 43 -> 45, of which waited for: 23 -> 17; matrix products, arithmetic and copies ran while one was open for 8% -> 7% of each run, Pallas kernels for 22% -> 23%
where the time goes in v8:
time: 259 us; the launch traced here: 258 us
  waiting for transfers between devices  104 us (40%)
  Pallas kernels  70.6 us (27%)
  starting transfers between devices  44.6 us (17%)
  local copies, waits for them, and re-layouts  23.1 us (9%)
  other arithmetic  14.5 us (6%)
    ppermute x27, waiting for transfers between devices, send(): return lax.ppermute(value, 'exp', pairs)  94.8 us
    ppermute x27, starting transfers between devices, send(): return lax.ppermute(value, 'exp', pairs)  36.8 us
    pallas_call x3, Pallas kernels, routed_expert(): pl.pallas_call(functools.partial(routed_kernel, parts, len(more), entries...  36.4 us
    unnamed x64, local copies, waits for them, and re-layouts  15.7 us
    pallas_call x2, Pallas kernels, shared_expert(): pl.pallas_call(functools.partial(shared_kernel, len(pieces)), out_shape=j...  11.4 us
    pallas_call x2, Pallas kernels, attend(): pl.pallas_call(functools.partial(attend_kernel, members, tokens, tok_rows...  10.3 us
    ppermute x17, waiting for transfers between devices, send_req(): return lax.ppermute(value, 'req', pairs)  8.91 us
    pallas_call x3, Pallas kernels, join(): pl.pallas_call(join_kernel, out_shape=jax.ShapeDtypeStruct((len(parts) *...  6.82 us
  transfers between devices with their start and end apart: 45, of which 17 were waited for; matrix products, arithmetic and copies ran while one was open for 7% of the time, Pallas kernels for 23%

profile of v8, /device:TPU:0, one launch (start us, length us, event | category | flops | bytes accessed | tf_op | source)
XLA Modules:
  0.0 258.3 jit_solution(3139072333918743449)
XLA Ops:
  0.0 4.0 %collective-permute-start.3 = (bf16[64,2048]{1,0:T(8,128)(2,1)}, bf16[64,2048]{1,0:T(8,128)(2,1)S(1)}, u32[]{:S(2)}, u32[]{:S(2)}) collective-permute-start(bf16[64,2048]{1,0:T(8,128)(2,1)} %refs_11_.1), channel_id=1, source_target_pairs={{0,4},{1,5},{2,6},{3,7},{4,0},{5,1},{6,2},{7,3},{8,12},{9,13},{10,... | collective-permute-start | bytes 786440 | tf_op jit(solution)/shard_map/ppermute | solution.py:431
  8.2 2.5 shard_map.181
  10.8 2.5 collective-permute-start.2
  26.1 1.9 collective-permute-start.4
  28.1 16.8 %collective-permute-done.8.refs_0_ = bf16[64,2048]{1,0:T(8,128)(2,1)S(1)} collective-permute-done((bf16[64,2048]{1,0:T(8,128)(2,1)}, bf16[64,2048]{1,0:T(8,128)(2,1)S(1)}, u32[]{:S(2)}, u32[]{:S(2)}) %collective-permute-start.8) | collective-permute-done | bytes 262176 | tf_op jit(solution)/shard_map/ppermute | solution.py:431
  49.2 3.3 %collective-permute-start.7 = (f32[2,2,4,64]{3,0,1,2:T(2,128)S(1)}, f32[2,2,4,64]{3,0,1,2:T(2,128)S(1)}, u32[]{:S(2)}, u32[]{:S(2)}) collective-permute-start(f32[2,2,4,64]{3,0,1,2:T(2,128)S(1)} %copy.36), channel_id=1, source_target_pairs={{0,4},{1,5},{2,6},{3,7},{4,0},{5,1},{6,2},{7,3},{8,12},{9,13},{10,... | collective-permute-start | bytes 12296 | tf_op jit(solution)/shard_map/ppermute | solution.py:431
  52.7 5.2 %shard_map.184 = (bf16[512,256]{1,0:T(8,128)(2,1)S(1)}, f32[4,1,256]{2,1,0:T(1,128)S(1)}) custom-call(s32[8]{0:T(128)S(1)} %get-tuple-element.174.page_req, s32[8]{0:T(128)S(1)} %get-tuple-element.173.page_slot, bf16[592,512]{1,0:T(8,128)(2,1)S(1)} %get-tuple-element.93.refs_0_, bf16[592,512]{1,0:T(8,128)(2,1)} %collective-permute-done.refs_1_, ...), custom_call_target="tpu_custom_call" | custom-call | flops 536870912 | bytes 2686976 | tf_op jit(solution)/shard_map/pallas_call | solution.py:112
  58.6 2.2 collective-permute-start.13
  61.3 5.1 %shard_map.182 = (bf16[512,256]{1,0:T(8,128)(2,1)S(1)}, f32[4,1,256]{2,1,0:T(1,128)S(1)}) custom-call(s32[8]{0:T(128)S(1)} %get-tuple-element.174.page_req, s32[8]{0:T(128)S(1)} %get-tuple-element.173.page_slot, bf16[592,512]{1,0:T(8,128)(2,1)S(1)} %get-tuple-element.93.refs_0_, bf16[592,512]{1,0:T(8,128)(2,1)} %collective-permute-done.refs_1_, ...), custom_call_target="tpu_custom_call" | custom-call | flops 536870912 | bytes 2686976 | tf_op jit(solution)/shard_map/pallas_call | solution.py:112
  67.3 6.2 %collective-permute-done.14.their_level = f32[4,1,256]{2,1,0:T(1,128)S(1)} collective-permute-done((f32[4,1,256]{2,1,0:T(1,128)S(1)}, f32[4,1,256]{2,1,0:T(1,128)S(1)}, u32[]{:S(2)}, u32[]{:S(2)}) %collective-permute-start.14) | collective-permute-done | bytes 4128 | tf_op jit(solution)/shard_map/ppermute | solution.py:431
  78.1 5.9 %collective-permute-done.16 = bf16[64,2048]{1,0:T(8,128)(2,1)S(1)} collective-permute-done((bf16[64,2048]{1,0:T(8,128)(2,1)S(1)}, bf16[64,2048]{1,0:T(8,128)(2,1)S(1)}, u32[]{:S(2)}, u32[]{:S(2)}) %collective-permute-start.16) | collective-permute-done | bytes 262176 | tf_op jit(solution)/shard_map/ppermute | solution.py:431
  84.4 3.6 %collective-permute-done.15 = bf16[64,2048]{1,0:T(8,128)(2,1)S(1)} collective-permute-done((bf16[64,2048]{1,0:T(8,128)(2,1)S(1)}, bf16[64,2048]{1,0:T(8,128)(2,1)S(1)}, u32[]{:S(2)}, u32[]{:S(2)}) %collective-permute-start.15) | collective-permute-done | bytes 262176 | tf_op jit(solution)/shard_map/ppermute | solution.py:431
  88.0 2.5 collective-permute-done.17
  91.0 2.0 collective-permute-start.19
  95.9 7.0 %collective-permute-done.19.refs_3_ = bf16[64,2048]{1,0:T(8,128)(2,1)} collective-permute-done((bf16[64,2048]{1,0:T(8,128)(2,1)S(1)}, bf16[64,2048]{1,0:T(8,128)(2,1)}, u32[]{:S(2)}, u32[]{:S(2)}) %collective-permute-start.19) | collective-permute-done | bytes 262176 | tf_op jit(solution)/shard_map/ppermute | solution.py:431
  112.5 2.3 shard_map.187.refs_0_
  114.8 1.8 copy-done.3
  119.4 5.6 %shard_map.188.refs_6_ = bf16[256,2048]{1,0:T(8,128)(2,1)S(1)} custom-call(bf16[64,2048]{1,0:T(8,128)(2,1)} %collective-permute-done.18.refs_0_, bf16[64,2048]{1,0:T(8,128)(2,1)} %collective-permute-done.20.refs_1_, bf16[64,2048]{1,0:T(8,128)(2,1)S(1)} %copy-done.10, bf16[64,2048]{1,0:T(8,128)(2,1)} %collective-permute-done.19.refs_3_, ...), custom_call_target="tpu_custom_call" | custom-call | flops 2214592512 | bytes 10747904 | tf_op jit(solution)/shard_map/pallas_call | solution.py:255
  126.0 1.9 collective-permute-done.28.refs_1_
  127.9 2.2 shard_map.191.refs_0_
  130.2 2.3 shard_map.189.refs_1_
  140.0 5.8 %shard_map.190.refs_7_ = bf16[256,2048]{1,0:T(8,128)(2,1)S(1)} custom-call(bf16[64,2048]{1,0:T(8,128)(2,1)} %collective-permute-done.22.refs_0_, bf16[64,2048]{1,0:T(8,128)(2,1)} %collective-permute-done.24.refs_1_, bf16[64,2048]{1,0:T(8,128)(2,1)S(1)} %copy-done.14, bf16[64,2048]{1,0:T(8,128)(2,1)} %collective-permute-done.23.refs_3_, ...), custom_call_target="tpu_custom_call" | custom-call | flops 2214592512 | bytes 10747904 | tf_op jit(solution)/shard_map/pallas_call | solution.py:255
  147.8 15.2 %shard_map.192 = (bf16[256,2048]{1,0:T(8,128)(2,1)}, bf16[256,2048]{1,0:T(8,128)(2,1)}, bf16[256,2048]{1,0:T(8,128)(2,1)}, bf16[256,2048]{1,0:T(8,128)(2,1)}) custom-call(bf16[256,2048]{1,0:T(8,128)(2,1)} %shard_map.187.refs_0_, bf16[256,2048]{1,0:T(8,128)(2,1)} %shard_map.189.refs_1_, bf16[256,2048]{1,0:T(8,128)(2,1)} %collective-permute-done.30.refs_2_, ...), custom_call_target="tpu_custom_call" | custom-call | flops 8254390272 | bytes 25690112 | tf_op jit(solution)/shard_map/pallas_call | solution.py:350
  163.6 3.1 %collective-permute-done.36 = bf16[256,2048]{1,0:T(8,128)(2,1)S(1)} collective-permute-done((bf16[256,2048]{1,0:T(8,128)(2,1)}, bf16[256,2048]{1,0:T(8,128)(2,1)S(1)}, u32[]{:S(2)}, u32[]{:S(2)}) %collective-permute-start.36) | collective-permute-done | bytes 1048608 | tf_op jit(solution)/shard_map/ppermute | solution.py:441
  169.4 10.6 %shard_map.193 = bf16[512,2048]{1,0:T(8,128)(2,1)} custom-call(bf16[256,2048]{1,0:T(8,128)(2,1)} %collective-permute-done.32.refs_0_, bf16[256,2048]{1,0:T(8,128)(2,1)} %copy-done.18, s32[1,1,512]{2,1,0:T(1,128)} %get-tuple-element.184.refs_2_, f32[1,1,512]{2,1,0:T(1,128)} %get-tuple-element.180.refs_3_, bf16[1,2048,1408]{2,1,0:T(8,128)(2,1)} %refs_4_.3, ...), custom_call_target="tpu_custom_call" | custom-call | flops 4127195136 | bytes 21495808 | tf_op jit(solution)/shard_map/pallas_call | solution.py:350
  181.2 10.6 %shard_map.194 = (bf16[128,2048]{1,0:T(8,128)(2,1)}, bf16[128,2048]{1,0:T(8,128)(2,1)}, bf16[128,2048]{1,0:T(8,128)(2,1)}, bf16[128,2048]{1,0:T(8,128)(2,1)}) custom-call(bf16[256,2048]{1,0:T(8,128)(2,1)} %shard_map.191.refs_0_, bf16[256,2048]{1,0:T(8,128)(2,1)} %copy-done.19, s32[1,1,512]{2,1,0:T(1,128)} %get-tuple-element.183.refs_2_, ...), custom_call_target="tpu_custom_call" | custom-call | flops 4127195136 | bytes 21495808 | tf_op jit(solution)/shard_map/pallas_call | solution.py:350
  191.8 13.8 %collective-permute-done.38 = bf16[256,2048]{1,0:T(8,128)(2,1)S(1)} collective-permute-done((bf16[256,2048]{1,0:T(8,128)(2,1)S(1)}, bf16[256,2048]{1,0:T(8,128)(2,1)S(1)}, u32[]{:S(2)}, u32[]{:S(2)}) %collective-permute-start.38) | collective-permute-done | bytes 1048608 | tf_op jit(solution)/shard_map/ppermute | solution.py:431
  210.1 11.6 %collective-permute-done.40 = bf16[128,2048]{1,0:T(8,128)(2,1)S(1)} collective-permute-done((bf16[128,2048]{1,0:T(8,128)(2,1)S(1)}, bf16[128,2048]{1,0:T(8,128)(2,1)S(1)}, u32[]{:S(2)}, u32[]{:S(2)}) %collective-permute-start.40) | collective-permute-done | bytes 524320 | tf_op jit(solution)/shard_map/ppermute | solution.py:431
  222.3 9.2 %collective-permute-done.39 = bf16[128,2048]{1,0:T(8,128)(2,1)S(1)} collective-permute-done((bf16[128,2048]{1,0:T(8,128)(2,1)S(1)}, bf16[128,2048]{1,0:T(8,128)(2,1)S(1)}, u32[]{:S(2)}, u32[]{:S(2)}) %collective-permute-start.39) | collective-permute-done | bytes 524320 | tf_op jit(solution)/shard_map/ppermute | solution.py:431
  235.4 9.2 %collective-permute-done.43 = bf16[128,2048]{1,0:T(8,128)(2,1)S(1)} collective-permute-done((bf16[128,2048]{1,0:T(8,128)(2,1)S(1)}, bf16[128,2048]{1,0:T(8,128)(2,1)S(1)}, u32[]{:S(2)}, u32[]{:S(2)}) %collective-permute-start.43) | collective-permute-done | bytes 524320 | tf_op jit(solution)/shard_map/ppermute | solution.py:431
  246.5 2.3 collective-permute-start.44
  248.8 8.6 %collective-permute-done.44 = bf16[64,2048]{1,0:T(8,128)(2,1)S(1)} collective-permute-done((bf16[64,2048]{1,0:T(8,128)(2,1)S(1)}, bf16[64,2048]{1,0:T(8,128)(2,1)S(1)}, u32[]{:S(2)}, u32[]{:S(2)}) %collective-permute-start.44) | collective-permute-done | bytes 262176 | tf_op jit(solution)/shard_map/ppermute | solution.py:431
  (223 shorter events, 69.3 us)
Async XLA Ops:
  0.0 25.3 %collective-permute-start.3 = (bf16[64,2048]{1,0:T(8,128)(2,1)}, bf16[64,2048]{1,0:T(8,128)(2,1)S(1)}, u32[]{:S(2)}, u32[]{:S(2)}) collective-permute-start(bf16[64,2048]{1,0:T(8,128)(2,1)} %refs_11_.1), channel_id=1, source_target_pairs={{0,4},{1,5},{2,6},{3,7},{4,0},{5,1},{6,2},{7,3},{8,12},{9,13},{10,... | collective-permute-start | bytes 786440 | tf_op jit(solution)/shard_map/ppermute | solution.py:431
  10.8 36.8 %collective-permute-start.2 = (bf16[592,512]{1,0:T(8,128)(2,1)}, bf16[592,512]{1,0:T(8,128)(2,1)S(1)}, u32[]{:S(2)}, u32[]{:S(2)}) collective-permute-start(bf16[592,512]{1,0:T(8,128)(2,1)} %get-tuple-element.92), channel_id=1, source_target_pairs={{0,3},{1,2},{2,1},{3,0},{4,7},{5,6},{6,5},{7,4},{8,11},{9,10},{10,... | collective-permute-start | bytes 1818632 | tf_op jit(solution)/shard_map/ppermute | solution.py:431
  13.3 35.2 %collective-permute-start.1 = (bf16[592,512]{1,0:T(8,128)(2,1)}, bf16[592,512]{1,0:T(8,128)(2,1)S(1)}, u32[]{:S(2)}, u32[]{:S(2)}) collective-permute-start(bf16[592,512]{1,0:T(8,128)(2,1)} %get-tuple-element.91), channel_id=1, source_target_pairs={{0,2},{1,3},{2,0},{3,1},{4,6},{5,7},{6,4},{7,5},{8,10},{9,11},{10,... | collective-permute-start | bytes 1818632 | tf_op jit(solution)/shard_map/ppermute | solution.py:431
  13.7 34.7 %collective-permute-start = (bf16[592,512]{1,0:T(8,128)(2,1)}, bf16[592,512]{1,0:T(8,128)(2,1)}, u32[]{:S(2)}, u32[]{:S(2)}) collective-permute-start(bf16[592,512]{1,0:T(8,128)(2,1)} %get-tuple-element.90), channel_id=1, source_target_pairs={{0,1},{1,0},{2,3},{3,2},{4,5},{5,4},{6,7},{7,6},{8,9},{9,8},{10,11... | collective-permute-start | bytes 1818632 | tf_op jit(solution)/shard_map/ppermute | solution.py:431
  15.0 29.9 %collective-permute-start.8 = (bf16[64,2048]{1,0:T(8,128)(2,1)}, bf16[64,2048]{1,0:T(8,128)(2,1)S(1)}, u32[]{:S(2)}, u32[]{:S(2)}) collective-permute-start(bf16[64,2048]{1,0:T(8,128)(2,1)} %constant_dynamic-slice_fusion), channel_id=1, source_target_pairs={{0,4},{1,5},{2,6},{3,7},{4,0},{5,1},{6,2},{7,3},{8,12},{9,13},{10,... | collective-permute-start | bytes 786440 | tf_op jit(solution)/shard_map/ppermute | solution.py:431
  26.1 19.9 %collective-permute-start.4 = (bf16[64,512]{1,0:T(8,128)(2,1)S(1)}, bf16[64,512]{1,0:T(8,128)(2,1)S(1)}, u32[]{:S(2)}, u32[]{:S(2)}) collective-permute-start(bf16[64,512]{1,0:T(8,128)(2,1)S(1)} %get-tuple-element.101), channel_id=1, source_target_pairs={{0,1},{1,0},{2,3},{3,2},{4,5},{5,4},{6,7},{7,6},{8,9},{9,8},{10,11... | collective-permute-start | bytes 196616 | tf_op jit(solution)/shard_map/ppermute | solution.py:431
  46.0 11.9 %collective-permute-start.9 = (bf16[64,2048]{1,0:T(8,128)(2,1)S(1)}, bf16[64,2048]{1,0:T(8,128)(2,1)S(1)}, u32[]{:S(2)}, u32[]{:S(2)}) collective-permute-start(bf16[64,2048]{1,0:T(8,128)(2,1)S(1)} %collective-permute-done.8.refs_0_), channel_id=1, source_target_pairs={{0,16},{8,24},{16,0},{24,8},{1,17},{9,25},{17,1},{25,9},{2,18},{10... | collective-permute-start | bytes 786440 | tf_op jit(solution)/shard_map/ppermute | solution.py:445
  58.6 15.0 %collective-permute-start.13 = (bf16[512,256]{1,0:T(8,128)(2,1)S(1)}, bf16[512,256]{1,0:T(8,128)(2,1)S(1)}, u32[]{:S(2)}, u32[]{:S(2)}) collective-permute-start(bf16[512,256]{1,0:T(8,128)(2,1)S(1)} %get-tuple-element.112), channel_id=1, source_target_pairs={{0,4},{1,5},{2,6},{3,7},{4,0},{5,1},{6,2},{7,3},{8,12},{9,13},{10,... | collective-permute-start | bytes 786440 | tf_op jit(solution)/shard_map/ppermute | solution.py:431
  74.7 9.3 %collective-permute-start.16 = (bf16[64,2048]{1,0:T(8,128)(2,1)S(1)}, bf16[64,2048]{1,0:T(8,128)(2,1)S(1)}, u32[]{:S(2)}, u32[]{:S(2)}) collective-permute-start(bf16[64,2048]{1,0:T(8,128)(2,1)S(1)} %get-tuple-element.118), channel_id=1, source_target_pairs={{0,1},{1,0},{2,3},{3,2},{4,5},{5,4},{6,7},{7,6},{8,9},{9,8},{10,11... | collective-permute-start | bytes 786440 | tf_op jit(solution)/shard_map/ppermute | solution.py:431
  77.3 10.7 %collective-permute-start.15 = (bf16[64,2048]{1,0:T(8,128)(2,1)S(1)}, bf16[64,2048]{1,0:T(8,128)(2,1)S(1)}, u32[]{:S(2)}, u32[]{:S(2)}) collective-permute-start(bf16[64,2048]{1,0:T(8,128)(2,1)S(1)} %get-tuple-element.121), channel_id=1, source_target_pairs={{0,1},{1,0},{2,3},{3,2},{4,5},{5,4},{6,7},{7,6},{8,9},{9,8},{10,11... | collective-permute-start | bytes 786440 | tf_op jit(solution)/shard_map/ppermute | solution.py:431
  91.0 12.0 %collective-permute-start.19 = (bf16[64,2048]{1,0:T(8,128)(2,1)S(1)}, bf16[64,2048]{1,0:T(8,128)(2,1)}, u32[]{:S(2)}, u32[]{:S(2)}) collective-permute-start(bf16[64,2048]{1,0:T(8,128)(2,1)S(1)} %multiply_convert_fusion.refs_2_), channel_id=1, source_target_pairs={{0,4},{1,5},{2,6},{3,7},{4,0},{5,1},{6,2},{7,3},{8,12},{9,13},{10,... | collective-permute-start | bytes 786440 | tf_op jit(solution)/shard_map/ppermute | solution.py:431
  93.0 10.4 %collective-permute-start.18 = (bf16[64,2048]{1,0:T(8,128)(2,1)S(1)}, bf16[64,2048]{1,0:T(8,128)(2,1)}, u32[]{:S(2)}, u32[]{:S(2)}) collective-permute-start(bf16[64,2048]{1,0:T(8,128)(2,1)S(1)} %multiply_convert_fusion.refs_2_), channel_id=1, source_target_pairs={{0,2},{1,3},{2,0},{3,1},{4,6},{5,7},{6,4},{7,5},{8,10},{9,11},{10,... | collective-permute-start | bytes 786440 | tf_op jit(solution)/shard_map/ppermute | solution.py:431
  94.8 13.5 %collective-permute-start.21 = (bf16[64,2048]{1,0:T(8,128)(2,1)S(1)}, bf16[64,2048]{1,0:T(8,128)(2,1)S(1)}, u32[]{:S(2)}, u32[]{:S(2)}) collective-permute-start(bf16[64,2048]{1,0:T(8,128)(2,1)S(1)} %multiply_convert_fusion.refs_2_), channel_id=1, source_target_pairs={{0,1},{1,0},{2,3},{3,2},{4,5},{5,4},{6,7},{7,6},{8,9},{9,8},{10,11... | collective-permute-start | bytes 786440 | tf_op jit(solution)/shard_map/ppermute | solution.py:431
  95.3 13.4 %collective-permute-start.25 = (bf16[64,2048]{1,0:T(8,128)(2,1)S(1)}, bf16[64,2048]{1,0:T(8,128)(2,1)}, u32[]{:S(2)}, u32[]{:S(2)}) collective-permute-start(bf16[64,2048]{1,0:T(8,128)(2,1)S(1)} %multiply_convert_fusion.refs_2_), channel_id=1, source_target_pairs={{0,16},{8,24},{16,0},{24,8},{1,17},{9,25},{17,1},{25,9},{2,18},{10... | collective-permute-start | bytes 786440 | tf_op jit(solution)/shard_map/ppermute | solution.py:441
  107.2 18.8 %collective-permute-start.23 = (bf16[64,2048]{1,0:T(8,128)(2,1)}, bf16[64,2048]{1,0:T(8,128)(2,1)}, u32[]{:S(2)}, u32[]{:S(2)}) collective-permute-start(bf16[64,2048]{1,0:T(8,128)(2,1)} %collective-permute-done.19.refs_3_), channel_id=1, source_target_pairs={{0,1},{1,0},{2,3},{3,2},{4,5},{5,4},{6,7},{7,6},{8,9},{9,8},{10,11... | collective-permute-start | bytes 786440 | tf_op jit(solution)/shard_map/ppermute | solution.py:431
  108.3 17.7 %collective-permute-start.26 = (bf16[64,2048]{1,0:T(8,128)(2,1)}, bf16[64,2048]{1,0:T(8,128)(2,1)}, u32[]{:S(2)}, u32[]{:S(2)}) collective-permute-start(bf16[64,2048]{1,0:T(8,128)(2,1)} %collective-permute-done.18.refs_0_), channel_id=1, source_target_pairs={{0,16},{8,24},{16,0},{24,8},{1,17},{9,25},{17,1},{25,9},{2,18},{10... | collective-permute-start | bytes 786440 | tf_op jit(solution)/shard_map/ppermute | solution.py:441
  108.7 17.3 %collective-permute-start.27 = (bf16[64,2048]{1,0:T(8,128)(2,1)}, bf16[64,2048]{1,0:T(8,128)(2,1)}, u32[]{:S(2)}, u32[]{:S(2)}) collective-permute-start(bf16[64,2048]{1,0:T(8,128)(2,1)} %collective-permute-done.19.refs_3_), channel_id=1, source_target_pairs={{0,16},{8,24},{16,0},{24,8},{1,17},{9,25},{17,1},{25,9},{2,18},{10... | collective-permute-start | bytes 786440 | tf_op jit(solution)/shard_map/ppermute | solution.py:441
  110.3 15.7 %collective-permute-start.24 = (bf16[64,2048]{1,0:T(8,128)(2,1)}, bf16[64,2048]{1,0:T(8,128)(2,1)}, u32[]{:S(2)}, u32[]{:S(2)}) collective-permute-start(bf16[64,2048]{1,0:T(8,128)(2,1)} %collective-permute-done.20.refs_1_), channel_id=1, source_target_pairs={{0,1},{1,0},{2,3},{3,2},{4,5},{5,4},{6,7},{7,6},{8,9},{9,8},{10,11... | collective-permute-start | bytes 786440 | tf_op jit(solution)/shard_map/ppermute | solution.py:431
  111.6 16.3 %collective-permute-start.28 = (bf16[64,2048]{1,0:T(8,128)(2,1)}, bf16[64,2048]{1,0:T(8,128)(2,1)}, u32[]{:S(2)}, u32[]{:S(2)}) collective-permute-start(bf16[64,2048]{1,0:T(8,128)(2,1)} %collective-permute-done.20.refs_1_), channel_id=1, source_target_pairs={{0,16},{8,24},{16,0},{24,8},{1,17},{9,25},{17,1},{25,9},{2,18},{10... | collective-permute-start | bytes 786440 | tf_op jit(solution)/shard_map/ppermute | solution.py:441
  126.0 20.9 %collective-permute-start.30 = (bf16[256,2048]{1,0:T(8,128)(2,1)}, bf16[256,2048]{1,0:T(8,128)(2,1)}, u32[]{:S(2)}, u32[]{:S(2)}) collective-permute-start(bf16[256,2048]{1,0:T(8,128)(2,1)} %shard_map.187.refs_0_), channel_id=1, source_target_pairs={{0,8},{8,0},{16,24},{24,16},{1,9},{9,1},{17,25},{25,17},{2,10},{10... | collective-permute-start | bytes 3145736 | tf_op jit(solution)/shard_map/ppermute | solution.py:441
  130.1 16.7 %collective-permute-start.32 = (bf16[256,2048]{1,0:T(8,128)(2,1)}, bf16[256,2048]{1,0:T(8,128)(2,1)}, u32[]{:S(2)}, u32[]{:S(2)}) collective-permute-start(bf16[256,2048]{1,0:T(8,128)(2,1)} %shard_map.191.refs_0_), channel_id=1, source_target_pairs={{0,8},{8,0},{16,24},{24,16},{1,9},{9,1},{17,25},{25,17},{2,10},{10... | collective-permute-start | bytes 3145736 | tf_op jit(solution)/shard_map/ppermute | solution.py:441
  132.5 14.4 %collective-permute-start.31 = (bf16[256,2048]{1,0:T(8,128)(2,1)}, bf16[256,2048]{1,0:T(8,128)(2,1)S(1)}, u32[]{:S(2)}, u32[]{:S(2)}) collective-permute-start(bf16[256,2048]{1,0:T(8,128)(2,1)} %shard_map.189.refs_1_), channel_id=1, source_target_pairs={{0,8},{8,0},{16,24},{24,16},{1,9},{9,1},{17,25},{25,17},{2,10},{10... | collective-permute-start | bytes 3145736 | tf_op jit(solution)/shard_map/ppermute | solution.py:441
  134.1 28.9 %collective-permute-start.33 = (bf16[256,2048]{1,0:T(8,128)(2,1)}, bf16[256,2048]{1,0:T(8,128)(2,1)S(1)}, u32[]{:S(2)}, u32[]{:S(2)}) collective-permute-start(bf16[256,2048]{1,0:T(8,128)(2,1)} %shard_map.191.refs_0_), channel_id=1, source_target_pairs={{0,1},{1,0},{2,3},{3,2},{4,5},{5,4},{6,7},{7,6},{8,9},{9,8},{10,11... | collective-permute-start | bytes 3145736 | tf_op jit(solution)/shard_map/ppermute | solution.py:431
  180.0 25.6 %collective-permute-start.37 = (bf16[512,2048]{1,0:T(8,128)(2,1)}, bf16[512,2048]{1,0:T(8,128)(2,1)S(1)}, u32[]{:S(2)}, u32[]{:S(2)}) collective-permute-start(bf16[512,2048]{1,0:T(8,128)(2,1)} %shard_map.193), channel_id=1, source_target_pairs={{0,8},{8,0},{16,24},{24,16},{1,9},{9,1},{17,25},{25,17},{2,10},{10... | collective-permute-start | bytes 6291464 | tf_op jit(solution)/shard_map/ppermute | solution.py:441
  180.2 25.4 %collective-permute-start.38 = (bf16[256,2048]{1,0:T(8,128)(2,1)S(1)}, bf16[256,2048]{1,0:T(8,128)(2,1)S(1)}, u32[]{:S(2)}, u32[]{:S(2)}) collective-permute-start(bf16[256,2048]{1,0:T(8,128)(2,1)S(1)} %add_convert_fusion), channel_id=1, source_target_pairs={{0,1},{1,0},{2,3},{3,2},{4,5},{5,4},{6,7},{7,6},{8,9},{9,8},{10,11... | collective-permute-start | bytes 3145736 | tf_op jit(solution)/shard_map/ppermute | solution.py:431
  206.8 14.9 %collective-permute-start.40 = (bf16[128,2048]{1,0:T(8,128)(2,1)S(1)}, bf16[128,2048]{1,0:T(8,128)(2,1)S(1)}, u32[]{:S(2)}, u32[]{:S(2)}) collective-permute-start(bf16[128,2048]{1,0:T(8,128)(2,1)S(1)} %add_convert_fusion.5), channel_id=1, source_target_pairs={{0,1},{1,0},{2,3},{3,2},{4,5},{5,4},{6,7},{7,6},{8,9},{9,8},{10,11... | collective-permute-start | bytes 1572872 | tf_op jit(solution)/shard_map/ppermute | solution.py:431
  207.8 25.2 %collective-permute-start.34 = (bf16[256,2048]{1,0:T(8,128)(2,1)S(1)}, bf16[256,2048]{1,0:T(8,128)(2,1)S(1)}, u32[]{:S(2)}, u32[]{:S(2)}) collective-permute-start(bf16[256,2048]{1,0:T(8,128)(2,1)S(1)} %copy-done.30), channel_id=1, source_target_pairs={{0,8},{8,0},{16,24},{24,16},{1,9},{9,1},{17,25},{25,17},{2,10},{10... | collective-permute-start | bytes 3145736 | tf_op jit(solution)/shard_map/ppermute | solution.py:441
  209.0 22.5 %collective-permute-start.39 = (bf16[128,2048]{1,0:T(8,128)(2,1)S(1)}, bf16[128,2048]{1,0:T(8,128)(2,1)S(1)}, u32[]{:S(2)}, u32[]{:S(2)}) collective-permute-start(bf16[128,2048]{1,0:T(8,128)(2,1)S(1)} %add_convert_fusion.4), channel_id=1, source_target_pairs={{0,1},{1,0},{2,3},{3,2},{4,5},{5,4},{6,7},{7,6},{8,9},{9,8},{10,11... | collective-permute-start | bytes 1572872 | tf_op jit(solution)/shard_map/ppermute | solution.py:431
  222.0 11.1 %collective-permute-start.41 = (bf16[128,2048]{1,0:T(8,128)(2,1)S(1)}, bf16[128,2048]{1,0:T(8,128)(2,1)S(1)}, u32[]{:S(2)}, u32[]{:S(2)}) collective-permute-start(bf16[128,2048]{1,0:T(8,128)(2,1)S(1)} %add_convert_fusion.3), channel_id=1, source_target_pairs={{0,16},{8,24},{16,0},{24,8},{1,17},{9,25},{17,1},{25,9},{2,18},{10... | collective-permute-start | bytes 1572872 | tf_op jit(solution)/shard_map/ppermute | solution.py:441
  233.4 11.3 %collective-permute-start.43 = (bf16[128,2048]{1,0:T(8,128)(2,1)S(1)}, bf16[128,2048]{1,0:T(8,128)(2,1)S(1)}, u32[]{:S(2)}, u32[]{:S(2)}) collective-permute-start(bf16[128,2048]{1,0:T(8,128)(2,1)S(1)} %add_convert_fusion.1), channel_id=1, source_target_pairs={{0,2},{1,3},{2,0},{3,1},{4,6},{5,7},{6,4},{7,5},{8,10},{9,11},{10,... | collective-permute-start | bytes 1572872 | tf_op jit(solution)/shard_map/ppermute | solution.py:431
  235.1 10.9 %collective-permute-start.42 = (bf16[128,2048]{1,0:T(8,128)(2,1)S(1)}, bf16[128,2048]{1,0:T(8,128)(2,1)S(1)}, u32[]{:S(2)}, u32[]{:S(2)}) collective-permute-start(bf16[128,2048]{1,0:T(8,128)(2,1)S(1)} %add_convert_fusion.2), channel_id=1, source_target_pairs={{0,16},{8,24},{16,0},{24,8},{1,17},{9,25},{17,1},{25,9},{2,18},{10... | collective-permute-start | bytes 1572872 | tf_op jit(solution)/shard_map/ppermute | solution.py:441
  246.5 11.0 %collective-permute-start.44 = (bf16[64,2048]{1,0:T(8,128)(2,1)S(1)}, bf16[64,2048]{1,0:T(8,128)(2,1)S(1)}, u32[]{:S(2)}, u32[]{:S(2)}) collective-permute-start(bf16[64,2048]{1,0:T(8,128)(2,1)S(1)} %slice.259), channel_id=1, source_target_pairs={{0,4},{1,5},{2,6},{3,7},{4,0},{5,1},{6,2},{7,3},{8,12},{9,13},{10,... | collective-permute-start | bytes 786440 | tf_op jit(solution)/shard_map/ppermute | solution.py:431
  (45 other events, 463.8 us)

commit v9 on v8

--- a/solution.py
+++ b/solution.py
@@ -13,50 +13,54 @@
 Z_CHIPS = 4
 
 
-def pack_kernel(members, *refs):
-    keys, values, queries = (refs[i * members : (i + 1) * members] for i in range(3))
-    gates, blocks = refs[3 * members], refs[3 * members + 1 :]
-    weights = gates[...]
-    high = weights.astype(jnp.bfloat16).astype(jnp.float32)
-    middle = (weights - high).astype(jnp.bfloat16).astype(jnp.float32)
-    low = weights - high - middle
-    weights = jnp.concatenate([high, middle, low, jnp.zeros_like(low)], axis=0)
-    weights = weights.astype(jnp.bfloat16)
+def pack_kernel(members, parts, columns, order, *refs):
+    sources, refs = refs[:parts], refs[parts:]
+    gates, blocks, sems = refs[:-1 - members], refs[-1 - members : -1], refs[-1]
+    copies = []
     for m in range(members):
-        tokens, rows = keys[m].shape[0], queries[m].shape[0]
-        blocks[m][:tokens, :] = keys[m][...]
-        blocks[m][tokens : 2 * tokens, :] = values[m][...]
-        blocks[m][2 * tokens : 2 * tokens + rows, :] = queries[m][...]
-        blocks[m][2 * tokens + rows :, :] = weights
-
-
-def pack_far_kernel(members, *refs):
-    for m in range(members):
-        refs[members + m][...] = refs[m][...]
+        at = 0
+        for source in sources:
+            rows = source.shape[0]
+            for j in range(2):
+                place = pl.multiple_of(order[2 * m + j] * columns, columns)
+                copies.append(
+                    pltpu.make_async_copy(
+                        source.at[:, pl.ds(place, columns)],
+                        blocks[m].at[pl.ds(at, rows), pl.ds(j * columns, columns)],
+                        sems.at[len(copies)],
+                    )
+                )
+            at += rows
+    for copy in copies:
+        copy.start()
+    if gates:
+        weights = gates[0][...]
+        high = weights.astype(jnp.bfloat16).astype(jnp.float32)
+        middle = (weights - high).astype(jnp.bfloat16).astype(jnp.float32)
+        low = weights - high - middle
+        weights = jnp.concatenate([high, middle, low, jnp.zeros_like(low)], axis=0)
+        for m in range(members):
+            blocks[m][at:, :] = weights.astype(jnp.bfloat16)
+    for copy in copies:
+        copy.wait()
 
 
 def pack(parts, gates, order, columns):
     members = order.shape[0] // 2
     rows = sum(p.shape[0] for p in parts) + (0 if gates is None else 4 * gates.shape[0])
-    kernel = functools.partial(pack_far_kernel if gates is None else pack_kernel, members)
-
-    def column(n, m):
-        return pl.BlockSpec((n, columns), lambda j, order: (0, order[2 * m + j]))
-
-    in_specs = [column(p.shape[0], m) for p in parts for m in range(members)]
-    operands = [p for p in parts for m in range(members)]
+    vmem = pl.BlockSpec(memory_space=pltpu.VMEM)
+    in_specs = [pl.BlockSpec(memory_space=pltpu.SMEM)]
+    in_specs += [pl.BlockSpec(memory_space=pl.ANY)] * len(parts)
+    operands = list(parts)
     if gates is not None:
-        in_specs.append(pl.BlockSpec((gates.shape[0], columns), lambda j, order: (0, j)))
+        in_specs.append(vmem)
         operands.append(gates)
     return pl.pallas_call(
-        lambda order, *refs: kernel(*refs),
+        functools.partial(pack_kernel, members, len(parts), columns),
         out_shape=[jax.ShapeDtypeStruct((rows, 2 * columns), parts[0].dtype)] * members,
-        grid_spec=pltpu.PrefetchScalarGridSpec(
-            num_scalar_prefetch=1,
-            grid=(2,),
-            in_specs=in_specs,
-            out_specs=[pl.BlockSpec((rows, columns), lambda j, order: (0, j))] * members,
-        ),
+        in_specs=in_specs,
+        out_specs=[vmem] * members,
+        scratch_shapes=[pltpu.SemaphoreType.DMA((2 * members * len(parts),))],
         compiler_params=pltpu.CompilerParams(vmem_limit_bytes=32 * 1024 * 1024),
         cost_estimate=pl.CostEstimate(
             flops=0, bytes_accessed=8 * members * rows * columns, transcendentals=0
@@ -221,17 +225,21 @@
 
 
 def shared_kernel(count, *refs):
-    pieces, (scalar, gate_w, up_w, down_w, out, gate_v, up_v, down_v, sems) = (
+    pieces, (scalar, gate_w, up_w, down_w, out, rows, gate_v, up_v, down_v, sems) = (
         refs[:count],
         refs[count:],
     )
+    moves = [(gate_w, gate_v), (up_w, up_v), (down_w, down_v)]
+    size = pieces[0].shape[0]
+    moves += [(piece, rows.at[pl.ds(i * size, size)]) for i, piece in enumerate(pieces)]
     copies = [
-        pltpu.make_async_copy(src, dst, sems.at[i])
-        for i, (src, dst) in enumerate(((gate_w, gate_v), (up_w, up_v), (down_w, down_v)))
+        pltpu.make_async_copy(src, dst, sems.at[i]) for i, (src, dst) in enumerate(moves)
     ]
-    for copy in copies:
+    for copy in copies[3:] + copies[:3]:
         copy.start()
-    block = jnp.concatenate([piece[...] for piece in pieces], axis=0)
+    for copy in copies[3:]:
+        copy.wait()
+    block = rows[...]
     logit = jnp.sum(
         block.astype(jnp.float32) * scalar[...].astype(jnp.float32), axis=1, keepdims=True
     )
@@ -255,13 +263,14 @@
     return pl.pallas_call(
         functools.partial(shared_kernel, len(pieces)),
         out_shape=jax.ShapeDtypeStruct((rows, width), jnp.bfloat16),
-        in_specs=[vmem] * (len(pieces) + 1) + [any_spec] * 3,
+        in_specs=[any_spec] * len(pieces) + [vmem] + [any_spec] * 3,
         out_specs=vmem,
         scratch_shapes=[
+            pltpu.VMEM((rows, width), jnp.bfloat16),
             pltpu.VMEM(gate_w.shape, jnp.bfloat16),
             pltpu.VMEM(up_w.shape, jnp.bfloat16),
             pltpu.VMEM(down_w.shape, jnp.bfloat16),
-            pltpu.SemaphoreType.DMA((3,)),
+            pltpu.SemaphoreType.DMA((3 + len(pieces),)),
         ],
         compiler_params=pltpu.CompilerParams(vmem_limit_bytes=40 * 1024 * 1024),
         cost_estimate=pl.CostEstimate(
@@ -584,18 +593,6 @@
         chunks[dy, 0] = [half] + [send(half, 0, 0, dx) for dx in range(1, nx)]
         for dc in range(1, nc):
             chunks[dy, dc] = [send_req(half, 0, dc)]
-    for dx in range(1, nx):
-        shared.append(shared_expert(halves[dx], *shared_weights))
-    early = [chunks[0, dc] for dc in range(1, nc)] + [
-        chunks[dy, dc] for dy in range(1, ny) for dc in range(1, nc)
-    ]
-    shared, early = tie((shared, early))
-    names = [(0, dc) for dc in range(1, nc)] + [
-        (dy, dc) for dy in range(1, ny) for dc in range(1, nc)
-    ]
-    for name, chunk in zip(names, early):
-        chunks[name] = chunk
-
     def answers_of(dy, dcs, more, cuts):
         return routed_expert(
             [chunks[dy, dc] for dc in dcs],
@@ -615,20 +612,26 @@
     cores = list(range(nc))
     kept, comes = {}, {}
     for dy in range(ny - 1):
-        answers = answers_of(dy, cores, shared, nx)
-        shared = []
+        answers = answers_of(dy, cores, [], nx)
         if dy:
             answers, comes[dy - 1] = tie((answers, comes[dy - 1]))
         answers, chunks[dy + 1, 0] = tie((answers, chunks[dy + 1, 0]))
         for dc in range(1, nc):
             chunks[dy + 1, dc] += [send_req(part, 0, dc) for part in chunks[dy + 1, 0][1:]]
         others = [[send_req(part, 0, -dc) for part in answers[dc][::-1]][::-1] for dc in cores[1:]]
-        kept[dy] = [answers[0][0]] + [other[0] for other in others]
-        gone = [
-            add_up([answers[0][dx]] + [other[dx] for other in others]).astype(bf16)
-            for dx in range(1, nx)
+        parts = [answers[0]] + others
+        if not dy:
+            for dx in range(1, nx):
+                halves[dx], _ = tie((halves[dx], answers[0]))
+                shared.append(shared_expert(halves[dx], *shared_weights))
+            parts.append(shared)
+        gone = [add_up([part[dx] for part in parts]).astype(bf16) for dx in range(1, nx)]
+        kept[dy] = [part[0] for part in parts]
+        cut = chunk_rows // (2 * nx)
+        comes[dy] = [
+            [send(go[k * cut : (k + 1) * cut], 0, 0, -dx) for dx, go in enumerate(gone, 1)]
+            for k in range(2)
         ]
-        comes[dy] = [send(go, 0, 0, -dx) for dx, go in enumerate(gone, 1)]
         following = [chunks[dy + 1, dc] for dc in cores]
         following, _ = tie((following, gone))
         for dc in cores:
@@ -637,11 +640,11 @@
     others = []
     for dc in cores[1:]:
         (answer,) = answers_of(end, [dc], [], 1)
+        answer, comes[end - 1][0] = tie((answer, comes[end - 1][0]))
         chunks[end, 0], _ = tie((chunks[end, 0], answer))
         others.append(send_req(answer[0], 0, -dc))
-    (answer,) = answers_of(end, [0], shared, 2 * nx)
+    (answer,) = answers_of(end, [0], [], 2 * nx)
     answer, others, comes = tie((answer, others, comes))
-    cut = chunk_rows // (2 * nx)
 
     last = {}
     for k in range(2):
@@ -658,7 +661,7 @@
     def line_of(dy, k):
         rows = slice(k * cut, (k + 1) * cut)
         if dy < end:
-            return add_up([part[rows] for part in kept[dy] + comes[dy]])
+            return add_up([part[rows] for part in kept[dy]] + comes[dy][k])
         return add_up([answer[k]] + [other[rows] for other in others] + last[k])
 
     home = {}

time: 259 us -> 251 us (0.969)
  local copies, waits for them, and re-layouts: 23.1 us -> 18.3 us
    unnamed x64 -> x60, local copies, waits for them, and re-layouts: 15.7 us -> 10.9 us
    ppermute x17, waiting for transfers between devices: 8.91 us -> 6.26 us  [send_req(): return lax.ppermute(value, 'req', pairs)]
    ppermute x27 -> x28, waiting for transfers between devices: 94.8 us -> 96.1 us  [send(): return lax.ppermute(value, 'exp', pairs)]
    ppermute x27 -> x28, starting transfers between devices: 36.8 us -> 36.2 us  [send(): return lax.ppermute(value, 'exp', pairs)]
  transfers between devices with their start and end apart: 45 -> 46, of which waited for: 17 -> 20; matrix products, arithmetic and copies ran while one was open for 7% -> 7% of each run, Pallas kernels for 23% -> 27%
where the time goes in v9:
time: 251 us; the launch traced here: 250 us
  waiting for transfers between devices  102 us (41%)
  Pallas kernels  70.8 us (28%)
  starting transfers between devices  43.7 us (17%)
  local copies, waits for them, and re-layouts  18.3 us (7%)
  other arithmetic  13 us (5%)
    ppermute x28, waiting for transfers between devices, send(): return lax.ppermute(value, 'exp', pairs)  96.1 us
    pallas_call x3, Pallas kernels, routed_expert(): pl.pallas_call(functools.partial(routed_kernel, parts, len(more), entries...  36.7 us
    ppermute x28, starting transfers between devices, send(): return lax.ppermute(value, 'exp', pairs)  36.2 us
    unnamed x60, local copies, waits for them, and re-layouts  10.9 us
    pallas_call x2, Pallas kernels, shared_expert(): pl.pallas_call(functools.partial(shared_kernel, len(pieces)), out_shape=j...  10.1 us
    pallas_call x2, Pallas kernels, attend(): pl.pallas_call(functools.partial(attend_kernel, members, tokens, tok_rows...  8.93 us
    pallas_call x3, Pallas kernels, join(): pl.pallas_call(join_kernel, out_shape=jax.ShapeDtypeStruct((len(parts) *...  6.8 us
    ppermute x17, waiting for transfers between devices, send_req(): return lax.ppermute(value, 'req', pairs)  6.26 us
  transfers between devices with their start and end apart: 46, of which 20 were waited for; matrix products, arithmetic and copies ran while one was open for 7% of the time, Pallas kernels for 27%

profile of v9, /device:TPU:0, one launch (start us, length us, event | category | flops | bytes accessed | tf_op | source)
XLA Modules:
  0.0 250.0 jit_solution(6864612588208602300)
XLA Ops:
  0.0 4.0 %collective-permute-start.3 = (bf16[64,2048]{1,0:T(8,128)(2,1)}, bf16[64,2048]{1,0:T(8,128)(2,1)}, u32[]{:S(2)}, u32[]{:S(2)}) collective-permute-start(bf16[64,2048]{1,0:T(8,128)(2,1)} %refs_2_.1), channel_id=1, source_target_pairs={{0,4},{1,5},{2,6},{3,7},{4,0},{5,1},{6,2},{7,3},{8,12},{9,13},{10,... | collective-permute-start | bytes 786440 | tf_op jit(solution)/shard_map/ppermute | solution.py:440
  8.2 2.4 shard_map.181
  28.7 16.4 %collective-permute-done.8.refs_0_ = bf16[64,2048]{1,0:T(8,128)(2,1)} collective-permute-done((bf16[64,2048]{1,0:T(8,128)(2,1)}, bf16[64,2048]{1,0:T(8,128)(2,1)}, u32[]{:S(2)}, u32[]{:S(2)}) %collective-permute-start.8) | collective-permute-done | bytes 262176 | tf_op jit(solution)/shard_map/ppermute | solution.py:440
  48.9 3.3 %collective-permute-start.7 = (f32[2,2,4,64]{3,0,1,2:T(2,128)S(1)}, f32[2,2,4,64]{3,0,1,2:T(2,128)S(1)}, u32[]{:S(2)}, u32[]{:S(2)}) collective-permute-start(f32[2,2,4,64]{3,0,1,2:T(2,128)S(1)} %copy.36), channel_id=1, source_target_pairs={{0,4},{1,5},{2,6},{3,7},{4,0},{5,1},{6,2},{7,3},{8,12},{9,13},{10,... | collective-permute-start | bytes 12296 | tf_op jit(solution)/shard_map/ppermute | solution.py:440
  53.2 4.5 %shard_map.184 = (bf16[512,256]{1,0:T(8,128)(2,1)S(1)}, f32[4,1,256]{2,1,0:T(1,128)S(1)}) custom-call(s32[8]{0:T(128)S(1)} %get-tuple-element.178.page_req, s32[8]{0:T(128)S(1)} %get-tuple-element.177.page_slot, bf16[592,512]{1,0:T(8,128)(2,1)S(1)} %get-tuple-element.95.refs_0_, bf16[592,512]{1,0:T(8,128)(2,1)S(1)} %collective-permute-done.refs_1_, ...), custom_call_target="tpu_custom_call" | custom-call | flops 536870912 | bytes 2686976 | tf_op jit(solution)/shard_map/pallas_call | solution.py:116
  58.3 2.1 collective-permute-start.13
  61.1 4.4 %shard_map.182 = (bf16[512,256]{1,0:T(8,128)(2,1)S(1)}, f32[4,1,256]{2,1,0:T(1,128)S(1)}) custom-call(s32[8]{0:T(128)S(1)} %get-tuple-element.178.page_req, s32[8]{0:T(128)S(1)} %get-tuple-element.177.page_slot, bf16[592,512]{1,0:T(8,128)(2,1)S(1)} %get-tuple-element.95.refs_0_, bf16[592,512]{1,0:T(8,128)(2,1)S(1)} %collective-permute-done.refs_1_, ...), custom_call_target="tpu_custom_call" | custom-call | flops 536870912 | bytes 2686976 | tf_op jit(solution)/shard_map/pallas_call | solution.py:116
  66.4 6.9 %collective-permute-done.14.their_level = f32[4,1,256]{2,1,0:T(1,128)S(1)} collective-permute-done((f32[4,1,256]{2,1,0:T(1,128)S(1)}, f32[4,1,256]{2,1,0:T(1,128)S(1)}, u32[]{:S(2)}, u32[]{:S(2)}) %collective-permute-start.14) | collective-permute-done | bytes 4128 | tf_op jit(solution)/shard_map/ppermute | solution.py:440
  73.3 2.1 shard_map.185
  76.1 2.1 shard_map.186
  79.8 5.0 %collective-permute-done.16 = bf16[64,2048]{1,0:T(8,128)(2,1)S(1)} collective-permute-done((bf16[64,2048]{1,0:T(8,128)(2,1)S(1)}, bf16[64,2048]{1,0:T(8,128)(2,1)S(1)}, u32[]{:S(2)}, u32[]{:S(2)}) %collective-permute-start.16) | collective-permute-done | bytes 262176 | tf_op jit(solution)/shard_map/ppermute | solution.py:440
  85.0 3.6 %collective-permute-done.15 = bf16[64,2048]{1,0:T(8,128)(2,1)S(1)} collective-permute-done((bf16[64,2048]{1,0:T(8,128)(2,1)S(1)}, bf16[64,2048]{1,0:T(8,128)(2,1)S(1)}, u32[]{:S(2)}, u32[]{:S(2)}) %collective-permute-start.15) | collective-permute-done | bytes 262176 | tf_op jit(solution)/shard_map/ppermute | solution.py:440
  88.6 2.7 %collective-permute-done.17 = bf16[64,2048]{1,0:T(8,128)(2,1)S(1)} collective-permute-done((bf16[64,2048]{1,0:T(8,128)(2,1)S(1)}, bf16[64,2048]{1,0:T(8,128)(2,1)S(1)}, u32[]{:S(2)}, u32[]{:S(2)}) %collective-permute-start.17) | collective-permute-done | bytes 262176 | tf_op jit(solution)/shard_map/ppermute | solution.py:440
  91.7 1.9 collective-permute-start.19
  96.6 6.9 %collective-permute-done.19.refs_3_ = bf16[64,2048]{1,0:T(8,128)(2,1)} collective-permute-done((bf16[64,2048]{1,0:T(8,128)(2,1)S(1)}, bf16[64,2048]{1,0:T(8,128)(2,1)}, u32[]{:S(2)}, u32[]{:S(2)}) %collective-permute-start.19) | collective-permute-done | bytes 262176 | tf_op jit(solution)/shard_map/ppermute | solution.py:440
  113.3 2.3 shard_map.187.refs_0_
  120.2 5.0 %shard_map.188 = bf16[256,2048]{1,0:T(8,128)(2,1)S(1)} custom-call(bf16[64,2048]{1,0:T(8,128)(2,1)} %collective-permute-done.18.refs_0_, bf16[64,2048]{1,0:T(8,128)(2,1)} %collective-permute-done.20.refs_1_, bf16[64,2048]{1,0:T(8,128)(2,1)S(1)} %copy-done.9, bf16[64,2048]{1,0:T(8,128)(2,1)} %collective-permute-done.19.refs_3_, ...), custom_call_target="tpu_custom_call" | custom-call | flops 2214592512 | bytes 10747904 | tf_op jit(solution)/shard_map/pallas_call | solution.py:263
  126.2 2.3 collective-permute-done.28.refs_1_
  128.5 2.3 shard_map.189.refs_1_
  132.0 2.2 shard_map.191.refs_0_
  136.1 15.2 %shard_map.190 = (bf16[256,2048]{1,0:T(8,128)(2,1)}, bf16[256,2048]{1,0:T(8,128)(2,1)}, bf16[256,2048]{1,0:T(8,128)(2,1)}, bf16[256,2048]{1,0:T(8,128)(2,1)}) custom-call(bf16[256,2048]{1,0:T(8,128)(2,1)} %shard_map.187.refs_0_, bf16[256,2048]{1,0:T(8,128)(2,1)} %shard_map.189.refs_1_, bf16[256,2048]{1,0:T(8,128)(2,1)} %collective-permute-done.30.refs_2_, ...), custom_call_target="tpu_custom_call" | custom-call | flops 8254390272 | bytes 25690112 | tf_op jit(solution)/shard_map/pallas_call | solution.py:359
  151.3 8.8 %collective-permute-done.32.refs_1_ = bf16[256,2048]{1,0:T(8,128)(2,1)} collective-permute-done((bf16[256,2048]{1,0:T(8,128)(2,1)}, bf16[256,2048]{1,0:T(8,128)(2,1)}, u32[]{:S(2)}, u32[]{:S(2)}) %collective-permute-start.32) | collective-permute-done | bytes 1048608 | tf_op jit(solution)/shard_map/ppermute | solution.py:440
  162.5 5.1 %shard_map.192 = bf16[256,2048]{1,0:T(8,128)(2,1)S(1)} custom-call(bf16[64,2048]{1,0:T(8,128)(2,1)} %collective-permute-done.22.refs_0_, bf16[64,2048]{1,0:T(8,128)(2,1)} %collective-permute-done.24.refs_1_, bf16[64,2048]{1,0:T(8,128)(2,1)S(1)} %copy-done.13, bf16[64,2048]{1,0:T(8,128)(2,1)} %collective-permute-done.23.refs_3_, ...), custom_call_target="tpu_custom_call" | custom-call | flops 2214592512 | bytes 10747904 | tf_op jit(solution)/shard_map/pallas_call | solution.py:263
  168.9 10.6 %shard_map.193 = bf16[512,2048]{1,0:T(8,128)(2,1)} custom-call(bf16[256,2048]{1,0:T(8,128)(2,1)} %collective-permute-done.34.refs_0_, bf16[256,2048]{1,0:T(8,128)(2,1)} %collective-permute-done.35.refs_1_, s32[1,1,512]{2,1,0:T(1,128)} %get-tuple-element.190.refs_2_, f32[1,1,512]{2,1,0:T(1,128)} %get-tuple-element.186.refs_3_, ...), custom_call_target="tpu_custom_call" | custom-call | flops 4127195136 | bytes 21495808 | tf_op jit(solution)/shard_map/pallas_call | solution.py:359
  179.5 3.1 %collective-permute-done.37 = bf16[128,2048]{1,0:T(8,128)(2,1)S(1)} collective-permute-done((bf16[128,2048]{1,0:T(8,128)(2,1)S(1)}, bf16[128,2048]{1,0:T(8,128)(2,1)S(1)}, u32[]{:S(2)}, u32[]{:S(2)}) %collective-permute-start.37) | collective-permute-done | bytes 524320 | tf_op jit(solution)/shard_map/ppermute | solution.py:440
  183.3 10.9 %shard_map.194 = (bf16[128,2048]{1,0:T(8,128)(2,1)}, bf16[128,2048]{1,0:T(8,128)(2,1)}, bf16[128,2048]{1,0:T(8,128)(2,1)}, bf16[128,2048]{1,0:T(8,128)(2,1)}) custom-call(bf16[256,2048]{1,0:T(8,128)(2,1)} %shard_map.191.refs_0_, bf16[256,2048]{1,0:T(8,128)(2,1)} %collective-permute-done.32.refs_1_, s32[1,1,512]{2,1,0:T(1,128)} %get-tuple-element.189.refs_2_, ...), custom_call_target="tpu_custom_call" | custom-call | flops 4127195136 | bytes 21495808 | tf_op jit(solution)/shard_map/pallas_call | solution.py:359
  194.2 2.8 %collective-permute-done.39 = bf16[128,2048]{1,0:T(8,128)(2,1)S(1)} collective-permute-done((bf16[128,2048]{1,0:T(8,128)(2,1)S(1)}, bf16[128,2048]{1,0:T(8,128)(2,1)S(1)}, u32[]{:S(2)}, u32[]{:S(2)}) %collective-permute-start.39) | collective-permute-done | bytes 524320 | tf_op jit(solution)/shard_map/ppermute | solution.py:440
  201.5 11.5 %collective-permute-done.41 = bf16[128,2048]{1,0:T(8,128)(2,1)S(1)} collective-permute-done((bf16[128,2048]{1,0:T(8,128)(2,1)S(1)}, bf16[128,2048]{1,0:T(8,128)(2,1)S(1)}, u32[]{:S(2)}, u32[]{:S(2)}) %collective-permute-start.41) | collective-permute-done | bytes 524320 | tf_op jit(solution)/shard_map/ppermute | solution.py:440
  213.9 9.1 %collective-permute-done.40 = bf16[128,2048]{1,0:T(8,128)(2,1)S(1)} collective-permute-done((bf16[128,2048]{1,0:T(8,128)(2,1)S(1)}, bf16[128,2048]{1,0:T(8,128)(2,1)S(1)}, u32[]{:S(2)}, u32[]{:S(2)}) %collective-permute-start.40) | collective-permute-done | bytes 524320 | tf_op jit(solution)/shard_map/ppermute | solution.py:440
  227.4 9.1 %collective-permute-done.44 = bf16[128,2048]{1,0:T(8,128)(2,1)S(1)} collective-permute-done((bf16[128,2048]{1,0:T(8,128)(2,1)S(1)}, bf16[128,2048]{1,0:T(8,128)(2,1)S(1)}, u32[]{:S(2)}, u32[]{:S(2)}) %collective-permute-start.44) | collective-permute-done | bytes 524320 | tf_op jit(solution)/shard_map/ppermute | solution.py:440
  238.2 2.9 %collective-permute-start.45 = (bf16[64,2048]{1,0:T(8,128)(2,1)S(1)}, bf16[64,2048]{1,0:T(8,128)(2,1)S(1)}, u32[]{:S(2)}, u32[]{:S(2)}) collective-permute-start(bf16[64,2048]{1,0:T(8,128)(2,1)S(1)} %slice.269), channel_id=1, source_target_pairs={{0,4},{1,5},{2,6},{3,7},{4,0},{5,1},{6,2},{7,3},{8,12},{9,13},{10,... | collective-permute-start | bytes 786440 | tf_op jit(solution)/shard_map/ppermute | solution.py:440
  241.1 8.1 %collective-permute-done.45 = bf16[64,2048]{1,0:T(8,128)(2,1)S(1)} collective-permute-done((bf16[64,2048]{1,0:T(8,128)(2,1)S(1)}, bf16[64,2048]{1,0:T(8,128)(2,1)S(1)}, u32[]{:S(2)}, u32[]{:S(2)}) %collective-permute-start.45) | collective-permute-done | bytes 262176 | tf_op jit(solution)/shard_map/ppermute | solution.py:440
  (222 shorter events, 68.4 us)
Async XLA Ops:
  0.0 25.4 %collective-permute-start.3 = (bf16[64,2048]{1,0:T(8,128)(2,1)}, bf16[64,2048]{1,0:T(8,128)(2,1)}, u32[]{:S(2)}, u32[]{:S(2)}) collective-permute-start(bf16[64,2048]{1,0:T(8,128)(2,1)} %refs_2_.1), channel_id=1, source_target_pairs={{0,4},{1,5},{2,6},{3,7},{4,0},{5,1},{6,2},{7,3},{8,12},{9,13},{10,... | collective-permute-start | bytes 786440 | tf_op jit(solution)/shard_map/ppermute | solution.py:440
  10.7 37.3 %collective-permute-start = (bf16[592,512]{1,0:T(8,128)(2,1)}, bf16[592,512]{1,0:T(8,128)(2,1)S(1)}, u32[]{:S(2)}, u32[]{:S(2)}) collective-permute-start(bf16[592,512]{1,0:T(8,128)(2,1)} %get-tuple-element.92), channel_id=1, source_target_pairs={{0,1},{1,0},{2,3},{3,2},{4,5},{5,4},{6,7},{7,6},{8,9},{9,8},{10,11... | collective-permute-start | bytes 1818632 | tf_op jit(solution)/shard_map/ppermute | solution.py:440
  12.3 36.5 %collective-permute-start.1 = (bf16[592,512]{1,0:T(8,128)(2,1)}, bf16[592,512]{1,0:T(8,128)(2,1)S(1)}, u32[]{:S(2)}, u32[]{:S(2)}) collective-permute-start(bf16[592,512]{1,0:T(8,128)(2,1)} %get-tuple-element.93), channel_id=1, source_target_pairs={{0,2},{1,3},{2,0},{3,1},{4,6},{5,7},{6,4},{7,5},{8,10},{9,11},{10,... | collective-permute-start | bytes 1818632 | tf_op jit(solution)/shard_map/ppermute | solution.py:440
  13.8 35.0 %collective-permute-start.2 = (bf16[592,512]{1,0:T(8,128)(2,1)}, bf16[592,512]{1,0:T(8,128)(2,1)S(1)}, u32[]{:S(2)}, u32[]{:S(2)}) collective-permute-start(bf16[592,512]{1,0:T(8,128)(2,1)} %get-tuple-element.94), channel_id=1, source_target_pairs={{0,3},{1,2},{2,1},{3,0},{4,7},{5,6},{6,5},{7,4},{8,11},{9,10},{10,... | collective-permute-start | bytes 1818632 | tf_op jit(solution)/shard_map/ppermute | solution.py:440
  15.0 30.2 %collective-permute-start.8 = (bf16[64,2048]{1,0:T(8,128)(2,1)}, bf16[64,2048]{1,0:T(8,128)(2,1)}, u32[]{:S(2)}, u32[]{:S(2)}) collective-permute-start(bf16[64,2048]{1,0:T(8,128)(2,1)} %constant_dynamic-slice_fusion), channel_id=1, source_target_pairs={{0,4},{1,5},{2,6},{3,7},{4,0},{5,1},{6,2},{7,3},{8,12},{9,13},{10,... | collective-permute-start | bytes 786440 | tf_op jit(solution)/shard_map/ppermute | solution.py:440
  26.9 19.6 %collective-permute-start.4 = (bf16[64,512]{1,0:T(8,128)(2,1)S(1)}, bf16[64,512]{1,0:T(8,128)(2,1)S(1)}, u32[]{:S(2)}, u32[]{:S(2)}) collective-permute-start(bf16[64,512]{1,0:T(8,128)(2,1)S(1)} %get-tuple-element.103), channel_id=1, source_target_pairs={{0,1},{1,0},{2,3},{3,2},{4,5},{5,4},{6,7},{7,6},{8,9},{9,8},{10,11... | collective-permute-start | bytes 196616 | tf_op jit(solution)/shard_map/ppermute | solution.py:440
  46.5 11.3 %collective-permute-start.9 = (bf16[64,2048]{1,0:T(8,128)(2,1)}, bf16[64,2048]{1,0:T(8,128)(2,1)S(1)}, u32[]{:S(2)}, u32[]{:S(2)}) collective-permute-start(bf16[64,2048]{1,0:T(8,128)(2,1)} %collective-permute-done.8.refs_0_), channel_id=1, source_target_pairs={{0,16},{8,24},{16,0},{24,8},{1,17},{9,25},{17,1},{25,9},{2,18},{10... | collective-permute-start | bytes 786440 | tf_op jit(solution)/shard_map/ppermute | solution.py:454
  48.9 8.8 %collective-permute-start.7 = (f32[2,2,4,64]{3,0,1,2:T(2,128)S(1)}, f32[2,2,4,64]{3,0,1,2:T(2,128)S(1)}, u32[]{:S(2)}, u32[]{:S(2)}) collective-permute-start(f32[2,2,4,64]{3,0,1,2:T(2,128)S(1)} %copy.36), channel_id=1, source_target_pairs={{0,4},{1,5},{2,6},{3,7},{4,0},{5,1},{6,2},{7,3},{8,12},{9,13},{10,... | collective-permute-start | bytes 12296 | tf_op jit(solution)/shard_map/ppermute | solution.py:440
  58.3 15.0 %collective-permute-start.13 = (bf16[512,256]{1,0:T(8,128)(2,1)S(1)}, bf16[512,256]{1,0:T(8,128)(2,1)S(1)}, u32[]{:S(2)}, u32[]{:S(2)}) collective-permute-start(bf16[512,256]{1,0:T(8,128)(2,1)S(1)} %get-tuple-element.114), channel_id=1, source_target_pairs={{0,4},{1,5},{2,6},{3,7},{4,0},{5,1},{6,2},{7,3},{8,12},{9,13},{10,... | collective-permute-start | bytes 786440 | tf_op jit(solution)/shard_map/ppermute | solution.py:440
  75.5 9.3 %collective-permute-start.16 = (bf16[64,2048]{1,0:T(8,128)(2,1)S(1)}, bf16[64,2048]{1,0:T(8,128)(2,1)S(1)}, u32[]{:S(2)}, u32[]{:S(2)}) collective-permute-start(bf16[64,2048]{1,0:T(8,128)(2,1)S(1)} %get-tuple-element.120), channel_id=1, source_target_pairs={{0,1},{1,0},{2,3},{3,2},{4,5},{5,4},{6,7},{7,6},{8,9},{9,8},{10,11... | collective-permute-start | bytes 786440 | tf_op jit(solution)/shard_map/ppermute | solution.py:440
  78.3 10.3 %collective-permute-start.15 = (bf16[64,2048]{1,0:T(8,128)(2,1)S(1)}, bf16[64,2048]{1,0:T(8,128)(2,1)S(1)}, u32[]{:S(2)}, u32[]{:S(2)}) collective-permute-start(bf16[64,2048]{1,0:T(8,128)(2,1)S(1)} %get-tuple-element.123), channel_id=1, source_target_pairs={{0,1},{1,0},{2,3},{3,2},{4,5},{5,4},{6,7},{7,6},{8,9},{9,8},{10,11... | collective-permute-start | bytes 786440 | tf_op jit(solution)/shard_map/ppermute | solution.py:440
  91.7 11.8 %collective-permute-start.19 = (bf16[64,2048]{1,0:T(8,128)(2,1)S(1)}, bf16[64,2048]{1,0:T(8,128)(2,1)}, u32[]{:S(2)}, u32[]{:S(2)}) collective-permute-start(bf16[64,2048]{1,0:T(8,128)(2,1)S(1)} %multiply_convert_fusion.refs_2_), channel_id=1, source_target_pairs={{0,4},{1,5},{2,6},{3,7},{4,0},{5,1},{6,2},{7,3},{8,12},{9,13},{10,... | collective-permute-start | bytes 786440 | tf_op jit(solution)/shard_map/ppermute | solution.py:440
  93.6 10.4 %collective-permute-start.18 = (bf16[64,2048]{1,0:T(8,128)(2,1)S(1)}, bf16[64,2048]{1,0:T(8,128)(2,1)}, u32[]{:S(2)}, u32[]{:S(2)}) collective-permute-start(bf16[64,2048]{1,0:T(8,128)(2,1)S(1)} %multiply_convert_fusion.refs_2_), channel_id=1, source_target_pairs={{0,2},{1,3},{2,0},{3,1},{4,6},{5,7},{6,4},{7,5},{8,10},{9,11},{10,... | collective-permute-start | bytes 786440 | tf_op jit(solution)/shard_map/ppermute | solution.py:440
  95.4 13.5 %collective-permute-start.21 = (bf16[64,2048]{1,0:T(8,128)(2,1)S(1)}, bf16[64,2048]{1,0:T(8,128)(2,1)S(1)}, u32[]{:S(2)}, u32[]{:S(2)}) collective-permute-start(bf16[64,2048]{1,0:T(8,128)(2,1)S(1)} %multiply_convert_fusion.refs_2_), channel_id=1, source_target_pairs={{0,1},{1,0},{2,3},{3,2},{4,5},{5,4},{6,7},{7,6},{8,9},{9,8},{10,11... | collective-permute-start | bytes 786440 | tf_op jit(solution)/shard_map/ppermute | solution.py:440
  96.0 13.5 %collective-permute-start.25 = (bf16[64,2048]{1,0:T(8,128)(2,1)S(1)}, bf16[64,2048]{1,0:T(8,128)(2,1)}, u32[]{:S(2)}, u32[]{:S(2)}) collective-permute-start(bf16[64,2048]{1,0:T(8,128)(2,1)S(1)} %multiply_convert_fusion.refs_2_), channel_id=1, source_target_pairs={{0,16},{8,24},{16,0},{24,8},{1,17},{9,25},{17,1},{25,9},{2,18},{10... | collective-permute-start | bytes 786440 | tf_op jit(solution)/shard_map/ppermute | solution.py:450
  107.4 18.8 %collective-permute-start.23 = (bf16[64,2048]{1,0:T(8,128)(2,1)}, bf16[64,2048]{1,0:T(8,128)(2,1)}, u32[]{:S(2)}, u32[]{:S(2)}) collective-permute-start(bf16[64,2048]{1,0:T(8,128)(2,1)} %collective-permute-done.19.refs_3_), channel_id=1, source_target_pairs={{0,1},{1,0},{2,3},{3,2},{4,5},{5,4},{6,7},{7,6},{8,9},{9,8},{10,11... | collective-permute-start | bytes 786440 | tf_op jit(solution)/shard_map/ppermute | solution.py:440
  108.9 17.3 %collective-permute-start.26 = (bf16[64,2048]{1,0:T(8,128)(2,1)}, bf16[64,2048]{1,0:T(8,128)(2,1)}, u32[]{:S(2)}, u32[]{:S(2)}) collective-permute-start(bf16[64,2048]{1,0:T(8,128)(2,1)} %collective-permute-done.18.refs_0_), channel_id=1, source_target_pairs={{0,16},{8,24},{16,0},{24,8},{1,17},{9,25},{17,1},{25,9},{2,18},{10... | collective-permute-start | bytes 786440 | tf_op jit(solution)/shard_map/ppermute | solution.py:450
  109.5 16.7 %collective-permute-start.27 = (bf16[64,2048]{1,0:T(8,128)(2,1)}, bf16[64,2048]{1,0:T(8,128)(2,1)}, u32[]{:S(2)}, u32[]{:S(2)}) collective-permute-start(bf16[64,2048]{1,0:T(8,128)(2,1)} %collective-permute-done.19.refs_3_), channel_id=1, source_target_pairs={{0,16},{8,24},{16,0},{24,8},{1,17},{9,25},{17,1},{25,9},{2,18},{10... | collective-permute-start | bytes 786440 | tf_op jit(solution)/shard_map/ppermute | solution.py:450
  110.9 15.3 %collective-permute-start.24 = (bf16[64,2048]{1,0:T(8,128)(2,1)}, bf16[64,2048]{1,0:T(8,128)(2,1)}, u32[]{:S(2)}, u32[]{:S(2)}) collective-permute-start(bf16[64,2048]{1,0:T(8,128)(2,1)} %collective-permute-done.20.refs_1_), channel_id=1, source_target_pairs={{0,1},{1,0},{2,3},{3,2},{4,5},{5,4},{6,7},{7,6},{8,9},{9,8},{10,11... | collective-permute-start | bytes 786440 | tf_op jit(solution)/shard_map/ppermute | solution.py:440
  112.6 15.9 %collective-permute-start.28 = (bf16[64,2048]{1,0:T(8,128)(2,1)}, bf16[64,2048]{1,0:T(8,128)(2,1)}, u32[]{:S(2)}, u32[]{:S(2)}) collective-permute-start(bf16[64,2048]{1,0:T(8,128)(2,1)} %collective-permute-done.20.refs_1_), channel_id=1, source_target_pairs={{0,16},{8,24},{16,0},{24,8},{1,17},{9,25},{17,1},{25,9},{2,18},{10... | collective-permute-start | bytes 786440 | tf_op jit(solution)/shard_map/ppermute | solution.py:450
  126.2 9.9 %collective-permute-start.30 = (bf16[256,2048]{1,0:T(8,128)(2,1)}, bf16[256,2048]{1,0:T(8,128)(2,1)}, u32[]{:S(2)}, u32[]{:S(2)}) collective-permute-start(bf16[256,2048]{1,0:T(8,128)(2,1)} %shard_map.187.refs_0_), channel_id=1, source_target_pairs={{0,8},{8,0},{16,24},{24,16},{1,9},{9,1},{17,25},{25,17},{2,10},{10... | collective-permute-start | bytes 3145736 | tf_op jit(solution)/shard_map/ppermute | solution.py:450
  134.2 25.9 %collective-permute-start.32 = (bf16[256,2048]{1,0:T(8,128)(2,1)}, bf16[256,2048]{1,0:T(8,128)(2,1)}, u32[]{:S(2)}, u32[]{:S(2)}) collective-permute-start(bf16[256,2048]{1,0:T(8,128)(2,1)} %shard_map.191.refs_0_), channel_id=1, source_target_pairs={{0,1},{1,0},{2,3},{3,2},{4,5},{5,4},{6,7},{7,6},{8,9},{9,8},{10,11... | collective-permute-start | bytes 3145736 | tf_op jit(solution)/shard_map/ppermute | solution.py:440
  168.2 14.4 %collective-permute-start.37 = (bf16[128,2048]{1,0:T(8,128)(2,1)S(1)}, bf16[128,2048]{1,0:T(8,128)(2,1)S(1)}, u32[]{:S(2)}, u32[]{:S(2)}) collective-permute-start(bf16[128,2048]{1,0:T(8,128)(2,1)S(1)} %get-tuple-element.184), channel_id=1, source_target_pairs={{0,1},{1,0},{2,3},{3,2},{4,5},{5,4},{6,7},{7,6},{8,9},{9,8},{10,11... | collective-permute-start | bytes 1572872 | tf_op jit(solution)/shard_map/ppermute | solution.py:440
  182.6 14.3 %collective-permute-start.38 = (bf16[512,2048]{1,0:T(8,128)(2,1)}, bf16[512,2048]{1,0:T(8,128)(2,1)S(1)}, u32[]{:S(2)}, u32[]{:S(2)}) collective-permute-start(bf16[512,2048]{1,0:T(8,128)(2,1)} %shard_map.193), channel_id=1, source_target_pairs={{0,8},{8,0},{16,24},{24,16},{1,9},{9,1},{17,25},{25,17},{2,10},{10... | collective-permute-start | bytes 6291464 | tf_op jit(solution)/shard_map/ppermute | solution.py:450
  182.6 14.3 %collective-permute-start.39 = (bf16[128,2048]{1,0:T(8,128)(2,1)S(1)}, bf16[128,2048]{1,0:T(8,128)(2,1)S(1)}, u32[]{:S(2)}, u32[]{:S(2)}) collective-permute-start(bf16[128,2048]{1,0:T(8,128)(2,1)S(1)} %get-tuple-element.183), channel_id=1, source_target_pairs={{0,1},{1,0},{2,3},{3,2},{4,5},{5,4},{6,7},{7,6},{8,9},{9,8},{10,11... | collective-permute-start | bytes 1572872 | tf_op jit(solution)/shard_map/ppermute | solution.py:440
  198.1 14.9 %collective-permute-start.41 = (bf16[128,2048]{1,0:T(8,128)(2,1)S(1)}, bf16[128,2048]{1,0:T(8,128)(2,1)S(1)}, u32[]{:S(2)}, u32[]{:S(2)}) collective-permute-start(bf16[128,2048]{1,0:T(8,128)(2,1)S(1)} %add_convert_fusion.5), channel_id=1, source_target_pairs={{0,1},{1,0},{2,3},{3,2},{4,5},{5,4},{6,7},{7,6},{8,9},{9,8},{10,11... | collective-permute-start | bytes 1572872 | tf_op jit(solution)/shard_map/ppermute | solution.py:440
  198.8 25.9 %collective-permute-start.33 = (bf16[256,2048]{1,0:T(8,128)(2,1)S(1)}, bf16[256,2048]{1,0:T(8,128)(2,1)S(1)}, u32[]{:S(2)}, u32[]{:S(2)}) collective-permute-start(bf16[256,2048]{1,0:T(8,128)(2,1)S(1)} %copy-done.29), channel_id=1, source_target_pairs={{0,8},{8,0},{16,24},{24,16},{1,9},{9,1},{17,25},{25,17},{2,10},{10... | collective-permute-start | bytes 3145736 | tf_op jit(solution)/shard_map/ppermute | solution.py:450
  200.0 23.0 %collective-permute-start.40 = (bf16[128,2048]{1,0:T(8,128)(2,1)S(1)}, bf16[128,2048]{1,0:T(8,128)(2,1)S(1)}, u32[]{:S(2)}, u32[]{:S(2)}) collective-permute-start(bf16[128,2048]{1,0:T(8,128)(2,1)S(1)} %add_convert_fusion.4), channel_id=1, source_target_pairs={{0,1},{1,0},{2,3},{3,2},{4,5},{5,4},{6,7},{7,6},{8,9},{9,8},{10,11... | collective-permute-start | bytes 1572872 | tf_op jit(solution)/shard_map/ppermute | solution.py:440
  213.3 11.5 %collective-permute-start.42 = (bf16[128,2048]{1,0:T(8,128)(2,1)S(1)}, bf16[128,2048]{1,0:T(8,128)(2,1)S(1)}, u32[]{:S(2)}, u32[]{:S(2)}) collective-permute-start(bf16[128,2048]{1,0:T(8,128)(2,1)S(1)} %add_convert_fusion.3), channel_id=1, source_target_pairs={{0,16},{8,24},{16,0},{24,8},{1,17},{9,25},{17,1},{25,9},{2,18},{10... | collective-permute-start | bytes 1572872 | tf_op jit(solution)/shard_map/ppermute | solution.py:450
  225.2 11.3 %collective-permute-start.44 = (bf16[128,2048]{1,0:T(8,128)(2,1)S(1)}, bf16[128,2048]{1,0:T(8,128)(2,1)S(1)}, u32[]{:S(2)}, u32[]{:S(2)}) collective-permute-start(bf16[128,2048]{1,0:T(8,128)(2,1)S(1)} %add_convert_fusion.1), channel_id=1, source_target_pairs={{0,2},{1,3},{2,0},{3,1},{4,6},{5,7},{6,4},{7,5},{8,10},{9,11},{10,... | collective-permute-start | bytes 1572872 | tf_op jit(solution)/shard_map/ppermute | solution.py:440
  226.8 10.9 %collective-permute-start.43 = (bf16[128,2048]{1,0:T(8,128)(2,1)S(1)}, bf16[128,2048]{1,0:T(8,128)(2,1)S(1)}, u32[]{:S(2)}, u32[]{:S(2)}) collective-permute-start(bf16[128,2048]{1,0:T(8,128)(2,1)S(1)} %add_convert_fusion.2), channel_id=1, source_target_pairs={{0,16},{8,24},{16,0},{24,8},{1,17},{9,25},{17,1},{25,9},{2,18},{10... | collective-permute-start | bytes 1572872 | tf_op jit(solution)/shard_map/ppermute | solution.py:450
  238.2 11.0 %collective-permute-start.45 = (bf16[64,2048]{1,0:T(8,128)(2,1)S(1)}, bf16[64,2048]{1,0:T(8,128)(2,1)S(1)}, u32[]{:S(2)}, u32[]{:S(2)}) collective-permute-start(bf16[64,2048]{1,0:T(8,128)(2,1)S(1)} %slice.269), channel_id=1, source_target_pairs={{0,4},{1,5},{2,6},{3,7},{4,0},{5,1},{6,2},{7,3},{8,12},{9,13},{10,... | collective-permute-start | bytes 786440 | tf_op jit(solution)/shard_map/ppermute | solution.py:440
  (44 other events, 506.1 us)

commit v10 on v9

--- a/solution.py
+++ b/solution.py
@@ -61,7 +61,7 @@
         in_specs=in_specs,
         out_specs=[vmem] * members,
         scratch_shapes=[pltpu.SemaphoreType.DMA((2 * members * len(parts),))],
-        compiler_params=pltpu.CompilerParams(vmem_limit_bytes=32 * 1024 * 1024),
+        compiler_params=pltpu.CompilerParams(vmem_limit_bytes=56 * 1024 * 1024),
         cost_estimate=pl.CostEstimate(
             flops=0, bytes_accessed=8 * members * rows * columns, transcendentals=0
         ),
@@ -272,7 +272,7 @@
             pltpu.VMEM(down_w.shape, jnp.bfloat16),
             pltpu.SemaphoreType.DMA((3 + len(pieces),)),
         ],
-        compiler_params=pltpu.CompilerParams(vmem_limit_bytes=40 * 1024 * 1024),
+        compiler_params=pltpu.CompilerParams(vmem_limit_bytes=56 * 1024 * 1024),
         cost_estimate=pl.CostEstimate(
             flops=6 * rows * gate_w.size,
             bytes_accessed=6 * gate_w.size + 4 * rows * width,
@@ -582,17 +582,19 @@
     for dc in range(1, nc):
         chunks[0, dc] = [send_req(chunks[0, 0][0], 0, dc)]
     over_x, over_y, shared, row_gate = tie((over_x, over_y, shared, row_gate))
+    for dy in range(1, ny):
+        half = join([over_y[i, dy] for i in order])
+        chunks[dy, 0] = [half] + [send(half, 0, 0, dx) for dx in range(1, nx)]
+        for dc in range(1, nc):
+            chunks[dy, dc] = [send_req(half, 0, dc)]
+        over_x, _ = tie((over_x, half))
     for dx in range(1, nx):
         half = [over_x[i, dx] for i in order]
         chunks[0, 0].append(join(half))
         for dc in range(1, nc):
             chunks[0, dc].append(send_req(chunks[0, 0][dx], 0, dc))
         halves.append(half)
-    for dy in range(1, ny):
-        half = join([over_y[i, dy] for i in order])
-        chunks[dy, 0] = [half] + [send(half, 0, 0, dx) for dx in range(1, nx)]
-        for dc in range(1, nc):
-            chunks[dy, dc] = [send_req(half, 0, dc)]
+
     def answers_of(dy, dcs, more, cuts):
         return routed_expert(
             [chunks[dy, dc] for dc in dcs],
@@ -611,25 +613,31 @@
 
     cores = list(range(nc))
     kept, comes = {}, {}
+    half_rows = 2 * tok_rows
     for dy in range(ny - 1):
         answers = answers_of(dy, cores, [], nx)
         if dy:
             answers, comes[dy - 1] = tie((answers, comes[dy - 1]))
-        answers, chunks[dy + 1, 0] = tie((answers, chunks[dy + 1, 0]))
-        for dc in range(1, nc):
-            chunks[dy + 1, dc] += [send_req(part, 0, dc) for part in chunks[dy + 1, 0][1:]]
         others = [[send_req(part, 0, -dc) for part in answers[dc][::-1]][::-1] for dc in cores[1:]]
         parts = [answers[0]] + others
-        if not dy:
+        if dy:
+            following = answers[0][0]
+        else:
             for dx in range(1, nx):
                 halves[dx], _ = tie((halves[dx], answers[0]))
                 shared.append(shared_expert(halves[dx], *shared_weights))
             parts.append(shared)
+            following = shared[-1]
+        chunks[dy + 1, 0], _ = tie((chunks[dy + 1, 0], following))
+        for dc in range(1, nc):
+            chunks[dy + 1, dc] += [send_req(part, 0, dc) for part in chunks[dy + 1, 0][1:]]
         gone = [add_up([part[dx] for part in parts]).astype(bf16) for dx in range(1, nx)]
         kept[dy] = [part[0] for part in parts]
-        cut = chunk_rows // (2 * nx)
         comes[dy] = [
-            [send(go[k * cut : (k + 1) * cut], 0, 0, -dx) for dx, go in enumerate(gone, 1)]
+            [
+                send(go[k * half_rows : (k + 1) * half_rows], 0, 0, -dx)
+                for dx, go in enumerate(gone, 1)
+            ]
             for k in range(2)
         ]
         following = [chunks[dy + 1, dc] for dc in cores]
@@ -643,39 +651,42 @@
         answer, comes[end - 1][0] = tie((answer, comes[end - 1][0]))
         chunks[end, 0], _ = tie((chunks[end, 0], answer))
         others.append(send_req(answer[0], 0, -dc))
-    (answer,) = answers_of(end, [0], [], 2 * nx)
+    (answer,) = answers_of(end, [0], [], 4 * nx)
     answer, others, comes = tie((answer, others, comes))
 
+    turns = [1, 3, 0, 2]
+    block = lambda a, p: a[p * tok_rows : (p + 1) * tok_rows]
     last = {}
-    for k in range(2):
+    for p in turns:
         gone = [
-            add_up(
-                [answer[2 * dx + k]]
-                + [other[(2 * dx + k) * cut : (2 * dx + k + 1) * cut] for other in others]
-            ).astype(bf16)
+            add_up([answer[4 * dx + p]] + [block(other, 4 * dx + p) for other in others])
             for dx in range(1, nx)
         ]
-        last[k] = [send(go, 0, 0, -dx) for dx, go in enumerate(gone, 1)]
+        gone = [go.astype(bf16) for go in gone]
+        last[p] = [send(go, 0, 0, -dx) for dx, go in enumerate(gone, 1)]
         others, _ = tie((others, gone))
 
-    def line_of(dy, k):
-        rows = slice(k * cut, (k + 1) * cut)
+    def line_of(dy, p):
         if dy < end:
-            return add_up([part[rows] for part in kept[dy]] + comes[dy][k])
-        return add_up([answer[k]] + [other[rows] for other in others] + last[k])
-
-    home = {}
-    for k in range(2):
-        goes = [line_of(dy, k).astype(bf16) for dy in range(1, ny)]
-        if k:
-            goes, home[0] = tie((goes, home[0]))
-        else:
-            last[1], _ = tie((last[1], goes))
-        home[k] = [send_req(go, -dy, 0) for dy, go in enumerate(goes, 1)]
-    near = send(add_up([line_of(0, 0)] + home[0]).astype(bf16), 0, 1, 0)
-    total = add_up([line_of(0, 1)] + home[1] + [near])
-    far = send(total[tok_rows:].astype(bf16), 1, 0, 0)
-    total = add_up([stream, total[:tok_rows], far])
+            arrived = [block(come, p % 2) for come in comes[dy][p // 2]]
+            return add_up([block(part, p) for part in kept[dy]] + arrived)
+        return add_up([answer[p]] + [block(other, p) for other in others] + last[p])
+
+    home, near = {}, {}
+    for turn, p in enumerate(turns):
+        goes = [line_of(dy, p).astype(bf16) for dy in range(1, ny)]
+        home[p] = [send_req(go, -dy, 0) for dy, go in enumerate(goes, 1)]
+        if turn + 1 < len(turns):
+            after = turns[turn + 1]
+            last[after], _ = tie((last[after], goes))
+    for p in (1, 0):
+        go = add_up([line_of(0, p)] + home[p]).astype(bf16)
+        if p:
+            home[0], _ = tie((home[0], go))
+        near[p] = send(go, 0, 1, 0)
+    far = add_up([line_of(0, 3)] + home[3] + [near[1]]).astype(bf16)
+    far = send(far, 1, 0, 0)
+    total = add_up([stream, line_of(0, 2)] + home[2] + [near[0], far])
     return total.astype(bf16)
 
 

time: 251 us -> 237 us (0.944)
  waiting for transfers between devices: 102 us -> 79 us
  Pallas kernels: 70.8 us -> 78.2 us
  starting transfers between devices: 43.7 us -> 50.5 us
  local copies, waits for them, and re-layouts: 18.3 us -> 11.6 us
    ppermute x28 -> x31, waiting for transfers between devices: 96.1 us -> 75.5 us  [send(): return lax.ppermute(value, 'exp', pairs)]
    unnamed x60 -> x66, local copies, waits for them, and re-layouts: 10.9 us -> 3.27 us
    pallas_call x2, Pallas kernels: 10.1 us -> 15.1 us  [shared_expert(): pl.pallas_call(functools.partial(shared_kernel, len(pieces)), out_shape=j...]
    ppermute x28 -> x31, starting transfers between devices: 36.2 us -> 40.4 us  [send(): return lax.ppermute(value, 'exp', pairs)]
    ppermute x17 -> x19, waiting for transfers between devices: 6.26 us -> 3.48 us  [send_req(): return lax.ppermute(value, 'req', pairs)]
    pallas_call x2, Pallas kernels: 3.94 us -> 6.46 us  [pack(): pl.pallas_call(functools.partial(pack_kernel, members, len(parts), column...]
    ppermute x17 -> x19, starting transfers between devices: 6.05 us -> 8.53 us  [send_req(): return lax.ppermute(value, 'req', pairs)]
  transfers between devices with their start and end apart: 46 -> 51, of which waited for: 20 -> 20; matrix products, arithmetic and copies ran while one was open for 7% -> 9% of each run, Pallas kernels for 27% -> 32%
where the time goes in v10:
time: 237 us; the launch traced here: 236 us
  waiting for transfers between devices  79 us (33%)
  Pallas kernels  78.2 us (33%)
  starting transfers between devices  50.5 us (21%)
  other arithmetic  15.2 us (6%)
  local copies, waits for them, and re-layouts  11.6 us (5%)
    ppermute x31, waiting for transfers between devices, send(): return lax.ppermute(value, 'exp', pairs)  75.5 us
    ppermute x31, starting transfers between devices, send(): return lax.ppermute(value, 'exp', pairs)  40.4 us
    pallas_call x3, Pallas kernels, routed_expert(): pl.pallas_call(functools.partial(routed_kernel, parts, len(more), entries...  36.4 us
    pallas_call x2, Pallas kernels, shared_expert(): pl.pallas_call(functools.partial(shared_kernel, len(pieces)), out_shape=j...  15.1 us
    pallas_call x2, Pallas kernels, attend(): pl.pallas_call(functools.partial(attend_kernel, members, tokens, tok_rows...  9.13 us
    ppermute x19, starting transfers between devices, send_req(): return lax.ppermute(value, 'req', pairs)  8.53 us
    pallas_call x3, Pallas kernels, join(): pl.pallas_call(join_kernel, out_shape=jax.ShapeDtypeStruct((len(parts) *...  6.83 us
    pallas_call x2, Pallas kernels, pack(): pl.pallas_call(functools.partial(pack_kernel, members, len(parts), column...  6.46 us
  transfers between devices with their start and end apart: 51, of which 20 were waited for; matrix products, arithmetic and copies ran while one was open for 9% of the time, Pallas kernels for 32%

profile of v10, /device:TPU:0, one launch (start us, length us, event | category | flops | bytes accessed | tf_op | source)
XLA Modules:
  0.0 236.2 jit_solution(3929735639030423356)
XLA Ops:
  0.0 4.1 %collective-permute-start.3 = (bf16[64,2048]{1,0:T(8,128)(2,1)}, bf16[64,2048]{1,0:T(8,128)(2,1)}, u32[]{:S(2)}, u32[]{:S(2)}) collective-permute-start(bf16[64,2048]{1,0:T(8,128)(2,1)} %refs_2_.1), channel_id=1, source_target_pairs={{0,4},{1,5},{2,6},{3,7},{4,0},{5,1},{6,2},{7,3},{8,12},{9,13},{10,... | collective-permute-start | bytes 786440 | tf_op jit(solution)/shard_map/ppermute | solution.py:440
  6.0 4.1 %shard_map.181 = (bf16[592,512]{1,0:T(8,128)(2,1)}, bf16[592,512]{1,0:T(8,128)(2,1)}, bf16[592,512]{1,0:T(8,128)(2,1)}, bf16[592,512]{1,0:T(8,128)(2,1)}) custom-call(s32[8]{0:T(128)} %stack.156.order, bf16[256,2048]{1,0:T(8,128)(2,1)} %bitcast.89, bf16[256,2048]{1,0:T(8,128)(2,1)} %bitcast.90, bf16[64,2048]{1,0:T(8,128)(2,1)} %refs_2_.1, f32[4,512]{1,0:T(4,128)} %pad.4.refs_3_), custom_call_target="tpu_custom_call" | custom-call | bytes 4849664 | tf_op jit(solution)/shard_map/pallas_call | solution.py:58
  10.2 2.6 %collective-permute-start.2 = (bf16[592,512]{1,0:T(8,128)(2,1)}, bf16[592,512]{1,0:T(8,128)(2,1)S(1)}, u32[]{:S(2)}, u32[]{:S(2)}) collective-permute-start(bf16[592,512]{1,0:T(8,128)(2,1)} %get-tuple-element.105), channel_id=1, source_target_pairs={{0,3},{1,2},{2,1},{3,0},{4,7},{5,6},{6,5},{7,4},{8,11},{9,10},{10,... | collective-permute-start | bytes 1818632 | tf_op jit(solution)/shard_map/ppermute | solution.py:440
  25.9 2.3 shard_map.183
  30.0 14.4 %collective-permute-done.8.refs_0_ = bf16[64,2048]{1,0:T(8,128)(2,1)} collective-permute-done((bf16[64,2048]{1,0:T(8,128)(2,1)}, bf16[64,2048]{1,0:T(8,128)(2,1)}, u32[]{:S(2)}, u32[]{:S(2)}) %collective-permute-start.8) | collective-permute-done | bytes 262176 | tf_op jit(solution)/shard_map/ppermute | solution.py:440
  48.1 3.4 %collective-permute-start.7 = (f32[2,2,4,64]{3,0,1,2:T(2,128)S(1)}, f32[2,2,4,64]{3,0,1,2:T(2,128)S(1)}, u32[]{:S(2)}, u32[]{:S(2)}) collective-permute-start(f32[2,2,4,64]{3,0,1,2:T(2,128)S(1)} %copy.36), channel_id=1, source_target_pairs={{0,4},{1,5},{2,6},{3,7},{4,0},{5,1},{6,2},{7,3},{8,12},{9,13},{10,... | collective-permute-start | bytes 12296 | tf_op jit(solution)/shard_map/ppermute | solution.py:440
  53.7 4.5 %shard_map.184 = (bf16[512,256]{1,0:T(8,128)(2,1)S(1)}, f32[4,1,256]{2,1,0:T(1,128)S(1)}) custom-call(s32[8]{0:T(128)S(1)} %get-tuple-element.200.page_req, s32[8]{0:T(128)S(1)} %get-tuple-element.199.page_slot, bf16[592,512]{1,0:T(8,128)(2,1)S(1)} %copy-done.1, bf16[592,512]{1,0:T(8,128)(2,1)S(1)} %collective-permute-done.refs_1_, ...), custom_call_target="tpu_custom_call" | custom-call | flops 536870912 | bytes 2686976 | tf_op jit(solution)/shard_map/pallas_call | solution.py:116
  61.3 4.6 %shard_map.182 = (bf16[512,256]{1,0:T(8,128)(2,1)S(1)}, f32[4,1,256]{2,1,0:T(1,128)S(1)}) custom-call(s32[8]{0:T(128)S(1)} %get-tuple-element.200.page_req, s32[8]{0:T(128)S(1)} %get-tuple-element.199.page_slot, bf16[592,512]{1,0:T(8,128)(2,1)S(1)} %copy-done.1, bf16[592,512]{1,0:T(8,128)(2,1)S(1)} %collective-permute-done.refs_1_, ...), custom_call_target="tpu_custom_call" | custom-call | flops 536870912 | bytes 2686976 | tf_op jit(solution)/shard_map/pallas_call | solution.py:116
  67.0 6.8 %collective-permute-done.14.their_level = f32[4,1,256]{2,1,0:T(1,128)S(1)} collective-permute-done((f32[4,1,256]{2,1,0:T(1,128)S(1)}, f32[4,1,256]{2,1,0:T(1,128)S(1)}, u32[]{:S(2)}, u32[]{:S(2)}) %collective-permute-start.14) | collective-permute-done | bytes 4128 | tf_op jit(solution)/shard_map/ppermute | solution.py:440
  76.6 2.1 shard_map.186
  80.3 5.0 %collective-permute-done.16 = bf16[64,2048]{1,0:T(8,128)(2,1)S(1)} collective-permute-done((bf16[64,2048]{1,0:T(8,128)(2,1)S(1)}, bf16[64,2048]{1,0:T(8,128)(2,1)S(1)}, u32[]{:S(2)}, u32[]{:S(2)}) %collective-permute-start.16) | collective-permute-done | bytes 262176 | tf_op jit(solution)/shard_map/ppermute | solution.py:440
  85.4 3.7 %collective-permute-done.15 = bf16[64,2048]{1,0:T(8,128)(2,1)S(1)} collective-permute-done((bf16[64,2048]{1,0:T(8,128)(2,1)S(1)}, bf16[64,2048]{1,0:T(8,128)(2,1)S(1)}, u32[]{:S(2)}, u32[]{:S(2)}) %collective-permute-start.15) | collective-permute-done | bytes 262176 | tf_op jit(solution)/shard_map/ppermute | solution.py:440
  89.2 2.6 %collective-permute-done.17 = bf16[64,2048]{1,0:T(8,128)(2,1)S(1)} collective-permute-done((bf16[64,2048]{1,0:T(8,128)(2,1)S(1)}, bf16[64,2048]{1,0:T(8,128)(2,1)S(1)}, u32[]{:S(2)}, u32[]{:S(2)}) %collective-permute-start.17) | collective-permute-done | bytes 262176 | tf_op jit(solution)/shard_map/ppermute | solution.py:440
  96.9 6.8 %collective-permute-done.19.refs_3_ = bf16[64,2048]{1,0:T(8,128)(2,1)S(1)} collective-permute-done((bf16[64,2048]{1,0:T(8,128)(2,1)S(1)}, bf16[64,2048]{1,0:T(8,128)(2,1)S(1)}, u32[]{:S(2)}, u32[]{:S(2)}) %collective-permute-start.19) | collective-permute-done | bytes 262176 | tf_op jit(solution)/shard_map/ppermute | solution.py:440
  111.0 2.5 %collective-permute-done.22.refs_0_ = bf16[64,2048]{1,0:T(8,128)(2,1)S(1)} collective-permute-done((bf16[64,2048]{1,0:T(8,128)(2,1)S(1)}, bf16[64,2048]{1,0:T(8,128)(2,1)S(1)}, u32[]{:S(2)}, u32[]{:S(2)}) %collective-permute-start.22) | collective-permute-done | bytes 262176 | tf_op jit(solution)/shard_map/ppermute | solution.py:440
  114.2 2.3 shard_map.187.refs_0_
  116.5 7.5 %shard_map.188 = bf16[256,2048]{1,0:T(8,128)(2,1)} custom-call(bf16[64,2048]{1,0:T(8,128)(2,1)} %copy-done.16, bf16[64,2048]{1,0:T(8,128)(2,1)} %collective-permute-done.20.refs_1_, bf16[64,2048]{1,0:T(8,128)(2,1)} %copy-done.5, bf16[64,2048]{1,0:T(8,128)(2,1)} %copy-done.15, bf16[1,2048]{1,0:T(2,128)(2,1)} %reshape.537.refs_4_, bf16[704,2048]{1,0:T(8,128)(2,1)} %bitcast.84, ...), custom_call_target="tpu_custom_call" | custom-call | flops 2214592512 | bytes 10747904 | tf_op jit(solution)/shard_map/pallas_call | solution.py:263
  124.2 2.8 %collective-permute-done.28.refs_1_ = bf16[64,2048]{1,0:T(8,128)(2,1)} collective-permute-done((bf16[64,2048]{1,0:T(8,128)(2,1)}, bf16[64,2048]{1,0:T(8,128)(2,1)}, u32[]{:S(2)}, u32[]{:S(2)}) %collective-permute-start.28) | collective-permute-done | bytes 262176 | tf_op jit(solution)/shard_map/ppermute | solution.py:450
  127.1 2.2 shard_map.189.refs_0_
  129.3 2.3 shard_map.190.refs_1_
  135.6 15.2 %shard_map.191 = (bf16[256,2048]{1,0:T(8,128)(2,1)}, bf16[256,2048]{1,0:T(8,128)(2,1)}, bf16[256,2048]{1,0:T(8,128)(2,1)}, bf16[256,2048]{1,0:T(8,128)(2,1)}) custom-call(bf16[256,2048]{1,0:T(8,128)(2,1)} %shard_map.187.refs_0_, bf16[256,2048]{1,0:T(8,128)(2,1)} %shard_map.190.refs_1_, bf16[256,2048]{1,0:T(8,128)(2,1)} %collective-permute-done.30.refs_2_, ...), custom_call_target="tpu_custom_call" | custom-call | flops 8254390272 | bytes 25690112 | tf_op jit(solution)/shard_map/pallas_call | solution.py:359
  151.4 7.6 %shard_map.192 = bf16[256,2048]{1,0:T(8,128)(2,1)} custom-call(bf16[64,2048]{1,0:T(8,128)(2,1)} %copy-done.12, bf16[64,2048]{1,0:T(8,128)(2,1)} %copy-done.14, bf16[64,2048]{1,0:T(8,128)(2,1)} %copy-done.11, bf16[64,2048]{1,0:T(8,128)(2,1)} %copy-done.13, bf16[1,2048]{1,0:T(2,128)(2,1)} %reshape.537.refs_4_, bf16[704,2048]{1,0:T(8,128)(2,1)} %bitcast.85, ...), custom_call_target="tpu_custom_call" | custom-call | flops 2214592512 | bytes 10747904 | tf_op jit(solution)/shard_map/pallas_call | solution.py:263
  164.0 10.7 %shard_map.193 = bf16[512,2048]{1,0:T(8,128)(2,1)} custom-call(bf16[256,2048]{1,0:T(8,128)(2,1)} %copy-done.6, bf16[256,2048]{1,0:T(8,128)(2,1)} %copy-done.7, s32[1,1,512]{2,1,0:T(1,128)} %get-tuple-element.214.refs_2_, f32[1,1,512]{2,1,0:T(1,128)} %get-tuple-element.210.refs_3_, bf16[1,2048,1408]{2,1,0:T(8,128)(2,1)} %refs_4_.3, ...), custom_call_target="tpu_custom_call" | custom-call | flops 4127195136 | bytes 21495808 | tf_op jit(solution)/shard_map/pallas_call | solution.py:359
  177.0 10.5 %shard_map.194 = (bf16[64,2048]{1,0:T(8,128)(2,1)}, bf16[64,2048]{1,0:T(8,128)(2,1)}, bf16[64,2048]{1,0:T(8,128)(2,1)}, bf16[64,2048]{1,0:T(8,128)(2,1)}, bf16[6...) custom-call(bf16[256,2048]{1,0:T(8,128)(2,1)} %shard_map.189.refs_0_, ...), custom_call_target="tpu_custom_call" | custom-call | flops 4127195136 | bytes 21495808 | tf_op jit(solution)/shard_map/pallas_call | solution.py:359
  187.5 2.2 collective-permute-done.39
  197.2 2.8 %collective-permute-done.43 = bf16[64,2048]{1,0:T(8,128)(2,1)S(1)} collective-permute-done((bf16[64,2048]{1,0:T(8,128)(2,1)S(1)}, bf16[64,2048]{1,0:T(8,128)(2,1)S(1)}, u32[]{:S(2)}, u32[]{:S(2)}) %collective-permute-start.43) | collective-permute-done | bytes 262176 | tf_op jit(solution)/shard_map/ppermute | solution.py:440
  200.9 4.7 %collective-permute-done.42 = bf16[64,2048]{1,0:T(8,128)(2,1)S(1)} collective-permute-done((bf16[64,2048]{1,0:T(8,128)(2,1)S(1)}, bf16[64,2048]{1,0:T(8,128)(2,1)S(1)}, u32[]{:S(2)}, u32[]{:S(2)}) %collective-permute-start.42) | collective-permute-done | bytes 262176 | tf_op jit(solution)/shard_map/ppermute | solution.py:440
  206.5 4.8 %collective-permute-done.41 = bf16[64,2048]{1,0:T(8,128)(2,1)S(1)} collective-permute-done((bf16[64,2048]{1,0:T(8,128)(2,1)S(1)}, bf16[64,2048]{1,0:T(8,128)(2,1)S(1)}, u32[]{:S(2)}, u32[]{:S(2)}) %collective-permute-start.41) | collective-permute-done | bytes 262176 | tf_op jit(solution)/shard_map/ppermute | solution.py:440
  212.1 3.5 %collective-permute-done.40 = bf16[64,2048]{1,0:T(8,128)(2,1)S(1)} collective-permute-done((bf16[64,2048]{1,0:T(8,128)(2,1)S(1)}, bf16[64,2048]{1,0:T(8,128)(2,1)S(1)}, u32[]{:S(2)}, u32[]{:S(2)}) %collective-permute-start.40) | collective-permute-done | bytes 262176 | tf_op jit(solution)/shard_map/ppermute | solution.py:440
  218.1 4.8 %collective-permute-done.49 = bf16[64,2048]{1,0:T(8,128)(2,1)S(1)} collective-permute-done((bf16[64,2048]{1,0:T(8,128)(2,1)S(1)}, bf16[64,2048]{1,0:T(8,128)(2,1)S(1)}, u32[]{:S(2)}, u32[]{:S(2)}) %collective-permute-start.49) | collective-permute-done | bytes 262176 | tf_op jit(solution)/shard_map/ppermute | solution.py:440
  224.9 2.3 collective-permute-start.50
  227.1 8.1 %collective-permute-done.47 = bf16[64,2048]{1,0:T(8,128)(2,1)S(1)} collective-permute-done((bf16[64,2048]{1,0:T(8,128)(2,1)S(1)}, bf16[64,2048]{1,0:T(8,128)(2,1)S(1)}, u32[]{:S(2)}, u32[]{:S(2)}) %collective-permute-start.47) | collective-permute-done | bytes 262176 | tf_op jit(solution)/shard_map/ppermute | solution.py:440
  (241 shorter events, 70.5 us)
Async XLA Ops:
  0.0 25.9 %collective-permute-start.3 = (bf16[64,2048]{1,0:T(8,128)(2,1)}, bf16[64,2048]{1,0:T(8,128)(2,1)}, u32[]{:S(2)}, u32[]{:S(2)}) collective-permute-start(bf16[64,2048]{1,0:T(8,128)(2,1)} %refs_2_.1), channel_id=1, source_target_pairs={{0,4},{1,5},{2,6},{3,7},{4,0},{5,1},{6,2},{7,3},{8,12},{9,13},{10,... | collective-permute-start | bytes 786440 | tf_op jit(solution)/shard_map/ppermute | solution.py:440
  10.2 37.2 %collective-permute-start.2 = (bf16[592,512]{1,0:T(8,128)(2,1)}, bf16[592,512]{1,0:T(8,128)(2,1)S(1)}, u32[]{:S(2)}, u32[]{:S(2)}) collective-permute-start(bf16[592,512]{1,0:T(8,128)(2,1)} %get-tuple-element.105), channel_id=1, source_target_pairs={{0,3},{1,2},{2,1},{3,0},{4,7},{5,6},{6,5},{7,4},{8,11},{9,10},{10,... | collective-permute-start | bytes 1818632 | tf_op jit(solution)/shard_map/ppermute | solution.py:440
  12.8 35.2 %collective-permute-start.1 = (bf16[592,512]{1,0:T(8,128)(2,1)}, bf16[592,512]{1,0:T(8,128)(2,1)S(1)}, u32[]{:S(2)}, u32[]{:S(2)}) collective-permute-start(bf16[592,512]{1,0:T(8,128)(2,1)} %get-tuple-element.104), channel_id=1, source_target_pairs={{0,2},{1,3},{2,0},{3,1},{4,6},{5,7},{6,4},{7,5},{8,10},{9,11},{10,... | collective-permute-start | bytes 1818632 | tf_op jit(solution)/shard_map/ppermute | solution.py:440
  13.2 34.8 %collective-permute-start = (bf16[592,512]{1,0:T(8,128)(2,1)}, bf16[592,512]{1,0:T(8,128)(2,1)S(1)}, u32[]{:S(2)}, u32[]{:S(2)}) collective-permute-start(bf16[592,512]{1,0:T(8,128)(2,1)} %get-tuple-element.103), channel_id=1, source_target_pairs={{0,1},{1,0},{2,3},{3,2},{4,5},{5,4},{6,7},{7,6},{8,9},{9,8},{10,11... | collective-permute-start | bytes 1818632 | tf_op jit(solution)/shard_map/ppermute | solution.py:440
  14.5 29.9 %collective-permute-start.8 = (bf16[64,2048]{1,0:T(8,128)(2,1)}, bf16[64,2048]{1,0:T(8,128)(2,1)}, u32[]{:S(2)}, u32[]{:S(2)}) collective-permute-start(bf16[64,2048]{1,0:T(8,128)(2,1)} %constant_dynamic-slice_fusion), channel_id=1, source_target_pairs={{0,4},{1,5},{2,6},{3,7},{4,0},{5,1},{6,2},{7,3},{8,12},{9,13},{10,... | collective-permute-start | bytes 786440 | tf_op jit(solution)/shard_map/ppermute | solution.py:440
  28.3 17.6 %collective-permute-start.4 = (bf16[64,512]{1,0:T(8,128)(2,1)}, bf16[64,512]{1,0:T(8,128)(2,1)S(1)}, u32[]{:S(2)}, u32[]{:S(2)}) collective-permute-start(bf16[64,512]{1,0:T(8,128)(2,1)} %get-tuple-element.114), channel_id=1, source_target_pairs={{0,1},{1,0},{2,3},{3,2},{4,5},{5,4},{6,7},{7,6},{8,9},{9,8},{10,11... | collective-permute-start | bytes 196616 | tf_op jit(solution)/shard_map/ppermute | solution.py:440
  45.9 12.4 %collective-permute-start.9 = (bf16[64,2048]{1,0:T(8,128)(2,1)}, bf16[64,2048]{1,0:T(8,128)(2,1)S(1)}, u32[]{:S(2)}, u32[]{:S(2)}) collective-permute-start(bf16[64,2048]{1,0:T(8,128)(2,1)} %collective-permute-done.8.refs_0_), channel_id=1, source_target_pairs={{0,16},{8,24},{16,0},{24,8},{1,17},{9,25},{17,1},{25,9},{2,18},{10... | collective-permute-start | bytes 786440 | tf_op jit(solution)/shard_map/ppermute | solution.py:454
  58.8 15.0 %collective-permute-start.13 = (bf16[512,256]{1,0:T(8,128)(2,1)S(1)}, bf16[512,256]{1,0:T(8,128)(2,1)S(1)}, u32[]{:S(2)}, u32[]{:S(2)}) collective-permute-start(bf16[512,256]{1,0:T(8,128)(2,1)S(1)} %get-tuple-element.125), channel_id=1, source_target_pairs={{0,4},{1,5},{2,6},{3,7},{4,0},{5,1},{6,2},{7,3},{8,12},{9,13},{10,... | collective-permute-start | bytes 786440 | tf_op jit(solution)/shard_map/ppermute | solution.py:440
  78.8 10.4 %collective-permute-start.15 = (bf16[64,2048]{1,0:T(8,128)(2,1)S(1)}, bf16[64,2048]{1,0:T(8,128)(2,1)S(1)}, u32[]{:S(2)}, u32[]{:S(2)}) collective-permute-start(bf16[64,2048]{1,0:T(8,128)(2,1)S(1)} %get-tuple-element.134), channel_id=1, source_target_pairs={{0,1},{1,0},{2,3},{3,2},{4,5},{5,4},{6,7},{7,6},{8,9},{9,8},{10,11... | collective-permute-start | bytes 786440 | tf_op jit(solution)/shard_map/ppermute | solution.py:440
  92.2 11.4 %collective-permute-start.19 = (bf16[64,2048]{1,0:T(8,128)(2,1)S(1)}, bf16[64,2048]{1,0:T(8,128)(2,1)S(1)}, u32[]{:S(2)}, u32[]{:S(2)}) collective-permute-start(bf16[64,2048]{1,0:T(8,128)(2,1)S(1)} %multiply_convert_fusion.refs_2_), channel_id=1, source_target_pairs={{0,4},{1,5},{2,6},{3,7},{4,0},{5,1},{6,2},{7,3},{8,12},{9,13},{10,... | collective-permute-start | bytes 786440 | tf_op jit(solution)/shard_map/ppermute | solution.py:440
  93.8 10.4 %collective-permute-start.18 = (bf16[64,2048]{1,0:T(8,128)(2,1)S(1)}, bf16[64,2048]{1,0:T(8,128)(2,1)S(1)}, u32[]{:S(2)}, u32[]{:S(2)}) collective-permute-start(bf16[64,2048]{1,0:T(8,128)(2,1)S(1)} %multiply_convert_fusion.refs_2_), channel_id=1, source_target_pairs={{0,2},{1,3},{2,0},{3,1},{4,6},{5,7},{6,4},{7,5},{8,10},{9,11},{10,... | collective-permute-start | bytes 786440 | tf_op jit(solution)/shard_map/ppermute | solution.py:440
  95.6 12.1 %collective-permute-start.21 = (bf16[64,2048]{1,0:T(8,128)(2,1)S(1)}, bf16[64,2048]{1,0:T(8,128)(2,1)S(1)}, u32[]{:S(2)}, u32[]{:S(2)}) collective-permute-start(bf16[64,2048]{1,0:T(8,128)(2,1)S(1)} %multiply_convert_fusion.refs_2_), channel_id=1, source_target_pairs={{0,1},{1,0},{2,3},{3,2},{4,5},{5,4},{6,7},{7,6},{8,9},{9,8},{10,11... | collective-permute-start | bytes 786440 | tf_op jit(solution)/shard_map/ppermute | solution.py:440
  96.2 12.0 %collective-permute-start.25 = (bf16[64,2048]{1,0:T(8,128)(2,1)S(1)}, bf16[64,2048]{1,0:T(8,128)(2,1)S(1)}, u32[]{:S(2)}, u32[]{:S(2)}) collective-permute-start(bf16[64,2048]{1,0:T(8,128)(2,1)S(1)} %multiply_convert_fusion.refs_2_), channel_id=1, source_target_pairs={{0,16},{8,24},{16,0},{24,8},{1,17},{9,25},{17,1},{25,9},{2,18},{10... | collective-permute-start | bytes 786440 | tf_op jit(solution)/shard_map/ppermute | solution.py:450
  106.1 17.9 %collective-permute-start.23 = (bf16[64,2048]{1,0:T(8,128)(2,1)S(1)}, bf16[64,2048]{1,0:T(8,128)(2,1)S(1)}, u32[]{:S(2)}, u32[]{:S(2)}) collective-permute-start(bf16[64,2048]{1,0:T(8,128)(2,1)S(1)} %collective-permute-done.19.refs_3_), channel_id=1, source_target_pairs={{0,1},{1,0},{2,3},{3,2},{4,5},{5,4},{6,7},{7,6},{8,9},{9,8},{10,11... | collective-permute-start | bytes 786440 | tf_op jit(solution)/shard_map/ppermute | solution.py:440
  107.6 16.5 %collective-permute-start.26 = (bf16[64,2048]{1,0:T(8,128)(2,1)S(1)}, bf16[64,2048]{1,0:T(8,128)(2,1)}, u32[]{:S(2)}, u32[]{:S(2)}) collective-permute-start(bf16[64,2048]{1,0:T(8,128)(2,1)S(1)} %collective-permute-done.18.refs_0_), channel_id=1, source_target_pairs={{0,16},{8,24},{16,0},{24,8},{1,17},{9,25},{17,1},{25,9},{2,18},{10... | collective-permute-start | bytes 786440 | tf_op jit(solution)/shard_map/ppermute | solution.py:450
  108.2 16.0 %collective-permute-start.27 = (bf16[64,2048]{1,0:T(8,128)(2,1)S(1)}, bf16[64,2048]{1,0:T(8,128)(2,1)}, u32[]{:S(2)}, u32[]{:S(2)}) collective-permute-start(bf16[64,2048]{1,0:T(8,128)(2,1)S(1)} %collective-permute-done.19.refs_3_), channel_id=1, source_target_pairs={{0,16},{8,24},{16,0},{24,8},{1,17},{9,25},{17,1},{25,9},{2,18},{10... | collective-permute-start | bytes 786440 | tf_op jit(solution)/shard_map/ppermute | solution.py:450
  110.3 13.9 %collective-permute-start.24 = (bf16[64,2048]{1,0:T(8,128)(2,1)}, bf16[64,2048]{1,0:T(8,128)(2,1)S(1)}, u32[]{:S(2)}, u32[]{:S(2)}) collective-permute-start(bf16[64,2048]{1,0:T(8,128)(2,1)} %collective-permute-done.20.refs_1_), channel_id=1, source_target_pairs={{0,1},{1,0},{2,3},{3,2},{4,5},{5,4},{6,7},{7,6},{8,9},{9,8},{10,11... | collective-permute-start | bytes 786440 | tf_op jit(solution)/shard_map/ppermute | solution.py:440
  113.5 13.6 %collective-permute-start.28 = (bf16[64,2048]{1,0:T(8,128)(2,1)}, bf16[64,2048]{1,0:T(8,128)(2,1)}, u32[]{:S(2)}, u32[]{:S(2)}) collective-permute-start(bf16[64,2048]{1,0:T(8,128)(2,1)} %collective-permute-done.20.refs_1_), channel_id=1, source_target_pairs={{0,16},{8,24},{16,0},{24,8},{1,17},{9,25},{17,1},{25,9},{2,18},{10... | collective-permute-start | bytes 786440 | tf_op jit(solution)/shard_map/ppermute | solution.py:450
  124.1 10.5 %collective-permute-start.30 = (bf16[256,2048]{1,0:T(8,128)(2,1)S(1)}, bf16[256,2048]{1,0:T(8,128)(2,1)}, u32[]{:S(2)}, u32[]{:S(2)}) collective-permute-start(bf16[256,2048]{1,0:T(8,128)(2,1)S(1)} %copy-done.8), channel_id=1, source_target_pairs={{0,8},{8,0},{16,24},{24,16},{1,9},{9,1},{17,25},{25,17},{2,10},{10... | collective-permute-start | bytes 3145736 | tf_op jit(solution)/shard_map/ppermute | solution.py:450
  132.8 26.2 %collective-permute-start.33 = (bf16[256,2048]{1,0:T(8,128)(2,1)S(1)}, bf16[256,2048]{1,0:T(8,128)(2,1)}, u32[]{:S(2)}, u32[]{:S(2)}) collective-permute-start(bf16[256,2048]{1,0:T(8,128)(2,1)S(1)} %copy-done.4), channel_id=1, source_target_pairs={{0,1},{1,0},{2,3},{3,2},{4,5},{5,4},{6,7},{7,6},{8,9},{9,8},{10,11... | collective-permute-start | bytes 3145736 | tf_op jit(solution)/shard_map/ppermute | solution.py:440
  151.1 11.5 %collective-permute-start.34 = (bf16[256,2048]{1,0:T(8,128)(2,1)S(1)}, bf16[256,2048]{1,0:T(8,128)(2,1)S(1)}, u32[]{:S(2)}, u32[]{:S(2)}) collective-permute-start(bf16[256,2048]{1,0:T(8,128)(2,1)S(1)} %copy-done.4), channel_id=1, source_target_pairs={{0,8},{8,0},{16,24},{24,16},{1,9},{9,1},{17,25},{25,17},{2,10},{10... | collective-permute-start | bytes 3145736 | tf_op jit(solution)/shard_map/ppermute | solution.py:450
  161.1 14.2 %collective-permute-start.37 = (bf16[128,2048]{1,0:T(8,128)(2,1)S(1)}, bf16[128,2048]{1,0:T(8,128)(2,1)S(1)}, u32[]{:S(2)}, u32[]{:S(2)}) collective-permute-start(bf16[128,2048]{1,0:T(8,128)(2,1)S(1)} %get-tuple-element.208), channel_id=1, source_target_pairs={{0,1},{1,0},{2,3},{3,2},{4,5},{5,4},{6,7},{7,6},{8,9},{9,8},{10,11... | collective-permute-start | bytes 1572872 | tf_op jit(solution)/shard_map/ppermute | solution.py:440
  175.4 14.3 %collective-permute-start.38 = (bf16[512,2048]{1,0:T(8,128)(2,1)}, bf16[512,2048]{1,0:T(8,128)(2,1)S(1)}, u32[]{:S(2)}, u32[]{:S(2)}) collective-permute-start(bf16[512,2048]{1,0:T(8,128)(2,1)} %shard_map.193), channel_id=1, source_target_pairs={{0,8},{8,0},{16,24},{24,16},{1,9},{9,1},{17,25},{25,17},{2,10},{10... | collective-permute-start | bytes 6291464 | tf_op jit(solution)/shard_map/ppermute | solution.py:450
  175.4 14.3 %collective-permute-start.39 = (bf16[128,2048]{1,0:T(8,128)(2,1)S(1)}, bf16[128,2048]{1,0:T(8,128)(2,1)S(1)}, u32[]{:S(2)}, u32[]{:S(2)}) collective-permute-start(bf16[128,2048]{1,0:T(8,128)(2,1)S(1)} %get-tuple-element.207), channel_id=1, source_target_pairs={{0,1},{1,0},{2,3},{3,2},{4,5},{5,4},{6,7},{7,6},{8,9},{9,8},{10,11... | collective-permute-start | bytes 1572872 | tf_op jit(solution)/shard_map/ppermute | solution.py:440
  176.8 38.9 %collective-permute-start.32 = (bf16[256,2048]{1,0:T(8,128)(2,1)S(1)}, bf16[256,2048]{1,0:T(8,128)(2,1)S(1)}, u32[]{:S(2)}, u32[]{:S(2)}) collective-permute-start(bf16[256,2048]{1,0:T(8,128)(2,1)S(1)} %copy-done.31), channel_id=1, source_target_pairs={{0,8},{8,0},{16,24},{24,16},{1,9},{9,1},{17,25},{25,17},{2,10},{10... | collective-permute-start | bytes 3145736 | tf_op jit(solution)/shard_map/ppermute | solution.py:450
  193.3 12.4 %collective-permute-start.42 = (bf16[64,2048]{1,0:T(8,128)(2,1)S(1)}, bf16[64,2048]{1,0:T(8,128)(2,1)S(1)}, u32[]{:S(2)}, u32[]{:S(2)}) collective-permute-start(bf16[64,2048]{1,0:T(8,128)(2,1)S(1)} %add_convert_fusion.11), channel_id=1, source_target_pairs={{0,1},{1,0},{2,3},{3,2},{4,5},{5,4},{6,7},{7,6},{8,9},{9,8},{10,11... | collective-permute-start | bytes 786440 | tf_op jit(solution)/shard_map/ppermute | solution.py:440
  195.0 16.3 %collective-permute-start.41 = (bf16[64,2048]{1,0:T(8,128)(2,1)S(1)}, bf16[64,2048]{1,0:T(8,128)(2,1)S(1)}, u32[]{:S(2)}, u32[]{:S(2)}) collective-permute-start(bf16[64,2048]{1,0:T(8,128)(2,1)S(1)} %add_convert_fusion.10), channel_id=1, source_target_pairs={{0,1},{1,0},{2,3},{3,2},{4,5},{5,4},{6,7},{7,6},{8,9},{9,8},{10,11... | collective-permute-start | bytes 786440 | tf_op jit(solution)/shard_map/ppermute | solution.py:440
  196.5 19.1 %collective-permute-start.40 = (bf16[64,2048]{1,0:T(8,128)(2,1)S(1)}, bf16[64,2048]{1,0:T(8,128)(2,1)S(1)}, u32[]{:S(2)}, u32[]{:S(2)}) collective-permute-start(bf16[64,2048]{1,0:T(8,128)(2,1)S(1)} %add_convert_fusion.9), channel_id=1, source_target_pairs={{0,1},{1,0},{2,3},{3,2},{4,5},{5,4},{6,7},{7,6},{8,9},{9,8},{10,11... | collective-permute-start | bytes 786440 | tf_op jit(solution)/shard_map/ppermute | solution.py:440
  200.2 15.5 %collective-permute-start.46 = (bf16[64,2048]{1,0:T(8,128)(2,1)S(1)}, bf16[64,2048]{1,0:T(8,128)(2,1)S(1)}, u32[]{:S(2)}, u32[]{:S(2)}) collective-permute-start(bf16[64,2048]{1,0:T(8,128)(2,1)S(1)} %add_convert_fusion.8), channel_id=1, source_target_pairs={{0,16},{8,24},{16,0},{24,8},{1,17},{9,25},{17,1},{25,9},{2,18},{10... | collective-permute-start | bytes 786440 | tf_op jit(solution)/shard_map/ppermute | solution.py:450
  205.8 12.4 %collective-permute-start.48 = (bf16[64,2048]{1,0:T(8,128)(2,1)S(1)}, bf16[64,2048]{1,0:T(8,128)(2,1)S(1)}, u32[]{:S(2)}, u32[]{:S(2)}) collective-permute-start(bf16[64,2048]{1,0:T(8,128)(2,1)S(1)} %add_convert_fusion.7), channel_id=1, source_target_pairs={{0,16},{8,24},{16,0},{24,8},{1,17},{9,25},{17,1},{25,9},{2,18},{10... | collective-permute-start | bytes 786440 | tf_op jit(solution)/shard_map/ppermute | solution.py:450
  223.4 11.8 %collective-permute-start.47 = (bf16[64,2048]{1,0:T(8,128)(2,1)S(1)}, bf16[64,2048]{1,0:T(8,128)(2,1)S(1)}, u32[]{:S(2)}, u32[]{:S(2)}) collective-permute-start(bf16[64,2048]{1,0:T(8,128)(2,1)S(1)} %get-tuple-element.205), channel_id=1, source_target_pairs={{0,2},{1,3},{2,0},{3,1},{4,6},{5,7},{6,4},{7,5},{8,10},{9,11},{10,... | collective-permute-start | bytes 786440 | tf_op jit(solution)/shard_map/ppermute | solution.py:440
  224.9 10.4 %collective-permute-start.50 = (bf16[64,2048]{1,0:T(8,128)(2,1)S(1)}, bf16[64,2048]{1,0:T(8,128)(2,1)S(1)}, u32[]{:S(2)}, u32[]{:S(2)}) collective-permute-start(bf16[64,2048]{1,0:T(8,128)(2,1)S(1)} %get-tuple-element.206), channel_id=1, source_target_pairs={{0,4},{1,5},{2,6},{3,7},{4,0},{5,1},{6,2},{7,3},{8,12},{9,13},{10,... | collective-permute-start | bytes 786440 | tf_op jit(solution)/shard_map/ppermute | solution.py:440
  (52 other events, 575.4 us)

commit v11 on v10

--- a/solution.py
+++ b/solution.py
@@ -244,14 +244,14 @@
         block.astype(jnp.float32) * scalar[...].astype(jnp.float32), axis=1, keepdims=True
     )
     scale = 1.0 / (1.0 + jnp.exp(-logit))
-    across = (((1,), (1,)), ((), ()))
+    across, along = (((1,), (1,)), ((), ())), (((0,), (0,)), ((), ()))
     copies[0].wait()
-    gate = lax.dot_general(block, gate_v[...], across, preferred_element_type=jnp.float32)
+    gate = lax.dot_general(gate_v[...], block, across, preferred_element_type=jnp.float32)
     copies[1].wait()
-    upper = lax.dot_general(block, up_v[...], across, preferred_element_type=jnp.float32)
+    upper = lax.dot_general(up_v[...], block, across, preferred_element_type=jnp.float32)
     hidden = (silu(gate) * upper).astype(jnp.bfloat16)
     copies[2].wait()
-    result = jnp.dot(hidden, down_v[...], preferred_element_type=jnp.float32)
+    result = lax.dot_general(hidden, down_v[...], along, preferred_element_type=jnp.float32)
     out[...] = (scale * result).astype(jnp.bfloat16)
 
 
@@ -287,7 +287,7 @@
     place, row_gate = refs[:2]
     more, refs = refs[2 : 2 + extras], refs[2 + extras :]
     (gate_w, up_w, down_w), refs = refs[:3], refs[3:]
-    outs, refs = refs[: count * cuts], refs[count * cuts :]
+    outs, refs = refs[: sum(cuts)], refs[sum(cuts) :]
     rows, packed, gate_v, up_v, down_v, more_v, sems = refs
     moves, chunk_copies = [], []
     for c, n in enumerate(parts):
@@ -329,7 +329,6 @@
     )
     for i in range(extras):
         copies[total + 3 + i].wait()
-    cut = size // cuts
     for c in range(count):
         scaled = answer[c * entries : (c + 1) * entries, :].astype(jnp.float32) * weights[c]
         placed = lax.dot_general(
@@ -341,8 +340,9 @@
         if c == 0 and extras:
             placed = placed + more_v[...].astype(jnp.float32)
         placed = placed.astype(jnp.bfloat16)
-        for k in range(cuts):
-            outs[c * cuts + k][...] = placed[k * cut : (k + 1) * cut, :]
+        cut = size // cuts[c]
+        for k in range(cuts[c]):
+            outs[sum(cuts[:c]) + k][...] = placed[k * cut : (k + 1) * cut, :]
 
 
 def routed_expert(chunks, place, row_gate, more, gate_w, up_w, down_w, entries, cuts):
@@ -354,13 +354,15 @@
     hidden = gate_w.shape[2]
     any_spec = pl.BlockSpec(memory_space=pl.ANY)
     vmem = pl.BlockSpec(memory_space=pltpu.VMEM)
-    out_shape = jax.ShapeDtypeStruct((size // cuts, width), jnp.bfloat16)
+    out_shape = [
+        jax.ShapeDtypeStruct((size // n, width), jnp.bfloat16) for n in cuts for k in range(n)
+    ]
     more_rows = sum(extra.shape[0] for extra in more) if more else 16
     outs = pl.pallas_call(
         functools.partial(routed_kernel, parts, len(more), entries, cuts),
-        out_shape=[out_shape] * (count * cuts),
+        out_shape=out_shape,
         in_specs=[any_spec] * total + [vmem] * 2 + [any_spec] * (len(more) + 3),
-        out_specs=[vmem] * (count * cuts),
+        out_specs=[vmem] * sum(cuts),
         scratch_shapes=[
             pltpu.VMEM((count, size, width), jnp.bfloat16),
             pltpu.VMEM((count * entries, width), jnp.bfloat16),
@@ -377,7 +379,7 @@
             transcendentals=count * entries * hidden,
         ),
     )(*[piece for chunk in chunks for piece in chunk], place, row_gate, *more, gate_w, up_w, down_w)
-    return [outs[c * cuts : (c + 1) * cuts] for c in range(count)]
+    return [outs[sum(cuts[:c]) : sum(cuts[: c + 1])] for c in range(count)]
 
 
 def rms_normed(stream, norm_gain):
@@ -473,13 +475,12 @@
     quarter = lax.dynamic_slice_in_dim(
         out_proj, (iy % 2 * nc + ic) * quarter_rows, quarter_rows, 0
     )
-    quarters = [send(quarter, 1, 0, 0)]
     quarter_order = jnp.stack(
         [(iy + dy) % 2 * nc + (ic + dc) % nc for dc in range(nc) for dy in range(2)]
     ).astype(i32)
     far_queries = send(queries, 1, 0, 0)
     members = [(dl, dx) for dl in range(2) for dx in range(nx)]
-    order = jnp.stack(
+    member_columns = jnp.stack(
         [
             ((ih + j) % 2 * 2 + (il + dl) % 2) * nx + (ix + dx) % nx
             for dl, dx in members
@@ -487,13 +488,15 @@
         ]
     ).astype(i32)
     gates = jnp.pad(jnp.transpose(route_gate), ((0, 0), (0, 2 * columns - tok_rows)))
-    blocks = pack([keys, values, queries], gates, order, columns)
+    blocks = pack([keys, values, queries], gates, member_columns, columns)
     blocks = [send(blocks[m], 0, *members[m]) for m in range(len(members))]
-    far = list(pack([far_queries], None, order, columns))
+    far = list(pack([far_queries], None, member_columns, columns))
     for m in range(1, len(members)):
         if m > 2:
             far[m], far[m - 2] = tie((far[m], far[m - 2]))
         far[m] = send(far[m], 0, *members[m])
+    quarter, far[1] = tie((quarter, far[1]))
+    quarters = [send(quarter, 1, 0, 0)]
     page_ids = (
         rel_exp[: len(members), None] * pages_here + jnp.arange(pages_here, dtype=i32)[None, :]
     ).reshape(-1)
@@ -512,7 +515,8 @@
     twins = slot_expert == own_expert
     copies = jnp.sum(twins.astype(i32))
     own_rank = jnp.sum((twins & (slot_ids < own_slot)).astype(i32))
-    rel_rows = jnp.transpose(rel_exp.reshape(2, 2, nx)[:, ::-1], (2, 1, 0)).reshape(-1)
+    order = [1, 3, 2, 0]
+    rel_rows = jnp.stack([rel_exp.reshape(4, nx)[i] for i in order], axis=1).reshape(-1)
     rel_slots = (rel_req[:, None] * exp_count + rel_rows[None, :]).reshape(-1)
     named = (route_expert == own_expert).reshape(slot_count, tok_rows, TOPK)[rel_slots]
     named = jnp.transpose(named, (0, 2, 1))
@@ -538,15 +542,16 @@
             tok_rows,
         )
 
+    theirs, their_level = attend_half(1, far)
+    theirs, their_level, quarters = tie((theirs, their_level, quarters))
+    theirs, their_level = send(theirs, 1, 0, 0), send(their_level, 1, 0, 0)
+    quarters.append(swap_y(quarters[0]))
     gates = jnp.stack([send(gates, dh, 0, 0) for dh in range(2)])
-    quarters.append(swap_y(quarters[0]))
-    theirs, their_level = attend_half(1, far)
-    theirs, their_level, gates, quarters = tie((theirs, their_level, gates, quarters))
-    theirs, their_level = send(theirs, 1, 0, 0), send(their_level, 1, 0, 0)
-    gates = jnp.stack([send_req(gates, dy, 0) for dy in range(ny)])
-    quarters += [send_req(q, 0, dc) for dc in range(1, nc) for q in quarters[:2]]
     mine, level = attend_half(0, [])
     mine, level, gates, quarters = tie((mine, level, gates, quarters))
+    quarters += [send_req(q, 0, dc) for dc in range(1, nc) for q in quarters[:2]]
+    gates = jnp.stack([send_req(gates, dy, 0) for dy in range(ny)])
+    theirs, their_level, gates, quarters = tie((theirs, their_level, gates, quarters))
 
     stays, comes = {}, {}
     proj = out_proj
@@ -565,13 +570,13 @@
     stream = stream + line.astype(f32)
     normed = rms_normed(stream, norm_gain)
     gates = jnp.stack([send_req(gates, 0, dc) for dc in range(nc)], axis=1)
-    gates = jnp.transpose(gates[:, :, :, ::-1], (0, 1, 4, 3, 2, 5, 6))
+    gates = gates.reshape(ny, nc, 4, nx, TOPK, tok_rows)
+    gates = jnp.stack([gates[:, :, i] for i in order], axis=3)
     gates = gates.reshape(slot_count, TOPK, tok_rows)
     row_gate = jnp.sum(jnp.where(named, gates, 0.0), axis=1).reshape(ny, nc, 1, chunk_rows)
 
     far_line = send(normed, 1, 0, 0)
     line = [normed, send(normed, 0, 1, 0), far_line, send(far_line, 0, 1, 0)]
-    order = [1, 3, 0, 2]
     over_x = {(i, dx): send(line[i], 0, 0, dx) for i in order for dx in range(1, nx)}
     over_y = {(i, dy): send_req(line[i], dy, 0) for i in order for dy in range(1, ny)}
 
@@ -613,9 +618,9 @@
 
     cores = list(range(nc))
     kept, comes = {}, {}
-    half_rows = 2 * tok_rows
+    cuts = [slice(0, 3 * tok_rows), slice(3 * tok_rows, 4 * tok_rows)]
     for dy in range(ny - 1):
-        answers = answers_of(dy, cores, [], nx)
+        answers = answers_of(dy, cores, [], [nx] * nc)
         if dy:
             answers, comes[dy - 1] = tie((answers, comes[dy - 1]))
         others = [[send_req(part, 0, -dc) for part in answers[dc][::-1]][::-1] for dc in cores[1:]]
@@ -634,32 +639,24 @@
         gone = [add_up([part[dx] for part in parts]).astype(bf16) for dx in range(1, nx)]
         kept[dy] = [part[0] for part in parts]
         comes[dy] = [
-            [
-                send(go[k * half_rows : (k + 1) * half_rows], 0, 0, -dx)
-                for dx, go in enumerate(gone, 1)
-            ]
-            for k in range(2)
+            [send(go[rows], 0, 0, -dx) for dx, go in enumerate(gone, 1)] for rows in cuts
         ]
         following = [chunks[dy + 1, dc] for dc in cores]
         following, _ = tie((following, gone))
         for dc in cores:
             chunks[dy + 1, dc] = following[dc]
     end = ny - 1
-    others = []
-    for dc in cores[1:]:
-        (answer,) = answers_of(end, [dc], [], 1)
-        answer, comes[end - 1][0] = tie((answer, comes[end - 1][0]))
-        chunks[end, 0], _ = tie((chunks[end, 0], answer))
-        others.append(send_req(answer[0], 0, -dc))
-    (answer,) = answers_of(end, [0], [], 4 * nx)
-    answer, others, comes = tie((answer, others, comes))
-
-    turns = [1, 3, 0, 2]
+    answers = answers_of(end, cores, [], [4 * nx] + [nx] * (nc - 1))
+    answers, comes[end - 1][0] = tie((answers, comes[end - 1][0]))
+    answer = answers[0]
+    others = [[send_req(part, 0, -dc) for part in answers[dc][::-1]][::-1] for dc in cores[1:]]
+
+    turns = [1, 2, 0, 3]
     block = lambda a, p: a[p * tok_rows : (p + 1) * tok_rows]
     last = {}
     for p in turns:
         gone = [
-            add_up([answer[4 * dx + p]] + [block(other, 4 * dx + p) for other in others])
+            add_up([answer[4 * dx + p]] + [block(other[dx], p) for other in others])
             for dx in range(1, nx)
         ]
         gone = [go.astype(bf16) for go in gone]
@@ -668,25 +665,26 @@
 
     def line_of(dy, p):
         if dy < end:
-            arrived = [block(come, p % 2) for come in comes[dy][p // 2]]
+            arrived = [come if p == 3 else block(come, p) for come in comes[dy][p // 3]]
             return add_up([block(part, p) for part in kept[dy]] + arrived)
-        return add_up([answer[p]] + [block(other, p) for other in others] + last[p])
+        return add_up([answer[p]] + [block(other[0], p) for other in others] + last[p])
 
     home, near = {}, {}
     for turn, p in enumerate(turns):
         goes = [line_of(dy, p).astype(bf16) for dy in range(1, ny)]
         home[p] = [send_req(go, -dy, 0) for dy, go in enumerate(goes, 1)]
+        if turn == 1:
+            go = add_up([line_of(0, 1)] + home[1]).astype(bf16)
+            near[1] = send(go, 0, 1, 0)
+            goes.append(go)
         if turn + 1 < len(turns):
             after = turns[turn + 1]
             last[after], _ = tie((last[after], goes))
-    for p in (1, 0):
-        go = add_up([line_of(0, p)] + home[p]).astype(bf16)
-        if p:
-            home[0], _ = tie((home[0], go))
-        near[p] = send(go, 0, 1, 0)
-    far = add_up([line_of(0, 3)] + home[3] + [near[1]]).astype(bf16)
+    far = add_up([line_of(0, 2)] + home[2] + [near[1]]).astype(bf16)
+    home[0], _ = tie((home[0], far))
     far = send(far, 1, 0, 0)
-    total = add_up([stream, line_of(0, 2)] + home[2] + [near[0], far])
+    near[0] = send(add_up([line_of(0, 0)] + home[0]).astype(bf16), 0, 1, 0)
+    total = add_up([stream, line_of(0, 3)] + home[3] + [near[0], far])
     return total.astype(bf16)
 
 

time: 237 us -> 245 us (1.034)
  starting transfers between devices: 50.5 us -> 61.3 us
  Pallas kernels: 78.2 us -> 71.6 us
  waiting for transfers between devices: 79 us -> 82.2 us
    ppermute x19 -> x20, waiting for transfers between devices: 3.48 us -> 18.8 us  [send_req(): return lax.ppermute(value, 'req', pairs)]
    ppermute x31, waiting for transfers between devices: 75.5 us -> 63.4 us  [send(): return lax.ppermute(value, 'exp', pairs)]
    ppermute x31, starting transfers between devices: 40.4 us -> 47.7 us  [send(): return lax.ppermute(value, 'exp', pairs)]
    pallas_call x3 -> x2, Pallas kernels: 36.4 us -> 30.3 us  [routed_expert(): pl.pallas_call(functools.partial(routed_kernel, parts, len(more), entries...]
    ppermute x19 -> x20, starting transfers between devices: 8.53 us -> 12 us  [send_req(): return lax.ppermute(value, 'req', pairs)]
  transfers between devices with their start and end apart: 51 -> 52, of which waited for: 20 -> 24; matrix products, arithmetic and copies ran while one was open for 9% -> 9% of each run, Pallas kernels for 32% -> 29%
where the time goes in v11:
time: 245 us; the launch traced here: 244 us
  waiting for transfers between devices  82.2 us (34%)
  Pallas kernels  71.6 us (29%)
  starting transfers between devices  61.3 us (25%)
  other arithmetic  16.4 us (7%)
  local copies, waits for them, and re-layouts  10.2 us (4%)
    ppermute x31, waiting for transfers between devices, send(): return lax.ppermute(value, 'exp', pairs)  63.4 us
    ppermute x31, starting transfers between devices, send(): return lax.ppermute(value, 'exp', pairs)  47.7 us
    pallas_call x2, Pallas kernels, routed_expert(): pl.pallas_call(functools.partial(routed_kernel, parts, len(more), entries...  30.3 us
    ppermute x20, waiting for transfers between devices, send_req(): return lax.ppermute(value, 'req', pairs)  18.8 us
    pallas_call x2, Pallas kernels, shared_expert(): pl.pallas_call(functools.partial(shared_kernel, len(pieces)), out_shape=j...  16.7 us
    ppermute x20, starting transfers between devices, send_req(): return lax.ppermute(value, 'req', pairs)  12 us
    pallas_call x2, Pallas kernels, attend(): pl.pallas_call(functools.partial(attend_kernel, members, tokens, tok_rows...  9.13 us
    pallas_call x3, Pallas kernels, join(): pl.pallas_call(join_kernel, out_shape=jax.ShapeDtypeStruct((len(parts) *...  6.72 us
  transfers between devices with their start and end apart: 52, of which 24 were waited for; matrix products, arithmetic and copies ran while one was open for 9% of the time, Pallas kernels for 29%

profile of v11, /device:TPU:0, one launch (start us, length us, event | category | flops | bytes accessed | tf_op | source)
XLA Modules:
  0.0 243.8 jit_solution(11369617754903977488)
XLA Ops:
  0.0 4.1 %collective-permute-start.4 = (bf16[64,2048]{1,0:T(8,128)(2,1)}, bf16[64,2048]{1,0:T(8,128)(2,1)S(1)}, u32[]{:S(2)}, u32[]{:S(2)}) collective-permute-start(bf16[64,2048]{1,0:T(8,128)(2,1)} %refs_2_.1), channel_id=1, source_target_pairs={{0,4},{1,5},{2,6},{3,7},{4,0},{5,1},{6,2},{7,3},{8,12},{9,13},{10,... | collective-permute-start | bytes 786440 | tf_op jit(solution)/shard_map/ppermute | solution.py:442
  6.1 4.0 %shard_map.181 = (bf16[592,512]{1,0:T(8,128)(2,1)}, bf16[592,512]{1,0:T(8,128)(2,1)}, bf16[592,512]{1,0:T(8,128)(2,1)}, bf16[592,512]{1,0:T(8,128)(2,1)}) custom-call(s32[8]{0:T(128)} %stack.172.order, bf16[256,2048]{1,0:T(8,128)(2,1)} %bitcast.111, bf16[256,2048]{1,0:T(8,128)(2,1)} %bitcast.112, bf16[64,2048]{1,0:T(8,128)(2,1)} %refs_2_.1, f32[4,512]{1,0:T(4,128)} %pad.4.refs_3_), custom_call_target="tpu_custom_call" | custom-call | bytes 4849664 | tf_op jit(solution)/shard_map/pallas_call | solution.py:58
  25.2 2.3 shard_map.183
  29.2 14.7 %collective-permute-done.5.refs_5_ = bf16[64,512]{1,0:T(8,128)(2,1)S(1)} collective-permute-done((bf16[64,512]{1,0:T(8,128)(2,1)}, bf16[64,512]{1,0:T(8,128)(2,1)S(1)}, u32[]{:S(2)}, u32[]{:S(2)}) %collective-permute-start.5) | collective-permute-done | bytes 65568 | tf_op jit(solution)/shard_map/ppermute | solution.py:442
  48.5 2.3 collective-permute-done.6.refs_6_
  54.7 4.5 %shard_map.184 = (bf16[512,256]{1,0:T(8,128)(2,1)S(1)}, f32[4,1,256]{2,1,0:T(1,128)S(1)}) custom-call(s32[8]{0:T(128)S(1)} %get-tuple-element.212.page_req, s32[8]{0:T(128)S(1)} %get-tuple-element.211.page_slot, bf16[592,512]{1,0:T(8,128)(2,1)S(1)} %copy-done.1, bf16[592,512]{1,0:T(8,128)(2,1)S(1)} %collective-permute-done.refs_1_, ...), custom_call_target="tpu_custom_call" | custom-call | flops 536870912 | bytes 2686976 | tf_op jit(solution)/shard_map/pallas_call | solution.py:116
  60.9 2.9 %collective-permute-start.3 = (f32[2,2,4,64]{3,2,1,0:T(4,128)S(1)}, f32[2,2,4,64]{3,2,1,0:T(4,128)S(1)}, u32[]{:S(2)}, u32[]{:S(2)}) collective-permute-start(f32[2,2,4,64]{3,2,1,0:T(4,128)S(1)} %bitcast.119), channel_id=1, source_target_pairs={{0,4},{1,5},{2,6},{3,7},{4,0},{5,1},{6,2},{7,3},{8,12},{9,13},{10,... | collective-permute-start | bytes 12296 | tf_op jit(solution)/shard_map/ppermute | solution.py:442
  63.9 4.6 %shard_map.182 = (bf16[512,256]{1,0:T(8,128)(2,1)S(1)}, f32[4,1,256]{2,1,0:T(1,128)S(1)}) custom-call(s32[8]{0:T(128)S(1)} %get-tuple-element.212.page_req, s32[8]{0:T(128)S(1)} %get-tuple-element.211.page_slot, bf16[592,512]{1,0:T(8,128)(2,1)S(1)} %copy-done.1, bf16[592,512]{1,0:T(8,128)(2,1)S(1)} %collective-permute-done.refs_1_, ...), custom_call_target="tpu_custom_call" | custom-call | flops 536870912 | bytes 2686976 | tf_op jit(solution)/shard_map/pallas_call | solution.py:116
  69.7 2.8 %collective-permute-start.11 = (f32[4,1,256]{2,1,0:T(1,128)S(1)}, f32[4,1,256]{2,1,0:T(1,128)S(1)}, u32[]{:S(2)}, u32[]{:S(2)}) collective-permute-start(f32[4,1,256]{2,1,0:T(1,128)S(1)} %get-tuple-element.132), channel_id=1, source_target_pairs={{0,4},{1,5},{2,6},{3,7},{4,0},{5,1},{6,2},{7,3},{8,12},{9,13},{10,... | collective-permute-start | bytes 12296 | tf_op jit(solution)/shard_map/ppermute | solution.py:442
  72.9 3.2 %collective-permute-done.11.their_level = f32[4,1,256]{2,1,0:T(1,128)S(1)} collective-permute-done((f32[4,1,256]{2,1,0:T(1,128)S(1)}, f32[4,1,256]{2,1,0:T(1,128)S(1)}, u32[]{:S(2)}, u32[]{:S(2)}) %collective-permute-start.11) | collective-permute-done | bytes 4128 | tf_op jit(solution)/shard_map/ppermute | solution.py:442
  77.3 4.1 %collective-permute-start.16 = (bf16[64,2048]{1,0:T(8,128)(2,1)S(1)}, bf16[64,2048]{1,0:T(8,128)(2,1)S(1)}, u32[]{:S(2)}, u32[]{:S(2)}) collective-permute-start(bf16[64,2048]{1,0:T(8,128)(2,1)S(1)} %get-tuple-element.142), channel_id=1, source_target_pairs={{0,1},{1,0},{2,3},{3,2},{4,5},{5,4},{6,7},{7,6},{8,9},{9,8},{10,11... | collective-permute-start | bytes 786440 | tf_op jit(solution)/shard_map/ppermute | solution.py:442
  82.7 5.9 %collective-permute-done.16 = bf16[64,2048]{1,0:T(8,128)(2,1)S(1)} collective-permute-done((bf16[64,2048]{1,0:T(8,128)(2,1)S(1)}, bf16[64,2048]{1,0:T(8,128)(2,1)S(1)}, u32[]{:S(2)}, u32[]{:S(2)}) %collective-permute-start.16) | collective-permute-done | bytes 262176 | tf_op jit(solution)/shard_map/ppermute | solution.py:442
  89.0 3.1 %collective-permute-done.15 = bf16[64,2048]{1,0:T(8,128)(2,1)S(1)} collective-permute-done((bf16[64,2048]{1,0:T(8,128)(2,1)S(1)}, bf16[64,2048]{1,0:T(8,128)(2,1)S(1)}, u32[]{:S(2)}, u32[]{:S(2)}) %collective-permute-start.15) | collective-permute-done | bytes 262176 | tf_op jit(solution)/shard_map/ppermute | solution.py:442
  92.1 5.3 %collective-permute-done.17 = bf16[64,2048]{1,0:T(8,128)(2,1)S(1)} collective-permute-done((bf16[64,2048]{1,0:T(8,128)(2,1)S(1)}, bf16[64,2048]{1,0:T(8,128)(2,1)S(1)}, u32[]{:S(2)}, u32[]{:S(2)}) %collective-permute-start.17) | collective-permute-done | bytes 262176 | tf_op jit(solution)/shard_map/ppermute | solution.py:442
  98.0 4.8 %collective-permute-start.21 = (bf16[64,2048]{1,0:T(8,128)(2,1)S(1)}, bf16[64,2048]{1,0:T(8,128)(2,1)S(1)}, u32[]{:S(2)}, u32[]{:S(2)}) collective-permute-start(bf16[64,2048]{1,0:T(8,128)(2,1)S(1)} %multiply_convert_fusion.refs_3_), channel_id=1, source_target_pairs={{0,1},{1,0},{2,3},{3,2},{4,5},{5,4},{6,7},{7,6},{8,9},{9,8},{10,11... | collective-permute-start | bytes 786440 | tf_op jit(solution)/shard_map/ppermute | solution.py:442
  104.4 3.2 %collective-permute-done.19.refs_2_ = bf16[64,2048]{1,0:T(8,128)(2,1)S(1)} collective-permute-done((bf16[64,2048]{1,0:T(8,128)(2,1)S(1)}, bf16[64,2048]{1,0:T(8,128)(2,1)S(1)}, u32[]{:S(2)}, u32[]{:S(2)}) %collective-permute-start.19) | collective-permute-done | bytes 262176 | tf_op jit(solution)/shard_map/ppermute | solution.py:442
  109.5 2.5 %collective-permute-start.22 = (bf16[64,2048]{1,0:T(8,128)(2,1)S(1)}, bf16[64,2048]{1,0:T(8,128)(2,1)S(1)}, u32[]{:S(2)}, u32[]{:S(2)}) collective-permute-start(bf16[64,2048]{1,0:T(8,128)(2,1)S(1)} %collective-permute-done.18.refs_0_), channel_id=1, source_target_pairs={{0,1},{1,0},{2,3},{3,2},{4,5},{5,4},{6,7},{7,6},{8,9},{9,8},{10,11... | collective-permute-start | bytes 786440 | tf_op jit(solution)/shard_map/ppermute | solution.py:442
  115.8 2.6 %collective-permute-start.24 = (bf16[64,2048]{1,0:T(8,128)(2,1)}, bf16[64,2048]{1,0:T(8,128)(2,1)S(1)}, u32[]{:S(2)}, u32[]{:S(2)}) collective-permute-start(bf16[64,2048]{1,0:T(8,128)(2,1)} %collective-permute-done.20.refs_1_), channel_id=1, source_target_pairs={{0,1},{1,0},{2,3},{3,2},{4,5},{5,4},{6,7},{7,6},{8,9},{9,8},{10,11... | collective-permute-start | bytes 786440 | tf_op jit(solution)/shard_map/ppermute | solution.py:442
  120.0 2.3 shard_map.187.refs_0_
  122.3 8.4 %shard_map.188 = bf16[256,2048]{1,0:T(8,128)(2,1)} custom-call(bf16[64,2048]{1,0:T(8,128)(2,1)} %copy-done.14, bf16[64,2048]{1,0:T(8,128)(2,1)} %collective-permute-done.20.refs_1_, bf16[64,2048]{1,0:T(8,128)(2,1)} %copy-done.12, bf16[64,2048]{1,0:T(8,128)(2,1)} %copy-done.4, bf16[1,2048]{1,0:T(2,128)(2,1)} %reshape.550.refs_4_, ...), custom_call_target="tpu_custom_call" | custom-call | flops 2214592512 | bytes 10747904 | tf_op jit(solution)/shard_map/pallas_call | solution.py:263
  130.9 2.3 collective-permute-done.28.refs_1_
  133.2 2.2 shard_map.189.refs_0_
  141.5 15.2 %shard_map.191 = (bf16[256,2048]{1,0:T(8,128)(2,1)}, bf16[256,2048]{1,0:T(8,128)(2,1)}, bf16[256,2048]{1,0:T(8,128)(2,1)}, bf16[256,2048]{1,0:T(8,128)(2,1)}) custom-call(bf16[256,2048]{1,0:T(8,128)(2,1)} %shard_map.187.refs_0_, bf16[256,2048]{1,0:T(8,128)(2,1)} %shard_map.190.refs_1_, bf16[256,2048]{1,0:T(8,128)(2,1)} %collective-permute-done.30.refs_2_, ...), custom_call_target="tpu_custom_call" | custom-call | flops 8254390272 | bytes 25690112 | tf_op jit(solution)/shard_map/pallas_call | solution.py:361
  157.3 8.3 %shard_map.192 = bf16[256,2048]{1,0:T(8,128)(2,1)} custom-call(bf16[64,2048]{1,0:T(8,128)(2,1)} %copy-done.10, bf16[64,2048]{1,0:T(8,128)(2,1)} %copy-done.13, bf16[64,2048]{1,0:T(8,128)(2,1)} %copy-done.11, bf16[64,2048]{1,0:T(8,128)(2,1)} %copy-done.9, bf16[1,2048]{1,0:T(2,128)(2,1)} %reshape.550.refs_4_, bf16[704,2048]{1,0:T(8,128)(2,1)} %bitcast.107, ...), custom_call_target="tpu_custom_call" | custom-call | flops 2214592512 | bytes 10747904 | tf_op jit(solution)/shard_map/pallas_call | solution.py:263
  170.9 15.1 %shard_map.193 = (bf16[64,2048]{1,0:T(8,128)(2,1)}, bf16[64,2048]{1,0:T(8,128)(2,1)}, bf16[64,2048]{1,0:T(8,128)(2,1)}, bf16[64,2048]{1,0:T(8,128)(2,1)}, bf16[6...) custom-call(bf16[256,2048]{1,0:T(8,128)(2,1)} %shard_map.189.refs_0_, ...), custom_call_target="tpu_custom_call" | custom-call | flops 8254390272 | bytes 25690112 | tf_op jit(solution)/shard_map/pallas_call | solution.py:361
  186.0 2.3 collective-permute-done.38
  198.4 5.3 %collective-permute-done.44 = bf16[64,2048]{1,0:T(8,128)(2,1)S(1)} collective-permute-done((bf16[64,2048]{1,0:T(8,128)(2,1)S(1)}, bf16[64,2048]{1,0:T(8,128)(2,1)S(1)}, u32[]{:S(2)}, u32[]{:S(2)}) %collective-permute-start.44) | collective-permute-done | bytes 262176 | tf_op jit(solution)/shard_map/ppermute | solution.py:442
  205.4 3.9 %collective-permute-done.43 = bf16[64,2048]{1,0:T(8,128)(2,1)S(1)} collective-permute-done((bf16[64,2048]{1,0:T(8,128)(2,1)S(1)}, bf16[64,2048]{1,0:T(8,128)(2,1)S(1)}, u32[]{:S(2)}, u32[]{:S(2)}) %collective-permute-start.43) | collective-permute-done | bytes 262176 | tf_op jit(solution)/shard_map/ppermute | solution.py:442
  211.5 7.0 %collective-permute-done.45 = bf16[64,2048]{1,0:T(8,128)(2,1)S(1)} collective-permute-done((bf16[64,2048]{1,0:T(8,128)(2,1)S(1)}, bf16[64,2048]{1,0:T(8,128)(2,1)S(1)}, u32[]{:S(2)}, u32[]{:S(2)}) %collective-permute-start.45) | collective-permute-done | bytes 262176 | tf_op jit(solution)/shard_map/ppermute | solution.py:452
  225.4 4.7 %collective-permute-done.47 = bf16[64,2048]{1,0:T(8,128)(2,1)S(1)} collective-permute-done((bf16[64,2048]{1,0:T(8,128)(2,1)S(1)}, bf16[64,2048]{1,0:T(8,128)(2,1)S(1)}, u32[]{:S(2)}, u32[]{:S(2)}) %collective-permute-start.47) | collective-permute-done | bytes 262176 | tf_op jit(solution)/shard_map/ppermute | solution.py:452
  233.6 5.8 %collective-permute-done.50 = bf16[64,2048]{1,0:T(8,128)(2,1)S(1)} collective-permute-done((bf16[64,2048]{1,0:T(8,128)(2,1)S(1)}, bf16[64,2048]{1,0:T(8,128)(2,1)S(1)}, u32[]{:S(2)}, u32[]{:S(2)}) %collective-permute-start.50) | collective-permute-done | bytes 262176 | tf_op jit(solution)/shard_map/ppermute | solution.py:442
  239.4 3.4 %collective-permute-done.51 = bf16[64,2048]{1,0:T(8,128)(2,1)S(1)} collective-permute-done((bf16[64,2048]{1,0:T(8,128)(2,1)S(1)}, bf16[64,2048]{1,0:T(8,128)(2,1)S(1)}, u32[]{:S(2)}, u32[]{:S(2)}) %collective-permute-start.51) | collective-permute-done | bytes 262176 | tf_op jit(solution)/shard_map/ppermute | solution.py:442
  (247 shorter events, 78.3 us)
Async XLA Ops:
  0.0 24.5 %collective-permute-start.4 = (bf16[64,2048]{1,0:T(8,128)(2,1)}, bf16[64,2048]{1,0:T(8,128)(2,1)S(1)}, u32[]{:S(2)}, u32[]{:S(2)}) collective-permute-start(bf16[64,2048]{1,0:T(8,128)(2,1)} %refs_2_.1), channel_id=1, source_target_pairs={{0,4},{1,5},{2,6},{3,7},{4,0},{5,1},{6,2},{7,3},{8,12},{9,13},{10,... | collective-permute-start | bytes 786440 | tf_op jit(solution)/shard_map/ppermute | solution.py:442
  10.1 36.5 %collective-permute-start = (bf16[592,512]{1,0:T(8,128)(2,1)}, bf16[592,512]{1,0:T(8,128)(2,1)S(1)}, u32[]{:S(2)}, u32[]{:S(2)}) collective-permute-start(bf16[592,512]{1,0:T(8,128)(2,1)} %get-tuple-element.109), channel_id=1, source_target_pairs={{0,1},{1,0},{2,3},{3,2},{4,5},{5,4},{6,7},{7,6},{8,9},{9,8},{10,11... | collective-permute-start | bytes 1818632 | tf_op jit(solution)/shard_map/ppermute | solution.py:442
  11.7 36.8 %collective-permute-start.1 = (bf16[592,512]{1,0:T(8,128)(2,1)}, bf16[592,512]{1,0:T(8,128)(2,1)S(1)}, u32[]{:S(2)}, u32[]{:S(2)}) collective-permute-start(bf16[592,512]{1,0:T(8,128)(2,1)} %get-tuple-element.110), channel_id=1, source_target_pairs={{0,2},{1,3},{2,0},{3,1},{4,6},{5,7},{6,4},{7,5},{8,10},{9,11},{10,... | collective-permute-start | bytes 1818632 | tf_op jit(solution)/shard_map/ppermute | solution.py:442
  13.3 35.2 %collective-permute-start.2 = (bf16[592,512]{1,0:T(8,128)(2,1)}, bf16[592,512]{1,0:T(8,128)(2,1)S(1)}, u32[]{:S(2)}, u32[]{:S(2)}) collective-permute-start(bf16[592,512]{1,0:T(8,128)(2,1)} %get-tuple-element.111), channel_id=1, source_target_pairs={{0,3},{1,2},{2,1},{3,0},{4,7},{5,6},{6,5},{7,4},{8,11},{9,10},{10,... | collective-permute-start | bytes 1818632 | tf_op jit(solution)/shard_map/ppermute | solution.py:442
  27.6 16.4 %collective-permute-start.5 = (bf16[64,512]{1,0:T(8,128)(2,1)}, bf16[64,512]{1,0:T(8,128)(2,1)S(1)}, u32[]{:S(2)}, u32[]{:S(2)}) collective-permute-start(bf16[64,512]{1,0:T(8,128)(2,1)} %get-tuple-element.120), channel_id=1, source_target_pairs={{0,1},{1,0},{2,3},{3,2},{4,5},{5,4},{6,7},{7,6},{8,9},{9,8},{10,11... | collective-permute-start | bytes 196616 | tf_op jit(solution)/shard_map/ppermute | solution.py:442
  43.9 15.3 %collective-permute-start.8 = (bf16[64,2048]{1,0:T(8,128)(2,1)S(1)}, bf16[64,2048]{1,0:T(8,128)(2,1)S(1)}, u32[]{:S(2)}, u32[]{:S(2)}) collective-permute-start(bf16[64,2048]{1,0:T(8,128)(2,1)S(1)} %constant_dynamic-slice_fusion), channel_id=1, source_target_pairs={{0,4},{1,5},{2,6},{3,7},{4,0},{5,1},{6,2},{7,3},{8,12},{9,13},{10,... | collective-permute-start | bytes 786440 | tf_op jit(solution)/shard_map/ppermute | solution.py:442
  63.8 12.3 %collective-permute-start.10 = (bf16[512,256]{1,0:T(8,128)(2,1)S(1)}, bf16[512,256]{1,0:T(8,128)(2,1)S(1)}, u32[]{:S(2)}, u32[]{:S(2)}) collective-permute-start(bf16[512,256]{1,0:T(8,128)(2,1)S(1)} %get-tuple-element.131), channel_id=1, source_target_pairs={{0,4},{1,5},{2,6},{3,7},{4,0},{5,1},{6,2},{7,3},{8,12},{9,13},{10,... | collective-permute-start | bytes 786440 | tf_op jit(solution)/shard_map/ppermute | solution.py:442
  77.3 11.3 %collective-permute-start.16 = (bf16[64,2048]{1,0:T(8,128)(2,1)S(1)}, bf16[64,2048]{1,0:T(8,128)(2,1)S(1)}, u32[]{:S(2)}, u32[]{:S(2)}) collective-permute-start(bf16[64,2048]{1,0:T(8,128)(2,1)S(1)} %get-tuple-element.142), channel_id=1, source_target_pairs={{0,1},{1,0},{2,3},{3,2},{4,5},{5,4},{6,7},{7,6},{8,9},{9,8},{10,11... | collective-permute-start | bytes 786440 | tf_op jit(solution)/shard_map/ppermute | solution.py:442
  82.6 9.5 %collective-permute-start.15 = (bf16[64,2048]{1,0:T(8,128)(2,1)S(1)}, bf16[64,2048]{1,0:T(8,128)(2,1)S(1)}, u32[]{:S(2)}, u32[]{:S(2)}) collective-permute-start(bf16[64,2048]{1,0:T(8,128)(2,1)S(1)} %get-tuple-element.145), channel_id=1, source_target_pairs={{0,1},{1,0},{2,3},{3,2},{4,5},{5,4},{6,7},{7,6},{8,9},{9,8},{10,11... | collective-permute-start | bytes 786440 | tf_op jit(solution)/shard_map/ppermute | solution.py:442
  97.9 9.7 %collective-permute-start.19 = (bf16[64,2048]{1,0:T(8,128)(2,1)S(1)}, bf16[64,2048]{1,0:T(8,128)(2,1)S(1)}, u32[]{:S(2)}, u32[]{:S(2)}) collective-permute-start(bf16[64,2048]{1,0:T(8,128)(2,1)S(1)} %multiply_convert_fusion.refs_3_), channel_id=1, source_target_pairs={{0,4},{1,5},{2,6},{3,7},{4,0},{5,1},{6,2},{7,3},{8,12},{9,13},{10,... | collective-permute-start | bytes 786440 | tf_op jit(solution)/shard_map/ppermute | solution.py:442
  97.9 11.5 %collective-permute-start.18 = (bf16[64,2048]{1,0:T(8,128)(2,1)S(1)}, bf16[64,2048]{1,0:T(8,128)(2,1)S(1)}, u32[]{:S(2)}, u32[]{:S(2)}) collective-permute-start(bf16[64,2048]{1,0:T(8,128)(2,1)S(1)} %multiply_convert_fusion.refs_3_), channel_id=1, source_target_pairs={{0,2},{1,3},{2,0},{3,1},{4,6},{5,7},{6,4},{7,5},{8,10},{9,11},{10,... | collective-permute-start | bytes 786440 | tf_op jit(solution)/shard_map/ppermute | solution.py:442
  98.0 15.4 %collective-permute-start.21 = (bf16[64,2048]{1,0:T(8,128)(2,1)S(1)}, bf16[64,2048]{1,0:T(8,128)(2,1)S(1)}, u32[]{:S(2)}, u32[]{:S(2)}) collective-permute-start(bf16[64,2048]{1,0:T(8,128)(2,1)S(1)} %multiply_convert_fusion.refs_3_), channel_id=1, source_target_pairs={{0,1},{1,0},{2,3},{3,2},{4,5},{5,4},{6,7},{7,6},{8,9},{9,8},{10,11... | collective-permute-start | bytes 786440 | tf_op jit(solution)/shard_map/ppermute | solution.py:442
  102.8 12.2 %collective-permute-start.25 = (bf16[64,2048]{1,0:T(8,128)(2,1)S(1)}, bf16[64,2048]{1,0:T(8,128)(2,1)S(1)}, u32[]{:S(2)}, u32[]{:S(2)}) collective-permute-start(bf16[64,2048]{1,0:T(8,128)(2,1)S(1)} %multiply_convert_fusion.refs_3_), channel_id=1, source_target_pairs={{0,16},{8,24},{16,0},{24,8},{1,17},{9,25},{17,1},{25,9},{2,18},{10... | collective-permute-start | bytes 786440 | tf_op jit(solution)/shard_map/ppermute | solution.py:452
  113.3 17.4 %collective-permute-start.23 = (bf16[64,2048]{1,0:T(8,128)(2,1)S(1)}, bf16[64,2048]{1,0:T(8,128)(2,1)S(1)}, u32[]{:S(2)}, u32[]{:S(2)}) collective-permute-start(bf16[64,2048]{1,0:T(8,128)(2,1)S(1)} %collective-permute-done.19.refs_2_), channel_id=1, source_target_pairs={{0,1},{1,0},{2,3},{3,2},{4,5},{5,4},{6,7},{7,6},{8,9},{9,8},{10,11... | collective-permute-start | bytes 786440 | tf_op jit(solution)/shard_map/ppermute | solution.py:442
  113.4 17.4 %collective-permute-start.26 = (bf16[64,2048]{1,0:T(8,128)(2,1)S(1)}, bf16[64,2048]{1,0:T(8,128)(2,1)}, u32[]{:S(2)}, u32[]{:S(2)}) collective-permute-start(bf16[64,2048]{1,0:T(8,128)(2,1)S(1)} %collective-permute-done.18.refs_0_), channel_id=1, source_target_pairs={{0,16},{8,24},{16,0},{24,8},{1,17},{9,25},{17,1},{25,9},{2,18},{10... | collective-permute-start | bytes 786440 | tf_op jit(solution)/shard_map/ppermute | solution.py:452
  115.1 15.8 %collective-permute-start.27 = (bf16[64,2048]{1,0:T(8,128)(2,1)S(1)}, bf16[64,2048]{1,0:T(8,128)(2,1)}, u32[]{:S(2)}, u32[]{:S(2)}) collective-permute-start(bf16[64,2048]{1,0:T(8,128)(2,1)S(1)} %collective-permute-done.19.refs_2_), channel_id=1, source_target_pairs={{0,16},{8,24},{16,0},{24,8},{1,17},{9,25},{17,1},{25,9},{2,18},{10... | collective-permute-start | bytes 786440 | tf_op jit(solution)/shard_map/ppermute | solution.py:452
  115.8 15.1 %collective-permute-start.24 = (bf16[64,2048]{1,0:T(8,128)(2,1)}, bf16[64,2048]{1,0:T(8,128)(2,1)S(1)}, u32[]{:S(2)}, u32[]{:S(2)}) collective-permute-start(bf16[64,2048]{1,0:T(8,128)(2,1)} %collective-permute-done.20.refs_1_), channel_id=1, source_target_pairs={{0,1},{1,0},{2,3},{3,2},{4,5},{5,4},{6,7},{7,6},{8,9},{9,8},{10,11... | collective-permute-start | bytes 786440 | tf_op jit(solution)/shard_map/ppermute | solution.py:442
  118.3 14.9 %collective-permute-start.28 = (bf16[64,2048]{1,0:T(8,128)(2,1)}, bf16[64,2048]{1,0:T(8,128)(2,1)}, u32[]{:S(2)}, u32[]{:S(2)}) collective-permute-start(bf16[64,2048]{1,0:T(8,128)(2,1)} %collective-permute-done.20.refs_1_), channel_id=1, source_target_pairs={{0,16},{8,24},{16,0},{24,8},{1,17},{9,25},{17,1},{25,9},{2,18},{10... | collective-permute-start | bytes 786440 | tf_op jit(solution)/shard_map/ppermute | solution.py:452
  130.7 9.8 %collective-permute-start.30 = (bf16[256,2048]{1,0:T(8,128)(2,1)S(1)}, bf16[256,2048]{1,0:T(8,128)(2,1)}, u32[]{:S(2)}, u32[]{:S(2)}) collective-permute-start(bf16[256,2048]{1,0:T(8,128)(2,1)S(1)} %copy-done.7), channel_id=1, source_target_pairs={{0,8},{8,0},{16,24},{24,16},{1,9},{9,1},{17,25},{25,17},{2,10},{10... | collective-permute-start | bytes 3145736 | tf_op jit(solution)/shard_map/ppermute | solution.py:452
  138.3 27.4 %collective-permute-start.35 = (bf16[256,2048]{1,0:T(8,128)(2,1)}, bf16[256,2048]{1,0:T(8,128)(2,1)S(1)}, u32[]{:S(2)}, u32[]{:S(2)}) collective-permute-start(bf16[256,2048]{1,0:T(8,128)(2,1)} %shard_map.189.refs_0_), channel_id=1, source_target_pairs={{0,1},{1,0},{2,3},{3,2},{4,5},{5,4},{6,7},{7,6},{8,9},{9,8},{10,11... | collective-permute-start | bytes 3145736 | tf_op jit(solution)/shard_map/ppermute | solution.py:442
  156.7 9.9 %collective-permute-start.33 = (bf16[256,2048]{1,0:T(8,128)(2,1)}, bf16[256,2048]{1,0:T(8,128)(2,1)S(1)}, u32[]{:S(2)}, u32[]{:S(2)}) collective-permute-start(bf16[256,2048]{1,0:T(8,128)(2,1)} %get-tuple-element.168), channel_id=1, source_target_pairs={{0,8},{8,0},{16,24},{24,16},{1,9},{9,1},{17,25},{25,17},{2,10},{10... | collective-permute-start | bytes 3145736 | tf_op jit(solution)/shard_map/ppermute | solution.py:452
  157.0 13.8 %collective-permute-start.36 = (bf16[256,2048]{1,0:T(8,128)(2,1)S(1)}, bf16[256,2048]{1,0:T(8,128)(2,1)}, u32[]{:S(2)}, u32[]{:S(2)}) collective-permute-start(bf16[256,2048]{1,0:T(8,128)(2,1)S(1)} %copy-done.6), channel_id=1, source_target_pairs={{0,8},{8,0},{16,24},{24,16},{1,9},{9,1},{17,25},{25,17},{2,10},{10... | collective-permute-start | bytes 3145736 | tf_op jit(solution)/shard_map/ppermute | solution.py:452
  168.5 19.7 %collective-permute-start.38 = (bf16[192,2048]{1,0:T(8,128)(2,1)S(1)}, bf16[192,2048]{1,0:T(8,128)(2,1)S(1)}, u32[]{:S(2)}, u32[]{:S(2)}) collective-permute-start(bf16[192,2048]{1,0:T(8,128)(2,1)S(1)} %slice.285), channel_id=1, source_target_pairs={{0,1},{1,0},{2,3},{3,2},{4,5},{5,4},{6,7},{7,6},{8,9},{9,8},{10,11... | collective-permute-start | bytes 2359304 | tf_op jit(solution)/shard_map/ppermute | solution.py:442
  188.8 22.1 %collective-permute-start.32 = (bf16[256,2048]{1,0:T(8,128)(2,1)S(1)}, bf16[256,2048]{1,0:T(8,128)(2,1)S(1)}, u32[]{:S(2)}, u32[]{:S(2)}) collective-permute-start(bf16[256,2048]{1,0:T(8,128)(2,1)S(1)} %copy-done.30), channel_id=1, source_target_pairs={{0,8},{8,0},{16,24},{24,16},{1,9},{9,1},{17,25},{25,17},{2,10},{10... | collective-permute-start | bytes 3145736 | tf_op jit(solution)/shard_map/ppermute | solution.py:452
  188.9 43.0 %collective-permute-start.34 = (bf16[64,2048]{1,0:T(8,128)(2,1)S(1)}, bf16[64,2048]{1,0:T(8,128)(2,1)S(1)}, u32[]{:S(2)}, u32[]{:S(2)}) collective-permute-start(bf16[64,2048]{1,0:T(8,128)(2,1)S(1)} %slice.284), channel_id=1, source_target_pairs={{0,1},{1,0},{2,3},{3,2},{4,5},{5,4},{6,7},{7,6},{8,9},{9,8},{10,11... | collective-permute-start | bytes 786440 | tf_op jit(solution)/shard_map/ppermute | solution.py:442
  192.2 11.5 %collective-permute-start.44 = (bf16[64,2048]{1,0:T(8,128)(2,1)S(1)}, bf16[64,2048]{1,0:T(8,128)(2,1)S(1)}, u32[]{:S(2)}, u32[]{:S(2)}) collective-permute-start(bf16[64,2048]{1,0:T(8,128)(2,1)S(1)} %add_convert_fusion.12), channel_id=1, source_target_pairs={{0,1},{1,0},{2,3},{3,2},{4,5},{5,4},{6,7},{7,6},{8,9},{9,8},{10,11... | collective-permute-start | bytes 786440 | tf_op jit(solution)/shard_map/ppermute | solution.py:442
  195.2 14.1 %collective-permute-start.43 = (bf16[64,2048]{1,0:T(8,128)(2,1)S(1)}, bf16[64,2048]{1,0:T(8,128)(2,1)S(1)}, u32[]{:S(2)}, u32[]{:S(2)}) collective-permute-start(bf16[64,2048]{1,0:T(8,128)(2,1)S(1)} %add_convert_fusion.11), channel_id=1, source_target_pairs={{0,1},{1,0},{2,3},{3,2},{4,5},{5,4},{6,7},{7,6},{8,9},{9,8},{10,11... | collective-permute-start | bytes 786440 | tf_op jit(solution)/shard_map/ppermute | solution.py:442
  197.9 22.8 %collective-permute-start.42 = (bf16[64,2048]{1,0:T(8,128)(2,1)S(1)}, bf16[64,2048]{1,0:T(8,128)(2,1)S(1)}, u32[]{:S(2)}, u32[]{:S(2)}) collective-permute-start(bf16[64,2048]{1,0:T(8,128)(2,1)S(1)} %add_convert_fusion.10), channel_id=1, source_target_pairs={{0,1},{1,0},{2,3},{3,2},{4,5},{5,4},{6,7},{7,6},{8,9},{9,8},{10,11... | collective-permute-start | bytes 786440 | tf_op jit(solution)/shard_map/ppermute | solution.py:442
  203.7 18.7 %collective-permute-start.41 = (bf16[64,2048]{1,0:T(8,128)(2,1)S(1)}, bf16[64,2048]{1,0:T(8,128)(2,1)S(1)}, u32[]{:S(2)}, u32[]{:S(2)}) collective-permute-start(bf16[64,2048]{1,0:T(8,128)(2,1)S(1)} %add_convert_fusion.9), channel_id=1, source_target_pairs={{0,1},{1,0},{2,3},{3,2},{4,5},{5,4},{6,7},{7,6},{8,9},{9,8},{10,11... | collective-permute-start | bytes 786440 | tf_op jit(solution)/shard_map/ppermute | solution.py:442
  211.0 13.2 %collective-permute-start.48 = (bf16[64,2048]{1,0:T(8,128)(2,1)S(1)}, bf16[64,2048]{1,0:T(8,128)(2,1)S(1)}, u32[]{:S(2)}, u32[]{:S(2)}) collective-permute-start(bf16[64,2048]{1,0:T(8,128)(2,1)S(1)} %add_convert_fusion.7), channel_id=1, source_target_pairs={{0,16},{8,24},{16,0},{24,8},{1,17},{9,25},{17,1},{25,9},{2,18},{10... | collective-permute-start | bytes 786440 | tf_op jit(solution)/shard_map/ppermute | solution.py:452
  222.5 11.1 %collective-permute-start.46 = (bf16[64,2048]{1,0:T(8,128)(2,1)S(1)}, bf16[64,2048]{1,0:T(8,128)(2,1)S(1)}, u32[]{:S(2)}, u32[]{:S(2)}) collective-permute-start(bf16[64,2048]{1,0:T(8,128)(2,1)S(1)} %add_convert_fusion.4), channel_id=1, source_target_pairs={{0,16},{8,24},{16,0},{24,8},{1,17},{9,25},{17,1},{25,9},{2,18},{10... | collective-permute-start | bytes 786440 | tf_op jit(solution)/shard_map/ppermute | solution.py:452
  231.9 10.9 %collective-permute-start.51 = (bf16[64,2048]{1,0:T(8,128)(2,1)S(1)}, bf16[64,2048]{1,0:T(8,128)(2,1)S(1)}, u32[]{:S(2)}, u32[]{:S(2)}) collective-permute-start(bf16[64,2048]{1,0:T(8,128)(2,1)S(1)} %add_convert_fusion.3), channel_id=1, source_target_pairs={{0,4},{1,5},{2,6},{3,7},{4,0},{5,1},{6,2},{7,3},{8,12},{9,13},{10,... | collective-permute-start | bytes 786440 | tf_op jit(solution)/shard_map/ppermute | solution.py:442
  (53 other events, 673.1 us)

commit v12 on v11

--- a/solution.py
+++ b/solution.py
@@ -244,14 +244,14 @@
         block.astype(jnp.float32) * scalar[...].astype(jnp.float32), axis=1, keepdims=True
     )
     scale = 1.0 / (1.0 + jnp.exp(-logit))
-    across, along = (((1,), (1,)), ((), ())), (((0,), (0,)), ((), ()))
+    across = (((1,), (1,)), ((), ()))
     copies[0].wait()
-    gate = lax.dot_general(gate_v[...], block, across, preferred_element_type=jnp.float32)
+    gate = lax.dot_general(block, gate_v[...], across, preferred_element_type=jnp.float32)
     copies[1].wait()
-    upper = lax.dot_general(up_v[...], block, across, preferred_element_type=jnp.float32)
+    upper = lax.dot_general(block, up_v[...], across, preferred_element_type=jnp.float32)
     hidden = (silu(gate) * upper).astype(jnp.bfloat16)
     copies[2].wait()
-    result = lax.dot_general(hidden, down_v[...], along, preferred_element_type=jnp.float32)
+    result = jnp.dot(hidden, down_v[...], preferred_element_type=jnp.float32)
     out[...] = (scale * result).astype(jnp.bfloat16)
 
 
@@ -495,7 +495,6 @@
         if m > 2:
             far[m], far[m - 2] = tie((far[m], far[m - 2]))
         far[m] = send(far[m], 0, *members[m])
-    quarter, far[1] = tie((quarter, far[1]))
     quarters = [send(quarter, 1, 0, 0)]
     page_ids = (
         rel_exp[: len(members), None] * pages_here + jnp.arange(pages_here, dtype=i32)[None, :]
@@ -542,16 +541,15 @@
             tok_rows,
         )
 
+    quarters.append(swap_y(quarters[0]))
     theirs, their_level = attend_half(1, far)
     theirs, their_level, quarters = tie((theirs, their_level, quarters))
     theirs, their_level = send(theirs, 1, 0, 0), send(their_level, 1, 0, 0)
-    quarters.append(swap_y(quarters[0]))
-    gates = jnp.stack([send(gates, dh, 0, 0) for dh in range(2)])
+    quarters += [send_req(q, 0, dc) for dc in range(1, nc) for q in quarters[:2]]
     mine, level = attend_half(0, [])
     mine, level, gates, quarters = tie((mine, level, gates, quarters))
-    quarters += [send_req(q, 0, dc) for dc in range(1, nc) for q in quarters[:2]]
-    gates = jnp.stack([send_req(gates, dy, 0) for dy in range(ny)])
-    theirs, their_level, gates, quarters = tie((theirs, their_level, gates, quarters))
+    gates = jnp.stack([send(gates, dh, 0, 0) for dh in range(2)])
+    theirs, their_level, gates = tie((theirs, their_level, gates))
 
     stays, comes = {}, {}
     proj = out_proj
@@ -568,6 +566,8 @@
     line = send(line, 0, 1, 0)
     stream = sum([come.astype(f32) for come in comes[0]], resid.astype(f32) + stays[0])
     stream = stream + line.astype(f32)
+    gates = jnp.stack([send_req(gates, dy, 0) for dy in range(ny)])
+    stream, gates = tie((stream, gates))
     normed = rms_normed(stream, norm_gain)
     gates = jnp.stack([send_req(gates, 0, dc) for dc in range(nc)], axis=1)
     gates = gates.reshape(ny, nc, 4, nx, TOPK, tok_rows)
@@ -638,8 +638,10 @@
             chunks[dy + 1, dc] += [send_req(part, 0, dc) for part in chunks[dy + 1, 0][1:]]
         gone = [add_up([part[dx] for part in parts]).astype(bf16) for dx in range(1, nx)]
         kept[dy] = [part[0] for part in parts]
+        waiting = [go[cuts[1]] for go in gone]
         comes[dy] = [
-            [send(go[rows], 0, 0, -dx) for dx, go in enumerate(gone, 1)] for rows in cuts
+            [send(go[rows], 0, 0, -dx) for dx, go in enumerate(gone, 1)]
+            for rows in (cuts if dy + 2 < ny else cuts[:1])
         ]
         following = [chunks[dy + 1, dc] for dc in cores]
         following, _ = tie((following, gone))
@@ -647,7 +649,7 @@
             chunks[dy + 1, dc] = following[dc]
     end = ny - 1
     answers = answers_of(end, cores, [], [4 * nx] + [nx] * (nc - 1))
-    answers, comes[end - 1][0] = tie((answers, comes[end - 1][0]))
+    answers, comes, kept = tie((answers, comes, kept))
     answer = answers[0]
     others = [[send_req(part, 0, -dc) for part in answers[dc][::-1]][::-1] for dc in cores[1:]]
 
@@ -662,6 +664,8 @@
         gone = [go.astype(bf16) for go in gone]
         last[p] = [send(go, 0, 0, -dx) for dx, go in enumerate(gone, 1)]
         others, _ = tie((others, gone))
+    waiting, _ = tie((waiting, gone))
+    comes[end - 1].append([send(go, 0, 0, -dx) for dx, go in enumerate(waiting, 1)])
 
     def line_of(dy, p):
         if dy < end:

time: 245 us -> 228 us (0.931)
  starting transfers between devices: 61.3 us -> 46.4 us
    ppermute x31, starting transfers between devices: 47.7 us -> 36.7 us  [send(): return lax.ppermute(value, 'exp', pairs)]
    ppermute x20, waiting for transfers between devices: 18.8 us -> 13.2 us  [send_req(): return lax.ppermute(value, 'req', pairs)]
    ppermute x31, waiting for transfers between devices: 63.4 us -> 68.5 us  [send(): return lax.ppermute(value, 'exp', pairs)]
    ppermute x20, starting transfers between devices: 12 us -> 8.18 us  [send_req(): return lax.ppermute(value, 'req', pairs)]
  transfers between devices with their start and end apart: 52 -> 52, of which waited for: 24 -> 24; matrix products, arithmetic and copies ran while one was open for 9% -> 10% of each run, Pallas kernels for 29% -> 30%
where the time goes in v12:
time: 228 us; the launch traced here: 227 us
  waiting for transfers between devices  81.8 us (36%)
  Pallas kernels  70.2 us (31%)
  starting transfers between devices  46.4 us (20%)
  other arithmetic  16.3 us (7%)
  local copies, waits for them, and re-layouts  10.6 us (5%)
    ppermute x31, waiting for transfers between devices, send(): return lax.ppermute(value, 'exp', pairs)  68.5 us
    ppermute x31, starting transfers between devices, send(): return lax.ppermute(value, 'exp', pairs)  36.7 us
    pallas_call x2, Pallas kernels, routed_expert(): pl.pallas_call(functools.partial(routed_kernel, parts, len(more), entries...  30.5 us
    pallas_call x2, Pallas kernels, shared_expert(): pl.pallas_call(functools.partial(shared_kernel, len(pieces)), out_shape=j...  15.1 us
    ppermute x20, waiting for transfers between devices, send_req(): return lax.ppermute(value, 'req', pairs)  13.2 us
    pallas_call x2, Pallas kernels, attend(): pl.pallas_call(functools.partial(attend_kernel, members, tokens, tok_rows...  9.14 us
    ppermute x20, starting transfers between devices, send_req(): return lax.ppermute(value, 'req', pairs)  8.18 us
    pallas_call x3, Pallas kernels, join(): pl.pallas_call(join_kernel, out_shape=jax.ShapeDtypeStruct((len(parts) *...  6.74 us
  transfers between devices with their start and end apart: 52, of which 24 were waited for; matrix products, arithmetic and copies ran while one was open for 10% of the time, Pallas kernels for 30%

profile of v12, /device:TPU:0, one launch (start us, length us, event | category | flops | bytes accessed | tf_op | source)
XLA Modules:
  0.0 227.2 jit_solution(7403363980257591773)
XLA Ops:
  0.0 4.1 %collective-permute-start.3 = (bf16[64,2048]{1,0:T(8,128)(2,1)}, bf16[64,2048]{1,0:T(8,128)(2,1)S(1)}, u32[]{:S(2)}, u32[]{:S(2)}) collective-permute-start(bf16[64,2048]{1,0:T(8,128)(2,1)} %refs_2_.1), channel_id=1, source_target_pairs={{0,4},{1,5},{2,6},{3,7},{4,0},{5,1},{6,2},{7,3},{8,12},{9,13},{10,... | collective-permute-start | bytes 786440 | tf_op jit(solution)/shard_map/ppermute | solution.py:442
  6.1 4.0 %shard_map.181 = (bf16[592,512]{1,0:T(8,128)(2,1)}, bf16[592,512]{1,0:T(8,128)(2,1)}, bf16[592,512]{1,0:T(8,128)(2,1)}, bf16[592,512]{1,0:T(8,128)(2,1)}) custom-call(s32[8]{0:T(128)} %stack.175.order, bf16[256,2048]{1,0:T(8,128)(2,1)} %bitcast.111, bf16[256,2048]{1,0:T(8,128)(2,1)} %bitcast.112, bf16[64,2048]{1,0:T(8,128)(2,1)} %refs_2_.1, f32[4,512]{1,0:T(4,128)} %pad.4.refs_3_), custom_call_target="tpu_custom_call" | custom-call | bytes 4849664 | tf_op jit(solution)/shard_map/pallas_call | solution.py:58
  26.1 2.3 %shard_map.183 = (bf16[64,512]{1,0:T(8,128)(2,1)}, bf16[64,512]{1,0:T(8,128)(2,1)}, bf16[64,512]{1,0:T(8,128)(2,1)}, bf16[64,512]{1,0:T(8,128)(2,1)}) custom-call(s32[8]{0:T(128)} %stack.175.order, bf16[64,2048]{1,0:T(8,128)(2,1)} %copy-done.16), custom_call_target="tpu_custom_call" | custom-call | bytes 524288 | tf_op jit(solution)/shard_map/pallas_call | solution.py:58
  30.0 14.5 %collective-permute-done.7.refs_0_ = bf16[64,2048]{1,0:T(8,128)(2,1)S(1)} collective-permute-done((bf16[64,2048]{1,0:T(8,128)(2,1)}, bf16[64,2048]{1,0:T(8,128)(2,1)S(1)}, u32[]{:S(2)}, u32[]{:S(2)}) %collective-permute-start.7) | collective-permute-done | bytes 262176 | tf_op jit(solution)/shard_map/ppermute | solution.py:442
  48.9 2.1 collective-permute-done.5.refs_6_
  51.1 2.3 collective-permute-done.6.refs_7_
  55.3 4.5 %shard_map.184 = (bf16[512,256]{1,0:T(8,128)(2,1)S(1)}, f32[4,1,256]{2,1,0:T(1,128)S(1)}) custom-call(s32[8]{0:T(128)S(1)} %get-tuple-element.218.page_req, s32[8]{0:T(128)S(1)} %get-tuple-element.217.page_slot, bf16[592,512]{1,0:T(8,128)(2,1)S(1)} %copy-done.1, bf16[592,512]{1,0:T(8,128)(2,1)S(1)} %collective-permute-done.refs_1_, ...), custom_call_target="tpu_custom_call" | custom-call | flops 536870912 | bytes 2686976 | tf_op jit(solution)/shard_map/pallas_call | solution.py:116
  60.4 2.1 collective-permute-start.11
  62.5 4.6 %shard_map.182 = (bf16[512,256]{1,0:T(8,128)(2,1)S(1)}, f32[4,1,256]{2,1,0:T(1,128)S(1)}) custom-call(s32[8]{0:T(128)S(1)} %get-tuple-element.218.page_req, s32[8]{0:T(128)S(1)} %get-tuple-element.217.page_slot, bf16[592,512]{1,0:T(8,128)(2,1)S(1)} %copy-done.1, bf16[592,512]{1,0:T(8,128)(2,1)S(1)} %collective-permute-done.refs_1_, ...), custom_call_target="tpu_custom_call" | custom-call | flops 536870912 | bytes 2686976 | tf_op jit(solution)/shard_map/pallas_call | solution.py:116
  70.1 5.6 %collective-permute-done.13 = f32[2,2,4,64]{3,2,1,0:T(4,128)S(1)} collective-permute-done((f32[2,2,4,64]{3,2,1,0:T(4,128)S(1)}, f32[2,2,4,64]{3,2,1,0:T(4,128)S(1)}, u32[]{:S(2)}, u32[]{:S(2)}) %collective-permute-start.13) | collective-permute-done | bytes 4128 | tf_op jit(solution)/shard_map/ppermute | solution.py:442
  80.4 5.9 %collective-permute-done.15 = bf16[64,2048]{1,0:T(8,128)(2,1)S(1)} collective-permute-done((bf16[64,2048]{1,0:T(8,128)(2,1)S(1)}, bf16[64,2048]{1,0:T(8,128)(2,1)S(1)}, u32[]{:S(2)}, u32[]{:S(2)}) %collective-permute-start.15) | collective-permute-done | bytes 262176 | tf_op jit(solution)/shard_map/ppermute | solution.py:442
  87.1 3.2 %collective-permute-done.17 = f32[2,2,2,4,64]{4,3,2,1,0:T(4,128)S(1)} collective-permute-done((f32[2,2,2,4,64]{4,3,2,1,0:T(4,128)S(1)}, f32[2,2,2,4,64]{4,3,2,1,0:T(4,128)S(1)}, u32[]{:S(2)}, u32[]{:S(2)}) %collective-permute-start.17) | collective-permute-done | bytes 8224 | tf_op jit(solution)/shard_map/ppermute | solution.py:452
  90.3 2.5 %collective-permute-done.16 = bf16[64,2048]{1,0:T(8,128)(2,1)S(1)} collective-permute-done((bf16[64,2048]{1,0:T(8,128)(2,1)S(1)}, bf16[64,2048]{1,0:T(8,128)(2,1)S(1)}, u32[]{:S(2)}, u32[]{:S(2)}) %collective-permute-start.16) | collective-permute-done | bytes 262176 | tf_op jit(solution)/shard_map/ppermute | solution.py:442
  98.3 6.6 %collective-permute-done.21.refs_2_ = bf16[64,2048]{1,0:T(8,128)(2,1)S(1)} collective-permute-done((bf16[64,2048]{1,0:T(8,128)(2,1)S(1)}, bf16[64,2048]{1,0:T(8,128)(2,1)S(1)}, u32[]{:S(2)}, u32[]{:S(2)}) %collective-permute-start.21) | collective-permute-done | bytes 262176 | tf_op jit(solution)/shard_map/ppermute | solution.py:442
  106.8 2.1 collective-permute-start.22
  111.7 3.3 %collective-permute-done.20.refs_0_ = bf16[64,2048]{1,0:T(8,128)(2,1)S(1)} collective-permute-done((bf16[64,2048]{1,0:T(8,128)(2,1)}, bf16[64,2048]{1,0:T(8,128)(2,1)S(1)}, u32[]{:S(2)}, u32[]{:S(2)}) %collective-permute-start.20) | collective-permute-done | bytes 262176 | tf_op jit(solution)/shard_map/ppermute | solution.py:442
  115.6 2.3 shard_map.189.refs_0_
  117.9 7.6 %shard_map.187 = bf16[256,2048]{1,0:T(8,128)(2,1)} custom-call(bf16[64,2048]{1,0:T(8,128)(2,1)} %collective-permute-done.19.refs_0_, bf16[64,2048]{1,0:T(8,128)(2,1)} %collective-permute-done.23.refs_1_, bf16[64,2048]{1,0:T(8,128)(2,1)} %copy-done.12, bf16[64,2048]{1,0:T(8,128)(2,1)} %copy-done.4, bf16[1,2048]{1,0:T(2,128)(2,1)} %reshape.550.refs_4_, ...), custom_call_target="tpu_custom_call" | custom-call | flops 2214592512 | bytes 10747904 | tf_op jit(solution)/shard_map/pallas_call | solution.py:263
  125.6 2.9 %collective-permute-done.28.refs_1_ = bf16[64,2048]{1,0:T(8,128)(2,1)} collective-permute-done((bf16[64,2048]{1,0:T(8,128)(2,1)}, bf16[64,2048]{1,0:T(8,128)(2,1)}, u32[]{:S(2)}, u32[]{:S(2)}) %collective-permute-start.28) | collective-permute-done | bytes 262176 | tf_op jit(solution)/shard_map/ppermute | solution.py:452
  128.5 2.2 shard_map.188.refs_0_
  130.8 2.2 shard_map.190.refs_1_
  136.9 15.3 %shard_map.191 = (bf16[256,2048]{1,0:T(8,128)(2,1)}, bf16[256,2048]{1,0:T(8,128)(2,1)}, bf16[256,2048]{1,0:T(8,128)(2,1)}, bf16[256,2048]{1,0:T(8,128)(2,1)}) custom-call(bf16[256,2048]{1,0:T(8,128)(2,1)} %shard_map.189.refs_0_, bf16[256,2048]{1,0:T(8,128)(2,1)} %shard_map.190.refs_1_, bf16[256,2048]{1,0:T(8,128)(2,1)} %collective-permute-done.31.refs_2_, ...), custom_call_target="tpu_custom_call" | custom-call | flops 8254390272 | bytes 25690112 | tf_op jit(solution)/shard_map/pallas_call | solution.py:361
  152.7 7.6 %shard_map.192 = bf16[256,2048]{1,0:T(8,128)(2,1)} custom-call(bf16[64,2048]{1,0:T(8,128)(2,1)} %copy-done.10, bf16[64,2048]{1,0:T(8,128)(2,1)} %copy-done.13, bf16[64,2048]{1,0:T(8,128)(2,1)} %copy-done.11, bf16[64,2048]{1,0:T(8,128)(2,1)} %copy-done.9, bf16[1,2048]{1,0:T(2,128)(2,1)} %reshape.550.refs_4_, bf16[704,2048]{1,0:T(8,128)(2,1)} %bitcast.107, ...), custom_call_target="tpu_custom_call" | custom-call | flops 2214592512 | bytes 10747904 | tf_op jit(solution)/shard_map/pallas_call | solution.py:263
  164.4 15.2 %shard_map.193 = (bf16[64,2048]{1,0:T(8,128)(2,1)}, bf16[64,2048]{1,0:T(8,128)(2,1)}, bf16[64,2048]{1,0:T(8,128)(2,1)}, bf16[64,2048]{1,0:T(8,128)(2,1)}, bf16[6...) custom-call(bf16[256,2048]{1,0:T(8,128)(2,1)} %shard_map.188.refs_0_, ...), custom_call_target="tpu_custom_call" | custom-call | flops 8254390272 | bytes 25690112 | tf_op jit(solution)/shard_map/pallas_call | solution.py:361
  179.7 3.3 %collective-permute-done.36 = bf16[192,2048]{1,0:T(8,128)(2,1)S(1)} collective-permute-done((bf16[192,2048]{1,0:T(8,128)(2,1)S(1)}, bf16[192,2048]{1,0:T(8,128)(2,1)S(1)}, u32[]{:S(2)}, u32[]{:S(2)}) %collective-permute-start.36) | collective-permute-done | bytes 786464 | tf_op jit(solution)/shard_map/ppermute | solution.py:442
  183.5 2.3 %collective-permute-done.39 = bf16[256,2048]{1,0:T(8,128)(2,1)S(1)} collective-permute-done((bf16[256,2048]{1,0:T(8,128)(2,1)}, bf16[256,2048]{1,0:T(8,128)(2,1)S(1)}, u32[]{:S(2)}, u32[]{:S(2)}) %collective-permute-start.39) | collective-permute-done | bytes 1048608 | tf_op jit(solution)/shard_map/ppermute | solution.py:452
  193.8 2.3 %collective-permute-done.44 = bf16[64,2048]{1,0:T(8,128)(2,1)S(1)} collective-permute-done((bf16[64,2048]{1,0:T(8,128)(2,1)S(1)}, bf16[64,2048]{1,0:T(8,128)(2,1)S(1)}, u32[]{:S(2)}, u32[]{:S(2)}) %collective-permute-start.44) | collective-permute-done | bytes 262176 | tf_op jit(solution)/shard_map/ppermute | solution.py:442
  196.8 4.9 %collective-permute-done.43 = bf16[64,2048]{1,0:T(8,128)(2,1)S(1)} collective-permute-done((bf16[64,2048]{1,0:T(8,128)(2,1)S(1)}, bf16[64,2048]{1,0:T(8,128)(2,1)S(1)}, u32[]{:S(2)}, u32[]{:S(2)}) %collective-permute-start.43) | collective-permute-done | bytes 262176 | tf_op jit(solution)/shard_map/ppermute | solution.py:442
  204.7 2.7 %collective-permute-done.42 = bf16[64,2048]{1,0:T(8,128)(2,1)S(1)} collective-permute-done((bf16[64,2048]{1,0:T(8,128)(2,1)S(1)}, bf16[64,2048]{1,0:T(8,128)(2,1)S(1)}, u32[]{:S(2)}, u32[]{:S(2)}) %collective-permute-start.42) | collective-permute-done | bytes 262176 | tf_op jit(solution)/shard_map/ppermute | solution.py:442
  208.0 4.9 %collective-permute-done.41 = bf16[64,2048]{1,0:T(8,128)(2,1)S(1)} collective-permute-done((bf16[64,2048]{1,0:T(8,128)(2,1)S(1)}, bf16[64,2048]{1,0:T(8,128)(2,1)S(1)}, u32[]{:S(2)}, u32[]{:S(2)}) %collective-permute-start.41) | collective-permute-done | bytes 262176 | tf_op jit(solution)/shard_map/ppermute | solution.py:442
  215.9 2.1 collective-permute-start.51
  219.9 6.3 %collective-permute-done.50 = bf16[64,2048]{1,0:T(8,128)(2,1)S(1)} collective-permute-done((bf16[64,2048]{1,0:T(8,128)(2,1)S(1)}, bf16[64,2048]{1,0:T(8,128)(2,1)S(1)}, u32[]{:S(2)}, u32[]{:S(2)}) %collective-permute-start.50) | collective-permute-done | bytes 262176 | tf_op jit(solution)/shard_map/ppermute | solution.py:442
  (244 shorter events, 71.2 us)
Async XLA Ops:
  0.0 25.4 %collective-permute-start.3 = (bf16[64,2048]{1,0:T(8,128)(2,1)}, bf16[64,2048]{1,0:T(8,128)(2,1)S(1)}, u32[]{:S(2)}, u32[]{:S(2)}) collective-permute-start(bf16[64,2048]{1,0:T(8,128)(2,1)} %refs_2_.1), channel_id=1, source_target_pairs={{0,4},{1,5},{2,6},{3,7},{4,0},{5,1},{6,2},{7,3},{8,12},{9,13},{10,... | collective-permute-start | bytes 786440 | tf_op jit(solution)/shard_map/ppermute | solution.py:442
  10.1 37.9 %collective-permute-start = (bf16[592,512]{1,0:T(8,128)(2,1)}, bf16[592,512]{1,0:T(8,128)(2,1)S(1)}, u32[]{:S(2)}, u32[]{:S(2)}) collective-permute-start(bf16[592,512]{1,0:T(8,128)(2,1)} %get-tuple-element.112), channel_id=1, source_target_pairs={{0,1},{1,0},{2,3},{3,2},{4,5},{5,4},{6,7},{7,6},{8,9},{9,8},{10,11... | collective-permute-start | bytes 1818632 | tf_op jit(solution)/shard_map/ppermute | solution.py:442
  11.7 37.0 %collective-permute-start.1 = (bf16[592,512]{1,0:T(8,128)(2,1)}, bf16[592,512]{1,0:T(8,128)(2,1)S(1)}, u32[]{:S(2)}, u32[]{:S(2)}) collective-permute-start(bf16[592,512]{1,0:T(8,128)(2,1)} %get-tuple-element.113), channel_id=1, source_target_pairs={{0,2},{1,3},{2,0},{3,1},{4,6},{5,7},{6,4},{7,5},{8,10},{9,11},{10,... | collective-permute-start | bytes 1818632 | tf_op jit(solution)/shard_map/ppermute | solution.py:442
  13.2 35.7 %collective-permute-start.2 = (bf16[592,512]{1,0:T(8,128)(2,1)}, bf16[592,512]{1,0:T(8,128)(2,1)S(1)}, u32[]{:S(2)}, u32[]{:S(2)}) collective-permute-start(bf16[592,512]{1,0:T(8,128)(2,1)} %get-tuple-element.114), channel_id=1, source_target_pairs={{0,3},{1,2},{2,1},{3,0},{4,7},{5,6},{6,5},{7,4},{8,11},{9,10},{10,... | collective-permute-start | bytes 1818632 | tf_op jit(solution)/shard_map/ppermute | solution.py:442
  14.4 30.2 %collective-permute-start.7 = (bf16[64,2048]{1,0:T(8,128)(2,1)}, bf16[64,2048]{1,0:T(8,128)(2,1)S(1)}, u32[]{:S(2)}, u32[]{:S(2)}) collective-permute-start(bf16[64,2048]{1,0:T(8,128)(2,1)} %constant_dynamic-slice_fusion), channel_id=1, source_target_pairs={{0,4},{1,5},{2,6},{3,7},{4,0},{5,1},{6,2},{7,3},{8,12},{9,13},{10,... | collective-permute-start | bytes 786440 | tf_op jit(solution)/shard_map/ppermute | solution.py:442
  28.4 18.2 %collective-permute-start.4 = (bf16[64,512]{1,0:T(8,128)(2,1)}, bf16[64,512]{1,0:T(8,128)(2,1)S(1)}, u32[]{:S(2)}, u32[]{:S(2)}) collective-permute-start(bf16[64,512]{1,0:T(8,128)(2,1)} %get-tuple-element.123), channel_id=1, source_target_pairs={{0,1},{1,0},{2,3},{3,2},{4,5},{5,4},{6,7},{7,6},{8,9},{9,8},{10,11... | collective-permute-start | bytes 196616 | tf_op jit(solution)/shard_map/ppermute | solution.py:442
  44.6 15.2 %collective-permute-start.8 = (bf16[64,2048]{1,0:T(8,128)(2,1)S(1)}, bf16[64,2048]{1,0:T(8,128)(2,1)S(1)}, u32[]{:S(2)}, u32[]{:S(2)}) collective-permute-start(bf16[64,2048]{1,0:T(8,128)(2,1)S(1)} %collective-permute-done.7.refs_0_), channel_id=1, source_target_pairs={{0,16},{8,24},{16,0},{24,8},{1,17},{9,25},{17,1},{25,9},{2,18},{10... | collective-permute-start | bytes 786440 | tf_op jit(solution)/shard_map/ppermute | solution.py:456
  60.4 15.4 %collective-permute-start.11 = (bf16[512,256]{1,0:T(8,128)(2,1)S(1)}, bf16[512,256]{1,0:T(8,128)(2,1)S(1)}, u32[]{:S(2)}, u32[]{:S(2)}) collective-permute-start(bf16[512,256]{1,0:T(8,128)(2,1)S(1)} %get-tuple-element.133), channel_id=1, source_target_pairs={{0,4},{1,5},{2,6},{3,7},{4,0},{5,1},{6,2},{7,3},{8,12},{9,13},{10,... | collective-permute-start | bytes 786440 | tf_op jit(solution)/shard_map/ppermute | solution.py:442
  78.8 11.5 %collective-permute-start.14 = (bf16[64,2048]{1,0:T(8,128)(2,1)S(1)}, bf16[64,2048]{1,0:T(8,128)(2,1)S(1)}, u32[]{:S(2)}, u32[]{:S(2)}) collective-permute-start(bf16[64,2048]{1,0:T(8,128)(2,1)S(1)} %get-tuple-element.145), channel_id=1, source_target_pairs={{0,1},{1,0},{2,3},{3,2},{4,5},{5,4},{6,7},{7,6},{8,9},{9,8},{10,11... | collective-permute-start | bytes 786440 | tf_op jit(solution)/shard_map/ppermute | solution.py:442
  93.3 11.6 %collective-permute-start.21 = (bf16[64,2048]{1,0:T(8,128)(2,1)S(1)}, bf16[64,2048]{1,0:T(8,128)(2,1)S(1)}, u32[]{:S(2)}, u32[]{:S(2)}) collective-permute-start(bf16[64,2048]{1,0:T(8,128)(2,1)S(1)} %multiply_convert_fusion.refs_3_), channel_id=1, source_target_pairs={{0,4},{1,5},{2,6},{3,7},{4,0},{5,1},{6,2},{7,3},{8,12},{9,13},{10,... | collective-permute-start | bytes 786440 | tf_op jit(solution)/shard_map/ppermute | solution.py:442
  95.1 10.4 %collective-permute-start.19 = (bf16[64,2048]{1,0:T(8,128)(2,1)S(1)}, bf16[64,2048]{1,0:T(8,128)(2,1)}, u32[]{:S(2)}, u32[]{:S(2)}) collective-permute-start(bf16[64,2048]{1,0:T(8,128)(2,1)S(1)} %multiply_convert_fusion.refs_3_), channel_id=1, source_target_pairs={{0,2},{1,3},{2,0},{3,1},{4,6},{5,7},{6,4},{7,5},{8,10},{9,11},{10,... | collective-permute-start | bytes 786440 | tf_op jit(solution)/shard_map/ppermute | solution.py:442
  96.8 12.1 %collective-permute-start.18 = (bf16[64,2048]{1,0:T(8,128)(2,1)S(1)}, bf16[64,2048]{1,0:T(8,128)(2,1)S(1)}, u32[]{:S(2)}, u32[]{:S(2)}) collective-permute-start(bf16[64,2048]{1,0:T(8,128)(2,1)S(1)} %multiply_convert_fusion.refs_3_), channel_id=1, source_target_pairs={{0,1},{1,0},{2,3},{3,2},{4,5},{5,4},{6,7},{7,6},{8,9},{9,8},{10,11... | collective-permute-start | bytes 786440 | tf_op jit(solution)/shard_map/ppermute | solution.py:442
  97.7 11.6 %collective-permute-start.25 = (bf16[64,2048]{1,0:T(8,128)(2,1)S(1)}, bf16[64,2048]{1,0:T(8,128)(2,1)S(1)}, u32[]{:S(2)}, u32[]{:S(2)}) collective-permute-start(bf16[64,2048]{1,0:T(8,128)(2,1)S(1)} %multiply_convert_fusion.refs_3_), channel_id=1, source_target_pairs={{0,16},{8,24},{16,0},{24,8},{1,17},{9,25},{17,1},{25,9},{2,18},{10... | collective-permute-start | bytes 786440 | tf_op jit(solution)/shard_map/ppermute | solution.py:452
  105.5 9.5 %collective-permute-start.20 = (bf16[64,2048]{1,0:T(8,128)(2,1)}, bf16[64,2048]{1,0:T(8,128)(2,1)S(1)}, u32[]{:S(2)}, u32[]{:S(2)}) collective-permute-start(bf16[64,2048]{1,0:T(8,128)(2,1)} %collective-permute-done.19.refs_0_), channel_id=1, source_target_pairs={{0,1},{1,0},{2,3},{3,2},{4,5},{5,4},{6,7},{7,6},{8,9},{9,8},{10,11... | collective-permute-start | bytes 786440 | tf_op jit(solution)/shard_map/ppermute | solution.py:442
  106.8 18.6 %collective-permute-start.22 = (bf16[64,2048]{1,0:T(8,128)(2,1)S(1)}, bf16[64,2048]{1,0:T(8,128)(2,1)S(1)}, u32[]{:S(2)}, u32[]{:S(2)}) collective-permute-start(bf16[64,2048]{1,0:T(8,128)(2,1)S(1)} %collective-permute-done.21.refs_2_), channel_id=1, source_target_pairs={{0,1},{1,0},{2,3},{3,2},{4,5},{5,4},{6,7},{7,6},{8,9},{9,8},{10,11... | collective-permute-start | bytes 786440 | tf_op jit(solution)/shard_map/ppermute | solution.py:442
  108.9 16.7 %collective-permute-start.26 = (bf16[64,2048]{1,0:T(8,128)(2,1)}, bf16[64,2048]{1,0:T(8,128)(2,1)}, u32[]{:S(2)}, u32[]{:S(2)}) collective-permute-start(bf16[64,2048]{1,0:T(8,128)(2,1)} %collective-permute-done.19.refs_0_), channel_id=1, source_target_pairs={{0,16},{8,24},{16,0},{24,8},{1,17},{9,25},{17,1},{25,9},{2,18},{10... | collective-permute-start | bytes 786440 | tf_op jit(solution)/shard_map/ppermute | solution.py:452
  109.4 16.2 %collective-permute-start.27 = (bf16[64,2048]{1,0:T(8,128)(2,1)S(1)}, bf16[64,2048]{1,0:T(8,128)(2,1)}, u32[]{:S(2)}, u32[]{:S(2)}) collective-permute-start(bf16[64,2048]{1,0:T(8,128)(2,1)S(1)} %collective-permute-done.21.refs_2_), channel_id=1, source_target_pairs={{0,16},{8,24},{16,0},{24,8},{1,17},{9,25},{17,1},{25,9},{2,18},{10... | collective-permute-start | bytes 786440 | tf_op jit(solution)/shard_map/ppermute | solution.py:452
  111.7 13.9 %collective-permute-start.24 = (bf16[64,2048]{1,0:T(8,128)(2,1)}, bf16[64,2048]{1,0:T(8,128)(2,1)S(1)}, u32[]{:S(2)}, u32[]{:S(2)}) collective-permute-start(bf16[64,2048]{1,0:T(8,128)(2,1)} %collective-permute-done.23.refs_1_), channel_id=1, source_target_pairs={{0,1},{1,0},{2,3},{3,2},{4,5},{5,4},{6,7},{7,6},{8,9},{9,8},{10,11... | collective-permute-start | bytes 786440 | tf_op jit(solution)/shard_map/ppermute | solution.py:442
  114.9 13.6 %collective-permute-start.28 = (bf16[64,2048]{1,0:T(8,128)(2,1)}, bf16[64,2048]{1,0:T(8,128)(2,1)}, u32[]{:S(2)}, u32[]{:S(2)}) collective-permute-start(bf16[64,2048]{1,0:T(8,128)(2,1)} %collective-permute-done.23.refs_1_), channel_id=1, source_target_pairs={{0,16},{8,24},{16,0},{24,8},{1,17},{9,25},{17,1},{25,9},{2,18},{10... | collective-permute-start | bytes 786440 | tf_op jit(solution)/shard_map/ppermute | solution.py:452
  133.6 26.7 %collective-permute-start.30 = (bf16[256,2048]{1,0:T(8,128)(2,1)}, bf16[256,2048]{1,0:T(8,128)(2,1)}, u32[]{:S(2)}, u32[]{:S(2)}) collective-permute-start(bf16[256,2048]{1,0:T(8,128)(2,1)} %shard_map.188.refs_0_), channel_id=1, source_target_pairs={{0,1},{1,0},{2,3},{3,2},{4,5},{5,4},{6,7},{7,6},{8,9},{9,8},{10,11... | collective-permute-start | bytes 3145736 | tf_op jit(solution)/shard_map/ppermute | solution.py:442
  152.1 9.4 %collective-permute-start.35 = (bf16[256,2048]{1,0:T(8,128)(2,1)}, bf16[256,2048]{1,0:T(8,128)(2,1)S(1)}, u32[]{:S(2)}, u32[]{:S(2)}) collective-permute-start(bf16[256,2048]{1,0:T(8,128)(2,1)} %get-tuple-element.174), channel_id=1, source_target_pairs={{0,8},{8,0},{16,24},{24,16},{1,9},{9,1},{17,25},{25,17},{2,10},{10... | collective-permute-start | bytes 3145736 | tf_op jit(solution)/shard_map/ppermute | solution.py:452
  152.3 12.1 %collective-permute-start.33 = (bf16[256,2048]{1,0:T(8,128)(2,1)S(1)}, bf16[256,2048]{1,0:T(8,128)(2,1)}, u32[]{:S(2)}, u32[]{:S(2)}) collective-permute-start(bf16[256,2048]{1,0:T(8,128)(2,1)S(1)} %copy-done.6), channel_id=1, source_target_pairs={{0,8},{8,0},{16,24},{24,16},{1,9},{9,1},{17,25},{25,17},{2,10},{10... | collective-permute-start | bytes 3145736 | tf_op jit(solution)/shard_map/ppermute | solution.py:452
  161.1 18.6 %collective-permute-start.37 = (bf16[256,2048]{1,0:T(8,128)(2,1)S(1)}, bf16[256,2048]{1,0:T(8,128)(2,1)S(1)}, u32[]{:S(2)}, u32[]{:S(2)}) collective-permute-start(bf16[256,2048]{1,0:T(8,128)(2,1)S(1)} %copy-done.29), channel_id=1, source_target_pairs={{0,8},{8,0},{16,24},{24,16},{1,9},{9,1},{17,25},{25,17},{2,10},{10... | collective-permute-start | bytes 3145736 | tf_op jit(solution)/shard_map/ppermute | solution.py:452
  163.4 19.6 %collective-permute-start.36 = (bf16[192,2048]{1,0:T(8,128)(2,1)S(1)}, bf16[192,2048]{1,0:T(8,128)(2,1)S(1)}, u32[]{:S(2)}, u32[]{:S(2)}) collective-permute-start(bf16[192,2048]{1,0:T(8,128)(2,1)S(1)} %slice.283), channel_id=1, source_target_pairs={{0,1},{1,0},{2,3},{3,2},{4,5},{5,4},{6,7},{7,6},{8,9},{9,8},{10,11... | collective-permute-start | bytes 2359304 | tf_op jit(solution)/shard_map/ppermute | solution.py:442
  188.5 13.3 %collective-permute-start.43 = (bf16[64,2048]{1,0:T(8,128)(2,1)S(1)}, bf16[64,2048]{1,0:T(8,128)(2,1)S(1)}, u32[]{:S(2)}, u32[]{:S(2)}) collective-permute-start(bf16[64,2048]{1,0:T(8,128)(2,1)S(1)} %add_convert_fusion.11), channel_id=1, source_target_pairs={{0,1},{1,0},{2,3},{3,2},{4,5},{5,4},{6,7},{7,6},{8,9},{9,8},{10,11... | collective-permute-start | bytes 786440 | tf_op jit(solution)/shard_map/ppermute | solution.py:442
  191.1 16.2 %collective-permute-start.42 = (bf16[64,2048]{1,0:T(8,128)(2,1)S(1)}, bf16[64,2048]{1,0:T(8,128)(2,1)S(1)}, u32[]{:S(2)}, u32[]{:S(2)}) collective-permute-start(bf16[64,2048]{1,0:T(8,128)(2,1)S(1)} %add_convert_fusion.10), channel_id=1, source_target_pairs={{0,1},{1,0},{2,3},{3,2},{4,5},{5,4},{6,7},{7,6},{8,9},{9,8},{10,11... | collective-permute-start | bytes 786440 | tf_op jit(solution)/shard_map/ppermute | solution.py:442
  191.8 21.2 %collective-permute-start.41 = (bf16[64,2048]{1,0:T(8,128)(2,1)S(1)}, bf16[64,2048]{1,0:T(8,128)(2,1)S(1)}, u32[]{:S(2)}, u32[]{:S(2)}) collective-permute-start(bf16[64,2048]{1,0:T(8,128)(2,1)S(1)} %add_convert_fusion.9), channel_id=1, source_target_pairs={{0,1},{1,0},{2,3},{3,2},{4,5},{5,4},{6,7},{7,6},{8,9},{9,8},{10,11... | collective-permute-start | bytes 786440 | tf_op jit(solution)/shard_map/ppermute | solution.py:442
  193.4 24.6 %collective-permute-start.40 = (bf16[64,2048]{1,0:T(8,128)(2,1)S(1)}, bf16[64,2048]{1,0:T(8,128)(2,1)S(1)}, u32[]{:S(2)}, u32[]{:S(2)}) collective-permute-start(bf16[64,2048]{1,0:T(8,128)(2,1)S(1)} %slice.284), channel_id=1, source_target_pairs={{0,1},{1,0},{2,3},{3,2},{4,5},{5,4},{6,7},{7,6},{8,9},{9,8},{10,11... | collective-permute-start | bytes 786440 | tf_op jit(solution)/shard_map/ppermute | solution.py:442
  201.9 11.8 %collective-permute-start.48 = (bf16[64,2048]{1,0:T(8,128)(2,1)S(1)}, bf16[64,2048]{1,0:T(8,128)(2,1)S(1)}, u32[]{:S(2)}, u32[]{:S(2)}) collective-permute-start(bf16[64,2048]{1,0:T(8,128)(2,1)S(1)} %add_convert_fusion.7), channel_id=1, source_target_pairs={{0,16},{8,24},{16,0},{24,8},{1,17},{9,25},{17,1},{25,9},{2,18},{10... | collective-permute-start | bytes 786440 | tf_op jit(solution)/shard_map/ppermute | solution.py:452
  203.2 10.5 %collective-permute-start.49 = (bf16[64,2048]{1,0:T(8,128)(2,1)S(1)}, bf16[64,2048]{1,0:T(8,128)(2,1)S(1)}, u32[]{:S(2)}, u32[]{:S(2)}) collective-permute-start(bf16[64,2048]{1,0:T(8,128)(2,1)S(1)} %add_convert_fusion.6), channel_id=1, source_target_pairs={{0,2},{1,3},{2,0},{3,1},{4,6},{5,7},{6,4},{7,5},{8,10},{9,11},{10,... | collective-permute-start | bytes 786440 | tf_op jit(solution)/shard_map/ppermute | solution.py:442
  214.4 11.8 %collective-permute-start.50 = (bf16[64,2048]{1,0:T(8,128)(2,1)S(1)}, bf16[64,2048]{1,0:T(8,128)(2,1)S(1)}, u32[]{:S(2)}, u32[]{:S(2)}) collective-permute-start(bf16[64,2048]{1,0:T(8,128)(2,1)S(1)} %add_convert_fusion.2), channel_id=1, source_target_pairs={{0,2},{1,3},{2,0},{3,1},{4,6},{5,7},{6,4},{7,5},{8,10},{9,11},{10,... | collective-permute-start | bytes 786440 | tf_op jit(solution)/shard_map/ppermute | solution.py:442
  215.9 10.3 %collective-permute-start.51 = (bf16[64,2048]{1,0:T(8,128)(2,1)S(1)}, bf16[64,2048]{1,0:T(8,128)(2,1)S(1)}, u32[]{:S(2)}, u32[]{:S(2)}) collective-permute-start(bf16[64,2048]{1,0:T(8,128)(2,1)S(1)} %add_convert_fusion.3), channel_id=1, source_target_pairs={{0,4},{1,5},{2,6},{3,7},{4,0},{5,1},{6,2},{7,3},{8,12},{9,13},{10,... | collective-permute-start | bytes 786440 | tf_op jit(solution)/shard_map/ppermute | solution.py:442
  (51 other events, 582.0 us)

commit v13 on v12

--- a/solution.py
+++ b/solution.py
@@ -288,7 +288,7 @@
     more, refs = refs[2 : 2 + extras], refs[2 + extras :]
     (gate_w, up_w, down_w), refs = refs[:3], refs[3:]
     outs, refs = refs[: sum(cuts)], refs[sum(cuts) :]
-    rows, packed, gate_v, up_v, down_v, more_v, sems = refs
+    rows, packed, hidden, gate_v, up_v, down_v, more_v, sems = refs
     moves, chunk_copies = [], []
     for c, n in enumerate(parts):
         at = 0
@@ -296,7 +296,12 @@
         for piece in pieces[sum(parts[:c]) : sum(parts[: c + 1])]:
             moves.append((piece, rows.at[c, pl.ds(at, piece.shape[0])]))
             at += piece.shape[0]
-    moves += [(gate_w.at[0], gate_v), (up_w.at[0], up_v), (down_w.at[0], down_v)]
+    hidden_units = gate_v.shape[1]
+    slices = [slice(n, min(n + 512, hidden_units)) for n in range(0, hidden_units, 512)]
+    for part in slices:
+        units = pl.ds(part.start, part.stop - part.start)
+        moves += [(w.at[0, :, units], v.at[:, units]) for w, v in ((gate_w, gate_v), (up_w, up_v))]
+    moves.append((down_w.at[0], down_v))
     at = 0
     for extra in more:
         moves.append((extra, more_v.at[pl.ds(at, extra.shape[0])]))
@@ -318,17 +323,19 @@
         packed[c * entries : (c + 1) * entries, :] = jnp.dot(
             picks[c], rows[c], preferred_element_type=jnp.float32
         ).astype(jnp.bfloat16)
-    copies[total].wait()
-    gate = jnp.dot(packed[...], gate_v[...], preferred_element_type=jnp.float32)
-    copies[total + 1].wait()
-    upper = jnp.dot(packed[...], up_v[...], preferred_element_type=jnp.float32)
-    hidden = (silu(gate) * upper).astype(jnp.bfloat16)
-    copies[total + 2].wait()
-    answer = jnp.dot(hidden, down_v[...], preferred_element_type=jnp.float32).astype(
+    for k, part in enumerate(slices):
+        copies[total + 2 * k].wait()
+        gate = jnp.dot(packed[...], gate_v[:, part], preferred_element_type=jnp.float32)
+        copies[total + 2 * k + 1].wait()
+        upper = jnp.dot(packed[...], up_v[:, part], preferred_element_type=jnp.float32)
+        hidden[:, part] = (silu(gate) * upper).astype(jnp.bfloat16)
+    behind = total + 2 * len(slices)
+    copies[behind].wait()
+    answer = jnp.dot(hidden[...], down_v[...], preferred_element_type=jnp.float32).astype(
         jnp.bfloat16
     )
     for i in range(extras):
-        copies[total + 3 + i].wait()
+        copies[behind + 1 + i].wait()
     for c in range(count):
         scaled = answer[c * entries : (c + 1) * entries, :].astype(jnp.float32) * weights[c]
         placed = lax.dot_general(
@@ -366,11 +373,12 @@
         scratch_shapes=[
             pltpu.VMEM((count, size, width), jnp.bfloat16),
             pltpu.VMEM((count * entries, width), jnp.bfloat16),
+            pltpu.VMEM((count * entries, hidden), jnp.bfloat16),
             pltpu.VMEM((width, hidden), jnp.bfloat16),
             pltpu.VMEM((width, hidden), jnp.bfloat16),
             pltpu.VMEM((hidden, width), jnp.bfloat16),
             pltpu.VMEM((more_rows, width), jnp.bfloat16),
-            pltpu.SemaphoreType.DMA((total + 3 + len(more),)),
+            pltpu.SemaphoreType.DMA((total + 1 + 2 * -(-hidden // 512) + len(more),)),
         ],
         compiler_params=pltpu.CompilerParams(vmem_limit_bytes=56 * 1024 * 1024),
         cost_estimate=pl.CostEstimate(
@@ -495,6 +503,7 @@
         if m > 2:
             far[m], far[m - 2] = tie((far[m], far[m - 2]))
         far[m] = send(far[m], 0, *members[m])
+    quarter, far[1] = tie((quarter, far[1]))
     quarters = [send(quarter, 1, 0, 0)]
     page_ids = (
         rel_exp[: len(members), None] * pages_here + jnp.arange(pages_here, dtype=i32)[None, :]
@@ -514,7 +523,7 @@
     twins = slot_expert == own_expert
     copies = jnp.sum(twins.astype(i32))
     own_rank = jnp.sum((twins & (slot_ids < own_slot)).astype(i32))
-    order = [1, 3, 2, 0]
+    order = [3, 2, 1, 0]
     rel_rows = jnp.stack([rel_exp.reshape(4, nx)[i] for i in order], axis=1).reshape(-1)
     rel_slots = (rel_req[:, None] * exp_count + rel_rows[None, :]).reshape(-1)
     named = (route_expert == own_expert).reshape(slot_count, tok_rows, TOPK)[rel_slots]
@@ -541,14 +550,16 @@
             tok_rows,
         )
 
-    quarters.append(swap_y(quarters[0]))
     theirs, their_level = attend_half(1, far)
-    theirs, their_level, quarters = tie((theirs, their_level, quarters))
+    theirs, their_level = tie((theirs, their_level))
+    near_blocks, _ = tie((blocks, theirs))
     theirs, their_level = send(theirs, 1, 0, 0), send(their_level, 1, 0, 0)
-    quarters += [send_req(q, 0, dc) for dc in range(1, nc) for q in quarters[:2]]
+    blocks = near_blocks
     mine, level = attend_half(0, [])
     mine, level, gates, quarters = tie((mine, level, gates, quarters))
+    quarters.append(swap_y(quarters[0]))
     gates = jnp.stack([send(gates, dh, 0, 0) for dh in range(2)])
+    quarters += [send_req(q, 0, dc) for dc in range(1, nc) for q in quarters[:2]]
     theirs, their_level, gates = tie((theirs, their_level, gates))
 
     stays, comes = {}, {}
@@ -586,19 +597,19 @@
     chunks = {(0, 0): [join(halves[0])]}
     for dc in range(1, nc):
         chunks[0, dc] = [send_req(chunks[0, 0][0], 0, dc)]
-    over_x, over_y, shared, row_gate = tie((over_x, over_y, shared, row_gate))
-    for dy in range(1, ny):
-        half = join([over_y[i, dy] for i in order])
-        chunks[dy, 0] = [half] + [send(half, 0, 0, dx) for dx in range(1, nx)]
-        for dc in range(1, nc):
-            chunks[dy, dc] = [send_req(half, 0, dc)]
-        over_x, _ = tie((over_x, half))
+    over_x, shared, row_gate = tie((over_x, shared, row_gate))
     for dx in range(1, nx):
         half = [over_x[i, dx] for i in order]
         chunks[0, 0].append(join(half))
         for dc in range(1, nc):
             chunks[0, dc].append(send_req(chunks[0, 0][dx], 0, dc))
         halves.append(half)
+    over_y, _ = tie((over_y, chunks[0, 0]))
+    for dy in range(1, ny):
+        half = join([over_y[i, dy] for i in order])
+        chunks[dy, 0] = [half] + [send(half, 0, 0, dx) for dx in range(1, nx)]
+        for dc in range(1, nc):
+            chunks[dy, dc] = [send_req(half, 0, dc)]
 
     def answers_of(dy, dcs, more, cuts):
         return routed_expert(
@@ -618,7 +629,7 @@
 
     cores = list(range(nc))
     kept, comes = {}, {}
-    cuts = [slice(0, 3 * tok_rows), slice(3 * tok_rows, 4 * tok_rows)]
+    cuts = [slice(0, 2 * tok_rows)] + [slice(p * tok_rows, (p + 1) * tok_rows) for p in (2, 3)]
     for dy in range(ny - 1):
         answers = answers_of(dy, cores, [], [nx] * nc)
         if dy:
@@ -638,7 +649,7 @@
             chunks[dy + 1, dc] += [send_req(part, 0, dc) for part in chunks[dy + 1, 0][1:]]
         gone = [add_up([part[dx] for part in parts]).astype(bf16) for dx in range(1, nx)]
         kept[dy] = [part[0] for part in parts]
-        waiting = [go[cuts[1]] for go in gone]
+        waiting = [[go[rows] for go in gone] for rows in cuts[1:]]
         comes[dy] = [
             [send(go[rows], 0, 0, -dx) for dx, go in enumerate(gone, 1)]
             for rows in (cuts if dy + 2 < ny else cuts[:1])
@@ -653,7 +664,7 @@
     answer = answers[0]
     others = [[send_req(part, 0, -dc) for part in answers[dc][::-1]][::-1] for dc in cores[1:]]
 
-    turns = [1, 2, 0, 3]
+    turns = [0, 1, 2, 3]
     block = lambda a, p: a[p * tok_rows : (p + 1) * tok_rows]
     last = {}
     for p in turns:
@@ -665,30 +676,35 @@
         last[p] = [send(go, 0, 0, -dx) for dx, go in enumerate(gone, 1)]
         others, _ = tie((others, gone))
     waiting, _ = tie((waiting, gone))
-    comes[end - 1].append([send(go, 0, 0, -dx) for dx, go in enumerate(waiting, 1)])
+    comes[end - 1] += [
+        [send(go, 0, 0, -dx) for dx, go in enumerate(piece, 1)] for piece in waiting
+    ]
 
     def line_of(dy, p):
         if dy < end:
-            arrived = [come if p == 3 else block(come, p) for come in comes[dy][p // 3]]
+            if p < 2:
+                arrived = [block(come, p) for come in comes[dy][0]]
+            else:
+                arrived = comes[dy][p - 1]
             return add_up([block(part, p) for part in kept[dy]] + arrived)
         return add_up([answer[p]] + [block(other[0], p) for other in others] + last[p])
 
     home, near = {}, {}
-    for turn, p in enumerate(turns):
+    for p in turns:
         goes = [line_of(dy, p).astype(bf16) for dy in range(1, ny)]
         home[p] = [send_req(go, -dy, 0) for dy, go in enumerate(goes, 1)]
-        if turn == 1:
-            go = add_up([line_of(0, 1)] + home[1]).astype(bf16)
-            near[1] = send(go, 0, 1, 0)
+        if p == 1:
+            go = add_up([line_of(0, 0)] + home[0]).astype(bf16)
+            near[0] = send(go, 0, 1, 0)
             goes.append(go)
-        if turn + 1 < len(turns):
-            after = turns[turn + 1]
-            last[after], _ = tie((last[after], goes))
-    far = add_up([line_of(0, 2)] + home[2] + [near[1]]).astype(bf16)
-    home[0], _ = tie((home[0], far))
-    far = send(far, 1, 0, 0)
-    near[0] = send(add_up([line_of(0, 0)] + home[0]).astype(bf16), 0, 1, 0)
-    total = add_up([stream, line_of(0, 3)] + home[3] + [near[0], far])
+        if p == 2:
+            go = add_up([line_of(0, 1)] + home[1] + [near[0]]).astype(bf16)
+            far = send(go, 1, 0, 0)
+            goes.append(go)
+        if p < 3:
+            last[p + 1], _ = tie((last[p + 1], goes))
+    near[2] = send(add_up([line_of(0, 2)] + home[2]).astype(bf16), 0, 1, 0)
+    total = add_up([stream, line_of(0, 3)] + home[3] + [near[2], far])
     return total.astype(bf16)
 
 

time: 228 us -> 261 us (1.14)
  waiting for transfers between devices: 81.8 us -> 101 us
  starting transfers between devices: 46.4 us -> 56.4 us
    ppermute x20, waiting for transfers between devices: 13.2 us -> 28.4 us  [send_req(): return lax.ppermute(value, 'req', pairs)]
    ppermute x31 -> x32, starting transfers between devices: 36.7 us -> 45.3 us  [send(): return lax.ppermute(value, 'exp', pairs)]
    ppermute x1, waiting for transfers between devices: 0.01 us -> 3.61 us  [swap_y(): return lax.ppermute(value, 'req', pairs)]
    ppermute x31 -> x32, waiting for transfers between devices: 68.5 us -> 69.4 us  [send(): return lax.ppermute(value, 'exp', pairs)]
  transfers between devices with their start and end apart: 52 -> 53, of which waited for: 24 -> 27; matrix products, arithmetic and copies ran while one was open for 10% -> 9% of each run, Pallas kernels for 30% -> 27%
where the time goes in v13:
time: 261 us; the launch traced here: 259 us
  waiting for transfers between devices  101 us (39%)
  Pallas kernels  70.5 us (27%)
  starting transfers between devices  56.4 us (22%)
  other arithmetic  17.3 us (7%)
  local copies, waits for them, and re-layouts  12 us (5%)
    ppermute x32, waiting for transfers between devices, send(): return lax.ppermute(value, 'exp', pairs)  69.4 us
    ppermute x32, starting transfers between devices, send(): return lax.ppermute(value, 'exp', pairs)  45.3 us
    pallas_call x2, Pallas kernels, routed_expert(): pl.pallas_call(functools.partial(routed_kernel, parts, len(more), entries...  30.1 us
    ppermute x20, waiting for transfers between devices, send_req(): return lax.ppermute(value, 'req', pairs)  28.4 us
    pallas_call x2, Pallas kernels, shared_expert(): pl.pallas_call(functools.partial(shared_kernel, len(pieces)), out_shape=j...  15 us
    pallas_call x2, Pallas kernels, attend(): pl.pallas_call(functools.partial(attend_kernel, members, tokens, tok_rows...  9.8 us
    ppermute x20, starting transfers between devices, send_req(): return lax.ppermute(value, 'req', pairs)  9.49 us
    pallas_call x3, Pallas kernels, join(): pl.pallas_call(join_kernel, out_shape=jax.ShapeDtypeStruct((len(parts) *...  6.77 us
  transfers between devices with their start and end apart: 53, of which 27 were waited for; matrix products, arithmetic and copies ran while one was open for 9% of the time, Pallas kernels for 27%

profile of v13, /device:TPU:0, one launch (start us, length us, event | category | flops | bytes accessed | tf_op | source)
XLA Modules:
  0.0 259.5 jit_solution(1909773033536507514)
XLA Ops:
  0.0 4.1 %collective-permute-start.3 = (bf16[64,2048]{1,0:T(8,128)(2,1)}, bf16[64,2048]{1,0:T(8,128)(2,1)S(1)}, u32[]{:S(2)}, u32[]{:S(2)}) collective-permute-start(bf16[64,2048]{1,0:T(8,128)(2,1)} %refs_2_.1), channel_id=1, source_target_pairs={{0,4},{1,5},{2,6},{3,7},{4,0},{5,1},{6,2},{7,3},{8,12},{9,13},{10,... | collective-permute-start | bytes 786440 | tf_op jit(solution)/shard_map/ppermute | solution.py:450
  6.1 4.1 %shard_map.181 = (bf16[592,512]{1,0:T(8,128)(2,1)}, bf16[592,512]{1,0:T(8,128)(2,1)}, bf16[592,512]{1,0:T(8,128)(2,1)}, bf16[592,512]{1,0:T(8,128)(2,1)}) custom-call(s32[8]{0:T(128)} %stack.175.order, bf16[256,2048]{1,0:T(8,128)(2,1)} %bitcast.111, bf16[256,2048]{1,0:T(8,128)(2,1)} %bitcast.112, bf16[64,2048]{1,0:T(8,128)(2,1)} %refs_2_.1, f32[4,512]{1,0:T(4,128)} %pad.4.refs_3_), custom_call_target="tpu_custom_call" | custom-call | bytes 4849664 | tf_op jit(solution)/shard_map/pallas_call | solution.py:58
  10.1 2.6 collective-permute-start.2
  26.2 2.3 shard_map.182
  31.8 10.5 %collective-permute-done.4.refs_5_ = bf16[64,512]{1,0:T(8,128)(2,1)S(1)} collective-permute-done((bf16[64,512]{1,0:T(8,128)(2,1)}, bf16[64,512]{1,0:T(8,128)(2,1)S(1)}, u32[]{:S(2)}, u32[]{:S(2)}) %collective-permute-start.4) | collective-permute-done | bytes 65568 | tf_op jit(solution)/shard_map/ppermute | solution.py:450
  44.5 3.2 %collective-permute-done.6.refs_7_ = bf16[64,512]{1,0:T(8,128)(2,1)S(1)} collective-permute-done((bf16[64,512]{1,0:T(8,128)(2,1)}, bf16[64,512]{1,0:T(8,128)(2,1)S(1)}, u32[]{:S(2)}, u32[]{:S(2)}) %collective-permute-start.6) | collective-permute-done | bytes 65568 | tf_op jit(solution)/shard_map/ppermute | solution.py:450
  49.6 5.2 %shard_map.183 = (bf16[512,256]{1,0:T(8,128)(2,1)}, f32[4,1,256]{2,1,0:T(1,128)S(1)}) custom-call(s32[8]{0:T(128)S(1)} %get-tuple-element.208.page_req, s32[8]{0:T(128)S(1)} %get-tuple-element.207.page_slot, bf16[592,512]{1,0:T(8,128)(2,1)S(1)} %copy-done.1, bf16[592,512]{1,0:T(8,128)(2,1)S(1)} %collective-permute-done.refs_1_, ...), custom_call_target="tpu_custom_call" | custom-call | flops 536870912 | bytes 2686976 | tf_op jit(solution)/shard_map/pallas_call | solution.py:116
  54.8 4.6 %shard_map.184 = (bf16[512,256]{1,0:T(8,128)(2,1)S(1)}, f32[4,1,256]{2,1,0:T(1,128)S(1)}) custom-call(s32[8]{0:T(128)S(1)} %get-tuple-element.208.page_req, s32[8]{0:T(128)S(1)} %get-tuple-element.207.page_slot, bf16[592,512]{1,0:T(8,128)(2,1)S(1)} %copy-done.1, bf16[592,512]{1,0:T(8,128)(2,1)S(1)} %collective-permute-done.refs_1_, ...), custom_call_target="tpu_custom_call" | custom-call | flops 536870912 | bytes 2686976 | tf_op jit(solution)/shard_map/pallas_call | solution.py:116
  62.3 3.6 %collective-permute-done.11.refs_1_ = bf16[64,2048]{1,0:T(8,128)(2,1)S(1)} collective-permute-done((bf16[64,2048]{1,0:T(8,128)(2,1)S(1)}, bf16[64,2048]{1,0:T(8,128)(2,1)S(1)}, u32[]{:S(2)}, u32[]{:S(2)}) %collective-permute-start.11) | collective-permute-done | bytes 262176 | tf_op jit(solution)/shard_map/ppermute | solution.py:464
  65.9 2.7 %collective-permute-start.10 = (f32[2,2,4,64]{3,2,1,0:T(4,128)S(1)}, f32[2,2,4,64]{3,2,1,0:T(4,128)S(1)}, u32[]{:S(2)}, u32[]{:S(2)}) collective-permute-start(f32[2,2,4,64]{3,2,1,0:T(4,128)S(1)} %bitcast.119), channel_id=1, source_target_pairs={{0,4},{1,5},{2,6},{3,7},{4,0},{5,1},{6,2},{7,3},{8,12},{9,13},{10,... | collective-permute-start | bytes 12296 | tf_op jit(solution)/shard_map/ppermute | solution.py:450
  68.9 5.5 %collective-permute-done.10 = f32[2,2,4,64]{3,2,1,0:T(4,128)S(1)} collective-permute-done((f32[2,2,4,64]{3,2,1,0:T(4,128)S(1)}, f32[2,2,4,64]{3,2,1,0:T(4,128)S(1)}, u32[]{:S(2)}, u32[]{:S(2)}) %collective-permute-start.10) | collective-permute-done | bytes 4128 | tf_op jit(solution)/shard_map/ppermute | solution.py:450
  79.0 6.0 %collective-permute-done.15 = bf16[64,2048]{1,0:T(8,128)(2,1)S(1)} collective-permute-done((bf16[64,2048]{1,0:T(8,128)(2,1)S(1)}, bf16[64,2048]{1,0:T(8,128)(2,1)S(1)}, u32[]{:S(2)}, u32[]{:S(2)}) %collective-permute-start.15) | collective-permute-done | bytes 262176 | tf_op jit(solution)/shard_map/ppermute | solution.py:450
  92.6 2.4 collective-permute-start.21
  96.7 8.4 %collective-permute-done.21.refs_1_ = bf16[64,2048]{1,0:T(8,128)(2,1)} collective-permute-done((bf16[64,2048]{1,0:T(8,128)(2,1)}, bf16[64,2048]{1,0:T(8,128)(2,1)}, u32[]{:S(2)}, u32[]{:S(2)}) %collective-permute-start.21) | collective-permute-done | bytes 262176 | tf_op jit(solution)/shard_map/ppermute | solution.py:450
  109.9 2.6 %collective-permute-done.23.refs_0_ = bf16[64,2048]{1,0:T(8,128)(2,1)} collective-permute-done((bf16[64,2048]{1,0:T(8,128)(2,1)}, bf16[64,2048]{1,0:T(8,128)(2,1)}, u32[]{:S(2)}, u32[]{:S(2)}) %collective-permute-start.23) | collective-permute-done | bytes 262176 | tf_op jit(solution)/shard_map/ppermute | solution.py:450
  116.4 7.5 %shard_map.188 = bf16[256,2048]{1,0:T(8,128)(2,1)} custom-call(bf16[64,2048]{1,0:T(8,128)(2,1)} %collective-permute-done.23.refs_0_, bf16[64,2048]{1,0:T(8,128)(2,1)} %collective-permute-done.21.refs_1_, bf16[64,2048]{1,0:T(8,128)(2,1)} %collective-permute-done.19.refs_2_, bf16[64,2048]{1,0:T(8,128)(2,1)} %multiply_convert_fusion.refs_3_, ...), custom_call_target="tpu_custom_call" | custom-call | flops 2214592512 | bytes 10747904 | tf_op jit(solution)/shard_map/pallas_call | solution.py:263
  123.9 2.9 %collective-permute-done.26.refs_2_ = bf16[64,2048]{1,0:T(8,128)(2,1)S(1)} collective-permute-done((bf16[64,2048]{1,0:T(8,128)(2,1)}, bf16[64,2048]{1,0:T(8,128)(2,1)S(1)}, u32[]{:S(2)}, u32[]{:S(2)}) %collective-permute-start.26) | collective-permute-done | bytes 262176 | tf_op jit(solution)/shard_map/ppermute | solution.py:450
  126.9 5.2 %collective-permute-done.28.refs_0_ = bf16[64,2048]{1,0:T(8,128)(2,1)S(1)} collective-permute-done((bf16[64,2048]{1,0:T(8,128)(2,1)}, bf16[64,2048]{1,0:T(8,128)(2,1)S(1)}, u32[]{:S(2)}, u32[]{:S(2)}) %collective-permute-start.28) | collective-permute-done | bytes 262176 | tf_op jit(solution)/shard_map/ppermute | solution.py:450
  137.6 6.8 %collective-permute-done.18.refs_3_ = bf16[64,2048]{1,0:T(8,128)(2,1)S(1)} collective-permute-done((bf16[64,2048]{1,0:T(8,128)(2,1)}, bf16[64,2048]{1,0:T(8,128)(2,1)S(1)}, u32[]{:S(2)}, u32[]{:S(2)}) %collective-permute-start.18) | collective-permute-done | bytes 262176 | tf_op jit(solution)/shard_map/ppermute | solution.py:460
  145.5 4.5 %collective-permute-done.20.refs_2_ = bf16[64,2048]{1,0:T(8,128)(2,1)S(1)} collective-permute-done((bf16[64,2048]{1,0:T(8,128)(2,1)}, bf16[64,2048]{1,0:T(8,128)(2,1)S(1)}, u32[]{:S(2)}, u32[]{:S(2)}) %collective-permute-start.20) | collective-permute-done | bytes 262176 | tf_op jit(solution)/shard_map/ppermute | solution.py:460
  150.0 5.6 %collective-permute-done.22.refs_1_ = bf16[64,2048]{1,0:T(8,128)(2,1)S(1)} collective-permute-done((bf16[64,2048]{1,0:T(8,128)(2,1)}, bf16[64,2048]{1,0:T(8,128)(2,1)S(1)}, u32[]{:S(2)}, u32[]{:S(2)}) %collective-permute-start.22) | collective-permute-done | bytes 262176 | tf_op jit(solution)/shard_map/ppermute | solution.py:460
  155.6 5.2 %collective-permute-done.24.refs_0_ = bf16[64,2048]{1,0:T(8,128)(2,1)S(1)} collective-permute-done((bf16[64,2048]{1,0:T(8,128)(2,1)}, bf16[64,2048]{1,0:T(8,128)(2,1)S(1)}, u32[]{:S(2)}, u32[]{:S(2)}) %collective-permute-start.24) | collective-permute-done | bytes 262176 | tf_op jit(solution)/shard_map/ppermute | solution.py:460
  165.9 15.1 %shard_map.191 = (bf16[256,2048]{1,0:T(8,128)(2,1)}, bf16[256,2048]{1,0:T(8,128)(2,1)}, bf16[256,2048]{1,0:T(8,128)(2,1)}, bf16[256,2048]{1,0:T(8,128)(2,1)}) custom-call(bf16[256,2048]{1,0:T(8,128)(2,1)} %shard_map.187.refs_0_, bf16[256,2048]{1,0:T(8,128)(2,1)} %shard_map.189.refs_1_, bf16[256,2048]{1,0:T(8,128)(2,1)} %collective-permute-done.31.refs_2_, ...), custom_call_target="tpu_custom_call" | custom-call | flops 8254390272 | bytes 25690112 | tf_op jit(solution)/shard_map/pallas_call | solution.py:368
  181.6 7.6 %shard_map.192 = bf16[256,2048]{1,0:T(8,128)(2,1)} custom-call(bf16[64,2048]{1,0:T(8,128)(2,1)} %copy-done.10, bf16[64,2048]{1,0:T(8,128)(2,1)} %copy-done.8, bf16[64,2048]{1,0:T(8,128)(2,1)} %copy-done.9, bf16[64,2048]{1,0:T(8,128)(2,1)} %copy-done.7, bf16[1,2048]{1,0:T(2,128)(2,1)} %reshape.550.refs_4_, bf16[704,2048]{1,0:T(8,128)(2,1)} %bitcast.107, ...), custom_call_target="tpu_custom_call" | custom-call | flops 2214592512 | bytes 10747904 | tf_op jit(solution)/shard_map/pallas_call | solution.py:263
  194.8 15.0 %shard_map.193 = (bf16[64,2048]{1,0:T(8,128)(2,1)}, bf16[64,2048]{1,0:T(8,128)(2,1)}, bf16[64,2048]{1,0:T(8,128)(2,1)}, bf16[64,2048]{1,0:T(8,128)(2,1)}, bf16[6...) custom-call(bf16[256,2048]{1,0:T(8,128)(2,1)} %shard_map.190.refs_0_, ...), custom_call_target="tpu_custom_call" | custom-call | flops 8254390272 | bytes 25690112 | tf_op jit(solution)/shard_map/pallas_call | solution.py:368
  220.3 2.8 %collective-permute-done.44 = bf16[64,2048]{1,0:T(8,128)(2,1)S(1)} collective-permute-done((bf16[64,2048]{1,0:T(8,128)(2,1)S(1)}, bf16[64,2048]{1,0:T(8,128)(2,1)S(1)}, u32[]{:S(2)}, u32[]{:S(2)}) %collective-permute-start.44) | collective-permute-done | bytes 262176 | tf_op jit(solution)/shard_map/ppermute | solution.py:450
  223.8 4.9 %collective-permute-done.43 = bf16[64,2048]{1,0:T(8,128)(2,1)S(1)} collective-permute-done((bf16[64,2048]{1,0:T(8,128)(2,1)S(1)}, bf16[64,2048]{1,0:T(8,128)(2,1)S(1)}, u32[]{:S(2)}, u32[]{:S(2)}) %collective-permute-start.43) | collective-permute-done | bytes 262176 | tf_op jit(solution)/shard_map/ppermute | solution.py:450
  230.2 4.2 %collective-permute-done.42 = bf16[64,2048]{1,0:T(8,128)(2,1)S(1)} collective-permute-done((bf16[64,2048]{1,0:T(8,128)(2,1)S(1)}, bf16[64,2048]{1,0:T(8,128)(2,1)S(1)}, u32[]{:S(2)}, u32[]{:S(2)}) %collective-permute-start.42) | collective-permute-done | bytes 262176 | tf_op jit(solution)/shard_map/ppermute | solution.py:450
  237.4 2.5 collective-permute-done.49
  242.0 3.7 %collective-permute-done.41 = bf16[64,2048]{1,0:T(8,128)(2,1)S(1)} collective-permute-done((bf16[64,2048]{1,0:T(8,128)(2,1)S(1)}, bf16[64,2048]{1,0:T(8,128)(2,1)S(1)}, u32[]{:S(2)}, u32[]{:S(2)}) %collective-permute-start.41) | collective-permute-done | bytes 262176 | tf_op jit(solution)/shard_map/ppermute | solution.py:450
  248.0 3.4 %collective-permute-start.52 = (bf16[64,2048]{1,0:T(8,128)(2,1)S(1)}, bf16[64,2048]{1,0:T(8,128)(2,1)S(1)}, u32[]{:S(2)}, u32[]{:S(2)}) collective-permute-start(bf16[64,2048]{1,0:T(8,128)(2,1)S(1)} %get-tuple-element.212), channel_id=1, source_target_pairs={{0,4},{1,5},{2,6},{3,7},{4,0},{5,1},{6,2},{7,3},{8,12},{9,13},{10,... | collective-permute-start | bytes 786440 | tf_op jit(solution)/shard_map/ppermute | solution.py:450
  252.3 5.2 %collective-permute-done.51 = bf16[64,2048]{1,0:T(8,128)(2,1)S(1)} collective-permute-done((bf16[64,2048]{1,0:T(8,128)(2,1)S(1)}, bf16[64,2048]{1,0:T(8,128)(2,1)S(1)}, u32[]{:S(2)}, u32[]{:S(2)}) %collective-permute-start.51) | collective-permute-done | bytes 262176 | tf_op jit(solution)/shard_map/ppermute | solution.py:450
  (246 shorter events, 87.9 us)
Async XLA Ops:
  0.0 25.5 %collective-permute-start.3 = (bf16[64,2048]{1,0:T(8,128)(2,1)}, bf16[64,2048]{1,0:T(8,128)(2,1)S(1)}, u32[]{:S(2)}, u32[]{:S(2)}) collective-permute-start(bf16[64,2048]{1,0:T(8,128)(2,1)} %refs_2_.1), channel_id=1, source_target_pairs={{0,4},{1,5},{2,6},{3,7},{4,0},{5,1},{6,2},{7,3},{8,12},{9,13},{10,... | collective-permute-start | bytes 786440 | tf_op jit(solution)/shard_map/ppermute | solution.py:450
  10.1 33.2 %collective-permute-start.2 = (bf16[592,512]{1,0:T(8,128)(2,1)}, bf16[592,512]{1,0:T(8,128)(2,1)S(1)}, u32[]{:S(2)}, u32[]{:S(2)}) collective-permute-start(bf16[592,512]{1,0:T(8,128)(2,1)} %get-tuple-element.109), channel_id=1, source_target_pairs={{0,3},{1,2},{2,1},{3,0},{4,7},{5,6},{6,5},{7,4},{8,11},{9,10},{10,... | collective-permute-start | bytes 1818632 | tf_op jit(solution)/shard_map/ppermute | solution.py:450
  12.7 31.7 %collective-permute-start.1 = (bf16[592,512]{1,0:T(8,128)(2,1)}, bf16[592,512]{1,0:T(8,128)(2,1)S(1)}, u32[]{:S(2)}, u32[]{:S(2)}) collective-permute-start(bf16[592,512]{1,0:T(8,128)(2,1)} %get-tuple-element.108), channel_id=1, source_target_pairs={{0,2},{1,3},{2,0},{3,1},{4,6},{5,7},{6,4},{7,5},{8,10},{9,11},{10,... | collective-permute-start | bytes 1818632 | tf_op jit(solution)/shard_map/ppermute | solution.py:450
  13.2 31.3 %collective-permute-start = (bf16[592,512]{1,0:T(8,128)(2,1)}, bf16[592,512]{1,0:T(8,128)(2,1)S(1)}, u32[]{:S(2)}, u32[]{:S(2)}) collective-permute-start(bf16[592,512]{1,0:T(8,128)(2,1)} %get-tuple-element.107), channel_id=1, source_target_pairs={{0,1},{1,0},{2,3},{3,2},{4,5},{5,4},{6,7},{7,6},{8,9},{9,8},{10,11... | collective-permute-start | bytes 1818632 | tf_op jit(solution)/shard_map/ppermute | solution.py:450
  28.5 13.7 %collective-permute-start.4 = (bf16[64,512]{1,0:T(8,128)(2,1)}, bf16[64,512]{1,0:T(8,128)(2,1)S(1)}, u32[]{:S(2)}, u32[]{:S(2)}) collective-permute-start(bf16[64,512]{1,0:T(8,128)(2,1)} %get-tuple-element.116), channel_id=1, source_target_pairs={{0,1},{1,0},{2,3},{3,2},{4,5},{5,4},{6,7},{7,6},{8,9},{9,8},{10,11... | collective-permute-start | bytes 196616 | tf_op jit(solution)/shard_map/ppermute | solution.py:450
  30.2 14.3 %collective-permute-start.5 = (bf16[64,512]{1,0:T(8,128)(2,1)}, bf16[64,512]{1,0:T(8,128)(2,1)S(1)}, u32[]{:S(2)}, u32[]{:S(2)}) collective-permute-start(bf16[64,512]{1,0:T(8,128)(2,1)} %get-tuple-element.119), channel_id=1, source_target_pairs={{0,2},{1,3},{2,0},{3,1},{4,6},{5,7},{6,4},{7,5},{8,10},{9,11},{10,... | collective-permute-start | bytes 196616 | tf_op jit(solution)/shard_map/ppermute | solution.py:450
  43.4 16.1 %collective-permute-start.7 = (bf16[64,2048]{1,0:T(8,128)(2,1)}, bf16[64,2048]{1,0:T(8,128)(2,1)S(1)}, u32[]{:S(2)}, u32[]{:S(2)}) collective-permute-start(bf16[64,2048]{1,0:T(8,128)(2,1)} %constant_dynamic-slice_fusion), channel_id=1, source_target_pairs={{0,4},{1,5},{2,6},{3,7},{4,0},{5,1},{6,2},{7,3},{8,12},{9,13},{10,... | collective-permute-start | bytes 786440 | tf_op jit(solution)/shard_map/ppermute | solution.py:450
  61.0 13.4 %collective-permute-start.8 = (bf16[512,256]{1,0:T(8,128)(2,1)}, bf16[512,256]{1,0:T(8,128)(2,1)S(1)}, u32[]{:S(2)}, u32[]{:S(2)}) collective-permute-start(bf16[512,256]{1,0:T(8,128)(2,1)} %get-tuple-element.121), channel_id=1, source_target_pairs={{0,4},{1,5},{2,6},{3,7},{4,0},{5,1},{6,2},{7,3},{8,12},{9,13},{10,... | collective-permute-start | bytes 786440 | tf_op jit(solution)/shard_map/ppermute | solution.py:450
  62.3 12.1 %collective-permute-start.12 = (bf16[64,2048]{1,0:T(8,128)(2,1)S(1)}, bf16[64,2048]{1,0:T(8,128)(2,1)S(1)}, u32[]{:S(2)}, u32[]{:S(2)}) collective-permute-start(bf16[64,2048]{1,0:T(8,128)(2,1)S(1)} %collective-permute-done.7.refs_0_), channel_id=1, source_target_pairs={{0,8},{8,0},{16,24},{24,16},{1,9},{9,1},{17,25},{25,17},{2,10},{10... | collective-permute-start | bytes 786440 | tf_op jit(solution)/shard_map/ppermute | solution.py:460
  78.3 12.6 %collective-permute-start.14 = (bf16[64,2048]{1,0:T(8,128)(2,1)S(1)}, bf16[64,2048]{1,0:T(8,128)(2,1)S(1)}, u32[]{:S(2)}, u32[]{:S(2)}) collective-permute-start(bf16[64,2048]{1,0:T(8,128)(2,1)S(1)} %get-tuple-element.139), channel_id=1, source_target_pairs={{0,1},{1,0},{2,3},{3,2},{4,5},{5,4},{6,7},{7,6},{8,9},{9,8},{10,11... | collective-permute-start | bytes 786440 | tf_op jit(solution)/shard_map/ppermute | solution.py:450
  92.6 12.5 %collective-permute-start.21 = (bf16[64,2048]{1,0:T(8,128)(2,1)}, bf16[64,2048]{1,0:T(8,128)(2,1)}, u32[]{:S(2)}, u32[]{:S(2)}) collective-permute-start(bf16[64,2048]{1,0:T(8,128)(2,1)} %multiply_convert_fusion.refs_3_), channel_id=1, source_target_pairs={{0,4},{1,5},{2,6},{3,7},{4,0},{5,1},{6,2},{7,3},{8,12},{9,13},{10,... | collective-permute-start | bytes 786440 | tf_op jit(solution)/shard_map/ppermute | solution.py:450
  95.0 13.5 %collective-permute-start.19 = (bf16[64,2048]{1,0:T(8,128)(2,1)}, bf16[64,2048]{1,0:T(8,128)(2,1)}, u32[]{:S(2)}, u32[]{:S(2)}) collective-permute-start(bf16[64,2048]{1,0:T(8,128)(2,1)} %multiply_convert_fusion.refs_3_), channel_id=1, source_target_pairs={{0,2},{1,3},{2,0},{3,1},{4,6},{5,7},{6,4},{7,5},{8,10},{9,11},{10,... | collective-permute-start | bytes 786440 | tf_op jit(solution)/shard_map/ppermute | solution.py:450
  106.3 17.6 %collective-permute-start.25 = (bf16[64,2048]{1,0:T(8,128)(2,1)}, bf16[64,2048]{1,0:T(8,128)(2,1)S(1)}, u32[]{:S(2)}, u32[]{:S(2)}) collective-permute-start(bf16[64,2048]{1,0:T(8,128)(2,1)} %multiply_convert_fusion.refs_3_), channel_id=1, source_target_pairs={{0,1},{1,0},{2,3},{3,2},{4,5},{5,4},{6,7},{7,6},{8,9},{9,8},{10,11... | collective-permute-start | bytes 786440 | tf_op jit(solution)/shard_map/ppermute | solution.py:450
  107.8 19.0 %collective-permute-start.27 = (bf16[64,2048]{1,0:T(8,128)(2,1)}, bf16[64,2048]{1,0:T(8,128)(2,1)S(1)}, u32[]{:S(2)}, u32[]{:S(2)}) collective-permute-start(bf16[64,2048]{1,0:T(8,128)(2,1)} %collective-permute-done.21.refs_1_), channel_id=1, source_target_pairs={{0,1},{1,0},{2,3},{3,2},{4,5},{5,4},{6,7},{7,6},{8,9},{9,8},{10,11... | collective-permute-start | bytes 786440 | tf_op jit(solution)/shard_map/ppermute | solution.py:450
  108.5 18.3 %collective-permute-start.26 = (bf16[64,2048]{1,0:T(8,128)(2,1)}, bf16[64,2048]{1,0:T(8,128)(2,1)S(1)}, u32[]{:S(2)}, u32[]{:S(2)}) collective-permute-start(bf16[64,2048]{1,0:T(8,128)(2,1)} %collective-permute-done.19.refs_2_), channel_id=1, source_target_pairs={{0,1},{1,0},{2,3},{3,2},{4,5},{5,4},{6,7},{7,6},{8,9},{9,8},{10,11... | collective-permute-start | bytes 786440 | tf_op jit(solution)/shard_map/ppermute | solution.py:450
  112.6 19.5 %collective-permute-start.28 = (bf16[64,2048]{1,0:T(8,128)(2,1)}, bf16[64,2048]{1,0:T(8,128)(2,1)S(1)}, u32[]{:S(2)}, u32[]{:S(2)}) collective-permute-start(bf16[64,2048]{1,0:T(8,128)(2,1)} %collective-permute-done.23.refs_0_), channel_id=1, source_target_pairs={{0,1},{1,0},{2,3},{3,2},{4,5},{5,4},{6,7},{7,6},{8,9},{9,8},{10,11... | collective-permute-start | bytes 786440 | tf_op jit(solution)/shard_map/ppermute | solution.py:450
  116.4 49.5 %collective-permute-start.31 = (bf16[256,2048]{1,0:T(8,128)(2,1)}, bf16[256,2048]{1,0:T(8,128)(2,1)}, u32[]{:S(2)}, u32[]{:S(2)}) collective-permute-start(bf16[256,2048]{1,0:T(8,128)(2,1)} %shard_map.187.refs_0_), channel_id=1, source_target_pairs={{0,8},{8,0},{16,24},{24,16},{1,9},{9,1},{17,25},{25,17},{2,10},{10... | collective-permute-start | bytes 3145736 | tf_op jit(solution)/shard_map/ppermute | solution.py:460
  135.1 30.8 %collective-permute-start.32 = (bf16[256,2048]{1,0:T(8,128)(2,1)}, bf16[256,2048]{1,0:T(8,128)(2,1)}, u32[]{:S(2)}, u32[]{:S(2)}) collective-permute-start(bf16[256,2048]{1,0:T(8,128)(2,1)} %shard_map.189.refs_1_), channel_id=1, source_target_pairs={{0,8},{8,0},{16,24},{24,16},{1,9},{9,1},{17,25},{25,17},{2,10},{10... | collective-permute-start | bytes 3145736 | tf_op jit(solution)/shard_map/ppermute | solution.py:460
  135.6 14.4 %collective-permute-start.20 = (bf16[64,2048]{1,0:T(8,128)(2,1)}, bf16[64,2048]{1,0:T(8,128)(2,1)S(1)}, u32[]{:S(2)}, u32[]{:S(2)}) collective-permute-start(bf16[64,2048]{1,0:T(8,128)(2,1)} %collective-permute-done.19.refs_2_), channel_id=1, source_target_pairs={{0,16},{8,24},{16,0},{24,8},{1,17},{9,25},{17,1},{25,9},{2,18},{10... | collective-permute-start | bytes 786440 | tf_op jit(solution)/shard_map/ppermute | solution.py:460
  137.1 18.5 %collective-permute-start.22 = (bf16[64,2048]{1,0:T(8,128)(2,1)}, bf16[64,2048]{1,0:T(8,128)(2,1)S(1)}, u32[]{:S(2)}, u32[]{:S(2)}) collective-permute-start(bf16[64,2048]{1,0:T(8,128)(2,1)} %collective-permute-done.21.refs_1_), channel_id=1, source_target_pairs={{0,16},{8,24},{16,0},{24,8},{1,17},{9,25},{17,1},{25,9},{2,18},{10... | collective-permute-start | bytes 786440 | tf_op jit(solution)/shard_map/ppermute | solution.py:460
  144.4 16.5 %collective-permute-start.24 = (bf16[64,2048]{1,0:T(8,128)(2,1)}, bf16[64,2048]{1,0:T(8,128)(2,1)S(1)}, u32[]{:S(2)}, u32[]{:S(2)}) collective-permute-start(bf16[64,2048]{1,0:T(8,128)(2,1)} %collective-permute-done.23.refs_0_), channel_id=1, source_target_pairs={{0,16},{8,24},{16,0},{24,8},{1,17},{9,25},{17,1},{25,9},{2,18},{10... | collective-permute-start | bytes 786440 | tf_op jit(solution)/shard_map/ppermute | solution.py:460
  163.8 25.3 %collective-permute-start.30 = (bf16[256,2048]{1,0:T(8,128)(2,1)}, bf16[256,2048]{1,0:T(8,128)(2,1)S(1)}, u32[]{:S(2)}, u32[]{:S(2)}) collective-permute-start(bf16[256,2048]{1,0:T(8,128)(2,1)} %shard_map.190.refs_0_), channel_id=1, source_target_pairs={{0,1},{1,0},{2,3},{3,2},{4,5},{5,4},{6,7},{7,6},{8,9},{9,8},{10,11... | collective-permute-start | bytes 3145736 | tf_op jit(solution)/shard_map/ppermute | solution.py:450
  181.1 11.7 %collective-permute-start.33 = (bf16[256,2048]{1,0:T(8,128)(2,1)S(1)}, bf16[256,2048]{1,0:T(8,128)(2,1)}, u32[]{:S(2)}, u32[]{:S(2)}) collective-permute-start(bf16[256,2048]{1,0:T(8,128)(2,1)S(1)} %copy-done.4), channel_id=1, source_target_pairs={{0,8},{8,0},{16,24},{24,16},{1,9},{9,1},{17,25},{25,17},{2,10},{10... | collective-permute-start | bytes 3145736 | tf_op jit(solution)/shard_map/ppermute | solution.py:460
  190.7 19.2 %collective-permute-start.37 = (bf16[256,2048]{1,0:T(8,128)(2,1)}, bf16[256,2048]{1,0:T(8,128)(2,1)S(1)}, u32[]{:S(2)}, u32[]{:S(2)}) collective-permute-start(bf16[256,2048]{1,0:T(8,128)(2,1)} %get-tuple-element.179), channel_id=1, source_target_pairs={{0,8},{8,0},{16,24},{24,16},{1,9},{9,1},{17,25},{25,17},{2,10},{10... | collective-permute-start | bytes 3145736 | tf_op jit(solution)/shard_map/ppermute | solution.py:460
  193.8 16.1 %collective-permute-start.36 = (bf16[128,2048]{1,0:T(8,128)(2,1)S(1)}, bf16[128,2048]{1,0:T(8,128)(2,1)S(1)}, u32[]{:S(2)}, u32[]{:S(2)}) collective-permute-start(bf16[128,2048]{1,0:T(8,128)(2,1)S(1)} %slice.283), channel_id=1, source_target_pairs={{0,1},{1,0},{2,3},{3,2},{4,5},{5,4},{6,7},{7,6},{8,9},{9,8},{10,11... | collective-permute-start | bytes 1572872 | tf_op jit(solution)/shard_map/ppermute | solution.py:450
  215.9 12.8 %collective-permute-start.43 = (bf16[64,2048]{1,0:T(8,128)(2,1)S(1)}, bf16[64,2048]{1,0:T(8,128)(2,1)S(1)}, u32[]{:S(2)}, u32[]{:S(2)}) collective-permute-start(bf16[64,2048]{1,0:T(8,128)(2,1)S(1)} %add_convert_fusion.11), channel_id=1, source_target_pairs={{0,1},{1,0},{2,3},{3,2},{4,5},{5,4},{6,7},{7,6},{8,9},{9,8},{10,11... | collective-permute-start | bytes 786440 | tf_op jit(solution)/shard_map/ppermute | solution.py:450
  218.1 16.3 %collective-permute-start.42 = (bf16[64,2048]{1,0:T(8,128)(2,1)S(1)}, bf16[64,2048]{1,0:T(8,128)(2,1)S(1)}, u32[]{:S(2)}, u32[]{:S(2)}) collective-permute-start(bf16[64,2048]{1,0:T(8,128)(2,1)S(1)} %add_convert_fusion.10), channel_id=1, source_target_pairs={{0,1},{1,0},{2,3},{3,2},{4,5},{5,4},{6,7},{7,6},{8,9},{9,8},{10,11... | collective-permute-start | bytes 786440 | tf_op jit(solution)/shard_map/ppermute | solution.py:450
  219.2 20.8 %collective-permute-start.49 = (bf16[64,2048]{1,0:T(8,128)(2,1)S(1)}, bf16[64,2048]{1,0:T(8,128)(2,1)S(1)}, u32[]{:S(2)}, u32[]{:S(2)}) collective-permute-start(bf16[64,2048]{1,0:T(8,128)(2,1)S(1)} %get-tuple-element.206), channel_id=1, source_target_pairs={{0,1},{1,0},{2,3},{3,2},{4,5},{5,4},{6,7},{7,6},{8,9},{9,8},{10,11... | collective-permute-start | bytes 786440 | tf_op jit(solution)/shard_map/ppermute | solution.py:450
  228.8 12.1 %collective-permute-start.46 = (bf16[64,2048]{1,0:T(8,128)(2,1)S(1)}, bf16[64,2048]{1,0:T(8,128)(2,1)S(1)}, u32[]{:S(2)}, u32[]{:S(2)}) collective-permute-start(bf16[64,2048]{1,0:T(8,128)(2,1)S(1)} %add_convert_fusion.7), channel_id=1, source_target_pairs={{0,16},{8,24},{16,0},{24,8},{1,17},{9,25},{17,1},{25,9},{2,18},{10... | collective-permute-start | bytes 786440 | tf_op jit(solution)/shard_map/ppermute | solution.py:460
  239.9 11.4 %collective-permute-start.40 = (bf16[64,2048]{1,0:T(8,128)(2,1)S(1)}, bf16[64,2048]{1,0:T(8,128)(2,1)S(1)}, u32[]{:S(2)}, u32[]{:S(2)}) collective-permute-start(bf16[64,2048]{1,0:T(8,128)(2,1)S(1)} %get-tuple-element.195), channel_id=1, source_target_pairs={{0,1},{1,0},{2,3},{3,2},{4,5},{5,4},{6,7},{7,6},{8,9},{9,8},{10,11... | collective-permute-start | bytes 786440 | tf_op jit(solution)/shard_map/ppermute | solution.py:450
  247.3 10.2 %collective-permute-start.51 = (bf16[64,2048]{1,0:T(8,128)(2,1)S(1)}, bf16[64,2048]{1,0:T(8,128)(2,1)S(1)}, u32[]{:S(2)}, u32[]{:S(2)}) collective-permute-start(bf16[64,2048]{1,0:T(8,128)(2,1)S(1)} %get-tuple-element.211), channel_id=1, source_target_pairs={{0,2},{1,3},{2,0},{3,1},{4,6},{5,7},{6,4},{7,5},{8,10},{9,11},{10,... | collective-permute-start | bytes 786440 | tf_op jit(solution)/shard_map/ppermute | solution.py:450
  248.0 10.5 %collective-permute-start.52 = (bf16[64,2048]{1,0:T(8,128)(2,1)S(1)}, bf16[64,2048]{1,0:T(8,128)(2,1)S(1)}, u32[]{:S(2)}, u32[]{:S(2)}) collective-permute-start(bf16[64,2048]{1,0:T(8,128)(2,1)S(1)} %get-tuple-element.212), channel_id=1, source_target_pairs={{0,4},{1,5},{2,6},{3,7},{4,0},{5,1},{6,2},{7,3},{8,12},{9,13},{10,... | collective-permute-start | bytes 786440 | tf_op jit(solution)/shard_map/ppermute | solution.py:450
  (52 other events, 539.9 us)

commit v14 on v12

--- a/solution.py
+++ b/solution.py
@@ -40,7 +40,7 @@
         low = weights - high - middle
         weights = jnp.concatenate([high, middle, low, jnp.zeros_like(low)], axis=0)
         for m in range(members):
-            blocks[m][at:, :] = weights.astype(jnp.bfloat16)
+            blocks[m][at:, : weights.shape[1]] = weights.astype(jnp.bfloat16)
     for copy in copies:
         copy.wait()
 
@@ -199,25 +199,27 @@
     )(order, mine, mine_level, theirs, their_level, own, *quarters)
 
 
-def join_kernel(*refs):
-    parts, out = refs[:-1], refs[-1]
-    rows = parts[0].shape[0]
-    for i, part in enumerate(parts):
-        out[i * rows : (i + 1) * rows, :] = part[...]
-
-
-def join(parts):
-    rows, width = parts[0].shape
+def join_kernel(sizes, *refs):
+    parts, outs = refs[: sum(sizes)], refs[sum(sizes) :]
+    for n, out in enumerate(outs):
+        rows = out.shape[0] // sizes[n]
+        for i in range(sizes[n]):
+            out[i * rows : (i + 1) * rows, :] = parts[sum(sizes[:n]) + i][...]
+
+
+def join(*groups):
+    rows, width = groups[0][0].shape
+    sizes = [len(group) for group in groups]
     vmem = pl.BlockSpec(memory_space=pltpu.VMEM)
     return pl.pallas_call(
-        join_kernel,
-        out_shape=jax.ShapeDtypeStruct((len(parts) * rows, width), parts[0].dtype),
-        in_specs=[vmem] * len(parts),
-        out_specs=vmem,
+        functools.partial(join_kernel, sizes),
+        out_shape=[jax.ShapeDtypeStruct((n * rows, width), groups[0][0].dtype) for n in sizes],
+        in_specs=[vmem] * sum(sizes),
+        out_specs=[vmem] * len(sizes),
         cost_estimate=pl.CostEstimate(
-            flops=0, bytes_accessed=4 * len(parts) * rows * width, transcendentals=0
-        ),
-    )(*parts)
+            flops=0, bytes_accessed=4 * sum(sizes) * rows * width, transcendentals=0
+        ),
+    )(*[part for group in groups for part in group])
 
 
 def silu(value):
@@ -487,7 +489,7 @@
             for j in range(2)
         ]
     ).astype(i32)
-    gates = jnp.pad(jnp.transpose(route_gate), ((0, 0), (0, 2 * columns - tok_rows)))
+    gates = jnp.transpose(route_gate)
     blocks = pack([keys, values, queries], gates, member_columns, columns)
     blocks = [send(blocks[m], 0, *members[m]) for m in range(len(members))]
     far = list(pack([far_queries], None, member_columns, columns))
@@ -583,22 +585,19 @@
     halves = [[line[i] for i in order]]
     shared_weights = (shared_scalar, shared_gate.T, shared_up.T, shared_down)
     shared = [shared_expert(halves[0], *shared_weights)]
-    chunks = {(0, 0): [join(halves[0])]}
+    chunks = {(0, 0): join(halves[0])}
     for dc in range(1, nc):
         chunks[0, dc] = [send_req(chunks[0, 0][0], 0, dc)]
     over_x, over_y, shared, row_gate = tie((over_x, over_y, shared, row_gate))
-    for dy in range(1, ny):
-        half = join([over_y[i, dy] for i in order])
+    halves += [[over_x[i, dx] for i in order] for dx in range(1, nx)]
+    joined = join(*halves[1:], *[[over_y[i, dy] for i in order] for dy in range(1, ny)])
+    chunks[0, 0] += joined[: nx - 1]
+    for dc in range(1, nc):
+        chunks[0, dc] += [send_req(half, 0, dc) for half in joined[: nx - 1]]
+    for dy, half in enumerate(joined[nx - 1 :], 1):
         chunks[dy, 0] = [half] + [send(half, 0, 0, dx) for dx in range(1, nx)]
         for dc in range(1, nc):
             chunks[dy, dc] = [send_req(half, 0, dc)]
-        over_x, _ = tie((over_x, half))
-    for dx in range(1, nx):
-        half = [over_x[i, dx] for i in order]
-        chunks[0, 0].append(join(half))
-        for dc in range(1, nc):
-            chunks[0, dc].append(send_req(chunks[0, 0][dx], 0, dc))
-        halves.append(half)
 
     def answers_of(dy, dcs, more, cuts):
         return routed_expert(
@@ -681,12 +680,13 @@
             go = add_up([line_of(0, 1)] + home[1]).astype(bf16)
             near[1] = send(go, 0, 1, 0)
             goes.append(go)
+        if turn == 2:
+            go = add_up([line_of(0, 2)] + home[2] + [near[1]]).astype(bf16)
+            far = send(go, 1, 0, 0)
+            goes.append(go)
         if turn + 1 < len(turns):
             after = turns[turn + 1]
             last[after], _ = tie((last[after], goes))
-    far = add_up([line_of(0, 2)] + home[2] + [near[1]]).astype(bf16)
-    home[0], _ = tie((home[0], far))
-    far = send(far, 1, 0, 0)
     near[0] = send(add_up([line_of(0, 0)] + home[0]).astype(bf16), 0, 1, 0)
     total = add_up([stream, line_of(0, 3)] + home[3] + [near[0], far])
     return total.astype(bf16)

time: 228 us -> 230 us (level)
  waiting for transfers between devices: 81.8 us -> 85 us
  local copies, waits for them, and re-layouts: 10.6 us -> 8.01 us
    pallas_call x3 -> x2, Pallas kernels: 6.74 us -> 5.14 us  [join(): pl.pallas_call(functools.partial(join_kernel, sizes), out_shape=[jax.Shap...]
  transfers between devices with their start and end apart: 52 -> 52, of which waited for: 24 -> 26; matrix products, arithmetic and copies ran while one was open for 10% -> 9% of each run, Pallas kernels for 30% -> 29%
where the time goes in v14:
time: 230 us; the launch traced here: 229 us
  waiting for transfers between devices  85 us (37%)
  Pallas kernels  68.5 us (30%)
  starting transfers between devices  48.6 us (21%)
  other arithmetic  17.3 us (8%)
  local copies, waits for them, and re-layouts  8.01 us (3%)
    ppermute x31, waiting for transfers between devices, send(): return lax.ppermute(value, 'exp', pairs)  69.9 us
    ppermute x31, starting transfers between devices, send(): return lax.ppermute(value, 'exp', pairs)  37.4 us
    pallas_call x2, Pallas kernels, routed_expert(): pl.pallas_call(functools.partial(routed_kernel, parts, len(more), entries...  30.5 us
    ppermute x20, waiting for transfers between devices, send_req(): return lax.ppermute(value, 'req', pairs)  15.1 us
    pallas_call x2, Pallas kernels, shared_expert(): pl.pallas_call(functools.partial(shared_kernel, len(pieces)), out_shape=j...  15.1 us
    ppermute x20, starting transfers between devices, send_req(): return lax.ppermute(value, 'req', pairs)  9.61 us
    pallas_call x2, Pallas kernels, attend(): pl.pallas_call(functools.partial(attend_kernel, members, tokens, tok_rows...  9.12 us
    pallas_call x2, Pallas kernels, pack(): pl.pallas_call(functools.partial(pack_kernel, members, len(parts), column...  6.34 us
  transfers between devices with their start and end apart: 52, of which 26 were waited for; matrix products, arithmetic and copies ran while one was open for 9% of the time, Pallas kernels for 29%

profile of v14, /device:TPU:0, one launch (start us, length us, event | category | flops | bytes accessed | tf_op | source)
XLA Modules:
  0.0 229.3 jit_solution(15978655566449568235)
XLA Ops:
  0.0 4.1 %collective-permute-start.3 = (bf16[64,2048]{1,0:T(8,128)(2,1)}, bf16[64,2048]{1,0:T(8,128)(2,1)}, u32[]{:S(2)}, u32[]{:S(2)}) collective-permute-start(bf16[64,2048]{1,0:T(8,128)(2,1)} %refs_2_.1), channel_id=1, source_target_pairs={{0,4},{1,5},{2,6},{3,7},{4,0},{5,1},{6,2},{7,3},{8,12},{9,13},{10,... | collective-permute-start | bytes 786440 | tf_op jit(solution)/shard_map/ppermute | solution.py:444
  4.8 4.0 %shard_map.181 = (bf16[592,512]{1,0:T(8,128)(2,1)}, bf16[592,512]{1,0:T(8,128)(2,1)}, bf16[592,512]{1,0:T(8,128)(2,1)}, bf16[592,512]{1,0:T(8,128)(2,1)}) custom-call(s32[8]{0:T(128)} %stack.175.order, bf16[256,2048]{1,0:T(8,128)(2,1)} %bitcast.111, bf16[256,2048]{1,0:T(8,128)(2,1)} %bitcast.112, bf16[64,2048]{1,0:T(8,128)(2,1)} %refs_2_.1, f32[4,64]{1,0:T(4,128)} %bitcast.125), custom_call_target="tpu_custom_call" | custom-call | bytes 4849664 | tf_op jit(solution)/shard_map/pallas_call | solution.py:58
  23.4 2.3 %shard_map.183 = (bf16[64,512]{1,0:T(8,128)(2,1)}, bf16[64,512]{1,0:T(8,128)(2,1)}, bf16[64,512]{1,0:T(8,128)(2,1)}, bf16[64,512]{1,0:T(8,128)(2,1)}) custom-call(s32[8]{0:T(128)} %stack.175.order, bf16[64,2048]{1,0:T(8,128)(2,1)} %collective-permute-done.3.refs_0_), custom_call_target="tpu_custom_call" | custom-call | bytes 524288 | tf_op jit(solution)/shard_map/pallas_call | solution.py:58
  27.4 15.8 %collective-permute-done.7.refs_0_ = bf16[64,2048]{1,0:T(8,128)(2,1)S(1)} collective-permute-done((bf16[64,2048]{1,0:T(8,128)(2,1)S(1)}, bf16[64,2048]{1,0:T(8,128)(2,1)S(1)}, u32[]{:S(2)}, u32[]{:S(2)}) %collective-permute-start.7) | collective-permute-done | bytes 262176 | tf_op jit(solution)/shard_map/ppermute | solution.py:444
  53.9 4.5 %shard_map.184 = (bf16[512,256]{1,0:T(8,128)(2,1)S(1)}, f32[4,1,256]{2,1,0:T(1,128)S(1)}) custom-call(s32[8]{0:T(128)S(1)} %get-tuple-element.212.page_req, s32[8]{0:T(128)S(1)} %get-tuple-element.211.page_slot, bf16[592,512]{1,0:T(8,128)(2,1)S(1)} %copy-done.1, bf16[592,512]{1,0:T(8,128)(2,1)S(1)} %collective-permute-done.refs_1_, ...), custom_call_target="tpu_custom_call" | custom-call | flops 536870912 | bytes 2686976 | tf_op jit(solution)/shard_map/pallas_call | solution.py:116
  59.0 2.2 collective-permute-start.11
  61.2 4.6 %shard_map.182 = (bf16[512,256]{1,0:T(8,128)(2,1)S(1)}, f32[4,1,256]{2,1,0:T(1,128)S(1)}) custom-call(s32[8]{0:T(128)S(1)} %get-tuple-element.212.page_req, s32[8]{0:T(128)S(1)} %get-tuple-element.211.page_slot, bf16[592,512]{1,0:T(8,128)(2,1)S(1)} %copy-done.1, bf16[592,512]{1,0:T(8,128)(2,1)S(1)} %collective-permute-done.refs_1_, ...), custom_call_target="tpu_custom_call" | custom-call | flops 536870912 | bytes 2686976 | tf_op jit(solution)/shard_map/pallas_call | solution.py:116
  66.7 2.1 collective-permute-start.12
  68.9 5.5 %collective-permute-done.13 = f32[2,2,4,64]{3,2,1,0:T(4,128)S(1)} collective-permute-done((f32[2,2,4,64]{3,2,1,0:T(4,128)S(1)}, f32[2,2,4,64]{3,2,1,0:T(4,128)S(1)}, u32[]{:S(2)}, u32[]{:S(2)}) %collective-permute-start.13) | collective-permute-done | bytes 4128 | tf_op jit(solution)/shard_map/ppermute | solution.py:444
  79.0 6.0 %collective-permute-done.15 = bf16[64,2048]{1,0:T(8,128)(2,1)S(1)} collective-permute-done((bf16[64,2048]{1,0:T(8,128)(2,1)S(1)}, bf16[64,2048]{1,0:T(8,128)(2,1)S(1)}, u32[]{:S(2)}, u32[]{:S(2)}) %collective-permute-start.15) | collective-permute-done | bytes 262176 | tf_op jit(solution)/shard_map/ppermute | solution.py:444
  86.1 2.9 %collective-permute-done.17 = f32[2,2,2,4,64]{4,3,2,1,0:T(4,128)S(1)} collective-permute-done((f32[2,2,2,4,64]{4,3,2,1,0:T(4,128)S(1)}, f32[2,2,2,4,64]{4,3,2,1,0:T(4,128)S(1)}, u32[]{:S(2)}, u32[]{:S(2)}) %collective-permute-start.17) | collective-permute-done | bytes 8224 | tf_op jit(solution)/shard_map/ppermute | solution.py:454
  89.0 2.5 %collective-permute-done.16 = bf16[64,2048]{1,0:T(8,128)(2,1)S(1)} collective-permute-done((bf16[64,2048]{1,0:T(8,128)(2,1)S(1)}, bf16[64,2048]{1,0:T(8,128)(2,1)S(1)}, u32[]{:S(2)}, u32[]{:S(2)}) %collective-permute-start.16) | collective-permute-done | bytes 262176 | tf_op jit(solution)/shard_map/ppermute | solution.py:444
  97.2 6.4 %collective-permute-done.21.refs_2_ = bf16[64,2048]{1,0:T(8,128)(2,1)S(1)} collective-permute-done((bf16[64,2048]{1,0:T(8,128)(2,1)S(1)}, bf16[64,2048]{1,0:T(8,128)(2,1)S(1)}, u32[]{:S(2)}, u32[]{:S(2)}) %collective-permute-start.21) | collective-permute-done | bytes 262176 | tf_op jit(solution)/shard_map/ppermute | solution.py:444
  105.6 2.0 collective-permute-start.22
  110.4 3.0 %collective-permute-done.20.refs_0_ = bf16[64,2048]{1,0:T(8,128)(2,1)S(1)} collective-permute-done((bf16[64,2048]{1,0:T(8,128)(2,1)S(1)}, bf16[64,2048]{1,0:T(8,128)(2,1)S(1)}, u32[]{:S(2)}, u32[]{:S(2)}) %collective-permute-start.20) | collective-permute-done | bytes 262176 | tf_op jit(solution)/shard_map/ppermute | solution.py:444
  114.0 2.2 shard_map.189.refs_0_
  116.3 7.6 %shard_map.187 = bf16[256,2048]{1,0:T(8,128)(2,1)} custom-call(bf16[64,2048]{1,0:T(8,128)(2,1)} %copy-done.13, bf16[64,2048]{1,0:T(8,128)(2,1)} %copy-done.14, bf16[64,2048]{1,0:T(8,128)(2,1)} %copy-done.11, bf16[64,2048]{1,0:T(8,128)(2,1)} %copy-done.4, bf16[1,2048]{1,0:T(2,128)(2,1)} %reshape.550.refs_4_, bf16[704,2048]{1,0:T(8,128)(2,1)} %bitcast.106, ...), custom_call_target="tpu_custom_call" | custom-call | flops 2214592512 | bytes 10747904 | tf_op jit(solution)/shard_map/pallas_call | solution.py:265
  124.0 3.0 %collective-permute-done.28.refs_5_ = bf16[64,2048]{1,0:T(8,128)(2,1)} collective-permute-done((bf16[64,2048]{1,0:T(8,128)(2,1)S(1)}, bf16[64,2048]{1,0:T(8,128)(2,1)}, u32[]{:S(2)}, u32[]{:S(2)}) %collective-permute-start.28) | collective-permute-done | bytes 262176 | tf_op jit(solution)/shard_map/ppermute | solution.py:454
  127.1 2.9 %shard_map.188 = (bf16[256,2048]{1,0:T(8,128)(2,1)}, bf16[256,2048]{1,0:T(8,128)(2,1)}) custom-call(bf16[64,2048]{1,0:T(8,128)(2,1)} %copy-done.9, bf16[64,2048]{1,0:T(8,128)(2,1)} %copy-done.12, bf16[64,2048]{1,0:T(8,128)(2,1)} %copy-done.10, bf16[64,2048]{1,0:T(8,128)(2,1)} %copy-done.8, bf16[64,2048]{1,0:T(8,128)(2,1)} %collective-permute-done.26.refs_4_, ...), custom_call_target="tpu_custom_call" | custom-call | bytes 4194304 | tf_op jit(solution)/shard_map/pallas_call | solution.py:214
  133.8 15.3 %shard_map.190 = (bf16[256,2048]{1,0:T(8,128)(2,1)}, bf16[256,2048]{1,0:T(8,128)(2,1)}, bf16[256,2048]{1,0:T(8,128)(2,1)}, bf16[256,2048]{1,0:T(8,128)(2,1)}) custom-call(bf16[256,2048]{1,0:T(8,128)(2,1)} %shard_map.189.refs_0_, bf16[256,2048]{1,0:T(8,128)(2,1)} %get-tuple-element.158.refs_1_, bf16[256,2048]{1,0:T(8,128)(2,1)} %collective-permute-done.31.refs_2_, ...), custom_call_target="tpu_custom_call" | custom-call | flops 8254390272 | bytes 25690112 | tf_op jit(solution)/shard_map/pallas_call | solution.py:363
  149.7 7.5 %shard_map.191 = bf16[256,2048]{1,0:T(8,128)(2,1)} custom-call(bf16[64,2048]{1,0:T(8,128)(2,1)} %copy-done.9, bf16[64,2048]{1,0:T(8,128)(2,1)} %copy-done.12, bf16[64,2048]{1,0:T(8,128)(2,1)} %copy-done.10, bf16[64,2048]{1,0:T(8,128)(2,1)} %copy-done.8, bf16[1,2048]{1,0:T(2,128)(2,1)} %reshape.550.refs_4_, bf16[704,2048]{1,0:T(8,128)(2,1)} %bitcast.107, ...), custom_call_target="tpu_custom_call" | custom-call | flops 2214592512 | bytes 10747904 | tf_op jit(solution)/shard_map/pallas_call | solution.py:265
  161.4 15.2 %shard_map.192 = (bf16[64,2048]{1,0:T(8,128)(2,1)}, bf16[64,2048]{1,0:T(8,128)(2,1)}, bf16[64,2048]{1,0:T(8,128)(2,1)}, bf16[64,2048]{1,0:T(8,128)(2,1)}, bf16[6...) custom-call(bf16[256,2048]{1,0:T(8,128)(2,1)} %get-tuple-element.170, ...), custom_call_target="tpu_custom_call" | custom-call | flops 8254390272 | bytes 25690112 | tf_op jit(solution)/shard_map/pallas_call | solution.py:363
  176.6 3.4 %collective-permute-done.36 = bf16[192,2048]{1,0:T(8,128)(2,1)S(1)} collective-permute-done((bf16[192,2048]{1,0:T(8,128)(2,1)S(1)}, bf16[192,2048]{1,0:T(8,128)(2,1)S(1)}, u32[]{:S(2)}, u32[]{:S(2)}) %collective-permute-start.36) | collective-permute-done | bytes 786464 | tf_op jit(solution)/shard_map/ppermute | solution.py:444
  180.5 2.4 %collective-permute-done.39 = bf16[256,2048]{1,0:T(8,128)(2,1)S(1)} collective-permute-done((bf16[256,2048]{1,0:T(8,128)(2,1)}, bf16[256,2048]{1,0:T(8,128)(2,1)S(1)}, u32[]{:S(2)}, u32[]{:S(2)}) %collective-permute-start.39) | collective-permute-done | bytes 1048608 | tf_op jit(solution)/shard_map/ppermute | solution.py:454
  189.6 3.5 %collective-permute-done.44 = bf16[64,2048]{1,0:T(8,128)(2,1)S(1)} collective-permute-done((bf16[64,2048]{1,0:T(8,128)(2,1)S(1)}, bf16[64,2048]{1,0:T(8,128)(2,1)S(1)}, u32[]{:S(2)}, u32[]{:S(2)}) %collective-permute-start.44) | collective-permute-done | bytes 262176 | tf_op jit(solution)/shard_map/ppermute | solution.py:444
  193.7 4.9 %collective-permute-done.43 = bf16[64,2048]{1,0:T(8,128)(2,1)S(1)} collective-permute-done((bf16[64,2048]{1,0:T(8,128)(2,1)S(1)}, bf16[64,2048]{1,0:T(8,128)(2,1)S(1)}, u32[]{:S(2)}, u32[]{:S(2)}) %collective-permute-start.43) | collective-permute-done | bytes 262176 | tf_op jit(solution)/shard_map/ppermute | solution.py:444
  200.2 3.4 %collective-permute-done.42 = bf16[64,2048]{1,0:T(8,128)(2,1)S(1)} collective-permute-done((bf16[64,2048]{1,0:T(8,128)(2,1)S(1)}, bf16[64,2048]{1,0:T(8,128)(2,1)S(1)}, u32[]{:S(2)}, u32[]{:S(2)}) %collective-permute-start.42) | collective-permute-done | bytes 262176 | tf_op jit(solution)/shard_map/ppermute | solution.py:444
  207.7 3.5 %collective-permute-done.49 = bf16[64,2048]{1,0:T(8,128)(2,1)S(1)} collective-permute-done((bf16[64,2048]{1,0:T(8,128)(2,1)S(1)}, bf16[64,2048]{1,0:T(8,128)(2,1)S(1)}, u32[]{:S(2)}, u32[]{:S(2)}) %collective-permute-start.49) | collective-permute-done | bytes 262176 | tf_op jit(solution)/shard_map/ppermute | solution.py:454
  211.9 3.0 %collective-permute-done.41 = bf16[64,2048]{1,0:T(8,128)(2,1)S(1)} collective-permute-done((bf16[64,2048]{1,0:T(8,128)(2,1)S(1)}, bf16[64,2048]{1,0:T(8,128)(2,1)S(1)}, u32[]{:S(2)}, u32[]{:S(2)}) %collective-permute-start.41) | collective-permute-done | bytes 262176 | tf_op jit(solution)/shard_map/ppermute | solution.py:444
  217.2 3.4 %collective-permute-start.51 = (bf16[64,2048]{1,0:T(8,128)(2,1)S(1)}, bf16[64,2048]{1,0:T(8,128)(2,1)S(1)}, u32[]{:S(2)}, u32[]{:S(2)}) collective-permute-start(bf16[64,2048]{1,0:T(8,128)(2,1)S(1)} %get-tuple-element.216), channel_id=1, source_target_pairs={{0,4},{1,5},{2,6},{3,7},{4,0},{5,1},{6,2},{7,3},{8,12},{9,13},{10,... | collective-permute-start | bytes 786440 | tf_op jit(solution)/shard_map/ppermute | solution.py:444
  221.5 4.2 %collective-permute-done.50 = bf16[64,2048]{1,0:T(8,128)(2,1)S(1)} collective-permute-done((bf16[64,2048]{1,0:T(8,128)(2,1)S(1)}, bf16[64,2048]{1,0:T(8,128)(2,1)S(1)}, u32[]{:S(2)}, u32[]{:S(2)}) %collective-permute-start.50) | collective-permute-done | bytes 262176 | tf_op jit(solution)/shard_map/ppermute | solution.py:444
  225.7 2.7 %collective-permute-done.51 = bf16[64,2048]{1,0:T(8,128)(2,1)S(1)} collective-permute-done((bf16[64,2048]{1,0:T(8,128)(2,1)S(1)}, bf16[64,2048]{1,0:T(8,128)(2,1)S(1)}, u32[]{:S(2)}, u32[]{:S(2)}) %collective-permute-start.51) | collective-permute-done | bytes 262176 | tf_op jit(solution)/shard_map/ppermute | solution.py:444
  (239 shorter events, 71.5 us)
Async XLA Ops:
  0.0 23.4 %collective-permute-start.3 = (bf16[64,2048]{1,0:T(8,128)(2,1)}, bf16[64,2048]{1,0:T(8,128)(2,1)}, u32[]{:S(2)}, u32[]{:S(2)}) collective-permute-start(bf16[64,2048]{1,0:T(8,128)(2,1)} %refs_2_.1), channel_id=1, source_target_pairs={{0,4},{1,5},{2,6},{3,7},{4,0},{5,1},{6,2},{7,3},{8,12},{9,13},{10,... | collective-permute-start | bytes 786440 | tf_op jit(solution)/shard_map/ppermute | solution.py:444
  8.9 37.7 %collective-permute-start = (bf16[592,512]{1,0:T(8,128)(2,1)}, bf16[592,512]{1,0:T(8,128)(2,1)S(1)}, u32[]{:S(2)}, u32[]{:S(2)}) collective-permute-start(bf16[592,512]{1,0:T(8,128)(2,1)} %get-tuple-element.109), channel_id=1, source_target_pairs={{0,1},{1,0},{2,3},{3,2},{4,5},{5,4},{6,7},{7,6},{8,9},{9,8},{10,11... | collective-permute-start | bytes 1818632 | tf_op jit(solution)/shard_map/ppermute | solution.py:444
  10.4 36.9 %collective-permute-start.1 = (bf16[592,512]{1,0:T(8,128)(2,1)}, bf16[592,512]{1,0:T(8,128)(2,1)S(1)}, u32[]{:S(2)}, u32[]{:S(2)}) collective-permute-start(bf16[592,512]{1,0:T(8,128)(2,1)} %get-tuple-element.110), channel_id=1, source_target_pairs={{0,2},{1,3},{2,0},{3,1},{4,6},{5,7},{6,4},{7,5},{8,10},{9,11},{10,... | collective-permute-start | bytes 1818632 | tf_op jit(solution)/shard_map/ppermute | solution.py:444
  12.0 37.0 %collective-permute-start.2 = (bf16[592,512]{1,0:T(8,128)(2,1)}, bf16[592,512]{1,0:T(8,128)(2,1)S(1)}, u32[]{:S(2)}, u32[]{:S(2)}) collective-permute-start(bf16[592,512]{1,0:T(8,128)(2,1)} %get-tuple-element.111), channel_id=1, source_target_pairs={{0,3},{1,2},{2,1},{3,0},{4,7},{5,6},{6,5},{7,4},{8,11},{9,10},{10,... | collective-permute-start | bytes 1818632 | tf_op jit(solution)/shard_map/ppermute | solution.py:444
  12.4 30.8 %collective-permute-start.7 = (bf16[64,2048]{1,0:T(8,128)(2,1)S(1)}, bf16[64,2048]{1,0:T(8,128)(2,1)S(1)}, u32[]{:S(2)}, u32[]{:S(2)}) collective-permute-start(bf16[64,2048]{1,0:T(8,128)(2,1)S(1)} %constant_dynamic-slice_fusion), channel_id=1, source_target_pairs={{0,4},{1,5},{2,6},{3,7},{4,0},{5,1},{6,2},{7,3},{8,12},{9,13},{10,... | collective-permute-start | bytes 786440 | tf_op jit(solution)/shard_map/ppermute | solution.py:444
  25.7 19.5 %collective-permute-start.4 = (bf16[64,512]{1,0:T(8,128)(2,1)}, bf16[64,512]{1,0:T(8,128)(2,1)S(1)}, u32[]{:S(2)}, u32[]{:S(2)}) collective-permute-start(bf16[64,512]{1,0:T(8,128)(2,1)} %get-tuple-element.120), channel_id=1, source_target_pairs={{0,1},{1,0},{2,3},{3,2},{4,5},{5,4},{6,7},{7,6},{8,9},{9,8},{10,11... | collective-permute-start | bytes 196616 | tf_op jit(solution)/shard_map/ppermute | solution.py:444
  43.2 15.2 %collective-permute-start.8 = (bf16[64,2048]{1,0:T(8,128)(2,1)S(1)}, bf16[64,2048]{1,0:T(8,128)(2,1)S(1)}, u32[]{:S(2)}, u32[]{:S(2)}) collective-permute-start(bf16[64,2048]{1,0:T(8,128)(2,1)S(1)} %collective-permute-done.7.refs_0_), channel_id=1, source_target_pairs={{0,16},{8,24},{16,0},{24,8},{1,17},{9,25},{17,1},{25,9},{2,18},{10... | collective-permute-start | bytes 786440 | tf_op jit(solution)/shard_map/ppermute | solution.py:458
  59.0 15.4 %collective-permute-start.11 = (bf16[512,256]{1,0:T(8,128)(2,1)S(1)}, bf16[512,256]{1,0:T(8,128)(2,1)S(1)}, u32[]{:S(2)}, u32[]{:S(2)}) collective-permute-start(bf16[512,256]{1,0:T(8,128)(2,1)S(1)} %get-tuple-element.130), channel_id=1, source_target_pairs={{0,4},{1,5},{2,6},{3,7},{4,0},{5,1},{6,2},{7,3},{8,12},{9,13},{10,... | collective-permute-start | bytes 786440 | tf_op jit(solution)/shard_map/ppermute | solution.py:444
  75.7 9.3 %collective-permute-start.15 = (bf16[64,2048]{1,0:T(8,128)(2,1)S(1)}, bf16[64,2048]{1,0:T(8,128)(2,1)S(1)}, u32[]{:S(2)}, u32[]{:S(2)}) collective-permute-start(bf16[64,2048]{1,0:T(8,128)(2,1)S(1)} %get-tuple-element.139), channel_id=1, source_target_pairs={{0,1},{1,0},{2,3},{3,2},{4,5},{5,4},{6,7},{7,6},{8,9},{9,8},{10,11... | collective-permute-start | bytes 786440 | tf_op jit(solution)/shard_map/ppermute | solution.py:444
  77.8 11.2 %collective-permute-start.14 = (bf16[64,2048]{1,0:T(8,128)(2,1)S(1)}, bf16[64,2048]{1,0:T(8,128)(2,1)S(1)}, u32[]{:S(2)}, u32[]{:S(2)}) collective-permute-start(bf16[64,2048]{1,0:T(8,128)(2,1)S(1)} %get-tuple-element.142), channel_id=1, source_target_pairs={{0,1},{1,0},{2,3},{3,2},{4,5},{5,4},{6,7},{7,6},{8,9},{9,8},{10,11... | collective-permute-start | bytes 786440 | tf_op jit(solution)/shard_map/ppermute | solution.py:444
  91.9 11.7 %collective-permute-start.21 = (bf16[64,2048]{1,0:T(8,128)(2,1)S(1)}, bf16[64,2048]{1,0:T(8,128)(2,1)S(1)}, u32[]{:S(2)}, u32[]{:S(2)}) collective-permute-start(bf16[64,2048]{1,0:T(8,128)(2,1)S(1)} %multiply_convert_fusion.refs_3_), channel_id=1, source_target_pairs={{0,4},{1,5},{2,6},{3,7},{4,0},{5,1},{6,2},{7,3},{8,12},{9,13},{10,... | collective-permute-start | bytes 786440 | tf_op jit(solution)/shard_map/ppermute | solution.py:444
  93.8 10.4 %collective-permute-start.19 = (bf16[64,2048]{1,0:T(8,128)(2,1)S(1)}, bf16[64,2048]{1,0:T(8,128)(2,1)S(1)}, u32[]{:S(2)}, u32[]{:S(2)}) collective-permute-start(bf16[64,2048]{1,0:T(8,128)(2,1)S(1)} %multiply_convert_fusion.refs_3_), channel_id=1, source_target_pairs={{0,2},{1,3},{2,0},{3,1},{4,6},{5,7},{6,4},{7,5},{8,10},{9,11},{10,... | collective-permute-start | bytes 786440 | tf_op jit(solution)/shard_map/ppermute | solution.py:444
  95.5 12.1 %collective-permute-start.18 = (bf16[64,2048]{1,0:T(8,128)(2,1)S(1)}, bf16[64,2048]{1,0:T(8,128)(2,1)S(1)}, u32[]{:S(2)}, u32[]{:S(2)}) collective-permute-start(bf16[64,2048]{1,0:T(8,128)(2,1)S(1)} %multiply_convert_fusion.refs_3_), channel_id=1, source_target_pairs={{0,1},{1,0},{2,3},{3,2},{4,5},{5,4},{6,7},{7,6},{8,9},{9,8},{10,11... | collective-permute-start | bytes 786440 | tf_op jit(solution)/shard_map/ppermute | solution.py:444
  96.5 11.6 %collective-permute-start.25 = (bf16[64,2048]{1,0:T(8,128)(2,1)S(1)}, bf16[64,2048]{1,0:T(8,128)(2,1)S(1)}, u32[]{:S(2)}, u32[]{:S(2)}) collective-permute-start(bf16[64,2048]{1,0:T(8,128)(2,1)S(1)} %multiply_convert_fusion.refs_3_), channel_id=1, source_target_pairs={{0,16},{8,24},{16,0},{24,8},{1,17},{9,25},{17,1},{25,9},{2,18},{10... | collective-permute-start | bytes 786440 | tf_op jit(solution)/shard_map/ppermute | solution.py:454
  104.2 9.2 %collective-permute-start.20 = (bf16[64,2048]{1,0:T(8,128)(2,1)S(1)}, bf16[64,2048]{1,0:T(8,128)(2,1)S(1)}, u32[]{:S(2)}, u32[]{:S(2)}) collective-permute-start(bf16[64,2048]{1,0:T(8,128)(2,1)S(1)} %collective-permute-done.19.refs_0_), channel_id=1, source_target_pairs={{0,1},{1,0},{2,3},{3,2},{4,5},{5,4},{6,7},{7,6},{8,9},{9,8},{10,11... | collective-permute-start | bytes 786440 | tf_op jit(solution)/shard_map/ppermute | solution.py:444
  105.6 18.3 %collective-permute-start.22 = (bf16[64,2048]{1,0:T(8,128)(2,1)S(1)}, bf16[64,2048]{1,0:T(8,128)(2,1)S(1)}, u32[]{:S(2)}, u32[]{:S(2)}) collective-permute-start(bf16[64,2048]{1,0:T(8,128)(2,1)S(1)} %collective-permute-done.21.refs_2_), channel_id=1, source_target_pairs={{0,1},{1,0},{2,3},{3,2},{4,5},{5,4},{6,7},{7,6},{8,9},{9,8},{10,11... | collective-permute-start | bytes 786440 | tf_op jit(solution)/shard_map/ppermute | solution.py:444
  107.6 16.4 %collective-permute-start.26 = (bf16[64,2048]{1,0:T(8,128)(2,1)S(1)}, bf16[64,2048]{1,0:T(8,128)(2,1)}, u32[]{:S(2)}, u32[]{:S(2)}) collective-permute-start(bf16[64,2048]{1,0:T(8,128)(2,1)S(1)} %collective-permute-done.19.refs_0_), channel_id=1, source_target_pairs={{0,16},{8,24},{16,0},{24,8},{1,17},{9,25},{17,1},{25,9},{2,18},{10... | collective-permute-start | bytes 786440 | tf_op jit(solution)/shard_map/ppermute | solution.py:454
  108.1 15.9 %collective-permute-start.27 = (bf16[64,2048]{1,0:T(8,128)(2,1)S(1)}, bf16[64,2048]{1,0:T(8,128)(2,1)}, u32[]{:S(2)}, u32[]{:S(2)}) collective-permute-start(bf16[64,2048]{1,0:T(8,128)(2,1)S(1)} %collective-permute-done.21.refs_2_), channel_id=1, source_target_pairs={{0,16},{8,24},{16,0},{24,8},{1,17},{9,25},{17,1},{25,9},{2,18},{10... | collective-permute-start | bytes 786440 | tf_op jit(solution)/shard_map/ppermute | solution.py:454
  110.4 13.6 %collective-permute-start.24 = (bf16[64,2048]{1,0:T(8,128)(2,1)S(1)}, bf16[64,2048]{1,0:T(8,128)(2,1)S(1)}, u32[]{:S(2)}, u32[]{:S(2)}) collective-permute-start(bf16[64,2048]{1,0:T(8,128)(2,1)S(1)} %collective-permute-done.23.refs_1_), channel_id=1, source_target_pairs={{0,1},{1,0},{2,3},{3,2},{4,5},{5,4},{6,7},{7,6},{8,9},{9,8},{10,11... | collective-permute-start | bytes 786440 | tf_op jit(solution)/shard_map/ppermute | solution.py:444
  113.5 13.6 %collective-permute-start.28 = (bf16[64,2048]{1,0:T(8,128)(2,1)S(1)}, bf16[64,2048]{1,0:T(8,128)(2,1)}, u32[]{:S(2)}, u32[]{:S(2)}) collective-permute-start(bf16[64,2048]{1,0:T(8,128)(2,1)S(1)} %collective-permute-done.23.refs_1_), channel_id=1, source_target_pairs={{0,16},{8,24},{16,0},{24,8},{1,17},{9,25},{17,1},{25,9},{2,18},{10... | collective-permute-start | bytes 786440 | tf_op jit(solution)/shard_map/ppermute | solution.py:454
  130.6 26.7 %collective-permute-start.30 = (bf16[256,2048]{1,0:T(8,128)(2,1)}, bf16[256,2048]{1,0:T(8,128)(2,1)}, u32[]{:S(2)}, u32[]{:S(2)}) collective-permute-start(bf16[256,2048]{1,0:T(8,128)(2,1)} %get-tuple-element.170.refs_0_), channel_id=1, source_target_pairs={{0,1},{1,0},{2,3},{3,2},{4,5},{5,4},{6,7},{7,6},{8,9},{9,8},{10,11... | collective-permute-start | bytes 3145736 | tf_op jit(solution)/shard_map/ppermute | solution.py:444
  149.1 9.3 %collective-permute-start.35 = (bf16[256,2048]{1,0:T(8,128)(2,1)}, bf16[256,2048]{1,0:T(8,128)(2,1)S(1)}, u32[]{:S(2)}, u32[]{:S(2)}) collective-permute-start(bf16[256,2048]{1,0:T(8,128)(2,1)} %get-tuple-element.169), channel_id=1, source_target_pairs={{0,8},{8,0},{16,24},{24,16},{1,9},{9,1},{17,25},{25,17},{2,10},{10... | collective-permute-start | bytes 3145736 | tf_op jit(solution)/shard_map/ppermute | solution.py:454
  149.3 12.0 %collective-permute-start.33 = (bf16[256,2048]{1,0:T(8,128)(2,1)S(1)}, bf16[256,2048]{1,0:T(8,128)(2,1)}, u32[]{:S(2)}, u32[]{:S(2)}) collective-permute-start(bf16[256,2048]{1,0:T(8,128)(2,1)S(1)} %copy-done.28), channel_id=1, source_target_pairs={{0,8},{8,0},{16,24},{24,16},{1,9},{9,1},{17,25},{25,17},{2,10},{10... | collective-permute-start | bytes 3145736 | tf_op jit(solution)/shard_map/ppermute | solution.py:454
  158.0 18.5 %collective-permute-start.37 = (bf16[256,2048]{1,0:T(8,128)(2,1)}, bf16[256,2048]{1,0:T(8,128)(2,1)S(1)}, u32[]{:S(2)}, u32[]{:S(2)}) collective-permute-start(bf16[256,2048]{1,0:T(8,128)(2,1)} %get-tuple-element.184), channel_id=1, source_target_pairs={{0,8},{8,0},{16,24},{24,16},{1,9},{9,1},{17,25},{25,17},{2,10},{10... | collective-permute-start | bytes 3145736 | tf_op jit(solution)/shard_map/ppermute | solution.py:454
  160.3 19.6 %collective-permute-start.36 = (bf16[192,2048]{1,0:T(8,128)(2,1)S(1)}, bf16[192,2048]{1,0:T(8,128)(2,1)S(1)}, u32[]{:S(2)}, u32[]{:S(2)}) collective-permute-start(bf16[192,2048]{1,0:T(8,128)(2,1)S(1)} %slice.283), channel_id=1, source_target_pairs={{0,1},{1,0},{2,3},{3,2},{4,5},{5,4},{6,7},{7,6},{8,9},{9,8},{10,11... | collective-permute-start | bytes 2359304 | tf_op jit(solution)/shard_map/ppermute | solution.py:444
  183.9 9.2 %collective-permute-start.44 = (bf16[64,2048]{1,0:T(8,128)(2,1)S(1)}, bf16[64,2048]{1,0:T(8,128)(2,1)S(1)}, u32[]{:S(2)}, u32[]{:S(2)}) collective-permute-start(bf16[64,2048]{1,0:T(8,128)(2,1)S(1)} %add_convert_fusion.12), channel_id=1, source_target_pairs={{0,1},{1,0},{2,3},{3,2},{4,5},{5,4},{6,7},{7,6},{8,9},{9,8},{10,11... | collective-permute-start | bytes 786440 | tf_op jit(solution)/shard_map/ppermute | solution.py:444
  185.4 13.3 %collective-permute-start.43 = (bf16[64,2048]{1,0:T(8,128)(2,1)S(1)}, bf16[64,2048]{1,0:T(8,128)(2,1)S(1)}, u32[]{:S(2)}, u32[]{:S(2)}) collective-permute-start(bf16[64,2048]{1,0:T(8,128)(2,1)S(1)} %add_convert_fusion.11), channel_id=1, source_target_pairs={{0,1},{1,0},{2,3},{3,2},{4,5},{5,4},{6,7},{7,6},{8,9},{9,8},{10,11... | collective-permute-start | bytes 786440 | tf_op jit(solution)/shard_map/ppermute | solution.py:444
  188.1 15.5 %collective-permute-start.42 = (bf16[64,2048]{1,0:T(8,128)(2,1)S(1)}, bf16[64,2048]{1,0:T(8,128)(2,1)S(1)}, u32[]{:S(2)}, u32[]{:S(2)}) collective-permute-start(bf16[64,2048]{1,0:T(8,128)(2,1)S(1)} %add_convert_fusion.10), channel_id=1, source_target_pairs={{0,1},{1,0},{2,3},{3,2},{4,5},{5,4},{6,7},{7,6},{8,9},{9,8},{10,11... | collective-permute-start | bytes 786440 | tf_op jit(solution)/shard_map/ppermute | solution.py:444
  205.6 9.3 %collective-permute-start.41 = (bf16[64,2048]{1,0:T(8,128)(2,1)S(1)}, bf16[64,2048]{1,0:T(8,128)(2,1)S(1)}, u32[]{:S(2)}, u32[]{:S(2)}) collective-permute-start(bf16[64,2048]{1,0:T(8,128)(2,1)S(1)} %add_convert_fusion.9), channel_id=1, source_target_pairs={{0,1},{1,0},{2,3},{3,2},{4,5},{5,4},{6,7},{7,6},{8,9},{9,8},{10,11... | collective-permute-start | bytes 786440 | tf_op jit(solution)/shard_map/ppermute | solution.py:444
  206.9 13.7 %collective-permute-start.40 = (bf16[64,2048]{1,0:T(8,128)(2,1)S(1)}, bf16[64,2048]{1,0:T(8,128)(2,1)S(1)}, u32[]{:S(2)}, u32[]{:S(2)}) collective-permute-start(bf16[64,2048]{1,0:T(8,128)(2,1)S(1)} %slice.284), channel_id=1, source_target_pairs={{0,1},{1,0},{2,3},{3,2},{4,5},{5,4},{6,7},{7,6},{8,9},{9,8},{10,11... | collective-permute-start | bytes 786440 | tf_op jit(solution)/shard_map/ppermute | solution.py:444
  216.6 9.0 %collective-permute-start.50 = (bf16[64,2048]{1,0:T(8,128)(2,1)S(1)}, bf16[64,2048]{1,0:T(8,128)(2,1)S(1)}, u32[]{:S(2)}, u32[]{:S(2)}) collective-permute-start(bf16[64,2048]{1,0:T(8,128)(2,1)S(1)} %get-tuple-element.215), channel_id=1, source_target_pairs={{0,2},{1,3},{2,0},{3,1},{4,6},{5,7},{6,4},{7,5},{8,10},{9,11},{10,... | collective-permute-start | bytes 786440 | tf_op jit(solution)/shard_map/ppermute | solution.py:444
  217.2 11.1 %collective-permute-start.51 = (bf16[64,2048]{1,0:T(8,128)(2,1)S(1)}, bf16[64,2048]{1,0:T(8,128)(2,1)S(1)}, u32[]{:S(2)}, u32[]{:S(2)}) collective-permute-start(bf16[64,2048]{1,0:T(8,128)(2,1)S(1)} %get-tuple-element.216), channel_id=1, source_target_pairs={{0,4},{1,5},{2,6},{3,7},{4,0},{5,1},{6,2},{7,3},{8,12},{9,13},{10,... | collective-permute-start | bytes 786440 | tf_op jit(solution)/shard_map/ppermute | solution.py:444
  (50 other events, 550.6 us)

commit v15 on v14

--- a/solution.py
+++ b/solution.py
@@ -130,7 +130,7 @@
                 pl.BlockSpec((1, 1, rows), lambda h, *_: (h, 0, 0)),
             ],
         ),
-        compiler_params=pltpu.CompilerParams(vmem_limit_bytes=48 * 1024 * 1024),
+        compiler_params=pltpu.CompilerParams(vmem_limit_bytes=56 * 1024 * 1024),
         cost_estimate=pl.CostEstimate(
             flops=4 * rows * members * tokens * columns,
             bytes_accessed=2 * members * (block_rows + tok_rows) * columns,
@@ -680,13 +680,12 @@
             go = add_up([line_of(0, 1)] + home[1]).astype(bf16)
             near[1] = send(go, 0, 1, 0)
             goes.append(go)
-        if turn == 2:
-            go = add_up([line_of(0, 2)] + home[2] + [near[1]]).astype(bf16)
-            far = send(go, 1, 0, 0)
-            goes.append(go)
         if turn + 1 < len(turns):
             after = turns[turn + 1]
             last[after], _ = tie((last[after], goes))
+    far = add_up([line_of(0, 2)] + home[2] + [near[1]]).astype(bf16)
+    home[0], _ = tie((home[0], far))
+    far = send(far, 1, 0, 0)
     near[0] = send(add_up([line_of(0, 0)] + home[0]).astype(bf16), 0, 1, 0)
     total = add_up([stream, line_of(0, 3)] + home[3] + [near[0], far])
     return total.astype(bf16)

time: 230 us -> 232 us (level)
  waiting for transfers between devices: 85 us -> 80.2 us
  Pallas kernels: 68.5 us -> 72 us
  local copies, waits for them, and re-layouts: 8.01 us -> 11.3 us
    pallas_call x2, Pallas kernels: 9.12 us -> 12.5 us  [attend(): pl.pallas_call(functools.partial(attend_kernel, members, tokens, tok_rows...]
    ppermute x31, waiting for transfers between devices: 69.9 us -> 66.8 us  [send(): return lax.ppermute(value, 'exp', pairs)]
  transfers between devices with their start and end apart: 52 -> 52, of which waited for: 26 -> 23; matrix products, arithmetic and copies ran while one was open for 9% -> 11% of each run, Pallas kernels for 29% -> 31%
where the time goes in v15:
time: 232 us; the launch traced here: 231 us
  waiting for transfers between devices  80.2 us (35%)
  Pallas kernels  72 us (31%)
  starting transfers between devices  46.4 us (20%)
  other arithmetic  18.8 us (8%)
  local copies, waits for them, and re-layouts  11.3 us (5%)
    ppermute x31, waiting for transfers between devices, send(): return lax.ppermute(value, 'exp', pairs)  66.8 us
    ppermute x31, starting transfers between devices, send(): return lax.ppermute(value, 'exp', pairs)  36.8 us
    pallas_call x2, Pallas kernels, routed_expert(): pl.pallas_call(functools.partial(routed_kernel, parts, len(more), entries...  30.5 us
    pallas_call x2, Pallas kernels, shared_expert(): pl.pallas_call(functools.partial(shared_kernel, len(pieces)), out_shape=j...  15.2 us
    ppermute x20, waiting for transfers between devices, send_req(): return lax.ppermute(value, 'req', pairs)  13.4 us
    pallas_call x2, Pallas kernels, attend(): pl.pallas_call(functools.partial(attend_kernel, members, tokens, tok_rows...  12.5 us
    ppermute x20, starting transfers between devices, send_req(): return lax.ppermute(value, 'req', pairs)  8 us
    pallas_call x2, Pallas kernels, pack(): pl.pallas_call(functools.partial(pack_kernel, members, len(parts), column...  6.38 us
  transfers between devices with their start and end apart: 52, of which 23 were waited for; matrix products, arithmetic and copies ran while one was open for 11% of the time, Pallas kernels for 31%

profile of v15, /device:TPU:0, one launch (start us, length us, event | category | flops | bytes accessed | tf_op | source)
XLA Modules:
  0.0 230.7 jit_solution(5814590935328443919)
XLA Ops:
  0.0 4.1 %collective-permute-start.3 = (bf16[64,2048]{1,0:T(8,128)(2,1)}, bf16[64,2048]{1,0:T(8,128)(2,1)}, u32[]{:S(2)}, u32[]{:S(2)}) collective-permute-start(bf16[64,2048]{1,0:T(8,128)(2,1)} %refs_2_.1), channel_id=1, source_target_pairs={{0,4},{1,5},{2,6},{3,7},{4,0},{5,1},{6,2},{7,3},{8,12},{9,13},{10,... | collective-permute-start | bytes 786440 | tf_op jit(solution)/shard_map/ppermute | solution.py:444
  4.8 4.1 %shard_map.181 = (bf16[592,512]{1,0:T(8,128)(2,1)}, bf16[592,512]{1,0:T(8,128)(2,1)}, bf16[592,512]{1,0:T(8,128)(2,1)}, bf16[592,512]{1,0:T(8,128)(2,1)}) custom-call(s32[8]{0:T(128)} %stack.175.order, bf16[256,2048]{1,0:T(8,128)(2,1)} %bitcast.111, bf16[256,2048]{1,0:T(8,128)(2,1)} %bitcast.112, bf16[64,2048]{1,0:T(8,128)(2,1)} %refs_2_.1, f32[4,64]{1,0:T(4,128)} %bitcast.125), custom_call_target="tpu_custom_call" | custom-call | bytes 4849664 | tf_op jit(solution)/shard_map/pallas_call | solution.py:58
  24.1 2.3 %shard_map.183 = (bf16[64,512]{1,0:T(8,128)(2,1)}, bf16[64,512]{1,0:T(8,128)(2,1)}, bf16[64,512]{1,0:T(8,128)(2,1)}, bf16[64,512]{1,0:T(8,128)(2,1)}) custom-call(s32[8]{0:T(128)} %stack.175.order, bf16[64,2048]{1,0:T(8,128)(2,1)} %collective-permute-done.3.refs_0_), custom_call_target="tpu_custom_call" | custom-call | bytes 524288 | tf_op jit(solution)/shard_map/pallas_call | solution.py:58
  28.1 15.2 %collective-permute-done.7.refs_0_ = bf16[64,2048]{1,0:T(8,128)(2,1)S(1)} collective-permute-done((bf16[64,2048]{1,0:T(8,128)(2,1)}, bf16[64,2048]{1,0:T(8,128)(2,1)S(1)}, u32[]{:S(2)}, u32[]{:S(2)}) %collective-permute-start.7) | collective-permute-done | bytes 262176 | tf_op jit(solution)/shard_map/ppermute | solution.py:444
  52.1 2.2 collective-permute-done.6.refs_7_
  54.9 6.3 %shard_map.184 = (bf16[512,256]{1,0:T(8,128)(2,1)}, f32[4,1,256]{2,1,0:T(1,128)}) custom-call(s32[8]{0:T(128)} %get-tuple-element.214.page_req, s32[8]{0:T(128)} %get-tuple-element.213.page_slot, bf16[592,512]{1,0:T(8,128)(2,1)} %get-tuple-element.113.refs_0_, bf16[592,512]{1,0:T(8,128)(2,1)} %copy-done.4, bf16[592,512]{1,0:T(8,128)(2,1)} %copy-done.5, ...), custom_call_target="tpu_custom_call" | custom-call | flops 536870912 | bytes 2686976 | tf_op jit(solution)/shard_map/pallas_call | solution.py:116
  63.8 2.1 collective-permute-start.11
  65.9 6.2 %shard_map.182 = (bf16[512,256]{1,0:T(8,128)(2,1)}, f32[4,1,256]{2,1,0:T(1,128)}) custom-call(s32[8]{0:T(128)} %get-tuple-element.214.page_req, s32[8]{0:T(128)} %get-tuple-element.213.page_slot, bf16[592,512]{1,0:T(8,128)(2,1)} %get-tuple-element.113.refs_0_, bf16[592,512]{1,0:T(8,128)(2,1)} %copy-done.4, bf16[592,512]{1,0:T(8,128)(2,1)} %copy-done.5, ...), custom_call_target="tpu_custom_call" | custom-call | flops 536870912 | bytes 2686976 | tf_op jit(solution)/shard_map/pallas_call | solution.py:116
  73.1 2.1 collective-permute-start.12
  75.2 4.1 %collective-permute-done.13 = f32[2,2,4,64]{3,2,1,0:T(4,128)S(1)} collective-permute-done((f32[2,2,4,64]{3,2,1,0:T(4,128)S(1)}, f32[2,2,4,64]{3,2,1,0:T(4,128)S(1)}, u32[]{:S(2)}, u32[]{:S(2)}) %collective-permute-start.13) | collective-permute-done | bytes 4128 | tf_op jit(solution)/shard_map/ppermute | solution.py:444
  85.5 6.0 %collective-permute-done.15 = bf16[64,2048]{1,0:T(8,128)(2,1)S(1)} collective-permute-done((bf16[64,2048]{1,0:T(8,128)(2,1)S(1)}, bf16[64,2048]{1,0:T(8,128)(2,1)S(1)}, u32[]{:S(2)}, u32[]{:S(2)}) %collective-permute-start.15) | collective-permute-done | bytes 262176 | tf_op jit(solution)/shard_map/ppermute | solution.py:444
  92.3 3.2 %collective-permute-done.17 = f32[2,2,2,4,64]{4,3,2,1,0:T(4,128)S(1)} collective-permute-done((f32[2,2,2,4,64]{4,3,2,1,0:T(4,128)S(1)}, f32[2,2,2,4,64]{4,3,2,1,0:T(4,128)S(1)}, u32[]{:S(2)}, u32[]{:S(2)}) %collective-permute-start.17) | collective-permute-done | bytes 8224 | tf_op jit(solution)/shard_map/ppermute | solution.py:454
  95.5 2.5 %collective-permute-done.16 = bf16[64,2048]{1,0:T(8,128)(2,1)S(1)} collective-permute-done((bf16[64,2048]{1,0:T(8,128)(2,1)S(1)}, bf16[64,2048]{1,0:T(8,128)(2,1)S(1)}, u32[]{:S(2)}, u32[]{:S(2)}) %collective-permute-start.16) | collective-permute-done | bytes 262176 | tf_op jit(solution)/shard_map/ppermute | solution.py:444
  98.4 1.9 collective-permute-start.21
  103.5 6.6 %collective-permute-done.21.refs_2_ = bf16[64,2048]{1,0:T(8,128)(2,1)S(1)} collective-permute-done((bf16[64,2048]{1,0:T(8,128)(2,1)S(1)}, bf16[64,2048]{1,0:T(8,128)(2,1)S(1)}, u32[]{:S(2)}, u32[]{:S(2)}) %collective-permute-start.21) | collective-permute-done | bytes 262176 | tf_op jit(solution)/shard_map/ppermute | solution.py:444
  112.2 2.0 collective-permute-start.22
  117.0 3.0 %collective-permute-done.20.refs_0_ = bf16[64,2048]{1,0:T(8,128)(2,1)S(1)} collective-permute-done((bf16[64,2048]{1,0:T(8,128)(2,1)S(1)}, bf16[64,2048]{1,0:T(8,128)(2,1)S(1)}, u32[]{:S(2)}, u32[]{:S(2)}) %collective-permute-start.20) | collective-permute-done | bytes 262176 | tf_op jit(solution)/shard_map/ppermute | solution.py:444
  120.7 2.2 shard_map.189.refs_0_
  122.9 7.6 %shard_map.187 = bf16[256,2048]{1,0:T(8,128)(2,1)} custom-call(bf16[64,2048]{1,0:T(8,128)(2,1)} %copy-done.16, bf16[64,2048]{1,0:T(8,128)(2,1)} %copy-done.17, bf16[64,2048]{1,0:T(8,128)(2,1)} %copy-done.14, bf16[64,2048]{1,0:T(8,128)(2,1)} %copy-done.7, bf16[1,2048]{1,0:T(2,128)(2,1)} %reshape.550.refs_4_, bf16[704,2048]{1,0:T(8,128)(2,1)} %bitcast.106, ...), custom_call_target="tpu_custom_call" | custom-call | flops 2214592512 | bytes 10747904 | tf_op jit(solution)/shard_map/pallas_call | solution.py:265
  130.7 3.0 %collective-permute-done.28.refs_5_ = bf16[64,2048]{1,0:T(8,128)(2,1)} collective-permute-done((bf16[64,2048]{1,0:T(8,128)(2,1)S(1)}, bf16[64,2048]{1,0:T(8,128)(2,1)}, u32[]{:S(2)}, u32[]{:S(2)}) %collective-permute-start.28) | collective-permute-done | bytes 262176 | tf_op jit(solution)/shard_map/ppermute | solution.py:454
  133.6 2.9 %shard_map.188 = (bf16[256,2048]{1,0:T(8,128)(2,1)}, bf16[256,2048]{1,0:T(8,128)(2,1)}) custom-call(bf16[64,2048]{1,0:T(8,128)(2,1)} %copy-done.12, bf16[64,2048]{1,0:T(8,128)(2,1)} %copy-done.15, bf16[64,2048]{1,0:T(8,128)(2,1)} %copy-done.13, bf16[64,2048]{1,0:T(8,128)(2,1)} %copy-done.11, bf16[64,2048]{1,0:T(8,128)(2,1)} %collective-permute-done.26.refs_4_, ...), custom_call_target="tpu_custom_call" | custom-call | bytes 4194304 | tf_op jit(solution)/shard_map/pallas_call | solution.py:214
  140.4 15.3 %shard_map.190 = (bf16[256,2048]{1,0:T(8,128)(2,1)}, bf16[256,2048]{1,0:T(8,128)(2,1)}, bf16[256,2048]{1,0:T(8,128)(2,1)}, bf16[256,2048]{1,0:T(8,128)(2,1)}) custom-call(bf16[256,2048]{1,0:T(8,128)(2,1)} %shard_map.189.refs_0_, bf16[256,2048]{1,0:T(8,128)(2,1)} %get-tuple-element.159.refs_1_, bf16[256,2048]{1,0:T(8,128)(2,1)} %collective-permute-done.31.refs_2_, ...), custom_call_target="tpu_custom_call" | custom-call | flops 8254390272 | bytes 25690112 | tf_op jit(solution)/shard_map/pallas_call | solution.py:363
  156.2 7.6 %shard_map.191 = bf16[256,2048]{1,0:T(8,128)(2,1)} custom-call(bf16[64,2048]{1,0:T(8,128)(2,1)} %copy-done.12, bf16[64,2048]{1,0:T(8,128)(2,1)} %copy-done.15, bf16[64,2048]{1,0:T(8,128)(2,1)} %copy-done.13, bf16[64,2048]{1,0:T(8,128)(2,1)} %copy-done.11, bf16[1,2048]{1,0:T(2,128)(2,1)} %reshape.550.refs_4_, bf16[704,2048]{1,0:T(8,128)(2,1)} %bitcast.107, ...), custom_call_target="tpu_custom_call" | custom-call | flops 2214592512 | bytes 10747904 | tf_op jit(solution)/shard_map/pallas_call | solution.py:265
  167.9 15.2 %shard_map.192 = (bf16[64,2048]{1,0:T(8,128)(2,1)}, bf16[64,2048]{1,0:T(8,128)(2,1)}, bf16[64,2048]{1,0:T(8,128)(2,1)}, bf16[64,2048]{1,0:T(8,128)(2,1)}, bf16[6...) custom-call(bf16[256,2048]{1,0:T(8,128)(2,1)} %get-tuple-element.171, ...), custom_call_target="tpu_custom_call" | custom-call | flops 8254390272 | bytes 25690112 | tf_op jit(solution)/shard_map/pallas_call | solution.py:363
  183.2 3.3 %collective-permute-done.36 = bf16[192,2048]{1,0:T(8,128)(2,1)S(1)} collective-permute-done((bf16[192,2048]{1,0:T(8,128)(2,1)S(1)}, bf16[192,2048]{1,0:T(8,128)(2,1)S(1)}, u32[]{:S(2)}, u32[]{:S(2)}) %collective-permute-start.36) | collective-permute-done | bytes 786464 | tf_op jit(solution)/shard_map/ppermute | solution.py:444
  187.1 2.3 %collective-permute-done.39 = bf16[256,2048]{1,0:T(8,128)(2,1)S(1)} collective-permute-done((bf16[256,2048]{1,0:T(8,128)(2,1)}, bf16[256,2048]{1,0:T(8,128)(2,1)S(1)}, u32[]{:S(2)}, u32[]{:S(2)}) %collective-permute-start.39) | collective-permute-done | bytes 1048608 | tf_op jit(solution)/shard_map/ppermute | solution.py:454
  197.4 2.3 collective-permute-done.44
  200.3 5.0 %collective-permute-done.43 = bf16[64,2048]{1,0:T(8,128)(2,1)S(1)} collective-permute-done((bf16[64,2048]{1,0:T(8,128)(2,1)S(1)}, bf16[64,2048]{1,0:T(8,128)(2,1)S(1)}, u32[]{:S(2)}, u32[]{:S(2)}) %collective-permute-start.43) | collective-permute-done | bytes 262176 | tf_op jit(solution)/shard_map/ppermute | solution.py:444
  208.2 2.7 %collective-permute-done.42 = bf16[64,2048]{1,0:T(8,128)(2,1)S(1)} collective-permute-done((bf16[64,2048]{1,0:T(8,128)(2,1)S(1)}, bf16[64,2048]{1,0:T(8,128)(2,1)S(1)}, u32[]{:S(2)}, u32[]{:S(2)}) %collective-permute-start.42) | collective-permute-done | bytes 262176 | tf_op jit(solution)/shard_map/ppermute | solution.py:444
  211.5 5.0 %collective-permute-done.41 = bf16[64,2048]{1,0:T(8,128)(2,1)S(1)} collective-permute-done((bf16[64,2048]{1,0:T(8,128)(2,1)S(1)}, bf16[64,2048]{1,0:T(8,128)(2,1)S(1)}, u32[]{:S(2)}, u32[]{:S(2)}) %collective-permute-start.41) | collective-permute-done | bytes 262176 | tf_op jit(solution)/shard_map/ppermute | solution.py:444
  219.4 2.1 collective-permute-start.51
  223.4 6.3 %collective-permute-done.50 = bf16[64,2048]{1,0:T(8,128)(2,1)S(1)} collective-permute-done((bf16[64,2048]{1,0:T(8,128)(2,1)S(1)}, bf16[64,2048]{1,0:T(8,128)(2,1)S(1)}, u32[]{:S(2)}, u32[]{:S(2)}) %collective-permute-start.50) | collective-permute-done | bytes 262176 | tf_op jit(solution)/shard_map/ppermute | solution.py:444
  (256 shorter events, 72.0 us)
Async XLA Ops:
  0.0 24.0 %collective-permute-start.3 = (bf16[64,2048]{1,0:T(8,128)(2,1)}, bf16[64,2048]{1,0:T(8,128)(2,1)}, u32[]{:S(2)}, u32[]{:S(2)}) collective-permute-start(bf16[64,2048]{1,0:T(8,128)(2,1)} %refs_2_.1), channel_id=1, source_target_pairs={{0,4},{1,5},{2,6},{3,7},{4,0},{5,1},{6,2},{7,3},{8,12},{9,13},{10,... | collective-permute-start | bytes 786440 | tf_op jit(solution)/shard_map/ppermute | solution.py:444
  8.8 40.0 %collective-permute-start = (bf16[592,512]{1,0:T(8,128)(2,1)}, bf16[592,512]{1,0:T(8,128)(2,1)S(1)}, u32[]{:S(2)}, u32[]{:S(2)}) collective-permute-start(bf16[592,512]{1,0:T(8,128)(2,1)} %get-tuple-element.110), channel_id=1, source_target_pairs={{0,1},{1,0},{2,3},{3,2},{4,5},{5,4},{6,7},{7,6},{8,9},{9,8},{10,11... | collective-permute-start | bytes 1818632 | tf_op jit(solution)/shard_map/ppermute | solution.py:444
  10.4 39.9 %collective-permute-start.1 = (bf16[592,512]{1,0:T(8,128)(2,1)}, bf16[592,512]{1,0:T(8,128)(2,1)S(1)}, u32[]{:S(2)}, u32[]{:S(2)}) collective-permute-start(bf16[592,512]{1,0:T(8,128)(2,1)} %get-tuple-element.111), channel_id=1, source_target_pairs={{0,2},{1,3},{2,0},{3,1},{4,6},{5,7},{6,4},{7,5},{8,10},{9,11},{10,... | collective-permute-start | bytes 1818632 | tf_op jit(solution)/shard_map/ppermute | solution.py:444
  12.0 38.3 %collective-permute-start.2 = (bf16[592,512]{1,0:T(8,128)(2,1)}, bf16[592,512]{1,0:T(8,128)(2,1)S(1)}, u32[]{:S(2)}, u32[]{:S(2)}) collective-permute-start(bf16[592,512]{1,0:T(8,128)(2,1)} %get-tuple-element.112), channel_id=1, source_target_pairs={{0,3},{1,2},{2,1},{3,0},{4,7},{5,6},{6,5},{7,4},{8,11},{9,10},{10,... | collective-permute-start | bytes 1818632 | tf_op jit(solution)/shard_map/ppermute | solution.py:444
  13.1 30.2 %collective-permute-start.7 = (bf16[64,2048]{1,0:T(8,128)(2,1)}, bf16[64,2048]{1,0:T(8,128)(2,1)S(1)}, u32[]{:S(2)}, u32[]{:S(2)}) collective-permute-start(bf16[64,2048]{1,0:T(8,128)(2,1)} %constant_dynamic-slice_fusion), channel_id=1, source_target_pairs={{0,4},{1,5},{2,6},{3,7},{4,0},{5,1},{6,2},{7,3},{8,12},{9,13},{10,... | collective-permute-start | bytes 786440 | tf_op jit(solution)/shard_map/ppermute | solution.py:444
  26.4 21.2 %collective-permute-start.4 = (bf16[64,512]{1,0:T(8,128)(2,1)}, bf16[64,512]{1,0:T(8,128)(2,1)S(1)}, u32[]{:S(2)}, u32[]{:S(2)}) collective-permute-start(bf16[64,512]{1,0:T(8,128)(2,1)} %get-tuple-element.121), channel_id=1, source_target_pairs={{0,1},{1,0},{2,3},{3,2},{4,5},{5,4},{6,7},{7,6},{8,9},{9,8},{10,11... | collective-permute-start | bytes 196616 | tf_op jit(solution)/shard_map/ppermute | solution.py:444
  43.3 17.8 %collective-permute-start.8 = (bf16[64,2048]{1,0:T(8,128)(2,1)S(1)}, bf16[64,2048]{1,0:T(8,128)(2,1)S(1)}, u32[]{:S(2)}, u32[]{:S(2)}) collective-permute-start(bf16[64,2048]{1,0:T(8,128)(2,1)S(1)} %collective-permute-done.7.refs_0_), channel_id=1, source_target_pairs={{0,16},{8,24},{16,0},{24,8},{1,17},{9,25},{17,1},{25,9},{2,18},{10... | collective-permute-start | bytes 786440 | tf_op jit(solution)/shard_map/ppermute | solution.py:458
  61.2 11.0 %collective-permute-start.10 = (bf16[64,2048]{1,0:T(8,128)(2,1)S(1)}, bf16[64,2048]{1,0:T(8,128)(2,1)S(1)}, u32[]{:S(2)}, u32[]{:S(2)}) collective-permute-start(bf16[64,2048]{1,0:T(8,128)(2,1)S(1)} %collective-permute-done.8.refs_1_), channel_id=1, source_target_pairs={{0,8},{8,0},{16,24},{24,16},{1,9},{9,1},{17,25},{25,17},{2,10},{10... | collective-permute-start | bytes 786440 | tf_op jit(solution)/shard_map/ppermute | solution.py:454
  61.2 10.9 %collective-permute-start.9 = (bf16[64,2048]{1,0:T(8,128)(2,1)S(1)}, bf16[64,2048]{1,0:T(8,128)(2,1)S(1)}, u32[]{:S(2)}, u32[]{:S(2)}) collective-permute-start(bf16[64,2048]{1,0:T(8,128)(2,1)S(1)} %collective-permute-done.7.refs_0_), channel_id=1, source_target_pairs={{0,8},{8,0},{16,24},{24,16},{1,9},{9,1},{17,25},{25,17},{2,10},{10... | collective-permute-start | bytes 786440 | tf_op jit(solution)/shard_map/ppermute | solution.py:454
  63.8 15.5 %collective-permute-start.11 = (bf16[512,256]{1,0:T(8,128)(2,1)}, bf16[512,256]{1,0:T(8,128)(2,1)S(1)}, u32[]{:S(2)}, u32[]{:S(2)}) collective-permute-start(bf16[512,256]{1,0:T(8,128)(2,1)} %get-tuple-element.131), channel_id=1, source_target_pairs={{0,4},{1,5},{2,6},{3,7},{4,0},{5,1},{6,2},{7,3},{8,12},{9,13},{10,... | collective-permute-start | bytes 786440 | tf_op jit(solution)/shard_map/ppermute | solution.py:444
  84.3 11.2 %collective-permute-start.14 = (bf16[64,2048]{1,0:T(8,128)(2,1)S(1)}, bf16[64,2048]{1,0:T(8,128)(2,1)S(1)}, u32[]{:S(2)}, u32[]{:S(2)}) collective-permute-start(bf16[64,2048]{1,0:T(8,128)(2,1)S(1)} %get-tuple-element.143), channel_id=1, source_target_pairs={{0,1},{1,0},{2,3},{3,2},{4,5},{5,4},{6,7},{7,6},{8,9},{9,8},{10,11... | collective-permute-start | bytes 786440 | tf_op jit(solution)/shard_map/ppermute | solution.py:444
  98.4 11.7 %collective-permute-start.21 = (bf16[64,2048]{1,0:T(8,128)(2,1)S(1)}, bf16[64,2048]{1,0:T(8,128)(2,1)S(1)}, u32[]{:S(2)}, u32[]{:S(2)}) collective-permute-start(bf16[64,2048]{1,0:T(8,128)(2,1)S(1)} %multiply_convert_fusion.refs_3_), channel_id=1, source_target_pairs={{0,4},{1,5},{2,6},{3,7},{4,0},{5,1},{6,2},{7,3},{8,12},{9,13},{10,... | collective-permute-start | bytes 786440 | tf_op jit(solution)/shard_map/ppermute | solution.py:444
  100.3 10.4 %collective-permute-start.19 = (bf16[64,2048]{1,0:T(8,128)(2,1)S(1)}, bf16[64,2048]{1,0:T(8,128)(2,1)S(1)}, u32[]{:S(2)}, u32[]{:S(2)}) collective-permute-start(bf16[64,2048]{1,0:T(8,128)(2,1)S(1)} %multiply_convert_fusion.refs_3_), channel_id=1, source_target_pairs={{0,2},{1,3},{2,0},{3,1},{4,6},{5,7},{6,4},{7,5},{8,10},{9,11},{10,... | collective-permute-start | bytes 786440 | tf_op jit(solution)/shard_map/ppermute | solution.py:444
  102.1 12.1 %collective-permute-start.18 = (bf16[64,2048]{1,0:T(8,128)(2,1)S(1)}, bf16[64,2048]{1,0:T(8,128)(2,1)S(1)}, u32[]{:S(2)}, u32[]{:S(2)}) collective-permute-start(bf16[64,2048]{1,0:T(8,128)(2,1)S(1)} %multiply_convert_fusion.refs_3_), channel_id=1, source_target_pairs={{0,1},{1,0},{2,3},{3,2},{4,5},{5,4},{6,7},{7,6},{8,9},{9,8},{10,11... | collective-permute-start | bytes 786440 | tf_op jit(solution)/shard_map/ppermute | solution.py:444
  103.0 11.7 %collective-permute-start.25 = (bf16[64,2048]{1,0:T(8,128)(2,1)S(1)}, bf16[64,2048]{1,0:T(8,128)(2,1)S(1)}, u32[]{:S(2)}, u32[]{:S(2)}) collective-permute-start(bf16[64,2048]{1,0:T(8,128)(2,1)S(1)} %multiply_convert_fusion.refs_3_), channel_id=1, source_target_pairs={{0,16},{8,24},{16,0},{24,8},{1,17},{9,25},{17,1},{25,9},{2,18},{10... | collective-permute-start | bytes 786440 | tf_op jit(solution)/shard_map/ppermute | solution.py:454
  112.2 18.4 %collective-permute-start.22 = (bf16[64,2048]{1,0:T(8,128)(2,1)S(1)}, bf16[64,2048]{1,0:T(8,128)(2,1)S(1)}, u32[]{:S(2)}, u32[]{:S(2)}) collective-permute-start(bf16[64,2048]{1,0:T(8,128)(2,1)S(1)} %collective-permute-done.21.refs_2_), channel_id=1, source_target_pairs={{0,1},{1,0},{2,3},{3,2},{4,5},{5,4},{6,7},{7,6},{8,9},{9,8},{10,11... | collective-permute-start | bytes 786440 | tf_op jit(solution)/shard_map/ppermute | solution.py:444
  114.2 16.4 %collective-permute-start.26 = (bf16[64,2048]{1,0:T(8,128)(2,1)S(1)}, bf16[64,2048]{1,0:T(8,128)(2,1)}, u32[]{:S(2)}, u32[]{:S(2)}) collective-permute-start(bf16[64,2048]{1,0:T(8,128)(2,1)S(1)} %collective-permute-done.19.refs_0_), channel_id=1, source_target_pairs={{0,16},{8,24},{16,0},{24,8},{1,17},{9,25},{17,1},{25,9},{2,18},{10... | collective-permute-start | bytes 786440 | tf_op jit(solution)/shard_map/ppermute | solution.py:454
  114.7 16.0 %collective-permute-start.27 = (bf16[64,2048]{1,0:T(8,128)(2,1)S(1)}, bf16[64,2048]{1,0:T(8,128)(2,1)}, u32[]{:S(2)}, u32[]{:S(2)}) collective-permute-start(bf16[64,2048]{1,0:T(8,128)(2,1)S(1)} %collective-permute-done.21.refs_2_), channel_id=1, source_target_pairs={{0,16},{8,24},{16,0},{24,8},{1,17},{9,25},{17,1},{25,9},{2,18},{10... | collective-permute-start | bytes 786440 | tf_op jit(solution)/shard_map/ppermute | solution.py:454
  117.0 13.6 %collective-permute-start.24 = (bf16[64,2048]{1,0:T(8,128)(2,1)S(1)}, bf16[64,2048]{1,0:T(8,128)(2,1)S(1)}, u32[]{:S(2)}, u32[]{:S(2)}) collective-permute-start(bf16[64,2048]{1,0:T(8,128)(2,1)S(1)} %collective-permute-done.23.refs_1_), channel_id=1, source_target_pairs={{0,1},{1,0},{2,3},{3,2},{4,5},{5,4},{6,7},{7,6},{8,9},{9,8},{10,11... | collective-permute-start | bytes 786440 | tf_op jit(solution)/shard_map/ppermute | solution.py:444
  120.0 13.6 %collective-permute-start.28 = (bf16[64,2048]{1,0:T(8,128)(2,1)S(1)}, bf16[64,2048]{1,0:T(8,128)(2,1)}, u32[]{:S(2)}, u32[]{:S(2)}) collective-permute-start(bf16[64,2048]{1,0:T(8,128)(2,1)S(1)} %collective-permute-done.23.refs_1_), channel_id=1, source_target_pairs={{0,16},{8,24},{16,0},{24,8},{1,17},{9,25},{17,1},{25,9},{2,18},{10... | collective-permute-start | bytes 786440 | tf_op jit(solution)/shard_map/ppermute | solution.py:454
  137.1 26.7 %collective-permute-start.30 = (bf16[256,2048]{1,0:T(8,128)(2,1)}, bf16[256,2048]{1,0:T(8,128)(2,1)}, u32[]{:S(2)}, u32[]{:S(2)}) collective-permute-start(bf16[256,2048]{1,0:T(8,128)(2,1)} %get-tuple-element.171.refs_0_), channel_id=1, source_target_pairs={{0,1},{1,0},{2,3},{3,2},{4,5},{5,4},{6,7},{7,6},{8,9},{9,8},{10,11... | collective-permute-start | bytes 3145736 | tf_op jit(solution)/shard_map/ppermute | solution.py:444
  155.9 12.1 %collective-permute-start.33 = (bf16[256,2048]{1,0:T(8,128)(2,1)S(1)}, bf16[256,2048]{1,0:T(8,128)(2,1)}, u32[]{:S(2)}, u32[]{:S(2)}) collective-permute-start(bf16[256,2048]{1,0:T(8,128)(2,1)S(1)} %copy-done.35), channel_id=1, source_target_pairs={{0,8},{8,0},{16,24},{24,16},{1,9},{9,1},{17,25},{25,17},{2,10},{10... | collective-permute-start | bytes 3145736 | tf_op jit(solution)/shard_map/ppermute | solution.py:454
  164.6 18.6 %collective-permute-start.37 = (bf16[256,2048]{1,0:T(8,128)(2,1)S(1)}, bf16[256,2048]{1,0:T(8,128)(2,1)S(1)}, u32[]{:S(2)}, u32[]{:S(2)}) collective-permute-start(bf16[256,2048]{1,0:T(8,128)(2,1)S(1)} %copy-done.36), channel_id=1, source_target_pairs={{0,8},{8,0},{16,24},{24,16},{1,9},{9,1},{17,25},{25,17},{2,10},{10... | collective-permute-start | bytes 3145736 | tf_op jit(solution)/shard_map/ppermute | solution.py:454
  166.9 19.7 %collective-permute-start.36 = (bf16[192,2048]{1,0:T(8,128)(2,1)S(1)}, bf16[192,2048]{1,0:T(8,128)(2,1)S(1)}, u32[]{:S(2)}, u32[]{:S(2)}) collective-permute-start(bf16[192,2048]{1,0:T(8,128)(2,1)S(1)} %slice.283), channel_id=1, source_target_pairs={{0,1},{1,0},{2,3},{3,2},{4,5},{5,4},{6,7},{7,6},{8,9},{9,8},{10,11... | collective-permute-start | bytes 2359304 | tf_op jit(solution)/shard_map/ppermute | solution.py:444
  192.0 13.3 %collective-permute-start.43 = (bf16[64,2048]{1,0:T(8,128)(2,1)S(1)}, bf16[64,2048]{1,0:T(8,128)(2,1)S(1)}, u32[]{:S(2)}, u32[]{:S(2)}) collective-permute-start(bf16[64,2048]{1,0:T(8,128)(2,1)S(1)} %add_convert_fusion.11), channel_id=1, source_target_pairs={{0,1},{1,0},{2,3},{3,2},{4,5},{5,4},{6,7},{7,6},{8,9},{9,8},{10,11... | collective-permute-start | bytes 786440 | tf_op jit(solution)/shard_map/ppermute | solution.py:444
  194.7 16.2 %collective-permute-start.42 = (bf16[64,2048]{1,0:T(8,128)(2,1)S(1)}, bf16[64,2048]{1,0:T(8,128)(2,1)S(1)}, u32[]{:S(2)}, u32[]{:S(2)}) collective-permute-start(bf16[64,2048]{1,0:T(8,128)(2,1)S(1)} %add_convert_fusion.10), channel_id=1, source_target_pairs={{0,1},{1,0},{2,3},{3,2},{4,5},{5,4},{6,7},{7,6},{8,9},{9,8},{10,11... | collective-permute-start | bytes 786440 | tf_op jit(solution)/shard_map/ppermute | solution.py:444
  195.3 21.2 %collective-permute-start.41 = (bf16[64,2048]{1,0:T(8,128)(2,1)S(1)}, bf16[64,2048]{1,0:T(8,128)(2,1)S(1)}, u32[]{:S(2)}, u32[]{:S(2)}) collective-permute-start(bf16[64,2048]{1,0:T(8,128)(2,1)S(1)} %add_convert_fusion.9), channel_id=1, source_target_pairs={{0,1},{1,0},{2,3},{3,2},{4,5},{5,4},{6,7},{7,6},{8,9},{9,8},{10,11... | collective-permute-start | bytes 786440 | tf_op jit(solution)/shard_map/ppermute | solution.py:444
  196.9 24.6 %collective-permute-start.40 = (bf16[64,2048]{1,0:T(8,128)(2,1)S(1)}, bf16[64,2048]{1,0:T(8,128)(2,1)S(1)}, u32[]{:S(2)}, u32[]{:S(2)}) collective-permute-start(bf16[64,2048]{1,0:T(8,128)(2,1)S(1)} %slice.284), channel_id=1, source_target_pairs={{0,1},{1,0},{2,3},{3,2},{4,5},{5,4},{6,7},{7,6},{8,9},{9,8},{10,11... | collective-permute-start | bytes 786440 | tf_op jit(solution)/shard_map/ppermute | solution.py:444
  205.4 11.8 %collective-permute-start.48 = (bf16[64,2048]{1,0:T(8,128)(2,1)S(1)}, bf16[64,2048]{1,0:T(8,128)(2,1)S(1)}, u32[]{:S(2)}, u32[]{:S(2)}) collective-permute-start(bf16[64,2048]{1,0:T(8,128)(2,1)S(1)} %add_convert_fusion.7), channel_id=1, source_target_pairs={{0,16},{8,24},{16,0},{24,8},{1,17},{9,25},{17,1},{25,9},{2,18},{10... | collective-permute-start | bytes 786440 | tf_op jit(solution)/shard_map/ppermute | solution.py:454
  206.7 10.4 %collective-permute-start.49 = (bf16[64,2048]{1,0:T(8,128)(2,1)S(1)}, bf16[64,2048]{1,0:T(8,128)(2,1)S(1)}, u32[]{:S(2)}, u32[]{:S(2)}) collective-permute-start(bf16[64,2048]{1,0:T(8,128)(2,1)S(1)} %add_convert_fusion.6), channel_id=1, source_target_pairs={{0,2},{1,3},{2,0},{3,1},{4,6},{5,7},{6,4},{7,5},{8,10},{9,11},{10,... | collective-permute-start | bytes 786440 | tf_op jit(solution)/shard_map/ppermute | solution.py:444
  218.0 11.7 %collective-permute-start.50 = (bf16[64,2048]{1,0:T(8,128)(2,1)S(1)}, bf16[64,2048]{1,0:T(8,128)(2,1)S(1)}, u32[]{:S(2)}, u32[]{:S(2)}) collective-permute-start(bf16[64,2048]{1,0:T(8,128)(2,1)S(1)} %add_convert_fusion.2), channel_id=1, source_target_pairs={{0,2},{1,3},{2,0},{3,1},{4,6},{5,7},{6,4},{7,5},{8,10},{9,11},{10,... | collective-permute-start | bytes 786440 | tf_op jit(solution)/shard_map/ppermute | solution.py:444
  219.4 10.3 %collective-permute-start.51 = (bf16[64,2048]{1,0:T(8,128)(2,1)S(1)}, bf16[64,2048]{1,0:T(8,128)(2,1)S(1)}, u32[]{:S(2)}, u32[]{:S(2)}) collective-permute-start(bf16[64,2048]{1,0:T(8,128)(2,1)S(1)} %add_convert_fusion.3), channel_id=1, source_target_pairs={{0,4},{1,5},{2,6},{3,7},{4,0},{5,1},{6,2},{7,3},{8,12},{9,13},{10,... | collective-permute-start | bytes 786440 | tf_op jit(solution)/shard_map/ppermute | solution.py:444
  (58 other events, 602.6 us)

commit v16 on v15

--- a/solution.py
+++ b/solution.py
@@ -130,7 +130,7 @@
                 pl.BlockSpec((1, 1, rows), lambda h, *_: (h, 0, 0)),
             ],
         ),
-        compiler_params=pltpu.CompilerParams(vmem_limit_bytes=56 * 1024 * 1024),
+        compiler_params=pltpu.CompilerParams(vmem_limit_bytes=48 * 1024 * 1024),
         cost_estimate=pl.CostEstimate(
             flops=4 * rows * members * tokens * columns,
             bytes_accessed=2 * members * (block_rows + tok_rows) * columns,

time: 232 us -> 225 us (0.970)
  Pallas kernels: 72 us -> 68.6 us
  local copies, waits for them, and re-layouts: 11.3 us -> 8.01 us
  other arithmetic: 18.8 us -> 16.3 us
    pallas_call x2, Pallas kernels: 12.5 us -> 9.11 us  [attend(): pl.pallas_call(functools.partial(attend_kernel, members, tokens, tok_rows...]
    ppermute x31, waiting for transfers between devices: 66.8 us -> 69.4 us  [send(): return lax.ppermute(value, 'exp', pairs)]
  transfers between devices with their start and end apart: 52 -> 52, of which waited for: 23 -> 24; matrix products, arithmetic and copies ran while one was open for 11% -> 9% of each run, Pallas kernels for 31% -> 30%
where the time goes in v16:
time: 225 us; the launch traced here: 224 us
  waiting for transfers between devices  82.3 us (37%)
  Pallas kernels  68.6 us (30%)
  starting transfers between devices  47.2 us (21%)
  other arithmetic  16.3 us (7%)
  local copies, waits for them, and re-layouts  8.01 us (4%)
    ppermute x31, waiting for transfers between devices, send(): return lax.ppermute(value, 'exp', pairs)  69.4 us
    ppermute x31, starting transfers between devices, send(): return lax.ppermute(value, 'exp', pairs)  37 us
    pallas_call x2, Pallas kernels, routed_expert(): pl.pallas_call(functools.partial(routed_kernel, parts, len(more), entries...  30.5 us
    pallas_call x2, Pallas kernels, shared_expert(): pl.pallas_call(functools.partial(shared_kernel, len(pieces)), out_shape=j...  15.2 us
    ppermute x20, waiting for transfers between devices, send_req(): return lax.ppermute(value, 'req', pairs)  12.9 us
    pallas_call x2, Pallas kernels, attend(): pl.pallas_call(functools.partial(attend_kernel, members, tokens, tok_rows...  9.11 us
    ppermute x20, starting transfers between devices, send_req(): return lax.ppermute(value, 'req', pairs)  8.7 us
    pallas_call x2, Pallas kernels, pack(): pl.pallas_call(functools.partial(pack_kernel, members, len(parts), column...  6.34 us
  transfers between devices with their start and end apart: 52, of which 24 were waited for; matrix products, arithmetic and copies ran while one was open for 9% of the time, Pallas kernels for 30%

profile of v16, /device:TPU:0, one launch (start us, length us, event | category | flops | bytes accessed | tf_op | source)
XLA Modules:
  0.0 224.2 jit_solution(6777905518276420086)
XLA Ops:
  0.0 4.1 %collective-permute-start.3 = (bf16[64,2048]{1,0:T(8,128)(2,1)}, bf16[64,2048]{1,0:T(8,128)(2,1)}, u32[]{:S(2)}, u32[]{:S(2)}) collective-permute-start(bf16[64,2048]{1,0:T(8,128)(2,1)} %refs_2_.1), channel_id=1, source_target_pairs={{0,4},{1,5},{2,6},{3,7},{4,0},{5,1},{6,2},{7,3},{8,12},{9,13},{10,... | collective-permute-start | bytes 786440 | tf_op jit(solution)/shard_map/ppermute | solution.py:444
  4.8 4.0 %shard_map.181 = (bf16[592,512]{1,0:T(8,128)(2,1)}, bf16[592,512]{1,0:T(8,128)(2,1)}, bf16[592,512]{1,0:T(8,128)(2,1)}, bf16[592,512]{1,0:T(8,128)(2,1)}) custom-call(s32[8]{0:T(128)} %stack.175.order, bf16[256,2048]{1,0:T(8,128)(2,1)} %bitcast.111, bf16[256,2048]{1,0:T(8,128)(2,1)} %bitcast.112, bf16[64,2048]{1,0:T(8,128)(2,1)} %refs_2_.1, f32[4,64]{1,0:T(4,128)} %bitcast.125), custom_call_target="tpu_custom_call" | custom-call | bytes 4849664 | tf_op jit(solution)/shard_map/pallas_call | solution.py:58
  23.2 2.3 %shard_map.183 = (bf16[64,512]{1,0:T(8,128)(2,1)}, bf16[64,512]{1,0:T(8,128)(2,1)}, bf16[64,512]{1,0:T(8,128)(2,1)}, bf16[64,512]{1,0:T(8,128)(2,1)}) custom-call(s32[8]{0:T(128)} %stack.175.order, bf16[64,2048]{1,0:T(8,128)(2,1)} %collective-permute-done.3.refs_0_), custom_call_target="tpu_custom_call" | custom-call | bytes 524288 | tf_op jit(solution)/shard_map/pallas_call | solution.py:58
  27.3 15.9 %collective-permute-done.7.refs_0_ = bf16[64,2048]{1,0:T(8,128)(2,1)S(1)} collective-permute-done((bf16[64,2048]{1,0:T(8,128)(2,1)S(1)}, bf16[64,2048]{1,0:T(8,128)(2,1)S(1)}, u32[]{:S(2)}, u32[]{:S(2)}) %collective-permute-start.7) | collective-permute-done | bytes 262176 | tf_op jit(solution)/shard_map/ppermute | solution.py:444
  50.0 2.0 collective-permute-done.6.refs_7_
  53.9 4.5 %shard_map.184 = (bf16[512,256]{1,0:T(8,128)(2,1)S(1)}, f32[4,1,256]{2,1,0:T(1,128)S(1)}) custom-call(s32[8]{0:T(128)S(1)} %get-tuple-element.214.page_req, s32[8]{0:T(128)S(1)} %get-tuple-element.213.page_slot, bf16[592,512]{1,0:T(8,128)(2,1)S(1)} %copy-done.1, bf16[592,512]{1,0:T(8,128)(2,1)S(1)} %collective-permute-done.refs_1_, ...), custom_call_target="tpu_custom_call" | custom-call | flops 536870912 | bytes 2686976 | tf_op jit(solution)/shard_map/pallas_call | solution.py:116
  59.0 2.2 collective-permute-start.11
  61.2 4.6 %shard_map.182 = (bf16[512,256]{1,0:T(8,128)(2,1)S(1)}, f32[4,1,256]{2,1,0:T(1,128)S(1)}) custom-call(s32[8]{0:T(128)S(1)} %get-tuple-element.214.page_req, s32[8]{0:T(128)S(1)} %get-tuple-element.213.page_slot, bf16[592,512]{1,0:T(8,128)(2,1)S(1)} %copy-done.1, bf16[592,512]{1,0:T(8,128)(2,1)S(1)} %collective-permute-done.refs_1_, ...), custom_call_target="tpu_custom_call" | custom-call | flops 536870912 | bytes 2686976 | tf_op jit(solution)/shard_map/pallas_call | solution.py:116
  66.7 2.1 collective-permute-start.12
  68.8 5.5 %collective-permute-done.13 = f32[2,2,4,64]{3,2,1,0:T(4,128)S(1)} collective-permute-done((f32[2,2,4,64]{3,2,1,0:T(4,128)S(1)}, f32[2,2,4,64]{3,2,1,0:T(4,128)S(1)}, u32[]{:S(2)}, u32[]{:S(2)}) %collective-permute-start.13) | collective-permute-done | bytes 4128 | tf_op jit(solution)/shard_map/ppermute | solution.py:444
  79.0 6.0 %collective-permute-done.15 = bf16[64,2048]{1,0:T(8,128)(2,1)S(1)} collective-permute-done((bf16[64,2048]{1,0:T(8,128)(2,1)S(1)}, bf16[64,2048]{1,0:T(8,128)(2,1)S(1)}, u32[]{:S(2)}, u32[]{:S(2)}) %collective-permute-start.15) | collective-permute-done | bytes 262176 | tf_op jit(solution)/shard_map/ppermute | solution.py:444
  86.1 2.9 %collective-permute-done.17 = f32[2,2,2,4,64]{4,3,2,1,0:T(4,128)S(1)} collective-permute-done((f32[2,2,2,4,64]{4,3,2,1,0:T(4,128)S(1)}, f32[2,2,2,4,64]{4,3,2,1,0:T(4,128)S(1)}, u32[]{:S(2)}, u32[]{:S(2)}) %collective-permute-start.17) | collective-permute-done | bytes 8224 | tf_op jit(solution)/shard_map/ppermute | solution.py:454
  89.0 2.5 %collective-permute-done.16 = bf16[64,2048]{1,0:T(8,128)(2,1)S(1)} collective-permute-done((bf16[64,2048]{1,0:T(8,128)(2,1)S(1)}, bf16[64,2048]{1,0:T(8,128)(2,1)S(1)}, u32[]{:S(2)}, u32[]{:S(2)}) %collective-permute-start.16) | collective-permute-done | bytes 262176 | tf_op jit(solution)/shard_map/ppermute | solution.py:444
  97.2 6.4 %collective-permute-done.21.refs_2_ = bf16[64,2048]{1,0:T(8,128)(2,1)S(1)} collective-permute-done((bf16[64,2048]{1,0:T(8,128)(2,1)S(1)}, bf16[64,2048]{1,0:T(8,128)(2,1)S(1)}, u32[]{:S(2)}, u32[]{:S(2)}) %collective-permute-start.21) | collective-permute-done | bytes 262176 | tf_op jit(solution)/shard_map/ppermute | solution.py:444
  105.6 2.0 collective-permute-start.22
  110.4 3.1 %collective-permute-done.20.refs_0_ = bf16[64,2048]{1,0:T(8,128)(2,1)S(1)} collective-permute-done((bf16[64,2048]{1,0:T(8,128)(2,1)S(1)}, bf16[64,2048]{1,0:T(8,128)(2,1)S(1)}, u32[]{:S(2)}, u32[]{:S(2)}) %collective-permute-start.20) | collective-permute-done | bytes 262176 | tf_op jit(solution)/shard_map/ppermute | solution.py:444
  114.1 2.3 %shard_map.189.refs_0_ = bf16[256,2048]{1,0:T(8,128)(2,1)} custom-call(bf16[64,2048]{1,0:T(8,128)(2,1)} %copy-done.13, bf16[64,2048]{1,0:T(8,128)(2,1)} %copy-done.14, bf16[64,2048]{1,0:T(8,128)(2,1)} %copy-done.11, bf16[64,2048]{1,0:T(8,128)(2,1)} %copy-done.4), custom_call_target="tpu_custom_call" | custom-call | bytes 2097152 | tf_op jit(solution)/shard_map/pallas_call | solution.py:214
  116.3 7.6 %shard_map.187 = bf16[256,2048]{1,0:T(8,128)(2,1)} custom-call(bf16[64,2048]{1,0:T(8,128)(2,1)} %copy-done.13, bf16[64,2048]{1,0:T(8,128)(2,1)} %copy-done.14, bf16[64,2048]{1,0:T(8,128)(2,1)} %copy-done.11, bf16[64,2048]{1,0:T(8,128)(2,1)} %copy-done.4, bf16[1,2048]{1,0:T(2,128)(2,1)} %reshape.550.refs_4_, bf16[704,2048]{1,0:T(8,128)(2,1)} %bitcast.106, ...), custom_call_target="tpu_custom_call" | custom-call | flops 2214592512 | bytes 10747904 | tf_op jit(solution)/shard_map/pallas_call | solution.py:265
  124.1 3.0 %collective-permute-done.28.refs_5_ = bf16[64,2048]{1,0:T(8,128)(2,1)} collective-permute-done((bf16[64,2048]{1,0:T(8,128)(2,1)S(1)}, bf16[64,2048]{1,0:T(8,128)(2,1)}, u32[]{:S(2)}, u32[]{:S(2)}) %collective-permute-start.28) | collective-permute-done | bytes 262176 | tf_op jit(solution)/shard_map/ppermute | solution.py:454
  127.0 2.9 %shard_map.188 = (bf16[256,2048]{1,0:T(8,128)(2,1)}, bf16[256,2048]{1,0:T(8,128)(2,1)}) custom-call(bf16[64,2048]{1,0:T(8,128)(2,1)} %copy-done.9, bf16[64,2048]{1,0:T(8,128)(2,1)} %copy-done.12, bf16[64,2048]{1,0:T(8,128)(2,1)} %copy-done.10, bf16[64,2048]{1,0:T(8,128)(2,1)} %copy-done.8, bf16[64,2048]{1,0:T(8,128)(2,1)} %collective-permute-done.26.refs_4_, ...), custom_call_target="tpu_custom_call" | custom-call | bytes 4194304 | tf_op jit(solution)/shard_map/pallas_call | solution.py:214
  133.8 15.2 %shard_map.190 = (bf16[256,2048]{1,0:T(8,128)(2,1)}, bf16[256,2048]{1,0:T(8,128)(2,1)}, bf16[256,2048]{1,0:T(8,128)(2,1)}, bf16[256,2048]{1,0:T(8,128)(2,1)}) custom-call(bf16[256,2048]{1,0:T(8,128)(2,1)} %shard_map.189.refs_0_, bf16[256,2048]{1,0:T(8,128)(2,1)} %get-tuple-element.159.refs_1_, bf16[256,2048]{1,0:T(8,128)(2,1)} %collective-permute-done.31.refs_2_, ...), custom_call_target="tpu_custom_call" | custom-call | flops 8254390272 | bytes 25690112 | tf_op jit(solution)/shard_map/pallas_call | solution.py:363
  149.7 7.6 %shard_map.191 = bf16[256,2048]{1,0:T(8,128)(2,1)} custom-call(bf16[64,2048]{1,0:T(8,128)(2,1)} %copy-done.9, bf16[64,2048]{1,0:T(8,128)(2,1)} %copy-done.12, bf16[64,2048]{1,0:T(8,128)(2,1)} %copy-done.10, bf16[64,2048]{1,0:T(8,128)(2,1)} %copy-done.8, bf16[1,2048]{1,0:T(2,128)(2,1)} %reshape.550.refs_4_, bf16[704,2048]{1,0:T(8,128)(2,1)} %bitcast.107, ...), custom_call_target="tpu_custom_call" | custom-call | flops 2214592512 | bytes 10747904 | tf_op jit(solution)/shard_map/pallas_call | solution.py:265
  161.4 15.2 %shard_map.192 = (bf16[64,2048]{1,0:T(8,128)(2,1)}, bf16[64,2048]{1,0:T(8,128)(2,1)}, bf16[64,2048]{1,0:T(8,128)(2,1)}, bf16[64,2048]{1,0:T(8,128)(2,1)}, bf16[6...) custom-call(bf16[256,2048]{1,0:T(8,128)(2,1)} %get-tuple-element.171, ...), custom_call_target="tpu_custom_call" | custom-call | flops 8254390272 | bytes 25690112 | tf_op jit(solution)/shard_map/pallas_call | solution.py:363
  176.6 3.3 %collective-permute-done.36 = bf16[192,2048]{1,0:T(8,128)(2,1)S(1)} collective-permute-done((bf16[192,2048]{1,0:T(8,128)(2,1)S(1)}, bf16[192,2048]{1,0:T(8,128)(2,1)S(1)}, u32[]{:S(2)}, u32[]{:S(2)}) %collective-permute-start.36) | collective-permute-done | bytes 786464 | tf_op jit(solution)/shard_map/ppermute | solution.py:444
  180.5 2.3 %collective-permute-done.39 = bf16[256,2048]{1,0:T(8,128)(2,1)S(1)} collective-permute-done((bf16[256,2048]{1,0:T(8,128)(2,1)}, bf16[256,2048]{1,0:T(8,128)(2,1)S(1)}, u32[]{:S(2)}, u32[]{:S(2)}) %collective-permute-start.39) | collective-permute-done | bytes 1048608 | tf_op jit(solution)/shard_map/ppermute | solution.py:454
  190.8 2.3 %collective-permute-done.44 = bf16[64,2048]{1,0:T(8,128)(2,1)S(1)} collective-permute-done((bf16[64,2048]{1,0:T(8,128)(2,1)S(1)}, bf16[64,2048]{1,0:T(8,128)(2,1)S(1)}, u32[]{:S(2)}, u32[]{:S(2)}) %collective-permute-start.44) | collective-permute-done | bytes 262176 | tf_op jit(solution)/shard_map/ppermute | solution.py:444
  193.8 4.9 %collective-permute-done.43 = bf16[64,2048]{1,0:T(8,128)(2,1)S(1)} collective-permute-done((bf16[64,2048]{1,0:T(8,128)(2,1)S(1)}, bf16[64,2048]{1,0:T(8,128)(2,1)S(1)}, u32[]{:S(2)}, u32[]{:S(2)}) %collective-permute-start.43) | collective-permute-done | bytes 262176 | tf_op jit(solution)/shard_map/ppermute | solution.py:444
  201.6 2.7 %collective-permute-done.42 = bf16[64,2048]{1,0:T(8,128)(2,1)S(1)} collective-permute-done((bf16[64,2048]{1,0:T(8,128)(2,1)S(1)}, bf16[64,2048]{1,0:T(8,128)(2,1)S(1)}, u32[]{:S(2)}, u32[]{:S(2)}) %collective-permute-start.42) | collective-permute-done | bytes 262176 | tf_op jit(solution)/shard_map/ppermute | solution.py:444
  205.0 4.9 %collective-permute-done.41 = bf16[64,2048]{1,0:T(8,128)(2,1)S(1)} collective-permute-done((bf16[64,2048]{1,0:T(8,128)(2,1)S(1)}, bf16[64,2048]{1,0:T(8,128)(2,1)S(1)}, u32[]{:S(2)}, u32[]{:S(2)}) %collective-permute-start.41) | collective-permute-done | bytes 262176 | tf_op jit(solution)/shard_map/ppermute | solution.py:444
  212.9 2.0 collective-permute-start.51
  214.9 1.9 collective-permute-done.46
  216.8 6.3 %collective-permute-done.50 = bf16[64,2048]{1,0:T(8,128)(2,1)S(1)} collective-permute-done((bf16[64,2048]{1,0:T(8,128)(2,1)S(1)}, bf16[64,2048]{1,0:T(8,128)(2,1)S(1)}, u32[]{:S(2)}, u32[]{:S(2)}) %collective-permute-start.50) | collective-permute-done | bytes 262176 | tf_op jit(solution)/shard_map/ppermute | solution.py:444
  (244 shorter events, 67.7 us)
Async XLA Ops:
  0.0 23.2 %collective-permute-start.3 = (bf16[64,2048]{1,0:T(8,128)(2,1)}, bf16[64,2048]{1,0:T(8,128)(2,1)}, u32[]{:S(2)}, u32[]{:S(2)}) collective-permute-start(bf16[64,2048]{1,0:T(8,128)(2,1)} %refs_2_.1), channel_id=1, source_target_pairs={{0,4},{1,5},{2,6},{3,7},{4,0},{5,1},{6,2},{7,3},{8,12},{9,13},{10,... | collective-permute-start | bytes 786440 | tf_op jit(solution)/shard_map/ppermute | solution.py:444
  8.8 37.7 %collective-permute-start = (bf16[592,512]{1,0:T(8,128)(2,1)}, bf16[592,512]{1,0:T(8,128)(2,1)S(1)}, u32[]{:S(2)}, u32[]{:S(2)}) collective-permute-start(bf16[592,512]{1,0:T(8,128)(2,1)} %get-tuple-element.110), channel_id=1, source_target_pairs={{0,1},{1,0},{2,3},{3,2},{4,5},{5,4},{6,7},{7,6},{8,9},{9,8},{10,11... | collective-permute-start | bytes 1818632 | tf_op jit(solution)/shard_map/ppermute | solution.py:444
  10.4 36.9 %collective-permute-start.1 = (bf16[592,512]{1,0:T(8,128)(2,1)}, bf16[592,512]{1,0:T(8,128)(2,1)S(1)}, u32[]{:S(2)}, u32[]{:S(2)}) collective-permute-start(bf16[592,512]{1,0:T(8,128)(2,1)} %get-tuple-element.111), channel_id=1, source_target_pairs={{0,2},{1,3},{2,0},{3,1},{4,6},{5,7},{6,4},{7,5},{8,10},{9,11},{10,... | collective-permute-start | bytes 1818632 | tf_op jit(solution)/shard_map/ppermute | solution.py:444
  12.0 37.0 %collective-permute-start.2 = (bf16[592,512]{1,0:T(8,128)(2,1)}, bf16[592,512]{1,0:T(8,128)(2,1)S(1)}, u32[]{:S(2)}, u32[]{:S(2)}) collective-permute-start(bf16[592,512]{1,0:T(8,128)(2,1)} %get-tuple-element.112), channel_id=1, source_target_pairs={{0,3},{1,2},{2,1},{3,0},{4,7},{5,6},{6,5},{7,4},{8,11},{9,10},{10,... | collective-permute-start | bytes 1818632 | tf_op jit(solution)/shard_map/ppermute | solution.py:444
  12.4 30.8 %collective-permute-start.7 = (bf16[64,2048]{1,0:T(8,128)(2,1)S(1)}, bf16[64,2048]{1,0:T(8,128)(2,1)S(1)}, u32[]{:S(2)}, u32[]{:S(2)}) collective-permute-start(bf16[64,2048]{1,0:T(8,128)(2,1)S(1)} %constant_dynamic-slice_fusion), channel_id=1, source_target_pairs={{0,4},{1,5},{2,6},{3,7},{4,0},{5,1},{6,2},{7,3},{8,12},{9,13},{10,... | collective-permute-start | bytes 786440 | tf_op jit(solution)/shard_map/ppermute | solution.py:444
  25.6 19.7 %collective-permute-start.4 = (bf16[64,512]{1,0:T(8,128)(2,1)}, bf16[64,512]{1,0:T(8,128)(2,1)S(1)}, u32[]{:S(2)}, u32[]{:S(2)}) collective-permute-start(bf16[64,512]{1,0:T(8,128)(2,1)} %get-tuple-element.121), channel_id=1, source_target_pairs={{0,1},{1,0},{2,3},{3,2},{4,5},{5,4},{6,7},{7,6},{8,9},{9,8},{10,11... | collective-permute-start | bytes 196616 | tf_op jit(solution)/shard_map/ppermute | solution.py:444
  43.2 15.2 %collective-permute-start.8 = (bf16[64,2048]{1,0:T(8,128)(2,1)S(1)}, bf16[64,2048]{1,0:T(8,128)(2,1)S(1)}, u32[]{:S(2)}, u32[]{:S(2)}) collective-permute-start(bf16[64,2048]{1,0:T(8,128)(2,1)S(1)} %collective-permute-done.7.refs_0_), channel_id=1, source_target_pairs={{0,16},{8,24},{16,0},{24,8},{1,17},{9,25},{17,1},{25,9},{2,18},{10... | collective-permute-start | bytes 786440 | tf_op jit(solution)/shard_map/ppermute | solution.py:458
  59.0 15.4 %collective-permute-start.11 = (bf16[512,256]{1,0:T(8,128)(2,1)S(1)}, bf16[512,256]{1,0:T(8,128)(2,1)S(1)}, u32[]{:S(2)}, u32[]{:S(2)}) collective-permute-start(bf16[512,256]{1,0:T(8,128)(2,1)S(1)} %get-tuple-element.131), channel_id=1, source_target_pairs={{0,4},{1,5},{2,6},{3,7},{4,0},{5,1},{6,2},{7,3},{8,12},{9,13},{10,... | collective-permute-start | bytes 786440 | tf_op jit(solution)/shard_map/ppermute | solution.py:444
  75.6 9.3 %collective-permute-start.15 = (bf16[64,2048]{1,0:T(8,128)(2,1)S(1)}, bf16[64,2048]{1,0:T(8,128)(2,1)S(1)}, u32[]{:S(2)}, u32[]{:S(2)}) collective-permute-start(bf16[64,2048]{1,0:T(8,128)(2,1)S(1)} %get-tuple-element.140), channel_id=1, source_target_pairs={{0,1},{1,0},{2,3},{3,2},{4,5},{5,4},{6,7},{7,6},{8,9},{9,8},{10,11... | collective-permute-start | bytes 786440 | tf_op jit(solution)/shard_map/ppermute | solution.py:444
  77.8 11.2 %collective-permute-start.14 = (bf16[64,2048]{1,0:T(8,128)(2,1)S(1)}, bf16[64,2048]{1,0:T(8,128)(2,1)S(1)}, u32[]{:S(2)}, u32[]{:S(2)}) collective-permute-start(bf16[64,2048]{1,0:T(8,128)(2,1)S(1)} %get-tuple-element.143), channel_id=1, source_target_pairs={{0,1},{1,0},{2,3},{3,2},{4,5},{5,4},{6,7},{7,6},{8,9},{9,8},{10,11... | collective-permute-start | bytes 786440 | tf_op jit(solution)/shard_map/ppermute | solution.py:444
  91.9 11.7 %collective-permute-start.21 = (bf16[64,2048]{1,0:T(8,128)(2,1)S(1)}, bf16[64,2048]{1,0:T(8,128)(2,1)S(1)}, u32[]{:S(2)}, u32[]{:S(2)}) collective-permute-start(bf16[64,2048]{1,0:T(8,128)(2,1)S(1)} %multiply_convert_fusion.refs_3_), channel_id=1, source_target_pairs={{0,4},{1,5},{2,6},{3,7},{4,0},{5,1},{6,2},{7,3},{8,12},{9,13},{10,... | collective-permute-start | bytes 786440 | tf_op jit(solution)/shard_map/ppermute | solution.py:444
  93.8 10.4 %collective-permute-start.19 = (bf16[64,2048]{1,0:T(8,128)(2,1)S(1)}, bf16[64,2048]{1,0:T(8,128)(2,1)S(1)}, u32[]{:S(2)}, u32[]{:S(2)}) collective-permute-start(bf16[64,2048]{1,0:T(8,128)(2,1)S(1)} %multiply_convert_fusion.refs_3_), channel_id=1, source_target_pairs={{0,2},{1,3},{2,0},{3,1},{4,6},{5,7},{6,4},{7,5},{8,10},{9,11},{10,... | collective-permute-start | bytes 786440 | tf_op jit(solution)/shard_map/ppermute | solution.py:444
  95.5 12.1 %collective-permute-start.18 = (bf16[64,2048]{1,0:T(8,128)(2,1)S(1)}, bf16[64,2048]{1,0:T(8,128)(2,1)S(1)}, u32[]{:S(2)}, u32[]{:S(2)}) collective-permute-start(bf16[64,2048]{1,0:T(8,128)(2,1)S(1)} %multiply_convert_fusion.refs_3_), channel_id=1, source_target_pairs={{0,1},{1,0},{2,3},{3,2},{4,5},{5,4},{6,7},{7,6},{8,9},{9,8},{10,11... | collective-permute-start | bytes 786440 | tf_op jit(solution)/shard_map/ppermute | solution.py:444
  96.5 11.6 %collective-permute-start.25 = (bf16[64,2048]{1,0:T(8,128)(2,1)S(1)}, bf16[64,2048]{1,0:T(8,128)(2,1)S(1)}, u32[]{:S(2)}, u32[]{:S(2)}) collective-permute-start(bf16[64,2048]{1,0:T(8,128)(2,1)S(1)} %multiply_convert_fusion.refs_3_), channel_id=1, source_target_pairs={{0,16},{8,24},{16,0},{24,8},{1,17},{9,25},{17,1},{25,9},{2,18},{10... | collective-permute-start | bytes 786440 | tf_op jit(solution)/shard_map/ppermute | solution.py:454
  105.6 18.4 %collective-permute-start.22 = (bf16[64,2048]{1,0:T(8,128)(2,1)S(1)}, bf16[64,2048]{1,0:T(8,128)(2,1)S(1)}, u32[]{:S(2)}, u32[]{:S(2)}) collective-permute-start(bf16[64,2048]{1,0:T(8,128)(2,1)S(1)} %collective-permute-done.21.refs_2_), channel_id=1, source_target_pairs={{0,1},{1,0},{2,3},{3,2},{4,5},{5,4},{6,7},{7,6},{8,9},{9,8},{10,11... | collective-permute-start | bytes 786440 | tf_op jit(solution)/shard_map/ppermute | solution.py:444
  107.6 16.4 %collective-permute-start.26 = (bf16[64,2048]{1,0:T(8,128)(2,1)S(1)}, bf16[64,2048]{1,0:T(8,128)(2,1)}, u32[]{:S(2)}, u32[]{:S(2)}) collective-permute-start(bf16[64,2048]{1,0:T(8,128)(2,1)S(1)} %collective-permute-done.19.refs_0_), channel_id=1, source_target_pairs={{0,16},{8,24},{16,0},{24,8},{1,17},{9,25},{17,1},{25,9},{2,18},{10... | collective-permute-start | bytes 786440 | tf_op jit(solution)/shard_map/ppermute | solution.py:454
  108.1 15.9 %collective-permute-start.27 = (bf16[64,2048]{1,0:T(8,128)(2,1)S(1)}, bf16[64,2048]{1,0:T(8,128)(2,1)}, u32[]{:S(2)}, u32[]{:S(2)}) collective-permute-start(bf16[64,2048]{1,0:T(8,128)(2,1)S(1)} %collective-permute-done.21.refs_2_), channel_id=1, source_target_pairs={{0,16},{8,24},{16,0},{24,8},{1,17},{9,25},{17,1},{25,9},{2,18},{10... | collective-permute-start | bytes 786440 | tf_op jit(solution)/shard_map/ppermute | solution.py:454
  110.4 13.7 %collective-permute-start.24 = (bf16[64,2048]{1,0:T(8,128)(2,1)S(1)}, bf16[64,2048]{1,0:T(8,128)(2,1)S(1)}, u32[]{:S(2)}, u32[]{:S(2)}) collective-permute-start(bf16[64,2048]{1,0:T(8,128)(2,1)S(1)} %collective-permute-done.23.refs_1_), channel_id=1, source_target_pairs={{0,1},{1,0},{2,3},{3,2},{4,5},{5,4},{6,7},{7,6},{8,9},{9,8},{10,11... | collective-permute-start | bytes 786440 | tf_op jit(solution)/shard_map/ppermute | solution.py:444
  113.4 13.6 %collective-permute-start.28 = (bf16[64,2048]{1,0:T(8,128)(2,1)S(1)}, bf16[64,2048]{1,0:T(8,128)(2,1)}, u32[]{:S(2)}, u32[]{:S(2)}) collective-permute-start(bf16[64,2048]{1,0:T(8,128)(2,1)S(1)} %collective-permute-done.23.refs_1_), channel_id=1, source_target_pairs={{0,16},{8,24},{16,0},{24,8},{1,17},{9,25},{17,1},{25,9},{2,18},{10... | collective-permute-start | bytes 786440 | tf_op jit(solution)/shard_map/ppermute | solution.py:454
  130.6 26.7 %collective-permute-start.30 = (bf16[256,2048]{1,0:T(8,128)(2,1)}, bf16[256,2048]{1,0:T(8,128)(2,1)}, u32[]{:S(2)}, u32[]{:S(2)}) collective-permute-start(bf16[256,2048]{1,0:T(8,128)(2,1)} %get-tuple-element.171.refs_0_), channel_id=1, source_target_pairs={{0,1},{1,0},{2,3},{3,2},{4,5},{5,4},{6,7},{7,6},{8,9},{9,8},{10,11... | collective-permute-start | bytes 3145736 | tf_op jit(solution)/shard_map/ppermute | solution.py:444
  149.1 9.4 %collective-permute-start.35 = (bf16[256,2048]{1,0:T(8,128)(2,1)}, bf16[256,2048]{1,0:T(8,128)(2,1)S(1)}, u32[]{:S(2)}, u32[]{:S(2)}) collective-permute-start(bf16[256,2048]{1,0:T(8,128)(2,1)} %get-tuple-element.170), channel_id=1, source_target_pairs={{0,8},{8,0},{16,24},{24,16},{1,9},{9,1},{17,25},{25,17},{2,10},{10... | collective-permute-start | bytes 3145736 | tf_op jit(solution)/shard_map/ppermute | solution.py:454
  149.3 12.1 %collective-permute-start.33 = (bf16[256,2048]{1,0:T(8,128)(2,1)S(1)}, bf16[256,2048]{1,0:T(8,128)(2,1)}, u32[]{:S(2)}, u32[]{:S(2)}) collective-permute-start(bf16[256,2048]{1,0:T(8,128)(2,1)S(1)} %copy-done.29), channel_id=1, source_target_pairs={{0,8},{8,0},{16,24},{24,16},{1,9},{9,1},{17,25},{25,17},{2,10},{10... | collective-permute-start | bytes 3145736 | tf_op jit(solution)/shard_map/ppermute | solution.py:454
  158.1 18.6 %collective-permute-start.37 = (bf16[256,2048]{1,0:T(8,128)(2,1)S(1)}, bf16[256,2048]{1,0:T(8,128)(2,1)S(1)}, u32[]{:S(2)}, u32[]{:S(2)}) collective-permute-start(bf16[256,2048]{1,0:T(8,128)(2,1)S(1)} %copy-done.30), channel_id=1, source_target_pairs={{0,8},{8,0},{16,24},{24,16},{1,9},{9,1},{17,25},{25,17},{2,10},{10... | collective-permute-start | bytes 3145736 | tf_op jit(solution)/shard_map/ppermute | solution.py:454
  160.3 19.7 %collective-permute-start.36 = (bf16[192,2048]{1,0:T(8,128)(2,1)S(1)}, bf16[192,2048]{1,0:T(8,128)(2,1)S(1)}, u32[]{:S(2)}, u32[]{:S(2)}) collective-permute-start(bf16[192,2048]{1,0:T(8,128)(2,1)S(1)} %slice.283), channel_id=1, source_target_pairs={{0,1},{1,0},{2,3},{3,2},{4,5},{5,4},{6,7},{7,6},{8,9},{9,8},{10,11... | collective-permute-start | bytes 2359304 | tf_op jit(solution)/shard_map/ppermute | solution.py:444
  185.4 13.3 %collective-permute-start.43 = (bf16[64,2048]{1,0:T(8,128)(2,1)S(1)}, bf16[64,2048]{1,0:T(8,128)(2,1)S(1)}, u32[]{:S(2)}, u32[]{:S(2)}) collective-permute-start(bf16[64,2048]{1,0:T(8,128)(2,1)S(1)} %add_convert_fusion.11), channel_id=1, source_target_pairs={{0,1},{1,0},{2,3},{3,2},{4,5},{5,4},{6,7},{7,6},{8,9},{9,8},{10,11... | collective-permute-start | bytes 786440 | tf_op jit(solution)/shard_map/ppermute | solution.py:444
  188.1 16.2 %collective-permute-start.42 = (bf16[64,2048]{1,0:T(8,128)(2,1)S(1)}, bf16[64,2048]{1,0:T(8,128)(2,1)S(1)}, u32[]{:S(2)}, u32[]{:S(2)}) collective-permute-start(bf16[64,2048]{1,0:T(8,128)(2,1)S(1)} %add_convert_fusion.10), channel_id=1, source_target_pairs={{0,1},{1,0},{2,3},{3,2},{4,5},{5,4},{6,7},{7,6},{8,9},{9,8},{10,11... | collective-permute-start | bytes 786440 | tf_op jit(solution)/shard_map/ppermute | solution.py:444
  188.7 21.3 %collective-permute-start.41 = (bf16[64,2048]{1,0:T(8,128)(2,1)S(1)}, bf16[64,2048]{1,0:T(8,128)(2,1)S(1)}, u32[]{:S(2)}, u32[]{:S(2)}) collective-permute-start(bf16[64,2048]{1,0:T(8,128)(2,1)S(1)} %add_convert_fusion.9), channel_id=1, source_target_pairs={{0,1},{1,0},{2,3},{3,2},{4,5},{5,4},{6,7},{7,6},{8,9},{9,8},{10,11... | collective-permute-start | bytes 786440 | tf_op jit(solution)/shard_map/ppermute | solution.py:444
  190.3 24.6 %collective-permute-start.40 = (bf16[64,2048]{1,0:T(8,128)(2,1)S(1)}, bf16[64,2048]{1,0:T(8,128)(2,1)S(1)}, u32[]{:S(2)}, u32[]{:S(2)}) collective-permute-start(bf16[64,2048]{1,0:T(8,128)(2,1)S(1)} %slice.284), channel_id=1, source_target_pairs={{0,1},{1,0},{2,3},{3,2},{4,5},{5,4},{6,7},{7,6},{8,9},{9,8},{10,11... | collective-permute-start | bytes 786440 | tf_op jit(solution)/shard_map/ppermute | solution.py:444
  198.8 11.8 %collective-permute-start.48 = (bf16[64,2048]{1,0:T(8,128)(2,1)S(1)}, bf16[64,2048]{1,0:T(8,128)(2,1)S(1)}, u32[]{:S(2)}, u32[]{:S(2)}) collective-permute-start(bf16[64,2048]{1,0:T(8,128)(2,1)S(1)} %add_convert_fusion.7), channel_id=1, source_target_pairs={{0,16},{8,24},{16,0},{24,8},{1,17},{9,25},{17,1},{25,9},{2,18},{10... | collective-permute-start | bytes 786440 | tf_op jit(solution)/shard_map/ppermute | solution.py:454
  200.2 10.5 %collective-permute-start.49 = (bf16[64,2048]{1,0:T(8,128)(2,1)S(1)}, bf16[64,2048]{1,0:T(8,128)(2,1)S(1)}, u32[]{:S(2)}, u32[]{:S(2)}) collective-permute-start(bf16[64,2048]{1,0:T(8,128)(2,1)S(1)} %add_convert_fusion.6), channel_id=1, source_target_pairs={{0,2},{1,3},{2,0},{3,1},{4,6},{5,7},{6,4},{7,5},{8,10},{9,11},{10,... | collective-permute-start | bytes 786440 | tf_op jit(solution)/shard_map/ppermute | solution.py:444
  211.4 11.8 %collective-permute-start.50 = (bf16[64,2048]{1,0:T(8,128)(2,1)S(1)}, bf16[64,2048]{1,0:T(8,128)(2,1)S(1)}, u32[]{:S(2)}, u32[]{:S(2)}) collective-permute-start(bf16[64,2048]{1,0:T(8,128)(2,1)S(1)} %add_convert_fusion.2), channel_id=1, source_target_pairs={{0,2},{1,3},{2,0},{3,1},{4,6},{5,7},{6,4},{7,5},{8,10},{9,11},{10,... | collective-permute-start | bytes 786440 | tf_op jit(solution)/shard_map/ppermute | solution.py:444
  212.9 10.3 %collective-permute-start.51 = (bf16[64,2048]{1,0:T(8,128)(2,1)S(1)}, bf16[64,2048]{1,0:T(8,128)(2,1)S(1)}, u32[]{:S(2)}, u32[]{:S(2)}) collective-permute-start(bf16[64,2048]{1,0:T(8,128)(2,1)S(1)} %add_convert_fusion.3), channel_id=1, source_target_pairs={{0,4},{1,5},{2,6},{3,7},{4,0},{5,1},{6,2},{7,3},{8,12},{9,13},{10,... | collective-permute-start | bytes 786440 | tf_op jit(solution)/shard_map/ppermute | solution.py:444
  (52 other events, 573.5 us)

commit v17 on v16

--- a/solution.py
+++ b/solution.py
@@ -579,8 +579,8 @@
 
     far_line = send(normed, 1, 0, 0)
     line = [normed, send(normed, 0, 1, 0), far_line, send(far_line, 0, 1, 0)]
+    over_y = {(i, dy): send_req(line[i], dy, 0) for i in order for dy in range(1, ny)}
     over_x = {(i, dx): send(line[i], 0, 0, dx) for i in order for dx in range(1, nx)}
-    over_y = {(i, dy): send_req(line[i], dy, 0) for i in order for dy in range(1, ny)}
 
     halves = [[line[i] for i in order]]
     shared_weights = (shared_scalar, shared_gate.T, shared_up.T, shared_down)
@@ -588,7 +588,7 @@
     chunks = {(0, 0): join(halves[0])}
     for dc in range(1, nc):
         chunks[0, dc] = [send_req(chunks[0, 0][0], 0, dc)]
-    over_x, over_y, shared, row_gate = tie((over_x, over_y, shared, row_gate))
+    over_y, over_x, shared, row_gate = tie((over_y, over_x, shared, row_gate))
     halves += [[over_x[i, dx] for i in order] for dx in range(1, nx)]
     joined = join(*halves[1:], *[[over_y[i, dy] for i in order] for dy in range(1, ny)])
     chunks[0, 0] += joined[: nx - 1]

time: 225 us -> 226 us (level)
  no operation moved by 1% of the time
where the time goes in v17:
time: 226 us; the launch traced here: 225 us
  waiting for transfers between devices  82.5 us (37%)
  Pallas kernels  68.6 us (30%)
  starting transfers between devices  46.8 us (21%)
  other arithmetic  16.2 us (7%)
  local copies, waits for them, and re-layouts  8.73 us (4%)
    ppermute x31, waiting for transfers between devices, send(): return lax.ppermute(value, 'exp', pairs)  69.5 us
    ppermute x31, starting transfers between devices, send(): return lax.ppermute(value, 'exp', pairs)  37.1 us
    pallas_call x2, Pallas kernels, routed_expert(): pl.pallas_call(functools.partial(routed_kernel, parts, len(more), entries...  30.5 us
    pallas_call x2, Pallas kernels, shared_expert(): pl.pallas_call(functools.partial(shared_kernel, len(pieces)), out_shape=j...  15.2 us
    ppermute x20, waiting for transfers between devices, send_req(): return lax.ppermute(value, 'req', pairs)  12.9 us
    pallas_call x2, Pallas kernels, attend(): pl.pallas_call(functools.partial(attend_kernel, members, tokens, tok_rows...  9.12 us
    ppermute x20, starting transfers between devices, send_req(): return lax.ppermute(value, 'req', pairs)  8.26 us
    pallas_call x2, Pallas kernels, pack(): pl.pallas_call(functools.partial(pack_kernel, members, len(parts), column...  6.32 us
  transfers between devices with their start and end apart: 52, of which 24 were waited for; matrix products, arithmetic and copies ran while one was open for 9% of the time, Pallas kernels for 30%

profile of v17, /device:TPU:0, one launch (start us, length us, event | category | flops | bytes accessed | tf_op | source)
XLA Modules:
  0.0 224.8 jit_solution(3102011368907240483)
XLA Ops:
  0.0 4.1 %collective-permute-start.3 = (bf16[64,2048]{1,0:T(8,128)(2,1)}, bf16[64,2048]{1,0:T(8,128)(2,1)}, u32[]{:S(2)}, u32[]{:S(2)}) collective-permute-start(bf16[64,2048]{1,0:T(8,128)(2,1)} %refs_2_.1), channel_id=1, source_target_pairs={{0,4},{1,5},{2,6},{3,7},{4,0},{5,1},{6,2},{7,3},{8,12},{9,13},{10,... | collective-permute-start | bytes 786440 | tf_op jit(solution)/shard_map/ppermute | solution.py:444
  4.8 4.0 %shard_map.181 = (bf16[592,512]{1,0:T(8,128)(2,1)}, bf16[592,512]{1,0:T(8,128)(2,1)}, bf16[592,512]{1,0:T(8,128)(2,1)}, bf16[592,512]{1,0:T(8,128)(2,1)}) custom-call(s32[8]{0:T(128)} %stack.175.order, bf16[256,2048]{1,0:T(8,128)(2,1)} %bitcast.111, bf16[256,2048]{1,0:T(8,128)(2,1)} %bitcast.112, bf16[64,2048]{1,0:T(8,128)(2,1)} %refs_2_.1, f32[4,64]{1,0:T(4,128)} %bitcast.125), custom_call_target="tpu_custom_call" | custom-call | bytes 4849664 | tf_op jit(solution)/shard_map/pallas_call | solution.py:58
  23.4 2.3 %shard_map.183 = (bf16[64,512]{1,0:T(8,128)(2,1)}, bf16[64,512]{1,0:T(8,128)(2,1)}, bf16[64,512]{1,0:T(8,128)(2,1)}, bf16[64,512]{1,0:T(8,128)(2,1)}) custom-call(s32[8]{0:T(128)} %stack.175.order, bf16[64,2048]{1,0:T(8,128)(2,1)} %collective-permute-done.3.refs_0_), custom_call_target="tpu_custom_call" | custom-call | bytes 524288 | tf_op jit(solution)/shard_map/pallas_call | solution.py:58
  27.4 15.8 %collective-permute-done.7.refs_0_ = bf16[64,2048]{1,0:T(8,128)(2,1)S(1)} collective-permute-done((bf16[64,2048]{1,0:T(8,128)(2,1)S(1)}, bf16[64,2048]{1,0:T(8,128)(2,1)S(1)}, u32[]{:S(2)}, u32[]{:S(2)}) %collective-permute-start.7) | collective-permute-done | bytes 262176 | tf_op jit(solution)/shard_map/ppermute | solution.py:444
  50.0 2.0 collective-permute-done.6.refs_7_
  53.9 4.5 %shard_map.184 = (bf16[512,256]{1,0:T(8,128)(2,1)S(1)}, f32[4,1,256]{2,1,0:T(1,128)S(1)}) custom-call(s32[8]{0:T(128)S(1)} %get-tuple-element.214.page_req, s32[8]{0:T(128)S(1)} %get-tuple-element.213.page_slot, bf16[592,512]{1,0:T(8,128)(2,1)S(1)} %copy-done.1, bf16[592,512]{1,0:T(8,128)(2,1)S(1)} %collective-permute-done.refs_1_, ...), custom_call_target="tpu_custom_call" | custom-call | flops 536870912 | bytes 2686976 | tf_op jit(solution)/shard_map/pallas_call | solution.py:116
  59.0 2.2 collective-permute-start.11
  61.2 4.6 %shard_map.182 = (bf16[512,256]{1,0:T(8,128)(2,1)S(1)}, f32[4,1,256]{2,1,0:T(1,128)S(1)}) custom-call(s32[8]{0:T(128)S(1)} %get-tuple-element.214.page_req, s32[8]{0:T(128)S(1)} %get-tuple-element.213.page_slot, bf16[592,512]{1,0:T(8,128)(2,1)S(1)} %copy-done.1, bf16[592,512]{1,0:T(8,128)(2,1)S(1)} %collective-permute-done.refs_1_, ...), custom_call_target="tpu_custom_call" | custom-call | flops 536870912 | bytes 2686976 | tf_op jit(solution)/shard_map/pallas_call | solution.py:116
  66.7 2.1 collective-permute-start.12
  68.8 5.5 %collective-permute-done.13 = f32[2,2,4,64]{3,2,1,0:T(4,128)S(1)} collective-permute-done((f32[2,2,4,64]{3,2,1,0:T(4,128)S(1)}, f32[2,2,4,64]{3,2,1,0:T(4,128)S(1)}, u32[]{:S(2)}, u32[]{:S(2)}) %collective-permute-start.13) | collective-permute-done | bytes 4128 | tf_op jit(solution)/shard_map/ppermute | solution.py:444
  79.0 6.0 %collective-permute-done.15 = bf16[64,2048]{1,0:T(8,128)(2,1)S(1)} collective-permute-done((bf16[64,2048]{1,0:T(8,128)(2,1)S(1)}, bf16[64,2048]{1,0:T(8,128)(2,1)S(1)}, u32[]{:S(2)}, u32[]{:S(2)}) %collective-permute-start.15) | collective-permute-done | bytes 262176 | tf_op jit(solution)/shard_map/ppermute | solution.py:444
  86.1 2.9 %collective-permute-done.17 = f32[2,2,2,4,64]{4,3,2,1,0:T(4,128)S(1)} collective-permute-done((f32[2,2,2,4,64]{4,3,2,1,0:T(4,128)S(1)}, f32[2,2,2,4,64]{4,3,2,1,0:T(4,128)S(1)}, u32[]{:S(2)}, u32[]{:S(2)}) %collective-permute-start.17) | collective-permute-done | bytes 8224 | tf_op jit(solution)/shard_map/ppermute | solution.py:454
  89.0 2.5 %collective-permute-done.16 = bf16[64,2048]{1,0:T(8,128)(2,1)S(1)} collective-permute-done((bf16[64,2048]{1,0:T(8,128)(2,1)S(1)}, bf16[64,2048]{1,0:T(8,128)(2,1)S(1)}, u32[]{:S(2)}, u32[]{:S(2)}) %collective-permute-start.16) | collective-permute-done | bytes 262176 | tf_op jit(solution)/shard_map/ppermute | solution.py:444
  97.2 6.4 %collective-permute-done.21.refs_2_ = bf16[64,2048]{1,0:T(8,128)(2,1)S(1)} collective-permute-done((bf16[64,2048]{1,0:T(8,128)(2,1)S(1)}, bf16[64,2048]{1,0:T(8,128)(2,1)S(1)}, u32[]{:S(2)}, u32[]{:S(2)}) %collective-permute-start.21) | collective-permute-done | bytes 262176 | tf_op jit(solution)/shard_map/ppermute | solution.py:444
  107.7 2.0 collective-permute-start.27
  110.7 2.8 %collective-permute-done.20.refs_4_ = bf16[64,2048]{1,0:T(8,128)(2,1)S(1)} collective-permute-done((bf16[64,2048]{1,0:T(8,128)(2,1)S(1)}, bf16[64,2048]{1,0:T(8,128)(2,1)S(1)}, u32[]{:S(2)}, u32[]{:S(2)}) %collective-permute-start.20) | collective-permute-done | bytes 262176 | tf_op jit(solution)/shard_map/ppermute | solution.py:454
  113.6 2.3 %shard_map.189.refs_0_ = bf16[256,2048]{1,0:T(8,128)(2,1)} custom-call(bf16[64,2048]{1,0:T(8,128)(2,1)} %copy-done.12, bf16[64,2048]{1,0:T(8,128)(2,1)} %copy-done.13, bf16[64,2048]{1,0:T(8,128)(2,1)} %copy-done.11, bf16[64,2048]{1,0:T(8,128)(2,1)} %copy-done.4), custom_call_target="tpu_custom_call" | custom-call | bytes 2097152 | tf_op jit(solution)/shard_map/pallas_call | solution.py:214
  115.9 7.6 %shard_map.187 = bf16[256,2048]{1,0:T(8,128)(2,1)} custom-call(bf16[64,2048]{1,0:T(8,128)(2,1)} %copy-done.12, bf16[64,2048]{1,0:T(8,128)(2,1)} %copy-done.13, bf16[64,2048]{1,0:T(8,128)(2,1)} %copy-done.11, bf16[64,2048]{1,0:T(8,128)(2,1)} %copy-done.4, bf16[1,2048]{1,0:T(2,128)(2,1)} %reshape.550.refs_4_, bf16[704,2048]{1,0:T(8,128)(2,1)} %bitcast.106, ...), custom_call_target="tpu_custom_call" | custom-call | flops 2214592512 | bytes 10747904 | tf_op jit(solution)/shard_map/pallas_call | solution.py:265
  123.7 3.3 %collective-permute-done.28.refs_1_ = bf16[64,2048]{1,0:T(8,128)(2,1)S(1)} collective-permute-done((bf16[64,2048]{1,0:T(8,128)(2,1)S(1)}, bf16[64,2048]{1,0:T(8,128)(2,1)S(1)}, u32[]{:S(2)}, u32[]{:S(2)}) %collective-permute-start.28) | collective-permute-done | bytes 262176 | tf_op jit(solution)/shard_map/ppermute | solution.py:444
  127.7 2.9 %shard_map.188 = (bf16[256,2048]{1,0:T(8,128)(2,1)}, bf16[256,2048]{1,0:T(8,128)(2,1)}) custom-call(bf16[64,2048]{1,0:T(8,128)(2,1)} %copy-done.9, bf16[64,2048]{1,0:T(8,128)(2,1)} %copy-done.14, bf16[64,2048]{1,0:T(8,128)(2,1)} %copy-done.10, bf16[64,2048]{1,0:T(8,128)(2,1)} %copy-done.8, bf16[64,2048]{1,0:T(8,128)(2,1)} %copy-done.22, ...), custom_call_target="tpu_custom_call" | custom-call | bytes 4194304 | tf_op jit(solution)/shard_map/pallas_call | solution.py:214
  134.4 15.2 %shard_map.190 = (bf16[256,2048]{1,0:T(8,128)(2,1)}, bf16[256,2048]{1,0:T(8,128)(2,1)}, bf16[256,2048]{1,0:T(8,128)(2,1)}, bf16[256,2048]{1,0:T(8,128)(2,1)}) custom-call(bf16[256,2048]{1,0:T(8,128)(2,1)} %shard_map.189.refs_0_, bf16[256,2048]{1,0:T(8,128)(2,1)} %get-tuple-element.159.refs_1_, bf16[256,2048]{1,0:T(8,128)(2,1)} %collective-permute-done.31.refs_2_, ...), custom_call_target="tpu_custom_call" | custom-call | flops 8254390272 | bytes 25690112 | tf_op jit(solution)/shard_map/pallas_call | solution.py:363
  150.3 7.6 %shard_map.191 = bf16[256,2048]{1,0:T(8,128)(2,1)} custom-call(bf16[64,2048]{1,0:T(8,128)(2,1)} %copy-done.9, bf16[64,2048]{1,0:T(8,128)(2,1)} %copy-done.14, bf16[64,2048]{1,0:T(8,128)(2,1)} %copy-done.10, bf16[64,2048]{1,0:T(8,128)(2,1)} %copy-done.8, bf16[1,2048]{1,0:T(2,128)(2,1)} %reshape.550.refs_4_, bf16[704,2048]{1,0:T(8,128)(2,1)} %bitcast.107, ...), custom_call_target="tpu_custom_call" | custom-call | flops 2214592512 | bytes 10747904 | tf_op jit(solution)/shard_map/pallas_call | solution.py:265
  161.9 15.2 %shard_map.192 = (bf16[64,2048]{1,0:T(8,128)(2,1)}, bf16[64,2048]{1,0:T(8,128)(2,1)}, bf16[64,2048]{1,0:T(8,128)(2,1)}, bf16[64,2048]{1,0:T(8,128)(2,1)}, bf16[6...) custom-call(bf16[256,2048]{1,0:T(8,128)(2,1)} %get-tuple-element.171, ...), custom_call_target="tpu_custom_call" | custom-call | flops 8254390272 | bytes 25690112 | tf_op jit(solution)/shard_map/pallas_call | solution.py:363
  177.2 3.4 %collective-permute-done.36 = bf16[192,2048]{1,0:T(8,128)(2,1)S(1)} collective-permute-done((bf16[192,2048]{1,0:T(8,128)(2,1)S(1)}, bf16[192,2048]{1,0:T(8,128)(2,1)S(1)}, u32[]{:S(2)}, u32[]{:S(2)}) %collective-permute-start.36) | collective-permute-done | bytes 786464 | tf_op jit(solution)/shard_map/ppermute | solution.py:444
  181.1 2.3 %collective-permute-done.39 = bf16[256,2048]{1,0:T(8,128)(2,1)S(1)} collective-permute-done((bf16[256,2048]{1,0:T(8,128)(2,1)}, bf16[256,2048]{1,0:T(8,128)(2,1)S(1)}, u32[]{:S(2)}, u32[]{:S(2)}) %collective-permute-start.39) | collective-permute-done | bytes 1048608 | tf_op jit(solution)/shard_map/ppermute | solution.py:454
  191.4 2.3 %collective-permute-done.44 = bf16[64,2048]{1,0:T(8,128)(2,1)S(1)} collective-permute-done((bf16[64,2048]{1,0:T(8,128)(2,1)S(1)}, bf16[64,2048]{1,0:T(8,128)(2,1)S(1)}, u32[]{:S(2)}, u32[]{:S(2)}) %collective-permute-start.44) | collective-permute-done | bytes 262176 | tf_op jit(solution)/shard_map/ppermute | solution.py:444
  194.4 4.9 %collective-permute-done.43 = bf16[64,2048]{1,0:T(8,128)(2,1)S(1)} collective-permute-done((bf16[64,2048]{1,0:T(8,128)(2,1)S(1)}, bf16[64,2048]{1,0:T(8,128)(2,1)S(1)}, u32[]{:S(2)}, u32[]{:S(2)}) %collective-permute-start.43) | collective-permute-done | bytes 262176 | tf_op jit(solution)/shard_map/ppermute | solution.py:444
  202.2 2.7 %collective-permute-done.42 = bf16[64,2048]{1,0:T(8,128)(2,1)S(1)} collective-permute-done((bf16[64,2048]{1,0:T(8,128)(2,1)S(1)}, bf16[64,2048]{1,0:T(8,128)(2,1)S(1)}, u32[]{:S(2)}, u32[]{:S(2)}) %collective-permute-start.42) | collective-permute-done | bytes 262176 | tf_op jit(solution)/shard_map/ppermute | solution.py:444
  205.6 4.9 %collective-permute-done.41 = bf16[64,2048]{1,0:T(8,128)(2,1)S(1)} collective-permute-done((bf16[64,2048]{1,0:T(8,128)(2,1)S(1)}, bf16[64,2048]{1,0:T(8,128)(2,1)S(1)}, u32[]{:S(2)}, u32[]{:S(2)}) %collective-permute-start.41) | collective-permute-done | bytes 262176 | tf_op jit(solution)/shard_map/ppermute | solution.py:444
  213.5 2.1 collective-permute-start.51
  215.5 1.9 collective-permute-done.46
  217.5 6.3 %collective-permute-done.50 = bf16[64,2048]{1,0:T(8,128)(2,1)S(1)} collective-permute-done((bf16[64,2048]{1,0:T(8,128)(2,1)S(1)}, bf16[64,2048]{1,0:T(8,128)(2,1)S(1)}, u32[]{:S(2)}, u32[]{:S(2)}) %collective-permute-start.50) | collective-permute-done | bytes 262176 | tf_op jit(solution)/shard_map/ppermute | solution.py:444
  (246 shorter events, 68.2 us)
Async XLA Ops:
  0.0 23.3 %collective-permute-start.3 = (bf16[64,2048]{1,0:T(8,128)(2,1)}, bf16[64,2048]{1,0:T(8,128)(2,1)}, u32[]{:S(2)}, u32[]{:S(2)}) collective-permute-start(bf16[64,2048]{1,0:T(8,128)(2,1)} %refs_2_.1), channel_id=1, source_target_pairs={{0,4},{1,5},{2,6},{3,7},{4,0},{5,1},{6,2},{7,3},{8,12},{9,13},{10,... | collective-permute-start | bytes 786440 | tf_op jit(solution)/shard_map/ppermute | solution.py:444
  8.8 37.7 %collective-permute-start = (bf16[592,512]{1,0:T(8,128)(2,1)}, bf16[592,512]{1,0:T(8,128)(2,1)S(1)}, u32[]{:S(2)}, u32[]{:S(2)}) collective-permute-start(bf16[592,512]{1,0:T(8,128)(2,1)} %get-tuple-element.110), channel_id=1, source_target_pairs={{0,1},{1,0},{2,3},{3,2},{4,5},{5,4},{6,7},{7,6},{8,9},{9,8},{10,11... | collective-permute-start | bytes 1818632 | tf_op jit(solution)/shard_map/ppermute | solution.py:444
  10.4 36.9 %collective-permute-start.1 = (bf16[592,512]{1,0:T(8,128)(2,1)}, bf16[592,512]{1,0:T(8,128)(2,1)S(1)}, u32[]{:S(2)}, u32[]{:S(2)}) collective-permute-start(bf16[592,512]{1,0:T(8,128)(2,1)} %get-tuple-element.111), channel_id=1, source_target_pairs={{0,2},{1,3},{2,0},{3,1},{4,6},{5,7},{6,4},{7,5},{8,10},{9,11},{10,... | collective-permute-start | bytes 1818632 | tf_op jit(solution)/shard_map/ppermute | solution.py:444
  12.0 37.0 %collective-permute-start.2 = (bf16[592,512]{1,0:T(8,128)(2,1)}, bf16[592,512]{1,0:T(8,128)(2,1)S(1)}, u32[]{:S(2)}, u32[]{:S(2)}) collective-permute-start(bf16[592,512]{1,0:T(8,128)(2,1)} %get-tuple-element.112), channel_id=1, source_target_pairs={{0,3},{1,2},{2,1},{3,0},{4,7},{5,6},{6,5},{7,4},{8,11},{9,10},{10,... | collective-permute-start | bytes 1818632 | tf_op jit(solution)/shard_map/ppermute | solution.py:444
  12.4 30.8 %collective-permute-start.7 = (bf16[64,2048]{1,0:T(8,128)(2,1)S(1)}, bf16[64,2048]{1,0:T(8,128)(2,1)S(1)}, u32[]{:S(2)}, u32[]{:S(2)}) collective-permute-start(bf16[64,2048]{1,0:T(8,128)(2,1)S(1)} %constant_dynamic-slice_fusion), channel_id=1, source_target_pairs={{0,4},{1,5},{2,6},{3,7},{4,0},{5,1},{6,2},{7,3},{8,12},{9,13},{10,... | collective-permute-start | bytes 786440 | tf_op jit(solution)/shard_map/ppermute | solution.py:444
  25.6 19.6 %collective-permute-start.4 = (bf16[64,512]{1,0:T(8,128)(2,1)}, bf16[64,512]{1,0:T(8,128)(2,1)S(1)}, u32[]{:S(2)}, u32[]{:S(2)}) collective-permute-start(bf16[64,512]{1,0:T(8,128)(2,1)} %get-tuple-element.121), channel_id=1, source_target_pairs={{0,1},{1,0},{2,3},{3,2},{4,5},{5,4},{6,7},{7,6},{8,9},{9,8},{10,11... | collective-permute-start | bytes 196616 | tf_op jit(solution)/shard_map/ppermute | solution.py:444
  43.2 15.2 %collective-permute-start.8 = (bf16[64,2048]{1,0:T(8,128)(2,1)S(1)}, bf16[64,2048]{1,0:T(8,128)(2,1)S(1)}, u32[]{:S(2)}, u32[]{:S(2)}) collective-permute-start(bf16[64,2048]{1,0:T(8,128)(2,1)S(1)} %collective-permute-done.7.refs_0_), channel_id=1, source_target_pairs={{0,16},{8,24},{16,0},{24,8},{1,17},{9,25},{17,1},{25,9},{2,18},{10... | collective-permute-start | bytes 786440 | tf_op jit(solution)/shard_map/ppermute | solution.py:458
  59.0 15.4 %collective-permute-start.11 = (bf16[512,256]{1,0:T(8,128)(2,1)S(1)}, bf16[512,256]{1,0:T(8,128)(2,1)S(1)}, u32[]{:S(2)}, u32[]{:S(2)}) collective-permute-start(bf16[512,256]{1,0:T(8,128)(2,1)S(1)} %get-tuple-element.131), channel_id=1, source_target_pairs={{0,4},{1,5},{2,6},{3,7},{4,0},{5,1},{6,2},{7,3},{8,12},{9,13},{10,... | collective-permute-start | bytes 786440 | tf_op jit(solution)/shard_map/ppermute | solution.py:444
  75.6 9.3 %collective-permute-start.15 = (bf16[64,2048]{1,0:T(8,128)(2,1)S(1)}, bf16[64,2048]{1,0:T(8,128)(2,1)S(1)}, u32[]{:S(2)}, u32[]{:S(2)}) collective-permute-start(bf16[64,2048]{1,0:T(8,128)(2,1)S(1)} %get-tuple-element.140), channel_id=1, source_target_pairs={{0,1},{1,0},{2,3},{3,2},{4,5},{5,4},{6,7},{7,6},{8,9},{9,8},{10,11... | collective-permute-start | bytes 786440 | tf_op jit(solution)/shard_map/ppermute | solution.py:444
  77.8 11.2 %collective-permute-start.14 = (bf16[64,2048]{1,0:T(8,128)(2,1)S(1)}, bf16[64,2048]{1,0:T(8,128)(2,1)S(1)}, u32[]{:S(2)}, u32[]{:S(2)}) collective-permute-start(bf16[64,2048]{1,0:T(8,128)(2,1)S(1)} %get-tuple-element.143), channel_id=1, source_target_pairs={{0,1},{1,0},{2,3},{3,2},{4,5},{5,4},{6,7},{7,6},{8,9},{9,8},{10,11... | collective-permute-start | bytes 786440 | tf_op jit(solution)/shard_map/ppermute | solution.py:444
  91.9 11.7 %collective-permute-start.21 = (bf16[64,2048]{1,0:T(8,128)(2,1)S(1)}, bf16[64,2048]{1,0:T(8,128)(2,1)S(1)}, u32[]{:S(2)}, u32[]{:S(2)}) collective-permute-start(bf16[64,2048]{1,0:T(8,128)(2,1)S(1)} %multiply_convert_fusion.refs_3_), channel_id=1, source_target_pairs={{0,4},{1,5},{2,6},{3,7},{4,0},{5,1},{6,2},{7,3},{8,12},{9,13},{10,... | collective-permute-start | bytes 786440 | tf_op jit(solution)/shard_map/ppermute | solution.py:444
  93.8 10.4 %collective-permute-start.19 = (bf16[64,2048]{1,0:T(8,128)(2,1)S(1)}, bf16[64,2048]{1,0:T(8,128)(2,1)S(1)}, u32[]{:S(2)}, u32[]{:S(2)}) collective-permute-start(bf16[64,2048]{1,0:T(8,128)(2,1)S(1)} %multiply_convert_fusion.refs_3_), channel_id=1, source_target_pairs={{0,2},{1,3},{2,0},{3,1},{4,6},{5,7},{6,4},{7,5},{8,10},{9,11},{10,... | collective-permute-start | bytes 786440 | tf_op jit(solution)/shard_map/ppermute | solution.py:444
  95.5 12.1 %collective-permute-start.18 = (bf16[64,2048]{1,0:T(8,128)(2,1)S(1)}, bf16[64,2048]{1,0:T(8,128)(2,1)S(1)}, u32[]{:S(2)}, u32[]{:S(2)}) collective-permute-start(bf16[64,2048]{1,0:T(8,128)(2,1)S(1)} %multiply_convert_fusion.refs_3_), channel_id=1, source_target_pairs={{0,16},{8,24},{16,0},{24,8},{1,17},{9,25},{17,1},{25,9},{2,18},{10... | collective-permute-start | bytes 786440 | tf_op jit(solution)/shard_map/ppermute | solution.py:454
  96.0 11.6 %collective-permute-start.25 = (bf16[64,2048]{1,0:T(8,128)(2,1)S(1)}, bf16[64,2048]{1,0:T(8,128)(2,1)S(1)}, u32[]{:S(2)}, u32[]{:S(2)}) collective-permute-start(bf16[64,2048]{1,0:T(8,128)(2,1)S(1)} %multiply_convert_fusion.refs_3_), channel_id=1, source_target_pairs={{0,1},{1,0},{2,3},{3,2},{4,5},{5,4},{6,7},{7,6},{8,9},{9,8},{10,11... | collective-permute-start | bytes 786440 | tf_op jit(solution)/shard_map/ppermute | solution.py:444
  106.0 17.5 %collective-permute-start.22 = (bf16[64,2048]{1,0:T(8,128)(2,1)S(1)}, bf16[64,2048]{1,0:T(8,128)(2,1)}, u32[]{:S(2)}, u32[]{:S(2)}) collective-permute-start(bf16[64,2048]{1,0:T(8,128)(2,1)S(1)} %collective-permute-done.21.refs_2_), channel_id=1, source_target_pairs={{0,16},{8,24},{16,0},{24,8},{1,17},{9,25},{17,1},{25,9},{2,18},{10... | collective-permute-start | bytes 786440 | tf_op jit(solution)/shard_map/ppermute | solution.py:454
  107.6 16.0 %collective-permute-start.26 = (bf16[64,2048]{1,0:T(8,128)(2,1)S(1)}, bf16[64,2048]{1,0:T(8,128)(2,1)S(1)}, u32[]{:S(2)}, u32[]{:S(2)}) collective-permute-start(bf16[64,2048]{1,0:T(8,128)(2,1)S(1)} %collective-permute-done.19.refs_0_), channel_id=1, source_target_pairs={{0,1},{1,0},{2,3},{3,2},{4,5},{5,4},{6,7},{7,6},{8,9},{9,8},{10,11... | collective-permute-start | bytes 786440 | tf_op jit(solution)/shard_map/ppermute | solution.py:444
  107.7 16.0 %collective-permute-start.27 = (bf16[64,2048]{1,0:T(8,128)(2,1)S(1)}, bf16[64,2048]{1,0:T(8,128)(2,1)S(1)}, u32[]{:S(2)}, u32[]{:S(2)}) collective-permute-start(bf16[64,2048]{1,0:T(8,128)(2,1)S(1)} %collective-permute-done.21.refs_2_), channel_id=1, source_target_pairs={{0,1},{1,0},{2,3},{3,2},{4,5},{5,4},{6,7},{7,6},{8,9},{9,8},{10,11... | collective-permute-start | bytes 786440 | tf_op jit(solution)/shard_map/ppermute | solution.py:444
  110.4 13.2 %collective-permute-start.24 = (bf16[64,2048]{1,0:T(8,128)(2,1)S(1)}, bf16[64,2048]{1,0:T(8,128)(2,1)}, u32[]{:S(2)}, u32[]{:S(2)}) collective-permute-start(bf16[64,2048]{1,0:T(8,128)(2,1)S(1)} %collective-permute-done.23.refs_1_), channel_id=1, source_target_pairs={{0,16},{8,24},{16,0},{24,8},{1,17},{9,25},{17,1},{25,9},{2,18},{10... | collective-permute-start | bytes 786440 | tf_op jit(solution)/shard_map/ppermute | solution.py:454
  113.5 13.5 %collective-permute-start.28 = (bf16[64,2048]{1,0:T(8,128)(2,1)S(1)}, bf16[64,2048]{1,0:T(8,128)(2,1)S(1)}, u32[]{:S(2)}, u32[]{:S(2)}) collective-permute-start(bf16[64,2048]{1,0:T(8,128)(2,1)S(1)} %collective-permute-done.23.refs_1_), channel_id=1, source_target_pairs={{0,1},{1,0},{2,3},{3,2},{4,5},{5,4},{6,7},{7,6},{8,9},{9,8},{10,11... | collective-permute-start | bytes 786440 | tf_op jit(solution)/shard_map/ppermute | solution.py:444
  131.2 26.7 %collective-permute-start.30 = (bf16[256,2048]{1,0:T(8,128)(2,1)}, bf16[256,2048]{1,0:T(8,128)(2,1)}, u32[]{:S(2)}, u32[]{:S(2)}) collective-permute-start(bf16[256,2048]{1,0:T(8,128)(2,1)} %get-tuple-element.171.refs_0_), channel_id=1, source_target_pairs={{0,1},{1,0},{2,3},{3,2},{4,5},{5,4},{6,7},{7,6},{8,9},{9,8},{10,11... | collective-permute-start | bytes 3145736 | tf_op jit(solution)/shard_map/ppermute | solution.py:444
  149.7 9.4 %collective-permute-start.35 = (bf16[256,2048]{1,0:T(8,128)(2,1)}, bf16[256,2048]{1,0:T(8,128)(2,1)S(1)}, u32[]{:S(2)}, u32[]{:S(2)}) collective-permute-start(bf16[256,2048]{1,0:T(8,128)(2,1)} %get-tuple-element.170), channel_id=1, source_target_pairs={{0,8},{8,0},{16,24},{24,16},{1,9},{9,1},{17,25},{25,17},{2,10},{10... | collective-permute-start | bytes 3145736 | tf_op jit(solution)/shard_map/ppermute | solution.py:454
  149.9 12.1 %collective-permute-start.33 = (bf16[256,2048]{1,0:T(8,128)(2,1)S(1)}, bf16[256,2048]{1,0:T(8,128)(2,1)}, u32[]{:S(2)}, u32[]{:S(2)}) collective-permute-start(bf16[256,2048]{1,0:T(8,128)(2,1)S(1)} %copy-done.30), channel_id=1, source_target_pairs={{0,8},{8,0},{16,24},{24,16},{1,9},{9,1},{17,25},{25,17},{2,10},{10... | collective-permute-start | bytes 3145736 | tf_op jit(solution)/shard_map/ppermute | solution.py:454
  158.7 18.5 %collective-permute-start.37 = (bf16[256,2048]{1,0:T(8,128)(2,1)S(1)}, bf16[256,2048]{1,0:T(8,128)(2,1)S(1)}, u32[]{:S(2)}, u32[]{:S(2)}) collective-permute-start(bf16[256,2048]{1,0:T(8,128)(2,1)S(1)} %copy-done.31), channel_id=1, source_target_pairs={{0,8},{8,0},{16,24},{24,16},{1,9},{9,1},{17,25},{25,17},{2,10},{10... | collective-permute-start | bytes 3145736 | tf_op jit(solution)/shard_map/ppermute | solution.py:454
  160.9 19.7 %collective-permute-start.36 = (bf16[192,2048]{1,0:T(8,128)(2,1)S(1)}, bf16[192,2048]{1,0:T(8,128)(2,1)S(1)}, u32[]{:S(2)}, u32[]{:S(2)}) collective-permute-start(bf16[192,2048]{1,0:T(8,128)(2,1)S(1)} %slice.283), channel_id=1, source_target_pairs={{0,1},{1,0},{2,3},{3,2},{4,5},{5,4},{6,7},{7,6},{8,9},{9,8},{10,11... | collective-permute-start | bytes 2359304 | tf_op jit(solution)/shard_map/ppermute | solution.py:444
  186.0 13.3 %collective-permute-start.43 = (bf16[64,2048]{1,0:T(8,128)(2,1)S(1)}, bf16[64,2048]{1,0:T(8,128)(2,1)S(1)}, u32[]{:S(2)}, u32[]{:S(2)}) collective-permute-start(bf16[64,2048]{1,0:T(8,128)(2,1)S(1)} %add_convert_fusion.11), channel_id=1, source_target_pairs={{0,1},{1,0},{2,3},{3,2},{4,5},{5,4},{6,7},{7,6},{8,9},{9,8},{10,11... | collective-permute-start | bytes 786440 | tf_op jit(solution)/shard_map/ppermute | solution.py:444
  188.7 16.2 %collective-permute-start.42 = (bf16[64,2048]{1,0:T(8,128)(2,1)S(1)}, bf16[64,2048]{1,0:T(8,128)(2,1)S(1)}, u32[]{:S(2)}, u32[]{:S(2)}) collective-permute-start(bf16[64,2048]{1,0:T(8,128)(2,1)S(1)} %add_convert_fusion.10), channel_id=1, source_target_pairs={{0,1},{1,0},{2,3},{3,2},{4,5},{5,4},{6,7},{7,6},{8,9},{9,8},{10,11... | collective-permute-start | bytes 786440 | tf_op jit(solution)/shard_map/ppermute | solution.py:444
  189.3 21.3 %collective-permute-start.41 = (bf16[64,2048]{1,0:T(8,128)(2,1)S(1)}, bf16[64,2048]{1,0:T(8,128)(2,1)S(1)}, u32[]{:S(2)}, u32[]{:S(2)}) collective-permute-start(bf16[64,2048]{1,0:T(8,128)(2,1)S(1)} %add_convert_fusion.9), channel_id=1, source_target_pairs={{0,1},{1,0},{2,3},{3,2},{4,5},{5,4},{6,7},{7,6},{8,9},{9,8},{10,11... | collective-permute-start | bytes 786440 | tf_op jit(solution)/shard_map/ppermute | solution.py:444
  190.9 24.6 %collective-permute-start.40 = (bf16[64,2048]{1,0:T(8,128)(2,1)S(1)}, bf16[64,2048]{1,0:T(8,128)(2,1)S(1)}, u32[]{:S(2)}, u32[]{:S(2)}) collective-permute-start(bf16[64,2048]{1,0:T(8,128)(2,1)S(1)} %slice.284), channel_id=1, source_target_pairs={{0,1},{1,0},{2,3},{3,2},{4,5},{5,4},{6,7},{7,6},{8,9},{9,8},{10,11... | collective-permute-start | bytes 786440 | tf_op jit(solution)/shard_map/ppermute | solution.py:444
  199.4 11.8 %collective-permute-start.48 = (bf16[64,2048]{1,0:T(8,128)(2,1)S(1)}, bf16[64,2048]{1,0:T(8,128)(2,1)S(1)}, u32[]{:S(2)}, u32[]{:S(2)}) collective-permute-start(bf16[64,2048]{1,0:T(8,128)(2,1)S(1)} %add_convert_fusion.7), channel_id=1, source_target_pairs={{0,16},{8,24},{16,0},{24,8},{1,17},{9,25},{17,1},{25,9},{2,18},{10... | collective-permute-start | bytes 786440 | tf_op jit(solution)/shard_map/ppermute | solution.py:454
  200.8 10.5 %collective-permute-start.49 = (bf16[64,2048]{1,0:T(8,128)(2,1)S(1)}, bf16[64,2048]{1,0:T(8,128)(2,1)S(1)}, u32[]{:S(2)}, u32[]{:S(2)}) collective-permute-start(bf16[64,2048]{1,0:T(8,128)(2,1)S(1)} %add_convert_fusion.6), channel_id=1, source_target_pairs={{0,2},{1,3},{2,0},{3,1},{4,6},{5,7},{6,4},{7,5},{8,10},{9,11},{10,... | collective-permute-start | bytes 786440 | tf_op jit(solution)/shard_map/ppermute | solution.py:444
  212.0 11.8 %collective-permute-start.50 = (bf16[64,2048]{1,0:T(8,128)(2,1)S(1)}, bf16[64,2048]{1,0:T(8,128)(2,1)S(1)}, u32[]{:S(2)}, u32[]{:S(2)}) collective-permute-start(bf16[64,2048]{1,0:T(8,128)(2,1)S(1)} %add_convert_fusion.2), channel_id=1, source_target_pairs={{0,2},{1,3},{2,0},{3,1},{4,6},{5,7},{6,4},{7,5},{8,10},{9,11},{10,... | collective-permute-start | bytes 786440 | tf_op jit(solution)/shard_map/ppermute | solution.py:444
  213.5 10.3 %collective-permute-start.51 = (bf16[64,2048]{1,0:T(8,128)(2,1)S(1)}, bf16[64,2048]{1,0:T(8,128)(2,1)S(1)}, u32[]{:S(2)}, u32[]{:S(2)}) collective-permute-start(bf16[64,2048]{1,0:T(8,128)(2,1)S(1)} %add_convert_fusion.3), channel_id=1, source_target_pairs={{0,4},{1,5},{2,6},{3,7},{4,0},{5,1},{6,2},{7,3},{8,12},{9,13},{10,... | collective-permute-start | bytes 786440 | tf_op jit(solution)/shard_map/ppermute | solution.py:444
  (53 other events, 567.9 us)
